TPU v7x, 32 devices: a whole 2x2x4 slice. The times are simulated.
32 devices in a mesh: wide: 8 (over z, x), seq: 4 (over y, core).
Axes of the slice: x: 2, y: 2, z: 4, core: 2. Of those that a mesh axis runs over, the one named last changes fastest.
Arguments:
- tokens: bfloat16 [8, 2048, 2304], P('seq', 'wide'), may hold values from -6 to 6
- cotangent: bfloat16 [8, 2048, 2304], P('seq', 'wide'), may hold values from -6 to 6
- widths: int32 [8], P('seq'), may hold values from 0 to 2
- attn_codes: int32 [2304, 6144], P('wide'), may hold values from -128 to 127
- attn_exps: int32 [4096], replicated, may hold values from 11 to 13
- out_exps: int32 [2304], replicated, may hold values from 11 to 13
- mlp_codes: int32 [3, 9216, 2304], P(None, 'wide'), may hold values from -128 to 127
- gate_exps: int32 [2, 9216], replicated, may hold values from 11 to 13
- down_exps: int32 [2304], replicated, may hold values from 12 to 14
- gain_attn: float32 [2304], replicated, may hold values from 0.25 to 1.75
- gain_post_attn: float32 [2304], replicated, may hold values from 0.25 to 1.75
- gain_mlp: float32 [2304], replicated, may hold values from 0.25 to 1.75
- gain_post_mlp: float32 [2304], replicated, may hold values from 0.25 to 1.75
Outputs:
- layer_out: bfloat16 [8, 2048, 2304], P('seq', 'wide')
- grad_tokens: bfloat16 [8, 2048, 2304], P('seq', 'wide')
- grad_attn_weights: float32 [2304, 6144], P('wide')
- grad_mlp_weights: float32 [3, 9216, 2304], P(None, 'wide')
- grad_gain_attn: float32 [2304], replicated
- grad_gain_post_attn: float32 [2304], replicated
- grad_gain_mlp: float32 [2304], replicated
- grad_gain_post_mlp: float32 [2304], replicated
All inputs are finite; a program needn't handle non-finite values.
Results may differ from a plain program's by a relative error of at most 0.024.
The roundings to bfloat16 on the way count: a program that leaves them out, or rounds other values in their place, can miss the bound.
Values may be sent and summed in bfloat16 or wider, within the bound.
No kernel may reach another device: no remote copies, remote signals or barrier semaphores. Data moves between devices by JAX's collectives and lax.ppermute only.
A program may use at most 576 MiB of HBM per device.

v0:
```python
import math

import jax
import jax.numpy as jnp
from jax import lax
from jax.sharding import PartitionSpec as P

QUERY_HEADS = 8
KEY_VALUE_HEADS = 4
HEAD_SIZE = 256


eps_norm = 1e-06
soft_cap = 50.0
rope_base = 10000.0
masked_score = -1e30
gelu_coeff = math.sqrt(2.0 / math.pi)


def integer_slice_codes(code_values, width_id):
    four_bit = jnp.clip(jnp.floor_divide(code_values + 8, 16), -8, 7) * 16
    two_bit = jnp.clip(jnp.floor_divide(code_values + 32, 64), -2, 1) * 64
    return jnp.where(width_id == 0, code_values, jnp.where(width_id == 1, four_bit, two_bit))


def powers(exponents):
    return jnp.left_shift(jnp.ones_like(exponents), exponents).astype(jnp.float32)


def rms_norm(values, gain):
    factor = lax.rsqrt(jnp.mean(values * values, axis=-1, keepdims=True) + eps_norm)
    return values * factor * gain


def gelu_tanh(values):
    return (
        0.5 * values * (1.0 + jnp.tanh(gelu_coeff * (values + 0.044715 * values * values * values)))
    )


def rotary_rows(positions, head_dim):
    half_dim = head_dim // 2
    frequency = jnp.exp(
        jnp.arange(half_dim, dtype=jnp.float32) * (-2.0 * math.log(rope_base) / head_dim)
    )
    angles = positions.astype(jnp.float32)[:, None] * frequency[None, :]
    return (jnp.cos(angles)[:, None, :], jnp.sin(angles)[:, None, :])


def rotate(values, cosine, sine_table):
    half_dim = values.shape[-1] // 2
    first_half = values[..., :half_dim]
    second_half = values[..., half_dim:]
    return jnp.concatenate(
        [
            first_half * cosine - second_half * sine_table,
            second_half * cosine + first_half * sine_table,
        ],
        axis=-1,
    )


def rotate_back(values, cosine, sine_table):
    half_dim = values.shape[-1] // 2
    first_half = values[..., :half_dim]
    second_half = values[..., half_dim:]
    return jnp.concatenate(
        [
            first_half * cosine + second_half * sine_table,
            second_half * cosine - first_half * sine_table,
        ],
        axis=-1,
    )


def attention_values(code_values, width_id, column_power, output_power):
    column_total = column_power.shape[0]
    sliced = integer_slice_codes(code_values, width_id).astype(jnp.float32)
    return jnp.concatenate(
        [
            sliced[:, :column_total] / column_power[None, :],
            sliced[:, column_total:] / output_power[:, None],
        ],
        axis=1,
    ).astype(jnp.bfloat16)


def attention_codes(incoming_block, column_power, output_power):
    column_total = column_power.shape[0]
    return jnp.concatenate(
        [
            incoming_block[:, :column_total].astype(jnp.float32) * column_power[None, :],
            incoming_block[:, column_total:].astype(jnp.float32) * output_power[:, None],
        ],
        axis=1,
    ).astype(jnp.int32)


def mlp_values(code_values, width_id, gate_power, down_power):
    sliced = integer_slice_codes(code_values, width_id).astype(jnp.float32)
    return jnp.concatenate(
        [sliced[:2] / gate_power[:, :, None], sliced[2:] / down_power[None, None, :]], axis=0
    ).astype(jnp.bfloat16)


def split_rows_into_heads(rows_array, number_of_classes, head_groups):
    sequence_count, number_of_rows, total_cols = rows_array.shape
    split_view = rows_array.reshape(
        sequence_count,
        number_of_rows // number_of_classes,
        number_of_classes,
        head_groups,
        total_cols // head_groups,
    )
    return jnp.transpose(split_view, (0, 3, 2, 1, 4)).reshape(
        sequence_count,
        head_groups * number_of_classes,
        number_of_rows // number_of_classes,
        total_cols // head_groups,
    )


def heads_to_rows(incoming_block, number_of_classes):
    sequence_count, wide_slice_count, class_rows, piece_cols = incoming_block.shape
    split_view = incoming_block.reshape(
        sequence_count,
        wide_slice_count // number_of_classes,
        number_of_classes,
        class_rows,
        piece_cols,
    )
    return jnp.transpose(split_view, (0, 3, 2, 1, 4)).reshape(
        sequence_count,
        class_rows * number_of_classes,
        wide_slice_count // number_of_classes * piece_cols,
    )


def capped_scores(query_head_tensor, key_heads, allowed):
    raw_scores = jnp.einsum(
        "sjgd,std->sgjt", query_head_tensor, key_heads, preferred_element_type=jnp.float32
    )
    bounded = jnp.tanh(raw_scores / soft_cap)
    return (jnp.where(allowed, soft_cap * bounded, masked_score), bounded)


def per_device(
    tokens,
    cotangent,
    widths,
    attn_codes,
    attn_exps,
    out_exps,
    mlp_codes,
    gate_exps,
    down_exps,
    gain_attn,
    gain_post_attn,
    gain_mlp,
    gain_post_mlp,
):
    wide_slice_count = lax.axis_size("wide")
    wide_index = lax.axis_index("wide")
    sequence_count, number_of_rows, model_dim = tokens.shape
    length = number_of_rows * wide_slice_count
    number_of_classes = wide_slice_count // KEY_VALUE_HEADS
    class_rows = number_of_rows // number_of_classes
    query_count = length // number_of_classes
    paired_heads = QUERY_HEADS // KEY_VALUE_HEADS
    query_columns = QUERY_HEADS * HEAD_SIZE
    key_value_columns = KEY_VALUE_HEADS * HEAD_SIZE
    projection_cols = attn_exps.shape[0]
    class_index = wide_index % number_of_classes
    query_scale = HEAD_SIZE ** (-0.5)
    column_power = powers(attn_exps)
    output_power = powers(out_exps)
    gate_power = powers(gate_exps)
    down_power = powers(down_exps)
    attn_rows = attn_codes.shape[0]
    hidden_rows = mlp_codes.shape[1]
    own_out_power = lax.dynamic_slice_in_dim(output_power, wide_index * attn_rows, attn_rows)
    own_gate_power = lax.dynamic_slice_in_dim(gate_power, wide_index * hidden_rows, hidden_rows, 1)
    attn_send = attention_values(attn_codes, 0, column_power, own_out_power)
    attn_full = lax.all_gather(attn_send, "wide", axis=0, tiled=True)
    attn_weights = jax.vmap(
        lambda width_id: attention_values(
            attention_codes(attn_full, column_power, output_power),
            width_id,
            column_power,
            output_power,
        )
    )(widths)
    inputs = tokens.astype(jnp.float32)
    normalized_input = rms_norm(inputs, gain_attn).astype(jnp.bfloat16)
    projected_output = jnp.einsum(
        "nxv,nvb->nxb",
        normalized_input,
        attn_weights[:, :, :projection_cols],
        preferred_element_type=jnp.float32,
    )
    cosine, sine_table = rotary_rows(
        wide_index * number_of_rows + jnp.arange(number_of_rows), HEAD_SIZE
    )
    query_token_rows = (
        rotate(
            projected_output[..., :query_columns].reshape(
                sequence_count, number_of_rows, QUERY_HEADS, HEAD_SIZE
            ),
            cosine,
            sine_table,
        )
        * query_scale
    ).astype(jnp.bfloat16)
    key_rows = rotate(
        projected_output[..., query_columns : query_columns + key_value_columns].reshape(
            sequence_count, number_of_rows, KEY_VALUE_HEADS, HEAD_SIZE
        ),
        cosine,
        sine_table,
    ).astype(jnp.bfloat16)
    value_rows = (
        projected_output[..., query_columns + key_value_columns :]
        .reshape(sequence_count, number_of_rows, KEY_VALUE_HEADS, HEAD_SIZE)
        .astype(jnp.bfloat16)
    )
    query_send = split_rows_into_heads(
        query_token_rows.reshape(sequence_count, number_of_rows, query_columns),
        number_of_classes,
        KEY_VALUE_HEADS,
    )
    paired_rows = jnp.transpose(jnp.concatenate([key_rows, value_rows], axis=-1), (0, 2, 1, 3))
    pair_send = jnp.broadcast_to(
        paired_rows[:, :, None],
        (sequence_count, KEY_VALUE_HEADS, number_of_classes, number_of_rows, 2 * HEAD_SIZE),
    ).reshape(sequence_count, wide_slice_count, number_of_rows, 2 * HEAD_SIZE)
    query_recv, pair_recv = (
        lax.all_to_all(query_send, "wide", split_axis=1, concat_axis=1, tiled=True),
        lax.all_to_all(pair_send, "wide", split_axis=1, concat_axis=1, tiled=True),
    )
    query_head_tensor = query_recv.reshape(sequence_count, query_count, paired_heads, HEAD_SIZE)
    pair_heads = pair_recv.reshape(sequence_count, length, 2 * HEAD_SIZE)
    key_heads = pair_heads[..., :HEAD_SIZE]
    value_heads = pair_heads[..., HEAD_SIZE:]
    allowed = (
        jnp.arange(length)[None, :]
        <= (jnp.arange(query_count) * number_of_classes + class_index)[:, None]
    )
    capped, bounded = capped_scores(query_head_tensor, key_heads, allowed)
    top_score = jnp.max(capped, axis=-1, keepdims=True)
    exp_scores = jnp.exp(capped - top_score)
    row_total = jnp.sum(exp_scores, axis=-1, keepdims=True)
    log_total = top_score + jnp.log(row_total)
    attended = jnp.einsum(
        "sgjt,std->sjgd",
        (exp_scores / row_total).astype(jnp.bfloat16),
        value_heads,
        preferred_element_type=jnp.float32,
    ).astype(jnp.bfloat16)
    out_back = lax.all_to_all(
        attended.reshape(sequence_count, wide_slice_count, class_rows, paired_heads * HEAD_SIZE),
        "wide",
        split_axis=1,
        concat_axis=1,
        tiled=True,
    )
    attended_token_rows = heads_to_rows(out_back, number_of_classes)
    branch = jnp.einsum(
        "cui,czi->cuz",
        attended_token_rows,
        attn_weights[:, :, projection_cols:],
        preferred_element_type=jnp.float32,
    )
    middle = inputs + rms_norm(branch, gain_post_attn)
    normalized_feedforward = rms_norm(middle, gain_mlp).astype(jnp.bfloat16)
    slice_weights = jax.vmap(
        lambda width_id: mlp_values(mlp_codes, width_id, own_gate_power, down_power)
    )(widths)
    normalized_group = lax.all_gather(normalized_feedforward, "wide", axis=1, tiled=True)
    gate_group = jnp.einsum(
        "jiu,jbxu->jibx", normalized_group, slice_weights[:, :2], preferred_element_type=jnp.float32
    )
    hidden_group = (gelu_tanh(gate_group[:, :, 0]) * gate_group[:, :, 1]).astype(jnp.bfloat16)
    mixed_part = jnp.einsum(
        "qok,qkg->qog", hidden_group, slice_weights[:, 2], preferred_element_type=jnp.float32
    )
    mixed_out = lax.psum_scatter(
        mixed_part.astype(jnp.bfloat16), "wide", scatter_dimension=1, tiled=True
    ).astype(jnp.float32)
    layer_out = (middle + rms_norm(mixed_out, gain_post_mlp)).astype(jnp.bfloat16)
    grad_out = cotangent.astype(jnp.float32)
    unused, norm_pull = jax.vjp(rms_norm, mixed_out, gain_post_mlp)
    grad_mixed_full, grad_gain_fourth = norm_pull(grad_out)
    mixed_gradient = grad_mixed_full.astype(jnp.bfloat16)
    grad_group = lax.all_gather(mixed_gradient, "wide", axis=1, tiled=True)
    grad_hidden = jnp.einsum(
        "zuk,ztk->zut", grad_group, slice_weights[:, 2], preferred_element_type=jnp.float32
    )
    gelu_value, gelu_pull = jax.vjp(gelu_tanh, gate_group[:, :, 0])
    grad_gate = gelu_pull(grad_hidden * gate_group[:, :, 1])[0]
    gradient_partner = jnp.stack([grad_gate, grad_hidden * gelu_value], axis=2).astype(jnp.bfloat16)
    grad_part = jnp.einsum(
        "vczp,vzpb->vcb", gradient_partner, slice_weights[:, :2], preferred_element_type=jnp.float32
    )
    grad_normed_mlp = lax.psum_scatter(
        grad_part.astype(jnp.bfloat16), "wide", scatter_dimension=1, tiled=True
    ).astype(jnp.float32)
    pair_term = jnp.einsum(
        "pvxw,pvn->xwn", gradient_partner, normalized_group, preferred_element_type=jnp.float32
    )
    down_projection_piece = jnp.einsum(
        "jrw,jry->wy", hidden_group, grad_group, preferred_element_type=jnp.float32
    )
    mlp_part = jnp.concatenate([pair_term, down_projection_piece[None]], axis=0)
    unused, norm_pull = jax.vjp(rms_norm, middle, gain_mlp)
    grad_from_mlp, grad_gain_third = norm_pull(grad_normed_mlp)
    grad_middle = grad_out + grad_from_mlp
    unused, norm_pull = jax.vjp(rms_norm, branch, gain_post_attn)
    grad_branch_full, grad_gain_second = norm_pull(grad_middle)
    branch_gradient = grad_branch_full.astype(jnp.bfloat16)
    attended_gradient = jnp.einsum(
        "bjy,byo->bjo",
        branch_gradient,
        attn_weights[:, :, projection_cols:],
        preferred_element_type=jnp.float32,
    ).astype(jnp.bfloat16)
    outgoing_gradient = split_rows_into_heads(attended_gradient, number_of_classes, KEY_VALUE_HEADS)
    grad_heads = lax.all_to_all(
        outgoing_gradient, "wide", split_axis=1, concat_axis=1, tiled=True
    ).reshape(sequence_count, query_count, paired_heads, HEAD_SIZE)
    capped, bounded = capped_scores(query_head_tensor, key_heads, allowed)
    attn_probs = jnp.exp(capped - log_total)
    grad_probs = jnp.einsum(
        "sjgd,std->sgjt", grad_heads, value_heads, preferred_element_type=jnp.float32
    )
    grad_capped = attn_probs * (
        grad_probs - jnp.sum(attn_probs * grad_probs, axis=-1, keepdims=True)
    )
    grad_raw = (grad_capped * (1.0 - bounded * bounded)).astype(jnp.bfloat16)
    grad_value = jnp.einsum(
        "sgjt,sjgd->std",
        attn_probs.astype(jnp.bfloat16),
        grad_heads,
        preferred_element_type=jnp.float32,
    )
    grad_query = jnp.einsum(
        "sgjt,std->sjgd", grad_raw, key_heads, preferred_element_type=jnp.float32
    )
    grad_key = jnp.einsum(
        "sgjt,sjgd->std", grad_raw, query_head_tensor, preferred_element_type=jnp.float32
    )
    query_grad_send = grad_query.reshape(
        sequence_count, wide_slice_count, class_rows, paired_heads * HEAD_SIZE
    )
    pair_grad_send = jnp.concatenate([grad_key, grad_value], axis=-1).reshape(
        sequence_count, wide_slice_count, number_of_rows, 2 * HEAD_SIZE
    )
    query_grad_back, paired_gradient_return = (
        lax.all_to_all(
            query_grad_send.astype(jnp.bfloat16), "wide", split_axis=1, concat_axis=1, tiled=True
        ).astype(query_grad_send.dtype),
        lax.all_to_all(
            pair_grad_send.astype(jnp.bfloat16), "wide", split_axis=1, concat_axis=1, tiled=True
        ).astype(pair_grad_send.dtype),
    )
    grad_query_rows = rotate_back(
        heads_to_rows(query_grad_back, number_of_classes).reshape(
            sequence_count, number_of_rows, QUERY_HEADS, HEAD_SIZE
        )
        * query_scale,
        cosine,
        sine_table,
    )
    pair_total = jnp.transpose(
        jnp.sum(
            paired_gradient_return.reshape(
                sequence_count, KEY_VALUE_HEADS, number_of_classes, number_of_rows, 2 * HEAD_SIZE
            ),
            axis=2,
        ),
        (0, 2, 1, 3),
    )
    grad_key_rows = rotate_back(pair_total[..., :HEAD_SIZE], cosine, sine_table)
    projected_gradient = jnp.concatenate(
        [
            grad_query_rows.reshape(sequence_count, number_of_rows, query_columns),
            grad_key_rows.reshape(sequence_count, number_of_rows, key_value_columns),
            pair_total[..., HEAD_SIZE:].reshape(sequence_count, number_of_rows, key_value_columns),
        ],
        axis=-1,
    ).astype(jnp.bfloat16)
    grad_normed = jnp.einsum(
        "gwo,gko->gwk",
        projected_gradient,
        attn_weights[:, :, :projection_cols],
        preferred_element_type=jnp.float32,
    )
    unused, norm_pull = jax.vjp(rms_norm, inputs, gain_attn)
    grad_from_attn, grad_gain_first = norm_pull(grad_normed)
    grad_tokens = (grad_middle + grad_from_attn).astype(jnp.bfloat16)
    projection_term = jnp.einsum(
        "anx,anr->xr", normalized_input, projected_gradient, preferred_element_type=jnp.float32
    )
    output_term = jnp.einsum(
        "fug,fuw->gw", branch_gradient, attended_token_rows, preferred_element_type=jnp.float32
    )
    attn_part = lax.psum_scatter(
        jnp.concatenate([projection_term, output_term], axis=1).astype(jnp.bfloat16),
        "wide",
        scatter_dimension=0,
        tiled=True,
    )
    attn_grad, mlp_grad = (
        lax.psum(attn_part, "seq").astype(jnp.float32),
        lax.psum(mlp_part.astype(jnp.bfloat16), "seq").astype(jnp.float32),
    )
    gain_grads = lax.psum(
        jnp.stack([grad_gain_first, grad_gain_second, grad_gain_third, grad_gain_fourth]),
        ("wide", "seq"),
    )
    return (
        layer_out,
        grad_tokens,
        attn_grad,
        mlp_grad,
        gain_grads[0],
        gain_grads[1],
        gain_grads[2],
        gain_grads[3],
    )


def solution(mesh):
    placed = (
        P("seq", "wide", None),
        P("seq", "wide", None),
        P("seq"),
        P("wide", None),
        P(),
        P(),
        P(None, "wide", None),
        P(),
        P(),
        P(),
        P(),
        P(),
        P(),
    )
    return jax.shard_map(
        per_device,
        mesh=mesh,
        in_specs=placed,
        out_specs=(
            P("seq", "wide", None),
            P("seq", "wide", None),
            P("wide", None),
            P(None, "wide", None),
            P(),
            P(),
            P(),
            P(),
        ),
        check_vma=False,
    )
```

profile of v0, /device:TPU:0, one launch (start us, length us, event | category | flops | bytes accessed | tf_op | source)
XLA Modules:
  0.0 3974.9 jit_solution(10256088609646277244)
XLA Ops:
  26.3 538.5 %all-gather.4.cloned.1.call-done = bf16[2304,6144]{1,0:T(8,128)(2,1)} async-done(((bf16[288,6144]{1,0:T(8,128)(2,1)}), bf16[2304,6144]{1,0:T(8,128)(2,1)}) %all-gather.4.cloned.1.call-update) | async-done | bytes 28311568 | tf_op jit(solution)/shard_map/all_gather | solution.py:184
  564.8 11.8 convert_multiply_fusion.1
  576.6 21.2 convert_multiply_fusion
  597.8 37.9 maximum_convert_fusion
  635.7 96.6 %fusion.4 = (s32[2304,6144]{1,0:T(8,128)}, s32[2304,6144]{1,0:T(8,128)}) fusion(f32[2304,2048]{1,0:T(8,128)} %convert_multiply_fusion.1, f32[2304,4096]{1,0:T(8,128)} %convert_multiply_fusion), kind=kLoop, calls=%fused_computation.15 | loop fusion | flops 537919488 | bytes 169869312 | tf_op jit(solution)/shard_map/vmap()/mul | solution.py:21
  732.4 90.4 %select_convert_fusion = f32[2,2304,6144]{2,1,0:T(8,128)} fusion(s32[2304,6144]{1,0:T(8,128)} %get-tuple-element.28, s32[2304,6144]{1,0:T(8,128)} %get-tuple-element.27, s32[2304,6144]{1,0:T(8,128)} %maximum_convert_fusion, pred[2]{0:T(512)(128)(4,1)S(1)} %get-tuple-element.45, pred[2]{0:T(512)(128)(4,1)S(1)} %get-tuple-element.44), kind=kLoop, calls=%fused_computation.1 | loop fusion | flops 84934656 | bytes 283115520 | tf_op jit(solution)/shard_map/vmap()/convert_element_type | solution.py:78
  822.7 36.9 fusion.1
  859.6 19.9 fusion.79
  912.1 32.4 all-to-all-done.1
  962.7 81.8 %all-to-all-done = bf16[2,8,256,512]{3,2,0,1:T(8,128)(2,1)} async-done(((bf16[2,8,256,512]{3,2,0,1:T(8,128)(2,1)}), bf16[2,8,256,512]{3,2,0,1:T(8,128)(2,1)}, u32[]{:S(2)}, u32[]{:S(2)}) %all-to-all-start) | async-done | bytes 4194336 | tf_op jit(solution)/shard_map/all_to_all | solution.py:238
  1047.0 17.6 fusion.55
  1064.6 15.9 fusion.22
  1080.5 20.7 fusion.77
  1108.9 22.0 fusion.11
  1130.9 26.4 all-to-all-done.2
  1163.5 10.2 multiply_reduce_fusion.3
  1181.1 53.0 %fusion.16 = (s32[3,1152,2304]{2,1,0:T(8,128)}, s32[3,1152,2304]{2,1,0:T(8,128)}) fusion(s32[3,1152,2304]{2,1,0:T(8,128)} %param.19), kind=kLoop, calls=%fused_computation.51 | loop fusion | flops 286654464 | bytes 95551488 | tf_op jit(solution)/shard_map/vmap()/mul | solution.py:21
  1235.5 52.4 %select_convert_fusion.1 = f32[2,3,1152,2304]{3,2,0,1:T(8,128)} fusion(s32[3,1152,2304]{2,1,0:T(8,128)} %get-tuple-element.30, s32[3,1152,2304]{2,1,0:T(8,128)} %get-tuple-element.29, s32[3,1152,2304]{2,1,0:T(8,128)} %param.19, pred[2]{0:T(512)(128)(4,1)S(1)} %copy-done.65, pred[2]{0:T(512)(128)(4,1)S(1)} %copy-done.63), kind=kLoop, calls=%fused_computation.12 | loop fusion | flops 47775744 | bytes 159252480 | tf_op jit(solution)/shard_map/vmap()/convert_element_type | solution.py:100
  1287.9 22.2 fusion.10
  1310.1 232.6 %all-gather.6.cloned.1.call-done = bf16[2,2048,2304]{2,1,0:T(8,128)(2,1)} async-done(((bf16[2,256,2304]{2,1,0:T(8,128)(2,1)}), bf16[2,2048,2304]{2,1,0:T(8,128)(2,1)}) %all-gather.6.cloned.1.call-update) | async-done | bytes 18874384 | tf_op jit(solution)/shard_map/all_gather | solution.py:278
  1542.7 59.3 %fusion.25 = f32[2,2048,2,1152]{3,1,2,0:T(8,128)} fusion(bf16[2,2,1152,2304]{3,2,0,1:T(8,128)(2,1)} %fusion.10, bf16[2,2048,2304]{2,1,0:T(8,128)(2,1)} %all-gather.6.cloned.1.call-done), kind=kOutput, calls=%fused_computation.69 | convolution fusion | flops 43486543872 | bytes 77856768 | tf_op jit(solution)/shard_map/jiu,jbxu->jibx/dot_general | solution.py:279
  1602.0 18.0 multiply_convert_fusion.1
  1620.0 35.0 convolution_convert_fusion
  1655.1 313.4 %reduce-scatter.4.cloned.1.call-done = bf16[2,256,2304]{2,1,0:T(8,128)(2,1)} async-done(((bf16[2,2048,2304]{2,1,0:T(8,128)(2,1)}), bf16[2,256,2304]{2,1,0:T(8,128)(2,1)}) %reduce-scatter.4.cloned.1.call-update) | async-done | bytes 2359312 | tf_op jit(solution)/shard_map/reduce_scatter | solution.py:286
  1979.2 361.7 %all-gather.8.cloned.1.call-done = bf16[2,2048,2304]{2,1,0:T(8,128)(2,1)} async-done(((bf16[2,256,2304]{2,1,0:T(8,128)(2,1)}), bf16[2,2048,2304]{2,1,0:T(8,128)(2,1)}) %all-gather.8.cloned.1.call-update) | async-done | bytes 18874384 | tf_op jit(solution)/shard_map/all_gather | solution.py:294
  2340.9 54.9 %fusion.46 = (bf16[2,2048,1,1152]{3,1,0,2:T(8,128)(2,1)}, bf16[2,2048,1,1152]{3,1,0,2:T(8,128)(2,1)}) fusion(f32[2,2048,2,1152]{3,1,2,0:T(8,128)} %fusion.25, bf16[2,2048,2304]{2,1,0:T(8,128)(2,1)} %all-gather.8.cloned.1.call-done, f32[2304]{0:T(1024)S(1)} %copy-done.57, f32[2,3,1152,2304]{3,2,0,1:T(8,128)} %select_convert_fusion.1), kind=kOutput, calls=%fused_computation.105 | convolution fusion | flops 21886009344 | bytes 96740352 | tf_op jit(solution)/shard_map/zuk,ztk->zut/dot_general | solution.py:295
  2395.8 58.1 %bitcast_convert_fusion.1 = bf16[2,2048,2304]{2,1,0:T(8,128)(2,1)} fusion(bf16[2,2,1152,2304]{3,2,0,1:T(8,128)(2,1)} %fusion.10, bf16[2,2048,1,1152]{3,1,0,2:T(8,128)(2,1)} %get-tuple-element.26, bf16[2,2048,1,1152]{3,1,0,2:T(8,128)(2,1)} %get-tuple-element.25), kind=kOutput, calls=%fused_computation.37 | convolution fusion | flops 43505418240 | bytes 58982400 | tf_op jit(solution)/shard_map/vczp,vzpb->vcb/dot_general | solution.py:301
  2454.1 313.4 %reduce-scatter.6.cloned.1.call-done = bf16[2,256,2304]{2,1,0:T(8,128)(2,1)} async-done(((bf16[2,2048,2304]{2,1,0:T(8,128)(2,1)}), bf16[2,256,2304]{2,1,0:T(8,128)(2,1)}) %reduce-scatter.6.cloned.1.call-update) | async-done | bytes 2359312 | tf_op jit(solution)/shard_map/reduce_scatter | solution.py:304
  2772.7 8.5 multiply_reduce_fusion
  2785.8 12.6 convolution_convert_fusion.1
  2807.8 48.3 %all-to-all-done.3 = bf16[2,8,128,512]{3,2,0,1:T(8,128)(2,1)S(1)} async-done(((bf16[2,8,128,512]{3,2,0,1:T(8,128)(2,1)}), bf16[2,8,128,512]{3,2,0,1:T(8,128)(2,1)S(1)}, u32[]{:S(2)}, u32[]{:S(2)}) %all-to-all-start.3) | async-done | bytes 2097184 | tf_op jit(solution)/shard_map/all_to_all | solution.py:327
  2862.8 18.0 fusion.81
  2880.8 46.6 %fusion.76 = bf16[2,256,2,1024]{3,1,2,0:T(8,128)(2,1)} fusion(f32[2,2048,1024,2]{2,1,3,0:T(8,128)} %fusion.81, f32[2,2048,1024,2]{2,1,3,0:T(8,128)} %get-tuple-element.47, f32[2,2,1024]{2,1,0:T(2,128)S(1)} %log_add_fusion, pred[1024,2048]{0,1:T(8,128)(4,1)S(1)} %copy-done.11, bf16[2,2048,512]{2,1,0:T(8,128)(2,1)} %bitcast.260), kind=kOutput, calls=%fused_computation.174 | convolution fusion | flops 4421851136 | bytes 142639104 | tf_op jit(solution)/shard_map/sgjt,std->sjgd/dot_general | solution.py:345
  2936.1 46.8 %bitcast_convert_fusion.5 = bf16[2,2048,256]{1,2,0:T(8,128)(2,1)} fusion(bf16[2,1024,2,256]{1,3,2,0:T(8,128)(2,1)} %reshape.263, f32[2,2048,1024,2]{2,1,3,0:T(8,128)} %fusion.81, f32[2,2048,1024,2]{2,1,3,0:T(8,128)} %get-tuple-element.47, f32[2,2,1024]{2,1,0:T(2,128)S(1)} %log_add_fusion, pred[1024,2048]{0,1:T(8,128)(4,1)S(1)} %copy-done.11), kind=kOutput, calls=%fused_computation.158 | convolution fusion | flops 4421851136 | bytes 73416704 | tf_op jit(solution)/shard_map/sgjt,sjgd->std/dot_general | solution.py:348
  2983.0 17.0 bitcast_convert_fusion.4
  3008.8 9.3 bitcast_convert_fusion.3
  3041.7 59.3 %all-to-all-done.5 = bf16[2,8,256,512]{2,3,0,1:T(8,128)(2,1)} async-done(((bf16[2,8,256,512]{2,3,0,1:T(8,128)(2,1)}), bf16[2,8,256,512]{2,3,0,1:T(8,128)(2,1)}, u32[]{:S(2)}, u32[]{:S(2)}) %all-to-all-start.5) | async-done | bytes 4194336 | tf_op jit(solution)/shard_map/all_to_all | solution.py:361
  3125.9 16.0 bitcast_convert_fusion
  3141.8 19.3 pad_maximum_fusion
  3161.2 29.7 fusion.44
  3190.9 55.9 %bitcast_convert_fusion.2 = bf16[2,1152,2304]{2,1,0:T(8,128)(2,1)} fusion(bf16[2,2048,2304]{2,1,0:T(8,128)(2,1)} %all-gather.6.cloned.1.call-done, bf16[2,2048,1,1152]{3,1,0,2:T(8,128)(2,1)} %get-tuple-element.26, bf16[2,2048,1,1152]{3,1,0,2:T(8,128)(2,1)} %get-tuple-element.25), kind=kOutput, calls=%fused_computation.68 | convolution fusion | flops 43501289472 | bytes 48365568 | tf_op jit(solution)/shard_map/pvxw,pvn->xwn/dot_general | solution.py:307
  3246.8 13.4 pad_maximum_fusion.2
  3260.2 348.9 %reduce-scatter.8.cloned.1.call-done = bf16[288,6144]{1,0:T(8,128)(2,1)} async-done(((bf16[2304,6144]{1,0:T(8,128)(2,1)}), bf16[288,6144]{1,0:T(8,128)(2,1)}) %reduce-scatter.8.cloned.1.call-update) | async-done | bytes 3538960 | tf_op jit(solution)/shard_map/reduce_scatter | solution.py:406
  3609.2 20.0 fusion.57
  3629.3 41.8 %psum.23 = f32[4,2304]{1,0:T(4,128)S(1)} all-reduce(f32[4,2304]{1,0:T(4,128)S(1)} %pad_maximum_fusion.9), channel_id=1, replica_groups=mesh['wide'=8,'seq'=4] {'wide','seq'}, use_global_device_ids=true, to_apply=%region_21.22 | all-reduce | flops 9216 | bytes 73728 | tf_op jit(solution)/shard_map/psum | solution.py:416
  3671.7 7.1 fusion.66
  3678.8 265.5 %all-reduce.3.cloned.1.call-done = (bf16[288,6144]{1,0:T(8,128)(2,1)}, bf16[3,1152,2304]{2,1,0:T(8,128)(2,1)}) async-done(((bf16[288,6144]{1,0:T(8,128)(2,1)}, bf16[3,1152,2304]{2,1,0:T(8,128)(2,1)}), (bf16[288,6144]{1,0:T(8,128)(2,1)}, bf16[3,1152,2304]{2,1,0:T(8,128)(2,1)})) %all-reduce.3.cloned.1.call-update) | async-done | bytes 19464208 | tf_op jit(solution)/shard_map/psum | solution.py:413
  3950.2 17.7 convert_element_type.175
  (254 shorter events, 203.7 us)
Async XLA Ops:
  7.2 557.6 %all-gather.4.cloned.1.call-start = ((), (), s32[]{:S(2)}) async-start(), calls=%async_computation.9 | async-start | bytes 31850496 | tf_op jit(solution)/shard_map/all_gather | solution.py:184
  7.9 556.9 %copy-start.29 = (f32[2304]{0:T(1024)}, f32[2304]{0:T(1024)S(1)}, u32[]{:S(2)}) copy-start(f32[2304]{0:T(1024)S(1)} %shift-left_convert_fusion.2) | copy-start | bytes 27652
  8.7 568.0 %copy-start.27 = (f32[4096]{0:T(1024)}, f32[4096]{0:T(1024)S(1)}, u32[]{:S(2)}) copy-start(f32[4096]{0:T(1024)S(1)} %shift-left_convert_fusion) | copy-start | bytes 49156
  23.1 553.5 %copy-start.17 = (f32[256,128]{0,1:T(8,128)}, f32[256,128]{0,1:T(8,128)S(1)}, u32[]{:S(2)}) copy-start(f32[256,128]{0,1:T(8,128)S(1)} %get-tuple-element.42) | copy-start | bytes 393220
  23.1 553.5 %copy-start.20 = (f32[256,128]{0,1:T(8,128)}, f32[256,128]{0,1:T(8,128)S(1)}, u32[]{:S(2)}) copy-start(f32[256,128]{0,1:T(8,128)S(1)} %get-tuple-element.43) | copy-start | bytes 393220
  24.6 707.7 %copy-start.62 = (pred[2]{0:T(512)(128)(4,1)}, pred[2]{0:T(512)(128)(4,1)S(1)}, u32[]{:S(2)}) copy-start(pred[2]{0:T(512)(128)(4,1)S(1)} %get-tuple-element.44) | copy-start | bytes 10
  24.6 707.7 %copy-start.64 = (pred[2]{0:T(512)(128)(4,1)}, pred[2]{0:T(512)(128)(4,1)S(1)}, u32[]{:S(2)}) copy-start(pred[2]{0:T(512)(128)(4,1)S(1)} %get-tuple-element.45) | copy-start | bytes 10
  732.3 90.4 %copy-start.28 = (f32[4096]{0:T(1024)S(1)}, f32[4096]{0:T(1024)}, u32[]{:S(2)}) copy-start(f32[4096]{0:T(1024)} %copy-done.27) | copy-start | bytes 49156
  822.7 36.9 copy-start.6
  822.7 36.9 copy-start.54
  891.3 53.1 %all-to-all-start.1 = ((bf16[2,8,128,512]{3,2,0,1:T(8,128)(2,1)}), bf16[2,8,128,512]{3,2,0,1:T(8,128)(2,1)}, u32[]{:S(2)}, u32[]{:S(2)}) async-start(bf16[2,8,128,512]{3,2,0,1:T(8,128)(2,1)} %bitcast.8), calls=%async_computation.1 | async-start | bytes 4194304 | tf_op jit(solution)/shard_map/all_to_all | solution.py:237
  946.9 97.6 %all-to-all-start = ((bf16[2,8,256,512]{3,2,0,1:T(8,128)(2,1)}), bf16[2,8,256,512]{3,2,0,1:T(8,128)(2,1)}, u32[]{:S(2)}, u32[]{:S(2)}) async-start(bf16[2,8,256,512]{3,2,0,1:T(8,128)(2,1)} %bitcast.249), calls=%async_computation | async-start | bytes 8388608 | tf_op jit(solution)/shard_map/all_to_all | solution.py:238
  953.8 126.7 %copy-start.10 = (pred[1024,2048]{0,1:T(8,128)(4,1)}, pred[1024,2048]{0,1:T(8,128)(4,1)S(1)}, u32[]{:S(2)}) copy-start(pred[1024,2048]{0,1:T(8,128)(4,1)S(1)} %iota_compare_fusion) | copy-start | bytes 6291460
  1105.2 52.1 %all-to-all-start.2 = ((bf16[2,8,128,512]{2,3,0,1:T(8,128)(2,1)}), bf16[2,8,128,512]{2,3,0,1:T(8,128)(2,1)S(1)}, u32[]{:S(2)}, u32[]{:S(2)}) async-start(bf16[2,8,128,512]{2,3,0,1:T(8,128)(2,1)} %copy.96), calls=%async_computation.2 | async-start | bytes 4194304 | tf_op jit(solution)/shard_map/all_to_all | solution.py:259
  1108.8 433.9 %all-gather.6.cloned.1.call-start = ((), (), s32[]{:S(2)}) async-start(), calls=%async_computation.10 | async-start | bytes 21233664 | tf_op jit(solution)/shard_map/all_gather | solution.py:278
  1173.7 60.4 %copy-start.60 = (f32[2,256]{1,0:T(2,128)}, f32[2,256]{1,0:T(2,128)S(1)}, u32[]{:S(2)}) copy-start(f32[2,256]{1,0:T(2,128)S(1)} %get-tuple-element.48) | copy-start | bytes 6148
  1173.7 60.4 %copy-start.44 = (f32[2,256]{1,0:T(2,128)}, f32[2,256]{1,0:T(2,128)S(1)}, u32[]{:S(2)}) copy-start(f32[2,256]{1,0:T(2,128)S(1)} %fusion.85) | copy-start | bytes 6148
  1176.9 57.2 %copy-start.50 = (f32[2,256]{1,0:T(2,128)}, f32[2,256]{1,0:T(2,128)S(1)}, u32[]{:S(2)}) copy-start(f32[2,256]{1,0:T(2,128)S(1)} %get-tuple-element.23) | copy-start | bytes 6148
  1177.0 57.2 %copy-start.48 = (f32[2,256]{1,0:T(2,128)}, f32[2,256]{1,0:T(2,128)S(1)}, u32[]{:S(2)}) copy-start(f32[2,256]{1,0:T(2,128)S(1)} %fusion.86) | copy-start | bytes 6148
  1181.0 53.8 %copy-start.56 = (s32[2304]{0:T(1024)S(1)}, s32[2304]{0:T(1024)}, u32[]{:S(2)}) copy-start(s32[2304]{0:T(1024)} %param.21) | copy-start | bytes 27652
  1181.0 54.4 %copy-start.63 = (pred[2]{0:T(512)(128)(4,1)S(1)}, pred[2]{0:T(512)(128)(4,1)}, u32[]{:S(2)}) copy-start(pred[2]{0:T(512)(128)(4,1)} %copy-done.62) | copy-start | bytes 10
  1181.0 54.4 %copy-start.65 = (pred[2]{0:T(512)(128)(4,1)S(1)}, pred[2]{0:T(512)(128)(4,1)}, u32[]{:S(2)}) copy-start(pred[2]{0:T(512)(128)(4,1)} %copy-done.64) | copy-start | bytes 10
  1181.0 787.5 %reduce-scatter.4.cloned.1.call-start = ((), (), s32[]{:S(2)}) async-start(), calls=%async_computation.11 | async-start | bytes 21233664 | tf_op jit(solution)/shard_map/reduce_scatter | solution.py:286
  1655.0 315.7 %copy-start.4 = (bf16[2,256,2304]{2,1,0:T(8,128)(2,1)S(1)}, bf16[2,256,2304]{2,1,0:T(8,128)(2,1)}, u32[]{:S(2)}) copy-start(bf16[2,256,2304]{2,1,0:T(8,128)(2,1)} %param.14) | copy-start | bytes 7077892
  1655.0 315.7 %copy-start.33 = (f32[2304]{0:T(1024)S(1)}, f32[2304]{0:T(1024)}, u32[]{:S(2)}) copy-start(f32[2304]{0:T(1024)} %param.25) | copy-start | bytes 27652
  1655.1 685.9 %all-gather.8.cloned.1.call-start = ((), (), s32[]{:S(2)}) async-start(), calls=%async_computation.12 | async-start | bytes 21233664 | tf_op jit(solution)/shard_map/all_gather | solution.py:294
  1979.2 788.3 %reduce-scatter.6.cloned.1.call-start = ((), (), s32[]{:S(2)}) async-start(), calls=%async_computation.13 | async-start | bytes 21233664 | tf_op jit(solution)/shard_map/reduce_scatter | solution.py:304
  2454.0 313.5 %copy-start.36 = (f32[2304]{0:T(1024)S(1)}, f32[2304]{0:T(1024)}, u32[]{:S(2)}) copy-start(f32[2304]{0:T(1024)} %param.24) | copy-start | bytes 27652
  2454.0 313.5 %copy-start.49 = (f32[2,256]{1,0:T(2,128)S(1)}, f32[2,256]{1,0:T(2,128)}, u32[]{:S(2)}) copy-start(f32[2,256]{1,0:T(2,128)} %copy-done.48) | copy-start | bytes 6148
  2454.0 318.7 %copy-start.51 = (f32[2,256]{1,0:T(2,128)S(1)}, f32[2,256]{1,0:T(2,128)}, u32[]{:S(2)}) copy-start(f32[2,256]{1,0:T(2,128)} %copy-done.50) | copy-start | bytes 6148
  2454.0 318.7 %copy-start.3 = (bf16[2,256,2304]{2,1,0:T(8,128)(2,1)S(1)}, bf16[2,256,2304]{2,1,0:T(8,128)(2,1)}, u32[]{:S(2)}) copy-start(bf16[2,256,2304]{2,1,0:T(8,128)(2,1)} %reduce-scatter.4.cloned.1.call-done) | copy-start | bytes 7077892
  2454.0 318.7 %copy-start.32 = (f32[2304]{0:T(1024)S(1)}, f32[2304]{0:T(1024)}, u32[]{:S(2)}) copy-start(f32[2304]{0:T(1024)} %param.23) | copy-start | bytes 27652
  2454.0 318.7 %copy-start.34 = (f32[2304]{0:T(1024)S(1)}, f32[2304]{0:T(1024)}, u32[]{:S(2)}) copy-start(f32[2304]{0:T(1024)} %param.25) | copy-start | bytes 27652
  2454.0 318.7 %copy-start.45 = (f32[2,256]{1,0:T(2,128)S(1)}, f32[2,256]{1,0:T(2,128)}, u32[]{:S(2)}) copy-start(f32[2,256]{1,0:T(2,128)} %copy-done.44) | copy-start | bytes 6148
  2454.0 318.7 %copy-start.47 = (f32[2,256]{1,0:T(2,128)S(1)}, f32[2,256]{1,0:T(2,128)}, u32[]{:S(2)}) copy-start(f32[2,256]{1,0:T(2,128)} %copy-done.46) | copy-start | bytes 6148
  2454.1 327.2 %copy-start.61 = (f32[2,256]{1,0:T(2,128)S(1)}, f32[2,256]{1,0:T(2,128)}, u32[]{:S(2)}) copy-start(f32[2,256]{1,0:T(2,128)} %copy-done.60) | copy-start | bytes 6148
  2454.1 329.4 %slice-start = ((s8[4718592]{0:T(1024)(128)(4,1)}), s8[524288]{0:T(1024)(128)(4,1)S(1)}, s32[]{:S(2)}) async-start(s8[4718592]{0:T(1024)(128)(4,1)} %bitcast.247), calls=%async_computation.16 | async-start | bytes 1048576
  2803.8 52.3 %all-to-all-start.3 = ((bf16[2,8,128,512]{3,2,0,1:T(8,128)(2,1)}), bf16[2,8,128,512]{3,2,0,1:T(8,128)(2,1)S(1)}, u32[]{:S(2)}, u32[]{:S(2)}) async-start(bf16[2,8,128,512]{3,2,0,1:T(8,128)(2,1)} %bitcast.262), calls=%async_computation.5 | async-start | bytes 4194304 | tf_op jit(solution)/shard_map/all_to_all | solution.py:327
  2931.3 71.4 %all-to-all-start.4 = ((bf16[2,8,128,512]{2,3,0,1:T(8,128)(2,1)}), bf16[2,8,128,512]{2,3,0,1:T(8,128)(2,1)}, u32[]{:S(2)}, u32[]{:S(2)}) async-start(bf16[2,8,128,512]{2,3,0,1:T(8,128)(2,1)} %copy.106), calls=%async_computation.6 | async-start | bytes 4194304 | tf_op jit(solution)/shard_map/all_to_all | solution.py:358
  3002.7 98.2 %all-to-all-start.5 = ((bf16[2,8,256,512]{2,3,0,1:T(8,128)(2,1)}), bf16[2,8,256,512]{2,3,0,1:T(8,128)(2,1)}, u32[]{:S(2)}, u32[]{:S(2)}) async-start(bf16[2,8,256,512]{2,3,0,1:T(8,128)(2,1)} %bitcast.250), calls=%async_computation.7 | async-start | bytes 8388608 | tf_op jit(solution)/shard_map/all_to_all | solution.py:361
  3008.7 600.4 %reduce-scatter.8.cloned.1.call-start = ((), (), s32[]{:S(2)}) async-start(), calls=%async_computation.14 | async-start | bytes 31850496 | tf_op jit(solution)/shard_map/reduce_scatter | solution.py:406
  3035.8 71.2 %copy-start.19 = (f32[256,128]{0,1:T(8,128)S(1)}, f32[256,128]{0,1:T(8,128)}, u32[]{:S(2)}) copy-start(f32[256,128]{0,1:T(8,128)} %copy-done.17) | copy-start | bytes 393220
  3035.8 71.2 %copy-start.22 = (f32[256,128]{0,1:T(8,128)S(1)}, f32[256,128]{0,1:T(8,128)}, u32[]{:S(2)}) copy-start(f32[256,128]{0,1:T(8,128)} %copy-done.20) | copy-start | bytes 393220
  3161.2 783.2 %all-reduce.3.cloned.1.call-start = ((), (), s32[]{:S(2)}) async-start(), calls=%async_computation.15 | async-start | bytes 38928384 | tf_op jit(solution)/shard_map/psum | solution.py:413
  3260.2 348.9 %copy-start.42 = (f32[2304]{0:T(1024)S(1)}, f32[2304]{0:T(1024)}, u32[]{:S(2)}) copy-start(f32[2304]{0:T(1024)} %get-tuple-element.14) | copy-start | bytes 27652
  3260.2 348.9 %copy-start.43 = (f32[2304]{0:T(1024)S(1)}, f32[2304]{0:T(1024)}, u32[]{:S(2)}) copy-start(f32[2304]{0:T(1024)} %get-tuple-element.12) | copy-start | bytes 27652
  3260.2 349.0 %copy-start.41 = (f32[2304]{0:T(1024)S(1)}, f32[2304]{0:T(1024)}, u32[]{:S(2)}) copy-start(f32[2304]{0:T(1024)} %get-tuple-element.8) | copy-start | bytes 27652
  3609.2 62.5 %copy-start.53 = (f32[2,256]{1,0:T(2,128)S(1)}, f32[2,256]{1,0:T(2,128)}, u32[]{:S(2)}) copy-start(f32[2,256]{1,0:T(2,128)} %copy-done.52) | copy-start | bytes 6148
  (35 other events, 481.2 us)
Sparse Core Ops, SparseCore 0:
  22.7 542.1 all-gather.3
  1181.1 361.4 all-gather.5
  1655.2 313.3 reduce-scatter.3
  1979.3 361.5 all-gather.7
  2454.2 313.2 reduce-scatter.5
  3161.3 447.7 reduce-scatter.7
  3612.0 332.3 all-reduce.2
where the time goes:
time: 3980 us; the launch traced here: 3970 us
  waiting for transfers between devices  2620 us (66%)
  other arithmetic  608 us (15%)
  matrix products  548 us (14%)
  local copies, waits for them, and re-layouts  111 us (3%)
  blocking collectives  41.8 us (1%)
    all_gather x1, waiting for transfers between devices, per_device(): attn_full = lax.all_gather(attn_send, 'wide', axis=0, tiled=True)  539 us
    all_gather x1, waiting for transfers between devices, per_device(): grad_group = lax.all_gather(mixed_gradient, 'wide', axis=1, tiled=True)  362 us
    reduce_scatter x1, waiting for transfers between devices, per_device(): lax.psum_scatter(jnp.concatenate([projection_term, output_term], axis=1)....  349 us
    reduce_scatter x1, waiting for transfers between devices, per_device(): lax.psum_scatter(mixed_part.astype(jnp.bfloat16), 'wide', scatter_dimensi...  313 us
    reduce_scatter x1, waiting for transfers between devices, per_device(): lax.psum_scatter(grad_part.astype(jnp.bfloat16), 'wide', scatter_dimensio...  313 us
    psum x1, waiting for transfers between devices, per_device(): lax.psum(attn_part, 'seq').astype(jnp.float32)  266 us
    all_gather x1, waiting for transfers between devices, per_device(): lax.all_gather(normalized_feedforward, 'wide', axis=1, tiled=True)  233 us
    mul x2, other arithmetic, integer_slice_codes(): four_bit = jnp.clip(jnp.floor_divide(code_values + 8, 16), -8, 7) * 16  150 us
  transfers between devices with their start and end apart: 13, of which 12 were waited for; matrix products, arithmetic and copies ran while one was open for 10% of the time, Pallas kernels for 0%

commit v1 on v0

v1 whole, which is shorter than its diff:
```python
import functools
import math

import jax
import jax.numpy as jnp
from jax import lax
from jax.experimental import pallas as pl
from jax.experimental.pallas import tpu as pltpu
from jax.sharding import PartitionSpec as P

QUERY_HEADS = 8
KEY_VALUE_HEADS = 4
HEAD_SIZE = 256
PAIRED = QUERY_HEADS // KEY_VALUE_HEADS

eps_norm = 1e-06
soft_cap = 50.0
rope_base = 10000.0
gelu_coeff = math.sqrt(2.0 / math.pi)
f32 = jnp.float32
bf16 = jnp.bfloat16
VMEM_LIMIT = 56 * 1024 * 1024


def dot(a, b, dims):
    return lax.dot_general(a, b, (dims, ((), ())), preferred_element_type=f32)


NN = ((1,), (0,))
NT = ((1,), (1,))
TN = ((0,), (0,))


def inverse_powers(exponents):
    return 1.0 / jnp.left_shift(jnp.ones_like(exponents), exponents).astype(f32)


def norm_factor(values):
    return lax.rsqrt(jnp.mean(values * values, axis=-1, keepdims=True) + eps_norm)


def norm_back(values, factor, gain, grad):
    scaled = grad * gain
    inner = jnp.mean(values * scaled, axis=-1, keepdims=True)
    grad_values = factor * scaled - values * (factor * factor * factor * inner)
    return grad_values, jnp.sum(grad * values * factor, axis=0)


def gelu_parts(values):
    inner = gelu_coeff * (values + 0.044715 * values * values * values)
    return jnp.tanh(inner)


def rotary_rows(positions):
    half_dim = HEAD_SIZE // 2
    frequency = jnp.exp(
        jnp.arange(half_dim, dtype=f32) * (-2.0 * math.log(rope_base) / HEAD_SIZE)
    )
    angles = positions.astype(f32)[:, None] * frequency[None, :]
    return jnp.cos(angles)[:, None, :], jnp.sin(angles)[:, None, :]


def rotate(values, cosine, sine):
    half_dim = values.shape[-1] // 2
    a = values[..., :half_dim]
    b = values[..., half_dim:]
    return jnp.concatenate([a * cosine - b * sine, b * cosine + a * sine], axis=-1)


def ring_place(index, size):
    return jnp.where(index % 2 == 0, index // 2, size - 1 - index // 2)


def ring_index(place, size):
    return jnp.where(place < size // 2, 2 * place, 2 * (size - 1 - place) + 1)


def ring_perms(size):
    order = list(range(0, size, 2)) + list(range(size - 1, 0, -2))
    up = [(order[i], order[(i + 1) % size]) for i in range(size)]
    down = [(b, a) for a, b in up]
    return up, down


def ring_offsets(size):
    out = [0]
    for k in range(1, size // 2):
        out += [-k, k]
    return out + [size // 2]


def ring_gather(value, size):
    up, down = ring_perms(size)
    half = value.shape[0] // 2
    a = b = value
    out = [value]
    for _ in range(1, size // 2):
        a = lax.ppermute(a, "wide", up)
        b = lax.ppermute(b, "wide", down)
        out += [a, b]
    a = lax.ppermute(a[:half], "wide", up)
    b = lax.ppermute(b[half:], "wide", down)
    return out + [a, b]


def ring_scatter(part_of, rows, size):
    up, down = ring_perms(size)
    half = rows // 2
    far = part_of(size // 2)
    a = lax.ppermute(far[:half].astype(bf16), "wide", up)
    b = lax.ppermute(far[half:].astype(bf16), "wide", down)
    first = True
    for k in range(size // 2 - 1, 0, -1):
        own_a = part_of(k).astype(f32)
        own_b = part_of(-k).astype(f32)
        if first:
            a = jnp.concatenate([own_a[:half] + a.astype(f32), own_a[half:]], axis=0)
            b = jnp.concatenate([own_b[:half], own_b[half:] + b.astype(f32)], axis=0)
            first = False
        else:
            a = own_a + a.astype(f32)
            b = own_b + b.astype(f32)
        a = lax.ppermute(a.astype(bf16), "wide", up)
        b = lax.ppermute(b.astype(bf16), "wide", down)
    return part_of(0).astype(f32) + a.astype(f32) + b.astype(f32)


def swap(value, axis, bit):
    size = lax.axis_size(axis)
    return lax.ppermute(value, axis, [(i, i ^ bit) for i in range(size)])


def all_to_all(value):
    return lax.all_to_all(value, "wide", split_axis=0, concat_axis=0, tiled=True)


def slice_values(codes, width):
    add = jnp.where(width == 0, 0.0, jnp.where(width == 1, 8.0, 32.0)).astype(f32)
    inverse = jnp.where(width == 0, 1.0, jnp.where(width == 1, 1.0 / 16, 1.0 / 64)).astype(f32)
    step = jnp.where(width == 0, 1.0, jnp.where(width == 1, 16.0, 64.0)).astype(f32)
    top = jnp.where(width == 0, 127.0, jnp.where(width == 1, 112.0, 64.0)).astype(f32)
    low = jnp.where(width == 2, -128.0, -128.0).astype(f32)
    return jnp.maximum(jnp.minimum(jnp.floor((codes + add) * inverse) * step, top), low)


def attn_slice_kernel(places, info, own_ref, other_ref, col_ref, row_ref, *out_refs):
    mine = pl.program_id(1) == info[0]
    codes = jnp.where(mine, own_ref[0], other_ref[0]).astype(f32)
    scale = col_ref[...] * row_ref[...]
    for s, out_ref in enumerate(out_refs):
        out_ref[...] = (slice_values(codes, info[1 + s]) * scale).astype(bf16)


def attn_slices(own, other, places, info, col_scale, row_scale, count):
    blocks, rows, cols = own.shape
    grid_spec = pltpu.PrefetchScalarGridSpec(
        num_scalar_prefetch=2,
        grid=(blocks, 2),
        in_specs=[
            pl.BlockSpec((1, rows, cols), lambda k, j, p, i: (k, 0, 0)),
            pl.BlockSpec((1, rows, cols), lambda k, j, p, i: (k, 0, 0)),
            pl.BlockSpec((1, cols), lambda k, j, p, i: (0, j)),
            pl.BlockSpec((rows, 1), lambda k, j, p, i: (p[k], 0)),
        ],
        out_specs=[pl.BlockSpec((rows, cols), lambda k, j, p, i: (p[k], j))] * count,
    )
    return pl.pallas_call(
        attn_slice_kernel,
        grid_spec=grid_spec,
        out_shape=[jax.ShapeDtypeStruct((blocks * rows, 2 * cols), bf16)] * count,
        compiler_params=pltpu.CompilerParams(vmem_limit_bytes=VMEM_LIMIT),
        name="attn_slices",
    )(places, info, own, other, col_scale, row_scale)


def mlp_slice_kernel(info, code_ref, col_ref, row_ref, *out_refs):
    codes = code_ref[0].astype(f32)
    scale = col_ref[0] * row_ref[0]
    for s, out_ref in enumerate(out_refs):
        out_ref[0] = (slice_values(codes, info[1 + s]) * scale).astype(bf16)


def mlp_slices(codes, info, col_scale, row_scale, count):
    three, rows, cols = codes.shape
    block = 288 if rows % 288 == 0 else rows
    grid_spec = pltpu.PrefetchScalarGridSpec(
        num_scalar_prefetch=1,
        grid=(three, rows // block),
        in_specs=[
            pl.BlockSpec((1, block, cols), lambda k, j, i: (k, j, 0)),
            pl.BlockSpec((1, 1, cols), lambda k, j, i: (k, 0, 0)),
            pl.BlockSpec((1, block, 1), lambda k, j, i: (k, j, 0)),
        ],
        out_specs=[pl.BlockSpec((1, block, cols), lambda k, j, i: (k, j, 0))] * count,
    )
    return pl.pallas_call(
        mlp_slice_kernel,
        grid_spec=grid_spec,
        out_shape=[jax.ShapeDtypeStruct((three, rows, cols), bf16)] * count,
        compiler_params=pltpu.CompilerParams(vmem_limit_bytes=VMEM_LIMIT),
        name="mlp_slices",
    )(info, codes, col_scale, row_scale)


def tile_positions(tile, count, start, class_index, class_rows, rows):
    index = lax.broadcasted_iota(jnp.int32, (count, 1), 0)
    place = start + jnp.bitwise_and(index, tile - 1)
    shift = class_rows.bit_length() - 1
    return (
        jnp.right_shift(place, shift) * rows
        + class_index * class_rows
        + jnp.bitwise_and(place, class_rows - 1)
    )


def stack_heads(block):
    return jnp.concatenate(
        [block[:, j * HEAD_SIZE : (j + 1) * HEAD_SIZE] for j in range(PAIRED)], axis=0
    )


def key_ranges(start, tile, key_block, class_rows, rows):
    free = (start // class_rows) * rows // key_block
    last = (start + tile - 1) // class_rows
    total = ((last + 1) * rows + key_block - 1) // key_block
    return free, total


def attn_forward_kernel(
    info, q_ref, kv_ref, att_ref, exact_ref, lse_ref, *, tile, key_block, class_rows, rows
):
    start = pl.program_id(0) * tile
    free, total = key_ranges(start, tile, key_block, class_rows, rows)
    queries = stack_heads(q_ref[...])
    count = queries.shape[0]
    position = tile_positions(tile, count, start, info[0], class_rows, rows)

    def step(b, carry, masked):
        acc, row_sum = carry
        base = pl.multiple_of(b * key_block, key_block)
        keys = kv_ref[pl.ds(base, key_block), :HEAD_SIZE]
        values = kv_ref[pl.ds(base, key_block), HEAD_SIZE:]
        raw = dot(queries, keys, NT)
        weight = jnp.exp(soft_cap * jnp.tanh(raw * (1.0 / soft_cap)))
        if masked:
            key_place = base + lax.broadcasted_iota(jnp.int32, (1, key_block), 1)
            weight = jnp.where(key_place <= position, weight, 0.0)
        row_sum = row_sum + jnp.sum(weight, axis=-1, keepdims=True)
        acc = acc + dot(weight.astype(bf16), values, NN)
        return acc, row_sum

    carry = (jnp.zeros((count, HEAD_SIZE), f32), jnp.zeros((count, 1), f32))
    carry = lax.fori_loop(0, free, functools.partial(step, masked=False), carry)
    acc, row_sum = lax.fori_loop(free, total, functools.partial(step, masked=True), carry)
    exact = acc / row_sum
    lse = jnp.log(row_sum)
    for j in range(PAIRED):
        cols = slice(j * HEAD_SIZE, (j + 1) * HEAD_SIZE)
        exact_ref[:, cols] = exact[j * tile : (j + 1) * tile]
        att_ref[:, cols] = exact[j * tile : (j + 1) * tile].astype(bf16)
        lse_ref[:, j * 128 : (j + 1) * 128] = jnp.broadcast_to(
            lse[j * tile : (j + 1) * tile], (tile, 128)
        )


def attn_forward(info, queries, pairs, class_rows, rows):
    count, cols = queries.shape
    length = pairs.shape[0]
    tile = min(256, count)
    key_block = min(512, length)
    grid_spec = pltpu.PrefetchScalarGridSpec(
        num_scalar_prefetch=1,
        grid=(count // tile,),
        in_specs=[
            pl.BlockSpec((tile, cols), lambda i, c: (i, 0)),
            pl.BlockSpec((length, 2 * HEAD_SIZE), lambda i, c: (0, 0)),
        ],
        out_specs=[
            pl.BlockSpec((tile, cols), lambda i, c: (i, 0)),
            pl.BlockSpec((tile, cols), lambda i, c: (i, 0)),
            pl.BlockSpec((tile, PAIRED * 128), lambda i, c: (i, 0)),
        ],
    )
    return pl.pallas_call(
        functools.partial(
            attn_forward_kernel, tile=tile, key_block=key_block, class_rows=class_rows, rows=rows
        ),
        grid_spec=grid_spec,
        out_shape=[
            jax.ShapeDtypeStruct((count, cols), bf16),
            jax.ShapeDtypeStruct((count, cols), f32),
            jax.ShapeDtypeStruct((count, PAIRED * 128), f32),
        ],
        compiler_params=pltpu.CompilerParams(vmem_limit_bytes=VMEM_LIMIT),
        name="attn_forward",
    )(info, queries, pairs)


def attn_backward_kernel(
    info,
    q_ref,
    kv_ref,
    grad_ref,
    exact_ref,
    lse_ref,
    dq_ref,
    dkv_ref,
    sum_ref,
    *,
    tile,
    key_block,
    class_rows,
    rows,
):
    @pl.when(pl.program_id(0) == 0)
    def _():
        sum_ref[...] = jnp.zeros_like(sum_ref)

    start = pl.program_id(0) * tile
    free, total = key_ranges(start, tile, key_block, class_rows, rows)
    queries = stack_heads(q_ref[...])
    grads = stack_heads(grad_ref[...])
    count = queries.shape[0]
    delta = jnp.sum(grads.astype(f32) * stack_heads(exact_ref[...]), axis=-1, keepdims=True)
    lse = jnp.concatenate([lse_ref[:, j * 128 : j * 128 + 1] for j in range(PAIRED)], axis=0)
    position = tile_positions(tile, count, start, info[0], class_rows, rows)

    def step(b, acc, masked):
        base = pl.multiple_of(b * key_block, key_block)
        span = pl.ds(base, key_block)
        keys = kv_ref[span, :HEAD_SIZE]
        values = kv_ref[span, HEAD_SIZE:]
        bounded = jnp.tanh(dot(queries, keys, NT) * (1.0 / soft_cap))
        probs = jnp.exp(soft_cap * bounded - lse)
        if masked:
            key_place = base + lax.broadcasted_iota(jnp.int32, (1, key_block), 1)
            probs = jnp.where(key_place <= position, probs, 0.0)
        grad_probs = dot(grads, values, NT)
        grad_raw = (probs * (grad_probs - delta) * (1.0 - bounded * bounded)).astype(bf16)
        sum_ref[span, HEAD_SIZE:] += dot(probs.astype(bf16), grads, TN)
        sum_ref[span, :HEAD_SIZE] += dot(grad_raw, queries, TN)
        return acc + dot(grad_raw, keys, NN)

    acc = jnp.zeros((count, HEAD_SIZE), f32)
    acc = lax.fori_loop(0, free, functools.partial(step, masked=False), acc)
    acc = lax.fori_loop(free, total, functools.partial(step, masked=True), acc)
    for j in range(PAIRED):
        dq_ref[:, j * HEAD_SIZE : (j + 1) * HEAD_SIZE] = acc[j * tile : (j + 1) * tile].astype(bf16)

    @pl.when(pl.program_id(0) == pl.num_programs(0) - 1)
    def _():
        dkv_ref[...] = sum_ref[...].astype(bf16)


def attn_backward(info, queries, pairs, grads, exact, lse, class_rows, rows):
    count, cols = queries.shape
    length = pairs.shape[0]
    tile = min(256, count)
    key_block = min(512, length)
    row_spec = pl.BlockSpec((tile, cols), lambda i, c: (i, 0))
    whole_spec = pl.BlockSpec((length, 2 * HEAD_SIZE), lambda i, c: (0, 0))
    grid_spec = pltpu.PrefetchScalarGridSpec(
        num_scalar_prefetch=1,
        grid=(count // tile,),
        in_specs=[
            row_spec,
            whole_spec,
            row_spec,
            row_spec,
            pl.BlockSpec((tile, PAIRED * 128), lambda i, c: (i, 0)),
        ],
        out_specs=[row_spec, whole_spec],
        scratch_shapes=[pltpu.VMEM((length, 2 * HEAD_SIZE), f32)],
    )
    return pl.pallas_call(
        functools.partial(
            attn_backward_kernel, tile=tile, key_block=key_block, class_rows=class_rows, rows=rows
        ),
        grid_spec=grid_spec,
        out_shape=[
            jax.ShapeDtypeStruct((count, cols), bf16),
            jax.ShapeDtypeStruct((length, 2 * HEAD_SIZE), bf16),
        ],
        compiler_params=pltpu.CompilerParams(vmem_limit_bytes=VMEM_LIMIT),
        name="attn_backward",
    )(info, queries, pairs, grads, exact, lse)


def per_device(
    tokens,
    cotangent,
    widths,
    attn_codes,
    attn_exps,
    out_exps,
    mlp_codes,
    gate_exps,
    down_exps,
    gain_attn,
    gain_post_attn,
    gain_mlp,
    gain_post_mlp,
):
    wide = lax.axis_size("wide")
    seq_size = lax.axis_size("seq")
    wide_index = lax.axis_index("wide")
    side = lax.axis_index("seq") % 2
    is_low = side == 0
    place = ring_place(wide_index, wide)
    count, rows, model_dim = tokens.shape
    length = rows * wide
    classes = wide // KEY_VALUE_HEADS
    class_rows = rows // classes
    class_index = wide_index % classes
    query_cols = QUERY_HEADS * HEAD_SIZE
    key_cols = KEY_VALUE_HEADS * HEAD_SIZE
    head_cols = PAIRED * HEAD_SIZE
    proj_cols = attn_exps.shape[0]
    half_proj = proj_cols // 2
    half_out = (attn_codes.shape[1] - proj_cols) // 2
    query_scale = HEAD_SIZE ** (-0.5)
    attn_rows = attn_codes.shape[0]
    hidden = mlp_codes.shape[1]
    offsets = ring_offsets(wide)
    seqs = range(count)

    def index_at(offset):
        return ring_index(jnp.mod(place + offset, wide), wide)

    places = jnp.stack([index_at(o) for o in offsets]).astype(jnp.int32)
    info = jnp.concatenate([side[None].astype(jnp.int32), widths])
    class_info = class_index[None].astype(jnp.int32)

    def gather_columns(first, size):
        mine = lax.dynamic_slice_in_dim(attn_codes, first + side * size, size, 1).astype(bf16)
        own = jnp.concatenate(ring_gather(mine, wide), axis=0)
        own = own.reshape(wide, attn_rows, size)
        return own, swap(own, "seq", 1)

    column_scale = inverse_powers(attn_exps)[None, :]
    output_scale = inverse_powers(out_exps)[:, None]
    proj_own, proj_other = gather_columns(0, half_proj)
    proj_weights = attn_slices(
        proj_own,
        proj_other,
        places,
        info,
        column_scale,
        jnp.ones((model_dim, 1), f32),
        count,
    )
    out_own, out_other = gather_columns(proj_cols, half_out)
    out_weights = attn_slices(
        out_own,
        out_other,
        places,
        info,
        jnp.ones((1, 2 * half_out), f32),
        output_scale,
        count,
    )
    own_gate_scale = lax.dynamic_slice_in_dim(
        inverse_powers(gate_exps), wide_index * hidden, hidden, 1
    )
    down_scale = inverse_powers(down_exps)
    mlp_weights = mlp_slices(
        mlp_codes,
        info,
        jnp.concatenate([jnp.ones((2, 1, model_dim), f32), down_scale[None, None]], axis=0),
        jnp.concatenate([own_gate_scale, jnp.ones((1, hidden), f32)], axis=0)[:, :, None],
        count,
    )
    pair_weights = [w[:2].reshape(2 * hidden, model_dim) for w in mlp_weights]
    down_weights = [w[2] for w in mlp_weights]

    cosine, sine = rotary_rows(wide_index * rows + jnp.arange(rows))

    def rows_to_heads(values):
        split = values.reshape(classes, class_rows, KEY_VALUE_HEADS, head_cols)
        return jnp.transpose(split, (2, 0, 1, 3)).reshape(wide, class_rows, head_cols)

    def heads_to_rows(blocks):
        split = blocks.reshape(KEY_VALUE_HEADS, classes, class_rows, head_cols)
        return jnp.transpose(split, (1, 2, 0, 3)).reshape(rows, KEY_VALUE_HEADS * head_cols)

    inputs = [tokens[s].astype(f32) for s in seqs]
    grad_out = [cotangent[s].astype(f32) for s in seqs]
    input_factor = [norm_factor(v) for v in inputs]
    normed = [(inputs[s] * input_factor[s] * gain_attn).astype(bf16) for s in seqs]

    queries, pairs = [], []
    for s in seqs:
        projected = dot(normed[s], proj_weights[s], NN)
        query = rotate(
            projected[:, :query_cols].reshape(rows, QUERY_HEADS, HEAD_SIZE), cosine, sine
        )
        query = (query * query_scale).astype(bf16).reshape(rows, query_cols)
        key = rotate(
            projected[:, query_cols : query_cols + key_cols].reshape(
                rows, KEY_VALUE_HEADS, HEAD_SIZE
            ),
            cosine,
            sine,
        ).astype(bf16)
        value = (
            projected[:, query_cols + key_cols :]
            .reshape(rows, KEY_VALUE_HEADS, HEAD_SIZE)
            .astype(bf16)
        )
        pair = jnp.transpose(jnp.concatenate([key, value], axis=-1), (1, 0, 2))
        pair = jnp.broadcast_to(
            pair[:, None], (KEY_VALUE_HEADS, classes, rows, 2 * HEAD_SIZE)
        ).reshape(wide, rows, 2 * HEAD_SIZE)
        queries.append(all_to_all(rows_to_heads(query)).reshape(wide * class_rows, head_cols))
        pairs.append(all_to_all(pair).reshape(length, 2 * HEAD_SIZE))

    attended, exact, lse = [], [], []
    for s in seqs:
        out, full, log_sum = attn_forward(class_info, queries[s], pairs[s], class_rows, rows)
        exact.append(full)
        lse.append(log_sum)
        back = all_to_all(out.reshape(wide, class_rows, head_cols))
        attended.append(heads_to_rows(back))

    branch, branch_factor, middle, middle_factor, normed_mlp = [], [], [], [], []
    for s in seqs:
        value = dot(attended[s], out_weights[s], NT)
        factor = norm_factor(value)
        mid = inputs[s] + value * factor * gain_post_attn
        mid_factor = norm_factor(mid)
        branch.append(value)
        branch_factor.append(factor)
        middle.append(mid)
        middle_factor.append(mid_factor)
        normed_mlp.append((mid * mid_factor * gain_mlp).astype(bf16))

    gathered, gate, up, tanh_gate, hidden_rows, mixed = [], [], [], [], [], []
    for s in seqs:
        group = jnp.concatenate(ring_gather(normed_mlp[s], wide), axis=0)
        both = dot(group, pair_weights[s], NT)
        gate_s, up_s = both[:, :hidden], both[:, hidden:]
        bounded = gelu_parts(gate_s)
        hidden_s = (0.5 * gate_s * (1.0 + bounded) * up_s).astype(bf16)
        part = dot(hidden_s, down_weights[s], NN).astype(bf16)
        order = {o: i for i, o in enumerate(offsets)}
        mixed.append(
            ring_scatter(
                lambda o, part=part: part[order[o] * rows : (order[o] + 1) * rows], rows, wide
            )
        )
        gathered.append(group)
        gate.append(gate_s)
        up.append(up_s)
        hidden_rows.append(hidden_s)

    layer_out, grad_mixed, gain_fourth = [], [], 0.0
    for s in seqs:
        factor = norm_factor(mixed[s])
        layer_out.append((middle[s] + mixed[s] * factor * gain_post_mlp).astype(bf16))
        grad, gain = norm_back(mixed[s], factor, gain_post_mlp, grad_out[s])
        grad_mixed.append(grad.astype(bf16))
        gain_fourth = gain_fourth + gain

    grad_group, grad_pair, grad_normed_mlp = [], [], []
    for s in seqs:
        group = jnp.concatenate(ring_gather(grad_mixed[s], wide), axis=0)
        grad_hidden = dot(group, down_weights[s], NT)
        bounded = gelu_parts(gate[s])
        gelu_value = 0.5 * gate[s] * (1.0 + bounded)
        slope = 0.5 * (1.0 + bounded) + 0.5 * gate[s] * (1.0 - bounded * bounded) * gelu_coeff * (
            1.0 + 3.0 * 0.044715 * gate[s] * gate[s]
        )
        pair = jnp.concatenate(
            [
                (grad_hidden * up[s] * slope).astype(bf16),
                (grad_hidden * gelu_value).astype(bf16),
            ],
            axis=1,
        )
        part = dot(pair, pair_weights[s], NN).astype(bf16)
        order = {o: i for i, o in enumerate(offsets)}
        grad_normed_mlp.append(
            ring_scatter(
                lambda o, part=part: part[order[o] * rows : (order[o] + 1) * rows], rows, wide
            )
        )
        grad_group.append(group)
        grad_pair.append(pair)

    pair_term = sum(dot(grad_pair[s], gathered[s], TN) for s in seqs)
    down_term = sum(dot(hidden_rows[s], grad_group[s], TN) for s in seqs)
    half_hidden = hidden // 2
    mlp_part = jnp.concatenate(
        [pair_term.reshape(2, hidden, model_dim).astype(bf16), down_term[None].astype(bf16)], axis=0
    )
    keep = lax.dynamic_slice_in_dim(mlp_part, side * half_hidden, half_hidden, 1)
    send = lax.dynamic_slice_in_dim(mlp_part, (1 - side) * half_hidden, half_hidden, 1)
    total = keep.astype(f32) + swap(send, "seq", 1).astype(f32)
    bit = 2
    while bit < seq_size:
        low = total.astype(bf16)
        total = low.astype(f32) + swap(low, "seq", bit).astype(f32)
        bit *= 2
    low = total.astype(bf16)
    other = swap(low, "seq", 1)
    mlp_grad = jnp.concatenate(
        [jnp.where(is_low, low, other).astype(f32), jnp.where(is_low, other, low).astype(f32)],
        axis=1,
    )

    grad_middle, grad_branch, grad_heads = [], [], []
    gain_third = gain_second = 0.0
    for s in seqs:
        grad, gain = norm_back(middle[s], middle_factor[s], gain_mlp, grad_normed_mlp[s])
        gain_third = gain_third + gain
        grad_mid = grad_out[s] + grad
        grad_middle.append(grad_mid)
        grad, gain = norm_back(branch[s], branch_factor[s], gain_post_attn, grad_mid)
        gain_second = gain_second + gain
        grad_branch.append(grad.astype(bf16))
        grad_attended = dot(grad_branch[s], out_weights[s], NN).astype(bf16)
        grad_heads.append(
            all_to_all(rows_to_heads(grad_attended)).reshape(wide * class_rows, head_cols)
        )

    grad_query, grad_key_value = [], []
    for s in seqs:
        dq, dkv = attn_backward(
            class_info, queries[s], pairs[s], grad_heads[s], exact[s], lse[s], class_rows, rows
        )
        dq = heads_to_rows(all_to_all(dq.reshape(wide, class_rows, head_cols)))
        dq = rotate(
            dq.astype(f32).reshape(rows, QUERY_HEADS, HEAD_SIZE) * query_scale, cosine, -sine
        )
        dkv = all_to_all(dkv.reshape(wide, rows, 2 * HEAD_SIZE)).reshape(
            KEY_VALUE_HEADS, classes, rows, 2 * HEAD_SIZE
        )
        dkv = jnp.transpose(jnp.sum(dkv.astype(f32), axis=1), (1, 0, 2))
        dk = rotate(dkv[..., :HEAD_SIZE], cosine, -sine)
        grad_query.append(dq.reshape(rows, query_cols).astype(bf16))
        grad_key_value.append(
            jnp.concatenate(
                [dk.reshape(rows, key_cols), dkv[..., HEAD_SIZE:].reshape(rows, key_cols)], axis=1
            ).astype(bf16)
        )

    grad_tokens, gain_first = [], 0.0
    for s in seqs:
        grad_proj = jnp.concatenate([grad_query[s], grad_key_value[s]], axis=1)
        grad_normed = dot(grad_proj, proj_weights[s], NT)
        grad, gain = norm_back(inputs[s], input_factor[s], gain_attn, grad_normed)
        gain_first = gain_first + gain
        grad_tokens.append((grad_middle[s] + grad).astype(bf16))

    def scatter_columns(left, first_half, second_half):
        keep = jnp.where(is_low, first_half, second_half)
        send = jnp.where(is_low, second_half, first_half)
        received = swap(dot(left, send, TN).astype(bf16), "seq", 1)
        part = (dot(left, keep, TN) + received.astype(f32)).astype(bf16)
        own = ring_scatter(
            lambda o: lax.dynamic_slice_in_dim(part, index_at(o) * attn_rows, attn_rows, 0),
            attn_rows,
            wide,
        )
        bit = 2
        while bit < seq_size:
            low = own.astype(bf16)
            own = low.astype(f32) + swap(low, "seq", bit).astype(f32)
            bit *= 2
        low = own.astype(bf16)
        other = swap(low, "seq", 1)
        return [
            jnp.where(is_low, low, other).astype(f32),
            jnp.where(is_low, other, low).astype(f32),
        ]

    all_attended = jnp.concatenate(attended, axis=0)
    out_parts = scatter_columns(
        jnp.concatenate(grad_branch, axis=0), all_attended[:, :half_out], all_attended[:, half_out:]
    )
    proj_parts = scatter_columns(
        jnp.concatenate(normed, axis=0),
        jnp.concatenate(grad_query, axis=0),
        jnp.concatenate(grad_key_value, axis=0),
    )
    attn_grad = jnp.concatenate(proj_parts + out_parts, axis=1)

    gains = jnp.stack([gain_first, gain_second, gain_third, gain_fourth])
    for axis, size in (("seq", seq_size), ("wide", wide)):
        bit = 1
        while bit < size:
            gains = gains + swap(gains, axis, bit)
            bit *= 2
    return (
        jnp.stack(layer_out),
        jnp.stack(grad_tokens),
        attn_grad,
        mlp_grad,
        gains[0],
        gains[1],
        gains[2],
        gains[3],
    )


def solution(mesh):
    placed = (
        P("seq", "wide", None),
        P("seq", "wide", None),
        P("seq"),
        P("wide", None),
        P(),
        P(),
        P(None, "wide", None),
        P(),
        P(),
        P(),
        P(),
        P(),
        P(),
    )
    return jax.shard_map(
        per_device,
        mesh=mesh,
        in_specs=placed,
        out_specs=(
            P("seq", "wide", None),
            P("seq", "wide", None),
            P("wide", None),
            P(None, "wide", None),
            P(),
            P(),
            P(),
            P(),
        ),
        check_vma=False,
    )
```

time: 3980 us -> 2160 us (0.54)
  waiting for transfers between devices: 2620 us -> 1070 us
  other arithmetic: 608 us -> 148 us
  Pallas kernels: 0 us -> 181 us
  starting transfers between devices: 28.3 us -> 199 us
  matrix products: 548 us -> 398 us
  local copies, waits for them, and re-layouts: 111 us -> 158 us
  blocking collectives: 41.8 us -> 0 us
    all_gather x3 -> x0, waiting for transfers between devices: 1130 us -> none  [the longest x1 539 us: per_device(): attn_full = lax.all_gather(attn_send, 'wide', axis=0, tiled=True)]
    reduce_scatter x3 -> x0, waiting for transfers between devices: 976 us -> none  [the longest x1 349 us: per_device(): lax.psum_scatter(jnp.concatenate([projection_term, output_term], axis=1)....]
    ppermute x0 -> x112, waiting for transfers between devices: none -> 972 us  [the longest x18 272 us: ring_gather(): a = lax.ppermute(a, 'wide', up)]
    psum x1 -> x0, waiting for transfers between devices: 266 us -> none  [per_device(): lax.psum(attn_part, 'seq').astype(jnp.float32)]
    convert_element_type x17 -> x31, other arithmetic: 246 us -> 59.2 us  [the longest x2 18.1 us: per_device(): low = total.astype(bf16)]
    mul x5 -> x9, other arithmetic: 187 us -> 1.83 us  [the longest x2 1.77 us: per_device(): dq.astype(f32).reshape(rows, QUERY_HEADS, HEAD_SIZE) * query_scale]
    pallas_call x0 -> x7, Pallas kernels: none -> 181 us  [the longest x2 77.3 us: attn_slices(): pl.pallas_call(attn_slice_kernel, grid_spec=grid_spec, out_shape=[jax.Sha...]
    dot_general x18 -> x24, matrix products: 548 us -> 398 us  [dot(): return lax.dot_general(a, b, (dims, ((), ())), preferred_element_type=f32)]
  transfers between devices with their start and end apart: 13 -> 124, of which waited for: 12 -> 61; matrix products, arithmetic and copies ran while one was open for 10% -> 26% of each run, Pallas kernels for 0% -> 6%
where the time goes in v1:
time: 2160 us
  waiting for transfers between devices  1070 us (50%)
  matrix products  398 us (18%)
  starting transfers between devices  199 us (9%)
  Pallas kernels  181 us (8%)
  local copies, waits for them, and re-layouts  158 us (7%)
  other arithmetic  148 us (7%)
    dot_general x24, matrix products, dot(): return lax.dot_general(a, b, (dims, ((), ())), preferred_element_type=f32)  398 us
    ppermute x18, waiting for transfers between devices, ring_gather(): a = lax.ppermute(a, 'wide', up)  272 us
    ppermute x18, waiting for transfers between devices, ring_scatter(): a = lax.ppermute(a.astype(bf16), 'wide', up)  205 us
    ppermute x16, waiting for transfers between devices, swap(): return lax.ppermute(value, axis, [(i, i ^ bit) for i in range(size)])  192 us
    ppermute x18, waiting for transfers between devices, ring_scatter(): b = lax.ppermute(b.astype(bf16), 'wide', down)  140 us
    all_to_all x12, waiting for transfers between devices, all_to_all(): lax.all_to_all(value, 'wide', split_axis=0, concat_axis=0, tiled=True)  99.4 us
    ppermute x18, waiting for transfers between devices, ring_gather(): b = lax.ppermute(b, 'wide', down)  95.8 us
    pallas_call x2, Pallas kernels, attn_slices(): pl.pallas_call(attn_slice_kernel, grid_spec=grid_spec, out_shape=[jax.Sha...  77.3 us
  transfers between devices with their start and end apart: 124, of which 61 were waited for; matrix products, arithmetic and copies ran while one was open for 26% of the time, Pallas kernels for 6%

profile of v1, /device:TPU:0, one launch (start us, length us, event | category | flops | bytes accessed | tf_op | source)
XLA Modules:
  0.0 2158.6 jit_solution(10578685619491476728)
XLA Ops:
  6.6 25.9 %collective-permute-done = bf16[288,2048]{1,0:T(8,128)(2,1)S(1)} collective-permute-done((bf16[288,2048]{1,0:T(8,128)(2,1)S(1)}, bf16[288,2048]{1,0:T(8,128)(2,1)S(1)}, u32[]{:S(2)}, u32[]{:S(2)}) %collective-permute-start) | collective-permute-done | bytes 1179680 | tf_op jit(solution)/shard_map/ppermute | solution.py:98
  34.5 25.1 %collective-permute-done.2 = bf16[288,2048]{1,0:T(8,128)(2,1)S(1)} collective-permute-done((bf16[288,2048]{1,0:T(8,128)(2,1)S(1)}, bf16[288,2048]{1,0:T(8,128)(2,1)S(1)}, u32[]{:S(2)}, u32[]{:S(2)}) %collective-permute-start.2) | collective-permute-done | bytes 1179680 | tf_op jit(solution)/shard_map/ppermute | solution.py:98
  65.0 20.8 collective-permute-done.4
  117.4 51.1 %attn_slices.2 = (bf16[2304,4096]{1,0:T(8,128)(2,1)}, bf16[2304,4096]{1,0:T(8,128)(2,1)}) custom-call(s32[8]{0:T(128)} %stack.60.places, s32[3]{0:T(128)} %pad_add_fusion.info, bf16[8,288,2048]{2,1,0:T(8,128)(2,1)} %bitcast.12.own_ref, bf16[8,288,2048]{2,1,0:T(8,128)(2,1)} %collective-permute-done.8.other_ref, f32[1,4096]{1,0:T(1,128)} %bitcast.229, ...), custom_call_target="tpu_custom_call" | custom-call | tf_op jit(solution)/shard_map/attn_slices/pallas_call | solution.py:167
  209.9 18.4 all-to-all-done
  268.7 41.8 %collective-permute-done.9 = bf16[288,1024]{1,0:T(8,128)(2,1)} collective-permute-done((bf16[288,1024]{1,0:T(8,128)(2,1)S(1)}, bf16[288,1024]{1,0:T(8,128)(2,1)}, u32[]{:S(2)}, u32[]{:S(2)}) %collective-permute-start.9) | collective-permute-done | bytes 589856 | tf_op jit(solution)/shard_map/ppermute | solution.py:98
  351.6 33.0 %collective-permute-done.13 = bf16[288,1024]{1,0:T(8,128)(2,1)S(1)} collective-permute-done((bf16[288,1024]{1,0:T(8,128)(2,1)}, bf16[288,1024]{1,0:T(8,128)(2,1)S(1)}, u32[]{:S(2)}, u32[]{:S(2)}) %collective-permute-start.13) | collective-permute-done | bytes 589856 | tf_op jit(solution)/shard_map/ppermute | solution.py:98
  456.3 26.3 %attn_slices.3 = (bf16[2304,2048]{1,0:T(8,128)(2,1)}, bf16[2304,2048]{1,0:T(8,128)(2,1)}) custom-call(s32[8]{0:T(128)} %stack.60.places, s32[3]{0:T(128)} %pad_add_fusion.info, bf16[8,288,1024]{2,1,0:T(8,128)(2,1)} %bitcast.191, bf16[8,288,1024]{2,1,0:T(8,128)(2,1)} %collective-permute-done.17.other_ref, f32[1,2048]{1,0:T(1,128)} %broadcast_in_dim.30.col_ref, ...), custom_call_target="tpu_custom_call" | custom-call | tf_op jit(solution)/shard_map/attn_slices/pallas_call | solution.py:167
  515.2 45.6 %mlp_slices.1 = (bf16[3,1152,2304]{2,1,0:T(8,128)(2,1)}, bf16[3,1152,2304]{2,1,0:T(8,128)(2,1)}) custom-call(s32[3]{0:T(128)} %pad_add_fusion.info, s32[3,1152,2304]{2,1,0:T(8,128)} %code_ref.1, f32[3,1,2304]{2,1,0:T(1,128)} %concatenate.167.col_ref, f32[3,1152,1]{2,1,0:T(8,128)} %copy.95.row_ref), custom_call_target="tpu_custom_call" | custom-call | tf_op jit(solution)/shard_map/mlp_slices/pallas_call | solution.py:196
  584.1 19.3 collective-permute-done.21
  605.4 25.0 %collective-permute-done.36 = bf16[256,2304]{1,0:T(8,128)(2,1)S(1)} collective-permute-done((bf16[256,2304]{1,0:T(8,128)(2,1)S(1)}, bf16[256,2304]{1,0:T(8,128)(2,1)S(1)}, u32[]{:S(2)}, u32[]{:S(2)}) %collective-permute-start.36) | collective-permute-done | bytes 1179680 | tf_op jit(solution)/shard_map/ppermute | solution.py:98
  636.9 17.0 collective-permute-done.23
  656.2 24.8 %collective-permute-done.38 = bf16[256,2304]{1,0:T(8,128)(2,1)S(1)} collective-permute-done((bf16[256,2304]{1,0:T(8,128)(2,1)S(1)}, bf16[256,2304]{1,0:T(8,128)(2,1)S(1)}, u32[]{:S(2)}, u32[]{:S(2)}) %collective-permute-start.38) | collective-permute-done | bytes 1179680 | tf_op jit(solution)/shard_map/ppermute | solution.py:98
  705.1 26.9 %fusion.129 = f32[2048,2304]{1,0:T(8,128)} fusion(bf16[2048,2304]{1,0:T(8,128)(2,1)} %constant_dynamic-update-slice_fusion.27, bf16[2304,2304]{1,0:T(8,128)(2,1)S(1)} %bitcast.172), kind=kOutput, calls=%fused_computation.392 | convolution fusion | flops 21743271936 | bytes 38928384 | tf_op jit(solution)/shard_map/dot_general | solution.py:26
  760.0 30.4 %fusion.127 = f32[2048,2304]{1,0:T(8,128)} fusion(bf16[2048,2304]{1,0:T(8,128)(2,1)} %constant_dynamic-update-slice_fusion.18, bf16[2304,2304]{1,0:T(8,128)(2,1)} %bitcast.174), kind=kOutput, calls=%fused_computation.390 | convolution fusion | flops 21743271936 | bytes 38928384 | tf_op jit(solution)/shard_map/dot_general | solution.py:26
  800.6 17.0 convolution_convert_fusion.4
  838.7 22.5 %collective-permute-done.43 = bf16[256,2304]{1,0:T(8,128)(2,1)S(1)} collective-permute-done((bf16[256,2304]{1,0:T(8,128)(2,1)S(1)}, bf16[256,2304]{1,0:T(8,128)(2,1)S(1)}, u32[]{:S(2)}, u32[]{:S(2)}) %collective-permute-start.43) | collective-permute-done | bytes 1179680 | tf_op jit(solution)/shard_map/ppermute | solution.py:123
  863.7 22.7 %collective-permute-done.27 = bf16[256,2304]{1,0:T(8,128)(2,1)S(1)} collective-permute-done((bf16[256,2304]{1,0:T(8,128)(2,1)S(1)}, bf16[256,2304]{1,0:T(8,128)(2,1)S(1)}, u32[]{:S(2)}, u32[]{:S(2)}) %collective-permute-start.27) | collective-permute-done | bytes 1179680 | tf_op jit(solution)/shard_map/ppermute | solution.py:123
  887.1 24.6 %collective-permute-done.44 = bf16[256,2304]{1,0:T(8,128)(2,1)S(1)} collective-permute-done((bf16[256,2304]{1,0:T(8,128)(2,1)S(1)}, bf16[256,2304]{1,0:T(8,128)(2,1)S(1)}, u32[]{:S(2)}, u32[]{:S(2)}) %collective-permute-start.44) | collective-permute-done | bytes 1179680 | tf_op jit(solution)/shard_map/ppermute | solution.py:123
  913.8 18.7 collective-permute-done.28
  937.6 24.5 %collective-permute-done.32 = bf16[256,2304]{1,0:T(8,128)(2,1)S(1)} collective-permute-done((bf16[256,2304]{1,0:T(8,128)(2,1)S(1)}, bf16[256,2304]{1,0:T(8,128)(2,1)S(1)}, u32[]{:S(2)}, u32[]{:S(2)}) %collective-permute-start.32) | collective-permute-done | bytes 1179680 | tf_op jit(solution)/shard_map/ppermute | solution.py:124
  963.9 23.5 %collective-permute-done.49 = bf16[256,2304]{1,0:T(8,128)(2,1)S(1)} collective-permute-done((bf16[256,2304]{1,0:T(8,128)(2,1)S(1)}, bf16[256,2304]{1,0:T(8,128)(2,1)S(1)}, u32[]{:S(2)}, u32[]{:S(2)}) %collective-permute-start.49) | collective-permute-done | bytes 1179680 | tf_op jit(solution)/shard_map/ppermute | solution.py:124
  988.0 19.2 collective-permute-done.33
  1019.6 24.9 %collective-permute-done.51 = bf16[256,2304]{1,0:T(8,128)(2,1)S(1)} collective-permute-done((bf16[256,2304]{1,0:T(8,128)(2,1)S(1)}, bf16[256,2304]{1,0:T(8,128)(2,1)S(1)}, u32[]{:S(2)}, u32[]{:S(2)}) %collective-permute-start.51) | collective-permute-done | bytes 1179680 | tf_op jit(solution)/shard_map/ppermute | solution.py:99
  1046.5 24.7 %collective-permute-done.66 = bf16[256,2304]{1,0:T(8,128)(2,1)S(1)} collective-permute-done((bf16[256,2304]{1,0:T(8,128)(2,1)S(1)}, bf16[256,2304]{1,0:T(8,128)(2,1)S(1)}, u32[]{:S(2)}, u32[]{:S(2)}) %collective-permute-start.66) | collective-permute-done | bytes 1179680 | tf_op jit(solution)/shard_map/ppermute | solution.py:98
  1077.7 17.3 collective-permute-done.53
  1097.0 24.7 %collective-permute-done.68 = bf16[256,2304]{1,0:T(8,128)(2,1)S(1)} collective-permute-done((bf16[256,2304]{1,0:T(8,128)(2,1)S(1)}, bf16[256,2304]{1,0:T(8,128)(2,1)S(1)}, u32[]{:S(2)}, u32[]{:S(2)}) %collective-permute-start.68) | collective-permute-done | bytes 1179680 | tf_op jit(solution)/shard_map/ppermute | solution.py:98
  1128.3 17.3 collective-permute-done.55
  1147.8 24.5 %collective-permute-done.70 = bf16[256,2304]{1,0:T(8,128)(2,1)S(1)} collective-permute-done((bf16[256,2304]{1,0:T(8,128)(2,1)S(1)}, bf16[256,2304]{1,0:T(8,128)(2,1)S(1)}, u32[]{:S(2)}, u32[]{:S(2)}) %collective-permute-start.70) | collective-permute-done | bytes 1179680 | tf_op jit(solution)/shard_map/ppermute | solution.py:98
  1186.5 28.6 %fusion.11 = (bf16[2048,1152]{1,0:T(8,128)(2,1)}, bf16[2048,1152]{1,0:T(8,128)(2,1)}) fusion(f32[2048,2304]{1,0:T(8,128)} %fusion.127, bf16[2048,2304]{1,0:T(8,128)(2,1)} %constant_dynamic-update-slice_fusion.36, bf16[3,1152,2304]{2,1,0:T(8,128)(2,1)} %get-tuple-element.27), kind=kOutput, calls=%fused_computation.30 | convolution fusion | flops 10925899776 | bytes 43057152 | tf_op jit(solution)/shard_map/dot_general | solution.py:26
  1216.9 28.9 %fusion.16 = (bf16[2048,1152]{1,0:T(8,128)(2,1)}, bf16[2048,1152]{1,0:T(8,128)(2,1)}) fusion(f32[2048,2304]{1,0:T(8,128)} %fusion.129, bf16[2048,2304]{1,0:T(8,128)(2,1)} %constant_dynamic-update-slice_fusion.45, bf16[3,1152,2304]{2,1,0:T(8,128)(2,1)} %get-tuple-element.31), kind=kOutput, calls=%fused_computation.35 | convolution fusion | flops 10925899776 | bytes 43057152 | tf_op jit(solution)/shard_map/dot_general | solution.py:26
  1245.8 27.4 %convolution_convert_fusion.1 = bf16[2048,2304]{1,0:T(8,128)(2,1)S(1)} fusion(bf16[2304,2304]{1,0:T(8,128)(2,1)} %bitcast.175, bf16[2048,1152]{1,0:T(8,128)(2,1)} %get-tuple-element.85, bf16[2048,1152]{1,0:T(8,128)(2,1)} %get-tuple-element.84), kind=kOutput, calls=%fused_computation.16 | convolution fusion | flops 21766864896 | bytes 29491200 | tf_op jit(solution)/shard_map/dot_general | solution.py:26
  1275.5 27.6 %convolution_convert_fusion = bf16[2048,2304]{1,0:T(8,128)(2,1)S(1)} fusion(bf16[2304,2304]{1,0:T(8,128)(2,1)} %bitcast.173, bf16[2048,1152]{1,0:T(8,128)(2,1)} %get-tuple-element.87, bf16[2048,1152]{1,0:T(8,128)(2,1)} %get-tuple-element.86), kind=kOutput, calls=%fused_computation.15 | convolution fusion | flops 21766864896 | bytes 29491200 | tf_op jit(solution)/shard_map/dot_general | solution.py:26
  1322.7 22.1 %collective-permute-done.59 = bf16[256,2304]{1,0:T(8,128)(2,1)S(1)} collective-permute-done((bf16[256,2304]{1,0:T(8,128)(2,1)S(1)}, bf16[256,2304]{1,0:T(8,128)(2,1)S(1)}, u32[]{:S(2)}, u32[]{:S(2)}) %collective-permute-start.59) | collective-permute-done | bytes 1179680 | tf_op jit(solution)/shard_map/ppermute | solution.py:123
  1347.4 22.7 %collective-permute-done.75 = bf16[256,2304]{1,0:T(8,128)(2,1)S(1)} collective-permute-done((bf16[256,2304]{1,0:T(8,128)(2,1)S(1)}, bf16[256,2304]{1,0:T(8,128)(2,1)S(1)}, u32[]{:S(2)}, u32[]{:S(2)}) %collective-permute-start.75) | collective-permute-done | bytes 1179680 | tf_op jit(solution)/shard_map/ppermute | solution.py:123
  1371.0 22.6 %collective-permute-done.60 = bf16[256,2304]{1,0:T(8,128)(2,1)S(1)} collective-permute-done((bf16[256,2304]{1,0:T(8,128)(2,1)S(1)}, bf16[256,2304]{1,0:T(8,128)(2,1)S(1)}, u32[]{:S(2)}, u32[]{:S(2)}) %collective-permute-start.60) | collective-permute-done | bytes 1179680 | tf_op jit(solution)/shard_map/ppermute | solution.py:123
  1395.9 20.1 collective-permute-done.76
  1425.2 23.4 %collective-permute-done.80 = bf16[256,2304]{1,0:T(8,128)(2,1)S(1)} collective-permute-done((bf16[256,2304]{1,0:T(8,128)(2,1)S(1)}, bf16[256,2304]{1,0:T(8,128)(2,1)S(1)}, u32[]{:S(2)}, u32[]{:S(2)}) %collective-permute-start.80) | collective-permute-done | bytes 1179680 | tf_op jit(solution)/shard_map/ppermute | solution.py:124
  1536.0 29.6 %fusion.19 = f32[2304,2304]{1,0:T(8,128)} fusion(bf16[2048,2304]{1,0:T(8,128)(2,1)} %constant_dynamic-update-slice_fusion.27, bf16[2048,1152]{1,0:T(8,128)(2,1)} %get-tuple-element.87, bf16[2048,1152]{1,0:T(8,128)(2,1)} %get-tuple-element.86), kind=kOutput, calls=%fused_computation.49 | convolution fusion | flops 21762146304 | bytes 40108032 | tf_op jit(solution)/shard_map/dot_general | solution.py:26
  1565.6 17.4 attn_backward.3
  1589.3 31.4 %fusion = bf16[2304,2304]{1,0:T(8,128)(2,1)} fusion(f32[2304,2304]{1,0:T(8,128)} %fusion.19, bf16[2048,2304]{1,0:T(8,128)(2,1)} %constant_dynamic-update-slice_fusion.18, bf16[2048,1152]{1,0:T(8,128)(2,1)} %get-tuple-element.85, bf16[2048,1152]{1,0:T(8,128)(2,1)} %get-tuple-element.84), kind=kOutput, calls=%fused_computation.4 | convolution fusion | flops 21772763136 | bytes 50724864 | tf_op jit(solution)/shard_map/dot_general | solution.py:26
  1620.7 17.4 attn_backward.2
  1734.0 25.7 %all-to-all-done.11 = bf16[8,256,512]{2,1,0:T(8,128)(2,1)} async-done(((bf16[8,256,512]{2,1,0:T(8,128)(2,1)}), bf16[8,256,512]{2,1,0:T(8,128)(2,1)}, u32[]{:S(2)}, u32[]{:S(2)}) %all-to-all-start.11) | async-done | bytes 2097184 | tf_op jit(solution)/shard_map/all_to_all | solution.py:134
  1854.7 114.9 %collective-permute-done.105 = bf16[3,576,2304]{2,1,0:T(8,128)(2,1)} collective-permute-done((bf16[3,576,2304]{2,1,0:T(8,128)(2,1)}, bf16[3,576,2304]{2,1,0:T(8,128)(2,1)}, u32[]{:S(2)}, u32[]{:S(2)}) %collective-permute-start.105) | collective-permute-done | bytes 7962656 | tf_op jit(solution)/shard_map/ppermute | solution.py:130
  2017.4 21.2 collective-permute-done.88
  2058.3 17.7 collective-permute-done.109
  2087.4 24.7 %collective-permute-done.111 = f32[4,2304]{1,0:T(4,128)S(1)} collective-permute-done((f32[4,2304]{1,0:T(4,128)S(1)}, f32[4,2304]{1,0:T(4,128)S(1)}, u32[]{:S(2)}, u32[]{:S(2)}) %collective-permute-start.111) | collective-permute-done | bytes 36896 | tf_op jit(solution)/shard_map/ppermute | solution.py:130
  2122.7 19.1 collective-permute-done.91
  (697 shorter events, 875.2 us)
Async XLA Ops:
  260.1 68.2 %all-to-all-start.4 = ((bf16[8,256,512]{2,1,0:T(8,128)(2,1)}), bf16[8,256,512]{2,1,0:T(8,128)(2,1)}, u32[]{:S(2)}, u32[]{:S(2)}) async-start(bf16[8,256,512]{2,1,0:T(8,128)(2,1)} %bitcast.179), calls=%async_computation.4 | async-start | bytes 4194304 | tf_op jit(solution)/shard_map/all_to_all | solution.py:134
  268.6 55.0 %collective-permute-start.10 = (bf16[288,1024]{1,0:T(8,128)(2,1)S(1)}, bf16[288,1024]{1,0:T(8,128)(2,1)}, u32[]{:S(2)}, u32[]{:S(2)}) collective-permute-start(bf16[288,1024]{1,0:T(8,128)(2,1)S(1)} %get-tuple-element.81), channel_id=1, source_target_pairs={{8,0},{16,8},{24,16},{28,24},{20,28},{12,20},{4,12},{0,4},{9,1},{1... | collective-permute-start | bytes 1769480 | tf_op jit(solution)/shard_map/ppermute | solution.py:99
  329.8 89.8 %all-to-all-start.1 = ((bf16[8,256,512]{2,1,0:T(8,128)(2,1)}), bf16[8,256,512]{2,1,0:T(8,128)(2,1)}, u32[]{:S(2)}, u32[]{:S(2)}) async-start(bf16[8,256,512]{2,1,0:T(8,128)(2,1)} %bitcast.178), calls=%async_computation.1 | async-start | bytes 4194304 | tf_op jit(solution)/shard_map/all_to_all | solution.py:134
  345.8 53.1 %collective-permute-start.14 = (bf16[288,1024]{1,0:T(8,128)(2,1)}, bf16[288,1024]{1,0:T(8,128)(2,1)S(1)}, u32[]{:S(2)}, u32[]{:S(2)}) collective-permute-start(bf16[288,1024]{1,0:T(8,128)(2,1)} %collective-permute-done.12), channel_id=1, source_target_pairs={{8,0},{16,8},{24,16},{28,24},{20,28},{12,20},{4,12},{0,4},{9,1},{1... | collective-permute-start | bytes 1769480 | tf_op jit(solution)/shard_map/ppermute | solution.py:99
  506.7 67.6 %collective-permute-start.19 = (bf16[256,2304]{1,0:T(8,128)(2,1)}, bf16[256,2304]{1,0:T(8,128)(2,1)}, u32[]{:S(2)}, u32[]{:S(2)}) collective-permute-start(bf16[256,2304]{1,0:T(8,128)(2,1)} %get-tuple-element.73), channel_id=1, source_target_pairs={{8,0},{16,8},{24,16},{28,24},{20,28},{12,20},{4,12},{0,4},{9,1},{1... | collective-permute-start | bytes 3538952 | tf_op jit(solution)/shard_map/ppermute | solution.py:99
  508.7 67.6 %collective-permute-start.18 = (bf16[256,2304]{1,0:T(8,128)(2,1)}, bf16[256,2304]{1,0:T(8,128)(2,1)S(1)}, u32[]{:S(2)}, u32[]{:S(2)}) collective-permute-start(bf16[256,2304]{1,0:T(8,128)(2,1)} %get-tuple-element.73), channel_id=1, source_target_pairs={{0,8},{8,16},{16,24},{24,28},{28,20},{20,12},{12,4},{4,0},{1,9},{9... | collective-permute-start | bytes 3538952 | tf_op jit(solution)/shard_map/ppermute | solution.py:98
  508.7 67.6 %collective-permute-start.34 = (bf16[256,2304]{1,0:T(8,128)(2,1)}, bf16[256,2304]{1,0:T(8,128)(2,1)S(1)}, u32[]{:S(2)}, u32[]{:S(2)}) collective-permute-start(bf16[256,2304]{1,0:T(8,128)(2,1)} %get-tuple-element.185), channel_id=1, source_target_pairs={{0,8},{8,16},{16,24},{24,28},{28,20},{20,12},{12,4},{4,0},{1,9},{9... | collective-permute-start | bytes 3538952 | tf_op jit(solution)/shard_map/ppermute | solution.py:98
  510.7 67.6 %collective-permute-start.35 = (bf16[256,2304]{1,0:T(8,128)(2,1)}, bf16[256,2304]{1,0:T(8,128)(2,1)S(1)}, u32[]{:S(2)}, u32[]{:S(2)}) collective-permute-start(bf16[256,2304]{1,0:T(8,128)(2,1)} %get-tuple-element.185), channel_id=1, source_target_pairs={{8,0},{16,8},{24,16},{28,24},{20,28},{12,20},{4,12},{0,4},{9,1},{1... | collective-permute-start | bytes 3538952 | tf_op jit(solution)/shard_map/ppermute | solution.py:99
  576.3 54.1 %collective-permute-start.36 = (bf16[256,2304]{1,0:T(8,128)(2,1)S(1)}, bf16[256,2304]{1,0:T(8,128)(2,1)S(1)}, u32[]{:S(2)}, u32[]{:S(2)}) collective-permute-start(bf16[256,2304]{1,0:T(8,128)(2,1)S(1)} %collective-permute-done.34), channel_id=1, source_target_pairs={{0,8},{8,16},{16,24},{24,28},{28,20},{20,12},{12,4},{4,0},{1,9},{9... | collective-permute-start | bytes 3538952 | tf_op jit(solution)/shard_map/ppermute | solution.py:98
  578.3 52.2 %collective-permute-start.37 = (bf16[256,2304]{1,0:T(8,128)(2,1)S(1)}, bf16[256,2304]{1,0:T(8,128)(2,1)S(1)}, u32[]{:S(2)}, u32[]{:S(2)}) collective-permute-start(bf16[256,2304]{1,0:T(8,128)(2,1)S(1)} %collective-permute-done.35), channel_id=1, source_target_pairs={{8,0},{16,8},{24,16},{28,24},{20,28},{12,20},{4,12},{0,4},{9,1},{1... | collective-permute-start | bytes 3538952 | tf_op jit(solution)/shard_map/ppermute | solution.py:99
  603.4 50.6 %collective-permute-start.23 = (bf16[256,2304]{1,0:T(8,128)(2,1)S(1)}, bf16[256,2304]{1,0:T(8,128)(2,1)S(1)}, u32[]{:S(2)}, u32[]{:S(2)}) collective-permute-start(bf16[256,2304]{1,0:T(8,128)(2,1)S(1)} %collective-permute-done.21), channel_id=1, source_target_pairs={{8,0},{16,8},{24,16},{28,24},{20,28},{12,20},{4,12},{0,4},{9,1},{1... | collective-permute-start | bytes 3538952 | tf_op jit(solution)/shard_map/ppermute | solution.py:99
  605.4 50.7 %collective-permute-start.22 = (bf16[256,2304]{1,0:T(8,128)(2,1)S(1)}, bf16[256,2304]{1,0:T(8,128)(2,1)S(1)}, u32[]{:S(2)}, u32[]{:S(2)}) collective-permute-start(bf16[256,2304]{1,0:T(8,128)(2,1)S(1)} %collective-permute-done.20), channel_id=1, source_target_pairs={{0,8},{8,16},{16,24},{24,28},{28,20},{20,12},{12,4},{4,0},{1,9},{9... | collective-permute-start | bytes 3538952 | tf_op jit(solution)/shard_map/ppermute | solution.py:98
  630.5 50.6 %collective-permute-start.38 = (bf16[256,2304]{1,0:T(8,128)(2,1)S(1)}, bf16[256,2304]{1,0:T(8,128)(2,1)S(1)}, u32[]{:S(2)}, u32[]{:S(2)}) collective-permute-start(bf16[256,2304]{1,0:T(8,128)(2,1)S(1)} %collective-permute-done.36), channel_id=1, source_target_pairs={{0,8},{8,16},{16,24},{24,28},{28,20},{20,12},{12,4},{4,0},{1,9},{9... | collective-permute-start | bytes 3538952 | tf_op jit(solution)/shard_map/ppermute | solution.py:98
  630.5 50.7 %collective-permute-start.39 = (bf16[256,2304]{1,0:T(8,128)(2,1)S(1)}, bf16[256,2304]{1,0:T(8,128)(2,1)S(1)}, u32[]{:S(2)}, u32[]{:S(2)}) collective-permute-start(bf16[256,2304]{1,0:T(8,128)(2,1)S(1)} %collective-permute-done.37), channel_id=1, source_target_pairs={{8,0},{16,8},{24,16},{28,24},{20,28},{12,20},{4,12},{0,4},{9,1},{1... | collective-permute-start | bytes 3538952 | tf_op jit(solution)/shard_map/ppermute | solution.py:99
  654.0 105.2 %collective-permute-start.25 = (bf16[128,2304]{1,0:T(8,128)(2,1)S(1)}, bf16[128,2304]{1,0:T(8,128)(2,1)S(1)}, u32[]{:S(2)}, u32[]{:S(2)}) collective-permute-start(bf16[128,2304]{1,0:T(8,128)(2,1)S(1)} %slice.558), channel_id=1, source_target_pairs={{8,0},{16,8},{24,16},{28,24},{20,28},{12,20},{4,12},{0,4},{9,1},{1... | collective-permute-start | bytes 1769480 | tf_op jit(solution)/shard_map/ppermute | solution.py:102
  656.1 102.2 %collective-permute-start.24 = (bf16[128,2304]{1,0:T(8,128)(2,1)S(1)}, bf16[128,2304]{1,0:T(8,128)(2,1)S(1)}, u32[]{:S(2)}, u32[]{:S(2)}) collective-permute-start(bf16[128,2304]{1,0:T(8,128)(2,1)S(1)} %slice.557), channel_id=1, source_target_pairs={{0,8},{8,16},{16,24},{24,28},{28,20},{20,12},{12,4},{4,0},{1,9},{9... | collective-permute-start | bytes 1769480 | tf_op jit(solution)/shard_map/ppermute | solution.py:101
  756.2 65.4 %collective-permute-start.42 = (bf16[128,2304]{1,0:T(8,128)(2,1)S(1)}, bf16[128,2304]{1,0:T(8,128)(2,1)S(1)}, u32[]{:S(2)}, u32[]{:S(2)}) collective-permute-start(bf16[128,2304]{1,0:T(8,128)(2,1)S(1)} %get-tuple-element.128), channel_id=1, source_target_pairs={{0,8},{8,16},{16,24},{24,28},{28,20},{20,12},{12,4},{4,0},{1,9},{9... | collective-permute-start | bytes 1769480 | tf_op jit(solution)/shard_map/ppermute | solution.py:110
  756.6 65.0 %collective-permute-start.46 = (bf16[128,2304]{1,0:T(8,128)(2,1)S(1)}, bf16[128,2304]{1,0:T(8,128)(2,1)S(1)}, u32[]{:S(2)}, u32[]{:S(2)}) collective-permute-start(bf16[128,2304]{1,0:T(8,128)(2,1)S(1)} %get-tuple-element.129), channel_id=1, source_target_pairs={{8,0},{16,8},{24,16},{28,24},{20,28},{12,20},{4,12},{0,4},{9,1},{1... | collective-permute-start | bytes 1769480 | tf_op jit(solution)/shard_map/ppermute | solution.py:111
  836.3 50.2 %collective-permute-start.27 = (bf16[256,2304]{1,0:T(8,128)(2,1)S(1)}, bf16[256,2304]{1,0:T(8,128)(2,1)S(1)}, u32[]{:S(2)}, u32[]{:S(2)}) collective-permute-start(bf16[256,2304]{1,0:T(8,128)(2,1)S(1)} %pad_maximum_fusion.19), channel_id=1, source_target_pairs={{0,8},{8,16},{16,24},{24,28},{28,20},{20,12},{12,4},{4,0},{1,9},{9... | collective-permute-start | bytes 3538952 | tf_op jit(solution)/shard_map/ppermute | solution.py:123
  836.7 50.4 %collective-permute-start.47 = (bf16[256,2304]{1,0:T(8,128)(2,1)S(1)}, bf16[256,2304]{1,0:T(8,128)(2,1)S(1)}, u32[]{:S(2)}, u32[]{:S(2)}) collective-permute-start(bf16[256,2304]{1,0:T(8,128)(2,1)S(1)} %pad_maximum_fusion.22), channel_id=1, source_target_pairs={{8,0},{16,8},{24,16},{28,24},{20,28},{12,20},{4,12},{0,4},{9,1},{1... | collective-permute-start | bytes 3538952 | tf_op jit(solution)/shard_map/ppermute | solution.py:124
  861.5 50.2 %collective-permute-start.44 = (bf16[256,2304]{1,0:T(8,128)(2,1)S(1)}, bf16[256,2304]{1,0:T(8,128)(2,1)S(1)}, u32[]{:S(2)}, u32[]{:S(2)}) collective-permute-start(bf16[256,2304]{1,0:T(8,128)(2,1)S(1)} %add_convert_fusion.22), channel_id=1, source_target_pairs={{0,8},{8,16},{16,24},{24,28},{28,20},{20,12},{12,4},{4,0},{1,9},{9... | collective-permute-start | bytes 3538952 | tf_op jit(solution)/shard_map/ppermute | solution.py:123
  861.9 51.9 %collective-permute-start.31 = (bf16[256,2304]{1,0:T(8,128)(2,1)S(1)}, bf16[256,2304]{1,0:T(8,128)(2,1)S(1)}, u32[]{:S(2)}, u32[]{:S(2)}) collective-permute-start(bf16[256,2304]{1,0:T(8,128)(2,1)S(1)} %pad_maximum_fusion.20), channel_id=1, source_target_pairs={{8,0},{16,8},{24,16},{28,24},{20,28},{12,20},{4,12},{0,4},{9,1},{1... | collective-permute-start | bytes 3538952 | tf_op jit(solution)/shard_map/ppermute | solution.py:124
  935.2 52.8 %collective-permute-start.29 = (bf16[256,2304]{1,0:T(8,128)(2,1)S(1)}, bf16[256,2304]{1,0:T(8,128)(2,1)S(1)}, u32[]{:S(2)}, u32[]{:S(2)}) collective-permute-start(bf16[256,2304]{1,0:T(8,128)(2,1)S(1)} %get-tuple-element.116), channel_id=1, source_target_pairs={{0,8},{8,16},{16,24},{24,28},{28,20},{20,12},{12,4},{4,0},{1,9},{9... | collective-permute-start | bytes 3538952 | tf_op jit(solution)/shard_map/ppermute | solution.py:123
  936.1 51.2 %collective-permute-start.49 = (bf16[256,2304]{1,0:T(8,128)(2,1)S(1)}, bf16[256,2304]{1,0:T(8,128)(2,1)S(1)}, u32[]{:S(2)}, u32[]{:S(2)}) collective-permute-start(bf16[256,2304]{1,0:T(8,128)(2,1)S(1)} %add_convert_fusion.19), channel_id=1, source_target_pairs={{8,0},{16,8},{24,16},{28,24},{20,28},{12,20},{4,12},{0,4},{9,1},{1... | collective-permute-start | bytes 3538952 | tf_op jit(solution)/shard_map/ppermute | solution.py:124
  1017.6 53.6 %collective-permute-start.66 = (bf16[256,2304]{1,0:T(8,128)(2,1)S(1)}, bf16[256,2304]{1,0:T(8,128)(2,1)S(1)}, u32[]{:S(2)}, u32[]{:S(2)}) collective-permute-start(bf16[256,2304]{1,0:T(8,128)(2,1)S(1)} %get-tuple-element.143), channel_id=1, source_target_pairs={{0,8},{8,16},{16,24},{24,28},{28,20},{20,12},{12,4},{4,0},{1,9},{9... | collective-permute-start | bytes 3538952 | tf_op jit(solution)/shard_map/ppermute | solution.py:98
  1018.5 53.3 %collective-permute-start.67 = (bf16[256,2304]{1,0:T(8,128)(2,1)S(1)}, bf16[256,2304]{1,0:T(8,128)(2,1)S(1)}, u32[]{:S(2)}, u32[]{:S(2)}) collective-permute-start(bf16[256,2304]{1,0:T(8,128)(2,1)S(1)} %get-tuple-element.143), channel_id=1, source_target_pairs={{8,0},{16,8},{24,16},{28,24},{20,28},{12,20},{4,12},{0,4},{9,1},{1... | collective-permute-start | bytes 3538952 | tf_op jit(solution)/shard_map/ppermute | solution.py:99
  1044.5 50.6 %collective-permute-start.53 = (bf16[256,2304]{1,0:T(8,128)(2,1)S(1)}, bf16[256,2304]{1,0:T(8,128)(2,1)S(1)}, u32[]{:S(2)}, u32[]{:S(2)}) collective-permute-start(bf16[256,2304]{1,0:T(8,128)(2,1)S(1)} %collective-permute-done.51), channel_id=1, source_target_pairs={{8,0},{16,8},{24,16},{28,24},{20,28},{12,20},{4,12},{0,4},{9,1},{1... | collective-permute-start | bytes 3538952 | tf_op jit(solution)/shard_map/ppermute | solution.py:99
  1045.9 50.6 %collective-permute-start.52 = (bf16[256,2304]{1,0:T(8,128)(2,1)S(1)}, bf16[256,2304]{1,0:T(8,128)(2,1)S(1)}, u32[]{:S(2)}, u32[]{:S(2)}) collective-permute-start(bf16[256,2304]{1,0:T(8,128)(2,1)S(1)} %collective-permute-done.50), channel_id=1, source_target_pairs={{0,8},{8,16},{16,24},{24,28},{28,20},{20,12},{12,4},{4,0},{1,9},{9... | collective-permute-start | bytes 3538952 | tf_op jit(solution)/shard_map/ppermute | solution.py:98
  1071.2 50.6 %collective-permute-start.68 = (bf16[256,2304]{1,0:T(8,128)(2,1)S(1)}, bf16[256,2304]{1,0:T(8,128)(2,1)S(1)}, u32[]{:S(2)}, u32[]{:S(2)}) collective-permute-start(bf16[256,2304]{1,0:T(8,128)(2,1)S(1)} %collective-permute-done.66), channel_id=1, source_target_pairs={{0,8},{8,16},{16,24},{24,28},{28,20},{20,12},{12,4},{4,0},{1,9},{9... | collective-permute-start | bytes 3538952 | tf_op jit(solution)/shard_map/ppermute | solution.py:98
  1071.8 50.6 %collective-permute-start.69 = (bf16[256,2304]{1,0:T(8,128)(2,1)S(1)}, bf16[256,2304]{1,0:T(8,128)(2,1)S(1)}, u32[]{:S(2)}, u32[]{:S(2)}) collective-permute-start(bf16[256,2304]{1,0:T(8,128)(2,1)S(1)} %collective-permute-done.67), channel_id=1, source_target_pairs={{8,0},{16,8},{24,16},{28,24},{20,28},{12,20},{4,12},{0,4},{9,1},{1... | collective-permute-start | bytes 3538952 | tf_op jit(solution)/shard_map/ppermute | solution.py:99
  1095.0 50.6 %collective-permute-start.55 = (bf16[256,2304]{1,0:T(8,128)(2,1)S(1)}, bf16[256,2304]{1,0:T(8,128)(2,1)S(1)}, u32[]{:S(2)}, u32[]{:S(2)}) collective-permute-start(bf16[256,2304]{1,0:T(8,128)(2,1)S(1)} %collective-permute-done.53), channel_id=1, source_target_pairs={{8,0},{16,8},{24,16},{28,24},{20,28},{12,20},{4,12},{0,4},{9,1},{1... | collective-permute-start | bytes 3538952 | tf_op jit(solution)/shard_map/ppermute | solution.py:99
  1096.5 50.7 %collective-permute-start.54 = (bf16[256,2304]{1,0:T(8,128)(2,1)S(1)}, bf16[256,2304]{1,0:T(8,128)(2,1)S(1)}, u32[]{:S(2)}, u32[]{:S(2)}) collective-permute-start(bf16[256,2304]{1,0:T(8,128)(2,1)S(1)} %collective-permute-done.52), channel_id=1, source_target_pairs={{0,8},{8,16},{16,24},{24,28},{28,20},{20,12},{12,4},{4,0},{1,9},{9... | collective-permute-start | bytes 3538952 | tf_op jit(solution)/shard_map/ppermute | solution.py:98
  1121.8 50.6 %collective-permute-start.70 = (bf16[256,2304]{1,0:T(8,128)(2,1)S(1)}, bf16[256,2304]{1,0:T(8,128)(2,1)S(1)}, u32[]{:S(2)}, u32[]{:S(2)}) collective-permute-start(bf16[256,2304]{1,0:T(8,128)(2,1)S(1)} %collective-permute-done.68), channel_id=1, source_target_pairs={{0,8},{8,16},{16,24},{24,28},{28,20},{20,12},{12,4},{4,0},{1,9},{9... | collective-permute-start | bytes 3538952 | tf_op jit(solution)/shard_map/ppermute | solution.py:98
  1122.3 50.7 %collective-permute-start.71 = (bf16[256,2304]{1,0:T(8,128)(2,1)S(1)}, bf16[256,2304]{1,0:T(8,128)(2,1)S(1)}, u32[]{:S(2)}, u32[]{:S(2)}) collective-permute-start(bf16[256,2304]{1,0:T(8,128)(2,1)S(1)} %collective-permute-done.69), channel_id=1, source_target_pairs={{8,0},{16,8},{24,16},{28,24},{20,28},{12,20},{4,12},{0,4},{9,1},{1... | collective-permute-start | bytes 3538952 | tf_op jit(solution)/shard_map/ppermute | solution.py:99
  1320.5 49.6 %collective-permute-start.75 = (bf16[256,2304]{1,0:T(8,128)(2,1)S(1)}, bf16[256,2304]{1,0:T(8,128)(2,1)S(1)}, u32[]{:S(2)}, u32[]{:S(2)}) collective-permute-start(bf16[256,2304]{1,0:T(8,128)(2,1)S(1)} %pad_maximum_fusion.25), channel_id=1, source_target_pairs={{0,8},{8,16},{16,24},{24,28},{28,20},{20,12},{12,4},{4,0},{1,9},{9... | collective-permute-start | bytes 3538952 | tf_op jit(solution)/shard_map/ppermute | solution.py:123
  1345.8 50.1 %collective-permute-start.79 = (bf16[256,2304]{1,0:T(8,128)(2,1)S(1)}, bf16[256,2304]{1,0:T(8,128)(2,1)S(1)}, u32[]{:S(2)}, u32[]{:S(2)}) collective-permute-start(bf16[256,2304]{1,0:T(8,128)(2,1)S(1)} %pad_maximum_fusion.26), channel_id=1, source_target_pairs={{8,0},{16,8},{24,16},{28,24},{20,28},{12,20},{4,12},{0,4},{9,1},{1... | collective-permute-start | bytes 3538952 | tf_op jit(solution)/shard_map/ppermute | solution.py:124
  1419.4 53.6 %collective-permute-start.77 = (bf16[256,2304]{1,0:T(8,128)(2,1)S(1)}, bf16[256,2304]{1,0:T(8,128)(2,1)S(1)}, u32[]{:S(2)}, u32[]{:S(2)}) collective-permute-start(bf16[256,2304]{1,0:T(8,128)(2,1)S(1)} %get-tuple-element.108), channel_id=1, source_target_pairs={{0,8},{8,16},{16,24},{24,28},{28,20},{20,12},{12,4},{4,0},{1,9},{9... | collective-permute-start | bytes 3538952 | tf_op jit(solution)/shard_map/ppermute | solution.py:123
  1530.8 52.3 %all-to-all-start.6 = ((bf16[8,128,512]{2,1,0:T(8,128)(2,1)}), bf16[8,128,512]{2,1,0:T(8,128)(2,1)S(1)}, u32[]{:S(2)}, u32[]{:S(2)}) async-start(bf16[8,128,512]{2,1,0:T(8,128)(2,1)} %bitcast.45), calls=%async_computation.6 | async-start | bytes 2097152 | tf_op jit(solution)/shard_map/all_to_all | solution.py:134
  1583.0 55.1 %all-to-all-start.10 = ((bf16[8,128,512]{2,1,0:T(8,128)(2,1)}), bf16[8,128,512]{2,1,0:T(8,128)(2,1)S(1)}, u32[]{:S(2)}, u32[]{:S(2)}) async-start(bf16[8,128,512]{2,1,0:T(8,128)(2,1)} %bitcast.214), calls=%async_computation.10 | async-start | bytes 2097152 | tf_op jit(solution)/shard_map/all_to_all | solution.py:134
  1704.8 81.8 %collective-permute-start.104 = (bf16[3,576,2304]{2,1,0:T(8,128)(2,1)}, bf16[3,576,2304]{2,1,0:T(8,128)(2,1)}, u32[]{:S(2)}, u32[]{:S(2)}) collective-permute-start(bf16[3,576,2304]{2,1,0:T(8,128)(2,1)} %fusion.17), channel_id=1, source_target_pairs={{0,1},{1,0},{2,3},{3,2},{4,5},{5,4},{6,7},{7,6},{8,9},{9,8},{10,11... | collective-permute-start | bytes 23887880 | tf_op jit(solution)/shard_map/ppermute | solution.py:130
  1707.4 52.4 %all-to-all-start.11 = ((bf16[8,256,512]{2,1,0:T(8,128)(2,1)}), bf16[8,256,512]{2,1,0:T(8,128)(2,1)}, u32[]{:S(2)}, u32[]{:S(2)}) async-start(bf16[8,256,512]{2,1,0:T(8,128)(2,1)} %bitcast.205), calls=%async_computation.11 | async-start | bytes 4194304 | tf_op jit(solution)/shard_map/all_to_all | solution.py:134
  1780.4 55.2 %collective-permute-start.82 = (bf16[2304,2048]{1,0:T(8,128)(2,1)}, bf16[2304,2048]{1,0:T(8,128)(2,1)}, u32[]{:S(2)}, u32[]{:S(2)}) collective-permute-start(bf16[2304,2048]{1,0:T(8,128)(2,1)} %convolution_convert_fusion.2), channel_id=1, source_target_pairs={{0,1},{1,0},{2,3},{3,2},{4,5},{5,4},{6,7},{7,6},{8,9},{9,8},{10,11... | collective-permute-start | bytes 28311560 | tf_op jit(solution)/shard_map/ppermute | solution.py:130
  1795.7 174.0 %collective-permute-start.105 = (bf16[3,576,2304]{2,1,0:T(8,128)(2,1)}, bf16[3,576,2304]{2,1,0:T(8,128)(2,1)}, u32[]{:S(2)}, u32[]{:S(2)}) collective-permute-start(bf16[3,576,2304]{2,1,0:T(8,128)(2,1)} %add_convert_fusion.2), channel_id=1, source_target_pairs={{0,2},{1,3},{2,0},{3,1},{4,6},{5,7},{6,4},{7,5},{8,10},{9,11},{10,... | collective-permute-start | bytes 23887880 | tf_op jit(solution)/shard_map/ppermute | solution.py:130
  1817.9 177.0 %collective-permute-start.99 = (bf16[288,1024]{1,0:T(8,128)(2,1)}, bf16[288,1024]{1,0:T(8,128)(2,1)}, u32[]{:S(2)}, u32[]{:S(2)}) collective-permute-start(bf16[288,1024]{1,0:T(8,128)(2,1)} %pad_maximum_fusion.32), channel_id=1, source_target_pairs={{8,0},{16,8},{24,16},{28,24},{20,28},{12,20},{4,12},{0,4},{9,1},{1... | collective-permute-start | bytes 1769480 | tf_op jit(solution)/shard_map/ppermute | solution.py:124
  1834.8 160.1 %collective-permute-start.96 = (bf16[288,1024]{1,0:T(8,128)(2,1)}, bf16[288,1024]{1,0:T(8,128)(2,1)}, u32[]{:S(2)}, u32[]{:S(2)}) collective-permute-start(bf16[288,1024]{1,0:T(8,128)(2,1)} %add_convert_fusion.33), channel_id=1, source_target_pairs={{0,8},{8,16},{16,24},{24,28},{28,20},{20,12},{12,4},{4,0},{1,9},{9... | collective-permute-start | bytes 1769480 | tf_op jit(solution)/shard_map/ppermute | solution.py:123
  1852.7 126.2 %collective-permute-start.83 = (bf16[144,2048]{1,0:T(8,128)(2,1)S(1)}, bf16[144,2048]{1,0:T(8,128)(2,1)S(1)}, u32[]{:S(2)}, u32[]{:S(2)}) collective-permute-start(bf16[144,2048]{1,0:T(8,128)(2,1)S(1)} %get-tuple-element.96), channel_id=1, source_target_pairs={{0,8},{8,16},{16,24},{24,28},{28,20},{20,12},{12,4},{4,0},{1,9},{9... | collective-permute-start | bytes 1769480 | tf_op jit(solution)/shard_map/ppermute | solution.py:110
  1854.0 124.9 %collective-permute-start.87 = (bf16[144,2048]{1,0:T(8,128)(2,1)S(1)}, bf16[144,2048]{1,0:T(8,128)(2,1)S(1)}, u32[]{:S(2)}, u32[]{:S(2)}) collective-permute-start(bf16[144,2048]{1,0:T(8,128)(2,1)S(1)} %get-tuple-element.98), channel_id=1, source_target_pairs={{8,0},{16,8},{24,16},{28,24},{20,28},{12,20},{4,12},{0,4},{9,1},{1... | collective-permute-start | bytes 1769480 | tf_op jit(solution)/shard_map/ppermute | solution.py:111
  1978.8 137.6 %collective-permute-start.106 = (bf16[3,576,2304]{2,1,0:T(8,128)(2,1)}, bf16[3,576,2304]{2,1,0:T(8,128)(2,1)}, u32[]{:S(2)}, u32[]{:S(2)}) collective-permute-start(bf16[3,576,2304]{2,1,0:T(8,128)(2,1)} %add_convert_fusion.1), channel_id=1, source_target_pairs={{0,1},{1,0},{2,3},{3,2},{4,5},{5,4},{6,7},{7,6},{8,9},{9,8},{10,11... | collective-permute-start | bytes 23887880 | tf_op jit(solution)/shard_map/ppermute | solution.py:130
  (186 other events, 3843.3 us)

commit v2 on v1

--- a/solution.py
+++ b/solution.py
@@ -77,9 +77,12 @@
 
 def ring_perms(size):
     order = list(range(0, size, 2)) + list(range(size - 1, 0, -2))
-    up = [(order[i], order[(i + 1) % size]) for i in range(size)]
-    down = [(b, a) for a, b in up]
-    return up, down
+    up = [
+        (base + order[i], base + order[(i + 1) % size])
+        for base in range(0, lax.axis_size("wide"), size)
+        for i in range(size)
+    ]
+    return up, [(b, a) for a, b in up]
 
 
 def ring_offsets(size):
@@ -89,40 +92,48 @@
     return out + [size // 2]
 
 
-def ring_gather(value, size):
+def after(value, *earlier):
+    return lax.optimization_barrier((value,) + earlier)[0]
+
+
+def ring_gather(value, size, visit=lambda block: block):
     up, down = ring_perms(size)
     half = value.shape[0] // 2
     a = b = value
-    out = [value]
+    out = [visit(value)]
     for _ in range(1, size // 2):
         a = lax.ppermute(a, "wide", up)
         b = lax.ppermute(b, "wide", down)
-        out += [a, b]
+        out += [visit(a), visit(b)]
+    tokens = (a, b)
     a = lax.ppermute(a[:half], "wide", up)
     b = lax.ppermute(b[half:], "wide", down)
-    return out + [a, b]
-
-
-def ring_scatter(part_of, rows, size):
+    return out + [visit(a), visit(b)], tokens
+
+
+def ring_scatter(part_of, rows, size, earlier=()):
     up, down = ring_perms(size)
     half = rows // 2
-    far = part_of(size // 2)
-    a = lax.ppermute(far[:half].astype(bf16), "wide", up)
-    b = lax.ppermute(far[half:].astype(bf16), "wide", down)
-    first = True
+    far = part_of(size // 2).astype(bf16)
+    if earlier:
+        far = after(far, *earlier)
+    a = lax.ppermute(far[:half], "wide", up)
+    b = lax.ppermute(far[half:], "wide", down)
+    tokens = (a, b)
     for k in range(size // 2 - 1, 0, -1):
         own_a = part_of(k).astype(f32)
         own_b = part_of(-k).astype(f32)
-        if first:
+        if k == size // 2 - 1:
             a = jnp.concatenate([own_a[:half] + a.astype(f32), own_a[half:]], axis=0)
             b = jnp.concatenate([own_b[:half], own_b[half:] + b.astype(f32)], axis=0)
-            first = False
         else:
             a = own_a + a.astype(f32)
             b = own_b + b.astype(f32)
+        if k > 1 or size == 4:
+            tokens = (a, b)
         a = lax.ppermute(a.astype(bf16), "wide", up)
         b = lax.ppermute(b.astype(bf16), "wide", down)
-    return part_of(0).astype(f32) + a.astype(f32) + b.astype(f32)
+    return part_of(0).astype(f32) + a.astype(f32) + b.astype(f32), tokens
 
 
 def swap(value, axis, bit):
@@ -134,33 +145,54 @@
     return lax.all_to_all(value, "wide", split_axis=0, concat_axis=0, tiled=True)
 
 
+def heads_all_to_all(value):
+    size = lax.axis_size("wide")
+    classes = size // KEY_VALUE_HEADS
+    groups = [list(range(c, size, classes)) for c in range(classes)]
+    return lax.all_to_all(
+        value, "wide", split_axis=0, concat_axis=0, axis_index_groups=groups, tiled=True
+    )
+
+
+def class_ring(value):
+    size = lax.axis_size("wide")
+    classes = size // KEY_VALUE_HEADS
+    perm = [(i, i // classes * classes + (i + 1) % classes) for i in range(size)]
+    return lax.ppermute(value, "wide", perm)
+
+
 def slice_values(codes, width):
-    add = jnp.where(width == 0, 0.0, jnp.where(width == 1, 8.0, 32.0)).astype(f32)
-    inverse = jnp.where(width == 0, 1.0, jnp.where(width == 1, 1.0 / 16, 1.0 / 64)).astype(f32)
-    step = jnp.where(width == 0, 1.0, jnp.where(width == 1, 16.0, 64.0)).astype(f32)
-    top = jnp.where(width == 0, 127.0, jnp.where(width == 1, 112.0, 64.0)).astype(f32)
-    low = jnp.where(width == 2, -128.0, -128.0).astype(f32)
-    return jnp.maximum(jnp.minimum(jnp.floor((codes + add) * inverse) * step, top), low)
-
-
-def attn_slice_kernel(places, info, own_ref, other_ref, col_ref, row_ref, *out_refs):
+    lift = jnp.where(width == 0, 0.0, 0.5).astype(bf16)
+    large = jnp.where(width == 0, 0.0, jnp.where(width == 1, 1.5 * 2**11, 1.5 * 2**13)).astype(bf16)
+    top = jnp.where(width == 0, 127.0, jnp.where(width == 1, 112.0, 64.0)).astype(bf16)
+    return jnp.minimum(((codes + lift) + large) - large, top)
+
+
+def attn_slice_kernel(places, info, own_ref, other_ref, scale_ref, *out_refs):
+    def write(code_ref):
+        codes = code_ref[0]
+        scale = scale_ref[...].astype(bf16)
+        for s, out_ref in enumerate(out_refs):
+            out_ref[...] = slice_values(codes, info[1 + s]) * scale
+
     mine = pl.program_id(1) == info[0]
-    codes = jnp.where(mine, own_ref[0], other_ref[0]).astype(f32)
-    scale = col_ref[...] * row_ref[...]
-    for s, out_ref in enumerate(out_refs):
-        out_ref[...] = (slice_values(codes, info[1 + s]) * scale).astype(bf16)
-
-
-def attn_slices(own, other, places, info, col_scale, row_scale, count):
+    pl.when(mine)(lambda: write(own_ref))
+    pl.when(jnp.logical_not(mine))(lambda: write(other_ref))
+
+
+def attn_slices(own, other, places, info, scale, by_column, count):
     blocks, rows, cols = own.shape
+    if by_column:
+        scale_spec = pl.BlockSpec((1, cols), lambda k, j, p, i: (0, j))
+    else:
+        scale_spec = pl.BlockSpec((rows, 1), lambda k, j, p, i: (p[k], 0))
     grid_spec = pltpu.PrefetchScalarGridSpec(
         num_scalar_prefetch=2,
         grid=(blocks, 2),
         in_specs=[
             pl.BlockSpec((1, rows, cols), lambda k, j, p, i: (k, 0, 0)),
             pl.BlockSpec((1, rows, cols), lambda k, j, p, i: (k, 0, 0)),
-            pl.BlockSpec((1, cols), lambda k, j, p, i: (0, j)),
-            pl.BlockSpec((rows, 1), lambda k, j, p, i: (p[k], 0)),
+            scale_spec,
         ],
         out_specs=[pl.BlockSpec((rows, cols), lambda k, j, p, i: (p[k], j))] * count,
     )
@@ -169,37 +201,121 @@
         grid_spec=grid_spec,
         out_shape=[jax.ShapeDtypeStruct((blocks * rows, 2 * cols), bf16)] * count,
         compiler_params=pltpu.CompilerParams(vmem_limit_bytes=VMEM_LIMIT),
+        cost_estimate=pl.CostEstimate(
+            flops=10 * count * own.size,
+            bytes_accessed=4 * own.size * (1 + count),
+            transcendentals=0,
+        ),
         name="attn_slices",
-    )(places, info, own, other, col_scale, row_scale)
-
-
-def mlp_slice_kernel(info, code_ref, col_ref, row_ref, *out_refs):
-    codes = code_ref[0].astype(f32)
-    scale = col_ref[0] * row_ref[0]
-    for s, out_ref in enumerate(out_refs):
-        out_ref[0] = (slice_values(codes, info[1 + s]) * scale).astype(bf16)
-
-
-def mlp_slices(codes, info, col_scale, row_scale, count):
+    )(places, info, own, other, scale)
+
+
+def own_slice_kernel(pieces, info, code_ref, row_ref, col_ref, *out_refs):
+    count = len(out_refs) // 3
+    for m in range(3):
+        codes = code_ref[m].astype(f32).astype(bf16)
+        scale = (row_ref[m] if m < 2 else col_ref[...]).astype(bf16)
+        for s in range(count):
+            out_refs[m * count + s][...] = slice_values(codes, info[1 + s]) * scale
+
+
+def own_slices(codes, pieces, info, row_scale, col_scale, count):
     three, rows, cols = codes.shape
-    block = 288 if rows % 288 == 0 else rows
+    steps = pieces.shape[0]
+    piece = rows // steps
+    grid_spec = pltpu.PrefetchScalarGridSpec(
+        num_scalar_prefetch=2,
+        grid=(steps,),
+        in_specs=[
+            pl.BlockSpec((three, piece, cols), lambda j, p, i: (0, p[j], 0)),
+            pl.BlockSpec((2, piece, 1), lambda j, p, i: (0, j, 0)),
+            pl.BlockSpec((1, cols), lambda j, p, i: (0, 0)),
+        ],
+        out_specs=[pl.BlockSpec((piece, cols), lambda j, p, i: (j, 0))] * (three * count),
+    )
+    return pl.pallas_call(
+        own_slice_kernel,
+        grid_spec=grid_spec,
+        out_shape=[jax.ShapeDtypeStruct((2 * rows, cols), bf16)] * (three * count),
+        compiler_params=pltpu.CompilerParams(vmem_limit_bytes=VMEM_LIMIT),
+        cost_estimate=pl.CostEstimate(
+            flops=10 * count * codes.size,
+            bytes_accessed=codes.size * (4 + 2 * count),
+            transcendentals=0,
+        ),
+        name="own_slices",
+    )(pieces, info, codes, row_scale, col_scale)
+
+
+def partner_slice_kernel(info, *refs, steps, count):
+    piece_refs, scale_ref, out_refs = refs[:steps], refs[steps], refs[steps + 1 + count :]
+    for j in range(steps):
+
+        @pl.when(pl.program_id(0) == j)
+        def _():
+            codes = piece_refs[j][...]
+            scale = scale_ref[...].astype(bf16)
+            for s, out_ref in enumerate(out_refs):
+                out_ref[...] = slice_values(codes, info[1 + s]) * scale
+
+
+def partner_slices(pieces, info, scale, by_column, weights):
+    steps = len(pieces)
+    count = len(weights)
+    piece, cols = pieces[0].shape
+    if by_column:
+        scale_spec = pl.BlockSpec((1, cols), lambda j, i: (0, 0))
+    else:
+        scale_spec = pl.BlockSpec((piece, 1), lambda j, i: (steps + j, 0))
     grid_spec = pltpu.PrefetchScalarGridSpec(
         num_scalar_prefetch=1,
-        grid=(three, rows // block),
-        in_specs=[
-            pl.BlockSpec((1, block, cols), lambda k, j, i: (k, j, 0)),
-            pl.BlockSpec((1, 1, cols), lambda k, j, i: (k, 0, 0)),
-            pl.BlockSpec((1, block, 1), lambda k, j, i: (k, j, 0)),
-        ],
-        out_specs=[pl.BlockSpec((1, block, cols), lambda k, j, i: (k, j, 0))] * count,
+        grid=(steps,),
+        in_specs=[pl.BlockSpec((piece, cols), lambda j, i: (0, 0))] * steps
+        + [scale_spec]
+        + [pl.BlockSpec(memory_space=pl.ANY)] * count,
+        out_specs=[pl.BlockSpec((piece, cols), lambda j, i: (steps + j, 0))] * count,
     )
     return pl.pallas_call(
-        mlp_slice_kernel,
+        functools.partial(partner_slice_kernel, steps=steps, count=count),
         grid_spec=grid_spec,
-        out_shape=[jax.ShapeDtypeStruct((three, rows, cols), bf16)] * count,
+        out_shape=[jax.ShapeDtypeStruct(w.shape, bf16) for w in weights],
+        input_output_aliases={2 + steps + s: s for s in range(count)},
         compiler_params=pltpu.CompilerParams(vmem_limit_bytes=VMEM_LIMIT),
-        name="mlp_slices",
-    )(info, codes, col_scale, row_scale)
+        cost_estimate=pl.CostEstimate(
+            flops=10 * count * steps * piece * cols,
+            bytes_accessed=2 * (1 + count) * steps * piece * cols,
+            transcendentals=0,
+        ),
+        name="partner_slices",
+    )(info, *pieces, scale, *weights)
+
+
+def unpack_kernel(pieces, *refs):
+    out_ref = refs[-1]
+    for m, ref in enumerate(refs[:-1]):
+        out_ref[m] = ref[...].astype(f32)
+
+
+def unpack(grads, pieces):
+    steps = pieces.shape[0]
+    rows, cols = grads[0].shape
+    piece = rows // steps
+    grid_spec = pltpu.PrefetchScalarGridSpec(
+        num_scalar_prefetch=1,
+        grid=(steps,),
+        in_specs=[pl.BlockSpec((piece, cols), lambda j, p: (j, 0))] * len(grads),
+        out_specs=pl.BlockSpec((len(grads), piece, cols), lambda j, p: (0, p[j], 0)),
+    )
+    return pl.pallas_call(
+        unpack_kernel,
+        grid_spec=grid_spec,
+        out_shape=jax.ShapeDtypeStruct((len(grads), rows, cols), f32),
+        compiler_params=pltpu.CompilerParams(vmem_limit_bytes=VMEM_LIMIT),
+        cost_estimate=pl.CostEstimate(
+            flops=rows * cols, bytes_accessed=6 * len(grads) * rows * cols, transcendentals=0
+        ),
+        name="unpack",
+    )(pieces, *grads)
 
 
 def tile_positions(tile, count, start, class_index, class_rows, rows):
@@ -292,6 +408,9 @@
             jax.ShapeDtypeStruct((count, PAIRED * 128), f32),
         ],
         compiler_params=pltpu.CompilerParams(vmem_limit_bytes=VMEM_LIMIT),
+        cost_estimate=pl.CostEstimate(
+            flops=2 * count * PAIRED * length * 2 * HEAD_SIZE, bytes_accessed=8 * count * cols + 4 * length * HEAD_SIZE, transcendentals=2 * count * PAIRED * length
+        ),
         name="attn_forward",
     )(info, queries, pairs)
 
@@ -382,6 +501,9 @@
             jax.ShapeDtypeStruct((length, 2 * HEAD_SIZE), bf16),
         ],
         compiler_params=pltpu.CompilerParams(vmem_limit_bytes=VMEM_LIMIT),
+        cost_estimate=pl.CostEstimate(
+            flops=5 * count * PAIRED * length * 2 * HEAD_SIZE, bytes_accessed=10 * count * cols + 8 * length * HEAD_SIZE, transcendentals=2 * count * PAIRED * length
+        ),
         name="attn_backward",
     )(info, queries, pairs, grads, exact, lse)
 
@@ -404,7 +526,9 @@
     wide = lax.axis_size("wide")
     seq_size = lax.axis_size("seq")
     wide_index = lax.axis_index("wide")
-    side = lax.axis_index("seq") % 2
+    seq_index = lax.axis_index("seq")
+    side = seq_index % 2
+    half_wide = wide // 2
     is_low = side == 0
     place = ring_place(wide_index, wide)
     count, rows, model_dim = tokens.shape
@@ -422,6 +546,7 @@
     attn_rows = attn_codes.shape[0]
     hidden = mlp_codes.shape[1]
     offsets = ring_offsets(wide)
+    order = {o: i for i, o in enumerate(ring_offsets(half_wide))}
     seqs = range(count)
 
     def index_at(offset):
@@ -431,47 +556,62 @@
     info = jnp.concatenate([side[None].astype(jnp.int32), widths])
     class_info = class_index[None].astype(jnp.int32)
 
-    def gather_columns(first, size):
+    def gather_columns(first, size, earlier=()):
         mine = lax.dynamic_slice_in_dim(attn_codes, first + side * size, size, 1).astype(bf16)
-        own = jnp.concatenate(ring_gather(mine, wide), axis=0)
-        own = own.reshape(wide, attn_rows, size)
-        return own, swap(own, "seq", 1)
+        if earlier:
+            mine = after(mine, *earlier)
+        blocks, tokens = ring_gather(mine, wide, lambda block: (block, swap(block, "seq", 1)))
+        own = jnp.concatenate([block[0] for block in blocks], axis=0)
+        other = jnp.concatenate([block[1] for block in blocks], axis=0)
+        shape = (wide, attn_rows, size)
+        return own.reshape(shape), other.reshape(shape), tokens
 
     column_scale = inverse_powers(attn_exps)[None, :]
     output_scale = inverse_powers(out_exps)[:, None]
-    proj_own, proj_other = gather_columns(0, half_proj)
-    proj_weights = attn_slices(
-        proj_own,
-        proj_other,
-        places,
-        info,
-        column_scale,
-        jnp.ones((model_dim, 1), f32),
-        count,
-    )
-    out_own, out_other = gather_columns(proj_cols, half_out)
-    out_weights = attn_slices(
-        out_own,
-        out_other,
-        places,
-        info,
-        jnp.ones((1, 2 * half_out), f32),
-        output_scale,
-        count,
-    )
-    own_gate_scale = lax.dynamic_slice_in_dim(
-        inverse_powers(gate_exps), wide_index * hidden, hidden, 1
-    )
-    down_scale = inverse_powers(down_exps)
-    mlp_weights = mlp_slices(
-        mlp_codes,
-        info,
-        jnp.concatenate([jnp.ones((2, 1, model_dim), f32), down_scale[None, None]], axis=0),
-        jnp.concatenate([own_gate_scale, jnp.ones((1, hidden), f32)], axis=0)[:, :, None],
-        count,
-    )
-    pair_weights = [w[:2].reshape(2 * hidden, model_dim) for w in mlp_weights]
-    down_weights = [w[2] for w in mlp_weights]
+    proj_own, proj_other, ring_tokens = gather_columns(0, half_proj)
+    out_own, out_other, out_tokens = gather_columns(proj_cols, half_out, ring_tokens)
+    seq_bits = [1 << i for i in range(seq_size.bit_length() - 1)]
+    relative = [0]
+    for bit in reversed(seq_bits):
+        relative = relative + [r | bit for r in relative]
+    pieces = jnp.stack([jnp.bitwise_xor(seq_index, r) for r in relative]).astype(jnp.int32)
+    piece_rows = hidden // seq_size
+    partner = jnp.bitwise_xor(wide_index, half_wide)
+    gate_scale = inverse_powers(gate_exps)
+    row_scale = jnp.concatenate(
+        [
+            lax.dynamic_slice_in_dim(
+                gate_scale, block * hidden + pieces[j] * piece_rows, piece_rows, 1
+            )
+            for block in (wide_index, partner)
+            for j in range(seq_size)
+        ],
+        axis=1,
+    )[:, :, None]
+    down_scale = inverse_powers(down_exps)[None, :]
+    own_weights = own_slices(mlp_codes, pieces, info, row_scale, down_scale, count)
+    mlp_weights = []
+    token = ring_tokens
+    for m in range(3):
+        sent = lax.dynamic_slice_in_dim(mlp_codes[m], seq_index * piece_rows, piece_rows, 0)
+        sent = after(sent.astype(bf16), *token)
+        held = [swap(sent, "wide", half_wide)]
+        token = (held[0],)
+        for bit in reversed(seq_bits):
+            held = held + [swap(block, "seq", bit) for block in held]
+        mlp_weights.append(
+            partner_slices(
+                held,
+                info,
+                row_scale[m] if m < 2 else down_scale,
+                m == 2,
+                own_weights[m * count : (m + 1) * count],
+            )
+        )
+    gate_weights, up_weights, down_weights = mlp_weights
+    proj_own = after(proj_own, *own_weights)
+    proj_weights = attn_slices(proj_own, proj_other, places, info, column_scale, True, count)
+    out_weights = attn_slices(out_own, out_other, places, info, output_scale, False, count)
 
     cosine, sine = rotary_rows(wide_index * rows + jnp.arange(rows))
 
@@ -508,11 +648,17 @@
             .astype(bf16)
         )
         pair = jnp.transpose(jnp.concatenate([key, value], axis=-1), (1, 0, 2))
-        pair = jnp.broadcast_to(
-            pair[:, None], (KEY_VALUE_HEADS, classes, rows, 2 * HEAD_SIZE)
-        ).reshape(wide, rows, 2 * HEAD_SIZE)
+        pair = heads_all_to_all(pair)
+        held = [pair]
+        for _ in range(classes - 1):
+            held.append(class_ring(held[-1]))
+        held = jnp.stack(held)
+        held = [
+            lax.dynamic_index_in_dim(held, jnp.mod(class_index - c, classes), 0, keepdims=False)
+            for c in range(classes)
+        ]
+        pairs.append(jnp.stack(held, axis=1).reshape(length, 2 * HEAD_SIZE))
         queries.append(all_to_all(rows_to_heads(query)).reshape(wide * class_rows, head_cols))
-        pairs.append(all_to_all(pair).reshape(length, 2 * HEAD_SIZE))
 
     attended, exact, lse = [], [], []
     for s in seqs:
@@ -534,21 +680,23 @@
         middle_factor.append(mid_factor)
         normed_mlp.append((mid * mid_factor * gain_mlp).astype(bf16))
 
-    gathered, gate, up, tanh_gate, hidden_rows, mixed = [], [], [], [], [], []
-    for s in seqs:
-        group = jnp.concatenate(ring_gather(normed_mlp[s], wide), axis=0)
-        both = dot(group, pair_weights[s], NT)
-        gate_s, up_s = both[:, :hidden], both[:, hidden:]
+    def blocks_of(part):
+        return lambda o: part[order[o] * rows : (order[o] + 1) * rows]
+
+    gathered, gate, up, hidden_rows, mixed = [], [], [], [], []
+    for s in seqs:
+        blocks, ring_tokens = ring_gather(
+            after(normed_mlp[s], *ring_tokens) if s else normed_mlp[s], half_wide
+        )
+        gathered.append(jnp.concatenate(blocks, axis=0))
+    for s in seqs:
+        gate_s = dot(gathered[s], gate_weights[s], NT)
+        up_s = dot(gathered[s], up_weights[s], NT)
         bounded = gelu_parts(gate_s)
         hidden_s = (0.5 * gate_s * (1.0 + bounded) * up_s).astype(bf16)
         part = dot(hidden_s, down_weights[s], NN).astype(bf16)
-        order = {o: i for i, o in enumerate(offsets)}
-        mixed.append(
-            ring_scatter(
-                lambda o, part=part: part[order[o] * rows : (order[o] + 1) * rows], rows, wide
-            )
-        )
-        gathered.append(group)
+        total, ring_tokens = ring_scatter(blocks_of(part), rows, half_wide)
+        mixed.append(total)
         gate.append(gate_s)
         up.append(up_s)
         hidden_rows.append(hidden_s)
@@ -561,52 +709,42 @@
         grad_mixed.append(grad.astype(bf16))
         gain_fourth = gain_fourth + gain
 
-    grad_group, grad_pair, grad_normed_mlp = [], [], []
-    for s in seqs:
-        group = jnp.concatenate(ring_gather(grad_mixed[s], wide), axis=0)
-        grad_hidden = dot(group, down_weights[s], NT)
+    grad_group, grad_gate, grad_up, grad_normed_mlp = [], [], [], []
+    for s in seqs:
+        blocks, ring_tokens = ring_gather(
+            after(grad_mixed[s], *ring_tokens) if s else grad_mixed[s], half_wide
+        )
+        grad_group.append(jnp.concatenate(blocks, axis=0))
+    for s in seqs:
+        grad_hidden = dot(grad_group[s], down_weights[s], NT)
         bounded = gelu_parts(gate[s])
         gelu_value = 0.5 * gate[s] * (1.0 + bounded)
         slope = 0.5 * (1.0 + bounded) + 0.5 * gate[s] * (1.0 - bounded * bounded) * gelu_coeff * (
             1.0 + 3.0 * 0.044715 * gate[s] * gate[s]
         )
-        pair = jnp.concatenate(
-            [
-                (grad_hidden * up[s] * slope).astype(bf16),
-                (grad_hidden * gelu_value).astype(bf16),
-            ],
-            axis=1,
-        )
-        part = dot(pair, pair_weights[s], NN).astype(bf16)
-        order = {o: i for i, o in enumerate(offsets)}
-        grad_normed_mlp.append(
-            ring_scatter(
-                lambda o, part=part: part[order[o] * rows : (order[o] + 1) * rows], rows, wide
-            )
-        )
-        grad_group.append(group)
-        grad_pair.append(pair)
-
-    pair_term = sum(dot(grad_pair[s], gathered[s], TN) for s in seqs)
-    down_term = sum(dot(hidden_rows[s], grad_group[s], TN) for s in seqs)
-    half_hidden = hidden // 2
-    mlp_part = jnp.concatenate(
-        [pair_term.reshape(2, hidden, model_dim).astype(bf16), down_term[None].astype(bf16)], axis=0
-    )
-    keep = lax.dynamic_slice_in_dim(mlp_part, side * half_hidden, half_hidden, 1)
-    send = lax.dynamic_slice_in_dim(mlp_part, (1 - side) * half_hidden, half_hidden, 1)
-    total = keep.astype(f32) + swap(send, "seq", 1).astype(f32)
-    bit = 2
-    while bit < seq_size:
-        low = total.astype(bf16)
-        total = low.astype(f32) + swap(low, "seq", bit).astype(f32)
-        bit *= 2
-    low = total.astype(bf16)
-    other = swap(low, "seq", 1)
-    mlp_grad = jnp.concatenate(
-        [jnp.where(is_low, low, other).astype(f32), jnp.where(is_low, other, low).astype(f32)],
-        axis=1,
-    )
+        grad_gate.append((grad_hidden * up[s] * slope).astype(bf16))
+        grad_up.append((grad_hidden * gelu_value).astype(bf16))
+        part = dot(grad_gate[s], gate_weights[s], NN) + dot(grad_up[s], up_weights[s], NN)
+        total, ring_tokens = ring_scatter(blocks_of(part.astype(bf16)), rows, half_wide)
+        grad_normed_mlp.append(total)
+
+    def mlp_gradient(lefts, rights):
+        grad = sum(dot(lefts[s], rights[s], TN) for s in seqs).astype(bf16)
+        grad = grad.reshape(2, hidden, model_dim)
+        for bit in seq_bits:
+            split = grad.reshape(2, 2, grad.shape[1] // 2, model_dim)
+            received = swap(split[:, 1], "seq", bit)
+            grad = (split[:, 0].astype(f32) + received.astype(f32)).astype(bf16)
+        received = swap(grad[1], "wide", half_wide)
+        grad = (grad[0].astype(f32) + received.astype(f32)).astype(bf16)
+        for bit in reversed(seq_bits):
+            grad = jnp.concatenate([grad, swap(grad, "seq", bit)], axis=0)
+        return grad
+
+    down_grad = mlp_gradient(hidden_rows, grad_group)
+    up_grad = mlp_gradient(grad_up, gathered)
+    gate_grad = mlp_gradient(grad_gate, gathered)
+    mlp_grad = unpack([gate_grad, up_grad, down_grad], pieces)
 
     grad_middle, grad_branch, grad_heads = [], [], []
     gain_third = gain_second = 0.0
@@ -632,10 +770,16 @@
         dq = rotate(
             dq.astype(f32).reshape(rows, QUERY_HEADS, HEAD_SIZE) * query_scale, cosine, -sine
         )
-        dkv = all_to_all(dkv.reshape(wide, rows, 2 * HEAD_SIZE)).reshape(
-            KEY_VALUE_HEADS, classes, rows, 2 * HEAD_SIZE
-        )
-        dkv = jnp.transpose(jnp.sum(dkv.astype(f32), axis=1), (1, 0, 2))
+        dkv = dkv.reshape(KEY_VALUE_HEADS, classes, rows, 2 * HEAD_SIZE)
+        total = None
+        for step in range(1, classes + 1):
+            own = lax.dynamic_index_in_dim(
+                dkv, jnp.mod(class_index - step, classes), 1, keepdims=False
+            )
+            total = own if total is None else own.astype(f32) + class_ring(total).astype(f32)
+            total = total.astype(bf16)
+        dkv = heads_all_to_all(total)
+        dkv = jnp.transpose(dkv.astype(f32), (1, 0, 2))
         dk = rotate(dkv[..., :HEAD_SIZE], cosine, -sine)
         grad_query.append(dq.reshape(rows, query_cols).astype(bf16))
         grad_key_value.append(
@@ -652,15 +796,16 @@
         gain_first = gain_first + gain
         grad_tokens.append((grad_middle[s] + grad).astype(bf16))
 
-    def scatter_columns(left, first_half, second_half):
+    def scatter_columns(left, first_half, second_half, earlier=()):
         keep = jnp.where(is_low, first_half, second_half)
         send = jnp.where(is_low, second_half, first_half)
         received = swap(dot(left, send, TN).astype(bf16), "seq", 1)
         part = (dot(left, keep, TN) + received.astype(f32)).astype(bf16)
-        own = ring_scatter(
+        own, tokens = ring_scatter(
             lambda o: lax.dynamic_slice_in_dim(part, index_at(o) * attn_rows, attn_rows, 0),
             attn_rows,
             wide,
+            earlier,
         )
         bit = 2
         while bit < seq_size:
@@ -672,18 +817,7 @@
         return [
             jnp.where(is_low, low, other).astype(f32),
             jnp.where(is_low, other, low).astype(f32),
-        ]
-
-    all_attended = jnp.concatenate(attended, axis=0)
-    out_parts = scatter_columns(
-        jnp.concatenate(grad_branch, axis=0), all_attended[:, :half_out], all_attended[:, half_out:]
-    )
-    proj_parts = scatter_columns(
-        jnp.concatenate(normed, axis=0),
-        jnp.concatenate(grad_query, axis=0),
-        jnp.concatenate(grad_key_value, axis=0),
-    )
-    attn_grad = jnp.concatenate(proj_parts + out_parts, axis=1)
+        ], tokens
 
     gains = jnp.stack([gain_first, gain_second, gain_third, gain_fourth])
     for axis, size in (("seq", seq_size), ("wide", wide)):
@@ -691,6 +825,18 @@
         while bit < size:
             gains = gains + swap(gains, axis, bit)
             bit *= 2
+
+    all_attended = jnp.concatenate(attended, axis=0)
+    out_parts, ring_tokens = scatter_columns(
+        jnp.concatenate(grad_branch, axis=0), all_attended[:, :half_out], all_attended[:, half_out:]
+    )
+    proj_parts, ring_tokens = scatter_columns(
+        jnp.concatenate(normed, axis=0),
+        jnp.concatenate(grad_query, axis=0),
+        jnp.concatenate(grad_key_value, axis=0),
+        ring_tokens,
+    )
+    attn_grad = jnp.concatenate(proj_parts + out_parts, axis=1)
     return (
         jnp.stack(layer_out),
         jnp.stack(grad_tokens),

time: 2160 us -> 2050 us (0.949)
  waiting for transfers between devices: 1070 us -> 767 us
  starting transfers between devices: 199 us -> 317 us
  local copies, waits for them, and re-layouts: 158 us -> 198 us
  matrix products: 398 us -> 436 us
    ppermute x18 -> x10, waiting for transfers between devices: 272 us -> 49.2 us  [ring_gather(): a = lax.ppermute(a, 'wide', up)]
    ppermute x18 -> x10, waiting for transfers between devices: 205 us -> 52.1 us  [ring_scatter(): a = lax.ppermute(a.astype(bf16), 'wide', up)]
    all_to_all x12 -> x8, waiting for transfers between devices: 99.4 us -> 13.3 us  [all_to_all(): lax.all_to_all(value, 'wide', split_axis=0, concat_axis=0, tiled=True)]
    all_to_all x0 -> x4, waiting for transfers between devices: none -> 54.4 us  [heads_all_to_all(): lax.all_to_all(value, 'wide', split_axis=0, concat_axis=0, axis_index_gro...]
    ppermute x6, waiting for transfers between devices: 30 us -> 81.7 us  [ring_gather(): a = lax.ppermute(a[:half], 'wide', up)]
    dot_general x24 -> x30, matrix products: 398 us -> 436 us  [dot(): return lax.dot_general(a, b, (dims, ((), ())), preferred_element_type=f32)]
    ppermute x12 -> x16, waiting for transfers between devices: 31.8 us -> 64.1 us  [the longest x6 46.2 us: ring_scatter(): a = lax.ppermute(far[:half], 'wide', up)]
    squeeze x0 -> x12, local copies, waits for them, and re-layouts: none -> 30.3 us  [the longest x6 26.1 us: mlp_gradient(): received = swap(split[:, 1], 'seq', bit)]
  transfers between devices with their start and end apart: 124 -> 136, of which waited for: 61 -> 48; matrix products, arithmetic and copies ran while one was open for 26% -> 30% of each run, Pallas kernels for 6% -> 7%
where the time goes in v2:
time: 2050 us; the launch traced here: 2040 us
  waiting for transfers between devices  767 us (37%)
  matrix products  436 us (21%)
  starting transfers between devices  317 us (15%)
  local copies, waits for them, and re-layouts  198 us (10%)
  Pallas kernels  178 us (9%)
  other arithmetic  143 us (7%)
    dot_general x30, matrix products, dot(): return lax.dot_general(a, b, (dims, ((), ())), preferred_element_type=f32)  436 us
    ppermute x56, waiting for transfers between devices, swap(): return lax.ppermute(value, axis, [(i, i ^ bit) for i in range(size)])  222 us
    ppermute x10, waiting for transfers between devices, ring_scatter(): b = lax.ppermute(b.astype(bf16), 'wide', down)  132 us
    ppermute x10, waiting for transfers between devices, ring_gather(): b = lax.ppermute(b, 'wide', down)  97.8 us
    ppermute x6, waiting for transfers between devices, ring_gather(): a = lax.ppermute(a[:half], 'wide', up)  81.7 us
    unnamed x354, local copies, waits for them, and re-layouts  77.6 us
    all_to_all x8, starting transfers between devices, all_to_all(): lax.all_to_all(value, 'wide', split_axis=0, concat_axis=0, tiled=True)  67.7 us
    all_to_all x4, waiting for transfers between devices, heads_all_to_all(): lax.all_to_all(value, 'wide', split_axis=0, concat_axis=0, axis_index_gro...  54.4 us
  transfers between devices with their start and end apart: 136, of which 48 were waited for; matrix products, arithmetic and copies ran while one was open for 30% of the time, Pallas kernels for 7%

profile of v2, /device:TPU:0, one launch (start us, length us, event | category | flops | bytes accessed | tf_op | source)
XLA Modules:
  0.0 2043.5 jit_solution(11852510072407183770)
XLA Ops:
  11.6 25.3 %own_slices.1 = (bf16[2304,2304]{1,0:T(8,128)(2,1)}, bf16[2304,2304]{1,0:T(8,128)(2,1)}, bf16[2304,2304]{1,0:T(8,128)(2,1)}, bf16[2304,2304]{1,0:T(8,128)(2,1)},...) custom-call(s32[4]{0:T(128)} %pad_add_fusion.1.pieces, s32[3]{0:T(128)} %pad_add_fusion.info, ...), custom_call_target="tpu_custom_call" | custom-call | flops 159252480 | bytes 63700992 | tf_op jit(solution)/shard_map/own_slices/pallas_call | solution.py:236
  47.7 20.3 collective-permute-done.3
  77.4 17.7 collective-permute-done.5
  116.1 31.4 %attn_slices.2 = (bf16[2304,4096]{1,0:T(8,128)(2,1)}, bf16[2304,4096]{1,0:T(8,128)(2,1)}) custom-call(s32[8]{0:T(128)} %stack.111.places, s32[3]{0:T(128)} %pad_add_fusion.info, bf16[8,288,2048]{2,1,0:T(8,128)(2,1)} %bitcast.314, bf16[8,288,2048]{2,1,0:T(8,128)(2,1)} %bitcast.18.other_ref, f32[1,4096]{1,0:T(1,128)} %bitcast.394), custom_call_target="tpu_custom_call" | custom-call | flops 94371840 | bytes 56623104 | tf_op jit(solution)/shard_map/attn_slices/pallas_call | solution.py:199
  182.8 23.0 %all-to-all-done.1 = bf16[4,256,512]{2,1,0:T(8,128)(2,1)S(1)} async-done(((bf16[4,256,512]{2,1,0:T(8,128)(2,1)}), bf16[4,256,512]{2,1,0:T(8,128)(2,1)S(1)}, u32[]{:S(2)}, u32[]{:S(2)}) %all-to-all-start.1) | async-done | bytes 1048608 | tf_op jit(solution)/shard_map/all_to_all | solution.py:152
  239.0 21.9 %fusion.119 = (s32[1,1152,2304]{2,1,0:T(8,128)}, s32[1,1152,2304]{2,1,0:T(8,128)}, s32[1,1152,2304]{2,1,0:T(8,128)}) fusion(s32[3,1152,2304]{2,1,0:T(8,128)} %code_ref.1), kind=kLoop, calls=%fused_computation.420 | loop fusion | bytes 63700992 | tf_op jit(solution)/shard_map/slice | solution.py:596
  291.7 34.7 %collective-permute-done.18 = bf16[288,1024]{1,0:T(8,128)(2,1)} collective-permute-done((bf16[288,1024]{1,0:T(8,128)(2,1)}, bf16[288,1024]{1,0:T(8,128)(2,1)}, u32[]{:S(2)}, u32[]{:S(2)}) %collective-permute-start.18) | collective-permute-done | bytes 589856 | tf_op jit(solution)/shard_map/ppermute | solution.py:105
  328.4 20.6 %collective-permute-done.21 = bf16[288,1024]{1,0:T(8,128)(2,1)} collective-permute-done((bf16[288,1024]{1,0:T(8,128)(2,1)}, bf16[288,1024]{1,0:T(8,128)(2,1)}, u32[]{:S(2)}, u32[]{:S(2)}) %collective-permute-start.21) | collective-permute-done | bytes 589856 | tf_op jit(solution)/shard_map/ppermute | solution.py:106
  348.9 25.5 %collective-permute-start.20 = (bf16[288,1024]{1,0:T(8,128)(2,1)}, bf16[288,1024]{1,0:T(8,128)(2,1)}, u32[]{:S(2)}, u32[]{:S(2)}) collective-permute-start(bf16[288,1024]{1,0:T(8,128)(2,1)} %collective-permute-done.18), channel_id=1, source_target_pairs={{0,8},{8,16},{16,24},{24,28},{28,20},{20,12},{12,4},{4,0},{1,9},{9... | collective-permute-start | bytes 1769480 | tf_op jit(solution)/shard_map/ppermute | solution.py:105
  399.3 18.5 collective-permute-start.22
  450.1 20.2 collective-permute-start.25
  505.6 34.0 %all-to-all-start.5 = ((bf16[8,128,512]{2,1,0:T(8,128)(2,1)}), bf16[8,128,512]{2,1,0:T(8,128)(2,1)S(1)}, u32[]{:S(2)}, u32[]{:S(2)}) async-start(bf16[8,128,512]{2,1,0:T(8,128)(2,1)} %bitcast.371), calls=%async_computation.5 | async-start | bytes 2097152 | tf_op jit(solution)/shard_map/all_to_all | solution.py:145
  548.6 20.3 attn_slices.3
  645.3 31.5 %collective-permute-done.37 = bf16[128,2304]{1,0:T(8,128)(2,1)S(1)} collective-permute-done((bf16[128,2304]{1,0:T(8,128)(2,1)S(1)}, bf16[128,2304]{1,0:T(8,128)(2,1)S(1)}, u32[]{:S(2)}, u32[]{:S(2)}) %collective-permute-start.37) | collective-permute-done | bytes 589856 | tf_op jit(solution)/shard_map/ppermute | solution.py:109
  676.9 16.9 fusion.126
  693.9 21.3 %multiply_convert_fusion.3 = (bf16[1024,2304]{1,0:T(8,128)(2,1)}, f32[1024,2304]{1,0:T(8,128)}) fusion(f32[1024,2304]{1,0:T(8,128)} %fusion.126, bf16[1024,2304]{1,0:T(8,128)(2,1)} %copy-done.82, bf16[2304,2304]{1,0:T(8,128)(2,1)} %get-tuple-element.56), kind=kOutput, calls=%fused_computation.35 | convolution fusion | flops 10895228928 | bytes 38928384 | tf_op jit(solution)/shard_map/dot_general | solution.py:26
  715.2 15.1 convolution_convert_fusion.3
  758.6 17.0 fusion.128
  775.6 21.4 %multiply_convert_fusion.2 = (bf16[1024,2304]{1,0:T(8,128)(2,1)}, f32[1024,2304]{1,0:T(8,128)}) fusion(f32[1024,2304]{1,0:T(8,128)} %fusion.128, bf16[1024,2304]{1,0:T(8,128)(2,1)} %copy-done.78, bf16[2304,2304]{1,0:T(8,128)(2,1)} %get-tuple-element.64), kind=kOutput, calls=%fused_computation.34 | convolution fusion | flops 10895228928 | bytes 38928384 | tf_op jit(solution)/shard_map/dot_general | solution.py:26
  832.4 22.7 %collective-permute-done.54 = bf16[256,2304]{1,0:T(8,128)(2,1)S(1)} collective-permute-done((bf16[256,2304]{1,0:T(8,128)(2,1)S(1)}, bf16[256,2304]{1,0:T(8,128)(2,1)S(1)}, u32[]{:S(2)}, u32[]{:S(2)}) %collective-permute-start.54) | collective-permute-done | bytes 1179680 | tf_op jit(solution)/shard_map/ppermute | solution.py:135
  855.7 20.9 %collective-permute-done.63 = bf16[256,2304]{1,0:T(8,128)(2,1)S(1)} collective-permute-done((bf16[256,2304]{1,0:T(8,128)(2,1)S(1)}, bf16[256,2304]{1,0:T(8,128)(2,1)S(1)}, u32[]{:S(2)}, u32[]{:S(2)}) %collective-permute-start.63) | collective-permute-done | bytes 1179680 | tf_op jit(solution)/shard_map/ppermute | solution.py:135
  890.7 18.5 collective-permute-done.65
  924.6 27.6 %fusion.11 = (bf16[1024,2304]{1,0:T(8,128)(2,1)}, bf16[1024,2304]{1,0:T(8,128)(2,1)}) fusion(f32[1024,2304]{1,0:T(8,128)} %fusion.126, f32[1024,2304]{1,0:T(8,128)} %get-tuple-element.230, bf16[1024,2304]{1,0:T(8,128)(2,1)} %constant_dynamic-update-slice_fusion.46, bf16[2304,2304]{1,0:T(8,128)(2,1)} %get-tuple-element.58), kind=kOutput, calls=%fused_computation.23 | convolution fusion | flops 10925899776 | bytes 43646976 | tf_op jit(solution)/shard_map/dot_general | solution.py:26
  967.2 15.0 add_convert_fusion.6
  1003.9 20.8 %collective-permute-done.74 = bf16[256,2304]{1,0:T(8,128)(2,1)S(1)} collective-permute-done((bf16[256,2304]{1,0:T(8,128)(2,1)S(1)}, bf16[256,2304]{1,0:T(8,128)(2,1)S(1)}, u32[]{:S(2)}, u32[]{:S(2)}) %collective-permute-start.74) | collective-permute-done | bytes 1179680 | tf_op jit(solution)/shard_map/ppermute | solution.py:106
  1027.0 28.7 %collective-permute-done.75 = bf16[128,2304]{1,0:T(8,128)(2,1)S(1)} collective-permute-done((bf16[128,2304]{1,0:T(8,128)(2,1)S(1)}, bf16[128,2304]{1,0:T(8,128)(2,1)S(1)}, u32[]{:S(2)}, u32[]{:S(2)}) %collective-permute-start.75) | collective-permute-done | bytes 589856 | tf_op jit(solution)/shard_map/ppermute | solution.py:109
  1070.9 27.3 %fusion.16 = (bf16[1024,2304]{1,0:T(8,128)(2,1)}, bf16[1024,2304]{1,0:T(8,128)(2,1)}) fusion(f32[1024,2304]{1,0:T(8,128)} %fusion.128, f32[1024,2304]{1,0:T(8,128)} %get-tuple-element.232, bf16[1024,2304]{1,0:T(8,128)(2,1)} %copy-done.79, bf16[2304,2304]{1,0:T(8,128)(2,1)} %get-tuple-element.65), kind=kOutput, calls=%fused_computation.28 | convolution fusion | flops 10925899776 | bytes 43646976 | tf_op jit(solution)/shard_map/dot_general | solution.py:26
  1098.3 17.8 fusion.130
  1116.1 17.2 fusion.132
  1133.3 15.1 fusion.131
  1167.2 20.0 add_convert_fusion
  1192.4 19.9 add_convert_fusion.2
  1225.1 17.4 collective-permute-done.80
  1264.9 20.0 add_convert_fusion.1
  1306.8 17.4 attn_backward.3
  1330.3 17.4 attn_backward.2
  1372.8 15.1 collective-permute-done.72
  1586.5 34.7 %collective-permute-done.105 = bf16[2,288,2304]{2,1,0:T(8,128)(2,1)S(1)} collective-permute-done((bf16[2,288,2304]{2,1,0:T(8,128)(2,1)S(1)}, bf16[2,288,2304]{2,1,0:T(8,128)(2,1)S(1)}, u32[]{:S(2)}, u32[]{:S(2)}) %collective-permute-start.105) | collective-permute-done | bytes 2654240 | tf_op jit(solution)/shard_map/ppermute | solution.py:141
  1623.6 51.7 %collective-permute-done.110 = bf16[2,288,2304]{2,1,0:T(8,128)(2,1)} collective-permute-done((bf16[2,288,2304]{2,1,0:T(8,128)(2,1)S(1)}, bf16[2,288,2304]{2,1,0:T(8,128)(2,1)}, u32[]{:S(2)}, u32[]{:S(2)}) %collective-permute-start.110) | collective-permute-done | bytes 2654240 | tf_op jit(solution)/shard_map/ppermute | solution.py:141
  1713.5 46.0 %collective-permute-done.89 = bf16[288,2048]{1,0:T(8,128)(2,1)S(1)} collective-permute-done((bf16[288,2048]{1,0:T(8,128)(2,1)S(1)}, bf16[288,2048]{1,0:T(8,128)(2,1)S(1)}, u32[]{:S(2)}, u32[]{:S(2)}) %collective-permute-start.89) | collective-permute-done | bytes 1179680 | tf_op jit(solution)/shard_map/ppermute | solution.py:134
  1769.6 49.5 %collective-permute-done.116 = bf16[288,2304]{1,0:T(8,128)(2,1)S(1)} collective-permute-done((bf16[288,2304]{1,0:T(8,128)(2,1)S(1)}, bf16[288,2304]{1,0:T(8,128)(2,1)S(1)}, u32[]{:S(2)}, u32[]{:S(2)}) %collective-permute-start.116) | collective-permute-done | bytes 1327136 | tf_op jit(solution)/shard_map/ppermute | solution.py:141
  1819.1 24.5 %collective-permute-start.90 = (bf16[288,2048]{1,0:T(8,128)(2,1)S(1)}, bf16[288,2048]{1,0:T(8,128)(2,1)S(1)}, u32[]{:S(2)}, u32[]{:S(2)}) collective-permute-start(bf16[288,2048]{1,0:T(8,128)(2,1)S(1)} %add_convert_fusion.12), channel_id=1, source_target_pairs={{0,8},{8,16},{16,24},{24,28},{28,20},{20,12},{12,4},{4,0},{1,9},{9... | collective-permute-start | bytes 3538952 | tf_op jit(solution)/shard_map/ppermute | solution.py:134
  1848.2 52.1 %collective-permute-done.93 = bf16[288,2048]{1,0:T(8,128)(2,1)S(1)} collective-permute-done((bf16[288,2048]{1,0:T(8,128)(2,1)S(1)}, bf16[288,2048]{1,0:T(8,128)(2,1)S(1)}, u32[]{:S(2)}, u32[]{:S(2)}) %collective-permute-start.93) | collective-permute-done | bytes 1179680 | tf_op jit(solution)/shard_map/ppermute | solution.py:135
  1904.3 24.3 %collective-permute-start.94 = (bf16[288,2048]{1,0:T(8,128)(2,1)S(1)}, bf16[288,2048]{1,0:T(8,128)(2,1)S(1)}, u32[]{:S(2)}, u32[]{:S(2)}) collective-permute-start(bf16[288,2048]{1,0:T(8,128)(2,1)S(1)} %get-tuple-element.122), channel_id=1, source_target_pairs={{8,0},{16,8},{24,16},{28,24},{20,28},{12,20},{4,12},{0,4},{9,1},{1... | collective-permute-start | bytes 3538952 | tf_op jit(solution)/shard_map/ppermute | solution.py:135
  1934.5 19.2 collective-permute-done.94
  1960.9 27.3 %collective-permute-done.112 = bf16[288,2304]{1,0:T(8,128)(2,1)S(1)} collective-permute-done((bf16[288,2304]{1,0:T(8,128)(2,1)S(1)}, bf16[288,2304]{1,0:T(8,128)(2,1)S(1)}, u32[]{:S(2)}, u32[]{:S(2)}) %collective-permute-start.112) | collective-permute-done | bytes 1327136 | tf_op jit(solution)/shard_map/ppermute | solution.py:141
  1992.8 24.7 %collective-permute-done.96 = bf16[288,2048]{1,0:T(8,128)(2,1)S(1)} collective-permute-done((bf16[288,2048]{1,0:T(8,128)(2,1)S(1)}, bf16[288,2048]{1,0:T(8,128)(2,1)S(1)}, u32[]{:S(2)}, u32[]{:S(2)}) %collective-permute-start.96) | collective-permute-done | bytes 1179680 | tf_op jit(solution)/shard_map/ppermute | solution.py:141
  2023.7 16.1 unpack.1
  (848 shorter events, 874.6 us)
Async XLA Ops:
  3.7 66.3 %collective-permute-start.8 = (bf16[288,2048]{1,0:T(8,128)(2,1)S(1)}, bf16[288,2048]{1,0:T(8,128)(2,1)}, u32[]{:S(2)}, u32[]{:S(2)}) collective-permute-start(bf16[288,2048]{1,0:T(8,128)(2,1)S(1)} %get-tuple-element.113), channel_id=1, source_target_pairs={{0,1},{1,0},{2,3},{3,2},{4,5},{5,4},{6,7},{7,6},{8,9},{9,8},{10,11... | collective-permute-start | bytes 3538952 | tf_op jit(solution)/shard_map/ppermute | solution.py:141
  268.0 106.4 %collective-permute-start.39 = (bf16[288,2304]{1,0:T(8,128)(2,1)}, bf16[288,2304]{1,0:T(8,128)(2,1)}, u32[]{:S(2)}, u32[]{:S(2)}) collective-permute-start(bf16[288,2304]{1,0:T(8,128)(2,1)} %fusion.79), channel_id=1, source_target_pairs={{0,16},{4,20},{8,24},{12,28},{16,0},{20,4},{24,8},{28,12},{1,17},{... | collective-permute-start | bytes 3981320 | tf_op jit(solution)/shard_map/ppermute | solution.py:141
  273.6 100.8 %collective-permute-start.17 = (bf16[4,256,512]{2,1,0:T(8,128)(2,1)S(1)}, bf16[4,256,512]{2,1,0:T(8,128)(2,1)S(1)}, u32[]{:S(2)}, u32[]{:S(2)}) collective-permute-start(bf16[4,256,512]{2,1,0:T(8,128)(2,1)S(1)} %copy-done.36), channel_id=1, source_target_pairs={{0,4},{4,0},{8,12},{12,8},{16,20},{20,16},{24,28},{28,24},{1,5},{5... | collective-permute-start | bytes 3145736 | tf_op jit(solution)/shard_map/ppermute | solution.py:161
  276.0 117.7 %all-to-all-start.3 = ((bf16[8,128,512]{2,1,0:T(8,128)(2,1)}), bf16[8,128,512]{2,1,0:T(8,128)(2,1)}, u32[]{:S(2)}, u32[]{:S(2)}) async-start(bf16[8,128,512]{2,1,0:T(8,128)(2,1)} %bitcast.43), calls=%async_computation.3 | async-start | bytes 2097152 | tf_op jit(solution)/shard_map/all_to_all | solution.py:145
  286.6 62.3 %collective-permute-start.21 = (bf16[288,1024]{1,0:T(8,128)(2,1)}, bf16[288,1024]{1,0:T(8,128)(2,1)}, u32[]{:S(2)}, u32[]{:S(2)}) collective-permute-start(bf16[288,1024]{1,0:T(8,128)(2,1)} %collective-permute-done.19), channel_id=1, source_target_pairs={{8,0},{16,8},{24,16},{28,24},{20,28},{12,20},{4,12},{0,4},{9,1},{1... | collective-permute-start | bytes 1769480 | tf_op jit(solution)/shard_map/ppermute | solution.py:106
  291.6 99.3 %collective-permute-start.28 = (bf16[288,1024]{1,0:T(8,128)(2,1)}, bf16[288,1024]{1,0:T(8,128)(2,1)}, u32[]{:S(2)}, u32[]{:S(2)}) collective-permute-start(bf16[288,1024]{1,0:T(8,128)(2,1)} %collective-permute-done.19), channel_id=1, source_target_pairs={{0,1},{1,0},{2,3},{3,2},{4,5},{5,4},{6,7},{7,6},{8,9},{9,8},{10,11... | collective-permute-start | bytes 1769480 | tf_op jit(solution)/shard_map/ppermute | solution.py:141
  326.4 95.2 %collective-permute-start.27 = (bf16[288,1024]{1,0:T(8,128)(2,1)}, bf16[288,1024]{1,0:T(8,128)(2,1)}, u32[]{:S(2)}, u32[]{:S(2)}) collective-permute-start(bf16[288,1024]{1,0:T(8,128)(2,1)} %collective-permute-done.18), channel_id=1, source_target_pairs={{0,1},{1,0},{2,3},{3,2},{4,5},{5,4},{6,7},{7,6},{8,9},{9,8},{10,11... | collective-permute-start | bytes 1769480 | tf_op jit(solution)/shard_map/ppermute | solution.py:141
  348.9 50.3 %collective-permute-start.20 = (bf16[288,1024]{1,0:T(8,128)(2,1)}, bf16[288,1024]{1,0:T(8,128)(2,1)}, u32[]{:S(2)}, u32[]{:S(2)}) collective-permute-start(bf16[288,1024]{1,0:T(8,128)(2,1)} %collective-permute-done.18), channel_id=1, source_target_pairs={{0,8},{8,16},{16,24},{24,28},{28,20},{20,12},{12,4},{4,0},{1,9},{9... | collective-permute-start | bytes 1769480 | tf_op jit(solution)/shard_map/ppermute | solution.py:105
  374.4 51.0 %collective-permute-start.23 = (bf16[288,1024]{1,0:T(8,128)(2,1)}, bf16[288,1024]{1,0:T(8,128)(2,1)}, u32[]{:S(2)}, u32[]{:S(2)}) collective-permute-start(bf16[288,1024]{1,0:T(8,128)(2,1)} %collective-permute-done.21), channel_id=1, source_target_pairs={{8,0},{16,8},{24,16},{28,24},{20,28},{12,20},{4,12},{0,4},{9,1},{1... | collective-permute-start | bytes 1769480 | tf_op jit(solution)/shard_map/ppermute | solution.py:106
  374.5 96.7 %collective-permute-start.43 = (bf16[288,2304]{1,0:T(8,128)(2,1)}, bf16[288,2304]{1,0:T(8,128)(2,1)}, u32[]{:S(2)}, u32[]{:S(2)}) collective-permute-start(bf16[288,2304]{1,0:T(8,128)(2,1)} %fusion.80), channel_id=1, source_target_pairs={{0,16},{4,20},{8,24},{12,28},{16,0},{20,4},{24,8},{28,12},{1,17},{... | collective-permute-start | bytes 3981320 | tf_op jit(solution)/shard_map/ppermute | solution.py:141
  390.9 94.3 %collective-permute-start.55 = (bf16[4,256,512]{2,1,0:T(8,128)(2,1)S(1)}, bf16[4,256,512]{2,1,0:T(8,128)(2,1)S(1)}, u32[]{:S(2)}, u32[]{:S(2)}) collective-permute-start(bf16[4,256,512]{2,1,0:T(8,128)(2,1)S(1)} %all-to-all-done.4), channel_id=1, source_target_pairs={{0,4},{4,0},{8,12},{12,8},{16,20},{20,16},{24,28},{28,24},{1,5},{5... | collective-permute-start | bytes 3145736 | tf_op jit(solution)/shard_map/ppermute | solution.py:161
  393.8 111.8 %all-to-all-start.2 = ((bf16[8,128,512]{2,1,0:T(8,128)(2,1)}), bf16[8,128,512]{2,1,0:T(8,128)(2,1)S(1)}, u32[]{:S(2)}, u32[]{:S(2)}) async-start(bf16[8,128,512]{2,1,0:T(8,128)(2,1)} %bitcast.369), calls=%async_computation.2 | async-start | bytes 2097152 | tf_op jit(solution)/shard_map/all_to_all | solution.py:145
  425.5 65.7 %collective-permute-start.30 = (bf16[288,1024]{1,0:T(8,128)(2,1)}, bf16[288,1024]{1,0:T(8,128)(2,1)S(1)}, u32[]{:S(2)}, u32[]{:S(2)}) collective-permute-start(bf16[288,1024]{1,0:T(8,128)(2,1)} %collective-permute-done.21), channel_id=1, source_target_pairs={{0,1},{1,0},{2,3},{3,2},{4,5},{5,4},{6,7},{7,6},{8,9},{9,8},{10,11... | collective-permute-start | bytes 1769480 | tf_op jit(solution)/shard_map/ppermute | solution.py:141
  443.4 125.9 %collective-permute-start.40 = (bf16[288,2304]{1,0:T(8,128)(2,1)}, bf16[288,2304]{1,0:T(8,128)(2,1)}, u32[]{:S(2)}, u32[]{:S(2)}) collective-permute-start(bf16[288,2304]{1,0:T(8,128)(2,1)} %collective-permute-done.39.refs_0_), channel_id=1, source_target_pairs={{0,2},{1,3},{2,0},{3,1},{4,6},{5,7},{6,4},{7,5},{8,10},{9,11},{10,... | collective-permute-start | bytes 3981320 | tf_op jit(solution)/shard_map/ppermute | solution.py:141
  485.2 84.1 %collective-permute-start.47 = (bf16[288,2304]{1,0:T(8,128)(2,1)}, bf16[288,2304]{1,0:T(8,128)(2,1)}, u32[]{:S(2)}, u32[]{:S(2)}) collective-permute-start(bf16[288,2304]{1,0:T(8,128)(2,1)} %fusion.81), channel_id=1, source_target_pairs={{0,16},{4,20},{8,24},{12,28},{16,0},{20,4},{24,8},{28,12},{1,17},{... | collective-permute-start | bytes 3981320 | tf_op jit(solution)/shard_map/ppermute | solution.py:141
  491.2 78.3 %collective-permute-start.44 = (bf16[288,2304]{1,0:T(8,128)(2,1)}, bf16[288,2304]{1,0:T(8,128)(2,1)}, u32[]{:S(2)}, u32[]{:S(2)}) collective-permute-start(bf16[288,2304]{1,0:T(8,128)(2,1)} %collective-permute-done.43.refs_0_), channel_id=1, source_target_pairs={{0,2},{1,3},{2,0},{3,1},{4,6},{5,7},{6,4},{7,5},{8,10},{9,11},{10,... | collective-permute-start | bytes 3981320 | tf_op jit(solution)/shard_map/ppermute | solution.py:141
  493.6 48.5 %collective-permute-start.32 = (bf16[288,1024]{1,0:T(8,128)(2,1)}, bf16[288,1024]{1,0:T(8,128)(2,1)S(1)}, u32[]{:S(2)}, u32[]{:S(2)}) collective-permute-start(bf16[288,1024]{1,0:T(8,128)(2,1)} %collective-permute-done.23), channel_id=1, source_target_pairs={{0,1},{1,0},{2,3},{3,2},{4,5},{5,4},{6,7},{7,6},{8,9},{9,8},{10,11... | collective-permute-start | bytes 1769480 | tf_op jit(solution)/shard_map/ppermute | solution.py:141
  493.6 50.2 %collective-permute-start.31 = (bf16[288,1024]{1,0:T(8,128)(2,1)}, bf16[288,1024]{1,0:T(8,128)(2,1)}, u32[]{:S(2)}, u32[]{:S(2)}) collective-permute-start(bf16[288,1024]{1,0:T(8,128)(2,1)} %collective-permute-done.22), channel_id=1, source_target_pairs={{0,1},{1,0},{2,3},{3,2},{4,5},{5,4},{6,7},{7,6},{8,9},{9,8},{10,11... | collective-permute-start | bytes 1769480 | tf_op jit(solution)/shard_map/ppermute | solution.py:141
  505.6 73.6 %all-to-all-start.5 = ((bf16[8,128,512]{2,1,0:T(8,128)(2,1)}), bf16[8,128,512]{2,1,0:T(8,128)(2,1)S(1)}, u32[]{:S(2)}, u32[]{:S(2)}) async-start(bf16[8,128,512]{2,1,0:T(8,128)(2,1)} %bitcast.371), calls=%async_computation.5 | async-start | bytes 2097152 | tf_op jit(solution)/shard_map/all_to_all | solution.py:145
  634.6 99.0 %collective-permute-start.57 = (bf16[256,2304]{1,0:T(8,128)(2,1)S(1)}, bf16[256,2304]{1,0:T(8,128)(2,1)S(1)}, u32[]{:S(2)}, u32[]{:S(2)}) collective-permute-start(bf16[256,2304]{1,0:T(8,128)(2,1)S(1)} %multiply_convert_fusion.4), channel_id=1, source_target_pairs={{8,0},{12,8},{4,12},{0,4},{24,16},{28,24},{20,28},{16,20},{9,1},{1... | collective-permute-start | bytes 3538952 | tf_op jit(solution)/shard_map/ppermute | solution.py:106
  636.6 98.5 %collective-permute-start.56 = (bf16[256,2304]{1,0:T(8,128)(2,1)S(1)}, bf16[256,2304]{1,0:T(8,128)(2,1)S(1)}, u32[]{:S(2)}, u32[]{:S(2)}) collective-permute-start(bf16[256,2304]{1,0:T(8,128)(2,1)S(1)} %multiply_convert_fusion.4), channel_id=1, source_target_pairs={{0,8},{8,12},{12,4},{4,0},{16,24},{24,28},{28,20},{20,16},{1,9},{9... | collective-permute-start | bytes 3538952 | tf_op jit(solution)/shard_map/ppermute | solution.py:105
  830.2 46.4 %collective-permute-start.63 = (bf16[256,2304]{1,0:T(8,128)(2,1)S(1)}, bf16[256,2304]{1,0:T(8,128)(2,1)S(1)}, u32[]{:S(2)}, u32[]{:S(2)}) collective-permute-start(bf16[256,2304]{1,0:T(8,128)(2,1)S(1)} %pad_maximum_fusion.24), channel_id=1, source_target_pairs={{8,0},{12,8},{4,12},{0,4},{24,16},{28,24},{20,28},{16,20},{9,1},{1... | collective-permute-start | bytes 3538952 | tf_op jit(solution)/shard_map/ppermute | solution.py:135
  1000.7 221.0 %collective-permute-start.71 = (bf16[256,2304]{1,0:T(8,128)(2,1)}, bf16[256,2304]{1,0:T(8,128)(2,1)}, u32[]{:S(2)}, u32[]{:S(2)}) collective-permute-start(bf16[256,2304]{1,0:T(8,128)(2,1)} %pad_maximum_fusion.26), channel_id=1, source_target_pairs={{8,0},{12,8},{4,12},{0,4},{24,16},{28,24},{20,28},{16,20},{9,1},{1... | collective-permute-start | bytes 3538952 | tf_op jit(solution)/shard_map/ppermute | solution.py:135
  1003.4 218.4 %collective-permute-start.69 = (bf16[256,2304]{1,0:T(8,128)(2,1)}, bf16[256,2304]{1,0:T(8,128)(2,1)}, u32[]{:S(2)}, u32[]{:S(2)}) collective-permute-start(bf16[256,2304]{1,0:T(8,128)(2,1)} %pad_maximum_fusion.25), channel_id=1, source_target_pairs={{0,8},{8,12},{12,4},{4,0},{16,24},{24,28},{28,20},{20,16},{1,9},{9... | collective-permute-start | bytes 3538952 | tf_op jit(solution)/shard_map/ppermute | solution.py:134
  1165.1 47.1 %collective-permute-start.77 = (bf16[128,2304]{1,0:T(8,128)(2,1)S(1)}, bf16[128,2304]{1,0:T(8,128)(2,1)S(1)}, u32[]{:S(2)}, u32[]{:S(2)}) collective-permute-start(bf16[128,2304]{1,0:T(8,128)(2,1)S(1)} %get-tuple-element.148), channel_id=1, source_target_pairs={{0,8},{8,12},{12,4},{4,0},{16,24},{24,28},{28,20},{20,16},{1,9},{9... | collective-permute-start | bytes 1769480 | tf_op jit(solution)/shard_map/ppermute | solution.py:120
  1165.7 46.6 %collective-permute-start.79 = (bf16[128,2304]{1,0:T(8,128)(2,1)S(1)}, bf16[128,2304]{1,0:T(8,128)(2,1)S(1)}, u32[]{:S(2)}, u32[]{:S(2)}) collective-permute-start(bf16[128,2304]{1,0:T(8,128)(2,1)S(1)} %get-tuple-element.149), channel_id=1, source_target_pairs={{8,0},{12,8},{4,12},{0,4},{24,16},{28,24},{20,28},{16,20},{9,1},{1... | collective-permute-start | bytes 1769480 | tf_op jit(solution)/shard_map/ppermute | solution.py:121
  1192.4 198.0 %collective-permute-start.114 = (bf16[2,576,2304]{2,1,0:T(8,128)(2,1)}, bf16[2,576,2304]{2,1,0:T(8,128)(2,1)}, u32[]{:S(2)}, u32[]{:S(2)}) collective-permute-start(bf16[2,576,2304]{2,1,0:T(8,128)(2,1)} %slice_bitcast_fusion), channel_id=1, source_target_pairs={{0,1},{1,0},{2,3},{3,2},{4,5},{5,4},{6,7},{7,6},{8,9},{9,8},{10,11... | collective-permute-start | bytes 15925256 | tf_op jit(solution)/shard_map/ppermute | solution.py:141
  1221.7 184.6 %collective-permute-start.104 = (bf16[2,576,2304]{2,1,0:T(8,128)(2,1)}, bf16[2,576,2304]{2,1,0:T(8,128)(2,1)}, u32[]{:S(2)}, u32[]{:S(2)}) collective-permute-start(bf16[2,576,2304]{2,1,0:T(8,128)(2,1)} %slice_bitcast_fusion.4), channel_id=1, source_target_pairs={{0,1},{1,0},{2,3},{3,2},{4,5},{5,4},{6,7},{7,6},{8,9},{9,8},{10,11... | collective-permute-start | bytes 15925256 | tf_op jit(solution)/shard_map/ppermute | solution.py:141
  1306.8 127.5 %collective-permute-start.109 = (bf16[2,576,2304]{2,1,0:T(8,128)(2,1)}, bf16[2,576,2304]{2,1,0:T(8,128)(2,1)}, u32[]{:S(2)}, u32[]{:S(2)}) collective-permute-start(bf16[2,576,2304]{2,1,0:T(8,128)(2,1)} %slice_bitcast_fusion.2), channel_id=1, source_target_pairs={{0,1},{1,0},{2,3},{3,2},{4,5},{5,4},{6,7},{7,6},{8,9},{9,8},{10,11... | collective-permute-start | bytes 15925256 | tf_op jit(solution)/shard_map/ppermute | solution.py:141
  1370.0 156.7 %collective-permute-start.83 = (bf16[2304,1024]{1,0:T(8,128)(2,1)}, bf16[2304,1024]{1,0:T(8,128)(2,1)}, u32[]{:S(2)}, u32[]{:S(2)}) collective-permute-start(bf16[2304,1024]{1,0:T(8,128)(2,1)} %convolution_convert_fusion.1), channel_id=1, source_target_pairs={{0,1},{1,0},{2,3},{3,2},{4,5},{5,4},{6,7},{7,6},{8,9},{9,8},{10,11... | collective-permute-start | bytes 14155784 | tf_op jit(solution)/shard_map/ppermute | solution.py:141
  1406.1 176.0 %collective-permute-start.115 = (bf16[2,288,2304]{2,1,0:T(8,128)(2,1)}, bf16[2,288,2304]{2,1,0:T(8,128)(2,1)}, u32[]{:S(2)}, u32[]{:S(2)}) collective-permute-start(bf16[2,288,2304]{2,1,0:T(8,128)(2,1)} %slice_bitcast_fusion.6), channel_id=1, source_target_pairs={{0,2},{1,3},{2,0},{3,1},{4,6},{5,7},{6,4},{7,5},{8,10},{9,11},{10,... | collective-permute-start | bytes 7962632 | tf_op jit(solution)/shard_map/ppermute | solution.py:141
  1503.0 174.7 %collective-permute-start.82 = (bf16[2304,2048]{1,0:T(8,128)(2,1)}, bf16[2304,2048]{1,0:T(8,128)(2,1)}, u32[]{:S(2)}, u32[]{:S(2)}) collective-permute-start(bf16[2304,2048]{1,0:T(8,128)(2,1)} %convolution_convert_fusion), channel_id=1, source_target_pairs={{0,1},{1,0},{2,3},{3,2},{4,5},{5,4},{6,7},{7,6},{8,9},{9,8},{10,11... | collective-permute-start | bytes 28311560 | tf_op jit(solution)/shard_map/ppermute | solution.py:141
  1560.7 60.5 %collective-permute-start.105 = (bf16[2,288,2304]{2,1,0:T(8,128)(2,1)S(1)}, bf16[2,288,2304]{2,1,0:T(8,128)(2,1)S(1)}, u32[]{:S(2)}, u32[]{:S(2)}) collective-permute-start(bf16[2,288,2304]{2,1,0:T(8,128)(2,1)S(1)} %copy-done.42), channel_id=1, source_target_pairs={{0,2},{1,3},{2,0},{3,1},{4,6},{5,7},{6,4},{7,5},{8,10},{9,11},{10,... | collective-permute-start | bytes 7962632 | tf_op jit(solution)/shard_map/ppermute | solution.py:141
  1576.0 99.3 %collective-permute-start.110 = (bf16[2,288,2304]{2,1,0:T(8,128)(2,1)S(1)}, bf16[2,288,2304]{2,1,0:T(8,128)(2,1)}, u32[]{:S(2)}, u32[]{:S(2)}) collective-permute-start(bf16[2,288,2304]{2,1,0:T(8,128)(2,1)S(1)} %copy-done.43), channel_id=1, source_target_pairs={{0,2},{1,3},{2,0},{3,1},{4,6},{5,7},{6,4},{7,5},{8,10},{9,11},{10,... | collective-permute-start | bytes 7962632 | tf_op jit(solution)/shard_map/ppermute | solution.py:141
  1577.8 355.0 %collective-permute-start.123 = (f32[4,2304]{1,0:T(4,128)S(1)}, f32[4,2304]{1,0:T(4,128)S(1)}, u32[]{:S(2)}, u32[]{:S(2)}) collective-permute-start(f32[4,2304]{1,0:T(4,128)S(1)} %add.803), channel_id=1, source_target_pairs={{0,16},{4,20},{8,24},{12,28},{16,0},{20,4},{24,8},{28,12},{1,17},{... | collective-permute-start | bytes 110600 | tf_op jit(solution)/shard_map/ppermute | solution.py:141
  1582.1 126.5 %collective-permute-start.99 = (bf16[288,1024]{1,0:T(8,128)(2,1)}, bf16[288,1024]{1,0:T(8,128)(2,1)}, u32[]{:S(2)}, u32[]{:S(2)}) collective-permute-start(bf16[288,1024]{1,0:T(8,128)(2,1)} %get-tuple-element.130), channel_id=1, source_target_pairs={{0,8},{8,16},{16,24},{24,28},{28,20},{20,12},{12,4},{4,0},{1,9},{9... | collective-permute-start | bytes 1769480 | tf_op jit(solution)/shard_map/ppermute | solution.py:134
  1621.2 89.6 %collective-permute-start.101 = (bf16[288,1024]{1,0:T(8,128)(2,1)}, bf16[288,1024]{1,0:T(8,128)(2,1)}, u32[]{:S(2)}, u32[]{:S(2)}) collective-permute-start(bf16[288,1024]{1,0:T(8,128)(2,1)} %get-tuple-element.131), channel_id=1, source_target_pairs={{8,0},{16,8},{24,16},{28,24},{20,28},{12,20},{4,12},{0,4},{9,1},{1... | collective-permute-start | bytes 1769480 | tf_op jit(solution)/shard_map/ppermute | solution.py:135
  1704.6 114.5 %collective-permute-start.116 = (bf16[288,2304]{1,0:T(8,128)(2,1)S(1)}, bf16[288,2304]{1,0:T(8,128)(2,1)S(1)}, u32[]{:S(2)}, u32[]{:S(2)}) collective-permute-start(bf16[288,2304]{1,0:T(8,128)(2,1)S(1)} %copy-done.52), channel_id=1, source_target_pairs={{0,16},{4,20},{8,24},{12,28},{16,0},{20,4},{24,8},{28,12},{1,17},{... | collective-permute-start | bytes 3981320 | tf_op jit(solution)/shard_map/ppermute | solution.py:141
  1706.8 52.7 %collective-permute-start.89 = (bf16[288,2048]{1,0:T(8,128)(2,1)S(1)}, bf16[288,2048]{1,0:T(8,128)(2,1)S(1)}, u32[]{:S(2)}, u32[]{:S(2)}) collective-permute-start(bf16[288,2048]{1,0:T(8,128)(2,1)S(1)} %pad_maximum_fusion.29), channel_id=1, source_target_pairs={{0,8},{8,16},{16,24},{24,28},{28,20},{20,12},{12,4},{4,0},{1,9},{9... | collective-permute-start | bytes 3538952 | tf_op jit(solution)/shard_map/ppermute | solution.py:134
  1708.6 139.0 %collective-permute-start.106 = (bf16[288,2304]{1,0:T(8,128)(2,1)S(1)}, bf16[288,2304]{1,0:T(8,128)(2,1)S(1)}, u32[]{:S(2)}, u32[]{:S(2)}) collective-permute-start(bf16[288,2304]{1,0:T(8,128)(2,1)S(1)} %slice_bitcast_fusion.16), channel_id=1, source_target_pairs={{0,16},{4,20},{8,24},{12,28},{16,0},{20,4},{24,8},{28,12},{1,17},{... | collective-permute-start | bytes 3981320 | tf_op jit(solution)/shard_map/ppermute | solution.py:141
  1710.8 193.4 %collective-permute-start.111 = (bf16[288,2304]{1,0:T(8,128)(2,1)S(1)}, bf16[288,2304]{1,0:T(8,128)(2,1)S(1)}, u32[]{:S(2)}, u32[]{:S(2)}) collective-permute-start(bf16[288,2304]{1,0:T(8,128)(2,1)S(1)} %slice_bitcast_fusion.14), channel_id=1, source_target_pairs={{0,16},{4,20},{8,24},{12,28},{16,0},{20,4},{24,8},{28,12},{1,17},{... | collective-permute-start | bytes 3981320 | tf_op jit(solution)/shard_map/ppermute | solution.py:141
  1759.4 140.9 %collective-permute-start.93 = (bf16[288,2048]{1,0:T(8,128)(2,1)S(1)}, bf16[288,2048]{1,0:T(8,128)(2,1)S(1)}, u32[]{:S(2)}, u32[]{:S(2)}) collective-permute-start(bf16[288,2048]{1,0:T(8,128)(2,1)S(1)} %pad_maximum_fusion.30), channel_id=1, source_target_pairs={{8,0},{16,8},{24,16},{28,24},{20,28},{12,20},{4,12},{0,4},{9,1},{1... | collective-permute-start | bytes 3538952 | tf_op jit(solution)/shard_map/ppermute | solution.py:135
  1819.1 81.5 %collective-permute-start.90 = (bf16[288,2048]{1,0:T(8,128)(2,1)S(1)}, bf16[288,2048]{1,0:T(8,128)(2,1)S(1)}, u32[]{:S(2)}, u32[]{:S(2)}) collective-permute-start(bf16[288,2048]{1,0:T(8,128)(2,1)S(1)} %add_convert_fusion.12), channel_id=1, source_target_pairs={{0,8},{8,16},{16,24},{24,28},{28,20},{20,12},{12,4},{4,0},{1,9},{9... | collective-permute-start | bytes 3538952 | tf_op jit(solution)/shard_map/ppermute | solution.py:134
  1847.6 106.5 %collective-permute-start.102 = (bf16[288,1024]{1,0:T(8,128)(2,1)S(1)}, bf16[288,1024]{1,0:T(8,128)(2,1)S(1)}, u32[]{:S(2)}, u32[]{:S(2)}) collective-permute-start(bf16[288,1024]{1,0:T(8,128)(2,1)S(1)} %add_convert_fusion.16), channel_id=1, source_target_pairs={{0,2},{1,3},{2,0},{3,1},{4,6},{5,7},{6,4},{7,5},{8,10},{9,11},{10,... | collective-permute-start | bytes 1769480 | tf_op jit(solution)/shard_map/ppermute | solution.py:141
  1900.6 60.1 %collective-permute-start.107 = (bf16[288,2304]{1,0:T(8,128)(2,1)S(1)}, bf16[288,2304]{1,0:T(8,128)(2,1)S(1)}, u32[]{:S(2)}, u32[]{:S(2)}) collective-permute-start(bf16[288,2304]{1,0:T(8,128)(2,1)S(1)} %fusion.26), channel_id=1, source_target_pairs={{0,2},{1,3},{2,0},{3,1},{4,6},{5,7},{6,4},{7,5},{8,10},{9,11},{10,... | collective-permute-start | bytes 3981320 | tf_op jit(solution)/shard_map/ppermute | solution.py:141
  1904.3 49.4 %collective-permute-start.94 = (bf16[288,2048]{1,0:T(8,128)(2,1)S(1)}, bf16[288,2048]{1,0:T(8,128)(2,1)S(1)}, u32[]{:S(2)}, u32[]{:S(2)}) collective-permute-start(bf16[288,2048]{1,0:T(8,128)(2,1)S(1)} %get-tuple-element.122), channel_id=1, source_target_pairs={{8,0},{16,8},{24,16},{28,24},{20,28},{12,20},{4,12},{0,4},{9,1},{1... | collective-permute-start | bytes 3538952 | tf_op jit(solution)/shard_map/ppermute | solution.py:135
  1932.3 55.9 %collective-permute-start.112 = (bf16[288,2304]{1,0:T(8,128)(2,1)S(1)}, bf16[288,2304]{1,0:T(8,128)(2,1)S(1)}, u32[]{:S(2)}, u32[]{:S(2)}) collective-permute-start(bf16[288,2304]{1,0:T(8,128)(2,1)S(1)} %fusion.25), channel_id=1, source_target_pairs={{0,2},{1,3},{2,0},{3,1},{4,6},{5,7},{6,4},{7,5},{8,10},{9,11},{10,... | collective-permute-start | bytes 3981320 | tf_op jit(solution)/shard_map/ppermute | solution.py:141
  1932.8 57.3 %collective-permute-start.118 = (bf16[576,2304]{1,0:T(8,128)(2,1)S(1)}, bf16[576,2304]{1,0:T(8,128)(2,1)S(1)}, u32[]{:S(2)}, u32[]{:S(2)}) collective-permute-start(bf16[576,2304]{1,0:T(8,128)(2,1)S(1)} %pad_maximum_fusion.5), channel_id=1, source_target_pairs={{0,1},{1,0},{2,3},{3,2},{4,5},{5,4},{6,7},{7,6},{8,9},{9,8},{10,11... | collective-permute-start | bytes 7962632 | tf_op jit(solution)/shard_map/ppermute | solution.py:141
  (241 other events, 4891.3 us)

commit v3 on v2

--- a/solution.py
+++ b/solution.py
@@ -92,48 +92,71 @@
     return out + [size // 2]
 
 
-def after(value, *earlier):
-    return lax.optimization_barrier((value,) + earlier)[0]
-
-
-def ring_gather(value, size, visit=lambda block: block):
+class Clock:
+    def __init__(self, token):
+        self.token = token
+
+    def sync(self, *arrays):
+        *arrays, self.token = lax.optimization_barrier(tuple(arrays) + (self.token,))
+        return arrays
+
+    def hold(self, value):
+        return lax.optimization_barrier((value, self.token))[0]
+
+
+def hop(a, b, size):
     up, down = ring_perms(size)
+    return lax.ppermute(a, "wide", up), lax.ppermute(b, "wide", down)
+
+
+def low_sum(*terms):
+    return sum(t.astype(f32) for t in terms).astype(bf16)
+
+
+def halves(value):
     half = value.shape[0] // 2
-    a = b = value
-    out = [visit(value)]
-    for _ in range(1, size // 2):
-        a = lax.ppermute(a, "wide", up)
-        b = lax.ppermute(b, "wide", down)
-        out += [visit(a), visit(b)]
-    tokens = (a, b)
-    a = lax.ppermute(a[:half], "wide", up)
-    b = lax.ppermute(b[half:], "wide", down)
-    return out + [visit(a), visit(b)], tokens
-
-
-def ring_scatter(part_of, rows, size, earlier=()):
-    up, down = ring_perms(size)
-    half = rows // 2
-    far = part_of(size // 2).astype(bf16)
-    if earlier:
-        far = after(far, *earlier)
-    a = lax.ppermute(far[:half], "wide", up)
-    b = lax.ppermute(far[half:], "wide", down)
-    tokens = (a, b)
-    for k in range(size // 2 - 1, 0, -1):
-        own_a = part_of(k).astype(f32)
-        own_b = part_of(-k).astype(f32)
-        if k == size // 2 - 1:
-            a = jnp.concatenate([own_a[:half] + a.astype(f32), own_a[half:]], axis=0)
-            b = jnp.concatenate([own_b[:half], own_b[half:] + b.astype(f32)], axis=0)
-        else:
-            a = own_a + a.astype(f32)
-            b = own_b + b.astype(f32)
-        if k > 1 or size == 4:
-            tokens = (a, b)
-        a = lax.ppermute(a.astype(bf16), "wide", up)
-        b = lax.ppermute(b.astype(bf16), "wide", down)
-    return part_of(0).astype(f32) + a.astype(f32) + b.astype(f32), tokens
+    return value[:half], value[half:]
+
+
+def add_first(whole, part):
+    count = part.shape[0]
+    return jnp.concatenate([low_sum(whole[:count], part), whole[count:].astype(bf16)], axis=0)
+
+
+def add_last(whole, part):
+    count = whole.shape[0] - part.shape[0]
+    return jnp.concatenate([whole[:count].astype(bf16), low_sum(whole[count:], part)], axis=0)
+
+
+def ring_gather(clock, value, size, beside=lambda step: ()):
+    a = b = clock.hold(value)
+    out, other = [a], []
+    for k in range(1, size // 2 + 1):
+        if k == size // 2:
+            a, b = halves(a)[0], halves(b)[1]
+        work = beside(k - 1)
+        a, b = hop(a, b, size)
+        a, b, *work = clock.sync(a, b, *work)
+        out += [a, b]
+        other.append(work)
+    return out, other
+
+
+def ring_scatter(clock, part_of, rows, size, beside=lambda step: ()):
+    a, b = halves(clock.hold(part_of(size // 2).astype(bf16)))
+    other = []
+    for k in range(size // 2 - 1, -1, -1):
+        work = beside(size // 2 - 1 - k)
+        a, b = hop(a, b, size)
+        a, b, *work = clock.sync(a, b, *work)
+        other.append(work)
+        if k == size // 2 - 1 and k > 0:
+            a = add_first(part_of(k), a)
+            b = add_last(part_of(-k), b)
+        elif k > 0:
+            a = low_sum(part_of(k), a)
+            b = low_sum(part_of(-k), b)
+    return part_of(0).astype(f32) + a.astype(f32) + b.astype(f32), other
 
 
 def swap(value, axis, bit):
@@ -168,46 +191,63 @@
     return jnp.minimum(((codes + lift) + large) - large, top)
 
 
-def attn_slice_kernel(places, info, own_ref, other_ref, scale_ref, *out_refs):
-    def write(code_ref):
-        codes = code_ref[0]
-        scale = scale_ref[...].astype(bf16)
-        for s, out_ref in enumerate(out_refs):
-            out_ref[...] = slice_values(codes, info[1 + s]) * scale
+def attn_slice_kernel(places, info, *refs, fixed, split, by_column, count):
+    inputs = refs[: len(refs) - 1 - count]
+    scale_ref = refs[len(refs) - 1 - count]
+    out_refs = refs[len(refs) - count :]
+    per_side = len(inputs) // 2
+    member = info[1 + count]
+
+    def write(code_refs):
+        def put(codes, columns):
+            scale = (scale_ref[:, columns] if by_column else scale_ref[...]).astype(bf16)
+            for s, out_ref in enumerate(out_refs):
+                out_ref[:, columns] = slice_values(codes, info[1 + s]) * scale
+
+        if fixed:
+            put(code_refs[0][0][:, :fixed], slice(0, fixed))
+        for t in range(per_side):
+            first = fixed + jnp.bitwise_xor(member, t) * split
+            codes = code_refs[t][0][:, fixed:] if t == 0 and fixed else code_refs[t][0]
+            put(codes, pl.ds(pl.multiple_of(first, 128), split))
 
     mine = pl.program_id(1) == info[0]
-    pl.when(mine)(lambda: write(own_ref))
-    pl.when(jnp.logical_not(mine))(lambda: write(other_ref))
-
-
-def attn_slices(own, other, places, info, scale, by_column, count):
-    blocks, rows, cols = own.shape
+    pl.when(mine)(lambda: write(inputs[:per_side]))
+    pl.when(jnp.logical_not(mine))(lambda: write(inputs[per_side:]))
+
+
+def attn_slices(own, other, places, info, scale, fixed, by_column, count):
+    blocks, rows, cols = own[0].shape
+    split = cols - fixed
+    width = fixed + split * len(own)
     if by_column:
-        scale_spec = pl.BlockSpec((1, cols), lambda k, j, p, i: (0, j))
+        scale_spec = pl.BlockSpec((1, width), lambda k, j, p, i: (0, j))
     else:
         scale_spec = pl.BlockSpec((rows, 1), lambda k, j, p, i: (p[k], 0))
+    inputs = list(own) + list(other)
     grid_spec = pltpu.PrefetchScalarGridSpec(
         num_scalar_prefetch=2,
         grid=(blocks, 2),
         in_specs=[
-            pl.BlockSpec((1, rows, cols), lambda k, j, p, i: (k, 0, 0)),
-            pl.BlockSpec((1, rows, cols), lambda k, j, p, i: (k, 0, 0)),
-            scale_spec,
-        ],
-        out_specs=[pl.BlockSpec((rows, cols), lambda k, j, p, i: (p[k], j))] * count,
+            pl.BlockSpec((1, rows, v.shape[2]), lambda k, j, p, i: (k, 0, 0)) for v in inputs
+        ]
+        + [scale_spec],
+        out_specs=[pl.BlockSpec((rows, width), lambda k, j, p, i: (p[k], j))] * count,
     )
     return pl.pallas_call(
-        attn_slice_kernel,
+        functools.partial(
+            attn_slice_kernel, fixed=fixed, split=split, by_column=by_column, count=count
+        ),
         grid_spec=grid_spec,
-        out_shape=[jax.ShapeDtypeStruct((blocks * rows, 2 * cols), bf16)] * count,
+        out_shape=[jax.ShapeDtypeStruct((blocks * rows, 2 * width), bf16)] * count,
         compiler_params=pltpu.CompilerParams(vmem_limit_bytes=VMEM_LIMIT),
         cost_estimate=pl.CostEstimate(
-            flops=10 * count * own.size,
-            bytes_accessed=4 * own.size * (1 + count),
+            flops=20 * count * blocks * rows * width,
+            bytes_accessed=4 * blocks * rows * width * (1 + count),
             transcendentals=0,
         ),
         name="attn_slices",
-    )(places, info, own, other, scale)
+    )(places, info, *inputs, scale)
 
 
 def own_slice_kernel(pieces, info, code_ref, row_ref, col_ref, *out_refs):
@@ -528,8 +568,10 @@
     wide_index = lax.axis_index("wide")
     seq_index = lax.axis_index("seq")
     side = seq_index % 2
+    is_low = side == 0
+    members = seq_size // 2
+    member = seq_index // 2
     half_wide = wide // 2
-    is_low = side == 0
     place = ring_place(wide_index, wide)
     count, rows, model_dim = tokens.shape
     length = rows * wide
@@ -548,29 +590,20 @@
     offsets = ring_offsets(wide)
     order = {o: i for i, o in enumerate(ring_offsets(half_wide))}
     seqs = range(count)
+    seq_bits = [1 << i for i in range(seq_size.bit_length() - 1)]
+    clock = Clock(widths)
 
     def index_at(offset):
         return ring_index(jnp.mod(place + offset, wide), wide)
 
     places = jnp.stack([index_at(o) for o in offsets]).astype(jnp.int32)
-    info = jnp.concatenate([side[None].astype(jnp.int32), widths])
+    info = jnp.concatenate(
+        [side[None].astype(jnp.int32), widths, member[None].astype(jnp.int32)]
+    )
     class_info = class_index[None].astype(jnp.int32)
-
-    def gather_columns(first, size, earlier=()):
-        mine = lax.dynamic_slice_in_dim(attn_codes, first + side * size, size, 1).astype(bf16)
-        if earlier:
-            mine = after(mine, *earlier)
-        blocks, tokens = ring_gather(mine, wide, lambda block: (block, swap(block, "seq", 1)))
-        own = jnp.concatenate([block[0] for block in blocks], axis=0)
-        other = jnp.concatenate([block[1] for block in blocks], axis=0)
-        shape = (wide, attn_rows, size)
-        return own.reshape(shape), other.reshape(shape), tokens
-
     column_scale = inverse_powers(attn_exps)[None, :]
     output_scale = inverse_powers(out_exps)[:, None]
-    proj_own, proj_other, ring_tokens = gather_columns(0, half_proj)
-    out_own, out_other, out_tokens = gather_columns(proj_cols, half_out, ring_tokens)
-    seq_bits = [1 << i for i in range(seq_size.bit_length() - 1)]
+
     relative = [0]
     for bit in reversed(seq_bits):
         relative = relative + [r | bit for r in relative]
@@ -589,29 +622,75 @@
         axis=1,
     )[:, :, None]
     down_scale = inverse_powers(down_exps)[None, :]
-    own_weights = own_slices(mlp_codes, pieces, info, row_scale, down_scale, count)
-    mlp_weights = []
-    token = ring_tokens
-    for m in range(3):
-        sent = lax.dynamic_slice_in_dim(mlp_codes[m], seq_index * piece_rows, piece_rows, 0)
-        sent = after(sent.astype(bf16), *token)
-        held = [swap(sent, "wide", half_wide)]
-        token = (held[0],)
+
+    fixed = half_proj // 2
+    split_proj = (half_proj - fixed) // members
+    split_out = half_out // members
+
+    def columns(first, size):
+        return lax.dynamic_slice_in_dim(attn_codes, first, size, 1)
+
+    payload = jnp.concatenate(
+        [
+            columns(side * half_proj, fixed),
+            columns(side * half_proj + fixed + member * split_proj, split_proj),
+            columns(proj_cols + side * half_out + member * split_out, split_out),
+        ],
+        axis=1,
+    ).astype(bf16)
+    piece_codes = lax.dynamic_slice_in_dim(mlp_codes, seq_index * piece_rows, piece_rows, 1)
+    inputs = [tokens[s].astype(f32) for s in seqs]
+    grad_out = [cotangent[s].astype(f32) for s in seqs]
+
+    def early(step):
+        if step == 0:
+            return own_slices(mlp_codes, pieces, info, row_scale, down_scale, count)
+        if step == 1:
+            out = [piece_codes[m].astype(bf16) for m in range(3)]
+            for s in seqs:
+                factor = norm_factor(clock.hold(inputs[s]))
+                out += [factor, (inputs[s] * factor * gain_attn).astype(bf16)]
+            return out
+        return ()
+
+    blocks, work = ring_gather(clock, payload, wide, early)
+    work = sum((list(w) for w in work), [])
+    own_weights, work = work[: 3 * count], work[3 * count :]
+    sends, work = work[:3], work[3:]
+    input_factor, normed = work[0::2], work[1::2]
+
+    stacks = {}
+    for block in blocks:
+        shared = [block] + [None] * (members - 1)
+        for bit in seq_bits[1:]:
+            for t in range(bit // 2):
+                value = shared[t][:, fixed:] if t == 0 else shared[t]
+                shared[t + bit // 2] = swap(value, "seq", bit)
+        for t, value in enumerate(shared):
+            stacks.setdefault((0, t), []).append(value)
+            stacks.setdefault((1, t), []).append(swap(value, "seq", 1))
+    proj_in, out_in = [], []
+    for core in range(2):
+        for t in range(members):
+            values = jnp.concatenate(stacks[core, t], axis=0).reshape(wide, attn_rows, -1)
+            cut = values.shape[2] - split_out
+            proj_in.append(values[:, :, :cut])
+            out_in.append(values[:, :, cut:])
+
+    def exchange(m):
+        return swap(clock.hold(sends[m]), "wide", half_wide)
+
+    def share(block):
+        held = [block]
         for bit in reversed(seq_bits):
-            held = held + [swap(block, "seq", bit) for block in held]
-        mlp_weights.append(
-            partner_slices(
-                held,
-                info,
-                row_scale[m] if m < 2 else down_scale,
-                m == 2,
-                own_weights[m * count : (m + 1) * count],
-            )
+            held = held + [swap(value, "seq", bit) for value in held]
+        return held
+
+    def partner_weights(m, held):
+        scale = row_scale[m] if m < 2 else down_scale
+        return partner_slices(
+            held, info, scale, m == 2, own_weights[m * count : (m + 1) * count]
         )
-    gate_weights, up_weights, down_weights = mlp_weights
-    proj_own = after(proj_own, *own_weights)
-    proj_weights = attn_slices(proj_own, proj_other, places, info, column_scale, True, count)
-    out_weights = attn_slices(out_own, out_other, places, info, output_scale, False, count)
 
     cosine, sine = rotary_rows(wide_index * rows + jnp.arange(rows))
 
@@ -623,12 +702,11 @@
         split = blocks.reshape(KEY_VALUE_HEADS, classes, class_rows, head_cols)
         return jnp.transpose(split, (1, 2, 0, 3)).reshape(rows, KEY_VALUE_HEADS * head_cols)
 
-    inputs = [tokens[s].astype(f32) for s in seqs]
-    grad_out = [cotangent[s].astype(f32) for s in seqs]
-    input_factor = [norm_factor(v) for v in inputs]
-    normed = [(inputs[s] * input_factor[s] * gain_attn).astype(bf16) for s in seqs]
-
-    queries, pairs = [], []
+    received = exchange(0)
+    proj_weights = attn_slices(
+        proj_in[:members], proj_in[members:], places, info, column_scale, fixed, True, count
+    )
+    query_send, pair_send = [], []
     for s in seqs:
         projected = dot(normed[s], proj_weights[s], NN)
         query = rotate(
@@ -647,8 +725,12 @@
             .reshape(rows, KEY_VALUE_HEADS, HEAD_SIZE)
             .astype(bf16)
         )
-        pair = jnp.transpose(jnp.concatenate([key, value], axis=-1), (1, 0, 2))
-        pair = heads_all_to_all(pair)
+        pair_send.append(jnp.transpose(jnp.concatenate([key, value], axis=-1), (1, 0, 2)))
+        query_send.append(rows_to_heads(query))
+    received, *sent = clock.sync(received, *query_send, *pair_send)
+    query_send, pair_send = sent[:count], sent[count:]
+
+    def spread_pairs(pair):
         held = [pair]
         for _ in range(classes - 1):
             held.append(class_ring(held[-1]))
@@ -657,129 +739,389 @@
             lax.dynamic_index_in_dim(held, jnp.mod(class_index - c, classes), 0, keepdims=False)
             for c in range(classes)
         ]
-        pairs.append(jnp.stack(held, axis=1).reshape(length, 2 * HEAD_SIZE))
-        queries.append(all_to_all(rows_to_heads(query)).reshape(wide * class_rows, head_cols))
-
-    attended, exact, lse = [], [], []
+        return jnp.stack(held, axis=1).reshape(length, 2 * HEAD_SIZE)
+
+    attended_send, exact, lse, queries, pairs = [], [], [], [], []
+
+    def attend(s):
+        out, full, log_sum = attn_forward(class_info, queries[s], pairs[s], class_rows, rows)
+        return [out.reshape(wide, class_rows, head_cols), full, log_sum]
+
+    def keep_attend(work):
+        attended_send.append(work[0])
+        exact.append(work[1])
+        lse.append(work[2])
+
+    gate_held = share(received)
     for s in seqs:
-        out, full, log_sum = attn_forward(class_info, queries[s], pairs[s], class_rows, rows)
-        exact.append(full)
-        lse.append(log_sum)
-        back = all_to_all(out.reshape(wide, class_rows, head_cols))
-        attended.append(heads_to_rows(back))
-
-    branch, branch_factor, middle, middle_factor, normed_mlp = [], [], [], [], []
-    for s in seqs:
+        pair = heads_all_to_all(clock.hold(pair_send[s]))
+        if s:
+            pair, *work = clock.sync(pair, *attend(s - 1))
+            keep_attend(work)
+        else:
+            pair, *gate_held = clock.sync(pair, *gate_held)
+        query = all_to_all(clock.hold(query_send[s]))
+        pair = spread_pairs(pair)
+        if s == 0:
+            gate_weights = partner_weights(0, [clock.hold(v) for v in gate_held])
+            query, pair, *gate_weights = clock.sync(query, pair, *gate_weights)
+        elif s == 1:
+            out_weights = attn_slices(
+                [clock.hold(v) for v in out_in[:members]],
+                out_in[members:],
+                places,
+                info,
+                output_scale,
+                0,
+                False,
+                count,
+            )
+            query, pair, *out_weights = clock.sync(query, pair, *out_weights)
+        else:
+            query, pair = clock.sync(query, pair)
+        queries.append(query.reshape(wide * class_rows, head_cols))
+        pairs.append(pair)
+
+    attended, branch, branch_factor, middle, middle_factor, normed_mlp = [], [], [], [], [], []
+
+    def join(s):
         value = dot(attended[s], out_weights[s], NT)
         factor = norm_factor(value)
         mid = inputs[s] + value * factor * gain_post_attn
         mid_factor = norm_factor(mid)
-        branch.append(value)
-        branch_factor.append(factor)
-        middle.append(mid)
-        middle_factor.append(mid_factor)
-        normed_mlp.append((mid * mid_factor * gain_mlp).astype(bf16))
+        return [value, factor, mid, mid_factor, (mid * mid_factor * gain_mlp).astype(bf16)]
+
+    def keep_join(work):
+        for held, value in zip((branch, branch_factor, middle, middle_factor, normed_mlp), work):
+            held.append(value)
+
+    for s in seqs:
+        back = all_to_all(clock.hold(attended_send[s]))
+        work = []
+        if s == count - 2 or count == 1:
+            work = attend(count - 1)
+        if s:
+            joined = join(s - 1)
+            back, *joined = clock.sync(back, *joined)
+            keep_join(joined)
+        if work:
+            back, *work = clock.sync(back, *work)
+            keep_attend(work)
+        attended.append(heads_to_rows(back))
+
+    received, *joined = clock.sync(exchange(1), *join(count - 1))
+    keep_join(joined)
+    up_held = share(received)
 
     def blocks_of(part):
         return lambda o: part[order[o] * rows : (order[o] + 1) * rows]
 
-    gathered, gate, up, hidden_rows, mixed = [], [], [], [], []
-    for s in seqs:
-        blocks, ring_tokens = ring_gather(
-            after(normed_mlp[s], *ring_tokens) if s else normed_mlp[s], half_wide
-        )
+    gathered, gate, up, hidden_rows, mixed, parts = [], [], [], [], [], []
+
+    def open_gate(s):
+        return dot(clock.hold(gathered[s]), gate_weights[s], NT)
+
+    def open_up(s):
+        up_s = dot(clock.hold(gathered[s]), up_weights[s], NT)
+        hidden_s = (0.5 * gate[s] * (1.0 + gelu_parts(gate[s])) * up_s).astype(bf16)
+        return [up_s, hidden_s]
+
+    def keep_up(work):
+        up.append(work[0])
+        hidden_rows.append(work[1])
+
+    def mix(s):
+        return dot(clock.hold(hidden_rows[s]), down_weights[s], NN).astype(bf16)
+
+    blocks, work = ring_gather(
+        clock, normed_mlp[0], half_wide, lambda k: tuple(up_held) if k == half_wide // 2 - 1 else ()
+    )
+    up_held = work[-1]
+    gathered.append(jnp.concatenate(blocks, axis=0))
+    received = exchange(2)
+    up_weights = partner_weights(1, up_held)
+    gate.append(open_gate(0))
+    received, *work = clock.sync(received, *open_up(0), *up_weights, gate[0])
+    keep_up(work[:2])
+    up_weights = work[2 : 2 + count]
+    gate[0] = work[-1]
+    down_held = share(received)
+    for s in seqs[1:]:
+        blocks, _ = ring_gather(clock, normed_mlp[s], half_wide)
         gathered.append(jnp.concatenate(blocks, axis=0))
-    for s in seqs:
-        gate_s = dot(gathered[s], gate_weights[s], NT)
-        up_s = dot(gathered[s], up_weights[s], NT)
-        bounded = gelu_parts(gate_s)
-        hidden_s = (0.5 * gate_s * (1.0 + bounded) * up_s).astype(bf16)
-        part = dot(hidden_s, down_weights[s], NN).astype(bf16)
-        total, ring_tokens = ring_scatter(blocks_of(part), rows, half_wide)
-        mixed.append(total)
-        gate.append(gate_s)
-        up.append(up_s)
-        hidden_rows.append(hidden_s)
+    down_weights = partner_weights(2, down_held)
+    parts.append(clock.sync(mix(0))[0])
 
     layer_out, grad_mixed, gain_fourth = [], [], 0.0
-    for s in seqs:
+
+    def finish(s):
+        nonlocal gain_fourth
         factor = norm_factor(mixed[s])
         layer_out.append((middle[s] + mixed[s] * factor * gain_post_mlp).astype(bf16))
         grad, gain = norm_back(mixed[s], factor, gain_post_mlp, grad_out[s])
         grad_mixed.append(grad.astype(bf16))
         gain_fourth = gain_fourth + gain
 
-    grad_group, grad_gate, grad_up, grad_normed_mlp = [], [], [], []
-    for s in seqs:
-        blocks, ring_tokens = ring_gather(
-            after(grad_mixed[s], *ring_tokens) if s else grad_mixed[s], half_wide
-        )
-        grad_group.append(jnp.concatenate(blocks, axis=0))
-    for s in seqs:
-        grad_hidden = dot(grad_group[s], down_weights[s], NT)
+    def next_forward(s):
+        def beside(step):
+            if s + 1 >= count:
+                return ()
+            if step == 0:
+                return (open_gate(s + 1),)
+            return ()
+
+        return beside
+
+    grad_group, grad_gate, grad_up, grad_parts, grad_normed_mlp = [], [], [], [], []
+
+    def back_hidden(s):
+        grad_hidden = dot(clock.hold(grad_group[s]), down_weights[s], NT)
         bounded = gelu_parts(gate[s])
         gelu_value = 0.5 * gate[s] * (1.0 + bounded)
         slope = 0.5 * (1.0 + bounded) + 0.5 * gate[s] * (1.0 - bounded * bounded) * gelu_coeff * (
             1.0 + 3.0 * 0.044715 * gate[s] * gate[s]
         )
-        grad_gate.append((grad_hidden * up[s] * slope).astype(bf16))
-        grad_up.append((grad_hidden * gelu_value).astype(bf16))
-        part = dot(grad_gate[s], gate_weights[s], NN) + dot(grad_up[s], up_weights[s], NN)
-        total, ring_tokens = ring_scatter(blocks_of(part.astype(bf16)), rows, half_wide)
-        grad_normed_mlp.append(total)
-
-    def mlp_gradient(lefts, rights):
-        grad = sum(dot(lefts[s], rights[s], TN) for s in seqs).astype(bf16)
-        grad = grad.reshape(2, hidden, model_dim)
-        for bit in seq_bits:
-            split = grad.reshape(2, 2, grad.shape[1] // 2, model_dim)
-            received = swap(split[:, 1], "seq", bit)
-            grad = (split[:, 0].astype(f32) + received.astype(f32)).astype(bf16)
-        received = swap(grad[1], "wide", half_wide)
-        grad = (grad[0].astype(f32) + received.astype(f32)).astype(bf16)
+        return [(grad_hidden * up[s] * slope).astype(bf16), (grad_hidden * gelu_value).astype(bf16)]
+
+    def back_input(s):
+        return (
+            dot(clock.hold(grad_gate[s]), gate_weights[s], NN)
+            + dot(grad_up[s], up_weights[s], NN)
+        ).astype(bf16)
+
+    def keep_back(work):
+        grad_gate.append(work[0])
+        grad_up.append(work[1])
+
+    def first_sum(part):
+        a, b = hop(*halves(clock.hold(blocks_of(part)(half_wide // 2))), half_wide)
+        return a, b
+
+    def rest_sum(part, a, b, beside=lambda step: ()):
+        part_of = blocks_of(part)
+        other = []
+        for k in range(half_wide // 2 - 1, 0, -1):
+            if k == half_wide // 2 - 1:
+                a = add_first(part_of(k), a)
+                b = add_last(part_of(-k), b)
+            else:
+                a = low_sum(part_of(k), a)
+                b = low_sum(part_of(-k), b)
+            work = beside(half_wide // 2 - 1 - k)
+            a, b = hop(a, b, half_wide)
+            a, b, *work = clock.sync(a, b, *work)
+            other.append(work)
+        return part_of(0).astype(f32) + a.astype(f32) + b.astype(f32), other
+
+    for s in seqs:
+        a, b = first_sum(parts[s])
+        if s + 1 < count:
+            a, b, value = clock.sync(a, b, open_gate(s + 1))
+            gate.append(value)
+        elif s:
+            a, b, *work = clock.sync(a, b, *back_hidden(0))
+            keep_back(work)
+        else:
+            a, b = clock.sync(a, b)
+
+        def beside(step, s=s):
+            if step:
+                return ()
+            if s + 1 < count:
+                return tuple(open_up(s + 1))
+            return (back_input(0),) if s else ()
+
+        total, work = rest_sum(parts[s], a, b, beside)
+        if s + 1 < count:
+            keep_up(work[0])
+        elif s:
+            grad_parts.append(work[0][0])
+        mixed.append(total)
+        finish(s)
+        if s + 1 < count:
+            parts.append(mix(s + 1))
+            parts[-1], grad_mixed[s] = clock.sync(parts[-1], grad_mixed[s])
+        if s == 0:
+            blocks, _ = ring_gather(clock, grad_mixed[0], half_wide)
+            grad_group.append(jnp.concatenate(blocks, axis=0))
+    if count == 1:
+        keep_back(back_hidden(0))
+        grad_parts.append(back_input(0))
+
+    def weight_first(left, right):
+        return dot(clock.hold(left), right, TN)
+
+    def weight_rest(first, lefts, rights):
+        total = first + sum(dot(clock.hold(lefts[s]), rights[s], TN) for s in seqs[1:])
+        return total.astype(bf16).reshape(2, hidden, model_dim)
+
+    def core_half(grad):
+        split = grad.reshape(2, 2, grad.shape[1] // 2, model_dim)
+        return split[:, 0], split[:, 1]
+
+    def seq_sum(grad, bits):
+        for bit in bits:
+            keep, send = core_half(grad)
+            grad = low_sum(keep, swap(send, "seq", bit))
+        return grad
+
+    def seq_share(grad):
         for bit in reversed(seq_bits):
             grad = jnp.concatenate([grad, swap(grad, "seq", bit)], axis=0)
         return grad
 
-    down_grad = mlp_gradient(hidden_rows, grad_group)
-    up_grad = mlp_gradient(grad_up, gathered)
-    gate_grad = mlp_gradient(grad_gate, gathered)
-    mlp_grad = unpack([gate_grad, up_grad, down_grad], pieces)
-
-    grad_middle, grad_branch, grad_heads = [], [], []
+    grad_middle, grad_branch, grad_send = [], [], []
     gain_third = gain_second = 0.0
-    for s in seqs:
+
+    def back_branch(s):
+        nonlocal gain_third, gain_second
         grad, gain = norm_back(middle[s], middle_factor[s], gain_mlp, grad_normed_mlp[s])
         gain_third = gain_third + gain
         grad_mid = grad_out[s] + grad
-        grad_middle.append(grad_mid)
         grad, gain = norm_back(branch[s], branch_factor[s], gain_post_attn, grad_mid)
         gain_second = gain_second + gain
-        grad_branch.append(grad.astype(bf16))
-        grad_attended = dot(grad_branch[s], out_weights[s], NN).astype(bf16)
-        grad_heads.append(
-            all_to_all(rows_to_heads(grad_attended)).reshape(wide * class_rows, head_cols)
+        grad = grad.astype(bf16)
+        send = rows_to_heads(dot(grad, out_weights[s], NN).astype(bf16))
+        return [grad_mid, grad, send]
+
+    def keep_branch(work):
+        grad_middle.append(work[0])
+        grad_branch.append(work[1])
+        grad_send.append(work[2])
+
+    for s in seqs[1:]:
+        blocks, work = ring_gather(
+            clock,
+            grad_mixed[s],
+            half_wide,
+            lambda k: (weight_first(hidden_rows[0], grad_group[0]),) if k == 0 and s == 1 else (),
         )
-
-    grad_query, grad_key_value = [], []
+        if s == 1:
+            down_first = work[0][0]
+        grad_group.append(jnp.concatenate(blocks, axis=0))
+    if count == 1:
+        down_first = weight_first(hidden_rows[0], grad_group[0])
     for s in seqs:
-        dq, dkv = attn_backward(
-            class_info, queries[s], pairs[s], grad_heads[s], exact[s], lse[s], class_rows, rows
-        )
-        dq = heads_to_rows(all_to_all(dq.reshape(wide, class_rows, head_cols)))
-        dq = rotate(
-            dq.astype(f32).reshape(rows, QUERY_HEADS, HEAD_SIZE) * query_scale, cosine, -sine
-        )
+        a, b = first_sum(grad_parts[s])
+        if s + 1 < count:
+            a, b, *work = clock.sync(a, b, *back_hidden(s + 1))
+            keep_back(work)
+        elif s:
+            a, b, *work = clock.sync(a, b, *back_branch(s - 1))
+            keep_branch(work)
+        else:
+            a, b = clock.sync(a, b)
+
+        def beside(step, s=s):
+            if step:
+                return ()
+            if s + 1 < count:
+                return (back_input(s + 1),)
+            return (weight_rest(down_first, hidden_rows, grad_group),)
+
+        total, work = rest_sum(grad_parts[s], a, b, beside)
+        if s + 1 < count:
+            grad_parts.append(work[0][0])
+        else:
+            down_grad = work[0][0]
+        grad_normed_mlp.append(total)
+
+    down_grad = seq_sum(down_grad, seq_bits[:1])
+    last = back_branch(count - 1) if count > 1 else back_branch(0)
+    grad_heads = []
+    for s in seqs:
+        if s == count - 1 and count == 1:
+            keep_branch(clock.sync(*last))
+        back = all_to_all(clock.hold(grad_send[s]))
+        work = []
+        if s == count - 2:
+            work = last
+        if s:
+            pass
+        if work:
+            back, down_grad, *work = clock.sync(back, down_grad, *work)
+            keep_branch(work)
+            down_grad = seq_sum(down_grad, seq_bits[1:])
+        elif s == count - 1:
+            up_first = weight_first(grad_up[0], gathered[0])
+            dq_dkv = attn_backward(
+                class_info,
+                queries[0],
+                pairs[0],
+                clock.hold(grad_heads[0]) if s else back.reshape(wide * class_rows, head_cols),
+                exact[0],
+                lse[0],
+                class_rows,
+                rows,
+            )
+            back, up_first, *dq_dkv = clock.sync(back, up_first, *dq_dkv)
+        else:
+            (back,) = clock.sync(back)
+        grad_heads.append(back.reshape(wide * class_rows, head_cols))
+
+    def class_sum(dkv):
         dkv = dkv.reshape(KEY_VALUE_HEADS, classes, rows, 2 * HEAD_SIZE)
         total = None
         for step in range(1, classes + 1):
             own = lax.dynamic_index_in_dim(
                 dkv, jnp.mod(class_index - step, classes), 1, keepdims=False
             )
-            total = own if total is None else own.astype(f32) + class_ring(total).astype(f32)
-            total = total.astype(bf16)
-        dkv = heads_all_to_all(total)
-        dkv = jnp.transpose(dkv.astype(f32), (1, 0, 2))
+            total = own if total is None else low_sum(own, class_ring(total))
+        return total
+
+    query_back, pair_back = [], []
+    beside_query = {}
+    for s in seqs:
+        dq, dkv = dq_dkv
+        query = all_to_all(clock.hold(dq.reshape(wide, class_rows, head_cols)))
+        pair = class_sum(dkv)
+        if s + 1 < count:
+            dq_dkv = attn_backward(
+                class_info,
+                queries[s + 1],
+                pairs[s + 1],
+                clock.hold(grad_heads[s + 1]),
+                exact[s + 1],
+                lse[s + 1],
+                class_rows,
+                rows,
+            )
+            query, pair, *dq_dkv = clock.sync(query, pair, *dq_dkv)
+        elif s:
+            gate_first = weight_first(grad_gate[0], gathered[0])
+            query, pair, gate_first = clock.sync(query, pair, gate_first)
+        else:
+            query, pair = clock.sync(query, pair)
+        pair = heads_all_to_all(clock.hold(pair))
+        if s == 0:
+            up_grad = weight_rest(up_first, grad_up, gathered)
+            pair, up_grad = clock.sync(pair, up_grad)
+            up_grad = seq_sum(up_grad, seq_bits)
+        elif s == 1:
+            gate_grad = weight_rest(gate_first, grad_gate, gathered)
+            pair, gate_grad = clock.sync(pair, gate_grad)
+            gate_grad = seq_sum(gate_grad, seq_bits)
+        else:
+            (pair,) = clock.sync(pair)
+        query_back.append(query)
+        pair_back.append(pair)
+    if count == 1:
+        gate_grad = weight_rest(weight_first(grad_gate[0], gathered[0]), grad_gate, gathered)
+        gate_grad = seq_sum(gate_grad, seq_bits)
+
+    def owner_sum(grad):
+        return low_sum(grad[0], swap(clock.hold(grad[1]), "wide", half_wide))
+
+    down_grad = owner_sum(down_grad)
+    grad_query, grad_key_value, grad_tokens, gain_first = [], [], [], 0.0
+    for s in seqs:
+        dq = rotate(
+            heads_to_rows(query_back[s]).astype(f32).reshape(rows, QUERY_HEADS, HEAD_SIZE)
+            * query_scale,
+            cosine,
+            -sine,
+        )
+        dkv = jnp.transpose(pair_back[s].astype(f32), (1, 0, 2))
         dk = rotate(dkv[..., :HEAD_SIZE], cosine, -sine)
         grad_query.append(dq.reshape(rows, query_cols).astype(bf16))
         grad_key_value.append(
@@ -787,56 +1129,60 @@
                 [dk.reshape(rows, key_cols), dkv[..., HEAD_SIZE:].reshape(rows, key_cols)], axis=1
             ).astype(bf16)
         )
-
-    grad_tokens, gain_first = [], 0.0
+    first_half = jnp.concatenate(grad_query, axis=0)
+    second_half = jnp.concatenate(grad_key_value, axis=0)
+    all_normed = jnp.concatenate(normed, axis=0)
+    all_attended = jnp.concatenate(attended, axis=0)
+    all_branch = jnp.concatenate(grad_branch, axis=0)
+    keep_left = jnp.where(is_low, first_half, second_half)
+    send_right = jnp.where(is_low, second_half, first_half)
+    proj_sent = swap(dot(all_normed, send_right, TN).astype(bf16), "seq", 1)
+    low_out, high_out = all_attended[:, :half_out], all_attended[:, half_out:]
+    out_sent = swap(
+        dot(all_branch, jnp.where(is_low, high_out, low_out), TN).astype(bf16), "seq", 1
+    )
+    out_part = low_sum(dot(all_branch, jnp.where(is_low, low_out, high_out), TN), out_sent)
+    proj_part = low_sum(dot(all_normed, keep_left, TN), proj_sent)
     for s in seqs:
         grad_proj = jnp.concatenate([grad_query[s], grad_key_value[s]], axis=1)
         grad_normed = dot(grad_proj, proj_weights[s], NT)
         grad, gain = norm_back(inputs[s], input_factor[s], gain_attn, grad_normed)
         gain_first = gain_first + gain
         grad_tokens.append((grad_middle[s] + grad).astype(bf16))
-
-    def scatter_columns(left, first_half, second_half, earlier=()):
-        keep = jnp.where(is_low, first_half, second_half)
-        send = jnp.where(is_low, second_half, first_half)
-        received = swap(dot(left, send, TN).astype(bf16), "seq", 1)
-        part = (dot(left, keep, TN) + received.astype(f32)).astype(bf16)
-        own, tokens = ring_scatter(
-            lambda o: lax.dynamic_slice_in_dim(part, index_at(o) * attn_rows, attn_rows, 0),
-            attn_rows,
-            wide,
-            earlier,
-        )
-        bit = 2
-        while bit < seq_size:
-            low = own.astype(bf16)
-            own = low.astype(f32) + swap(low, "seq", bit).astype(f32)
-            bit *= 2
-        low = own.astype(bf16)
-        other = swap(low, "seq", 1)
-        return [
-            jnp.where(is_low, low, other).astype(f32),
-            jnp.where(is_low, other, low).astype(f32),
-        ], tokens
-
     gains = jnp.stack([gain_first, gain_second, gain_third, gain_fourth])
+    down_grad, proj_part, out_part, gains = clock.sync(down_grad, proj_part, out_part, gains)
     for axis, size in (("seq", seq_size), ("wide", wide)):
         bit = 1
         while bit < size:
             gains = gains + swap(gains, axis, bit)
             bit *= 2
-
-    all_attended = jnp.concatenate(attended, axis=0)
-    out_parts, ring_tokens = scatter_columns(
-        jnp.concatenate(grad_branch, axis=0), all_attended[:, :half_out], all_attended[:, half_out:]
-    )
-    proj_parts, ring_tokens = scatter_columns(
-        jnp.concatenate(normed, axis=0),
-        jnp.concatenate(grad_query, axis=0),
-        jnp.concatenate(grad_key_value, axis=0),
-        ring_tokens,
-    )
-    attn_grad = jnp.concatenate(proj_parts + out_parts, axis=1)
+    gains, *grad_tokens = clock.sync(gains, *grad_tokens)
+
+    def part_of(o):
+        first = index_at(o) * attn_rows
+        return jnp.concatenate(
+            [
+                lax.dynamic_slice_in_dim(proj_part, first, attn_rows, 0),
+                lax.dynamic_slice_in_dim(out_part, first, attn_rows, 0),
+            ],
+            axis=1,
+        )
+
+    total, _ = ring_scatter(clock, part_of, attn_rows, wide)
+    up_grad = owner_sum(up_grad)
+    for bit in seq_bits[1:]:
+        low = total.astype(bf16)
+        total = low.astype(f32) + swap(low, "seq", bit).astype(f32)
+    low = total.astype(bf16)
+    other = swap(low, "seq", 1)
+    (up_grad,) = clock.sync(up_grad)
+    gate_grad = owner_sum(gate_grad)
+    mlp_grad = unpack([seq_share(gate_grad), seq_share(up_grad), seq_share(down_grad)], pieces)
+    left, right = jnp.where(is_low, low, other), jnp.where(is_low, other, low)
+    attn_grad = jnp.concatenate(
+        [left[:, :half_proj], right[:, :half_proj], left[:, half_proj:], right[:, half_proj:]],
+        axis=1,
+    ).astype(f32)
     return (
         jnp.stack(layer_out),
         jnp.stack(grad_tokens),

time: 2050 us -> 1820 us (0.89)
  starting transfers between devices: 317 us -> 182 us
  waiting for transfers between devices: 767 us -> 641 us
    ppermute x64 -> x48, waiting for transfers between devices: 463 us -> 184 us  [hop(): return (lax.ppermute(a, 'wide', up), lax.ppermute(b, 'wide', down))]
    ppermute x56 -> x63, waiting for transfers between devices: 222 us -> 370 us  [swap(): return lax.ppermute(value, axis, [(i, i ^ bit) for i in range(size)])]
    ppermute x64 -> x48, starting transfers between devices: 199 us -> 77.9 us  [hop(): return (lax.ppermute(a, 'wide', up), lax.ppermute(b, 'wide', down))]
    all_to_all x4, waiting for transfers between devices: 54.4 us -> 13.8 us  [heads_all_to_all(): lax.all_to_all(value, 'wide', split_axis=0, concat_axis=0, axis_index_gro...]
    all_to_all x8, starting transfers between devices: 67.7 us -> 37.8 us  [all_to_all(): lax.all_to_all(value, 'wide', split_axis=0, concat_axis=0, tiled=True)]
    all_to_all x8, waiting for transfers between devices: 13.3 us -> 38.6 us  [all_to_all(): lax.all_to_all(value, 'wide', split_axis=0, concat_axis=0, tiled=True)]
    convert_element_type x27 -> x33, other arithmetic: 62.3 us -> 77.4 us  [the longest x21 42.8 us: low_sum(): return sum((t.astype(f32) for t in terms)).astype(bf16)]
    ppermute x56 -> x63, starting transfers between devices: 27.6 us -> 42.2 us  [swap(): return lax.ppermute(value, axis, [(i, i ^ bit) for i in range(size)])]
  transfers between devices with their start and end apart: 136 -> 127, of which waited for: 48 -> 55; matrix products, arithmetic and copies ran while one was open for 30% -> 35% of each run, Pallas kernels for 7% -> 9%
where the time goes in v3:
time: 1820 us; the launch traced here: 1810 us
  waiting for transfers between devices  641 us (35%)
  matrix products  438 us (24%)
  local copies, waits for them, and re-layouts  211 us (12%)
  starting transfers between devices  182 us (10%)
  Pallas kernels  178 us (10%)
  other arithmetic  153 us (8%)
    dot_general x30, matrix products, dot(): return lax.dot_general(a, b, (dims, ((), ())), preferred_element_type=f32)  438 us
    ppermute x63, waiting for transfers between devices, swap(): return lax.ppermute(value, axis, [(i, i ^ bit) for i in range(size)])  370 us
    ppermute x48, waiting for transfers between devices, hop(): return (lax.ppermute(a, 'wide', up), lax.ppermute(b, 'wide', down))  184 us
    ppermute x48, starting transfers between devices, hop(): return (lax.ppermute(a, 'wide', up), lax.ppermute(b, 'wide', down))  77.9 us
    unnamed x389, local copies, waits for them, and re-layouts  63.1 us
    pallas_call x2, Pallas kernels, attn_slices(): pl.pallas_call(functools.partial(attn_slice_kernel, fixed=fixed, split=sp...  51.9 us
    convert_element_type x21, other arithmetic, low_sum(): return sum((t.astype(f32) for t in terms)).astype(bf16)  42.8 us
    ppermute x63, starting transfers between devices, swap(): return lax.ppermute(value, axis, [(i, i ^ bit) for i in range(size)])  42.2 us
  transfers between devices with their start and end apart: 127, of which 55 were waited for; matrix products, arithmetic and copies ran while one was open for 35% of the time, Pallas kernels for 9%

profile of v3, /device:TPU:0, one launch (start us, length us, event | category | flops | bytes accessed | tf_op | source)
XLA Modules:
  0.0 1806.1 jit_solution(5725402495382207556)
XLA Ops:
  33.3 25.3 %own_slices.1 = (bf16[2304,2304]{1,0:T(8,128)(2,1)}, bf16[2304,2304]{1,0:T(8,128)(2,1)}, bf16[2304,2304]{1,0:T(8,128)(2,1)}, bf16[2304,2304]{1,0:T(8,128)(2,1)},...) custom-call(s32[4]{0:T(128)} %pad_add_fusion.pieces, s32[4]{0:T(128)} %pad_add_fusion.1.info, ...), custom_call_target="tpu_custom_call" | custom-call | flops 159252480 | bytes 63700992 | tf_op jit(solution)/shard_map/own_slices/pallas_call | solution.py:276
  105.6 13.8 collective-permute-done.12
  143.4 12.2 collective-permute-done.6
  210.4 31.5 %attn_slices.2 = (bf16[2304,4096]{1,0:T(8,128)(2,1)}, bf16[2304,4096]{1,0:T(8,128)(2,1)}) custom-call(s32[8]{0:T(128)} %stack.116.places, s32[4]{0:T(128)} %pad_add_fusion.1.info, bf16[8,288,1536]{2,1,0:T(8,128)(2,1)} %slice.546.refs_0_, bf16[8,288,512]{2,1,0:T(8,128)(2,1)} %get-tuple-element.631.refs_1_, bf16[8,288,1536]{2,1,0:T(8,128)(2,1)} %slice.548.refs_2_, ...), custom_call_target="tpu_custom_call" | custom-call | flops 188743680 | bytes 56623104 | tf_op jit(solution)/shard_map/attn_slices/pallas_call | solution.py:237
  292.3 26.7 %collective-permute-done.36.refs_1_ = bf16[288,2304]{1,0:T(8,128)(2,1)S(1)} collective-permute-done((bf16[288,2304]{1,0:T(8,128)(2,1)}, bf16[288,2304]{1,0:T(8,128)(2,1)S(1)}, u32[]{:S(2)}, u32[]{:S(2)}) %collective-permute-start.36) | collective-permute-done | bytes 1327136 | tf_op jit(solution)/shard_map/ppermute | solution.py:164
  340.0 23.1 %collective-permute-done.39 = bf16[4,256,512]{2,1,0:T(8,128)(2,1)S(1)} collective-permute-done((bf16[4,256,512]{2,1,0:T(8,128)(2,1)S(1)}, bf16[4,256,512]{2,1,0:T(8,128)(2,1)S(1)}, u32[]{:S(2)}, u32[]{:S(2)}) %collective-permute-start.39) | collective-permute-done | bytes 1048608 | tf_op jit(solution)/shard_map/ppermute | solution.py:184
  381.5 13.8 all-to-all-done.2
  408.6 20.4 %attn_slices.3 = (bf16[2304,2048]{1,0:T(8,128)(2,1)}, bf16[2304,2048]{1,0:T(8,128)(2,1)}) custom-call(s32[8]{0:T(128)} %stack.116.places, s32[4]{0:T(128)} %pad_add_fusion.1.info, bf16[8,288,512]{2,1,0:T(8,128)(2,1)} %slice.565.refs_0_, bf16[8,288,512]{2,1,0:T(8,128)(2,1)} %get-tuple-element.344.refs_1_, bf16[8,288,512]{2,1,0:T(8,128)(2,1)} %slice.567.refs_2_, ...), custom_call_target="tpu_custom_call" | custom-call | flops 94371840 | bytes 28311552 | tf_op jit(solution)/shard_map/attn_slices/pallas_call | solution.py:237
  452.8 14.2 all-to-all-done.4
  481.2 16.4 all-to-all-done.5
  508.7 56.4 %collective-permute-done.41.refs_0_ = bf16[288,2304]{1,0:T(8,128)(2,1)} collective-permute-done((bf16[288,2304]{1,0:T(8,128)(2,1)S(1)}, bf16[288,2304]{1,0:T(8,128)(2,1)}, u32[]{:S(2)}, u32[]{:S(2)}) %collective-permute-start.41) | collective-permute-done | bytes 1327136 | tf_op jit(solution)/shard_map/ppermute | solution.py:164
  568.1 28.4 %collective-permute-done.46.refs_1_ = bf16[288,2304]{1,0:T(8,128)(2,1)} collective-permute-done((bf16[288,2304]{1,0:T(8,128)(2,1)}, bf16[288,2304]{1,0:T(8,128)(2,1)}, u32[]{:S(2)}, u32[]{:S(2)}) %collective-permute-start.46) | collective-permute-done | bytes 1327136 | tf_op jit(solution)/shard_map/ppermute | solution.py:164
  620.7 15.3 fusion.132
  645.4 21.2 %fusion.8 = (bf16[1024,2304]{1,0:T(8,128)(2,1)}, f32[1024,2304]{1,0:T(8,128)}) fusion(f32[1024,2304]{1,0:T(8,128)} %fusion.132, bf16[1024,2304]{1,0:T(8,128)(2,1)} %copy-done.102, bf16[2304,2304]{1,0:T(8,128)(2,1)} %get-tuple-element.440), kind=kOutput, calls=%fused_computation.21 | convolution fusion | flops 10895228928 | bytes 38928384 | tf_op jit(solution)/shard_map/dot_general | solution.py:26
  666.6 12.4 collective-permute-done.49.refs_0_
  682.1 24.6 %collective-permute-done.50 = bf16[256,2304]{1,0:T(8,128)(2,1)S(1)} collective-permute-done((bf16[256,2304]{1,0:T(8,128)(2,1)S(1)}, bf16[256,2304]{1,0:T(8,128)(2,1)S(1)}, u32[]{:S(2)}, u32[]{:S(2)}) %collective-permute-start.50) | collective-permute-done | bytes 1179680 | tf_op jit(solution)/shard_map/ppermute | solution.py:109
  732.9 15.1 convolution_convert_fusion.3
  752.0 13.4 fusion.133
  770.3 21.3 %multiply_convert_fusion.2 = (bf16[1024,2304]{1,0:T(8,128)(2,1)}, f32[1024,2304]{1,0:T(8,128)}) fusion(f32[1024,2304]{1,0:T(8,128)} %fusion.133, bf16[1024,2304]{1,0:T(8,128)(2,1)} %copy-done.98, bf16[2304,2304]{1,0:T(8,128)(2,1)} %get-tuple-element.411), kind=kOutput, calls=%fused_computation.41 | convolution fusion | flops 10895228928 | bytes 38928384 | tf_op jit(solution)/shard_map/dot_general | solution.py:26
  803.6 13.5 convolution_convert_fusion.2
  819.4 23.2 %collective-permute-done.61 = bf16[256,2304]{1,0:T(8,128)(2,1)S(1)} collective-permute-done((bf16[256,2304]{1,0:T(8,128)(2,1)S(1)}, bf16[256,2304]{1,0:T(8,128)(2,1)S(1)}, u32[]{:S(2)}, u32[]{:S(2)}) %collective-permute-start.61) | collective-permute-done | bytes 1179680 | tf_op jit(solution)/shard_map/ppermute | solution.py:109
  860.7 27.3 %multiply_convert_fusion.1 = (bf16[1024,2304]{1,0:T(8,128)(2,1)}, bf16[1024,2304]{1,0:T(8,128)(2,1)}) fusion(f32[1024,2304]{1,0:T(8,128)} %fusion.132, f32[1024,2304]{1,0:T(8,128)} %get-tuple-element.432, bf16[1024,2304]{1,0:T(8,128)(2,1)} %copy-done.100, bf16[2304,2304]{1,0:T(8,128)(2,1)} %get-tuple-element.399), kind=kOutput, calls=%fused_computation.40 | convolution fusion | flops 10925899776 | bytes 43646976 | tf_op jit(solution)/shard_map/dot_general | solution.py:26
  888.0 16.6 fusion.134
  908.6 17.4 add_convert_fusion.6
  936.2 17.3 fusion.135
  960.7 12.2 collective-permute-done.71
  977.6 27.3 %multiply_convert_fusion = (bf16[1024,2304]{1,0:T(8,128)(2,1)}, bf16[1024,2304]{1,0:T(8,128)(2,1)}) fusion(f32[1024,2304]{1,0:T(8,128)} %fusion.133, f32[1024,2304]{1,0:T(8,128)} %get-tuple-element.455, bf16[1024,2304]{1,0:T(8,128)(2,1)} %copy-done.101, bf16[2304,2304]{1,0:T(8,128)(2,1)} %get-tuple-element.419), kind=kOutput, calls=%fused_computation.38 | convolution fusion | flops 10925899776 | bytes 43646976 | tf_op jit(solution)/shard_map/dot_general | solution.py:26
  1004.9 16.6 fusion.136
  1026.0 18.3 %add_convert_fusion.5 = bf16[1024,2304]{1,0:T(8,128)(2,1)} fusion(f32[1024,2304]{1,0:T(8,128)} %fusion.136, bf16[1024,2304]{1,0:T(8,128)(2,1)S(1)} %copy-done.133, bf16[2304,2304]{1,0:T(8,128)(2,1)} %get-tuple-element.411), kind=kOutput, calls=%fused_computation.37 | convolution fusion | flops 10876354560 | bytes 29491200 | tf_op jit(solution)/shard_map/dot_general | solution.py:26
  1070.0 18.6 %fusion.137 = f32[2304,2304]{1,0:T(8,128)} fusion(bf16[1024,2304]{1,0:T(8,128)(2,1)} %get-tuple-element.475, bf16[1024,2304]{1,0:T(8,128)(2,1)} %copy-done.101), kind=kOutput, calls=%fused_computation.454 | convolution fusion | flops 10871635968 | bytes 30670848 | tf_op jit(solution)/shard_map/dot_general | solution.py:26
  1091.2 13.8 add_convert_fusion.2
  1165.3 17.5 attn_backward.2
  1182.8 17.3 fusion.138
  1215.2 17.4 attn_backward.3
  1252.3 19.9 %add_convert_fusion.1 = bf16[2304,2304]{1,0:T(8,128)(2,1)} fusion(f32[2304,2304]{1,0:T(8,128)} %fusion.138, bf16[1024,2304]{1,0:T(8,128)(2,1)} %get-tuple-element.510, bf16[1024,2304]{1,0:T(8,128)(2,1)} %copy-done.98), kind=kOutput, calls=%fused_computation.1 | convolution fusion | flops 10882252800 | bytes 41287680 | tf_op jit(solution)/shard_map/dot_general | solution.py:26
  1288.9 18.7 %fusion.139 = f32[2304,2304]{1,0:T(8,128)} fusion(bf16[1024,2304]{1,0:T(8,128)(2,1)} %get-tuple-element.514, bf16[1024,2304]{1,0:T(8,128)(2,1)} %copy-done.102), kind=kOutput, calls=%fused_computation.456 | convolution fusion | flops 10871635968 | bytes 30670848 | tf_op jit(solution)/shard_map/dot_general | solution.py:26
  1315.4 20.0 %add_convert_fusion = bf16[2304,2304]{1,0:T(8,128)(2,1)} fusion(f32[2304,2304]{1,0:T(8,128)} %fusion.139, bf16[1024,2304]{1,0:T(8,128)(2,1)} %get-tuple-element.519, bf16[1024,2304]{1,0:T(8,128)(2,1)} %copy-done.98), kind=kOutput, calls=%fused_computation | convolution fusion | flops 10882252800 | bytes 41287680 | tf_op jit(solution)/shard_map/dot_general | solution.py:26
  1352.3 14.7 convolution_convert_fusion
  1399.2 12.2 fusion.53
  1411.6 31.9 %collective-permute-done.85 = bf16[288,2304]{1,0:T(8,128)(2,1)} collective-permute-done((bf16[288,2304]{1,0:T(8,128)(2,1)}, bf16[288,2304]{1,0:T(8,128)(2,1)}, u32[]{:S(2)}, u32[]{:S(2)}) %collective-permute-start.85) | collective-permute-done | bytes 1327136 | tf_op jit(solution)/shard_map/ppermute | solution.py:164
  1495.1 15.6 collective-permute-done.93
  1522.1 30.0 %collective-permute-done.104 = bf16[2,288,2304]{2,1,0:T(8,128)(2,1)} collective-permute-done((bf16[2,288,2304]{2,1,0:T(8,128)(2,1)}, bf16[2,288,2304]{2,1,0:T(8,128)(2,1)}, u32[]{:S(2)}, u32[]{:S(2)}) %collective-permute-start.104) | collective-permute-done | bytes 2654240 | tf_op jit(solution)/shard_map/ppermute | solution.py:164
  1564.8 48.5 %collective-permute-done.105 = bf16[288,2304]{1,0:T(8,128)(2,1)S(1)} collective-permute-done((bf16[288,2304]{1,0:T(8,128)(2,1)S(1)}, bf16[288,2304]{1,0:T(8,128)(2,1)S(1)}, u32[]{:S(2)}, u32[]{:S(2)}) %collective-permute-start.105) | collective-permute-done | bytes 1327136 | tf_op jit(solution)/shard_map/ppermute | solution.py:164
  1629.1 23.7 %collective-permute-start.99 = (bf16[288,3072]{1,0:T(8,128)(2,1)S(1)}, bf16[288,3072]{1,0:T(8,128)(2,1)S(1)}, u32[]{:S(2)}, u32[]{:S(2)}) collective-permute-start(bf16[288,3072]{1,0:T(8,128)(2,1)S(1)} %add_convert_fusion.10), channel_id=1, source_target_pairs={{0,8},{8,16},{16,24},{24,28},{28,20},{20,12},{12,4},{4,0},{1,9},{9... | collective-permute-start | bytes 5308424 | tf_op jit(solution)/shard_map/ppermute | solution.py:109
  1656.0 33.6 %collective-permute-done.100 = bf16[288,3072]{1,0:T(8,128)(2,1)S(1)} collective-permute-done((bf16[288,3072]{1,0:T(8,128)(2,1)S(1)}, bf16[288,3072]{1,0:T(8,128)(2,1)S(1)}, u32[]{:S(2)}, u32[]{:S(2)}) %collective-permute-start.100) | collective-permute-done | bytes 1769504 | tf_op jit(solution)/shard_map/ppermute | solution.py:109
  1699.7 50.0 %collective-permute-done.110 = bf16[288,2304]{1,0:T(8,128)(2,1)S(1)} collective-permute-done((bf16[288,2304]{1,0:T(8,128)(2,1)S(1)}, bf16[288,2304]{1,0:T(8,128)(2,1)S(1)}, u32[]{:S(2)}, u32[]{:S(2)}) %collective-permute-start.110) | collective-permute-done | bytes 1327136 | tf_op jit(solution)/shard_map/ppermute | solution.py:164
  1754.5 25.4 %collective-permute-done.111 = bf16[288,2304]{1,0:T(8,128)(2,1)S(1)} collective-permute-done((bf16[288,2304]{1,0:T(8,128)(2,1)S(1)}, bf16[288,2304]{1,0:T(8,128)(2,1)S(1)}, u32[]{:S(2)}, u32[]{:S(2)}) %collective-permute-start.111) | collective-permute-done | bytes 1327136 | tf_op jit(solution)/shard_map/ppermute | solution.py:164
  1789.8 16.1 unpack.1
  (905 shorter events, 762.3 us)
Async XLA Ops:
  3.6 63.4 %collective-permute-start = (bf16[288,2048]{1,0:T(8,128)(2,1)S(1)}, bf16[288,2048]{1,0:T(8,128)(2,1)}, u32[]{:S(2)}, u32[]{:S(2)}) collective-permute-start(bf16[288,2048]{1,0:T(8,128)(2,1)S(1)} %pad_maximum_fusion.15), channel_id=1, source_target_pairs={{0,8},{8,16},{16,24},{24,28},{28,20},{20,12},{12,4},{4,0},{1,9},{9... | collective-permute-start | bytes 3538952 | tf_op jit(solution)/shard_map/ppermute | solution.py:109
  6.6 60.3 %collective-permute-start.1 = (bf16[288,2048]{1,0:T(8,128)(2,1)S(1)}, bf16[288,2048]{1,0:T(8,128)(2,1)}, u32[]{:S(2)}, u32[]{:S(2)}) collective-permute-start(bf16[288,2048]{1,0:T(8,128)(2,1)S(1)} %pad_maximum_fusion.15), channel_id=1, source_target_pairs={{8,0},{16,8},{24,16},{28,24},{20,28},{12,20},{4,12},{0,4},{9,1},{1... | collective-permute-start | bytes 3538952 | tf_op jit(solution)/shard_map/ppermute | solution.py:109
  6.6 72.3 %collective-permute-start.18 = (bf16[288,2048]{1,0:T(8,128)(2,1)S(1)}, bf16[288,2048]{1,0:T(8,128)(2,1)}, u32[]{:S(2)}, u32[]{:S(2)}) collective-permute-start(bf16[288,2048]{1,0:T(8,128)(2,1)S(1)} %pad_maximum_fusion.15), channel_id=1, source_target_pairs={{0,1},{1,0},{2,3},{3,2},{4,5},{5,4},{6,7},{7,6},{8,9},{9,8},{10,11... | collective-permute-start | bytes 3538952 | tf_op jit(solution)/shard_map/ppermute | solution.py:164
  7.5 56.7 %collective-permute-start.9 = (bf16[288,1024]{1,0:T(8,128)(2,1)}, bf16[288,1024]{1,0:T(8,128)(2,1)}, u32[]{:S(2)}, u32[]{:S(2)}) collective-permute-start(bf16[288,1024]{1,0:T(8,128)(2,1)} %slice.425), channel_id=1, source_target_pairs={{0,2},{1,3},{2,0},{3,1},{4,6},{5,7},{6,4},{7,5},{8,10},{9,11},{10,... | collective-permute-start | bytes 1769480 | tf_op jit(solution)/shard_map/ppermute | solution.py:164
  68.0 31.5 %collective-permute-start.2 = (bf16[288,2048]{1,0:T(8,128)(2,1)}, bf16[288,2048]{1,0:T(8,128)(2,1)S(1)}, u32[]{:S(2)}, u32[]{:S(2)}) collective-permute-start(bf16[288,2048]{1,0:T(8,128)(2,1)} %collective-permute-done), channel_id=1, source_target_pairs={{0,8},{8,16},{16,24},{24,28},{28,20},{20,12},{12,4},{4,0},{1,9},{9... | collective-permute-start | bytes 3538952 | tf_op jit(solution)/shard_map/ppermute | solution.py:109
  105.0 36.5 %collective-permute-start.21 = (bf16[288,2048]{1,0:T(8,128)(2,1)S(1)}, bf16[288,2048]{1,0:T(8,128)(2,1)S(1)}, u32[]{:S(2)}, u32[]{:S(2)}) collective-permute-start(bf16[288,2048]{1,0:T(8,128)(2,1)S(1)} %collective-permute-done.2), channel_id=1, source_target_pairs={{0,1},{1,0},{2,3},{3,2},{4,5},{5,4},{6,7},{7,6},{8,9},{9,8},{10,11... | collective-permute-start | bytes 3538952 | tf_op jit(solution)/shard_map/ppermute | solution.py:164
  137.0 57.8 %collective-permute-start.23 = (bf16[288,2048]{1,0:T(8,128)(2,1)}, bf16[288,2048]{1,0:T(8,128)(2,1)}, u32[]{:S(2)}, u32[]{:S(2)}) collective-permute-start(bf16[288,2048]{1,0:T(8,128)(2,1)} %collective-permute-done.4), channel_id=1, source_target_pairs={{0,1},{1,0},{2,3},{3,2},{4,5},{5,4},{6,7},{7,6},{8,9},{9,8},{10,11... | collective-permute-start | bytes 3538952 | tf_op jit(solution)/shard_map/ppermute | solution.py:164
  142.1 55.1 %collective-permute-start.24 = (bf16[288,2048]{1,0:T(8,128)(2,1)}, bf16[288,2048]{1,0:T(8,128)(2,1)}, u32[]{:S(2)}, u32[]{:S(2)}) collective-permute-start(bf16[288,2048]{1,0:T(8,128)(2,1)} %collective-permute-done.5), channel_id=1, source_target_pairs={{0,1},{1,0},{2,3},{3,2},{4,5},{5,4},{6,7},{7,6},{8,9},{9,8},{10,11... | collective-permute-start | bytes 3538952 | tf_op jit(solution)/shard_map/ppermute | solution.py:164
  192.2 95.6 %collective-permute-start.8 = (bf16[288,2304]{1,0:T(8,128)(2,1)}, bf16[288,2304]{1,0:T(8,128)(2,1)}, u32[]{:S(2)}, u32[]{:S(2)}) collective-permute-start(bf16[288,2304]{1,0:T(8,128)(2,1)} %get-tuple-element.303), channel_id=1, source_target_pairs={{0,16},{4,20},{8,24},{12,28},{16,0},{20,4},{24,8},{28,12},{1,17},{... | collective-permute-start | bytes 3981320 | tf_op jit(solution)/shard_map/ppermute | solution.py:164
  322.2 43.2 %all-to-all-start.1 = ((bf16[8,128,512]{2,1,0:T(8,128)(2,1)}), bf16[8,128,512]{2,1,0:T(8,128)(2,1)}, u32[]{:S(2)}, u32[]{:S(2)}) async-start(bf16[8,128,512]{2,1,0:T(8,128)(2,1)} %bitcast.30), calls=%async_computation.1 | async-start | bytes 2097152 | tf_op jit(solution)/shard_map/all_to_all | solution.py:168
  326.6 36.5 %collective-permute-start.39 = (bf16[4,256,512]{2,1,0:T(8,128)(2,1)S(1)}, bf16[4,256,512]{2,1,0:T(8,128)(2,1)S(1)}, u32[]{:S(2)}, u32[]{:S(2)}) collective-permute-start(bf16[4,256,512]{2,1,0:T(8,128)(2,1)S(1)} %all-to-all-done), channel_id=1, source_target_pairs={{0,4},{4,0},{8,12},{12,8},{16,20},{20,16},{24,28},{28,24},{1,5},{5... | collective-permute-start | bytes 3145736 | tf_op jit(solution)/shard_map/ppermute | solution.py:184
  395.3 41.2 %all-to-all-start.3 = ((bf16[8,128,512]{2,1,0:T(8,128)(2,1)}), bf16[8,128,512]{2,1,0:T(8,128)(2,1)S(1)}, u32[]{:S(2)}, u32[]{:S(2)}) async-start(bf16[8,128,512]{2,1,0:T(8,128)(2,1)} %bitcast.32), calls=%async_computation.3 | async-start | bytes 2097152 | tf_op jit(solution)/shard_map/all_to_all | solution.py:168
  398.8 35.5 %collective-permute-start.40 = (bf16[4,256,512]{2,1,0:T(8,128)(2,1)S(1)}, bf16[4,256,512]{2,1,0:T(8,128)(2,1)S(1)}, u32[]{:S(2)}, u32[]{:S(2)}) collective-permute-start(bf16[4,256,512]{2,1,0:T(8,128)(2,1)S(1)} %all-to-all-done.2), channel_id=1, source_target_pairs={{0,4},{4,0},{8,12},{12,8},{16,20},{20,16},{24,28},{28,24},{1,5},{5... | collective-permute-start | bytes 3145736 | tf_op jit(solution)/shard_map/ppermute | solution.py:184
  505.7 59.4 %collective-permute-start.41 = (bf16[288,2304]{1,0:T(8,128)(2,1)S(1)}, bf16[288,2304]{1,0:T(8,128)(2,1)}, u32[]{:S(2)}, u32[]{:S(2)}) collective-permute-start(bf16[288,2304]{1,0:T(8,128)(2,1)S(1)} %copy-done.64), channel_id=1, source_target_pairs={{0,16},{4,20},{8,24},{12,28},{16,0},{20,4},{24,8},{28,12},{1,17},{... | collective-permute-start | bytes 3981320 | tf_op jit(solution)/shard_map/ppermute | solution.py:164
  565.1 31.3 %collective-permute-start.46 = (bf16[288,2304]{1,0:T(8,128)(2,1)}, bf16[288,2304]{1,0:T(8,128)(2,1)}, u32[]{:S(2)}, u32[]{:S(2)}) collective-permute-start(bf16[288,2304]{1,0:T(8,128)(2,1)} %collective-permute-done.41.refs_0_), channel_id=1, source_target_pairs={{0,2},{1,3},{2,0},{3,1},{4,6},{5,7},{6,4},{7,5},{8,10},{9,11},{10,... | collective-permute-start | bytes 3981320 | tf_op jit(solution)/shard_map/ppermute | solution.py:164
  566.0 33.9 %collective-permute-start.42 = (bf16[256,2304]{1,0:T(8,128)(2,1)}, bf16[256,2304]{1,0:T(8,128)(2,1)}, u32[]{:S(2)}, u32[]{:S(2)}) collective-permute-start(bf16[256,2304]{1,0:T(8,128)(2,1)} %multiply_convert_fusion.4), channel_id=1, source_target_pairs={{0,8},{8,12},{12,4},{4,0},{16,24},{24,28},{28,20},{20,16},{1,9},{9... | collective-permute-start | bytes 3538952 | tf_op jit(solution)/shard_map/ppermute | solution.py:109
  566.0 33.9 %collective-permute-start.43 = (bf16[256,2304]{1,0:T(8,128)(2,1)}, bf16[256,2304]{1,0:T(8,128)(2,1)}, u32[]{:S(2)}, u32[]{:S(2)}) collective-permute-start(bf16[256,2304]{1,0:T(8,128)(2,1)} %multiply_convert_fusion.4), channel_id=1, source_target_pairs={{8,0},{12,8},{4,12},{0,4},{24,16},{28,24},{20,28},{16,20},{9,1},{1... | collective-permute-start | bytes 3538952 | tf_op jit(solution)/shard_map/ppermute | solution.py:109
  568.1 39.3 %collective-permute-start.47 = (bf16[288,2304]{1,0:T(8,128)(2,1)}, bf16[288,2304]{1,0:T(8,128)(2,1)}, u32[]{:S(2)}, u32[]{:S(2)}) collective-permute-start(bf16[288,2304]{1,0:T(8,128)(2,1)} %collective-permute-done.41.refs_0_), channel_id=1, source_target_pairs={{0,1},{1,0},{2,3},{3,2},{4,5},{5,4},{6,7},{7,6},{8,9},{9,8},{10,11... | collective-permute-start | bytes 3981320 | tf_op jit(solution)/shard_map/ppermute | solution.py:164
  618.5 60.5 %collective-permute-start.49 = (bf16[288,2304]{1,0:T(8,128)(2,1)}, bf16[288,2304]{1,0:T(8,128)(2,1)}, u32[]{:S(2)}, u32[]{:S(2)}) collective-permute-start(bf16[288,2304]{1,0:T(8,128)(2,1)} %get-tuple-element.374), channel_id=1, source_target_pairs={{0,16},{4,20},{8,24},{12,28},{16,0},{20,4},{24,8},{28,12},{1,17},{... | collective-permute-start | bytes 3981320 | tf_op jit(solution)/shard_map/ppermute | solution.py:164
  682.0 39.4 %collective-permute-start.55 = (bf16[288,2304]{1,0:T(8,128)(2,1)}, bf16[288,2304]{1,0:T(8,128)(2,1)S(1)}, u32[]{:S(2)}, u32[]{:S(2)}) collective-permute-start(bf16[288,2304]{1,0:T(8,128)(2,1)} %collective-permute-done.49.refs_0_), channel_id=1, source_target_pairs={{0,1},{1,0},{2,3},{3,2},{4,5},{5,4},{6,7},{7,6},{8,9},{9,8},{10,11... | collective-permute-start | bytes 3981320 | tf_op jit(solution)/shard_map/ppermute | solution.py:164
  1118.7 34.1 %all-to-all-start.6 = ((bf16[8,128,512]{2,1,0:T(8,128)(2,1)}), bf16[8,128,512]{2,1,0:T(8,128)(2,1)}, u32[]{:S(2)}, u32[]{:S(2)}) async-start(bf16[8,128,512]{2,1,0:T(8,128)(2,1)} %bitcast.374), calls=%async_computation.6 | async-start | bytes 2097152 | tf_op jit(solution)/shard_map/all_to_all | solution.py:168
  1152.9 47.2 %all-to-all-start.7 = ((bf16[8,128,512]{2,1,0:T(8,128)(2,1)}), bf16[8,128,512]{2,1,0:T(8,128)(2,1)S(1)}, u32[]{:S(2)}, u32[]{:S(2)}) async-start(bf16[8,128,512]{2,1,0:T(8,128)(2,1)} %bitcast.85), calls=%async_computation.7 | async-start | bytes 2097152 | tf_op jit(solution)/shard_map/all_to_all | solution.py:168
  1165.3 207.0 %collective-permute-start.87 = (bf16[2304,1024]{1,0:T(8,128)(2,1)}, bf16[2304,1024]{1,0:T(8,128)(2,1)}, u32[]{:S(2)}, u32[]{:S(2)}) collective-permute-start(bf16[2304,1024]{1,0:T(8,128)(2,1)} %convolution_convert_fusion.1), channel_id=1, source_target_pairs={{0,1},{1,0},{2,3},{3,2},{4,5},{5,4},{6,7},{7,6},{8,9},{9,8},{10,11... | collective-permute-start | bytes 14155784 | tf_op jit(solution)/shard_map/ppermute | solution.py:164
  1203.6 34.8 %collective-permute-start.83 = (bf16[4,256,512]{1,2,0:T(8,128)(2,1)}, bf16[4,256,512]{1,2,0:T(8,128)(2,1)}, u32[]{:S(2)}, u32[]{:S(2)}) collective-permute-start(bf16[4,256,512]{1,2,0:T(8,128)(2,1)} %bitcast.407), channel_id=1, source_target_pairs={{0,4},{4,0},{8,12},{12,8},{16,20},{20,16},{24,28},{28,24},{1,5},{5... | collective-permute-start | bytes 3145736 | tf_op jit(solution)/shard_map/ppermute | solution.py:184
  1205.6 35.3 %all-to-all-start.8 = ((bf16[8,128,512]{2,1,0:T(8,128)(2,1)}), bf16[8,128,512]{2,1,0:T(8,128)(2,1)S(1)}, u32[]{:S(2)}, u32[]{:S(2)}) async-start(bf16[8,128,512]{2,1,0:T(8,128)(2,1)} %bitcast.405), calls=%async_computation.8 | async-start | bytes 2097152 | tf_op jit(solution)/shard_map/all_to_all | solution.py:168
  1213.6 153.5 %collective-permute-start.82 = (bf16[2,288,2304]{2,1,0:T(8,128)(2,1)}, bf16[2,288,2304]{2,1,0:T(8,128)(2,1)}, u32[]{:S(2)}, u32[]{:S(2)}) collective-permute-start(bf16[2,288,2304]{2,1,0:T(8,128)(2,1)} %slice_bitcast_fusion.10), channel_id=1, source_target_pairs={{0,2},{1,3},{2,0},{3,1},{4,6},{5,7},{6,4},{7,5},{8,10},{9,11},{10,... | collective-permute-start | bytes 7962632 | tf_op jit(solution)/shard_map/ppermute | solution.py:164
  1240.8 40.6 %all-to-all-start.9 = ((bf16[4,256,512]{1,2,0:T(8,128)(2,1)}), bf16[4,256,512]{1,2,0:T(8,128)(2,1)S(1)}, u32[]{:S(2)}, u32[]{:S(2)}) async-start(bf16[4,256,512]{1,2,0:T(8,128)(2,1)} %fusion.76), calls=%async_computation.9 | async-start | bytes 2097152 | tf_op jit(solution)/shard_map/all_to_all | solution.py:175
  1311.5 37.7 %all-to-all-start.11 = ((bf16[4,256,512]{1,2,0:T(8,128)(2,1)}), bf16[4,256,512]{1,2,0:T(8,128)(2,1)S(1)}, u32[]{:S(2)}, u32[]{:S(2)}) async-start(bf16[4,256,512]{1,2,0:T(8,128)(2,1)} %fusion.75), calls=%async_computation.11 | async-start | bytes 2097152 | tf_op jit(solution)/shard_map/all_to_all | solution.py:175
  1367.0 79.5 %collective-permute-start.86 = (bf16[2304,2048]{1,0:T(8,128)(2,1)}, bf16[2304,2048]{1,0:T(8,128)(2,1)}, u32[]{:S(2)}, u32[]{:S(2)}) collective-permute-start(bf16[2304,2048]{1,0:T(8,128)(2,1)} %convolution_convert_fusion), channel_id=1, source_target_pairs={{0,1},{1,0},{2,3},{3,2},{4,5},{5,4},{6,7},{7,6},{8,9},{9,8},{10,11... | collective-permute-start | bytes 28311560 | tf_op jit(solution)/shard_map/ppermute | solution.py:164
  1382.0 134.8 %collective-permute-start.108 = (bf16[2,576,2304]{2,1,0:T(8,128)(2,1)}, bf16[2,576,2304]{2,1,0:T(8,128)(2,1)}, u32[]{:S(2)}, u32[]{:S(2)}) collective-permute-start(bf16[2,576,2304]{2,1,0:T(8,128)(2,1)} %slice_bitcast_fusion), channel_id=1, source_target_pairs={{0,1},{1,0},{2,3},{3,2},{4,5},{5,4},{6,7},{7,6},{8,9},{9,8},{10,11... | collective-permute-start | bytes 15925256 | tf_op jit(solution)/shard_map/ppermute | solution.py:164
  1382.4 61.0 %collective-permute-start.85 = (bf16[288,2304]{1,0:T(8,128)(2,1)}, bf16[288,2304]{1,0:T(8,128)(2,1)}, u32[]{:S(2)}, u32[]{:S(2)}) collective-permute-start(bf16[288,2304]{1,0:T(8,128)(2,1)} %slice_bitcast_fusion.16), channel_id=1, source_target_pairs={{0,16},{4,20},{8,24},{12,28},{16,0},{20,4},{24,8},{28,12},{1,17},{... | collective-permute-start | bytes 3981320 | tf_op jit(solution)/shard_map/ppermute | solution.py:164
  1388.1 77.9 %collective-permute-start.103 = (bf16[2,576,2304]{2,1,0:T(8,128)(2,1)}, bf16[2,576,2304]{2,1,0:T(8,128)(2,1)}, u32[]{:S(2)}, u32[]{:S(2)}) collective-permute-start(bf16[2,576,2304]{2,1,0:T(8,128)(2,1)} %slice_bitcast_fusion.2), channel_id=1, source_target_pairs={{0,1},{1,0},{2,3},{3,2},{4,5},{5,4},{6,7},{7,6},{8,9},{9,8},{10,11... | collective-permute-start | bytes 15925256 | tf_op jit(solution)/shard_map/ppermute | solution.py:164
  1494.1 58.0 %collective-permute-start.104 = (bf16[2,288,2304]{2,1,0:T(8,128)(2,1)}, bf16[2,288,2304]{2,1,0:T(8,128)(2,1)}, u32[]{:S(2)}, u32[]{:S(2)}) collective-permute-start(bf16[2,288,2304]{2,1,0:T(8,128)(2,1)} %slice_bitcast_fusion.8), channel_id=1, source_target_pairs={{0,2},{1,3},{2,0},{3,1},{4,6},{5,7},{6,4},{7,5},{8,10},{9,11},{10,... | collective-permute-start | bytes 7962632 | tf_op jit(solution)/shard_map/ppermute | solution.py:164
  1513.2 43.8 %collective-permute-start.96 = (bf16[288,3072]{1,0:T(8,128)(2,1)}, bf16[288,3072]{1,0:T(8,128)(2,1)}, u32[]{:S(2)}, u32[]{:S(2)}) collective-permute-start(bf16[288,3072]{1,0:T(8,128)(2,1)} %pad_maximum_fusion.12), channel_id=1, source_target_pairs={{8,0},{16,8},{24,16},{28,24},{20,28},{12,20},{4,12},{0,4},{9,1},{1... | collective-permute-start | bytes 5308424 | tf_op jit(solution)/shard_map/ppermute | solution.py:109
  1515.6 41.4 %collective-permute-start.95 = (bf16[288,3072]{1,0:T(8,128)(2,1)}, bf16[288,3072]{1,0:T(8,128)(2,1)}, u32[]{:S(2)}, u32[]{:S(2)}) collective-permute-start(bf16[288,3072]{1,0:T(8,128)(2,1)} %fusion.82), channel_id=1, source_target_pairs={{0,8},{8,16},{16,24},{24,28},{28,20},{20,12},{12,4},{4,0},{1,9},{9... | collective-permute-start | bytes 5308424 | tf_op jit(solution)/shard_map/ppermute | solution.py:109
  1554.6 58.6 %collective-permute-start.105 = (bf16[288,2304]{1,0:T(8,128)(2,1)S(1)}, bf16[288,2304]{1,0:T(8,128)(2,1)S(1)}, u32[]{:S(2)}, u32[]{:S(2)}) collective-permute-start(bf16[288,2304]{1,0:T(8,128)(2,1)S(1)} %slice_bitcast_fusion.14), channel_id=1, source_target_pairs={{0,16},{4,20},{8,24},{12,28},{16,0},{20,4},{24,8},{28,12},{1,17},{... | collective-permute-start | bytes 3981320 | tf_op jit(solution)/shard_map/ppermute | solution.py:164
  1559.4 65.0 %collective-permute-start.98 = (bf16[288,3072]{1,0:T(8,128)(2,1)S(1)}, bf16[288,3072]{1,0:T(8,128)(2,1)S(1)}, u32[]{:S(2)}, u32[]{:S(2)}) collective-permute-start(bf16[288,3072]{1,0:T(8,128)(2,1)S(1)} %add_convert_fusion.11), channel_id=1, source_target_pairs={{8,0},{16,8},{24,16},{28,24},{20,28},{12,20},{4,12},{0,4},{9,1},{1... | collective-permute-start | bytes 5308424 | tf_op jit(solution)/shard_map/ppermute | solution.py:109
  1562.4 62.0 %collective-permute-start.97 = (bf16[288,3072]{1,0:T(8,128)(2,1)S(1)}, bf16[288,3072]{1,0:T(8,128)(2,1)S(1)}, u32[]{:S(2)}, u32[]{:S(2)}) collective-permute-start(bf16[288,3072]{1,0:T(8,128)(2,1)S(1)} %add_convert_fusion.12), channel_id=1, source_target_pairs={{0,8},{8,16},{16,24},{24,28},{28,20},{20,12},{12,4},{4,0},{1,9},{9... | collective-permute-start | bytes 5308424 | tf_op jit(solution)/shard_map/ppermute | solution.py:109
  1563.8 89.0 %collective-permute-start.109 = (bf16[2,288,2304]{2,1,0:T(8,128)(2,1)S(1)}, bf16[2,288,2304]{2,1,0:T(8,128)(2,1)S(1)}, u32[]{:S(2)}, u32[]{:S(2)}) collective-permute-start(bf16[2,288,2304]{2,1,0:T(8,128)(2,1)S(1)} %slice_bitcast_fusion.6), channel_id=1, source_target_pairs={{0,2},{1,3},{2,0},{3,1},{4,6},{5,7},{6,4},{7,5},{8,10},{9,11},{10,... | collective-permute-start | bytes 7962632 | tf_op jit(solution)/shard_map/ppermute | solution.py:164
  1613.6 42.2 %collective-permute-start.106 = (bf16[288,2304]{1,0:T(8,128)(2,1)S(1)}, bf16[288,2304]{1,0:T(8,128)(2,1)S(1)}, u32[]{:S(2)}, u32[]{:S(2)}) collective-permute-start(bf16[288,2304]{1,0:T(8,128)(2,1)S(1)} %fusion.33), channel_id=1, source_target_pairs={{0,2},{1,3},{2,0},{3,1},{4,6},{5,7},{6,4},{7,5},{8,10},{9,11},{10,... | collective-permute-start | bytes 3981320 | tf_op jit(solution)/shard_map/ppermute | solution.py:164
  1625.1 64.6 %collective-permute-start.100 = (bf16[288,3072]{1,0:T(8,128)(2,1)S(1)}, bf16[288,3072]{1,0:T(8,128)(2,1)S(1)}, u32[]{:S(2)}, u32[]{:S(2)}) collective-permute-start(bf16[288,3072]{1,0:T(8,128)(2,1)S(1)} %add_convert_fusion.9), channel_id=1, source_target_pairs={{8,0},{16,8},{24,16},{28,24},{20,28},{12,20},{4,12},{0,4},{9,1},{1... | collective-permute-start | bytes 5308424 | tf_op jit(solution)/shard_map/ppermute | solution.py:109
  1629.1 61.9 %collective-permute-start.99 = (bf16[288,3072]{1,0:T(8,128)(2,1)S(1)}, bf16[288,3072]{1,0:T(8,128)(2,1)S(1)}, u32[]{:S(2)}, u32[]{:S(2)}) collective-permute-start(bf16[288,3072]{1,0:T(8,128)(2,1)S(1)} %add_convert_fusion.10), channel_id=1, source_target_pairs={{0,8},{8,16},{16,24},{24,28},{28,20},{20,12},{12,4},{4,0},{1,9},{9... | collective-permute-start | bytes 5308424 | tf_op jit(solution)/shard_map/ppermute | solution.py:109
  1654.9 44.6 %collective-permute-start.113 = (bf16[288,2304]{1,0:T(8,128)(2,1)S(1)}, bf16[288,2304]{1,0:T(8,128)(2,1)S(1)}, u32[]{:S(2)}, u32[]{:S(2)}) collective-permute-start(bf16[288,2304]{1,0:T(8,128)(2,1)S(1)} %copy-done.21), channel_id=1, source_target_pairs={{0,2},{1,3},{2,0},{3,1},{4,6},{5,7},{6,4},{7,5},{8,10},{9,11},{10,... | collective-permute-start | bytes 3981320 | tf_op jit(solution)/shard_map/ppermute | solution.py:164
  1656.0 95.8 %collective-permute-start.107 = (bf16[576,2304]{1,0:T(8,128)(2,1)S(1)}, bf16[576,2304]{1,0:T(8,128)(2,1)S(1)}, u32[]{:S(2)}, u32[]{:S(2)}) collective-permute-start(bf16[576,2304]{1,0:T(8,128)(2,1)S(1)} %pad_maximum_fusion.3), channel_id=1, source_target_pairs={{0,1},{1,0},{2,3},{3,2},{4,5},{5,4},{6,7},{7,6},{8,9},{9,8},{10,11... | collective-permute-start | bytes 7962632 | tf_op jit(solution)/shard_map/ppermute | solution.py:164
  1691.0 58.6 %collective-permute-start.110 = (bf16[288,2304]{1,0:T(8,128)(2,1)S(1)}, bf16[288,2304]{1,0:T(8,128)(2,1)S(1)}, u32[]{:S(2)}, u32[]{:S(2)}) collective-permute-start(bf16[288,2304]{1,0:T(8,128)(2,1)S(1)} %slice_bitcast_fusion.12), channel_id=1, source_target_pairs={{0,16},{4,20},{8,24},{12,28},{16,0},{20,4},{24,8},{28,12},{1,17},{... | collective-permute-start | bytes 3981320 | tf_op jit(solution)/shard_map/ppermute | solution.py:164
  1694.3 56.6 %collective-permute-start.101 = (bf16[288,3072]{1,0:T(8,128)(2,1)S(1)}, bf16[288,3072]{1,0:T(8,128)(2,1)S(1)}, u32[]{:S(2)}, u32[]{:S(2)}) collective-permute-start(bf16[288,3072]{1,0:T(8,128)(2,1)S(1)} %add_convert_fusion.8), channel_id=1, source_target_pairs={{0,2},{1,3},{2,0},{3,1},{4,6},{5,7},{6,4},{7,5},{8,10},{9,11},{10,... | collective-permute-start | bytes 5308424 | tf_op jit(solution)/shard_map/ppermute | solution.py:164
  1699.6 80.6 %collective-permute-start.114 = (bf16[576,2304]{1,0:T(8,128)(2,1)S(1)}, bf16[576,2304]{1,0:T(8,128)(2,1)S(1)}, u32[]{:S(2)}, u32[]{:S(2)}) collective-permute-start(bf16[576,2304]{1,0:T(8,128)(2,1)S(1)} %pad_maximum_fusion.5), channel_id=1, source_target_pairs={{0,1},{1,0},{2,3},{3,2},{4,5},{5,4},{6,7},{7,6},{8,9},{9,8},{10,11... | collective-permute-start | bytes 7962632 | tf_op jit(solution)/shard_map/ppermute | solution.py:164
  1751.7 31.4 %collective-permute-start.102 = (bf16[288,3072]{1,0:T(8,128)(2,1)S(1)}, bf16[288,3072]{1,0:T(8,128)(2,1)S(1)}, u32[]{:S(2)}, u32[]{:S(2)}) collective-permute-start(bf16[288,3072]{1,0:T(8,128)(2,1)S(1)} %add_convert_fusion.7), channel_id=1, source_target_pairs={{0,1},{1,0},{2,3},{3,2},{4,5},{5,4},{6,7},{7,6},{8,9},{9,8},{10,11... | collective-permute-start | bytes 5308424 | tf_op jit(solution)/shard_map/ppermute | solution.py:164
  (252 other events, 3208.5 us)

commit v4 on v3

v4 whole, which is shorter than its diff:
```python
import functools
import math

import jax
import jax.numpy as jnp
from jax import lax
from jax.experimental import pallas as pl
from jax.experimental.pallas import tpu as pltpu
from jax.sharding import PartitionSpec as P

QUERY_HEADS = 8
KEY_VALUE_HEADS = 4
HEAD_SIZE = 256
PAIRED = QUERY_HEADS // KEY_VALUE_HEADS

eps_norm = 1e-06
soft_cap = 50.0
rope_base = 10000.0
gelu_coeff = math.sqrt(2.0 / math.pi)
f32 = jnp.float32
bf16 = jnp.bfloat16
VMEM_LIMIT = 56 * 1024 * 1024


def dot(a, b, dims):
    return lax.dot_general(a, b, (dims, ((), ())), preferred_element_type=f32)


NN = ((1,), (0,))
NT = ((1,), (1,))
TN = ((0,), (0,))


def inverse_powers(exponents):
    return 1.0 / jnp.left_shift(jnp.ones_like(exponents), exponents).astype(f32)


def norm_factor(values):
    return lax.rsqrt(jnp.mean(values * values, axis=-1, keepdims=True) + eps_norm)


def norm_back(values, factor, gain, grad):
    scaled = grad * gain
    inner = jnp.mean(values * scaled, axis=-1, keepdims=True)
    grad_values = factor * scaled - values * (factor * factor * factor * inner)
    return grad_values, jnp.sum(grad * values * factor, axis=0)


def gelu_parts(values):
    inner = gelu_coeff * (values + 0.044715 * values * values * values)
    return jnp.tanh(inner)


def rotary_rows(positions):
    half_dim = HEAD_SIZE // 2
    frequency = jnp.exp(
        jnp.arange(half_dim, dtype=f32) * (-2.0 * math.log(rope_base) / HEAD_SIZE)
    )
    angles = positions.astype(f32)[:, None] * frequency[None, :]
    return jnp.cos(angles), jnp.sin(angles)


def ring_place(index, size):
    return jnp.where(index % 2 == 0, index // 2, size - 1 - index // 2)


def ring_index(place, size):
    return jnp.where(place < size // 2, 2 * place, 2 * (size - 1 - place) + 1)


def ring_perms(size):
    order = list(range(0, size, 2)) + list(range(size - 1, 0, -2))
    up = [
        (base + order[i], base + order[(i + 1) % size])
        for base in range(0, lax.axis_size("wide"), size)
        for i in range(size)
    ]
    return up, [(b, a) for a, b in up]


def ring_offsets(size):
    out = [0]
    for k in range(1, size // 2):
        out += [-k, k]
    return out + [size // 2]


class Clock:
    def __init__(self, token):
        self.token = token

    def sync(self, *arrays):
        *arrays, self.token = lax.optimization_barrier(tuple(arrays) + (self.token,))
        return arrays

    def hold(self, value):
        return lax.optimization_barrier((value, self.token))[0]


def hop(a, b, size):
    up, down = ring_perms(size)
    return lax.ppermute(a, "wide", up), lax.ppermute(b, "wide", down)


def low_sum(*terms):
    return sum(t.astype(f32) for t in terms).astype(bf16)


def halves(value):
    half = value.shape[0] // 2
    return value[:half], value[half:]


def add_first(whole, part):
    count = part.shape[0]
    return jnp.concatenate([low_sum(whole[:count], part), whole[count:].astype(bf16)], axis=0)


def add_last(whole, part):
    count = whole.shape[0] - part.shape[0]
    return jnp.concatenate([whole[:count].astype(bf16), low_sum(whole[count:], part)], axis=0)


def ring_gather(clock, value, size, beside=lambda step: ()):
    a = b = clock.hold(value)
    out, other = [a], []
    for k in range(1, size // 2 + 1):
        if k == size // 2:
            a, b = halves(a)[0], halves(b)[1]
        work = beside(k - 1)
        a, b = hop(a, b, size)
        a, b, *work = clock.sync(a, b, *work)
        out += [a, b]
        other.append(work)
    return out, other


def ring_scatter(clock, part_of, rows, size, beside=lambda step: ()):
    a, b = halves(clock.hold(part_of(size // 2).astype(bf16)))
    other = []
    for k in range(size // 2 - 1, -1, -1):
        work = beside(size // 2 - 1 - k)
        a, b = hop(a, b, size)
        a, b, *work = clock.sync(a, b, *work)
        other.append(work)
        if k == size // 2 - 1 and k > 0:
            a = add_first(part_of(k), a)
            b = add_last(part_of(-k), b)
        elif k > 0:
            a = low_sum(part_of(k), a)
            b = low_sum(part_of(-k), b)
    return part_of(0).astype(f32) + a.astype(f32) + b.astype(f32), other


def swap(value, axis, bit):
    size = lax.axis_size(axis)
    return lax.ppermute(value, axis, [(i, i ^ bit) for i in range(size)])


def all_to_all(value):
    return lax.all_to_all(value, "wide", split_axis=0, concat_axis=0, tiled=True)


def heads_all_to_all(value):
    size = lax.axis_size("wide")
    classes = size // KEY_VALUE_HEADS
    groups = [list(range(c, size, classes)) for c in range(classes)]
    return lax.all_to_all(
        value, "wide", split_axis=0, concat_axis=0, axis_index_groups=groups, tiled=True
    )


def class_ring(value):
    size = lax.axis_size("wide")
    classes = size // KEY_VALUE_HEADS
    perm = [(i, i // classes * classes + (i + 1) % classes) for i in range(size)]
    return lax.ppermute(value, "wide", perm)


def slice_values(codes, width):
    lift = jnp.where(width == 0, 0.0, 0.5).astype(bf16)
    large = jnp.where(width == 0, 0.0, jnp.where(width == 1, 1.5 * 2**11, 1.5 * 2**13)).astype(bf16)
    top = jnp.where(width == 0, 127.0, jnp.where(width == 1, 112.0, 64.0)).astype(bf16)
    return jnp.minimum(((codes + lift) + large) - large, top)


def proj_slice_kernel(places, info, *refs, blocks, count):
    code_refs, scale_ref, out_refs = refs[: 2 * blocks], refs[2 * blocks], refs[len(refs) - count :]
    mine = pl.program_id(1) == info[0]

    def write(code_ref):
        codes = code_ref[...]
        scale = scale_ref[...].astype(bf16)
        for s, out_ref in enumerate(out_refs):
            out_ref[...] = slice_values(codes, info[1 + s]) * scale

    for k in range(blocks):
        here = pl.program_id(0) == k
        pl.when(jnp.logical_and(here, mine))(functools.partial(write, code_refs[2 * k]))
        pl.when(jnp.logical_and(here, jnp.logical_not(mine)))(
            functools.partial(write, code_refs[2 * k + 1])
        )


def proj_slices(own, other, places, info, scale, width, weights, total, count):
    blocks = len(own)
    rows = own[0].shape[0]
    inputs = [block for pair in zip(own, other) for block in pair] + [scale]
    grid_spec = pltpu.PrefetchScalarGridSpec(
        num_scalar_prefetch=2,
        grid=(blocks, 2),
        in_specs=[pl.BlockSpec((rows, width), lambda k, j, p, i: (0, 0))] * (2 * blocks)
        + [pl.BlockSpec((1, width), lambda k, j, p, i: (0, j))]
        + [pl.BlockSpec(memory_space=pl.ANY)] * len(weights),
        out_specs=[pl.BlockSpec((rows, width), lambda k, j, p, i: (p[k], j))] * count,
    )
    return pl.pallas_call(
        functools.partial(proj_slice_kernel, blocks=blocks, count=count),
        grid_spec=grid_spec,
        out_shape=[jax.ShapeDtypeStruct((total * rows, 2 * width), bf16)] * count,
        input_output_aliases={2 + len(inputs) + s: s for s in range(len(weights))},
        compiler_params=pltpu.CompilerParams(vmem_limit_bytes=VMEM_LIMIT),
        cost_estimate=pl.CostEstimate(
            flops=20 * count * blocks * rows * width,
            bytes_accessed=4 * blocks * rows * width * (1 + count),
            transcendentals=0,
        ),
        name="proj_slices",
    )(places, info, *inputs, *weights)


def out_slice_kernel(places, info, *refs, split, count):
    inputs, scale_ref, out_refs = refs[: -1 - count], refs[-1 - count], refs[-count:]
    members = len(inputs) // 2
    member = info[1 + count]
    mine = pl.program_id(1) == info[0]

    def write(code_refs):
        scale = scale_ref[...].astype(bf16)
        for t, code_ref in enumerate(code_refs):
            first = pl.multiple_of(jnp.bitwise_xor(member, t) * split, 128)
            for s, out_ref in enumerate(out_refs):
                out_ref[:, pl.ds(first, split)] = slice_values(code_ref[0], info[1 + s]) * scale

    pl.when(mine)(lambda: write(inputs[:members]))
    pl.when(jnp.logical_not(mine))(lambda: write(inputs[members:]))


def out_slices(own, other, places, info, scale, count):
    blocks, rows, split = own[0].shape
    width = split * len(own)
    inputs = list(own) + list(other)
    grid_spec = pltpu.PrefetchScalarGridSpec(
        num_scalar_prefetch=2,
        grid=(blocks, 2),
        in_specs=[pl.BlockSpec((1, rows, split), lambda k, j, p, i: (k, 0, 0))] * len(inputs)
        + [pl.BlockSpec((rows, 1), lambda k, j, p, i: (p[k], 0))],
        out_specs=[pl.BlockSpec((rows, width), lambda k, j, p, i: (p[k], j))] * count,
    )
    return pl.pallas_call(
        functools.partial(out_slice_kernel, split=split, count=count),
        grid_spec=grid_spec,
        out_shape=[jax.ShapeDtypeStruct((blocks * rows, 2 * width), bf16)] * count,
        compiler_params=pltpu.CompilerParams(vmem_limit_bytes=VMEM_LIMIT),
        cost_estimate=pl.CostEstimate(
            flops=20 * count * blocks * rows * width,
            bytes_accessed=4 * blocks * rows * width * (1 + count),
            transcendentals=0,
        ),
        name="out_slices",
    )(places, info, *inputs, scale)


def own_slice_kernel(pieces, info, code_ref, row_ref, col_ref, *out_refs):
    count = len(out_refs) // 3
    for m in range(3):
        codes = code_ref[m].astype(f32).astype(bf16)
        scale = (row_ref[m] if m < 2 else col_ref[...]).astype(bf16)
        for s in range(count):
            out_refs[m * count + s][...] = slice_values(codes, info[1 + s]) * scale


def own_slices(codes, pieces, info, row_scale, col_scale, count):
    three, rows, cols = codes.shape
    steps = pieces.shape[0]
    piece = rows // steps
    grid_spec = pltpu.PrefetchScalarGridSpec(
        num_scalar_prefetch=2,
        grid=(steps,),
        in_specs=[
            pl.BlockSpec((three, piece, cols), lambda j, p, i: (0, p[j], 0)),
            pl.BlockSpec((2, piece, 1), lambda j, p, i: (0, j, 0)),
            pl.BlockSpec((1, cols), lambda j, p, i: (0, 0)),
        ],
        out_specs=[pl.BlockSpec((piece, cols), lambda j, p, i: (j, 0))] * (three * count),
    )
    return pl.pallas_call(
        own_slice_kernel,
        grid_spec=grid_spec,
        out_shape=[jax.ShapeDtypeStruct((2 * rows, cols), bf16)] * (three * count),
        compiler_params=pltpu.CompilerParams(vmem_limit_bytes=VMEM_LIMIT),
        cost_estimate=pl.CostEstimate(
            flops=10 * count * codes.size,
            bytes_accessed=codes.size * (4 + 2 * count),
            transcendentals=0,
        ),
        name="own_slices",
    )(pieces, info, codes, row_scale, col_scale)


def partner_slice_kernel(info, *refs, steps, count):
    piece_refs, scale_ref, out_refs = refs[:steps], refs[steps], refs[steps + 1 + count :]
    for j in range(steps):

        @pl.when(pl.program_id(0) == j)
        def _():
            codes = piece_refs[j][...]
            scale = scale_ref[...].astype(bf16)
            for s, out_ref in enumerate(out_refs):
                out_ref[...] = slice_values(codes, info[1 + s]) * scale


def partner_slices(pieces, info, scale, by_column, weights):
    steps = len(pieces)
    count = len(weights)
    piece, cols = pieces[0].shape
    if by_column:
        scale_spec = pl.BlockSpec((1, cols), lambda j, i: (0, 0))
    else:
        scale_spec = pl.BlockSpec((piece, 1), lambda j, i: (steps + j, 0))
    grid_spec = pltpu.PrefetchScalarGridSpec(
        num_scalar_prefetch=1,
        grid=(steps,),
        in_specs=[pl.BlockSpec((piece, cols), lambda j, i: (0, 0))] * steps
        + [scale_spec]
        + [pl.BlockSpec(memory_space=pl.ANY)] * count,
        out_specs=[pl.BlockSpec((piece, cols), lambda j, i: (steps + j, 0))] * count,
    )
    return pl.pallas_call(
        functools.partial(partner_slice_kernel, steps=steps, count=count),
        grid_spec=grid_spec,
        out_shape=[jax.ShapeDtypeStruct(w.shape, bf16) for w in weights],
        input_output_aliases={2 + steps + s: s for s in range(count)},
        compiler_params=pltpu.CompilerParams(vmem_limit_bytes=VMEM_LIMIT),
        cost_estimate=pl.CostEstimate(
            flops=10 * count * steps * piece * cols,
            bytes_accessed=2 * (1 + count) * steps * piece * cols,
            transcendentals=0,
        ),
        name="partner_slices",
    )(info, *pieces, scale, *weights)


def unpack_kernel(pieces, grad_ref, *refs):
    refs[-1][0] = grad_ref[...].astype(f32)


def unpack(grad, pieces, matrix, held):
    steps = pieces.shape[0]
    rows, cols = grad.shape
    piece = rows // steps
    grid_spec = pltpu.PrefetchScalarGridSpec(
        num_scalar_prefetch=1,
        grid=(steps,),
        in_specs=[pl.BlockSpec((piece, cols), lambda j, p: (j, 0))]
        + [pl.BlockSpec(memory_space=pl.ANY)] * len(held),
        out_specs=pl.BlockSpec((1, piece, cols), lambda j, p: (matrix, p[j], 0)),
    )
    return pl.pallas_call(
        unpack_kernel,
        grid_spec=grid_spec,
        out_shape=jax.ShapeDtypeStruct((3, rows, cols), f32),
        input_output_aliases={2: 0} if held else {},
        compiler_params=pltpu.CompilerParams(vmem_limit_bytes=VMEM_LIMIT),
        cost_estimate=pl.CostEstimate(
            flops=rows * cols, bytes_accessed=6 * rows * cols, transcendentals=0
        ),
        name="unpack",
    )(pieces, grad, *held)


def turn(values, cosine, sine):
    half = HEAD_SIZE // 2
    out = []
    for j in range(values.shape[1] // HEAD_SIZE):
        a = values[:, j * HEAD_SIZE : j * HEAD_SIZE + half]
        b = values[:, j * HEAD_SIZE + half : (j + 1) * HEAD_SIZE]
        out += [a * cosine - b * sine, b * cosine + a * sine]
    return jnp.concatenate(out, axis=1)


def project_kernel(x_ref, wq_ref, wk_ref, wv_ref, cos_ref, sin_ref, q_ref, kv_ref):
    x = x_ref[...]
    cosine, sine = cos_ref[...], sin_ref[...]
    scale = HEAD_SIZE ** (-0.5)
    q_ref[0] = (turn(dot(x, wq_ref[...], NN), cosine, sine) * scale).astype(bf16)
    kv_ref[0, :, :HEAD_SIZE] = turn(dot(x, wk_ref[...], NN), cosine, sine).astype(bf16)
    kv_ref[0, :, HEAD_SIZE:] = dot(x, wv_ref[...], NN).astype(bf16)


def project(normed, weights, cosine, sine):
    rows, depth = normed.shape
    cols = PAIRED * HEAD_SIZE
    first_key = QUERY_HEADS
    first_value = QUERY_HEADS + KEY_VALUE_HEADS
    whole = lambda shape: pl.BlockSpec(shape, lambda h: (0, 0))
    return pl.pallas_call(
        project_kernel,
        grid=(KEY_VALUE_HEADS,),
        in_specs=[
            whole((rows, depth)),
            pl.BlockSpec((depth, cols), lambda h: (0, h)),
            pl.BlockSpec((depth, HEAD_SIZE), lambda h: (0, first_key + h)),
            pl.BlockSpec((depth, HEAD_SIZE), lambda h: (0, first_value + h)),
            whole(cosine.shape),
            whole(sine.shape),
        ],
        out_specs=[
            pl.BlockSpec((1, rows, cols), lambda h: (h, 0, 0)),
            pl.BlockSpec((1, rows, 2 * HEAD_SIZE), lambda h: (h, 0, 0)),
        ],
        out_shape=[
            jax.ShapeDtypeStruct((KEY_VALUE_HEADS, rows, cols), bf16),
            jax.ShapeDtypeStruct((KEY_VALUE_HEADS, rows, 2 * HEAD_SIZE), bf16),
        ],
        compiler_params=pltpu.CompilerParams(vmem_limit_bytes=VMEM_LIMIT),
        cost_estimate=pl.CostEstimate(
            flops=2 * rows * weights.size, bytes_accessed=2 * weights.size, transcendentals=0
        ),
        name="project",
    )(normed, weights, weights, weights, cosine, sine)


def turn_back_kernel(*refs, count):
    q_refs, kv_refs = refs[:count], refs[count : 2 * count]
    cos_ref, sin_ref, out_ref = refs[2 * count :]
    j = pl.program_id(1)
    scale = HEAD_SIZE ** (-0.5)
    keys = KEY_VALUE_HEADS // PAIRED
    for s in range(count):
        here = pl.program_id(0) == s

        @pl.when(jnp.logical_and(here, j < KEY_VALUE_HEADS))
        def _():
            grad = q_refs[s][0].astype(f32) * scale
            out_ref[...] = turn(grad, cos_ref[...], -sin_ref[...]).astype(bf16)

        @pl.when(jnp.logical_and(here, jnp.logical_and(j >= KEY_VALUE_HEADS, j < KEY_VALUE_HEADS + keys)))
        def _():
            grad = jnp.concatenate([kv_refs[s][i, :, :HEAD_SIZE] for i in range(PAIRED)], axis=1)
            out_ref[...] = turn(grad.astype(f32), cos_ref[...], -sin_ref[...]).astype(bf16)

        @pl.when(jnp.logical_and(here, j >= KEY_VALUE_HEADS + keys))
        def _():
            out_ref[...] = jnp.concatenate(
                [kv_refs[s][i, :, HEAD_SIZE:] for i in range(PAIRED)], axis=1
            )


def turn_back(queries, pairs, cosine, sine):
    count = len(queries)
    heads, rows, cols = queries[0].shape
    keys = heads // PAIRED
    grid = (count, heads + 2 * keys)
    whole = pl.BlockSpec(cosine.shape, lambda s, j: (0, 0))
    return pl.pallas_call(
        functools.partial(turn_back_kernel, count=count),
        grid=grid,
        in_specs=[
            pl.BlockSpec((1, rows, cols), lambda s, j: (jnp.minimum(j, heads - 1), 0, 0))
        ]
        * count
        + [
            pl.BlockSpec(
                (PAIRED, rows, cols), lambda s, j: (jnp.maximum(j - heads, 0) % keys, 0, 0)
            )
        ]
        * count
        + [whole, whole],
        out_specs=pl.BlockSpec((rows, cols), lambda s, j: (s, j)),
        out_shape=jax.ShapeDtypeStruct((count * rows, grid[1] * cols), bf16),
        compiler_params=pltpu.CompilerParams(vmem_limit_bytes=VMEM_LIMIT),
        cost_estimate=pl.CostEstimate(
            flops=4 * count * rows * grid[1] * cols,
            bytes_accessed=4 * count * rows * grid[1] * cols,
            transcendentals=0,
        ),
        name="turn_back",
    )(*queries, *pairs, cosine, sine)


def tile_positions(tile, count, start, class_index, class_rows, rows):
    index = lax.broadcasted_iota(jnp.int32, (count, 1), 0)
    place = start + jnp.bitwise_and(index, tile - 1)
    shift = class_rows.bit_length() - 1
    return (
        jnp.right_shift(place, shift) * rows
        + class_index * class_rows
        + jnp.bitwise_and(place, class_rows - 1)
    )


def stack_heads(block):
    return jnp.concatenate(
        [block[:, j * HEAD_SIZE : (j + 1) * HEAD_SIZE] for j in range(PAIRED)], axis=0
    )


def key_places(group, class_index, classes, rows):
    index = lax.broadcasted_iota(jnp.int32, (1, classes * rows), 1)
    shift = rows.bit_length() - 1
    back = jnp.bitwise_and(class_index - jnp.right_shift(index, shift), classes - 1)
    return (group * classes + back) * rows + jnp.bitwise_and(index, rows - 1)


def held_block(refs, group, cols):
    return jnp.concatenate([ref[group, :, cols] for ref in refs], axis=0)


def group_range(start, tile, class_rows, classes):
    return start // class_rows // classes, (start + tile - 1) // class_rows // classes + 1


def attn_forward_kernel(info, q_ref, *refs, tile, class_rows, rows, classes):
    kv_refs = refs[:classes]
    att_ref, exact_ref, lse_ref = refs[classes:]
    start = pl.program_id(0) * tile
    free, total = group_range(start, tile, class_rows, classes)
    queries = stack_heads(q_ref[...])
    count = queries.shape[0]
    position = tile_positions(tile, count, start, info[0], class_rows, rows)

    def step(group, carry, masked):
        acc, row_sum = carry
        keys = held_block(kv_refs, group, slice(0, HEAD_SIZE))
        values = held_block(kv_refs, group, slice(HEAD_SIZE, 2 * HEAD_SIZE))
        raw = dot(queries, keys, NT)
        weight = jnp.exp(soft_cap * jnp.tanh(raw * (1.0 / soft_cap)))
        if masked:
            weight = jnp.where(
                key_places(group, info[0], classes, rows) <= position, weight, 0.0
            )
        row_sum = row_sum + jnp.sum(weight, axis=-1, keepdims=True)
        acc = acc + dot(weight.astype(bf16), values, NN)
        return acc, row_sum

    carry = (jnp.zeros((count, HEAD_SIZE), f32), jnp.zeros((count, 1), f32))
    carry = lax.fori_loop(0, free, functools.partial(step, masked=False), carry)
    acc, row_sum = lax.fori_loop(free, total, functools.partial(step, masked=True), carry)
    exact = acc / row_sum
    lse = jnp.log(row_sum)
    for j in range(PAIRED):
        cols = slice(j * HEAD_SIZE, (j + 1) * HEAD_SIZE)
        exact_ref[:, cols] = exact[j * tile : (j + 1) * tile]
        att_ref[:, cols] = exact[j * tile : (j + 1) * tile].astype(bf16)
        lse_ref[:, j * 128 : (j + 1) * 128] = jnp.broadcast_to(
            lse[j * tile : (j + 1) * tile], (tile, 128)
        )


def attn_forward(info, queries, pairs, class_rows, rows):
    count, cols = queries.shape
    classes = len(pairs)
    length = classes * pairs[0].shape[0] * rows
    tile = min(256, count)
    grid_spec = pltpu.PrefetchScalarGridSpec(
        num_scalar_prefetch=1,
        grid=(count // tile,),
        in_specs=[pl.BlockSpec((tile, cols), lambda i, c: (i, 0))]
        + [pl.BlockSpec(p.shape, lambda i, c: (0, 0, 0)) for p in pairs],
        out_specs=[
            pl.BlockSpec((tile, cols), lambda i, c: (i, 0)),
            pl.BlockSpec((tile, cols), lambda i, c: (i, 0)),
            pl.BlockSpec((tile, PAIRED * 128), lambda i, c: (i, 0)),
        ],
    )
    return pl.pallas_call(
        functools.partial(
            attn_forward_kernel, tile=tile, class_rows=class_rows, rows=rows, classes=classes
        ),
        grid_spec=grid_spec,
        out_shape=[
            jax.ShapeDtypeStruct((count, cols), bf16),
            jax.ShapeDtypeStruct((count, cols), f32),
            jax.ShapeDtypeStruct((count, PAIRED * 128), f32),
        ],
        compiler_params=pltpu.CompilerParams(vmem_limit_bytes=VMEM_LIMIT),
        cost_estimate=pl.CostEstimate(
            flops=2 * count * PAIRED * length * 2 * HEAD_SIZE,
            bytes_accessed=8 * count * cols + 4 * length * HEAD_SIZE,
            transcendentals=2 * count * PAIRED * length,
        ),
        name="attn_forward",
    )(info, queries, *pairs)


def attn_backward_kernel(info, q_ref, grad_ref, exact_ref, lse_ref, *refs, tile, class_rows, rows, classes):
    kv_refs, dq_ref = refs[:classes], refs[classes]
    dkv_refs, sum_ref = refs[classes + 1 : 2 * classes + 1], refs[2 * classes + 1]

    @pl.when(pl.program_id(0) == 0)
    def _():
        sum_ref[...] = jnp.zeros_like(sum_ref)

    start = pl.program_id(0) * tile
    free, total = group_range(start, tile, class_rows, classes)
    queries = stack_heads(q_ref[...])
    grads = stack_heads(grad_ref[...])
    count = queries.shape[0]
    delta = jnp.sum(grads.astype(f32) * stack_heads(exact_ref[...]), axis=-1, keepdims=True)
    lse = jnp.concatenate([lse_ref[:, j * 128 : j * 128 + 1] for j in range(PAIRED)], axis=0)
    position = tile_positions(tile, count, start, info[0], class_rows, rows)

    def step(group, acc, masked):
        keys = held_block(kv_refs, group, slice(0, HEAD_SIZE))
        values = held_block(kv_refs, group, slice(HEAD_SIZE, 2 * HEAD_SIZE))
        bounded = jnp.tanh(dot(queries, keys, NT) * (1.0 / soft_cap))
        probs = jnp.exp(soft_cap * bounded - lse)
        if masked:
            probs = jnp.where(key_places(group, info[0], classes, rows) <= position, probs, 0.0)
        grad_probs = dot(grads, values, NT)
        grad_raw = (probs * (grad_probs - delta) * (1.0 - bounded * bounded)).astype(bf16)
        sum_ref[group, :, HEAD_SIZE:] += dot(probs.astype(bf16), grads, TN)
        sum_ref[group, :, :HEAD_SIZE] += dot(grad_raw, queries, TN)
        return acc + dot(grad_raw, keys, NN)

    acc = jnp.zeros((count, HEAD_SIZE), f32)
    acc = lax.fori_loop(0, free, functools.partial(step, masked=False), acc)
    acc = lax.fori_loop(free, total, functools.partial(step, masked=True), acc)
    for j in range(PAIRED):
        dq_ref[:, j * HEAD_SIZE : (j + 1) * HEAD_SIZE] = acc[j * tile : (j + 1) * tile].astype(bf16)

    @pl.when(pl.program_id(0) == pl.num_programs(0) - 1)
    def _():
        for h, ref in enumerate(dkv_refs):
            ref[...] = sum_ref[:, h * rows : (h + 1) * rows, :].astype(bf16)


def attn_backward(info, queries, pairs, grads, exact, lse, class_rows, rows):
    count, cols = queries.shape
    classes = len(pairs)
    groups = pairs[0].shape[0]
    length = classes * groups * rows
    tile = min(256, count)
    row_spec = pl.BlockSpec((tile, cols), lambda i, c: (i, 0))
    pair_specs = [pl.BlockSpec(p.shape, lambda i, c: (0, 0, 0)) for p in pairs]
    grid_spec = pltpu.PrefetchScalarGridSpec(
        num_scalar_prefetch=1,
        grid=(count // tile,),
        in_specs=[
            row_spec,
            row_spec,
            row_spec,
            pl.BlockSpec((tile, PAIRED * 128), lambda i, c: (i, 0)),
        ]
        + pair_specs,
        out_specs=[row_spec] + pair_specs,
        scratch_shapes=[pltpu.VMEM((groups, classes * rows, 2 * HEAD_SIZE), f32)],
    )
    return pl.pallas_call(
        functools.partial(
            attn_backward_kernel, tile=tile, class_rows=class_rows, rows=rows, classes=classes
        ),
        grid_spec=grid_spec,
        out_shape=[jax.ShapeDtypeStruct((count, cols), bf16)]
        + [jax.ShapeDtypeStruct(p.shape, bf16) for p in pairs],
        compiler_params=pltpu.CompilerParams(vmem_limit_bytes=VMEM_LIMIT),
        cost_estimate=pl.CostEstimate(
            flops=5 * count * PAIRED * length * 2 * HEAD_SIZE,
            bytes_accessed=10 * count * cols + 8 * length * HEAD_SIZE,
            transcendentals=2 * count * PAIRED * length,
        ),
        name="attn_backward",
    )(info, queries, grads, exact, lse, *pairs)


def per_device(
    tokens,
    cotangent,
    widths,
    attn_codes,
    attn_exps,
    out_exps,
    mlp_codes,
    gate_exps,
    down_exps,
    gain_attn,
    gain_post_attn,
    gain_mlp,
    gain_post_mlp,
):
    wide = lax.axis_size("wide")
    seq_size = lax.axis_size("seq")
    wide_index = lax.axis_index("wide")
    seq_index = lax.axis_index("seq")
    side = seq_index % 2
    is_low = side == 0
    members = seq_size // 2
    member = seq_index // 2
    half_wide = wide // 2
    place = ring_place(wide_index, wide)
    count, rows, model_dim = tokens.shape
    classes = wide // KEY_VALUE_HEADS
    class_rows = rows // classes
    class_index = wide_index % classes
    head_cols = PAIRED * HEAD_SIZE
    proj_cols = attn_exps.shape[0]
    half_proj = proj_cols // 2
    half_out = (attn_codes.shape[1] - proj_cols) // 2
    split_out = half_out // members
    attn_rows = attn_codes.shape[0]
    hidden = mlp_codes.shape[1]
    offsets = ring_offsets(wide)
    order = {o: i for i, o in enumerate(ring_offsets(half_wide))}
    seqs = range(count)
    seq_bits = [1 << i for i in range(seq_size.bit_length() - 1)]
    far_bits = list(reversed(seq_bits[1:]))
    clock = Clock(widths)

    def index_at(offset):
        return ring_index(jnp.mod(place + offset, wide), wide)

    places = jnp.stack([index_at(o) for o in offsets]).astype(jnp.int32)
    info = jnp.concatenate(
        [side[None].astype(jnp.int32), widths, member[None].astype(jnp.int32)]
    )
    class_info = class_index[None].astype(jnp.int32)
    column_scale = inverse_powers(attn_exps)[None, :]
    output_scale = inverse_powers(out_exps)[:, None]

    relative = [0]
    for bit in reversed(seq_bits):
        relative = relative + [r | bit for r in relative]
    pieces = jnp.stack([jnp.bitwise_xor(seq_index, r) for r in relative]).astype(jnp.int32)
    piece_rows = hidden // seq_size
    partner = jnp.bitwise_xor(wide_index, half_wide)
    gate_scale = inverse_powers(gate_exps)
    row_scale = jnp.concatenate(
        [
            lax.dynamic_slice_in_dim(
                gate_scale, block * hidden + pieces[j] * piece_rows, piece_rows, 1
            )
            for block in (wide_index, partner)
            for j in range(seq_size)
        ],
        axis=1,
    )[:, :, None]
    down_scale = inverse_powers(down_exps)[None, :]

    def columns(first, size):
        return lax.dynamic_slice_in_dim(attn_codes, first, size, 1)

    payload = jnp.concatenate(
        [
            columns(side * half_proj, half_proj),
            columns(proj_cols + side * half_out + member * split_out, split_out),
        ],
        axis=1,
    ).astype(bf16)
    piece_codes = lax.dynamic_slice_in_dim(mlp_codes, seq_index * piece_rows, piece_rows, 1)
    inputs = [tokens[s].astype(f32) for s in seqs]
    grad_out = [cotangent[s].astype(f32) for s in seqs]
    cosine, sine = rotary_rows(wide_index * rows + jnp.arange(rows))

    blocks, others = [clock.hold(payload)], []
    proj_weights = []

    def slice_more(first, last):
        return proj_slices(
            blocks[first:last],
            others[first:last],
            places[first:last],
            info,
            column_scale,
            half_proj,
            proj_weights,
            wide,
            count,
        )

    a = b = blocks[0]
    sliced = 0
    steps = half_wide
    for k in range(1, steps + 1):
        if k == steps:
            a, b = halves(a)[0], halves(b)[1]
        passed = [swap(v, "seq", 1) for v in blocks[len(others) :]]
        a, b = hop(a, b, wide)
        work = []
        if k == 1:
            work = own_slices(mlp_codes, pieces, info, row_scale, down_scale, count)
            a, b, *work = clock.sync(a, b, *passed, *work)
            passed, own_weights = work[: len(passed)], work[len(passed) :]
        elif k == 2:
            work = [piece_codes[m].astype(bf16) for m in range(3)]
            for s in seqs:
                factor = norm_factor(clock.hold(inputs[s]))
                work += [factor, (inputs[s] * factor * gain_attn).astype(bf16)]
            a, b, *work = clock.sync(a, b, *passed, *work)
            passed, work = work[: len(passed)], work[len(passed) :]
            sends, work = work[:3], work[3:]
            input_factor, normed = work[0::2], work[1::2]
        else:
            more = len(others)
            work = slice_more(sliced, more) if more > sliced else []
            a, b, *work = clock.sync(a, b, *passed, *work)
            passed, work = work[: len(passed)], work[len(passed) :]
            if work:
                proj_weights, sliced = list(work), more
        others += passed
        blocks += [a, b] if k < steps else [jnp.concatenate([a, b], axis=0)]

    def exchange(m):
        return swap(clock.hold(sends[m]), "wide", half_wide)

    def share(held, bits):
        for bit in bits:
            held = held + [swap(value, "seq", bit) for value in held]
        return held

    def partner_weights(m, held):
        scale = row_scale[m] if m < 2 else down_scale
        return partner_slices(
            held, info, scale, m == 2, own_weights[m * count : (m + 1) * count]
        )

    received = exchange(0)
    others += [swap(clock.hold(v), "seq", 1) for v in blocks[len(others) :]]
    proj_weights = slice_more(sliced, wide)
    query_send, pair_send = [], []
    for s in seqs:
        query, pair = project(normed[s], proj_weights[s], cosine, sine)
        query_send.append(query.reshape(wide, class_rows, head_cols))
        pair_send.append(pair)
    own_out = jnp.stack([clock.hold(v)[:, half_proj:] for v in blocks])
    other_out = jnp.stack([v[:, half_proj:] for v in others])
    out_own = share([own_out], far_bits)
    sent = clock.sync(received, *query_send, *pair_send, *out_own)
    received, sent = sent[0], sent[1:]
    query_send, pair_send, out_own = sent[:count], sent[count : 2 * count], sent[2 * count :]

    def start_spread(pair):
        held = [pair]
        for _ in range(classes - 1):
            held.append(class_ring(held[-1]))
        return held

    attended_send, exact, lse, queries, pairs = [], [], [], [], []

    def attend(s):
        out, full, log_sum = attn_forward(class_info, queries[s], pairs[s], class_rows, rows)
        return [out.reshape(wide, class_rows, head_cols), full, log_sum]

    def keep_attend(work):
        attended_send.append(work[0])
        exact.append(work[1])
        lse.append(work[2])

    out_other = [other_out] + [swap(v, "seq", 1) for v in out_own[1:]]
    pair = heads_all_to_all(clock.hold(pair_send[0]))
    gate_held = share([clock.hold(received)], far_bits)
    pair, *work = clock.sync(pair, *gate_held, *out_other)
    gate_held, out_other = work[: len(gate_held)], work[len(gate_held) :]
    for s in seqs[1:]:
        spread = start_spread(pair)
        pair = heads_all_to_all(clock.hold(pair_send[s]))
        work = []
        if s == 1:
            gate_held = share(gate_held, seq_bits[:1])
            work = out_slices(out_own, out_other, places, info, output_scale, count)
        pair, *rest = clock.sync(pair, *spread, *work, *gate_held)
        pairs.append(rest[:classes])
        if s == 1:
            out_weights = rest[classes : classes + count]
            gate_held = rest[classes + count :]
    spread = start_spread(pair)
    for s in seqs:
        query = all_to_all(clock.hold(query_send[s]))
        if s == 0:
            query, *rest = clock.sync(query, *spread)
            pairs.append(rest)
        else:
            query, *rest = clock.sync(query, *attend(s - 1))
            keep_attend(rest)
        queries.append(query.reshape(wide * class_rows, head_cols))

    attended, branch, branch_factor, middle, middle_factor, normed_mlp = [], [], [], [], [], []

    def heads_to_rows(values):
        split = values.reshape(KEY_VALUE_HEADS, rows, head_cols)
        return jnp.transpose(split, (1, 0, 2)).reshape(rows, KEY_VALUE_HEADS * head_cols)

    def join(s):
        value = dot(attended[s], out_weights[s], NT)
        factor = norm_factor(value)
        mid = inputs[s] + value * factor * gain_post_attn
        mid_factor = norm_factor(mid)
        return [value, factor, mid, mid_factor, (mid * mid_factor * gain_mlp).astype(bf16)]

    def keep_join(work):
        for held, value in zip((branch, branch_factor, middle, middle_factor, normed_mlp), work):
            held.append(value)

    for s in seqs:
        back = all_to_all(clock.hold(attended_send[s]))
        if s == 0:
            gate_weights = partner_weights(0, [clock.hold(v) for v in gate_held])
            back, *work = clock.sync(back, *attend(count - 1), *gate_weights)
            keep_attend(work[:3])
            gate_weights = work[3:]
        else:
            back, *work = clock.sync(back, *join(s - 1))
            keep_join(work)
        attended.append(heads_to_rows(back))

    received, *work = clock.sync(exchange(1), *join(count - 1))
    keep_join(work)

    def blocks_of(part):
        return lambda o: part[order[o] * rows : (order[o] + 1) * rows]

    gathered, gate, up, hidden_rows, mixed, parts = [], [], [], [], [], []

    def open_gate(s):
        return dot(clock.hold(gathered[s]), gate_weights[s], NT)

    def open_up(s):
        up_s = dot(clock.hold(gathered[s]), up_weights[s], NT)
        hidden_s = (0.5 * gate[s] * (1.0 + gelu_parts(gate[s])) * up_s).astype(bf16)
        return [up_s, hidden_s]

    def keep_up(work):
        up.append(work[0])
        hidden_rows.append(work[1])

    def mix(s):
        return dot(clock.hold(hidden_rows[s]), down_weights[s], NN).astype(bf16)

    def staged_share(received):
        held = [received]

        def beside(step):
            nonlocal held
            if step == 0:
                held = share([clock.hold(held[0])], far_bits)
            elif step == 1:
                held = share(held, seq_bits[:1])
            return tuple(held)

        def keep(work):
            nonlocal held
            held = work

        return beside, keep, lambda: held

    def shared_gather(value, received):
        beside, keep, result = staged_share(received)
        a = b = clock.hold(value)
        out = [a]
        for k in range(1, half_wide // 2 + 1):
            if k == half_wide // 2:
                a, b = halves(a)[0], halves(b)[1]
            work = beside(k - 1) if k <= 2 else ()
            a, b = hop(a, b, half_wide)
            a, b, *work = clock.sync(a, b, *work)
            if work:
                keep(work)
            out += [a, b]
        return jnp.concatenate(out, axis=0), result()

    group, up_held = shared_gather(normed_mlp[0], received)
    gathered.append(group)
    received = exchange(2)
    gate.append(open_gate(0))
    up_weights = partner_weights(1, up_held)
    received, *work = clock.sync(received, *open_up(0), *up_weights, gate[0])
    keep_up(work[:2])
    up_weights = work[2 : 2 + count]
    gate[0] = work[-1]
    for s in seqs[1:]:
        group, down_held = shared_gather(normed_mlp[s], received)
        gathered.append(group)
    down_weights = partner_weights(2, down_held)
    parts.append(clock.sync(mix(0))[0])

    layer_out, grad_mixed, gain_fourth = [], [], 0.0

    def finish(s):
        nonlocal gain_fourth
        factor = norm_factor(mixed[s])
        layer_out.append((middle[s] + mixed[s] * factor * gain_post_mlp).astype(bf16))
        grad, gain = norm_back(mixed[s], factor, gain_post_mlp, grad_out[s])
        grad_mixed.append(grad.astype(bf16))
        gain_fourth = gain_fourth + gain

    grad_group, grad_gate, grad_up, grad_parts, grad_normed_mlp = [], [], [], [], []

    def back_hidden(s):
        grad_hidden = dot(clock.hold(grad_group[s]), down_weights[s], NT)
        bounded = gelu_parts(gate[s])
        gelu_value = 0.5 * gate[s] * (1.0 + bounded)
        slope = 0.5 * (1.0 + bounded) + 0.5 * gate[s] * (1.0 - bounded * bounded) * gelu_coeff * (
            1.0 + 3.0 * 0.044715 * gate[s] * gate[s]
        )
        return [(grad_hidden * up[s] * slope).astype(bf16), (grad_hidden * gelu_value).astype(bf16)]

    def back_input(s):
        return (
            dot(clock.hold(grad_gate[s]), gate_weights[s], NN)
            + dot(grad_up[s], up_weights[s], NN)
        ).astype(bf16)

    def keep_back(work):
        grad_gate.append(work[0])
        grad_up.append(work[1])

    def first_sum(part):
        a, b = hop(*halves(clock.hold(blocks_of(part)(half_wide // 2))), half_wide)
        return a, b

    def rest_sum(part, a, b, beside=lambda step: ()):
        part_of = blocks_of(part)
        other = []
        for k in range(half_wide // 2 - 1, 0, -1):
            if k == half_wide // 2 - 1:
                a = add_first(part_of(k), a)
                b = add_last(part_of(-k), b)
            else:
                a = low_sum(part_of(k), a)
                b = low_sum(part_of(-k), b)
            work = beside(half_wide // 2 - 1 - k)
            a, b = hop(a, b, half_wide)
            a, b, *work = clock.sync(a, b, *work)
            other.append(work)
        return part_of(0).astype(f32) + a.astype(f32) + b.astype(f32), other

    for s in seqs:
        a, b = first_sum(parts[s])
        if s + 1 < count:
            a, b, value = clock.sync(a, b, open_gate(s + 1))
            gate.append(value)
        else:
            a, b, *work = clock.sync(a, b, *back_hidden(0))
            keep_back(work)

        def beside(step, s=s):
            if step:
                return ()
            return tuple(open_up(s + 1)) if s + 1 < count else (back_input(0),)

        total, work = rest_sum(parts[s], a, b, beside)
        if s + 1 < count:
            keep_up(work[0])
        else:
            grad_parts.append(work[0][0])
        mixed.append(total)
        finish(s)
        if s + 1 < count:
            parts.append(mix(s + 1))
        if s == 0:
            blocks, work = ring_gather(
                clock, grad_mixed[0], half_wide, lambda k: (parts[-1],) if k == 0 else ()
            )
            parts[-1] = work[0][0]
            grad_group.append(jnp.concatenate(blocks, axis=0))

    def weight_first(left, right):
        return dot(clock.hold(left), right, TN)

    def weight_rest(first, lefts, rights):
        for s in seqs[1:]:
            first = first + dot(clock.hold(lefts[s]), rights[s], TN)
        return first.astype(bf16).reshape(2, hidden, model_dim)

    def part_sum(grad, bit):
        split = grad.reshape(2, 2, grad.shape[1] // 2, model_dim)
        return low_sum(split[:, 0], swap(split[:, 1], "seq", bit))

    grad_middle, grad_branch, grad_send = [], [], []
    gain_third = gain_second = 0.0

    def back_branch(s):
        nonlocal gain_third, gain_second
        grad, gain = norm_back(middle[s], middle_factor[s], gain_mlp, grad_normed_mlp[s])
        gain_third = gain_third + gain
        grad_mid = grad_out[s] + grad
        grad, gain = norm_back(branch[s], branch_factor[s], gain_post_attn, grad_mid)
        gain_second = gain_second + gain
        grad = grad.astype(bf16)
        send = dot(grad, out_weights[s], NN).astype(bf16)
        send = jnp.transpose(send.reshape(rows, KEY_VALUE_HEADS, head_cols), (1, 0, 2))
        return [grad_mid, grad, send.reshape(wide, class_rows, head_cols)]

    def keep_branch(work):
        grad_middle.append(work[0])
        grad_branch.append(work[1])
        grad_send.append(work[2])

    for s in seqs[1:]:
        blocks, work = ring_gather(
            clock,
            grad_mixed[s],
            half_wide,
            lambda k: (weight_first(hidden_rows[0], grad_group[0]),) if k == 0 and s == 1 else (),
        )
        if s == 1:
            down_first = work[0][0]
        grad_group.append(jnp.concatenate(blocks, axis=0))
    for s in seqs:
        a, b = first_sum(grad_parts[s])
        if s + 1 < count:
            a, b, *work = clock.sync(a, b, *back_hidden(s + 1))
            keep_back(work)
        else:
            a, b, *work = clock.sync(a, b, *back_branch(s - 1))
            keep_branch(work)

        def beside(step, s=s):
            if step:
                return ()
            if s + 1 < count:
                return (back_input(s + 1),)
            return (weight_rest(down_first, hidden_rows, grad_group),)

        total, work = rest_sum(grad_parts[s], a, b, beside)
        if s + 1 < count:
            grad_parts.append(work[0][0])
        else:
            down_grad = work[0][0]
        grad_normed_mlp.append(total)

    def attend_back(s):
        dq, *dkv = attn_backward(
            class_info,
            queries[s],
            pairs[s],
            clock.hold(grad_heads[s]),
            exact[s],
            lse[s],
            class_rows,
            rows,
        )
        return [dq.reshape(wide, class_rows, head_cols)] + dkv

    def class_sum(dkv):
        total = dkv[1 % classes]
        for step in range(2, classes + 1):
            total = low_sum(dkv[step % classes], class_ring(total))
        return total

    grad_heads, grad_attend = [], []
    for s in seqs:
        back = all_to_all(clock.hold(grad_send[s]))
        if s == 0:
            work = back_branch(count - 1)
            down_grad = part_sum(down_grad, 1)
            back, down_grad, *work = clock.sync(back, down_grad, *work)
            keep_branch(work)
        else:
            back, *work = clock.sync(back, *attend_back(s - 1))
            grad_attend.append(work)
        grad_heads.append(back.reshape(wide * class_rows, head_cols))

    def far_sum_start(grad):
        split = grad.reshape(2, 2, grad.shape[1] // 2, model_dim)
        return split[:, 0], swap(clock.hold(split[:, 1]), "seq", seq_bits[1])

    down_keep, down_move = far_sum_start(down_grad)

    query_back, pair_back, pair_sum = [], [], []
    for s in seqs:
        dq, *dkv = grad_attend[s]
        query = all_to_all(clock.hold(dq))
        pair = class_sum(dkv)
        if s + 1 < count:
            query, pair, *work = clock.sync(query, pair, *attend_back(s + 1))
            grad_attend.append(work)
        else:
            up_first = weight_first(grad_up[0], gathered[0])
            up_grad = weight_rest(up_first, grad_up, gathered)
            query, pair, up_grad = clock.sync(query, pair, up_grad)
        query_back.append(query)
        pair_sum.append(pair)
    for s in seqs:
        pair = heads_all_to_all(clock.hold(pair_sum[s]))
        if s == 0:
            gate_first = weight_first(grad_gate[0], gathered[0])
            up_grad = part_sum(up_grad, 1)
            down_grad = low_sum(down_keep, down_move)
            pair, gate_first, up_grad, down_grad = clock.sync(pair, gate_first, up_grad, down_grad)
            up_keep, up_move = far_sum_start(up_grad)
        elif s == 1:
            gate_grad = weight_rest(gate_first, grad_gate, gathered)
            pair, gate_grad = clock.sync(pair, gate_grad)
        else:
            (pair,) = clock.sync(pair)
        pair_back.append(pair)

    def owner_start(grad):
        return grad[0], swap(clock.hold(grad[1]), "wide", half_wide)

    def last_sums(grad):
        for bit in seq_bits[2:]:
            grad = part_sum(grad, bit)
        return grad

    down_grad = last_sums(down_grad)
    down_own, down_other = owner_start(down_grad)
    grad_proj = turn_back(
        [v.reshape(KEY_VALUE_HEADS, rows, head_cols) for v in query_back], pair_back, cosine, sine
    )
    all_normed = jnp.concatenate(normed, axis=0)
    all_attended = jnp.concatenate(attended, axis=0)
    all_branch = jnp.concatenate(grad_branch, axis=0)

    def half_dot(left, right, which, size):
        return dot(left, lax.dynamic_slice_in_dim(right, which * size, size, 1), TN)

    proj_sent = swap(half_dot(all_normed, grad_proj, 1 - side, half_proj).astype(bf16), "seq", 1)
    out_sent = swap(half_dot(all_branch, all_attended, 1 - side, half_out).astype(bf16), "seq", 1)
    gate_grad = part_sum(gate_grad, 1)
    grad_tokens, gain_first = [], 0.0
    for s in seqs:
        grad_normed = dot(grad_proj[s * rows : (s + 1) * rows], proj_weights[s], NT)
        grad, gain = norm_back(inputs[s], input_factor[s], gain_attn, grad_normed)
        gain_first = gain_first + gain
        grad_tokens.append((grad_middle[s] + grad).astype(bf16))
    gains = jnp.stack([gain_first, gain_second, gain_third, gain_fourth])
    out_part = low_sum(half_dot(all_branch, all_attended, side, half_out), out_sent)
    proj_part = low_sum(half_dot(all_normed, grad_proj, side, half_proj), proj_sent)
    up_grad = low_sum(up_keep, up_move)
    down_other, proj_part, out_part, gains, gate_grad, up_grad, *grad_tokens = clock.sync(
        down_other, proj_part, out_part, gains, gate_grad, up_grad, *grad_tokens
    )
    gate_keep, gate_move = far_sum_start(gate_grad)

    def part_of(o):
        first = index_at(o) * attn_rows
        return jnp.concatenate(
            [
                lax.dynamic_slice_in_dim(proj_part, first, attn_rows, 0),
                lax.dynamic_slice_in_dim(out_part, first, attn_rows, 0),
            ],
            axis=1,
        )

    def spread_grad(grad, bits):
        for bit in bits:
            grad = jnp.concatenate([grad, swap(grad, "seq", bit)], axis=0)
        return grad

    for axis, size in (("seq", seq_size), ("wide", wide)):
        bit = 1
        while bit < size:
            gains = gains + swap(gains, axis, bit)
            bit *= 2
    down_grad = low_sum(down_own, down_other)

    def beside_ring(step):
        if step == 0:
            return (gains,)
        if step == 1:
            return (gate_move,)
        if step == 2:
            return (spread_grad(clock.hold(down_grad), far_bits),)
        return ()

    total, work = ring_scatter(clock, part_of, attn_rows, wide, beside_ring)
    gains, gate_move, down_grad = work[0][0], work[1][0], work[2][0]
    gate_grad = last_sums(low_sum(gate_keep, gate_move))

    up_own, up_other = owner_start(last_sums(up_grad))
    attn_low = total.astype(bf16)
    attn_move = swap(clock.hold(attn_low), "seq", seq_bits[1])
    mlp_grad = unpack(spread_grad(clock.hold(down_grad), seq_bits[:1]), pieces, 2, [])
    up_other, attn_move, mlp_grad = clock.sync(up_other, attn_move, mlp_grad)
    gate_own, gate_other = owner_start(gate_grad)
    for bit in seq_bits[2:]:
        attn_low = low_sum(attn_low, attn_move)
        attn_move = swap(attn_low, "seq", bit)
    low = low_sum(attn_low, attn_move)
    other = swap(low, "seq", 1)
    left, right = jnp.where(is_low, low, other), jnp.where(is_low, other, low)
    attn_grad = jnp.concatenate(
        [left[:, :half_proj], right[:, :half_proj], left[:, half_proj:], right[:, half_proj:]],
        axis=1,
    ).astype(f32)
    up_grad = spread_grad(low_sum(up_own, up_other), reversed(seq_bits))
    mlp_grad = unpack(up_grad, pieces, 1, [mlp_grad])
    gate_other, attn_grad, mlp_grad = clock.sync(gate_other, attn_grad, mlp_grad)
    gate_grad = spread_grad(low_sum(gate_own, gate_other), reversed(seq_bits))
    mlp_grad = unpack(gate_grad, pieces, 0, [mlp_grad])
    return (
        jnp.stack(layer_out),
        jnp.stack(grad_tokens),
        attn_grad,
        mlp_grad,
        gains[0],
        gains[1],
        gains[2],
        gains[3],
    )


def solution(mesh):
    placed = (
        P("seq", "wide", None),
        P("seq", "wide", None),
        P("seq"),
        P("wide", None),
        P(),
        P(),
        P(None, "wide", None),
        P(),
        P(),
        P(),
        P(),
        P(),
        P(),
    )
    return jax.shard_map(
        per_device,
        mesh=mesh,
        in_specs=placed,
        out_specs=(
            P("seq", "wide", None),
            P("seq", "wide", None),
            P("wide", None),
            P(None, "wide", None),
            P(),
            P(),
            P(),
            P(),
        ),
        check_vma=False,
    )
```

time: 1820 us -> 1760 us (0.967)
  local copies, waits for them, and re-layouts: 211 us -> 113 us
  waiting for transfers between devices: 641 us -> 711 us
  matrix products: 438 us -> 395 us
  starting transfers between devices: 182 us -> 139 us
  Pallas kernels: 178 us -> 218 us
    ppermute x48, waiting for transfers between devices: 184 us -> 233 us  [hop(): return (lax.ppermute(a, 'wide', up), lax.ppermute(b, 'wide', down))]
    dot_general x30 -> x28, matrix products: 438 us -> 395 us  [dot(): return lax.dot_general(a, b, (dims, ((), ())), preferred_element_type=f32)]
    slice x27 -> x0, local copies, waits for them, and re-layouts: 38.1 us -> none  [the longest x4 14.2 us: per_device(): out_in.append(values[:, :, cut:])]
    convert_element_type x6 -> x5, other arithmetic: 17.7 us -> 50.7 us  [the longest x2 34 us: back_hidden(): (grad_hidden * gelu_value).astype(bf16)]
    pallas_call x6 -> x11, Pallas kernels: 110 us -> 142 us  [the longest x2 34.9 us: attn_backward(): pl.pallas_call(functools.partial(attn_backward_kernel, tile=tile, class_r...]
    ppermute x48, starting transfers between devices: 77.9 us -> 52.9 us  [hop(): return (lax.ppermute(a, 'wide', up), lax.ppermute(b, 'wide', down))]
    ppermute x63 -> x46, starting transfers between devices: 42.2 us -> 28 us  [swap(): return lax.ppermute(value, axis, [(i, i ^ bit) for i in range(size)])]
    unnamed x389 -> x347, local copies, waits for them, and re-layouts: 63.1 us -> 49.4 us
  transfers between devices with their start and end apart: 127 -> 110, of which waited for: 55 -> 67; matrix products, arithmetic and copies ran while one was open for 35% -> 28% of each run, Pallas kernels for 9% -> 12%
where the time goes in v4:
time: 1760 us; the launch traced here: 1750 us
  waiting for transfers between devices  711 us (40%)
  matrix products  395 us (22%)
  Pallas kernels  218 us (12%)
  other arithmetic  170 us (10%)
  starting transfers between devices  139 us (8%)
  local copies, waits for them, and re-layouts  113 us (6%)
    dot_general x28, matrix products, dot(): return lax.dot_general(a, b, (dims, ((), ())), preferred_element_type=f32)  395 us
    ppermute x46, waiting for transfers between devices, swap(): return lax.ppermute(value, axis, [(i, i ^ bit) for i in range(size)])  382 us
    ppermute x48, waiting for transfers between devices, hop(): return (lax.ppermute(a, 'wide', up), lax.ppermute(b, 'wide', down))  233 us
    ppermute x48, starting transfers between devices, hop(): return (lax.ppermute(a, 'wide', up), lax.ppermute(b, 'wide', down))  52.9 us
    ppermute x4, waiting for transfers between devices, class_ring(): return lax.ppermute(value, 'wide', perm)  51.7 us
    unnamed x347, local copies, waits for them, and re-layouts  49.4 us
    all_to_all x8, waiting for transfers between devices, all_to_all(): lax.all_to_all(value, 'wide', split_axis=0, concat_axis=0, tiled=True)  44.2 us
    convert_element_type x22, other arithmetic, low_sum(): return sum((t.astype(f32) for t in terms)).astype(bf16)  43.9 us
  transfers between devices with their start and end apart: 110, of which 67 were waited for; matrix products, arithmetic and copies ran while one was open for 28% of the time, Pallas kernels for 12%

profile of v4, /device:TPU:0, one launch (start us, length us, event | category | flops | bytes accessed | tf_op | source)
XLA Modules:
  0.0 1750.1 jit_solution(1813799983483670615)
XLA Ops:
  11.2 25.2 %own_slices.1 = (bf16[2304,2304]{1,0:T(8,128)(2,1)}, bf16[2304,2304]{1,0:T(8,128)(2,1)}, bf16[2304,2304]{1,0:T(8,128)(2,1)}, bf16[2304,2304]{1,0:T(8,128)(2,1)},...) custom-call(s32[4]{0:T(128)} %pad_add_fusion.pieces, s32[4]{0:T(128)} %pad_add_fusion.1.info, ...), custom_call_target="tpu_custom_call" | custom-call | flops 159252480 | bytes 63700992 | tf_op jit(solution)/shard_map/own_slices/pallas_call | solution.py:297
  48.2 27.8 %collective-permute-done.3.refs_0_ = bf16[288,2560]{1,0:T(8,128)(2,1)} collective-permute-done((bf16[288,2560]{1,0:T(8,128)(2,1)}, bf16[288,2560]{1,0:T(8,128)(2,1)}, u32[]{:S(2)}, u32[]{:S(2)}) %collective-permute-start.3) | collective-permute-done | bytes 1474592 | tf_op jit(solution)/shard_map/ppermute | solution.py:102
  92.7 20.4 %collective-permute-done.7.refs_0_ = bf16[288,2560]{1,0:T(8,128)(2,1)S(1)} collective-permute-done((bf16[288,2560]{1,0:T(8,128)(2,1)}, bf16[288,2560]{1,0:T(8,128)(2,1)S(1)}, u32[]{:S(2)}, u32[]{:S(2)}) %collective-permute-start.7) | collective-permute-done | bytes 1474592 | tf_op jit(solution)/shard_map/ppermute | solution.py:102
  190.0 24.8 %collective-permute-done.15.refs_0_ = bf16[288,2304]{1,0:T(8,128)(2,1)S(1)} collective-permute-done((bf16[288,2304]{1,0:T(8,128)(2,1)}, bf16[288,2304]{1,0:T(8,128)(2,1)S(1)}, u32[]{:S(2)}, u32[]{:S(2)}) %collective-permute-start.15) | collective-permute-done | bytes 1327136 | tf_op jit(solution)/shard_map/ppermute | solution.py:157
  228.2 25.1 %collective-permute-done.18.refs_1_ = bf16[288,2304]{1,0:T(8,128)(2,1)} collective-permute-done((bf16[288,2304]{1,0:T(8,128)(2,1)}, bf16[288,2304]{1,0:T(8,128)(2,1)}, u32[]{:S(2)}, u32[]{:S(2)}) %collective-permute-start.18) | collective-permute-done | bytes 1327136 | tf_op jit(solution)/shard_map/ppermute | solution.py:157
  261.0 20.6 %out_slices.1 = (bf16[2304,2048]{1,0:T(8,128)(2,1)}, bf16[2304,2048]{1,0:T(8,128)(2,1)}) custom-call(s32[8]{0:T(128)} %stack.161.places, s32[4]{0:T(128)} %pad_add_fusion.1.info, bf16[8,288,512]{2,1,0:T(8,128)(2,1)} %bitcast_dynamic-update-slice_fusion.7.refs_0_, bf16[8,288,512]{2,1,0:T(8,128)(2,1)} %collective-permute-done.17.refs_1_, ...), custom_call_target="tpu_custom_call" | custom-call | flops 94371840 | bytes 28311552 | tf_op jit(solution)/shard_map/out_slices/pallas_call | solution.py:260
  290.9 33.3 %collective-permute-done.23.refs_1_ = bf16[4,256,512]{2,1,0:T(8,128)(2,1)S(1)} collective-permute-done((bf16[4,256,512]{2,1,0:T(8,128)(2,1)}, bf16[4,256,512]{2,1,0:T(8,128)(2,1)S(1)}, u32[]{:S(2)}, u32[]{:S(2)}) %collective-permute-start.23) | collective-permute-done | bytes 1048608 | tf_op jit(solution)/shard_map/ppermute | solution.py:177
  340.3 14.3 all-to-all-done.3
  398.1 16.2 all-to-all-done.5
  425.6 56.2 %collective-permute-done.24.refs_0_ = bf16[288,2304]{1,0:T(8,128)(2,1)} collective-permute-done((bf16[288,2304]{1,0:T(8,128)(2,1)S(1)}, bf16[288,2304]{1,0:T(8,128)(2,1)}, u32[]{:S(2)}, u32[]{:S(2)}) %collective-permute-start.24) | collective-permute-done | bytes 1327136 | tf_op jit(solution)/shard_map/ppermute | solution.py:157
  484.7 25.6 %collective-permute-done.25 = bf16[256,2304]{1,0:T(8,128)(2,1)S(1)} collective-permute-done((bf16[256,2304]{1,0:T(8,128)(2,1)S(1)}, bf16[256,2304]{1,0:T(8,128)(2,1)S(1)}, u32[]{:S(2)}, u32[]{:S(2)}) %collective-permute-start.25) | collective-permute-done | bytes 1179680 | tf_op jit(solution)/shard_map/ppermute | solution.py:102
  520.1 12.8 collective-permute-done.28
  535.7 15.3 fusion.104
  560.5 21.2 %fusion.8 = (bf16[1024,2304]{1,0:T(8,128)(2,1)}, f32[1024,2304]{1,0:T(8,128)}) fusion(f32[1024,2304]{1,0:T(8,128)} %fusion.104, bf16[1024,2304]{1,0:T(8,128)(2,1)} %copy-done.84, bf16[2304,2304]{1,0:T(8,128)(2,1)} %get-tuple-element.545), kind=kOutput, calls=%fused_computation.21 | convolution fusion | flops 10895228928 | bytes 38928384 | tf_op jit(solution)/shard_map/dot_general | solution.py:26
  596.4 25.0 %collective-permute-done.33 = bf16[256,2304]{1,0:T(8,128)(2,1)S(1)} collective-permute-done((bf16[256,2304]{1,0:T(8,128)(2,1)S(1)}, bf16[256,2304]{1,0:T(8,128)(2,1)S(1)}, u32[]{:S(2)}, u32[]{:S(2)}) %collective-permute-start.33) | collective-permute-done | bytes 1179680 | tf_op jit(solution)/shard_map/ppermute | solution.py:102
  649.7 15.1 convolution_convert_fusion.3
  667.1 13.5 fusion.105
  685.5 21.3 %multiply_convert_fusion.2 = (bf16[1024,2304]{1,0:T(8,128)(2,1)}, f32[1024,2304]{1,0:T(8,128)}) fusion(f32[1024,2304]{1,0:T(8,128)} %fusion.105, bf16[1024,2304]{1,0:T(8,128)(2,1)} %copy-done.87, bf16[2304,2304]{1,0:T(8,128)(2,1)} %get-tuple-element.518), kind=kOutput, calls=%fused_computation.41 | convolution fusion | flops 10895228928 | bytes 38928384 | tf_op jit(solution)/shard_map/dot_general | solution.py:26
  723.4 13.7 convolution_convert_fusion.2
  763.7 15.5 fusion.106
  782.4 16.0 multiply_convert_fusion.1
  799.5 14.9 fusion.107
  818.7 17.7 %add_convert_fusion.6 = bf16[1024,2304]{1,0:T(8,128)(2,1)} fusion(f32[1024,2304]{1,0:T(8,128)} %fusion.107, bf16[1024,2304]{1,0:T(8,128)(2,1)S(1)} %copy-done.29, bf16[2304,2304]{1,0:T(8,128)(2,1)} %get-tuple-element.545), kind=kOutput, calls=%fused_computation.39 | convolution fusion | flops 10876354560 | bytes 29491200 | tf_op jit(solution)/shard_map/dot_general | solution.py:26
  846.2 19.2 %fusion.108 = f32[2304,2304]{1,0:T(8,128)} fusion(bf16[1024,2304]{1,0:T(8,128)(2,1)} %get-tuple-element.551, bf16[1024,2304]{1,0:T(8,128)(2,1)} %constant_dynamic-update-slice_fusion.12), kind=kOutput, calls=%fused_computation.359 | convolution fusion | flops 10871635968 | bytes 30670848 | tf_op jit(solution)/shard_map/dot_general | solution.py:26
  880.6 13.5 fusion.109
  896.2 18.0 %multiply_convert_fusion = (bf16[1024,2304]{1,0:T(8,128)(2,1)}, bf16[1024,2304]{1,0:T(8,128)(2,1)}) fusion(f32[1024,2304]{1,0:T(8,128)} %fusion.109, f32[1024,2304]{1,0:T(8,128)} %fusion.105, f32[1024,2304]{1,0:T(8,128)} %get-tuple-element.560), kind=kLoop, calls=%fused_computation.38 | loop fusion | flops 54263808 | bytes 37748736 | tf_op jit(solution)/shard_map/convert_element_type | solution.py:1005
  914.3 15.1 fusion.110
  935.5 16.1 add_convert_fusion.5
  982.1 18.5 %fusion.111 = f32[2304,2304]{1,0:T(8,128)} fusion(bf16[1024,2304]{1,0:T(8,128)(2,1)} %get-tuple-element.580, bf16[1024,2304]{1,0:T(8,128)(2,1)} %copy-done.83), kind=kOutput, calls=%fused_computation.362 | convolution fusion | flops 10871635968 | bytes 30670848 | tf_op jit(solution)/shard_map/dot_general | solution.py:26
  1003.2 13.8 add_convert_fusion.2
  1063.6 17.4 attn_backward.2
  1101.7 17.5 attn_backward.3
  1128.6 19.2 %fusion.112 = f32[2304,2304]{1,0:T(8,128)} fusion(bf16[1024,2304]{1,0:T(8,128)(2,1)} %get-tuple-element.618, bf16[1024,2304]{1,0:T(8,128)(2,1)} %copy-done.87), kind=kOutput, calls=%fused_computation.363 | convolution fusion | flops 10871635968 | bytes 30670848 | tf_op jit(solution)/shard_map/dot_general | solution.py:26
  1153.9 20.0 %add_convert_fusion.1 = bf16[2304,2304]{1,0:T(8,128)(2,1)} fusion(f32[2304,2304]{1,0:T(8,128)} %fusion.112, bf16[1024,2304]{1,0:T(8,128)(2,1)} %get-tuple-element.617, bf16[1024,2304]{1,0:T(8,128)(2,1)} %copy-done.84), kind=kOutput, calls=%fused_computation.1 | convolution fusion | flops 10882252800 | bytes 41287680 | tf_op jit(solution)/shard_map/dot_general | solution.py:26
  1208.2 18.8 %fusion.113 = f32[2304,2304]{1,0:T(8,128)} fusion(bf16[1024,2304]{1,0:T(8,128)(2,1)} %get-tuple-element.621, bf16[1024,2304]{1,0:T(8,128)(2,1)} %copy-done.84), kind=kOutput, calls=%fused_computation.364 | convolution fusion | flops 10871635968 | bytes 30670848 | tf_op jit(solution)/shard_map/dot_general | solution.py:26
  1242.7 20.0 %add_convert_fusion = bf16[2304,2304]{1,0:T(8,128)(2,1)} fusion(f32[2304,2304]{1,0:T(8,128)} %fusion.113, bf16[1024,2304]{1,0:T(8,128)(2,1)} %get-tuple-element.630, bf16[1024,2304]{1,0:T(8,128)(2,1)} %copy-done.87), kind=kOutput, calls=%fused_computation | convolution fusion | flops 10882252800 | bytes 41287680 | tf_op jit(solution)/shard_map/dot_general | solution.py:26
  1264.1 13.4 turn_back.1
  1291.3 20.6 %fusion.63 = f32[256,2304]{1,0:T(8,128)} fusion(bf16[2304,4096]{1,0:T(8,128)(2,1)} %get-tuple-element.386.wq_ref.wk_ref.wv_ref, bf16[512,4096]{1,0:T(8,128)(2,1)} %turn_back.1), kind=kOutput, calls=%fused_computation.171 | convolution fusion | flops 4831838208 | bytes 23330816 | tf_op jit(solution)/shard_map/dot_general | solution.py:26
  1311.9 12.6 fusion.53
  1353.9 31.6 %collective-permute-done.69 = bf16[288,2304]{1,0:T(8,128)(2,1)} collective-permute-done((bf16[288,2304]{1,0:T(8,128)(2,1)}, bf16[288,2304]{1,0:T(8,128)(2,1)}, u32[]{:S(2)}, u32[]{:S(2)}) %collective-permute-start.69) | collective-permute-done | bytes 1327136 | tf_op jit(solution)/shard_map/ppermute | solution.py:157
  1404.9 17.1 collective-permute-done.79
  1430.6 30.4 %collective-permute-done.83 = bf16[2,288,2304]{2,1,0:T(8,128)(2,1)S(1)} collective-permute-done((bf16[2,288,2304]{2,1,0:T(8,128)(2,1)S(1)}, bf16[2,288,2304]{2,1,0:T(8,128)(2,1)S(1)}, u32[]{:S(2)}, u32[]{:S(2)}) %collective-permute-start.83) | collective-permute-done | bytes 2654240 | tf_op jit(solution)/shard_map/ppermute | solution.py:157
  1472.6 25.3 %collective-permute-done.86 = bf16[288,2304]{1,0:T(8,128)(2,1)S(1)} collective-permute-done((bf16[288,2304]{1,0:T(8,128)(2,1)S(1)}, bf16[288,2304]{1,0:T(8,128)(2,1)S(1)}, u32[]{:S(2)}, u32[]{:S(2)}) %collective-permute-start.86) | collective-permute-done | bytes 1327136 | tf_op jit(solution)/shard_map/ppermute | solution.py:157
  1508.2 33.3 %collective-permute-done.88 = bf16[288,3072]{1,0:T(8,128)(2,1)S(1)} collective-permute-done((bf16[288,3072]{1,0:T(8,128)(2,1)S(1)}, bf16[288,3072]{1,0:T(8,128)(2,1)S(1)}, u32[]{:S(2)}, u32[]{:S(2)}) %collective-permute-start.88) | collective-permute-done | bytes 1769504 | tf_op jit(solution)/shard_map/ppermute | solution.py:102
  1558.7 47.3 %collective-permute-done.89 = bf16[288,2304]{1,0:T(8,128)(2,1)S(1)} collective-permute-done((bf16[288,2304]{1,0:T(8,128)(2,1)S(1)}, bf16[288,2304]{1,0:T(8,128)(2,1)S(1)}, u32[]{:S(2)}, u32[]{:S(2)}) %collective-permute-start.89) | collective-permute-done | bytes 1327136 | tf_op jit(solution)/shard_map/ppermute | solution.py:157
  1612.6 27.2 %collective-permute-done.94 = bf16[288,2304]{1,0:T(8,128)(2,1)} collective-permute-done((bf16[288,2304]{1,0:T(8,128)(2,1)S(1)}, bf16[288,2304]{1,0:T(8,128)(2,1)}, u32[]{:S(2)}, u32[]{:S(2)}) %collective-permute-start.94) | collective-permute-done | bytes 1327136 | tf_op jit(solution)/shard_map/ppermute | solution.py:157
  1659.1 43.6 %collective-permute-done.92 = bf16[288,2304]{1,0:T(8,128)(2,1)S(1)} collective-permute-done((bf16[288,2304]{1,0:T(8,128)(2,1)S(1)}, bf16[288,2304]{1,0:T(8,128)(2,1)S(1)}, u32[]{:S(2)}, u32[]{:S(2)}) %collective-permute-start.92) | collective-permute-done | bytes 1327136 | tf_op jit(solution)/shard_map/ppermute | solution.py:157
  1704.0 30.2 %collective-permute-done.96 = bf16[288,2304]{1,0:T(8,128)(2,1)S(1)} collective-permute-done((bf16[288,2304]{1,0:T(8,128)(2,1)S(1)}, bf16[288,2304]{1,0:T(8,128)(2,1)S(1)}, u32[]{:S(2)}, u32[]{:S(2)}) %collective-permute-start.96) | collective-permute-done | bytes 1327136 | tf_op jit(solution)/shard_map/ppermute | solution.py:157
  (767 shorter events, 695.8 us)
Async XLA Ops:
  3.8 37.0 %collective-permute-start = (bf16[288,2560]{1,0:T(8,128)(2,1)S(1)}, bf16[288,2560]{1,0:T(8,128)(2,1)}, u32[]{:S(2)}, u32[]{:S(2)}) collective-permute-start(bf16[288,2560]{1,0:T(8,128)(2,1)S(1)} %pad_maximum_fusion.10.refs_0_), channel_id=1, source_target_pairs={{0,8},{8,16},{16,24},{24,28},{28,20},{20,12},{12,4},{4,0},{1,9},{9... | collective-permute-start | bytes 4423688 | tf_op jit(solution)/shard_map/ppermute | solution.py:102
  6.9 33.9 %collective-permute-start.1 = (bf16[288,2560]{1,0:T(8,128)(2,1)S(1)}, bf16[288,2560]{1,0:T(8,128)(2,1)}, u32[]{:S(2)}, u32[]{:S(2)}) collective-permute-start(bf16[288,2560]{1,0:T(8,128)(2,1)S(1)} %pad_maximum_fusion.10.refs_0_), channel_id=1, source_target_pairs={{8,0},{16,8},{24,16},{28,24},{20,28},{12,20},{4,12},{0,4},{9,1},{1... | collective-permute-start | bytes 4423688 | tf_op jit(solution)/shard_map/ppermute | solution.py:102
  6.9 33.9 %collective-permute-start.2 = (bf16[288,2560]{1,0:T(8,128)(2,1)S(1)}, bf16[288,2560]{1,0:T(8,128)(2,1)S(1)}, u32[]{:S(2)}, u32[]{:S(2)}) collective-permute-start(bf16[288,2560]{1,0:T(8,128)(2,1)S(1)} %pad_maximum_fusion.10.refs_0_), channel_id=1, source_target_pairs={{0,1},{1,0},{2,3},{3,2},{4,5},{5,4},{6,7},{7,6},{8,9},{9,8},{10,11... | collective-permute-start | bytes 4423688 | tf_op jit(solution)/shard_map/ppermute | solution.py:157
  40.8 35.1 %collective-permute-start.3 = (bf16[288,2560]{1,0:T(8,128)(2,1)}, bf16[288,2560]{1,0:T(8,128)(2,1)}, u32[]{:S(2)}, u32[]{:S(2)}) collective-permute-start(bf16[288,2560]{1,0:T(8,128)(2,1)} %collective-permute-done.refs_2_), channel_id=1, source_target_pairs={{0,8},{8,16},{16,24},{24,28},{28,20},{20,12},{12,4},{4,0},{1,9},{9... | collective-permute-start | bytes 4423688 | tf_op jit(solution)/shard_map/ppermute | solution.py:102
  42.9 35.0 %collective-permute-start.5 = (bf16[288,2560]{1,0:T(8,128)(2,1)}, bf16[288,2560]{1,0:T(8,128)(2,1)S(1)}, u32[]{:S(2)}, u32[]{:S(2)}) collective-permute-start(bf16[288,2560]{1,0:T(8,128)(2,1)} %collective-permute-done.refs_2_), channel_id=1, source_target_pairs={{0,1},{1,0},{2,3},{3,2},{4,5},{5,4},{6,7},{7,6},{8,9},{9,8},{10,11... | collective-permute-start | bytes 4423688 | tf_op jit(solution)/shard_map/ppermute | solution.py:157
  43.0 35.0 %collective-permute-start.4 = (bf16[288,2560]{1,0:T(8,128)(2,1)}, bf16[288,2560]{1,0:T(8,128)(2,1)}, u32[]{:S(2)}, u32[]{:S(2)}) collective-permute-start(bf16[288,2560]{1,0:T(8,128)(2,1)} %collective-permute-done.1.refs_4_), channel_id=1, source_target_pairs={{8,0},{16,8},{24,16},{28,24},{20,28},{12,20},{4,12},{0,4},{9,1},{1... | collective-permute-start | bytes 4423688 | tf_op jit(solution)/shard_map/ppermute | solution.py:102
  43.3 34.7 %collective-permute-start.6 = (bf16[288,2560]{1,0:T(8,128)(2,1)}, bf16[288,2560]{1,0:T(8,128)(2,1)S(1)}, u32[]{:S(2)}, u32[]{:S(2)}) collective-permute-start(bf16[288,2560]{1,0:T(8,128)(2,1)} %collective-permute-done.1.refs_4_), channel_id=1, source_target_pairs={{0,1},{1,0},{2,3},{3,2},{4,5},{5,4},{6,7},{7,6},{8,9},{9,8},{10,11... | collective-permute-start | bytes 4423688 | tf_op jit(solution)/shard_map/ppermute | solution.py:157
  79.1 34.1 %collective-permute-start.7 = (bf16[288,2560]{1,0:T(8,128)(2,1)}, bf16[288,2560]{1,0:T(8,128)(2,1)S(1)}, u32[]{:S(2)}, u32[]{:S(2)}) collective-permute-start(bf16[288,2560]{1,0:T(8,128)(2,1)} %collective-permute-done.3.refs_0_), channel_id=1, source_target_pairs={{0,8},{8,16},{16,24},{24,28},{28,20},{20,12},{12,4},{4,0},{1,9},{9... | collective-permute-start | bytes 4423688 | tf_op jit(solution)/shard_map/ppermute | solution.py:102
  80.6 33.8 %collective-permute-start.8 = (bf16[288,2560]{1,0:T(8,128)(2,1)}, bf16[288,2560]{1,0:T(8,128)(2,1)S(1)}, u32[]{:S(2)}, u32[]{:S(2)}) collective-permute-start(bf16[288,2560]{1,0:T(8,128)(2,1)} %collective-permute-done.4.refs_2_), channel_id=1, source_target_pairs={{8,0},{16,8},{24,16},{28,24},{20,28},{12,20},{4,12},{0,4},{9,1},{1... | collective-permute-start | bytes 4423688 | tf_op jit(solution)/shard_map/ppermute | solution.py:102
  81.1 33.3 %collective-permute-start.9 = (bf16[288,2560]{1,0:T(8,128)(2,1)}, bf16[288,2560]{1,0:T(8,128)(2,1)}, u32[]{:S(2)}, u32[]{:S(2)}) collective-permute-start(bf16[288,2560]{1,0:T(8,128)(2,1)} %collective-permute-done.3.refs_0_), channel_id=1, source_target_pairs={{0,1},{1,0},{2,3},{3,2},{4,5},{5,4},{6,7},{7,6},{8,9},{9,8},{10,11... | collective-permute-start | bytes 4423688 | tf_op jit(solution)/shard_map/ppermute | solution.py:157
  152.8 62.0 %collective-permute-start.17 = (bf16[8,288,512]{2,1,0:T(8,128)(2,1)}, bf16[8,288,512]{2,1,0:T(8,128)(2,1)}, u32[]{:S(2)}, u32[]{:S(2)}) collective-permute-start(bf16[8,288,512]{2,1,0:T(8,128)(2,1)} %bitcast_dynamic-update-slice_fusion.7.refs_0_), channel_id=1, source_target_pairs={{0,2},{1,3},{2,0},{3,1},{4,6},{5,7},{6,4},{7,5},{8,10},{9,11},{10,... | collective-permute-start | bytes 7077896 | tf_op jit(solution)/shard_map/ppermute | solution.py:157
  154.0 60.8 %collective-permute-start.15 = (bf16[288,2304]{1,0:T(8,128)(2,1)}, bf16[288,2304]{1,0:T(8,128)(2,1)S(1)}, u32[]{:S(2)}, u32[]{:S(2)}) collective-permute-start(bf16[288,2304]{1,0:T(8,128)(2,1)} %get-tuple-element.377), channel_id=1, source_target_pairs={{0,16},{4,20},{8,24},{12,28},{16,0},{20,4},{24,8},{28,12},{1,17},{... | collective-permute-start | bytes 3981320 | tf_op jit(solution)/shard_map/ppermute | solution.py:157
  215.9 37.4 %collective-permute-start.19 = (bf16[8,288,512]{2,1,0:T(8,128)(2,1)}, bf16[8,288,512]{2,1,0:T(8,128)(2,1)}, u32[]{:S(2)}, u32[]{:S(2)}) collective-permute-start(bf16[8,288,512]{2,1,0:T(8,128)(2,1)} %collective-permute-done.17.refs_1_), channel_id=1, source_target_pairs={{0,1},{1,0},{2,3},{3,2},{4,5},{5,4},{6,7},{7,6},{8,9},{9,8},{10,11... | collective-permute-start | bytes 7077896 | tf_op jit(solution)/shard_map/ppermute | solution.py:157
  216.9 36.4 %all-to-all-start = ((bf16[4,256,512]{2,1,0:T(8,128)(2,1)}), bf16[4,256,512]{2,1,0:T(8,128)(2,1)S(1)}, u32[]{:S(2)}, u32[]{:S(2)}) async-start(bf16[4,256,512]{2,1,0:T(8,128)(2,1)} %get-tuple-element.405), calls=%async_computation | async-start | bytes 2097152 | tf_op jit(solution)/shard_map/all_to_all | solution.py:168
  221.4 31.9 %collective-permute-start.18 = (bf16[288,2304]{1,0:T(8,128)(2,1)}, bf16[288,2304]{1,0:T(8,128)(2,1)}, u32[]{:S(2)}, u32[]{:S(2)}) collective-permute-start(bf16[288,2304]{1,0:T(8,128)(2,1)} %copy-done.60), channel_id=1, source_target_pairs={{0,2},{1,3},{2,0},{3,1},{4,6},{5,7},{6,4},{7,5},{8,10},{9,11},{10,... | collective-permute-start | bytes 3981320 | tf_op jit(solution)/shard_map/ppermute | solution.py:157
  253.3 30.5 %all-to-all-start.1 = ((bf16[4,256,512]{2,1,0:T(8,128)(2,1)}), bf16[4,256,512]{2,1,0:T(8,128)(2,1)}, u32[]{:S(2)}, u32[]{:S(2)}) async-start(bf16[4,256,512]{2,1,0:T(8,128)(2,1)} %get-tuple-element.410), calls=%async_computation.1 | async-start | bytes 2097152 | tf_op jit(solution)/shard_map/all_to_all | solution.py:168
  283.8 40.5 %all-to-all-start.2 = ((bf16[8,128,512]{2,1,0:T(8,128)(2,1)}), bf16[8,128,512]{2,1,0:T(8,128)(2,1)S(1)}, u32[]{:S(2)}, u32[]{:S(2)}) async-start(bf16[8,128,512]{2,1,0:T(8,128)(2,1)} %bitcast.341), calls=%async_computation.2 | async-start | bytes 2097152 | tf_op jit(solution)/shard_map/all_to_all | solution.py:161
  288.9 35.4 %collective-permute-start.23 = (bf16[4,256,512]{2,1,0:T(8,128)(2,1)}, bf16[4,256,512]{2,1,0:T(8,128)(2,1)S(1)}, u32[]{:S(2)}, u32[]{:S(2)}) collective-permute-start(bf16[4,256,512]{2,1,0:T(8,128)(2,1)} %all-to-all-done.1.refs_0_), channel_id=1, source_target_pairs={{0,4},{4,0},{8,12},{12,8},{16,20},{20,16},{24,28},{28,24},{1,5},{5... | collective-permute-start | bytes 3145736 | tf_op jit(solution)/shard_map/ppermute | solution.py:177
  324.3 30.3 %all-to-all-start.3 = ((bf16[8,128,512]{2,1,0:T(8,128)(2,1)}), bf16[8,128,512]{2,1,0:T(8,128)(2,1)S(1)}, u32[]{:S(2)}, u32[]{:S(2)}) async-start(bf16[8,128,512]{2,1,0:T(8,128)(2,1)} %bitcast.340), calls=%async_computation.3 | async-start | bytes 2097152 | tf_op jit(solution)/shard_map/all_to_all | solution.py:161
  422.6 59.2 %collective-permute-start.24 = (bf16[288,2304]{1,0:T(8,128)(2,1)S(1)}, bf16[288,2304]{1,0:T(8,128)(2,1)}, u32[]{:S(2)}, u32[]{:S(2)}) collective-permute-start(bf16[288,2304]{1,0:T(8,128)(2,1)S(1)} %copy-done.59), channel_id=1, source_target_pairs={{0,16},{4,20},{8,24},{12,28},{16,0},{20,4},{24,8},{28,12},{1,17},{... | collective-permute-start | bytes 3981320 | tf_op jit(solution)/shard_map/ppermute | solution.py:157
  481.8 31.4 %collective-permute-start.27 = (bf16[288,2304]{1,0:T(8,128)(2,1)}, bf16[288,2304]{1,0:T(8,128)(2,1)}, u32[]{:S(2)}, u32[]{:S(2)}) collective-permute-start(bf16[288,2304]{1,0:T(8,128)(2,1)} %collective-permute-done.24.refs_0_), channel_id=1, source_target_pairs={{0,2},{1,3},{2,0},{3,1},{4,6},{5,7},{6,4},{7,5},{8,10},{9,11},{10,... | collective-permute-start | bytes 3981320 | tf_op jit(solution)/shard_map/ppermute | solution.py:157
  533.5 60.0 %collective-permute-start.32 = (bf16[288,2304]{1,0:T(8,128)(2,1)}, bf16[288,2304]{1,0:T(8,128)(2,1)}, u32[]{:S(2)}, u32[]{:S(2)}) collective-permute-start(bf16[288,2304]{1,0:T(8,128)(2,1)} %get-tuple-element.474), channel_id=1, source_target_pairs={{0,16},{4,20},{8,24},{12,28},{16,0},{20,4},{24,8},{28,12},{1,17},{... | collective-permute-start | bytes 3981320 | tf_op jit(solution)/shard_map/ppermute | solution.py:157
  593.5 30.4 %collective-permute-start.35 = (bf16[288,2304]{1,0:T(8,128)(2,1)}, bf16[288,2304]{1,0:T(8,128)(2,1)S(1)}, u32[]{:S(2)}, u32[]{:S(2)}) collective-permute-start(bf16[288,2304]{1,0:T(8,128)(2,1)} %collective-permute-done.32.refs_0_), channel_id=1, source_target_pairs={{0,2},{1,3},{2,0},{3,1},{4,6},{5,7},{6,4},{7,5},{8,10},{9,11},{10,... | collective-permute-start | bytes 3981320 | tf_op jit(solution)/shard_map/ppermute | solution.py:157
  1025.1 31.4 %all-to-all-start.6 = ((bf16[8,128,512]{2,1,0:T(8,128)(2,1)}), bf16[8,128,512]{2,1,0:T(8,128)(2,1)}, u32[]{:S(2)}, u32[]{:S(2)}) async-start(bf16[8,128,512]{2,1,0:T(8,128)(2,1)} %bitcast.325), calls=%async_computation.6 | async-start | bytes 2097152 | tf_op jit(solution)/shard_map/all_to_all | solution.py:161
  1087.2 41.3 %all-to-all-start.8 = ((bf16[8,128,512]{2,1,0:T(8,128)(2,1)}), bf16[8,128,512]{2,1,0:T(8,128)(2,1)S(1)}, u32[]{:S(2)}, u32[]{:S(2)}) async-start(bf16[8,128,512]{2,1,0:T(8,128)(2,1)} %bitcast.343), calls=%async_computation.8 | async-start | bytes 2097152 | tf_op jit(solution)/shard_map/all_to_all | solution.py:161
  1092.1 35.1 %collective-permute-start.65 = (bf16[4,256,512]{2,1,0:T(8,128)(2,1)}, bf16[4,256,512]{2,1,0:T(8,128)(2,1)S(1)}, u32[]{:S(2)}, u32[]{:S(2)}) collective-permute-start(bf16[4,256,512]{2,1,0:T(8,128)(2,1)} %get-tuple-element.603), channel_id=1, source_target_pairs={{0,4},{4,0},{8,12},{12,8},{16,20},{20,16},{24,28},{28,24},{1,5},{5... | collective-permute-start | bytes 3145736 | tf_op jit(solution)/shard_map/ppermute | solution.py:177
  1100.8 96.0 %collective-permute-start.71 = (bf16[2304,1024]{1,0:T(8,128)(2,1)}, bf16[2304,1024]{1,0:T(8,128)(2,1)}, u32[]{:S(2)}, u32[]{:S(2)}) collective-permute-start(bf16[2304,1024]{1,0:T(8,128)(2,1)} %convolution_convert_fusion.1), channel_id=1, source_target_pairs={{0,1},{1,0},{2,3},{3,2},{4,5},{5,4},{6,7},{7,6},{8,9},{9,8},{10,11... | collective-permute-start | bytes 14155784 | tf_op jit(solution)/shard_map/ppermute | solution.py:157
  1100.8 91.0 %collective-permute-start.68 = (bf16[2,288,2304]{2,1,0:T(8,128)(2,1)}, bf16[2,288,2304]{2,1,0:T(8,128)(2,1)}, u32[]{:S(2)}, u32[]{:S(2)}) collective-permute-start(bf16[2,288,2304]{2,1,0:T(8,128)(2,1)} %slice_bitcast_fusion.10), channel_id=1, source_target_pairs={{0,2},{1,3},{2,0},{3,1},{4,6},{5,7},{6,4},{7,5},{8,10},{9,11},{10,... | collective-permute-start | bytes 7962632 | tf_op jit(solution)/shard_map/ppermute | solution.py:157
  1147.8 34.1 %collective-permute-start.66 = (bf16[4,256,512]{2,1,0:T(8,128)(2,1)}, bf16[4,256,512]{2,1,0:T(8,128)(2,1)S(1)}, u32[]{:S(2)}, u32[]{:S(2)}) collective-permute-start(bf16[4,256,512]{2,1,0:T(8,128)(2,1)} %get-tuple-element.616), channel_id=1, source_target_pairs={{0,4},{4,0},{8,12},{12,8},{16,20},{20,16},{24,28},{28,24},{1,5},{5... | collective-permute-start | bytes 3145736 | tf_op jit(solution)/shard_map/ppermute | solution.py:177
  1148.2 35.1 %all-to-all-start.9 = ((bf16[8,128,512]{2,1,0:T(8,128)(2,1)}), bf16[8,128,512]{2,1,0:T(8,128)(2,1)S(1)}, u32[]{:S(2)}, u32[]{:S(2)}) async-start(bf16[8,128,512]{2,1,0:T(8,128)(2,1)} %bitcast.89), calls=%async_computation.9 | async-start | bytes 2097152 | tf_op jit(solution)/shard_map/all_to_all | solution.py:161
  1189.0 38.1 %collective-permute-start.67 = (bf16[2,576,2304]{2,1,0:T(8,128)(2,1)}, bf16[2,576,2304]{2,1,0:T(8,128)(2,1)}, u32[]{:S(2)}, u32[]{:S(2)}) collective-permute-start(bf16[2,576,2304]{2,1,0:T(8,128)(2,1)} %slice_bitcast_fusion.2), channel_id=1, source_target_pairs={{0,1},{1,0},{2,3},{3,2},{4,5},{5,4},{6,7},{7,6},{8,9},{9,8},{10,11... | collective-permute-start | bytes 15925256 | tf_op jit(solution)/shard_map/ppermute | solution.py:157
  1202.9 30.5 %all-to-all-start.10 = ((bf16[4,256,512]{2,1,0:T(8,128)(2,1)}), bf16[4,256,512]{2,1,0:T(8,128)(2,1)S(1)}, u32[]{:S(2)}, u32[]{:S(2)}) async-start(bf16[4,256,512]{2,1,0:T(8,128)(2,1)} %add_convert_fusion.16), calls=%async_computation.10 | async-start | bytes 2097152 | tf_op jit(solution)/shard_map/all_to_all | solution.py:168
  1241.8 90.9 %collective-permute-start.73 = (bf16[2,288,2304]{2,1,0:T(8,128)(2,1)}, bf16[2,288,2304]{2,1,0:T(8,128)(2,1)}, u32[]{:S(2)}, u32[]{:S(2)}) collective-permute-start(bf16[2,288,2304]{2,1,0:T(8,128)(2,1)} %slice_bitcast_fusion.8), channel_id=1, source_target_pairs={{0,2},{1,3},{2,0},{3,1},{4,6},{5,7},{6,4},{7,5},{8,10},{9,11},{10,... | collective-permute-start | bytes 7962632 | tf_op jit(solution)/shard_map/ppermute | solution.py:157
  1286.8 54.6 %collective-permute-start.70 = (bf16[2304,2048]{1,0:T(8,128)(2,1)}, bf16[2304,2048]{1,0:T(8,128)(2,1)}, u32[]{:S(2)}, u32[]{:S(2)}) collective-permute-start(bf16[2304,2048]{1,0:T(8,128)(2,1)} %convolution_convert_fusion), channel_id=1, source_target_pairs={{0,1},{1,0},{2,3},{3,2},{4,5},{5,4},{6,7},{7,6},{8,9},{9,8},{10,11... | collective-permute-start | bytes 28311560 | tf_op jit(solution)/shard_map/ppermute | solution.py:157
  1290.8 45.2 %collective-permute-start.72 = (bf16[2,576,2304]{2,1,0:T(8,128)(2,1)}, bf16[2,576,2304]{2,1,0:T(8,128)(2,1)}, u32[]{:S(2)}, u32[]{:S(2)}) collective-permute-start(bf16[2,576,2304]{2,1,0:T(8,128)(2,1)} %slice_bitcast_fusion), channel_id=1, source_target_pairs={{0,1},{1,0},{2,3},{3,2},{4,5},{5,4},{6,7},{7,6},{8,9},{9,8},{10,11... | collective-permute-start | bytes 15925256 | tf_op jit(solution)/shard_map/ppermute | solution.py:157
  1324.5 60.9 %collective-permute-start.69 = (bf16[288,2304]{1,0:T(8,128)(2,1)}, bf16[288,2304]{1,0:T(8,128)(2,1)}, u32[]{:S(2)}, u32[]{:S(2)}) collective-permute-start(bf16[288,2304]{1,0:T(8,128)(2,1)} %slice_bitcast_fusion.18), channel_id=1, source_target_pairs={{0,16},{4,20},{8,24},{12,28},{16,0},{20,4},{24,8},{28,12},{1,17},{... | collective-permute-start | bytes 3981320 | tf_op jit(solution)/shard_map/ppermute | solution.py:157
  1403.6 57.4 %collective-permute-start.83 = (bf16[2,288,2304]{2,1,0:T(8,128)(2,1)S(1)}, bf16[2,288,2304]{2,1,0:T(8,128)(2,1)S(1)}, u32[]{:S(2)}, u32[]{:S(2)}) collective-permute-start(bf16[2,288,2304]{2,1,0:T(8,128)(2,1)S(1)} %slice_bitcast_fusion.6), channel_id=1, source_target_pairs={{0,2},{1,3},{2,0},{3,1},{4,6},{5,7},{6,4},{7,5},{8,10},{9,11},{10,... | collective-permute-start | bytes 7962632 | tf_op jit(solution)/shard_map/ppermute | solution.py:157
  1428.1 37.7 %collective-permute-start.82 = (bf16[288,3072]{1,0:T(8,128)(2,1)S(1)}, bf16[288,3072]{1,0:T(8,128)(2,1)S(1)}, u32[]{:S(2)}, u32[]{:S(2)}) collective-permute-start(bf16[288,3072]{1,0:T(8,128)(2,1)S(1)} %pad_maximum_fusion.9), channel_id=1, source_target_pairs={{8,0},{16,8},{24,16},{28,24},{20,28},{12,20},{4,12},{0,4},{9,1},{1... | collective-permute-start | bytes 5308424 | tf_op jit(solution)/shard_map/ppermute | solution.py:102
  1428.6 37.5 %collective-permute-start.81 = (bf16[288,3072]{1,0:T(8,128)(2,1)S(1)}, bf16[288,3072]{1,0:T(8,128)(2,1)S(1)}, u32[]{:S(2)}, u32[]{:S(2)}) collective-permute-start(bf16[288,3072]{1,0:T(8,128)(2,1)S(1)} %fusion.68), channel_id=1, source_target_pairs={{0,8},{8,16},{16,24},{24,28},{28,20},{20,12},{12,4},{4,0},{1,9},{9... | collective-permute-start | bytes 5308424 | tf_op jit(solution)/shard_map/ppermute | solution.py:102
  1466.7 37.4 %collective-permute-start.85 = (bf16[288,3072]{1,0:T(8,128)(2,1)S(1)}, bf16[288,3072]{1,0:T(8,128)(2,1)S(1)}, u32[]{:S(2)}, u32[]{:S(2)}) collective-permute-start(bf16[288,3072]{1,0:T(8,128)(2,1)S(1)} %add_convert_fusion.11), channel_id=1, source_target_pairs={{8,0},{16,8},{24,16},{28,24},{20,28},{12,20},{4,12},{0,4},{9,1},{1... | collective-permute-start | bytes 5308424 | tf_op jit(solution)/shard_map/ppermute | solution.py:102
  1468.4 36.3 %collective-permute-start.84 = (bf16[288,3072]{1,0:T(8,128)(2,1)S(1)}, bf16[288,3072]{1,0:T(8,128)(2,1)S(1)}, u32[]{:S(2)}, u32[]{:S(2)}) collective-permute-start(bf16[288,3072]{1,0:T(8,128)(2,1)S(1)} %add_convert_fusion.12), channel_id=1, source_target_pairs={{0,8},{8,16},{16,24},{24,28},{28,20},{20,12},{12,4},{4,0},{1,9},{9... | collective-permute-start | bytes 5308424 | tf_op jit(solution)/shard_map/ppermute | solution.py:102
  1505.4 36.1 %collective-permute-start.88 = (bf16[288,3072]{1,0:T(8,128)(2,1)S(1)}, bf16[288,3072]{1,0:T(8,128)(2,1)S(1)}, u32[]{:S(2)}, u32[]{:S(2)}) collective-permute-start(bf16[288,3072]{1,0:T(8,128)(2,1)S(1)} %add_convert_fusion.9), channel_id=1, source_target_pairs={{8,0},{16,8},{24,16},{28,24},{20,28},{12,20},{4,12},{0,4},{9,1},{1... | collective-permute-start | bytes 5308424 | tf_op jit(solution)/shard_map/ppermute | solution.py:102
  1507.9 35.2 %collective-permute-start.87 = (bf16[288,3072]{1,0:T(8,128)(2,1)S(1)}, bf16[288,3072]{1,0:T(8,128)(2,1)S(1)}, u32[]{:S(2)}, u32[]{:S(2)}) collective-permute-start(bf16[288,3072]{1,0:T(8,128)(2,1)S(1)} %add_convert_fusion.10), channel_id=1, source_target_pairs={{0,8},{8,16},{16,24},{24,28},{28,20},{20,12},{12,4},{4,0},{1,9},{9... | collective-permute-start | bytes 5308424 | tf_op jit(solution)/shard_map/ppermute | solution.py:102
  1544.0 63.1 %collective-permute-start.90 = (bf16[288,3072]{1,0:T(8,128)(2,1)S(1)}, bf16[288,3072]{1,0:T(8,128)(2,1)}, u32[]{:S(2)}, u32[]{:S(2)}) collective-permute-start(bf16[288,3072]{1,0:T(8,128)(2,1)S(1)} %add_convert_fusion.8), channel_id=1, source_target_pairs={{0,2},{1,3},{2,0},{3,1},{4,6},{5,7},{6,4},{7,5},{8,10},{9,11},{10,... | collective-permute-start | bytes 5308424 | tf_op jit(solution)/shard_map/ppermute | solution.py:157
  1545.4 60.7 %collective-permute-start.89 = (bf16[288,2304]{1,0:T(8,128)(2,1)S(1)}, bf16[288,2304]{1,0:T(8,128)(2,1)S(1)}, u32[]{:S(2)}, u32[]{:S(2)}) collective-permute-start(bf16[288,2304]{1,0:T(8,128)(2,1)S(1)} %slice_bitcast_fusion.17), channel_id=1, source_target_pairs={{0,16},{4,20},{8,24},{12,28},{16,0},{20,4},{24,8},{28,12},{1,17},{... | collective-permute-start | bytes 3981320 | tf_op jit(solution)/shard_map/ppermute | solution.py:157
  1608.7 31.0 %collective-permute-start.94 = (bf16[288,2304]{1,0:T(8,128)(2,1)S(1)}, bf16[288,2304]{1,0:T(8,128)(2,1)}, u32[]{:S(2)}, u32[]{:S(2)}) collective-permute-start(bf16[288,2304]{1,0:T(8,128)(2,1)S(1)} %fusion.33), channel_id=1, source_target_pairs={{0,2},{1,3},{2,0},{3,1},{4,6},{5,7},{6,4},{7,5},{8,10},{9,11},{10,... | collective-permute-start | bytes 3981320 | tf_op jit(solution)/shard_map/ppermute | solution.py:157
  1642.2 60.5 %collective-permute-start.92 = (bf16[288,2304]{1,0:T(8,128)(2,1)S(1)}, bf16[288,2304]{1,0:T(8,128)(2,1)S(1)}, u32[]{:S(2)}, u32[]{:S(2)}) collective-permute-start(bf16[288,2304]{1,0:T(8,128)(2,1)S(1)} %slice_bitcast_fusion.13), channel_id=1, source_target_pairs={{0,16},{4,20},{8,24},{12,28},{16,0},{20,4},{24,8},{28,12},{1,17},{... | collective-permute-start | bytes 3981320 | tf_op jit(solution)/shard_map/ppermute | solution.py:157
  1703.0 31.2 %collective-permute-start.96 = (bf16[288,2304]{1,0:T(8,128)(2,1)S(1)}, bf16[288,2304]{1,0:T(8,128)(2,1)S(1)}, u32[]{:S(2)}, u32[]{:S(2)}) collective-permute-start(bf16[288,2304]{1,0:T(8,128)(2,1)S(1)} %fusion.32), channel_id=1, source_target_pairs={{0,2},{1,3},{2,0},{3,1},{4,6},{5,7},{6,4},{7,5},{8,10},{9,11},{10,... | collective-permute-start | bytes 3981320 | tf_op jit(solution)/shard_map/ppermute | solution.py:157
  (222 other events, 3724.5 us)

commit v5 on v4

--- a/solution.py
+++ b/solution.py
@@ -839,11 +839,15 @@
     received, sent = sent[0], sent[1:]
     query_send, pair_send, out_own = sent[:count], sent[count : 2 * count], sent[2 * count :]
 
-    def start_spread(pair):
+    def spread(pair):
         held = [pair]
         for _ in range(classes - 1):
             held.append(class_ring(held[-1]))
-        return held
+        return held[1:]
+
+    def two_parts(value):
+        cut = value.shape[0] // 2
+        return value[:cut], value[cut:]
 
     attended_send, exact, lse, queries, pairs = [], [], [], [], []
 
@@ -857,32 +861,30 @@
         lse.append(work[2])
 
     out_other = [other_out] + [swap(v, "seq", 1) for v in out_own[1:]]
-    pair = heads_all_to_all(clock.hold(pair_send[0]))
+    pair_first, *out_other = clock.sync(heads_all_to_all(clock.hold(pair_send[0])), *out_other)
     gate_held = share([clock.hold(received)], far_bits)
-    pair, *work = clock.sync(pair, *gate_held, *out_other)
-    gate_held, out_other = work[: len(gate_held)], work[len(gate_held) :]
-    for s in seqs[1:]:
-        spread = start_spread(pair)
-        pair = heads_all_to_all(clock.hold(pair_send[s]))
-        work = []
-        if s == 1:
-            gate_held = share(gate_held, seq_bits[:1])
-            work = out_slices(out_own, out_other, places, info, output_scale, count)
-        pair, *rest = clock.sync(pair, *spread, *work, *gate_held)
-        pairs.append(rest[:classes])
-        if s == 1:
-            out_weights = rest[classes : classes + count]
-            gate_held = rest[classes + count :]
-    spread = start_spread(pair)
-    for s in seqs:
-        query = all_to_all(clock.hold(query_send[s]))
-        if s == 0:
-            query, *rest = clock.sync(query, *spread)
-            pairs.append(rest)
-        else:
-            query, *rest = clock.sync(query, *attend(s - 1))
-            keep_attend(rest)
-        queries.append(query.reshape(wide * class_rows, head_cols))
+    moved = spread(pair_first)
+    pair_last = heads_all_to_all(clock.hold(pair_send[1]))
+    out_weights = out_slices(out_own, out_other, places, info, output_scale, count)
+    work = clock.sync(pair_last, *moved, *out_weights, *gate_held)
+    pair_last, work = work[0], work[1:]
+    pairs.append([pair_first] + work[: classes - 1])
+    out_weights = work[classes - 1 : classes - 1 + count]
+    gate_held = share(work[classes - 1 + count :], seq_bits[:1])
+    part_a, part_b = two_parts(pair_last)
+    query = all_to_all(clock.hold(query_send[0]))
+    query, *work = clock.sync(query, *spread(part_a), *gate_held)
+    moved_a, gate_held = work[: classes - 1], work[classes - 1 :]
+    queries.append(query.reshape(wide * class_rows, head_cols))
+    moved_b = spread(clock.hold(part_b))
+    query = all_to_all(clock.hold(query_send[1]))
+    query, *work = clock.sync(query, *moved_b, *attend(0))
+    moved_b = work[: classes - 1]
+    keep_attend(work[classes - 1 :])
+    queries.append(query.reshape(wide * class_rows, head_cols))
+    pairs.append(
+        [pair_last] + [jnp.concatenate([x, y], axis=0) for x, y in zip(moved_a, moved_b)]
+    )
 
     attended, branch, branch_factor, middle, middle_factor, normed_mlp = [], [], [], [], [], []
 
@@ -936,51 +938,57 @@
     def mix(s):
         return dot(clock.hold(hidden_rows[s]), down_weights[s], NN).astype(bf16)
 
-    def staged_share(received):
-        held = [received]
-
-        def beside(step):
-            nonlocal held
-            if step == 0:
-                held = share([clock.hold(held[0])], far_bits)
-            elif step == 1:
-                held = share(held, seq_bits[:1])
-            return tuple(held)
-
-        def keep(work):
-            nonlocal held
-            held = work
-
-        return beside, keep, lambda: held
-
-    def shared_gather(value, received):
-        beside, keep, result = staged_share(received)
-        a = b = clock.hold(value)
-        out = [a]
-        for k in range(1, half_wide // 2 + 1):
-            if k == half_wide // 2:
-                a, b = halves(a)[0], halves(b)[1]
-            work = beside(k - 1) if k <= 2 else ()
-            a, b = hop(a, b, half_wide)
-            a, b, *work = clock.sync(a, b, *work)
-            if work:
-                keep(work)
-            out += [a, b]
-        return jnp.concatenate(out, axis=0), result()
-
-    group, up_held = shared_gather(normed_mlp[0], received)
-    gathered.append(group)
-    received = exchange(2)
-    gate.append(open_gate(0))
-    up_weights = partner_weights(1, up_held)
-    received, *work = clock.sync(received, *open_up(0), *up_weights, gate[0])
-    keep_up(work[:2])
-    up_weights = work[2 : 2 + count]
-    gate[0] = work[-1]
-    for s in seqs[1:]:
-        group, down_held = shared_gather(normed_mlp[s], received)
-        gathered.append(group)
-    down_weights = partner_weights(2, down_held)
+    up_held = share([clock.hold(received)], far_bits)
+    received, *up_held = clock.sync(exchange(2), *up_held)
+
+    def beside_first(step):
+        nonlocal up_held
+        if step == 0:
+            up_held = share(up_held, seq_bits[:1])
+            return tuple(up_held) + tuple(share([clock.hold(received)], far_bits))
+        if step == 1:
+            return tuple(partner_weights(1, [clock.hold(v) for v in up_held]))
+        return ()
+
+    a = b = clock.hold(normed_mlp[0])
+    blocks = [a]
+    for k in range(1, half_wide // 2 + 1):
+        if k == half_wide // 2:
+            a, b = halves(a)[0], halves(b)[1]
+        if k == 2:
+            down_held = share(down_held, seq_bits[:1])
+        work = beside_first(k - 1) + (tuple(down_held) if k == 2 else ())
+        a, b = hop(a, b, half_wide)
+        a, b, *work = clock.sync(a, b, *work)
+        if k == 1:
+            up_held, down_held = work[: len(up_held)], work[len(up_held) :]
+        elif k == 2:
+            up_weights, down_held = work[:count], work[count:]
+        blocks += [a, b]
+    gathered.append(jnp.concatenate(blocks, axis=0))
+
+    def beside_second(step):
+        if step == 0:
+            return [open_gate(0)] + list(partner_weights(2, [clock.hold(v) for v in down_held]))
+        if step == 1:
+            return open_up(0)
+        return ()
+
+    a = b = clock.hold(normed_mlp[1])
+    blocks = [a]
+    for k in range(1, half_wide // 2 + 1):
+        if k == half_wide // 2:
+            a, b = halves(a)[0], halves(b)[1]
+        work = beside_second(k - 1)
+        a, b = hop(a, b, half_wide)
+        a, b, *work = clock.sync(a, b, *work)
+        if k == 1:
+            gate.append(work[0])
+            down_weights = work[1:]
+        elif k == 2:
+            keep_up(work)
+        blocks += [a, b]
+    gathered.append(jnp.concatenate(blocks, axis=0))
     parts.append(clock.sync(mix(0))[0])
 
     layer_out, grad_mixed, gain_fourth = [], [], 0.0
@@ -1148,98 +1156,105 @@
             total = low_sum(dkv[step % classes], class_ring(total))
         return total
 
-    grad_heads, grad_attend = [], []
-    for s in seqs:
-        back = all_to_all(clock.hold(grad_send[s]))
-        if s == 0:
-            work = back_branch(count - 1)
-            down_grad = part_sum(down_grad, 1)
-            back, down_grad, *work = clock.sync(back, down_grad, *work)
-            keep_branch(work)
-        else:
-            back, *work = clock.sync(back, *attend_back(s - 1))
-            grad_attend.append(work)
-        grad_heads.append(back.reshape(wide * class_rows, head_cols))
-
-    def far_sum_start(grad):
+    def far_start(grad):
         split = grad.reshape(2, 2, grad.shape[1] // 2, model_dim)
         return split[:, 0], swap(clock.hold(split[:, 1]), "seq", seq_bits[1])
 
-    down_keep, down_move = far_sum_start(down_grad)
-
-    query_back, pair_back, pair_sum = [], [], []
-    for s in seqs:
-        dq, *dkv = grad_attend[s]
-        query = all_to_all(clock.hold(dq))
-        pair = class_sum(dkv)
-        if s + 1 < count:
-            query, pair, *work = clock.sync(query, pair, *attend_back(s + 1))
-            grad_attend.append(work)
-        else:
-            up_first = weight_first(grad_up[0], gathered[0])
-            up_grad = weight_rest(up_first, grad_up, gathered)
-            query, pair, up_grad = clock.sync(query, pair, up_grad)
-        query_back.append(query)
-        pair_sum.append(pair)
-    for s in seqs:
-        pair = heads_all_to_all(clock.hold(pair_sum[s]))
-        if s == 0:
-            gate_first = weight_first(grad_gate[0], gathered[0])
-            up_grad = part_sum(up_grad, 1)
-            down_grad = low_sum(down_keep, down_move)
-            pair, gate_first, up_grad, down_grad = clock.sync(pair, gate_first, up_grad, down_grad)
-            up_keep, up_move = far_sum_start(up_grad)
-        elif s == 1:
-            gate_grad = weight_rest(gate_first, grad_gate, gathered)
-            pair, gate_grad = clock.sync(pair, gate_grad)
-        else:
-            (pair,) = clock.sync(pair)
-        pair_back.append(pair)
-
-    def owner_start(grad):
-        return grad[0], swap(clock.hold(grad[1]), "wide", half_wide)
-
-    def last_sums(grad):
+    def far_end(kept, moved):
+        grad = low_sum(kept, moved)
         for bit in seq_bits[2:]:
             grad = part_sum(grad, bit)
         return grad
 
-    down_grad = last_sums(down_grad)
+    grad_heads, grad_attend = [], []
+    query_back, pair_back = [], []
+
+    def heads_of(value):
+        return value.reshape(wide * class_rows, head_cols)
+
+    back = all_to_all(clock.hold(grad_send[0]))
+    down_grad = part_sum(down_grad, 1)
+    back, down_grad, *work = clock.sync(back, down_grad, *back_branch(1))
+    keep_branch(work)
+    grad_heads.append(heads_of(back))
+    all_normed = jnp.concatenate(normed, axis=0)
+    all_attended = jnp.concatenate(attended, axis=0)
+    all_branch = jnp.concatenate(grad_branch, axis=0)
+
+    def half_dot(left, right, which, size):
+        return dot(left, lax.dynamic_slice_in_dim(right, which * size, size, 1), TN)
+
+    down_keep, down_move = far_start(down_grad)
+    back = all_to_all(clock.hold(grad_send[1]))
+    out_send = half_dot(all_branch, clock.hold(all_attended), 1 - side, half_out).astype(bf16)
+    back, out_send, *work = clock.sync(back, out_send, *attend_back(0))
+    grad_heads.append(heads_of(back))
+    grad_attend.append(work)
+
+    dq, *dkv = grad_attend[0]
+    parts_of_pair = [two_parts(v) for v in dkv]
+    out_sent = swap(out_send, "seq", 1)
+    query = all_to_all(clock.hold(dq))
+    pair_a = class_sum([v[0] for v in parts_of_pair])
+    out_part = low_sum(
+        half_dot(all_branch, clock.hold(all_attended), side, half_out), out_sent
+    )
+    query, pair_a, out_part, *work = clock.sync(query, pair_a, out_part, *attend_back(1))
+    query_back.append(query)
+    grad_attend.append(work)
+    dq, *dkv = grad_attend[1]
+    query = all_to_all(clock.hold(dq))
+    pair_b = class_sum([clock.hold(v[1]) for v in parts_of_pair])
+    up_first = weight_first(grad_up[0], gathered[0])
+    query, pair_b, up_first = clock.sync(query, pair_b, up_first)
+    query_back.append(query)
+
+    out_pieces = {
+        t: lax.dynamic_slice_in_dim(
+            out_part, jnp.bitwise_xor(member, t) * split_out, split_out, 1
+        )
+        for t in range(members)
+    }
+
+    pair = heads_all_to_all(clock.hold(jnp.concatenate([pair_a, pair_b], axis=0)))
+    pair_sum = class_sum(dkv)
+    up_grad = weight_rest(up_first, grad_up, gathered)
+    pair, pair_sum, up_grad, down_move = clock.sync(pair, pair_sum, up_grad, down_move)
+    pair_back.append(pair)
+    down_grad = far_end(down_keep, down_move)
+    for bit in seq_bits[1:]:
+        for t in range(members):
+            if not t & (bit // 2) and t in out_pieces and t | (bit // 2) in out_pieces:
+                out_pieces[t] = low_sum(
+                    out_pieces[t], swap(clock.hold(out_pieces.pop(t | (bit // 2))), "seq", bit)
+                )
+    pair = heads_all_to_all(clock.hold(pair_sum))
+    up_grad = part_sum(up_grad, 1)
+    pair, up_grad, down_grad = clock.sync(pair, up_grad, down_grad)
+    pair_back.append(pair)
+    up_keep, up_move = far_start(up_grad)
+
+    def owner_start(grad):
+        return grad[0], swap(clock.hold(grad[1]), "wide", half_wide)
+
     down_own, down_other = owner_start(down_grad)
     grad_proj = turn_back(
         [v.reshape(KEY_VALUE_HEADS, rows, head_cols) for v in query_back], pair_back, cosine, sine
     )
-    all_normed = jnp.concatenate(normed, axis=0)
-    all_attended = jnp.concatenate(attended, axis=0)
-    all_branch = jnp.concatenate(grad_branch, axis=0)
-
-    def half_dot(left, right, which, size):
-        return dot(left, lax.dynamic_slice_in_dim(right, which * size, size, 1), TN)
-
     proj_sent = swap(half_dot(all_normed, grad_proj, 1 - side, half_proj).astype(bf16), "seq", 1)
-    out_sent = swap(half_dot(all_branch, all_attended, 1 - side, half_out).astype(bf16), "seq", 1)
-    gate_grad = part_sum(gate_grad, 1)
-    grad_tokens, gain_first = [], 0.0
-    for s in seqs:
-        grad_normed = dot(grad_proj[s * rows : (s + 1) * rows], proj_weights[s], NT)
-        grad, gain = norm_back(inputs[s], input_factor[s], gain_attn, grad_normed)
-        gain_first = gain_first + gain
-        grad_tokens.append((grad_middle[s] + grad).astype(bf16))
-    gains = jnp.stack([gain_first, gain_second, gain_third, gain_fourth])
-    out_part = low_sum(half_dot(all_branch, all_attended, side, half_out), out_sent)
+    gate_first = weight_first(grad_gate[0], gathered[0])
     proj_part = low_sum(half_dot(all_normed, grad_proj, side, half_proj), proj_sent)
-    up_grad = low_sum(up_keep, up_move)
-    down_other, proj_part, out_part, gains, gate_grad, up_grad, *grad_tokens = clock.sync(
-        down_other, proj_part, out_part, gains, gate_grad, up_grad, *grad_tokens
-    )
-    gate_keep, gate_move = far_sum_start(gate_grad)
+    down_other, proj_part, out_piece, gate_first, up_move = clock.sync(
+        down_other, proj_part, out_pieces[0], gate_first, up_move
+    )
+    up_grad = far_end(up_keep, up_move)
 
     def part_of(o):
         first = index_at(o) * attn_rows
         return jnp.concatenate(
             [
                 lax.dynamic_slice_in_dim(proj_part, first, attn_rows, 0),
-                lax.dynamic_slice_in_dim(out_part, first, attn_rows, 0),
+                lax.dynamic_slice_in_dim(out_piece, first, attn_rows, 0),
             ],
             axis=1,
         )
@@ -1249,47 +1264,98 @@
             grad = jnp.concatenate([grad, swap(grad, "seq", bit)], axis=0)
         return grad
 
-    for axis, size in (("seq", seq_size), ("wide", wide)):
-        bit = 1
-        while bit < size:
-            gains = gains + swap(gains, axis, bit)
-            bit *= 2
+    grad_tokens, gain_first = [], 0.0
+
+    def back_tokens(s):
+        grad_normed = dot(clock.hold(grad_proj[s * rows : (s + 1) * rows]), proj_weights[s], NT)
+        grad, gain = norm_back(inputs[s], input_factor[s], gain_attn, grad_normed)
+        return [(grad_middle[s] + grad).astype(bf16), gain]
+
     down_grad = low_sum(down_own, down_other)
+    ring_work = {}
 
     def beside_ring(step):
         if step == 0:
-            return (gains,)
+            return (weight_rest(gate_first, grad_gate, gathered),)
         if step == 1:
-            return (gate_move,)
+            ring_work["down"] = spread_grad(clock.hold(down_grad), far_bits)
+            return (part_sum(ring_work["gate"], 1), *back_tokens(0))
         if step == 2:
-            return (spread_grad(clock.hold(down_grad), far_bits),)
+            ring_work["move"] = far_start(ring_work["gate"])
+            return (ring_work["down"], *back_tokens(1))
+        if step == half_wide - 1:
+            return tuple(ring_work["move"])
         return ()
 
-    total, work = ring_scatter(clock, part_of, attn_rows, wide, beside_ring)
-    gains, gate_move, down_grad = work[0][0], work[1][0], work[2][0]
-    gate_grad = last_sums(low_sum(gate_keep, gate_move))
-
-    up_own, up_other = owner_start(last_sums(up_grad))
-    attn_low = total.astype(bf16)
-    attn_move = swap(clock.hold(attn_low), "seq", seq_bits[1])
-    mlp_grad = unpack(spread_grad(clock.hold(down_grad), seq_bits[:1]), pieces, 2, [])
-    up_other, attn_move, mlp_grad = clock.sync(up_other, attn_move, mlp_grad)
+    a, b = halves(clock.hold(part_of(wide // 2)))
+    for k in range(wide // 2 - 1, -1, -1):
+        step = wide // 2 - 1 - k
+        work = beside_ring(step)
+        a, b = hop(a, b, wide)
+        a, b, *work = clock.sync(a, b, *work)
+        if step == 0:
+            ring_work["gate"] = work[0]
+        elif step == 1:
+            ring_work["gate"] = work[0]
+            grad_tokens.append(work[1])
+            gain_first = work[2]
+        elif step == 2:
+            down_grad = work[0]
+            grad_tokens.append(work[1])
+            gain_first = gain_first + work[2]
+        elif step == half_wide - 1:
+            gate_grad = far_end(*work)
+        if step == 0:
+            a, b = add_first(part_of(k), a), add_last(part_of(-k), b)
+        elif k > 0:
+            a, b = low_sum(part_of(k), a), low_sum(part_of(-k), b)
+    total = low_sum(part_of(0), a, b)
+
+    def add_swapped(gains, axis, bits):
+        for bit in bits:
+            gains = gains + swap(gains, axis, bit)
+        return gains
+
+    gains = jnp.stack([gain_first, gain_second, gain_third, gain_fourth])
+    wide_bits = [1 << i for i in range(wide.bit_length() - 1)]
+    (gains,) = clock.sync(add_swapped(clock.hold(gains), "wide", wide_bits[1:]))
+
+    up_own, up_other = owner_start(up_grad)
+    gains = add_swapped(add_swapped(gains, "wide", wide_bits[:1]), "seq", seq_bits)
+    proj_total = total[:, :half_proj]
+    out_totals = {0: total[:, half_proj:]}
+    for bit in seq_bits[1:]:
+        sent = jnp.concatenate([proj_total] + [out_totals[t] for t in sorted(out_totals)], axis=1)
+        moved = swap(clock.hold(sent), "seq", bit)
+        proj_total = low_sum(proj_total, moved[:, :half_proj])
+        for i, t in enumerate(sorted(out_totals)):
+            first = half_proj + i * split_out
+            out_totals[t | (bit // 2)] = moved[:, first : first + split_out]
+    out_totals = jnp.stack([out_totals[t] for t in range(members)])
+    low = jnp.concatenate(
+        [proj_total]
+        + [
+            lax.dynamic_index_in_dim(out_totals, jnp.bitwise_xor(member, j), 0, keepdims=False)
+            for j in range(members)
+        ],
+        axis=1,
+    )
+    up_other, low, gains = clock.sync(up_other, low, gains)
+    up_grad = low_sum(up_own, up_other)
     gate_own, gate_other = owner_start(gate_grad)
-    for bit in seq_bits[2:]:
-        attn_low = low_sum(attn_low, attn_move)
-        attn_move = swap(attn_low, "seq", bit)
-    low = low_sum(attn_low, attn_move)
+    up_grad = spread_grad(clock.hold(up_grad), far_bits)
     other = swap(low, "seq", 1)
     left, right = jnp.where(is_low, low, other), jnp.where(is_low, other, low)
     attn_grad = jnp.concatenate(
         [left[:, :half_proj], right[:, :half_proj], left[:, half_proj:], right[:, half_proj:]],
         axis=1,
     ).astype(f32)
-    up_grad = spread_grad(low_sum(up_own, up_other), reversed(seq_bits))
-    mlp_grad = unpack(up_grad, pieces, 1, [mlp_grad])
-    gate_other, attn_grad, mlp_grad = clock.sync(gate_other, attn_grad, mlp_grad)
-    gate_grad = spread_grad(low_sum(gate_own, gate_other), reversed(seq_bits))
-    mlp_grad = unpack(gate_grad, pieces, 0, [mlp_grad])
+    mlp_grad = unpack(spread_grad(clock.hold(down_grad), seq_bits[:1]), pieces, 2, [])
+    gate_other, up_grad, attn_grad, mlp_grad = clock.sync(gate_other, up_grad, attn_grad, mlp_grad)
+    gate_grad = spread_grad(low_sum(gate_own, gate_other), far_bits)
+    mlp_grad = unpack(spread_grad(clock.hold(up_grad), seq_bits[:1]), pieces, 1, [mlp_grad])
+    gate_grad, mlp_grad = clock.sync(gate_grad, mlp_grad)
+    mlp_grad = unpack(spread_grad(gate_grad, seq_bits[:1]), pieces, 0, [mlp_grad])
     return (
         jnp.stack(layer_out),
         jnp.stack(grad_tokens),

time: 1760 us -> 1760 us (level)
  waiting for transfers between devices: 711 us -> 662 us
  matrix products: 395 us -> 431 us
  local copies, waits for them, and re-layouts: 113 us -> 131 us
    ppermute x48, waiting for transfers between devices: 233 us -> 155 us  [hop(): return (lax.ppermute(a, 'wide', up), lax.ppermute(b, 'wide', down))]
    all_to_all x4, waiting for transfers between devices: 0.83 us -> 39.4 us  [heads_all_to_all(): lax.all_to_all(value, 'wide', split_axis=0, concat_axis=0, axis_index_gro...]
    dot_general x28, matrix products: 395 us -> 431 us  [dot(): return lax.dot_general(a, b, (dims, ((), ())), preferred_element_type=f32)]
    convert_element_type x4 -> x2, other arithmetic: 40.6 us -> 7.07 us  [back_tokens(): return [(grad_middle[s] + grad).astype(bf16), gain]]
    all_to_all x8, waiting for transfers between devices: 44.2 us -> 25.7 us  [all_to_all(): lax.all_to_all(value, 'wide', split_axis=0, concat_axis=0, tiled=True)]
    convert_element_type x22 -> x25, other arithmetic: 43.9 us -> 55.5 us  [low_sum(): return sum((t.astype(f32) for t in terms)).astype(bf16)]
    ppermute x46 -> x47, waiting for transfers between devices: 382 us -> 390 us  [swap(): return lax.ppermute(value, axis, [(i, i ^ bit) for i in range(size)])]
    unnamed x347 -> x324, local copies, waits for them, and re-layouts: 49.4 us -> 56.7 us
  transfers between devices with their start and end apart: 110 -> 113, of which waited for: 67 -> 60; matrix products, arithmetic and copies ran while one was open for 28% -> 30% of each run, Pallas kernels for 12% -> 11%
where the time goes in v5:
time: 1760 us; the launch traced here: 1750 us
  waiting for transfers between devices  662 us (38%)
  matrix products  431 us (24%)
  Pallas kernels  217 us (12%)
  other arithmetic  165 us (9%)
  starting transfers between devices  139 us (8%)
  local copies, waits for them, and re-layouts  131 us (7%)
    dot_general x28, matrix products, dot(): return lax.dot_general(a, b, (dims, ((), ())), preferred_element_type=f32)  431 us
    ppermute x47, waiting for transfers between devices, swap(): return lax.ppermute(value, axis, [(i, i ^ bit) for i in range(size)])  390 us
    ppermute x48, waiting for transfers between devices, hop(): return (lax.ppermute(a, 'wide', up), lax.ppermute(b, 'wide', down))  155 us
    unnamed x324, local copies, waits for them, and re-layouts  56.7 us
    convert_element_type x25, other arithmetic, low_sum(): return sum((t.astype(f32) for t in terms)).astype(bf16)  55.5 us
    ppermute x48, starting transfers between devices, hop(): return (lax.ppermute(a, 'wide', up), lax.ppermute(b, 'wide', down))  54.2 us
    ppermute x6, waiting for transfers between devices, class_ring(): return lax.ppermute(value, 'wide', perm)  52 us
    all_to_all x4, waiting for transfers between devices, heads_all_to_all(): lax.all_to_all(value, 'wide', split_axis=0, concat_axis=0, axis_index_gro...  39.4 us
  transfers between devices with their start and end apart: 113, of which 60 were waited for; matrix products, arithmetic and copies ran while one was open for 30% of the time, Pallas kernels for 11%

profile of v5, /device:TPU:0, one launch (start us, length us, event | category | flops | bytes accessed | tf_op | source)
XLA Modules:
  0.0 1749.1 jit_solution(12956145277313541291)
XLA Ops:
  11.3 25.2 %own_slices.1 = (bf16[2304,2304]{1,0:T(8,128)(2,1)}, bf16[2304,2304]{1,0:T(8,128)(2,1)}, bf16[2304,2304]{1,0:T(8,128)(2,1)}, bf16[2304,2304]{1,0:T(8,128)(2,1)},...) custom-call(s32[4]{0:T(128)} %pad_add_fusion.pieces, s32[4]{0:T(128)} %pad_add_fusion.1.info, ...), custom_call_target="tpu_custom_call" | custom-call | flops 159252480 | bytes 63700992 | tf_op jit(solution)/shard_map/own_slices/pallas_call | solution.py:297
  48.2 27.8 %collective-permute-done.3.refs_0_ = bf16[288,2560]{1,0:T(8,128)(2,1)} collective-permute-done((bf16[288,2560]{1,0:T(8,128)(2,1)}, bf16[288,2560]{1,0:T(8,128)(2,1)}, u32[]{:S(2)}, u32[]{:S(2)}) %collective-permute-start.3) | collective-permute-done | bytes 1474592 | tf_op jit(solution)/shard_map/ppermute | solution.py:102
  92.6 20.6 %collective-permute-done.7.refs_0_ = bf16[288,2560]{1,0:T(8,128)(2,1)S(1)} collective-permute-done((bf16[288,2560]{1,0:T(8,128)(2,1)}, bf16[288,2560]{1,0:T(8,128)(2,1)S(1)}, u32[]{:S(2)}, u32[]{:S(2)}) %collective-permute-start.7) | collective-permute-done | bytes 1474592 | tf_op jit(solution)/shard_map/ppermute | solution.py:102
  189.9 25.0 %collective-permute-done.15.refs_0_ = bf16[288,2304]{1,0:T(8,128)(2,1)S(1)} collective-permute-done((bf16[288,2304]{1,0:T(8,128)(2,1)}, bf16[288,2304]{1,0:T(8,128)(2,1)S(1)}, u32[]{:S(2)}, u32[]{:S(2)}) %collective-permute-start.15) | collective-permute-done | bytes 1327136 | tf_op jit(solution)/shard_map/ppermute | solution.py:157
  227.4 19.7 %all-to-all-done.refs_0_ = bf16[4,256,512]{2,1,0:T(8,128)(2,1)S(1)} async-done(((bf16[4,256,512]{2,1,0:T(8,128)(2,1)}), bf16[4,256,512]{2,1,0:T(8,128)(2,1)S(1)}, u32[]{:S(2)}, u32[]{:S(2)}) %all-to-all-start) | async-done | bytes 1048608 | tf_op jit(solution)/shard_map/all_to_all | solution.py:168
  254.9 20.6 %out_slices.1 = (bf16[2304,2048]{1,0:T(8,128)(2,1)}, bf16[2304,2048]{1,0:T(8,128)(2,1)}) custom-call(s32[8]{0:T(128)} %stack.172.places, s32[4]{0:T(128)} %pad_add_fusion.1.info, bf16[8,288,512]{2,1,0:T(8,128)(2,1)} %bitcast_dynamic-update-slice_fusion.7.refs_0_, bf16[8,288,512]{2,1,0:T(8,128)(2,1)} %collective-permute-done.17.refs_1_, ...), custom_call_target="tpu_custom_call" | custom-call | flops 94371840 | bytes 28311552 | tf_op jit(solution)/shard_map/out_slices/pallas_call | solution.py:260
  290.9 20.6 %collective-permute-done.21 = bf16[2,256,512]{2,1,0:T(8,128)(2,1)S(1)} collective-permute-done((bf16[2,256,512]{2,1,0:T(8,128)(2,1)S(1)}, bf16[2,256,512]{2,1,0:T(8,128)(2,1)S(1)}, u32[]{:S(2)}, u32[]{:S(2)}) %collective-permute-start.21) | collective-permute-done | bytes 524320 | tf_op jit(solution)/shard_map/ppermute | solution.py:177
  389.0 15.8 all-to-all-done.5
  416.1 55.1 %collective-permute-done.25.refs_0_ = bf16[288,2304]{1,0:T(8,128)(2,1)S(1)} collective-permute-done((bf16[288,2304]{1,0:T(8,128)(2,1)S(1)}, bf16[288,2304]{1,0:T(8,128)(2,1)S(1)}, u32[]{:S(2)}, u32[]{:S(2)}) %collective-permute-start.25) | collective-permute-done | bytes 1327136 | tf_op jit(solution)/shard_map/ppermute | solution.py:157
  472.1 30.2 %collective-permute-done.27.refs_1_ = bf16[288,2304]{1,0:T(8,128)(2,1)S(1)} collective-permute-done((bf16[288,2304]{1,0:T(8,128)(2,1)S(1)}, bf16[288,2304]{1,0:T(8,128)(2,1)S(1)}, u32[]{:S(2)}, u32[]{:S(2)}) %collective-permute-start.27) | collective-permute-done | bytes 1327136 | tf_op jit(solution)/shard_map/ppermute | solution.py:157
  502.3 29.0 %collective-permute-done.26.refs_0_ = bf16[288,2304]{1,0:T(8,128)(2,1)} collective-permute-done((bf16[288,2304]{1,0:T(8,128)(2,1)S(1)}, bf16[288,2304]{1,0:T(8,128)(2,1)}, u32[]{:S(2)}, u32[]{:S(2)}) %collective-permute-start.26) | collective-permute-done | bytes 1327136 | tf_op jit(solution)/shard_map/ppermute | solution.py:157
  535.1 26.1 %collective-permute-done.28 = bf16[256,2304]{1,0:T(8,128)(2,1)S(1)} collective-permute-done((bf16[256,2304]{1,0:T(8,128)(2,1)S(1)}, bf16[256,2304]{1,0:T(8,128)(2,1)S(1)}, u32[]{:S(2)}, u32[]{:S(2)}) %collective-permute-start.28) | collective-permute-done | bytes 1179680 | tf_op jit(solution)/shard_map/ppermute | solution.py:102
  589.4 16.7 fusion.96
  620.5 21.2 %multiply_convert_fusion.3 = (bf16[1024,2304]{1,0:T(8,128)(2,1)}, f32[1024,2304]{1,0:T(8,128)}) fusion(f32[1024,2304]{1,0:T(8,128)} %fusion.96, bf16[1024,2304]{1,0:T(8,128)(2,1)} %constant_dynamic-update-slice_fusion.4, bf16[2304,2304]{1,0:T(8,128)(2,1)} %get-tuple-element.547), kind=kOutput, calls=%fused_computation.35 | convolution fusion | flops 10895228928 | bytes 38928384 | tf_op jit(solution)/shard_map/dot_general | solution.py:26
  645.7 15.1 convolution_convert_fusion.3
  666.0 13.6 fusion.97
  684.5 21.3 %multiply_convert_fusion.2 = (bf16[1024,2304]{1,0:T(8,128)(2,1)}, f32[1024,2304]{1,0:T(8,128)}) fusion(f32[1024,2304]{1,0:T(8,128)} %fusion.97, bf16[1024,2304]{1,0:T(8,128)(2,1)} %copy-done.93, bf16[2304,2304]{1,0:T(8,128)(2,1)} %get-tuple-element.564), kind=kOutput, calls=%fused_computation.34 | convolution fusion | flops 10895228928 | bytes 38928384 | tf_op jit(solution)/shard_map/dot_general | solution.py:26
  720.9 13.5 convolution_convert_fusion.2
  761.5 27.3 %multiply_convert_fusion.1 = (bf16[1024,2304]{1,0:T(8,128)(2,1)}, bf16[1024,2304]{1,0:T(8,128)(2,1)}) fusion(f32[1024,2304]{1,0:T(8,128)} %fusion.96, f32[1024,2304]{1,0:T(8,128)} %get-tuple-element.583, bf16[1024,2304]{1,0:T(8,128)(2,1)} %copy-done.95, bf16[2304,2304]{1,0:T(8,128)(2,1)} %get-tuple-element.552), kind=kOutput, calls=%fused_computation.33 | convolution fusion | flops 10925899776 | bytes 43646976 | tf_op jit(solution)/shard_map/dot_general | solution.py:26
  788.8 16.7 fusion.98
  809.5 17.4 add_convert_fusion.6
  837.3 17.3 fusion.99
  862.9 12.2 collective-permute-done.55
  879.8 27.3 %multiply_convert_fusion = (bf16[1024,2304]{1,0:T(8,128)(2,1)}, bf16[1024,2304]{1,0:T(8,128)(2,1)}) fusion(f32[1024,2304]{1,0:T(8,128)} %fusion.97, f32[1024,2304]{1,0:T(8,128)} %get-tuple-element.604, bf16[1024,2304]{1,0:T(8,128)(2,1)} %copy-done.94, bf16[2304,2304]{1,0:T(8,128)(2,1)} %get-tuple-element.573), kind=kOutput, calls=%fused_computation.31 | convolution fusion | flops 10925899776 | bytes 43646976 | tf_op jit(solution)/shard_map/dot_general | solution.py:26
  907.1 16.6 fusion.100
  927.9 18.2 %add_convert_fusion.5 = bf16[1024,2304]{1,0:T(8,128)(2,1)} fusion(f32[1024,2304]{1,0:T(8,128)} %fusion.100, bf16[1024,2304]{1,0:T(8,128)(2,1)S(1)} %copy-done.125, bf16[2304,2304]{1,0:T(8,128)(2,1)} %get-tuple-element.564), kind=kOutput, calls=%fused_computation.30 | convolution fusion | flops 10876354560 | bytes 29491200 | tf_op jit(solution)/shard_map/dot_general | solution.py:26
  972.4 18.5 %fusion.101 = f32[2304,2304]{1,0:T(8,128)} fusion(bf16[1024,2304]{1,0:T(8,128)(2,1)} %get-tuple-element.624, bf16[1024,2304]{1,0:T(8,128)(2,1)} %copy-done.94), kind=kOutput, calls=%fused_computation.366 | convolution fusion | flops 10871635968 | bytes 30670848 | tf_op jit(solution)/shard_map/dot_general | solution.py:26
  993.5 13.8 add_convert_fusion.2
  1059.7 17.4 attn_backward.2
  1089.3 17.6 %attn_backward.3 = (bf16[1024,512]{1,0:T(8,128)(2,1)}, bf16[4,256,512]{2,1,0:T(8,128)(2,1)}, bf16[4,256,512]{2,1,0:T(8,128)(2,1)}) custom-call(s32[1]{0:T(128)} %bitcast.43.info, bf16[1024,512]{1,0:T(8,128)(2,1)} %bitcast.325, bf16[1024,512]{1,0:T(8,128)(2,1)} %bitcast.88.grad_ref, f32[1024,512]{1,0:T(8,128)} %get-tuple-element.655.exact_ref, ...), custom_call_target="tpu_custom_call" | custom-call | flops 10737418240 | bytes 9437184 | tf_op jit(solution)/shard_map/attn_backward/pallas_call | solution.py:660
  1122.7 18.7 %fusion.102 = f32[2304,2304]{1,0:T(8,128)} fusion(bf16[1024,2304]{1,0:T(8,128)(2,1)} %get-tuple-element.666, bf16[1024,2304]{1,0:T(8,128)(2,1)} %constant_dynamic-update-slice_fusion.4), kind=kOutput, calls=%fused_computation.367 | convolution fusion | flops 10871635968 | bytes 30670848 | tf_op jit(solution)/shard_map/dot_general | solution.py:26
  1142.6 18.9 %collective-permute-done.69 = bf16[4,256,512]{2,1,0:T(8,128)(2,1)S(1)} collective-permute-done((bf16[4,256,512]{2,1,0:T(8,128)(2,1)}, bf16[4,256,512]{2,1,0:T(8,128)(2,1)S(1)}, u32[]{:S(2)}, u32[]{:S(2)}) %collective-permute-start.69) | collective-permute-done | bytes 1048608 | tf_op jit(solution)/shard_map/ppermute | solution.py:177
  1168.8 20.0 %add_convert_fusion.1 = bf16[2304,2304]{1,0:T(8,128)(2,1)} fusion(f32[2304,2304]{1,0:T(8,128)} %fusion.102, bf16[1024,2304]{1,0:T(8,128)(2,1)} %get-tuple-element.673, bf16[1024,2304]{1,0:T(8,128)(2,1)} %copy-done.93), kind=kOutput, calls=%fused_computation.1 | convolution fusion | flops 10882252800 | bytes 41287680 | tf_op jit(solution)/shard_map/dot_general | solution.py:26
  1217.5 15.3 all-to-all-done.11.refs_3_
  1232.8 12.8 turn_back.1
  1260.1 52.4 %collective-permute-done.74 = bf16[2304,512]{1,0:T(8,128)(2,1)} collective-permute-done((bf16[2304,512]{1,0:T(8,128)(2,1)}, bf16[2304,512]{1,0:T(8,128)(2,1)}, u32[]{:S(2)}, u32[]{:S(2)}) %collective-permute-start.74) | collective-permute-done | bytes 2359328 | tf_op jit(solution)/shard_map/ppermute | solution.py:157
  1317.5 19.0 %fusion.103 = f32[2304,2304]{1,0:T(8,128)} fusion(bf16[1024,2304]{1,0:T(8,128)(2,1)} %get-tuple-element.690, bf16[1024,2304]{1,0:T(8,128)(2,1)} %constant_dynamic-update-slice_fusion.4), kind=kOutput, calls=%fused_computation.368 | convolution fusion | flops 10871635968 | bytes 30670848 | tf_op jit(solution)/shard_map/dot_general | solution.py:26
  1349.6 26.5 %collective-permute-done.72 = bf16[288,2304]{1,0:T(8,128)(2,1)S(1)} collective-permute-done((bf16[288,2304]{1,0:T(8,128)(2,1)S(1)}, bf16[288,2304]{1,0:T(8,128)(2,1)S(1)}, u32[]{:S(2)}, u32[]{:S(2)}) %collective-permute-start.72) | collective-permute-done | bytes 1327136 | tf_op jit(solution)/shard_map/ppermute | solution.py:157
  1377.6 18.5 %fusion.104 = f32[2304,2304]{1,0:T(8,128)} fusion(bf16[1024,2304]{1,0:T(8,128)(2,1)} %get-tuple-element.698, bf16[1024,2304]{1,0:T(8,128)(2,1)} %copy-done.93), kind=kOutput, calls=%fused_computation.369 | convolution fusion | flops 10871635968 | bytes 30670848 | tf_op jit(solution)/shard_map/dot_general | solution.py:26
  1406.3 13.8 add_convert_fusion
  1431.7 21.5 %fusion.41 = (f32[2304]{0:T(1024)}, f32[256]{0:T(256)S(1)}, f32[256,2304]{1,0:T(8,128)}) fusion(f32[256]{0:T(256)S(1)} %copy-done.118, bf16[2,256,2304]{2,1,0:T(8,128)(2,1)S(1)} %copy-done.9, f32[2304]{0:T(1024)S(1)} %copy-done.99, bf16[256,4096]{1,0:T(8,128)(2,1)} %get-tuple-element.705, bf16[2304,4096]{1,0:T(8,128)(2,1)} %get-tuple-element.419.wq_ref.wk_ref.wv_ref), kind=kOutput, calls=%fused_computation.116 | convolution fusion | flops 4835964928 | bytes 24530944 | tf_op jit(solution)/shard_map/dot_general | solution.py:26
  1482.6 21.3 %fusion.49 = (f32[2304]{0:T(1024)}, f32[256]{0:T(256)}, f32[256,2304]{1,0:T(8,128)}) fusion(f32[256]{0:T(256)S(1)} %copy-done.116, bf16[2,256,2304]{2,1,0:T(8,128)(2,1)S(1)} %copy-done.9, f32[2304]{0:T(1024)S(1)} %copy-done.99, bf16[256,4096]{1,0:T(8,128)(2,1)} %get-tuple-element.714, bf16[2304,4096]{1,0:T(8,128)(2,1)} %get-tuple-element.422.wq_ref.wk_ref.wv_ref), kind=kOutput, calls=%fused_computation.124 | convolution fusion | flops 4835964928 | bytes 24530944 | tf_op jit(solution)/shard_map/dot_general | solution.py:26
  1518.5 22.0 %collective-permute-done.86 = bf16[2,288,2304]{2,1,0:T(8,128)(2,1)} collective-permute-done((bf16[2,288,2304]{2,1,0:T(8,128)(2,1)}, bf16[2,288,2304]{2,1,0:T(8,128)(2,1)}, u32[]{:S(2)}, u32[]{:S(2)}) %collective-permute-start.86) | collective-permute-done | bytes 2654240 | tf_op jit(solution)/shard_map/ppermute | solution.py:157
  1566.1 23.3 %collective-permute-done.93 = f32[4,2304]{1,0:T(4,128)S(1)} collective-permute-done((f32[4,2304]{1,0:T(4,128)S(1)}, f32[4,2304]{1,0:T(4,128)S(1)}, u32[]{:S(2)}, u32[]{:S(2)}) %collective-permute-start.93) | collective-permute-done | bytes 36896 | tf_op jit(solution)/shard_map/ppermute | solution.py:157
  1590.2 33.4 %collective-permute-done.89 = bf16[288,2304]{1,0:T(8,128)(2,1)S(1)} collective-permute-done((bf16[288,2304]{1,0:T(8,128)(2,1)S(1)}, bf16[288,2304]{1,0:T(8,128)(2,1)S(1)}, u32[]{:S(2)}, u32[]{:S(2)}) %collective-permute-start.89) | collective-permute-done | bytes 1327136 | tf_op jit(solution)/shard_map/ppermute | solution.py:157
  1629.6 26.0 %collective-permute-done.95 = bf16[288,2304]{1,0:T(8,128)(2,1)S(1)} collective-permute-done((bf16[288,2304]{1,0:T(8,128)(2,1)S(1)}, bf16[288,2304]{1,0:T(8,128)(2,1)S(1)}, u32[]{:S(2)}, u32[]{:S(2)}) %collective-permute-start.95) | collective-permute-done | bytes 1327136 | tf_op jit(solution)/shard_map/ppermute | solution.py:157
  1670.3 19.0 %collective-permute-done.94 = bf16[288,2304]{1,0:T(8,128)(2,1)} collective-permute-done((bf16[288,2304]{1,0:T(8,128)(2,1)}, bf16[288,2304]{1,0:T(8,128)(2,1)}, u32[]{:S(2)}, u32[]{:S(2)}) %collective-permute-start.94) | collective-permute-done | bytes 1327136 | tf_op jit(solution)/shard_map/ppermute | solution.py:157
  1691.8 30.8 %collective-permute-done.98 = bf16[288,2304]{1,0:T(8,128)(2,1)S(1)} collective-permute-done((bf16[288,2304]{1,0:T(8,128)(2,1)S(1)}, bf16[288,2304]{1,0:T(8,128)(2,1)S(1)}, u32[]{:S(2)}, u32[]{:S(2)}) %collective-permute-start.98) | collective-permute-done | bytes 1327136 | tf_op jit(solution)/shard_map/ppermute | solution.py:157
  (757 shorter events, 695.5 us)
Async XLA Ops:
  3.8 37.0 %collective-permute-start = (bf16[288,2560]{1,0:T(8,128)(2,1)S(1)}, bf16[288,2560]{1,0:T(8,128)(2,1)}, u32[]{:S(2)}, u32[]{:S(2)}) collective-permute-start(bf16[288,2560]{1,0:T(8,128)(2,1)S(1)} %pad_maximum_fusion.10.refs_0_), channel_id=1, source_target_pairs={{0,8},{8,16},{16,24},{24,28},{28,20},{20,12},{12,4},{4,0},{1,9},{9... | collective-permute-start | bytes 4423688 | tf_op jit(solution)/shard_map/ppermute | solution.py:102
  6.9 34.0 %collective-permute-start.1 = (bf16[288,2560]{1,0:T(8,128)(2,1)S(1)}, bf16[288,2560]{1,0:T(8,128)(2,1)}, u32[]{:S(2)}, u32[]{:S(2)}) collective-permute-start(bf16[288,2560]{1,0:T(8,128)(2,1)S(1)} %pad_maximum_fusion.10.refs_0_), channel_id=1, source_target_pairs={{8,0},{16,8},{24,16},{28,24},{20,28},{12,20},{4,12},{0,4},{9,1},{1... | collective-permute-start | bytes 4423688 | tf_op jit(solution)/shard_map/ppermute | solution.py:102
  6.9 34.0 %collective-permute-start.2 = (bf16[288,2560]{1,0:T(8,128)(2,1)S(1)}, bf16[288,2560]{1,0:T(8,128)(2,1)S(1)}, u32[]{:S(2)}, u32[]{:S(2)}) collective-permute-start(bf16[288,2560]{1,0:T(8,128)(2,1)S(1)} %pad_maximum_fusion.10.refs_0_), channel_id=1, source_target_pairs={{0,1},{1,0},{2,3},{3,2},{4,5},{5,4},{6,7},{7,6},{8,9},{9,8},{10,11... | collective-permute-start | bytes 4423688 | tf_op jit(solution)/shard_map/ppermute | solution.py:157
  40.9 35.1 %collective-permute-start.3 = (bf16[288,2560]{1,0:T(8,128)(2,1)}, bf16[288,2560]{1,0:T(8,128)(2,1)}, u32[]{:S(2)}, u32[]{:S(2)}) collective-permute-start(bf16[288,2560]{1,0:T(8,128)(2,1)} %collective-permute-done.refs_2_), channel_id=1, source_target_pairs={{0,8},{8,16},{16,24},{24,28},{28,20},{20,12},{12,4},{4,0},{1,9},{9... | collective-permute-start | bytes 4423688 | tf_op jit(solution)/shard_map/ppermute | solution.py:102
  43.0 35.0 %collective-permute-start.5 = (bf16[288,2560]{1,0:T(8,128)(2,1)}, bf16[288,2560]{1,0:T(8,128)(2,1)S(1)}, u32[]{:S(2)}, u32[]{:S(2)}) collective-permute-start(bf16[288,2560]{1,0:T(8,128)(2,1)} %collective-permute-done.refs_2_), channel_id=1, source_target_pairs={{0,1},{1,0},{2,3},{3,2},{4,5},{5,4},{6,7},{7,6},{8,9},{9,8},{10,11... | collective-permute-start | bytes 4423688 | tf_op jit(solution)/shard_map/ppermute | solution.py:157
  43.0 35.0 %collective-permute-start.4 = (bf16[288,2560]{1,0:T(8,128)(2,1)}, bf16[288,2560]{1,0:T(8,128)(2,1)}, u32[]{:S(2)}, u32[]{:S(2)}) collective-permute-start(bf16[288,2560]{1,0:T(8,128)(2,1)} %collective-permute-done.1.refs_4_), channel_id=1, source_target_pairs={{8,0},{16,8},{24,16},{28,24},{20,28},{12,20},{4,12},{0,4},{9,1},{1... | collective-permute-start | bytes 4423688 | tf_op jit(solution)/shard_map/ppermute | solution.py:102
  43.3 34.7 %collective-permute-start.6 = (bf16[288,2560]{1,0:T(8,128)(2,1)}, bf16[288,2560]{1,0:T(8,128)(2,1)S(1)}, u32[]{:S(2)}, u32[]{:S(2)}) collective-permute-start(bf16[288,2560]{1,0:T(8,128)(2,1)} %collective-permute-done.1.refs_4_), channel_id=1, source_target_pairs={{0,1},{1,0},{2,3},{3,2},{4,5},{5,4},{6,7},{7,6},{8,9},{9,8},{10,11... | collective-permute-start | bytes 4423688 | tf_op jit(solution)/shard_map/ppermute | solution.py:157
  79.1 34.1 %collective-permute-start.7 = (bf16[288,2560]{1,0:T(8,128)(2,1)}, bf16[288,2560]{1,0:T(8,128)(2,1)S(1)}, u32[]{:S(2)}, u32[]{:S(2)}) collective-permute-start(bf16[288,2560]{1,0:T(8,128)(2,1)} %collective-permute-done.3.refs_0_), channel_id=1, source_target_pairs={{0,8},{8,16},{16,24},{24,28},{28,20},{20,12},{12,4},{4,0},{1,9},{9... | collective-permute-start | bytes 4423688 | tf_op jit(solution)/shard_map/ppermute | solution.py:102
  80.7 33.8 %collective-permute-start.8 = (bf16[288,2560]{1,0:T(8,128)(2,1)}, bf16[288,2560]{1,0:T(8,128)(2,1)S(1)}, u32[]{:S(2)}, u32[]{:S(2)}) collective-permute-start(bf16[288,2560]{1,0:T(8,128)(2,1)} %collective-permute-done.4.refs_2_), channel_id=1, source_target_pairs={{8,0},{16,8},{24,16},{28,24},{20,28},{12,20},{4,12},{0,4},{9,1},{1... | collective-permute-start | bytes 4423688 | tf_op jit(solution)/shard_map/ppermute | solution.py:102
  81.1 33.3 %collective-permute-start.9 = (bf16[288,2560]{1,0:T(8,128)(2,1)}, bf16[288,2560]{1,0:T(8,128)(2,1)}, u32[]{:S(2)}, u32[]{:S(2)}) collective-permute-start(bf16[288,2560]{1,0:T(8,128)(2,1)} %collective-permute-done.3.refs_0_), channel_id=1, source_target_pairs={{0,1},{1,0},{2,3},{3,2},{4,5},{5,4},{6,7},{7,6},{8,9},{9,8},{10,11... | collective-permute-start | bytes 4423688 | tf_op jit(solution)/shard_map/ppermute | solution.py:157
  152.9 62.0 %collective-permute-start.17 = (bf16[8,288,512]{2,1,0:T(8,128)(2,1)}, bf16[8,288,512]{2,1,0:T(8,128)(2,1)}, u32[]{:S(2)}, u32[]{:S(2)}) collective-permute-start(bf16[8,288,512]{2,1,0:T(8,128)(2,1)} %bitcast_dynamic-update-slice_fusion.7.refs_0_), channel_id=1, source_target_pairs={{0,2},{1,3},{2,0},{3,1},{4,6},{5,7},{6,4},{7,5},{8,10},{9,11},{10,... | collective-permute-start | bytes 7077896 | tf_op jit(solution)/shard_map/ppermute | solution.py:157
  154.1 60.8 %collective-permute-start.15 = (bf16[288,2304]{1,0:T(8,128)(2,1)}, bf16[288,2304]{1,0:T(8,128)(2,1)S(1)}, u32[]{:S(2)}, u32[]{:S(2)}) collective-permute-start(bf16[288,2304]{1,0:T(8,128)(2,1)} %get-tuple-element.410), channel_id=1, source_target_pairs={{0,16},{4,20},{8,24},{12,28},{16,0},{20,4},{24,8},{28,12},{1,17},{... | collective-permute-start | bytes 3981320 | tf_op jit(solution)/shard_map/ppermute | solution.py:157
  215.9 31.2 %collective-permute-start.18 = (bf16[8,288,512]{2,1,0:T(8,128)(2,1)}, bf16[8,288,512]{2,1,0:T(8,128)(2,1)}, u32[]{:S(2)}, u32[]{:S(2)}) collective-permute-start(bf16[8,288,512]{2,1,0:T(8,128)(2,1)} %collective-permute-done.17.refs_1_), channel_id=1, source_target_pairs={{0,1},{1,0},{2,3},{3,2},{4,5},{5,4},{6,7},{7,6},{8,9},{9,8},{10,11... | collective-permute-start | bytes 7077896 | tf_op jit(solution)/shard_map/ppermute | solution.py:157
  248.1 34.7 %all-to-all-start.1 = ((bf16[4,256,512]{2,1,0:T(8,128)(2,1)}), bf16[4,256,512]{2,1,0:T(8,128)(2,1)S(1)}, u32[]{:S(2)}, u32[]{:S(2)}) async-start(bf16[4,256,512]{2,1,0:T(8,128)(2,1)} %get-tuple-element.441), calls=%async_computation.1 | async-start | bytes 2097152 | tf_op jit(solution)/shard_map/all_to_all | solution.py:168
  251.6 31.1 %collective-permute-start.20 = (bf16[288,2304]{1,0:T(8,128)(2,1)}, bf16[288,2304]{1,0:T(8,128)(2,1)}, u32[]{:S(2)}, u32[]{:S(2)}) collective-permute-start(bf16[288,2304]{1,0:T(8,128)(2,1)} %copy-done.67), channel_id=1, source_target_pairs={{0,2},{1,3},{2,0},{3,1},{4,6},{5,7},{6,4},{7,5},{8,10},{9,11},{10,... | collective-permute-start | bytes 3981320 | tf_op jit(solution)/shard_map/ppermute | solution.py:157
  313.4 30.8 %all-to-all-start.3 = ((bf16[8,128,512]{2,1,0:T(8,128)(2,1)}), bf16[8,128,512]{2,1,0:T(8,128)(2,1)S(1)}, u32[]{:S(2)}, u32[]{:S(2)}) async-start(bf16[8,128,512]{2,1,0:T(8,128)(2,1)} %bitcast.328), calls=%async_computation.3 | async-start | bytes 2097152 | tf_op jit(solution)/shard_map/all_to_all | solution.py:161
  374.1 30.7 %all-to-all-start.5 = ((bf16[8,128,512]{2,1,0:T(8,128)(2,1)}), bf16[8,128,512]{2,1,0:T(8,128)(2,1)S(1)}, u32[]{:S(2)}, u32[]{:S(2)}) async-start(bf16[8,128,512]{2,1,0:T(8,128)(2,1)} %bitcast.332), calls=%async_computation.5 | async-start | bytes 2097152 | tf_op jit(solution)/shard_map/all_to_all | solution.py:161
  413.1 58.1 %collective-permute-start.25 = (bf16[288,2304]{1,0:T(8,128)(2,1)S(1)}, bf16[288,2304]{1,0:T(8,128)(2,1)S(1)}, u32[]{:S(2)}, u32[]{:S(2)}) collective-permute-start(bf16[288,2304]{1,0:T(8,128)(2,1)S(1)} %copy-done.66), channel_id=1, source_target_pairs={{0,16},{4,20},{8,24},{12,28},{16,0},{20,4},{24,8},{28,12},{1,17},{... | collective-permute-start | bytes 3981320 | tf_op jit(solution)/shard_map/ppermute | solution.py:157
  471.2 31.0 %collective-permute-start.27 = (bf16[288,2304]{1,0:T(8,128)(2,1)S(1)}, bf16[288,2304]{1,0:T(8,128)(2,1)S(1)}, u32[]{:S(2)}, u32[]{:S(2)}) collective-permute-start(bf16[288,2304]{1,0:T(8,128)(2,1)S(1)} %collective-permute-done.25.refs_0_), channel_id=1, source_target_pairs={{0,2},{1,3},{2,0},{3,1},{4,6},{5,7},{6,4},{7,5},{8,10},{9,11},{10,... | collective-permute-start | bytes 3981320 | tf_op jit(solution)/shard_map/ppermute | solution.py:157
  472.1 59.2 %collective-permute-start.26 = (bf16[288,2304]{1,0:T(8,128)(2,1)S(1)}, bf16[288,2304]{1,0:T(8,128)(2,1)}, u32[]{:S(2)}, u32[]{:S(2)}) collective-permute-start(bf16[288,2304]{1,0:T(8,128)(2,1)S(1)} %copy-done.65), channel_id=1, source_target_pairs={{0,16},{4,20},{8,24},{12,28},{16,0},{20,4},{24,8},{28,12},{1,17},{... | collective-permute-start | bytes 3981320 | tf_op jit(solution)/shard_map/ppermute | solution.py:157
  531.2 31.4 %collective-permute-start.32 = (bf16[288,2304]{1,0:T(8,128)(2,1)}, bf16[288,2304]{1,0:T(8,128)(2,1)}, u32[]{:S(2)}, u32[]{:S(2)}) collective-permute-start(bf16[288,2304]{1,0:T(8,128)(2,1)} %collective-permute-done.26.refs_0_), channel_id=1, source_target_pairs={{0,2},{1,3},{2,0},{3,1},{4,6},{5,7},{6,4},{7,5},{8,10},{9,11},{10,... | collective-permute-start | bytes 3981320 | tf_op jit(solution)/shard_map/ppermute | solution.py:157
  532.4 30.8 %collective-permute-start.30 = (bf16[288,2304]{1,0:T(8,128)(2,1)S(1)}, bf16[288,2304]{1,0:T(8,128)(2,1)S(1)}, u32[]{:S(2)}, u32[]{:S(2)}) collective-permute-start(bf16[288,2304]{1,0:T(8,128)(2,1)S(1)} %collective-permute-done.25.refs_0_), channel_id=1, source_target_pairs={{0,1},{1,0},{2,3},{3,2},{4,5},{5,4},{6,7},{7,6},{8,9},{9,8},{10,11... | collective-permute-start | bytes 3981320 | tf_op jit(solution)/shard_map/ppermute | solution.py:157
  532.4 30.8 %collective-permute-start.31 = (bf16[288,2304]{1,0:T(8,128)(2,1)S(1)}, bf16[288,2304]{1,0:T(8,128)(2,1)S(1)}, u32[]{:S(2)}, u32[]{:S(2)}) collective-permute-start(bf16[288,2304]{1,0:T(8,128)(2,1)S(1)} %collective-permute-done.27.refs_1_), channel_id=1, source_target_pairs={{0,1},{1,0},{2,3},{3,2},{4,5},{5,4},{6,7},{7,6},{8,9},{9,8},{10,11... | collective-permute-start | bytes 3981320 | tf_op jit(solution)/shard_map/ppermute | solution.py:157
  1017.3 31.1 %all-to-all-start.6 = ((bf16[8,128,512]{2,1,0:T(8,128)(2,1)}), bf16[8,128,512]{2,1,0:T(8,128)(2,1)}, u32[]{:S(2)}, u32[]{:S(2)}) async-start(bf16[8,128,512]{2,1,0:T(8,128)(2,1)} %bitcast.315), calls=%async_computation.6 | async-start | bytes 2097152 | tf_op jit(solution)/shard_map/all_to_all | solution.py:161
  1082.1 106.7 %collective-permute-start.70 = (bf16[2,288,2304]{2,1,0:T(8,128)(2,1)}, bf16[2,288,2304]{2,1,0:T(8,128)(2,1)}, u32[]{:S(2)}, u32[]{:S(2)}) collective-permute-start(bf16[2,288,2304]{2,1,0:T(8,128)(2,1)} %slice_bitcast_fusion.11), channel_id=1, source_target_pairs={{0,2},{1,3},{2,0},{3,1},{4,6},{5,7},{6,4},{7,5},{8,10},{9,11},{10,... | collective-permute-start | bytes 7962632 | tf_op jit(solution)/shard_map/ppermute | solution.py:157
  1116.5 46.4 %all-to-all-start.9 = ((bf16[8,128,512]{2,1,0:T(8,128)(2,1)}), bf16[8,128,512]{2,1,0:T(8,128)(2,1)S(1)}, u32[]{:S(2)}, u32[]{:S(2)}) async-start(bf16[8,128,512]{2,1,0:T(8,128)(2,1)} %bitcast.330), calls=%async_computation.9 | async-start | bytes 2097152 | tf_op jit(solution)/shard_map/all_to_all | solution.py:161
  1120.7 40.8 %collective-permute-start.69 = (bf16[4,256,512]{2,1,0:T(8,128)(2,1)}, bf16[4,256,512]{2,1,0:T(8,128)(2,1)S(1)}, u32[]{:S(2)}, u32[]{:S(2)}) collective-permute-start(bf16[4,256,512]{2,1,0:T(8,128)(2,1)} %get-tuple-element.671), channel_id=1, source_target_pairs={{0,4},{4,0},{8,12},{12,8},{16,20},{20,16},{24,28},{28,24},{1,5},{5... | collective-permute-start | bytes 3145736 | tf_op jit(solution)/shard_map/ppermute | solution.py:177
  1202.2 30.6 %all-to-all-start.11 = ((bf16[4,256,512]{2,1,0:T(8,128)(2,1)}), bf16[4,256,512]{2,1,0:T(8,128)(2,1)}, u32[]{:S(2)}, u32[]{:S(2)}) async-start(bf16[4,256,512]{2,1,0:T(8,128)(2,1)} %add_convert_fusion.17), calls=%async_computation.11 | async-start | bytes 2097152 | tf_op jit(solution)/shard_map/all_to_all | solution.py:168
  1255.2 83.7 %collective-permute-start.73 = (bf16[2304,2048]{1,0:T(8,128)(2,1)}, bf16[2304,2048]{1,0:T(8,128)(2,1)}, u32[]{:S(2)}, u32[]{:S(2)}) collective-permute-start(bf16[2304,2048]{1,0:T(8,128)(2,1)} %convolution_convert_fusion), channel_id=1, source_target_pairs={{0,1},{1,0},{2,3},{3,2},{4,5},{5,4},{6,7},{7,6},{8,9},{9,8},{10,11... | collective-permute-start | bytes 28311560 | tf_op jit(solution)/shard_map/ppermute | solution.py:157
  1258.4 54.0 %collective-permute-start.74 = (bf16[2304,512]{1,0:T(8,128)(2,1)}, bf16[2304,512]{1,0:T(8,128)(2,1)}, u32[]{:S(2)}, u32[]{:S(2)}) collective-permute-start(bf16[2304,512]{1,0:T(8,128)(2,1)} %constant_dynamic-slice_fusion.16), channel_id=1, source_target_pairs={{0,2},{1,3},{2,0},{3,1},{4,6},{5,7},{6,4},{7,5},{8,10},{9,11},{10,... | collective-permute-start | bytes 7077896 | tf_op jit(solution)/shard_map/ppermute | solution.py:157
  1315.7 60.5 %collective-permute-start.75 = (bf16[2,288,2304]{2,1,0:T(8,128)(2,1)S(1)}, bf16[2,288,2304]{2,1,0:T(8,128)(2,1)S(1)}, u32[]{:S(2)}, u32[]{:S(2)}) collective-permute-start(bf16[2,288,2304]{2,1,0:T(8,128)(2,1)S(1)} %slice_bitcast_fusion.9), channel_id=1, source_target_pairs={{0,2},{1,3},{2,0},{3,1},{4,6},{5,7},{6,4},{7,5},{8,10},{9,11},{10,... | collective-permute-start | bytes 7962632 | tf_op jit(solution)/shard_map/ppermute | solution.py:157
  1317.4 58.7 %collective-permute-start.72 = (bf16[288,2304]{1,0:T(8,128)(2,1)S(1)}, bf16[288,2304]{1,0:T(8,128)(2,1)S(1)}, u32[]{:S(2)}, u32[]{:S(2)}) collective-permute-start(bf16[288,2304]{1,0:T(8,128)(2,1)S(1)} %slice_bitcast_fusion.19), channel_id=1, source_target_pairs={{0,16},{4,20},{8,24},{12,28},{16,0},{20,4},{24,8},{28,12},{1,17},{... | collective-permute-start | bytes 3981320 | tf_op jit(solution)/shard_map/ppermute | solution.py:157
  1426.3 39.7 %collective-permute-start.80 = (bf16[2,576,2304]{2,1,0:T(8,128)(2,1)}, bf16[2,576,2304]{2,1,0:T(8,128)(2,1)}, u32[]{:S(2)}, u32[]{:S(2)}) collective-permute-start(bf16[2,576,2304]{2,1,0:T(8,128)(2,1)} %slice_bitcast_fusion), channel_id=1, source_target_pairs={{0,1},{1,0},{2,3},{3,2},{4,5},{5,4},{6,7},{7,6},{8,9},{9,8},{10,11... | collective-permute-start | bytes 15925256 | tf_op jit(solution)/shard_map/ppermute | solution.py:157
  1427.7 43.7 %collective-permute-start.79 = (bf16[288,2560]{1,0:T(8,128)(2,1)}, bf16[288,2560]{1,0:T(8,128)(2,1)}, u32[]{:S(2)}, u32[]{:S(2)}) collective-permute-start(bf16[288,2560]{1,0:T(8,128)(2,1)} %pad_maximum_fusion.12), channel_id=1, source_target_pairs={{8,0},{16,8},{24,16},{28,24},{20,28},{12,20},{4,12},{0,4},{9,1},{1... | collective-permute-start | bytes 4423688 | tf_op jit(solution)/shard_map/ppermute | solution.py:102
  1430.8 40.6 %collective-permute-start.78 = (bf16[288,2560]{1,0:T(8,128)(2,1)}, bf16[288,2560]{1,0:T(8,128)(2,1)}, u32[]{:S(2)}, u32[]{:S(2)}) collective-permute-start(bf16[288,2560]{1,0:T(8,128)(2,1)} %fusion.57), channel_id=1, source_target_pairs={{0,8},{8,16},{16,24},{24,28},{28,20},{20,12},{12,4},{4,0},{1,9},{9... | collective-permute-start | bytes 4423688 | tf_op jit(solution)/shard_map/ppermute | solution.py:102
  1431.2 31.3 %collective-permute-start.83 = (bf16[288,2304]{1,0:T(8,128)(2,1)}, bf16[288,2304]{1,0:T(8,128)(2,1)}, u32[]{:S(2)}, u32[]{:S(2)}) collective-permute-start(bf16[288,2304]{1,0:T(8,128)(2,1)} %fusion.27), channel_id=1, source_target_pairs={{0,2},{1,3},{2,0},{3,1},{4,6},{5,7},{6,4},{7,5},{8,10},{9,11},{10,... | collective-permute-start | bytes 3981320 | tf_op jit(solution)/shard_map/ppermute | solution.py:157
  1474.5 34.2 %collective-permute-start.82 = (bf16[288,2560]{1,0:T(8,128)(2,1)}, bf16[288,2560]{1,0:T(8,128)(2,1)}, u32[]{:S(2)}, u32[]{:S(2)}) collective-permute-start(bf16[288,2560]{1,0:T(8,128)(2,1)} %add_convert_fusion.12), channel_id=1, source_target_pairs={{8,0},{16,8},{24,16},{28,24},{20,28},{12,20},{4,12},{0,4},{9,1},{1... | collective-permute-start | bytes 4423688 | tf_op jit(solution)/shard_map/ppermute | solution.py:102
  1479.0 33.3 %collective-permute-start.81 = (bf16[288,2560]{1,0:T(8,128)(2,1)}, bf16[288,2560]{1,0:T(8,128)(2,1)}, u32[]{:S(2)}, u32[]{:S(2)}) collective-permute-start(bf16[288,2560]{1,0:T(8,128)(2,1)} %add_convert_fusion.13), channel_id=1, source_target_pairs={{0,8},{8,16},{16,24},{24,28},{28,20},{20,12},{12,4},{4,0},{1,9},{9... | collective-permute-start | bytes 4423688 | tf_op jit(solution)/shard_map/ppermute | solution.py:102
  1482.1 58.3 %collective-permute-start.86 = (bf16[2,288,2304]{2,1,0:T(8,128)(2,1)}, bf16[2,288,2304]{2,1,0:T(8,128)(2,1)}, u32[]{:S(2)}, u32[]{:S(2)}) collective-permute-start(bf16[2,288,2304]{2,1,0:T(8,128)(2,1)} %get-tuple-element.719), channel_id=1, source_target_pairs={{0,2},{1,3},{2,0},{3,1},{4,6},{5,7},{6,4},{7,5},{8,10},{9,11},{10,... | collective-permute-start | bytes 7962632 | tf_op jit(solution)/shard_map/ppermute | solution.py:157
  1514.2 32.2 %collective-permute-start.85 = (bf16[288,2560]{1,0:T(8,128)(2,1)S(1)}, bf16[288,2560]{1,0:T(8,128)(2,1)}, u32[]{:S(2)}, u32[]{:S(2)}) collective-permute-start(bf16[288,2560]{1,0:T(8,128)(2,1)S(1)} %add_convert_fusion.10), channel_id=1, source_target_pairs={{8,0},{16,8},{24,16},{28,24},{20,28},{12,20},{4,12},{0,4},{9,1},{1... | collective-permute-start | bytes 4423688 | tf_op jit(solution)/shard_map/ppermute | solution.py:102
  1517.0 32.0 %collective-permute-start.84 = (bf16[288,2560]{1,0:T(8,128)(2,1)S(1)}, bf16[288,2560]{1,0:T(8,128)(2,1)}, u32[]{:S(2)}, u32[]{:S(2)}) collective-permute-start(bf16[288,2560]{1,0:T(8,128)(2,1)S(1)} %add_convert_fusion.11), channel_id=1, source_target_pairs={{0,8},{8,16},{16,24},{24,28},{28,20},{20,12},{12,4},{4,0},{1,9},{9... | collective-permute-start | bytes 4423688 | tf_op jit(solution)/shard_map/ppermute | solution.py:102
  1562.7 60.9 %collective-permute-start.89 = (bf16[288,2304]{1,0:T(8,128)(2,1)S(1)}, bf16[288,2304]{1,0:T(8,128)(2,1)S(1)}, u32[]{:S(2)}, u32[]{:S(2)}) collective-permute-start(bf16[288,2304]{1,0:T(8,128)(2,1)S(1)} %slice_bitcast_fusion.14), channel_id=1, source_target_pairs={{0,16},{4,20},{8,24},{12,28},{16,0},{20,4},{24,8},{28,12},{1,17},{... | collective-permute-start | bytes 3981320 | tf_op jit(solution)/shard_map/ppermute | solution.py:157
  1623.6 32.1 %collective-permute-start.96 = (bf16[288,3072]{1,0:T(8,128)(2,1)S(1)}, bf16[288,3072]{1,0:T(8,128)(2,1)S(1)}, u32[]{:S(2)}, u32[]{:S(2)}) collective-permute-start(bf16[288,3072]{1,0:T(8,128)(2,1)S(1)} %pad_maximum_fusion.9), channel_id=1, source_target_pairs={{0,1},{1,0},{2,3},{3,2},{4,5},{5,4},{6,7},{7,6},{8,9},{9,8},{10,11... | collective-permute-start | bytes 5308424 | tf_op jit(solution)/shard_map/ppermute | solution.py:157
  1624.0 31.6 %collective-permute-start.95 = (bf16[288,2304]{1,0:T(8,128)(2,1)S(1)}, bf16[288,2304]{1,0:T(8,128)(2,1)S(1)}, u32[]{:S(2)}, u32[]{:S(2)}) collective-permute-start(bf16[288,2304]{1,0:T(8,128)(2,1)S(1)} %fusion.26), channel_id=1, source_target_pairs={{0,2},{1,3},{2,0},{3,1},{4,6},{5,7},{6,4},{7,5},{8,10},{9,11},{10,... | collective-permute-start | bytes 3981320 | tf_op jit(solution)/shard_map/ppermute | solution.py:157
  1628.1 31.7 %collective-permute-start.97 = (bf16[576,2304]{1,0:T(8,128)(2,1)S(1)}, bf16[576,2304]{1,0:T(8,128)(2,1)S(1)}, u32[]{:S(2)}, u32[]{:S(2)}) collective-permute-start(bf16[576,2304]{1,0:T(8,128)(2,1)S(1)} %copy-done.24), channel_id=1, source_target_pairs={{0,1},{1,0},{2,3},{3,2},{4,5},{5,4},{6,7},{7,6},{8,9},{9,8},{10,11... | collective-permute-start | bytes 7962632 | tf_op jit(solution)/shard_map/ppermute | solution.py:157
  1629.6 59.8 %collective-permute-start.94 = (bf16[288,2304]{1,0:T(8,128)(2,1)}, bf16[288,2304]{1,0:T(8,128)(2,1)}, u32[]{:S(2)}, u32[]{:S(2)}) collective-permute-start(bf16[288,2304]{1,0:T(8,128)(2,1)} %slice_bitcast_fusion.15), channel_id=1, source_target_pairs={{0,16},{4,20},{8,24},{12,28},{16,0},{20,4},{24,8},{28,12},{1,17},{... | collective-permute-start | bytes 3981320 | tf_op jit(solution)/shard_map/ppermute | solution.py:157
  1689.3 33.4 %collective-permute-start.99 = (bf16[576,2304]{1,0:T(8,128)(2,1)S(1)}, bf16[576,2304]{1,0:T(8,128)(2,1)S(1)}, u32[]{:S(2)}, u32[]{:S(2)}) collective-permute-start(bf16[576,2304]{1,0:T(8,128)(2,1)S(1)} %pad_maximum_fusion.4), channel_id=1, source_target_pairs={{0,1},{1,0},{2,3},{3,2},{4,5},{5,4},{6,7},{7,6},{8,9},{9,8},{10,11... | collective-permute-start | bytes 7962632 | tf_op jit(solution)/shard_map/ppermute | solution.py:157
  1691.0 31.6 %collective-permute-start.98 = (bf16[288,2304]{1,0:T(8,128)(2,1)S(1)}, bf16[288,2304]{1,0:T(8,128)(2,1)S(1)}, u32[]{:S(2)}, u32[]{:S(2)}) collective-permute-start(bf16[288,2304]{1,0:T(8,128)(2,1)S(1)} %fusion.25), channel_id=1, source_target_pairs={{0,2},{1,3},{2,0},{3,1},{4,6},{5,7},{6,4},{7,5},{8,10},{9,11},{10,... | collective-permute-start | bytes 3981320 | tf_op jit(solution)/shard_map/ppermute | solution.py:157
  (213 other events, 3549.5 us)

commit v6 on v5

--- a/solution.py
+++ b/solution.py
@@ -377,6 +377,162 @@
         ),
         name="unpack",
     )(pieces, grad, *held)
+
+
+def tile_of(size):
+    return 256 if size % 256 == 0 else size
+
+
+def tiles_of(size, part):
+    tile = tile_of(size)
+    tiles = size // tile
+    first_part = (tiles + 1) // 2
+    if part is None or tiles == 1:
+        return tile, 0, tiles
+    return (tile, 0, first_part) if part == 0 else (tile, first_part, tiles - first_part)
+
+
+def whole_spec(shape):
+    return pl.BlockSpec(shape, lambda i: (0, 0))
+
+
+def column_spec(rows, tile, first=0):
+    return pl.BlockSpec((rows, tile), lambda i: (0, first + i))
+
+
+def row_spec(tile, cols, first=0):
+    return pl.BlockSpec((tile, cols), lambda i: (first + i, 0))
+
+
+def kernel_call(kernel, grid, in_specs, out_specs, out_shape, flops, moved, name, held=()):
+    inputs = len(in_specs)
+    return pl.pallas_call(
+        lambda *refs: kernel(*refs[:inputs], *refs[inputs + len(held) :]),
+        grid=(grid,),
+        in_specs=in_specs + [pl.BlockSpec(memory_space=pl.ANY)] * len(held),
+        out_specs=out_specs,
+        out_shape=out_shape,
+        input_output_aliases={inputs + i: i for i in range(len(held))},
+        compiler_params=pltpu.CompilerParams(vmem_limit_bytes=VMEM_LIMIT),
+        cost_estimate=pl.CostEstimate(flops=flops, bytes_accessed=moved, transcendentals=0),
+        name=name,
+    )
+
+
+def row_parts(rows):
+    part = 512 if rows % 512 == 0 else rows
+    return [slice(first, first + part) for first in range(0, rows, part)]
+
+
+def open_kernel(x_ref, wg_ref, wu_ref, gate_ref, up_ref, hidden_ref):
+    for part in row_parts(x_ref.shape[0]):
+        x = x_ref[part]
+        gate = dot(x, wg_ref[...], NT)
+        up = dot(x, wu_ref[...], NT)
+        gate_ref[part] = gate
+        up_ref[part] = up
+        hidden_ref[part] = (gate * (0.5 + 0.5 * gelu_parts(gate)) * up).astype(bf16)
+
+
+def open_forward(x, gate_weights, up_weights, part, held=()):
+    rows, depth = x.shape
+    hidden = gate_weights.shape[0]
+    tile, first, tiles = tiles_of(hidden, part)
+    if held and tiles * tile == hidden:
+        return list(held)
+    return kernel_call(
+        open_kernel,
+        tiles,
+        [whole_spec(x.shape)] + [row_spec(tile, depth, first)] * 2,
+        [column_spec(rows, tile, first)] * 3,
+        [jax.ShapeDtypeStruct((rows, hidden), t) for t in (f32, f32, bf16)],
+        4 * rows * depth * tile * tiles,
+        2 * rows * depth + tiles * tile * (4 * depth + 10 * rows),
+        "open_forward",
+        held,
+    )(x, gate_weights, up_weights, *held)
+
+
+def open_back_kernel(x_ref, wd_ref, gate_ref, up_ref, grad_gate_ref, grad_up_ref):
+    for part in row_parts(x_ref.shape[0]):
+        grad = dot(x_ref[part], wd_ref[...], NT)
+        gate = gate_ref[part]
+        square = gate * gate
+        bounded = jnp.tanh(gate * (gelu_coeff + (0.044715 * gelu_coeff) * square))
+        half = 0.5 + 0.5 * bounded
+        steep = (0.5 * gelu_coeff) + (1.5 * 0.044715 * gelu_coeff) * square
+        slope = half + gate * (1.0 - bounded * bounded) * steep
+        grad_gate_ref[part] = (grad * up_ref[part] * slope).astype(bf16)
+        grad_up_ref[part] = (grad * (gate * half)).astype(bf16)
+
+
+def open_back(x, down_weights, gate, up, part, held=()):
+    rows, depth = x.shape
+    hidden = down_weights.shape[0]
+    tile, first, tiles = tiles_of(hidden, part)
+    if held and tiles * tile == hidden:
+        return list(held)
+    return kernel_call(
+        open_back_kernel,
+        tiles,
+        [whole_spec(x.shape), row_spec(tile, depth, first)] + [column_spec(rows, tile, first)] * 2,
+        [column_spec(rows, tile, first)] * 2,
+        [jax.ShapeDtypeStruct((rows, hidden), bf16)] * 2,
+        2 * rows * depth * tile * tiles,
+        2 * rows * depth + tiles * tile * (2 * depth + 12 * rows),
+        "open_back",
+        held,
+    )(x, down_weights, gate, up, *held)
+
+
+def input_back_kernel(gate_ref, up_ref, wg_ref, wu_ref, out_ref):
+    out_ref[...] = (
+        dot(gate_ref[...], wg_ref[...], NN) + dot(up_ref[...], wu_ref[...], NN)
+    ).astype(bf16)
+
+
+def input_back(grad_gate, grad_up, gate_weights, up_weights, part, held=()):
+    rows, hidden = grad_gate.shape
+    depth = gate_weights.shape[1]
+    tile, first, tiles = tiles_of(depth, part)
+    if held and tiles * tile == depth:
+        return list(held)
+    return kernel_call(
+        input_back_kernel,
+        tiles,
+        [whole_spec(grad_gate.shape)] * 2 + [column_spec(hidden, tile, first)] * 2,
+        [column_spec(rows, tile, first)],
+        [jax.ShapeDtypeStruct((rows, depth), bf16)],
+        4 * rows * hidden * tile * tiles,
+        4 * rows * hidden + tiles * tile * (4 * hidden + 2 * rows),
+        "input_back",
+        held,
+    )(grad_gate, grad_up, gate_weights, up_weights, *held)
+
+
+def weight_kernel(*refs, count):
+    out_ref = refs[-1]
+    total = dot(refs[0][...], refs[count][...], TN)
+    for s in range(1, count):
+        total = total + dot(refs[s][...], refs[count + s][...], TN)
+    out_ref[...] = total.astype(bf16)
+
+
+def weight_back(lefts, rights):
+    count = len(lefts)
+    rows, hidden = lefts[0].shape
+    depth = rights[0].shape[1]
+    tile = tile_of(hidden)
+    return kernel_call(
+        functools.partial(weight_kernel, count=count),
+        hidden // tile,
+        [column_spec(rows, tile)] * count + [whole_spec((rows, depth))] * count,
+        row_spec(tile, depth),
+        jax.ShapeDtypeStruct((hidden, depth), bf16),
+        2 * count * rows * depth * hidden,
+        2 * count * rows * (hidden + depth) + 2 * hidden * depth,
+        "weight_back",
+    )(*lefts, *rights)
 
 
 def turn(values, cosine, sine):
@@ -923,17 +1079,14 @@
 
     gathered, gate, up, hidden_rows, mixed, parts = [], [], [], [], [], []
 
-    def open_gate(s):
-        return dot(clock.hold(gathered[s]), gate_weights[s], NT)
-
-    def open_up(s):
-        up_s = dot(clock.hold(gathered[s]), up_weights[s], NT)
-        hidden_s = (0.5 * gate[s] * (1.0 + gelu_parts(gate[s])) * up_s).astype(bf16)
-        return [up_s, hidden_s]
-
-    def keep_up(work):
-        up.append(work[0])
-        hidden_rows.append(work[1])
+    def open_part(s, part, held=()):
+        group = clock.hold(gathered[s])
+        return open_forward(group, gate_weights[s], up_weights[s], part, held)
+
+    def keep_open(work):
+        gate.append(work[0])
+        up.append(work[1])
+        hidden_rows.append(work[2])
 
     def mix(s):
         return dot(clock.hold(hidden_rows[s]), down_weights[s], NN).astype(bf16)
@@ -969,9 +1122,9 @@
 
     def beside_second(step):
         if step == 0:
-            return [open_gate(0)] + list(partner_weights(2, [clock.hold(v) for v in down_held]))
+            return open_part(0, None)
         if step == 1:
-            return open_up(0)
+            return partner_weights(2, [clock.hold(v) for v in down_held])
         return ()
 
     a = b = clock.hold(normed_mlp[1])
@@ -983,10 +1136,9 @@
         a, b = hop(a, b, half_wide)
         a, b, *work = clock.sync(a, b, *work)
         if k == 1:
-            gate.append(work[0])
-            down_weights = work[1:]
+            keep_open(work)
         elif k == 2:
-            keep_up(work)
+            down_weights = work
         blocks += [a, b]
     gathered.append(jnp.concatenate(blocks, axis=0))
     parts.append(clock.sync(mix(0))[0])
@@ -1003,20 +1155,13 @@
 
     grad_group, grad_gate, grad_up, grad_parts, grad_normed_mlp = [], [], [], [], []
 
-    def back_hidden(s):
-        grad_hidden = dot(clock.hold(grad_group[s]), down_weights[s], NT)
-        bounded = gelu_parts(gate[s])
-        gelu_value = 0.5 * gate[s] * (1.0 + bounded)
-        slope = 0.5 * (1.0 + bounded) + 0.5 * gate[s] * (1.0 - bounded * bounded) * gelu_coeff * (
-            1.0 + 3.0 * 0.044715 * gate[s] * gate[s]
-        )
-        return [(grad_hidden * up[s] * slope).astype(bf16), (grad_hidden * gelu_value).astype(bf16)]
-
-    def back_input(s):
-        return (
-            dot(clock.hold(grad_gate[s]), gate_weights[s], NN)
-            + dot(grad_up[s], up_weights[s], NN)
-        ).astype(bf16)
+    def back_hidden(s, part, held=()):
+        group = clock.hold(grad_group[s])
+        return open_back(group, down_weights[s], gate[s], up[s], part, held)
+
+    def back_input(s, part, held=()):
+        grad = clock.hold(grad_gate[s])
+        return input_back(grad, grad_up[s], gate_weights[s], up_weights[s], part, held)
 
     def keep_back(work):
         grad_gate.append(work[0])
@@ -1042,43 +1187,44 @@
             other.append(work)
         return part_of(0).astype(f32) + a.astype(f32) + b.astype(f32), other
 
-    for s in seqs:
-        a, b = first_sum(parts[s])
-        if s + 1 < count:
-            a, b, value = clock.sync(a, b, open_gate(s + 1))
-            gate.append(value)
-        else:
-            a, b, *work = clock.sync(a, b, *back_hidden(0))
-            keep_back(work)
-
-        def beside(step, s=s):
-            if step:
-                return ()
-            return tuple(open_up(s + 1)) if s + 1 < count else (back_input(0),)
-
-        total, work = rest_sum(parts[s], a, b, beside)
-        if s + 1 < count:
-            keep_up(work[0])
-        else:
-            grad_parts.append(work[0][0])
-        mixed.append(total)
-        finish(s)
-        if s + 1 < count:
-            parts.append(mix(s + 1))
-        if s == 0:
-            blocks, work = ring_gather(
-                clock, grad_mixed[0], half_wide, lambda k: (parts[-1],) if k == 0 else ()
-            )
-            parts[-1] = work[0][0]
-            grad_group.append(jnp.concatenate(blocks, axis=0))
-
-    def weight_first(left, right):
-        return dot(clock.hold(left), right, TN)
-
-    def weight_rest(first, lefts, rights):
-        for s in seqs[1:]:
-            first = first + dot(clock.hold(lefts[s]), rights[s], TN)
-        return first.astype(bf16).reshape(2, hidden, model_dim)
+    a, b = first_sum(parts[0])
+    a, b, *opened = clock.sync(a, b, *open_part(1, 0))
+    total, work = rest_sum(
+        parts[0], a, b, lambda step: () if step else tuple(open_part(1, 1, opened))
+    )
+    keep_open(work[0])
+    mixed.append(total)
+    finish(0)
+    parts.append(mix(1))
+    blocks, work = ring_gather(
+        clock, grad_mixed[0], half_wide, lambda k: (parts[1],) if k == 0 else ()
+    )
+    parts[1] = work[0][0]
+    grad_group.append(jnp.concatenate(blocks, axis=0))
+    a, b = first_sum(parts[1])
+    a, b, *opened = clock.sync(a, b, *back_hidden(0, 0))
+
+    def beside_last(step):
+        if step:
+            return ()
+        keep_back(back_hidden(0, 1, opened))
+        return (grad_gate[0], grad_up[0], *input_back(
+            grad_gate[0], grad_up[0], gate_weights[0], up_weights[0], 0, ()
+        ))
+
+    total, work = rest_sum(parts[1], a, b, beside_last)
+    grad_gate[0], grad_up[0], opened = work[0][0], work[0][1], work[0][2:]
+    mixed.append(total)
+    finish(1)
+    blocks, work = ring_gather(
+        clock, grad_mixed[1], half_wide, lambda k: () if k else tuple(back_input(0, 1, opened))
+    )
+    grad_parts.append(work[0][0])
+    grad_group.append(jnp.concatenate(blocks, axis=0))
+
+    def weight_sum(lefts, rights):
+        lefts = [clock.hold(v) for v in lefts]
+        return weight_back(lefts, rights).reshape(2, hidden, model_dim)
 
     def part_sum(grad, bit):
         split = grad.reshape(2, 2, grad.shape[1] // 2, model_dim)
@@ -1104,38 +1250,32 @@
         grad_branch.append(work[1])
         grad_send.append(work[2])
 
-    for s in seqs[1:]:
-        blocks, work = ring_gather(
-            clock,
-            grad_mixed[s],
-            half_wide,
-            lambda k: (weight_first(hidden_rows[0], grad_group[0]),) if k == 0 and s == 1 else (),
-        )
-        if s == 1:
-            down_first = work[0][0]
-        grad_group.append(jnp.concatenate(blocks, axis=0))
-    for s in seqs:
-        a, b = first_sum(grad_parts[s])
-        if s + 1 < count:
-            a, b, *work = clock.sync(a, b, *back_hidden(s + 1))
-            keep_back(work)
-        else:
-            a, b, *work = clock.sync(a, b, *back_branch(s - 1))
-            keep_branch(work)
-
-        def beside(step, s=s):
-            if step:
-                return ()
-            if s + 1 < count:
-                return (back_input(s + 1),)
-            return (weight_rest(down_first, hidden_rows, grad_group),)
-
-        total, work = rest_sum(grad_parts[s], a, b, beside)
-        if s + 1 < count:
-            grad_parts.append(work[0][0])
-        else:
-            down_grad = work[0][0]
-        grad_normed_mlp.append(total)
+    a, b = first_sum(grad_parts[0])
+    a, b, *opened = clock.sync(a, b, *back_hidden(1, 0))
+
+    def beside_back(step):
+        if step:
+            return ()
+        keep_back(back_hidden(1, 1, opened))
+        return (grad_gate[1], grad_up[1], *input_back(
+            grad_gate[1], grad_up[1], gate_weights[1], up_weights[1], 0, ()
+        ))
+
+    total, work = rest_sum(grad_parts[0], a, b, beside_back)
+    grad_gate[1], grad_up[1], opened = work[0][0], work[0][1], work[0][2:]
+    grad_normed_mlp.append(total)
+    grad_parts += clock.sync(*back_input(1, 1, opened))
+    a, b = first_sum(grad_parts[1])
+    a, b, *work = clock.sync(a, b, *back_branch(0))
+    keep_branch(work)
+    total, work = rest_sum(
+        grad_parts[1],
+        a,
+        b,
+        lambda step: () if step else (weight_sum(hidden_rows, grad_group),),
+    )
+    down_grad = work[0][0]
+    grad_normed_mlp.append(total)
 
     def attend_back(s):
         dq, *dkv = attn_backward(
@@ -1199,14 +1339,17 @@
     out_part = low_sum(
         half_dot(all_branch, clock.hold(all_attended), side, half_out), out_sent
     )
-    query, pair_a, out_part, *work = clock.sync(query, pair_a, out_part, *attend_back(1))
+    query, pair_a, out_part, down_move, *work = clock.sync(
+        query, pair_a, out_part, down_move, *attend_back(1)
+    )
+    down_grad = far_end(down_keep, down_move)
     query_back.append(query)
     grad_attend.append(work)
     dq, *dkv = grad_attend[1]
     query = all_to_all(clock.hold(dq))
     pair_b = class_sum([clock.hold(v[1]) for v in parts_of_pair])
-    up_first = weight_first(grad_up[0], gathered[0])
-    query, pair_b, up_first = clock.sync(query, pair_b, up_first)
+    up_grad = weight_sum(grad_up, gathered)
+    query, pair_b, up_grad = clock.sync(query, pair_b, up_grad)
     query_back.append(query)
 
     out_pieces = {
@@ -1215,24 +1358,24 @@
         )
         for t in range(members)
     }
+    for bit in seq_bits[1:]:
+        for t in sorted(out_pieces):
+            if not t & (bit // 2) and t | (bit // 2) in out_pieces:
+                out_pieces[t] = low_sum(
+                    out_pieces[t], swap(out_pieces.pop(t | (bit // 2)), "seq", bit)
+                )
+    out_piece = out_pieces[0]
 
     pair = heads_all_to_all(clock.hold(jnp.concatenate([pair_a, pair_b], axis=0)))
-    pair_sum = class_sum(dkv)
-    up_grad = weight_rest(up_first, grad_up, gathered)
-    pair, pair_sum, up_grad, down_move = clock.sync(pair, pair_sum, up_grad, down_move)
-    pair_back.append(pair)
-    down_grad = far_end(down_keep, down_move)
-    for bit in seq_bits[1:]:
-        for t in range(members):
-            if not t & (bit // 2) and t in out_pieces and t | (bit // 2) in out_pieces:
-                out_pieces[t] = low_sum(
-                    out_pieces[t], swap(clock.hold(out_pieces.pop(t | (bit // 2))), "seq", bit)
-                )
-    pair = heads_all_to_all(clock.hold(pair_sum))
+    pair_sum = class_sum([clock.hold(v) for v in dkv])
     up_grad = part_sum(up_grad, 1)
-    pair, up_grad, down_grad = clock.sync(pair, up_grad, down_grad)
+    pair, pair_sum, up_grad, out_piece = clock.sync(pair, pair_sum, up_grad, out_piece)
     pair_back.append(pair)
     up_keep, up_move = far_start(up_grad)
+    pair = heads_all_to_all(clock.hold(pair_sum))
+    gate_grad = weight_sum(grad_gate, gathered)
+    pair, gate_grad = clock.sync(pair, gate_grad)
+    pair_back.append(pair)
 
     def owner_start(grad):
         return grad[0], swap(clock.hold(grad[1]), "wide", half_wide)
@@ -1242,12 +1385,13 @@
         [v.reshape(KEY_VALUE_HEADS, rows, head_cols) for v in query_back], pair_back, cosine, sine
     )
     proj_sent = swap(half_dot(all_normed, grad_proj, 1 - side, half_proj).astype(bf16), "seq", 1)
-    gate_first = weight_first(grad_gate[0], gathered[0])
+    gate_grad = part_sum(gate_grad, 1)
     proj_part = low_sum(half_dot(all_normed, grad_proj, side, half_proj), proj_sent)
-    down_other, proj_part, out_piece, gate_first, up_move = clock.sync(
-        down_other, proj_part, out_pieces[0], gate_first, up_move
+    down_other, proj_part, gate_grad, up_move = clock.sync(
+        down_other, proj_part, gate_grad, up_move
     )
     up_grad = far_end(up_keep, up_move)
+    gate_keep, gate_move = far_start(gate_grad)
 
     def part_of(o):
         first = index_at(o) * attn_rows
@@ -1268,6 +1412,7 @@
 
     def back_tokens(s):
         grad_normed = dot(clock.hold(grad_proj[s * rows : (s + 1) * rows]), proj_weights[s], NT)
+        grad_normed = lax.optimization_barrier(grad_normed)
         grad, gain = norm_back(inputs[s], input_factor[s], gain_attn, grad_normed)
         return [(grad_middle[s] + grad).astype(bf16), gain]
 
@@ -1276,15 +1421,14 @@
 
     def beside_ring(step):
         if step == 0:
-            return (weight_rest(gate_first, grad_gate, gathered),)
+            return back_tokens(0)
         if step == 1:
+            return back_tokens(1)
+        if step == 2:
             ring_work["down"] = spread_grad(clock.hold(down_grad), far_bits)
-            return (part_sum(ring_work["gate"], 1), *back_tokens(0))
-        if step == 2:
-            ring_work["move"] = far_start(ring_work["gate"])
-            return (ring_work["down"], *back_tokens(1))
+            return (gate_move,)
         if step == half_wide - 1:
-            return tuple(ring_work["move"])
+            return (ring_work["down"],)
         return ()
 
     a, b = halves(clock.hold(part_of(wide // 2)))
@@ -1293,18 +1437,13 @@
         work = beside_ring(step)
         a, b = hop(a, b, wide)
         a, b, *work = clock.sync(a, b, *work)
-        if step == 0:
-            ring_work["gate"] = work[0]
-        elif step == 1:
-            ring_work["gate"] = work[0]
-            grad_tokens.append(work[1])
-            gain_first = work[2]
+        if step < 2:
+            grad_tokens.append(work[0])
+            gain_first = gain_first + work[1]
         elif step == 2:
+            gate_grad = far_end(gate_keep, work[0])
+        elif step == half_wide - 1:
             down_grad = work[0]
-            grad_tokens.append(work[1])
-            gain_first = gain_first + work[2]
-        elif step == half_wide - 1:
-            gate_grad = far_end(*work)
         if step == 0:
             a, b = add_first(part_of(k), a), add_last(part_of(-k), b)
         elif k > 0:
@@ -1321,7 +1460,6 @@
     (gains,) = clock.sync(add_swapped(clock.hold(gains), "wide", wide_bits[1:]))
 
     up_own, up_other = owner_start(up_grad)
-    gains = add_swapped(add_swapped(gains, "wide", wide_bits[:1]), "seq", seq_bits)
     proj_total = total[:, :half_proj]
     out_totals = {0: total[:, half_proj:]}
     for bit in seq_bits[1:]:
@@ -1340,7 +1478,8 @@
         ],
         axis=1,
     )
-    up_other, low, gains = clock.sync(up_other, low, gains)
+    up_other, low = clock.sync(up_other, low)
+    gains = add_swapped(add_swapped(clock.hold(gains), "wide", wide_bits[:1]), "seq", seq_bits)
     up_grad = low_sum(up_own, up_other)
     gate_own, gate_other = owner_start(gate_grad)
     up_grad = spread_grad(clock.hold(up_grad), far_bits)
@@ -1351,7 +1490,9 @@
         axis=1,
     ).astype(f32)
     mlp_grad = unpack(spread_grad(clock.hold(down_grad), seq_bits[:1]), pieces, 2, [])
-    gate_other, up_grad, attn_grad, mlp_grad = clock.sync(gate_other, up_grad, attn_grad, mlp_grad)
+    gate_other, up_grad, attn_grad, mlp_grad, gains = clock.sync(
+        gate_other, up_grad, attn_grad, mlp_grad, gains
+    )
     gate_grad = spread_grad(low_sum(gate_own, gate_other), far_bits)
     mlp_grad = unpack(spread_grad(clock.hold(up_grad), seq_bits[:1]), pieces, 1, [mlp_grad])
     gate_grad, mlp_grad = clock.sync(gate_grad, mlp_grad)

time: 1760 us -> 1760 us (level)
  matrix products: 431 us -> 121 us
  Pallas kernels: 217 us -> 491 us
  waiting for transfers between devices: 662 us -> 711 us
  other arithmetic: 165 us -> 136 us
    dot_general x28 -> x12, matrix products: 431 us -> 121 us  [dot(): return lax.dot_general(a, b, (dims, ((), ())), preferred_element_type=f32)]
    pallas_call x0 -> x14, Pallas kernels: none -> 274 us  [the longest x3 87.1 us: weight_back(): kernel_call(functools.partial(weight_kernel, count=count), hidden // tile...]
    ppermute x48, waiting for transfers between devices: 155 us -> 251 us  [hop(): return (lax.ppermute(a, 'wide', up), lax.ppermute(b, 'wide', down))]
    convert_element_type x2 -> x0, other arithmetic: 27.6 us -> none  [weight_rest(): return first.astype(bf16).reshape(2, hidden, model_dim)]
    all_to_all x4, waiting for transfers between devices: 39.4 us -> 14.8 us  [heads_all_to_all(): lax.all_to_all(value, 'wide', split_axis=0, concat_axis=0, axis_index_gro...]
    ppermute x6, waiting for transfers between devices: 52 us -> 33.2 us  [class_ring(): return lax.ppermute(value, 'wide', perm)]
    unnamed x324 -> x302, local copies, waits for them, and re-layouts: 56.7 us -> 61.5 us
  transfers between devices with their start and end apart: 113 -> 113, of which waited for: 60 -> 57; matrix products, arithmetic and copies ran while one was open for 30% -> 14% of each run, Pallas kernels for 11% -> 26%
where the time goes in v6:
time: 1760 us; the launch traced here: 1750 us
  waiting for transfers between devices  711 us (40%)
  Pallas kernels  491 us (28%)
  local copies, waits for them, and re-layouts  144 us (8%)
  starting transfers between devices  142 us (8%)
  other arithmetic  136 us (8%)
  matrix products  121 us (7%)
    ppermute x47, waiting for transfers between devices, swap(): return lax.ppermute(value, axis, [(i, i ^ bit) for i in range(size)])  388 us
    ppermute x48, waiting for transfers between devices, hop(): return (lax.ppermute(a, 'wide', up), lax.ppermute(b, 'wide', down))  251 us
    dot_general x12, matrix products, dot(): return lax.dot_general(a, b, (dims, ((), ())), preferred_element_type=f32)  121 us
    pallas_call x3, Pallas kernels, weight_back(): kernel_call(functools.partial(weight_kernel, count=count), hidden // tile...  87.1 us
    pallas_call x4, Pallas kernels, input_back(): kernel_call(input_back_kernel, tiles, [whole_spec(grad_gate.shape)] * 2 +...  68.6 us
    pallas_call x3, Pallas kernels, open_forward(): kernel_call(open_kernel, tiles, [whole_spec(x.shape)] + [row_spec(tile, d...  62.5 us
    unnamed x302, local copies, waits for them, and re-layouts  61.5 us
    pallas_call x4, Pallas kernels, open_back(): kernel_call(open_back_kernel, tiles, [whole_spec(x.shape), row_spec(tile,...  55.4 us
  transfers between devices with their start and end apart: 113, of which 57 were waited for; matrix products, arithmetic and copies ran while one was open for 14% of the time, Pallas kernels for 26%

profile of v6, /device:TPU:0, one launch (start us, length us, event | category | flops | bytes accessed | tf_op | source)
XLA Modules:
  0.0 1746.4 jit_solution(10403315625414800535)
XLA Ops:
  12.3 25.0 %own_slices.1 = (bf16[2304,2304]{1,0:T(8,128)(2,1)}, bf16[2304,2304]{1,0:T(8,128)(2,1)}, bf16[2304,2304]{1,0:T(8,128)(2,1)}, bf16[2304,2304]{1,0:T(8,128)(2,1)},...) custom-call(s32[4]{0:T(128)} %pad_add_fusion.pieces, s32[4]{0:T(128)} %pad_add_fusion.1.info, ...), custom_call_target="tpu_custom_call" | custom-call | flops 159252480 | bytes 63700992 | tf_op jit(solution)/shard_map/own_slices/pallas_call | solution.py:297
  49.1 27.9 %collective-permute-done.3.refs_0_ = bf16[288,2560]{1,0:T(8,128)(2,1)} collective-permute-done((bf16[288,2560]{1,0:T(8,128)(2,1)}, bf16[288,2560]{1,0:T(8,128)(2,1)}, u32[]{:S(2)}, u32[]{:S(2)}) %collective-permute-start.3) | collective-permute-done | bytes 1474592 | tf_op jit(solution)/shard_map/ppermute | solution.py:102
  92.4 21.5 %collective-permute-done.7.refs_0_ = bf16[288,2560]{1,0:T(8,128)(2,1)} collective-permute-done((bf16[288,2560]{1,0:T(8,128)(2,1)}, bf16[288,2560]{1,0:T(8,128)(2,1)}, u32[]{:S(2)}, u32[]{:S(2)}) %collective-permute-start.7) | collective-permute-done | bytes 1474592 | tf_op jit(solution)/shard_map/ppermute | solution.py:102
  193.2 25.8 %collective-permute-done.15.refs_0_ = bf16[288,2304]{1,0:T(8,128)(2,1)} collective-permute-done((bf16[288,2304]{1,0:T(8,128)(2,1)}, bf16[288,2304]{1,0:T(8,128)(2,1)}, u32[]{:S(2)}, u32[]{:S(2)}) %collective-permute-start.15) | collective-permute-done | bytes 1327136 | tf_op jit(solution)/shard_map/ppermute | solution.py:157
  236.0 14.8 all-to-all-done.refs_0_
  258.1 20.6 %out_slices.1 = (bf16[2304,2048]{1,0:T(8,128)(2,1)}, bf16[2304,2048]{1,0:T(8,128)(2,1)}) custom-call(s32[8]{0:T(128)} %stack.172.places, s32[4]{0:T(128)} %pad_add_fusion.1.info, bf16[8,288,512]{2,1,0:T(8,128)(2,1)} %bitcast_dynamic-update-slice_fusion.7.refs_0_, bf16[8,288,512]{2,1,0:T(8,128)(2,1)} %collective-permute-done.17.refs_1_, ...), custom_call_target="tpu_custom_call" | custom-call | flops 94371840 | bytes 28311552 | tf_op jit(solution)/shard_map/out_slices/pallas_call | solution.py:260
  294.6 20.7 %collective-permute-done.21 = bf16[2,256,512]{2,1,0:T(8,128)(2,1)} collective-permute-done((bf16[2,256,512]{2,1,0:T(8,128)(2,1)S(1)}, bf16[2,256,512]{2,1,0:T(8,128)(2,1)}, u32[]{:S(2)}, u32[]{:S(2)}) %collective-permute-start.21) | collective-permute-done | bytes 524320 | tf_op jit(solution)/shard_map/ppermute | solution.py:177
  323.1 11.4 attn_forward.2
  364.5 11.4 attn_forward.3
  393.3 15.6 all-to-all-done.5
  421.2 55.2 %collective-permute-done.25.refs_0_ = bf16[288,2304]{1,0:T(8,128)(2,1)S(1)} collective-permute-done((bf16[288,2304]{1,0:T(8,128)(2,1)S(1)}, bf16[288,2304]{1,0:T(8,128)(2,1)S(1)}, u32[]{:S(2)}, u32[]{:S(2)}) %collective-permute-start.25) | collective-permute-done | bytes 1327136 | tf_op jit(solution)/shard_map/ppermute | solution.py:157
  476.8 30.6 %collective-permute-done.27.refs_1_ = bf16[288,2304]{1,0:T(8,128)(2,1)S(1)} collective-permute-done((bf16[288,2304]{1,0:T(8,128)(2,1)S(1)}, bf16[288,2304]{1,0:T(8,128)(2,1)S(1)}, u32[]{:S(2)}, u32[]{:S(2)}) %collective-permute-start.27) | collective-permute-done | bytes 1327136 | tf_op jit(solution)/shard_map/ppermute | solution.py:157
  507.4 28.5 %collective-permute-done.26.refs_0_ = bf16[288,2304]{1,0:T(8,128)(2,1)} collective-permute-done((bf16[288,2304]{1,0:T(8,128)(2,1)S(1)}, bf16[288,2304]{1,0:T(8,128)(2,1)}, u32[]{:S(2)}, u32[]{:S(2)}) %collective-permute-start.26) | collective-permute-done | bytes 1327136 | tf_op jit(solution)/shard_map/ppermute | solution.py:157
  540.1 26.1 %collective-permute-done.28 = bf16[256,2304]{1,0:T(8,128)(2,1)S(1)} collective-permute-done((bf16[256,2304]{1,0:T(8,128)(2,1)S(1)}, bf16[256,2304]{1,0:T(8,128)(2,1)S(1)}, u32[]{:S(2)}, u32[]{:S(2)}) %collective-permute-start.28) | collective-permute-done | bytes 1179680 | tf_op jit(solution)/shard_map/ppermute | solution.py:102
  593.5 29.0 %open_forward.3 = (f32[1024,2304]{1,0:T(8,128)}, f32[1024,2304]{1,0:T(8,128)}, bf16[1024,2304]{1,0:T(8,128)(2,1)}) custom-call(bf16[1024,2304]{1,0:T(8,128)(2,1)} %constant_dynamic-update-slice_fusion.4.refs_0_.refs_2_, bf16[2304,2304]{1,0:T(8,128)(2,1)} %get-tuple-element.555.refs_1_.refs_2_, bf16[2304,2304]{1,0:T(8,128)(2,1)} %get-tuple-element.556.refs_2_.refs_3_), custom_call_target="tpu_custom_call" | custom-call | flops 21743271936 | bytes 49545216 | tf_op jit(solution)/shard_map/open_forward/pallas_call | solution.py:443
  639.4 14.9 convolution_convert_fusion.3
  658.6 18.1 %open_forward.4 = (f32[1024,2304]{1,0:T(8,128)}, f32[1024,2304]{1,0:T(8,128)}, bf16[1024,2304]{1,0:T(8,128)(2,1)}) custom-call(bf16[1024,2304]{1,0:T(8,128)(2,1)} %constant_dynamic-update-slice_fusion.9.refs_0_.refs_3_, bf16[2304,2304]{1,0:T(8,128)(2,1)} %get-tuple-element.585.refs_1_.refs_2_, bf16[2304,2304]{1,0:T(8,128)(2,1)} %get-tuple-element.586.refs_2_.refs_3_), custom_call_target="tpu_custom_call" | custom-call | flops 12079595520 | bytes 29622272 | tf_op jit(solution)/shard_map/open_forward/pallas_call | solution.py:443
  680.4 15.3 open_forward.5
  712.6 13.5 convolution_convert_fusion.2
  756.1 14.9 open_back.4
  776.0 12.7 open_back.5
  788.7 18.5 %input_back.4.refs_4_ = bf16[1024,2304]{1,0:T(8,128)(2,1)} custom-call(bf16[1024,2304]{1,0:T(8,128)(2,1)} %get-tuple-element.735.refs_0_, bf16[1024,2304]{1,0:T(8,128)(2,1)} %get-tuple-element.721.refs_1_.refs_0_, bf16[2304,2304]{1,0:T(8,128)(2,1)} %get-tuple-element.555.refs_1_.refs_2_, bf16[2304,2304]{1,0:T(8,128)(2,1)} %get-tuple-element.556.refs_2_.refs_3_), custom_call_target="tpu_custom_call" | custom-call | flops 12079595520 | bytes 23855104 | tf_op jit(solution)/shard_map/input_back/pallas_call | solution.py:500
  821.8 15.8 input_back.5
  846.0 12.7 collective-permute-done.55
  864.7 15.0 open_back.6
  885.7 12.8 open_back.7
  898.5 18.5 %input_back.6.refs_4_ = bf16[1024,2304]{1,0:T(8,128)(2,1)} custom-call(bf16[1024,2304]{1,0:T(8,128)(2,1)} %get-tuple-element.736.refs_0_.refs_1_, bf16[1024,2304]{1,0:T(8,128)(2,1)} %get-tuple-element.722.refs_1_, bf16[2304,2304]{1,0:T(8,128)(2,1)} %get-tuple-element.585.refs_1_.refs_2_, bf16[2304,2304]{1,0:T(8,128)(2,1)} %get-tuple-element.586.refs_2_.refs_3_), custom_call_target="tpu_custom_call" | custom-call | flops 12079595520 | bytes 23855104 | tf_op jit(solution)/shard_map/input_back/pallas_call | solution.py:500
  933.3 15.9 input_back.7
  953.3 12.6 collective-permute-done.61
  968.5 29.0 %weight_back.3 = bf16[2304,2304]{1,0:T(8,128)(2,1)} custom-call(bf16[1024,2304]{1,0:T(8,128)(2,1)} %get-tuple-element.675.refs_0_, bf16[1024,2304]{1,0:T(8,128)(2,1)} %get-tuple-element.676.refs_1_, bf16[1024,2304]{1,0:T(8,128)(2,1)} %copy-done.8, bf16[1024,2304]{1,0:T(8,128)(2,1)} %constant_dynamic-update-slice_fusion.19.refs_0_.refs_3_), custom_call_target="tpu_custom_call" | custom-call | flops 21743271936 | bytes 29491200 | tf_op jit(solution)/shard_map/weight_back/pallas_call | solution.py:526
  1049.9 17.4 attn_backward.2
  1079.7 17.6 %attn_backward.3 = (bf16[1024,512]{1,0:T(8,128)(2,1)}, bf16[4,256,512]{2,1,0:T(8,128)(2,1)}, bf16[4,256,512]{2,1,0:T(8,128)(2,1)}) custom-call(s32[1]{0:T(128)} %bitcast.43.info, bf16[1024,512]{1,0:T(8,128)(2,1)} %bitcast.46.q_ref, bf16[1024,512]{1,0:T(8,128)(2,1)} %bitcast.91.grad_ref, f32[1024,512]{1,0:T(8,128)} %get-tuple-element.709.exact_ref, ...), custom_call_target="tpu_custom_call" | custom-call | flops 10737418240 | bytes 9437184 | tf_op jit(solution)/shard_map/attn_backward/pallas_call | solution.py:816
  1104.3 28.2 %collective-permute-done.68 = bf16[2,288,2304]{2,1,0:T(8,128)(2,1)} collective-permute-done((bf16[2,288,2304]{2,1,0:T(8,128)(2,1)}, bf16[2,288,2304]{2,1,0:T(8,128)(2,1)}, u32[]{:S(2)}, u32[]{:S(2)}) %collective-permute-start.68) | collective-permute-done | bytes 2654240 | tf_op jit(solution)/shard_map/ppermute | solution.py:157
  1137.7 29.0 %weight_back.4 = bf16[2304,2304]{1,0:T(8,128)(2,1)} custom-call(bf16[1024,2304]{1,0:T(8,128)(2,1)} %get-tuple-element.721.refs_1_.refs_0_, bf16[1024,2304]{1,0:T(8,128)(2,1)} %get-tuple-element.722.refs_1_, bf16[1024,2304]{1,0:T(8,128)(2,1)} %constant_dynamic-update-slice_fusion.4.refs_0_.refs_2_, ...), custom_call_target="tpu_custom_call" | custom-call | flops 21743271936 | bytes 29491200 | tf_op jit(solution)/shard_map/weight_back/pallas_call | solution.py:526
  1186.3 43.5 %collective-permute-done.72 = bf16[2304,512]{1,0:T(8,128)(2,1)} collective-permute-done((bf16[2304,512]{1,0:T(8,128)(2,1)}, bf16[2304,512]{1,0:T(8,128)(2,1)}, u32[]{:S(2)}, u32[]{:S(2)}) %collective-permute-start.72) | collective-permute-done | bytes 2359328 | tf_op jit(solution)/shard_map/ppermute | solution.py:157
  1248.5 29.0 %weight_back.5 = bf16[2304,2304]{1,0:T(8,128)(2,1)} custom-call(bf16[1024,2304]{1,0:T(8,128)(2,1)} %get-tuple-element.735.refs_0_, bf16[1024,2304]{1,0:T(8,128)(2,1)} %get-tuple-element.736.refs_0_.refs_1_, bf16[1024,2304]{1,0:T(8,128)(2,1)} %constant_dynamic-update-slice_fusion.4.refs_0_.refs_2_, ...), custom_call_target="tpu_custom_call" | custom-call | flops 21743271936 | bytes 29491200 | tf_op jit(solution)/shard_map/weight_back/pallas_call | solution.py:526
  1277.6 13.4 turn_back.1
  1340.3 28.8 %collective-permute-done.76 = bf16[2,288,2304]{2,1,0:T(8,128)(2,1)S(1)} collective-permute-done((bf16[2,288,2304]{2,1,0:T(8,128)(2,1)S(1)}, bf16[2,288,2304]{2,1,0:T(8,128)(2,1)S(1)}, u32[]{:S(2)}, u32[]{:S(2)}) %collective-permute-start.76) | collective-permute-done | bytes 2654240 | tf_op jit(solution)/shard_map/ppermute | solution.py:157
  1373.8 20.7 %fusion.83 = f32[256,2304]{1,0:T(8,128)} fusion(bf16[256,4096]{1,0:T(8,128)(2,1)} %get-tuple-element.752, bf16[2304,4096]{1,0:T(8,128)(2,1)} %get-tuple-element.444.wq_ref.wk_ref.wv_ref), kind=kOutput, calls=%fused_computation.334 | convolution fusion | flops 4831838208 | bytes 23330816 | tf_op jit(solution)/shard_map/dot_general | solution.py:26
  1423.6 20.4 %fusion.84 = f32[256,2304]{1,0:T(8,128)} fusion(bf16[256,4096]{1,0:T(8,128)(2,1)} %get-tuple-element.759, bf16[2304,4096]{1,0:T(8,128)(2,1)} %get-tuple-element.447.wq_ref.wk_ref.wv_ref), kind=kOutput, calls=%fused_computation.335 | convolution fusion | flops 4831838208 | bytes 23330816 | tf_op jit(solution)/shard_map/dot_general | solution.py:26
  1452.0 27.7 %collective-permute-done.80 = bf16[288,2560]{1,0:T(8,128)(2,1)S(1)} collective-permute-done((bf16[288,2560]{1,0:T(8,128)(2,1)S(1)}, bf16[288,2560]{1,0:T(8,128)(2,1)S(1)}, u32[]{:S(2)}, u32[]{:S(2)}) %collective-permute-start.80) | collective-permute-done | bytes 1474592 | tf_op jit(solution)/shard_map/ppermute | solution.py:102
  1485.4 28.8 %collective-permute-done.82 = bf16[288,2560]{1,0:T(8,128)(2,1)S(1)} collective-permute-done((bf16[288,2560]{1,0:T(8,128)(2,1)S(1)}, bf16[288,2560]{1,0:T(8,128)(2,1)S(1)}, u32[]{:S(2)}, u32[]{:S(2)}) %collective-permute-start.82) | collective-permute-done | bytes 1474592 | tf_op jit(solution)/shard_map/ppermute | solution.py:102
  1519.9 28.7 %collective-permute-done.85 = bf16[288,2560]{1,0:T(8,128)(2,1)} collective-permute-done((bf16[288,2560]{1,0:T(8,128)(2,1)S(1)}, bf16[288,2560]{1,0:T(8,128)(2,1)}, u32[]{:S(2)}, u32[]{:S(2)}) %collective-permute-start.85) | collective-permute-done | bytes 1474592 | tf_op jit(solution)/shard_map/ppermute | solution.py:102
  1563.6 23.8 %collective-permute-done.90 = bf16[288,2560]{1,0:T(8,128)(2,1)S(1)} collective-permute-done((bf16[288,2560]{1,0:T(8,128)(2,1)S(1)}, bf16[288,2560]{1,0:T(8,128)(2,1)S(1)}, u32[]{:S(2)}, u32[]{:S(2)}) %collective-permute-start.90) | collective-permute-done | bytes 1474592 | tf_op jit(solution)/shard_map/ppermute | solution.py:157
  1588.2 28.7 %collective-permute-done.89 = bf16[288,2304]{1,0:T(8,128)(2,1)S(1)} collective-permute-done((bf16[288,2304]{1,0:T(8,128)(2,1)S(1)}, bf16[288,2304]{1,0:T(8,128)(2,1)S(1)}, u32[]{:S(2)}, u32[]{:S(2)}) %collective-permute-start.89) | collective-permute-done | bytes 1327136 | tf_op jit(solution)/shard_map/ppermute | solution.py:157
  1626.2 24.2 %collective-permute-done.97 = f32[4,2304]{1,0:T(4,128)S(1)} collective-permute-done((f32[4,2304]{1,0:T(4,128)S(1)}, f32[4,2304]{1,0:T(4,128)S(1)}, u32[]{:S(2)}, u32[]{:S(2)}) %collective-permute-start.97) | collective-permute-done | bytes 36896 | tf_op jit(solution)/shard_map/ppermute | solution.py:157
  1666.6 19.9 %collective-permute-done.91 = bf16[288,2304]{1,0:T(8,128)(2,1)} collective-permute-done((bf16[288,2304]{1,0:T(8,128)(2,1)}, bf16[288,2304]{1,0:T(8,128)(2,1)}, u32[]{:S(2)}, u32[]{:S(2)}) %collective-permute-start.91) | collective-permute-done | bytes 1327136 | tf_op jit(solution)/shard_map/ppermute | solution.py:157
  1689.2 30.6 %collective-permute-done.98 = bf16[288,2304]{1,0:T(8,128)(2,1)S(1)} collective-permute-done((bf16[288,2304]{1,0:T(8,128)(2,1)S(1)}, bf16[288,2304]{1,0:T(8,128)(2,1)S(1)}, u32[]{:S(2)}, u32[]{:S(2)}) %collective-permute-start.98) | collective-permute-done | bytes 1327136 | tf_op jit(solution)/shard_map/ppermute | solution.py:157
  (728 shorter events, 678.6 us)
Async XLA Ops:
  4.9 36.8 %collective-permute-start = (bf16[288,2560]{1,0:T(8,128)(2,1)}, bf16[288,2560]{1,0:T(8,128)(2,1)}, u32[]{:S(2)}, u32[]{:S(2)}) collective-permute-start(bf16[288,2560]{1,0:T(8,128)(2,1)} %pad_maximum_fusion.10.refs_0_), channel_id=1, source_target_pairs={{0,8},{8,16},{16,24},{24,28},{28,20},{20,12},{12,4},{4,0},{1,9},{9... | collective-permute-start | bytes 4423688 | tf_op jit(solution)/shard_map/ppermute | solution.py:102
  7.9 34.1 %collective-permute-start.1 = (bf16[288,2560]{1,0:T(8,128)(2,1)}, bf16[288,2560]{1,0:T(8,128)(2,1)}, u32[]{:S(2)}, u32[]{:S(2)}) collective-permute-start(bf16[288,2560]{1,0:T(8,128)(2,1)} %pad_maximum_fusion.10.refs_0_), channel_id=1, source_target_pairs={{8,0},{16,8},{24,16},{28,24},{20,28},{12,20},{4,12},{0,4},{9,1},{1... | collective-permute-start | bytes 4423688 | tf_op jit(solution)/shard_map/ppermute | solution.py:102
  7.9 34.1 %collective-permute-start.2 = (bf16[288,2560]{1,0:T(8,128)(2,1)}, bf16[288,2560]{1,0:T(8,128)(2,1)}, u32[]{:S(2)}, u32[]{:S(2)}) collective-permute-start(bf16[288,2560]{1,0:T(8,128)(2,1)} %pad_maximum_fusion.10.refs_0_), channel_id=1, source_target_pairs={{0,1},{1,0},{2,3},{3,2},{4,5},{5,4},{6,7},{7,6},{8,9},{9,8},{10,11... | collective-permute-start | bytes 4423688 | tf_op jit(solution)/shard_map/ppermute | solution.py:157
  42.0 35.0 %collective-permute-start.3 = (bf16[288,2560]{1,0:T(8,128)(2,1)}, bf16[288,2560]{1,0:T(8,128)(2,1)}, u32[]{:S(2)}, u32[]{:S(2)}) collective-permute-start(bf16[288,2560]{1,0:T(8,128)(2,1)} %collective-permute-done.refs_2_), channel_id=1, source_target_pairs={{0,8},{8,16},{16,24},{24,28},{28,20},{20,12},{12,4},{4,0},{1,9},{9... | collective-permute-start | bytes 4423688 | tf_op jit(solution)/shard_map/ppermute | solution.py:102
  43.8 35.0 %collective-permute-start.5 = (bf16[288,2560]{1,0:T(8,128)(2,1)}, bf16[288,2560]{1,0:T(8,128)(2,1)}, u32[]{:S(2)}, u32[]{:S(2)}) collective-permute-start(bf16[288,2560]{1,0:T(8,128)(2,1)} %collective-permute-done.refs_2_), channel_id=1, source_target_pairs={{0,1},{1,0},{2,3},{3,2},{4,5},{5,4},{6,7},{7,6},{8,9},{9,8},{10,11... | collective-permute-start | bytes 4423688 | tf_op jit(solution)/shard_map/ppermute | solution.py:157
  44.0 34.8 %collective-permute-start.4 = (bf16[288,2560]{1,0:T(8,128)(2,1)}, bf16[288,2560]{1,0:T(8,128)(2,1)}, u32[]{:S(2)}, u32[]{:S(2)}) collective-permute-start(bf16[288,2560]{1,0:T(8,128)(2,1)} %collective-permute-done.1.refs_4_), channel_id=1, source_target_pairs={{8,0},{16,8},{24,16},{28,24},{20,28},{12,20},{4,12},{0,4},{9,1},{1... | collective-permute-start | bytes 4423688 | tf_op jit(solution)/shard_map/ppermute | solution.py:102
  44.3 34.5 %collective-permute-start.6 = (bf16[288,2560]{1,0:T(8,128)(2,1)}, bf16[288,2560]{1,0:T(8,128)(2,1)}, u32[]{:S(2)}, u32[]{:S(2)}) collective-permute-start(bf16[288,2560]{1,0:T(8,128)(2,1)} %collective-permute-done.1.refs_4_), channel_id=1, source_target_pairs={{0,1},{1,0},{2,3},{3,2},{4,5},{5,4},{6,7},{7,6},{8,9},{9,8},{10,11... | collective-permute-start | bytes 4423688 | tf_op jit(solution)/shard_map/ppermute | solution.py:157
  78.8 35.0 %collective-permute-start.7 = (bf16[288,2560]{1,0:T(8,128)(2,1)}, bf16[288,2560]{1,0:T(8,128)(2,1)}, u32[]{:S(2)}, u32[]{:S(2)}) collective-permute-start(bf16[288,2560]{1,0:T(8,128)(2,1)} %collective-permute-done.3.refs_0_), channel_id=1, source_target_pairs={{0,8},{8,16},{16,24},{24,28},{28,20},{20,12},{12,4},{4,0},{1,9},{9... | collective-permute-start | bytes 4423688 | tf_op jit(solution)/shard_map/ppermute | solution.py:102
  80.5 34.7 %collective-permute-start.8 = (bf16[288,2560]{1,0:T(8,128)(2,1)}, bf16[288,2560]{1,0:T(8,128)(2,1)}, u32[]{:S(2)}, u32[]{:S(2)}) collective-permute-start(bf16[288,2560]{1,0:T(8,128)(2,1)} %collective-permute-done.4.refs_2_), channel_id=1, source_target_pairs={{8,0},{16,8},{24,16},{28,24},{20,28},{12,20},{4,12},{0,4},{9,1},{1... | collective-permute-start | bytes 4423688 | tf_op jit(solution)/shard_map/ppermute | solution.py:102
  80.9 34.2 %collective-permute-start.9 = (bf16[288,2560]{1,0:T(8,128)(2,1)}, bf16[288,2560]{1,0:T(8,128)(2,1)}, u32[]{:S(2)}, u32[]{:S(2)}) collective-permute-start(bf16[288,2560]{1,0:T(8,128)(2,1)} %collective-permute-done.3.refs_0_), channel_id=1, source_target_pairs={{0,1},{1,0},{2,3},{3,2},{4,5},{5,4},{6,7},{7,6},{8,9},{9,8},{10,11... | collective-permute-start | bytes 4423688 | tf_op jit(solution)/shard_map/ppermute | solution.py:157
  156.4 62.5 %collective-permute-start.17 = (bf16[8,288,512]{2,1,0:T(8,128)(2,1)}, bf16[8,288,512]{2,1,0:T(8,128)(2,1)}, u32[]{:S(2)}, u32[]{:S(2)}) collective-permute-start(bf16[8,288,512]{2,1,0:T(8,128)(2,1)} %bitcast_dynamic-update-slice_fusion.7.refs_0_), channel_id=1, source_target_pairs={{0,2},{1,3},{2,0},{3,1},{4,6},{5,7},{6,4},{7,5},{8,10},{9,11},{10,... | collective-permute-start | bytes 7077896 | tf_op jit(solution)/shard_map/ppermute | solution.py:157
  158.0 60.9 %collective-permute-start.15 = (bf16[288,2304]{1,0:T(8,128)(2,1)}, bf16[288,2304]{1,0:T(8,128)(2,1)}, u32[]{:S(2)}, u32[]{:S(2)}) collective-permute-start(bf16[288,2304]{1,0:T(8,128)(2,1)} %get-tuple-element.435), channel_id=1, source_target_pairs={{0,16},{4,20},{8,24},{12,28},{16,0},{20,4},{24,8},{28,12},{1,17},{... | collective-permute-start | bytes 3981320 | tf_op jit(solution)/shard_map/ppermute | solution.py:157
  218.9 31.9 %collective-permute-start.18 = (bf16[8,288,512]{2,1,0:T(8,128)(2,1)}, bf16[8,288,512]{2,1,0:T(8,128)(2,1)}, u32[]{:S(2)}, u32[]{:S(2)}) collective-permute-start(bf16[8,288,512]{2,1,0:T(8,128)(2,1)} %collective-permute-done.17.refs_1_), channel_id=1, source_target_pairs={{0,1},{1,0},{2,3},{3,2},{4,5},{5,4},{6,7},{7,6},{8,9},{9,8},{10,11... | collective-permute-start | bytes 7077896 | tf_op jit(solution)/shard_map/ppermute | solution.py:157
  251.8 34.7 %all-to-all-start.1 = ((bf16[4,256,512]{2,1,0:T(8,128)(2,1)}), bf16[4,256,512]{2,1,0:T(8,128)(2,1)S(1)}, u32[]{:S(2)}, u32[]{:S(2)}) async-start(bf16[4,256,512]{2,1,0:T(8,128)(2,1)} %get-tuple-element.466), calls=%async_computation.1 | async-start | bytes 2097152 | tf_op jit(solution)/shard_map/all_to_all | solution.py:168
  377.2 31.7 %all-to-all-start.5 = ((bf16[8,128,512]{2,1,0:T(8,128)(2,1)}), bf16[8,128,512]{2,1,0:T(8,128)(2,1)}, u32[]{:S(2)}, u32[]{:S(2)}) async-start(bf16[8,128,512]{2,1,0:T(8,128)(2,1)} %bitcast.301), calls=%async_computation.5 | async-start | bytes 2097152 | tf_op jit(solution)/shard_map/all_to_all | solution.py:161
  418.1 58.2 %collective-permute-start.25 = (bf16[288,2304]{1,0:T(8,128)(2,1)S(1)}, bf16[288,2304]{1,0:T(8,128)(2,1)S(1)}, u32[]{:S(2)}, u32[]{:S(2)}) collective-permute-start(bf16[288,2304]{1,0:T(8,128)(2,1)S(1)} %copy-done.65), channel_id=1, source_target_pairs={{0,16},{4,20},{8,24},{12,28},{16,0},{20,4},{24,8},{28,12},{1,17},{... | collective-permute-start | bytes 3981320 | tf_op jit(solution)/shard_map/ppermute | solution.py:157
  476.8 59.1 %collective-permute-start.26 = (bf16[288,2304]{1,0:T(8,128)(2,1)S(1)}, bf16[288,2304]{1,0:T(8,128)(2,1)}, u32[]{:S(2)}, u32[]{:S(2)}) collective-permute-start(bf16[288,2304]{1,0:T(8,128)(2,1)S(1)} %copy-done.64), channel_id=1, source_target_pairs={{0,16},{4,20},{8,24},{12,28},{16,0},{20,4},{24,8},{28,12},{1,17},{... | collective-permute-start | bytes 3981320 | tf_op jit(solution)/shard_map/ppermute | solution.py:157
  589.7 33.9 %collective-permute-start.37 = (bf16[256,2304]{1,0:T(8,128)(2,1)S(1)}, bf16[256,2304]{1,0:T(8,128)(2,1)S(1)}, u32[]{:S(2)}, u32[]{:S(2)}) collective-permute-start(bf16[256,2304]{1,0:T(8,128)(2,1)S(1)} %multiply_convert_fusion), channel_id=1, source_target_pairs={{0,8},{8,12},{12,4},{4,0},{16,24},{24,28},{28,20},{20,16},{1,9},{9... | collective-permute-start | bytes 3538952 | tf_op jit(solution)/shard_map/ppermute | solution.py:102
  591.5 32.2 %collective-permute-start.38 = (bf16[256,2304]{1,0:T(8,128)(2,1)S(1)}, bf16[256,2304]{1,0:T(8,128)(2,1)S(1)}, u32[]{:S(2)}, u32[]{:S(2)}) collective-permute-start(bf16[256,2304]{1,0:T(8,128)(2,1)S(1)} %multiply_convert_fusion), channel_id=1, source_target_pairs={{8,0},{12,8},{4,12},{0,4},{24,16},{28,24},{20,28},{16,20},{9,1},{1... | collective-permute-start | bytes 3538952 | tf_op jit(solution)/shard_map/ppermute | solution.py:102
  772.8 34.3 %collective-permute-start.52 = (bf16[256,2304]{1,0:T(8,128)(2,1)S(1)}, bf16[256,2304]{1,0:T(8,128)(2,1)S(1)}, u32[]{:S(2)}, u32[]{:S(2)}) collective-permute-start(bf16[256,2304]{1,0:T(8,128)(2,1)S(1)} %pad_maximum_fusion.16), channel_id=1, source_target_pairs={{8,0},{12,8},{4,12},{0,4},{24,16},{28,24},{20,28},{16,20},{9,1},{1... | collective-permute-start | bytes 3538952 | tf_op jit(solution)/shard_map/ppermute | solution.py:102
  774.0 33.2 %collective-permute-start.51 = (bf16[256,2304]{1,0:T(8,128)(2,1)}, bf16[256,2304]{1,0:T(8,128)(2,1)S(1)}, u32[]{:S(2)}, u32[]{:S(2)}) collective-permute-start(bf16[256,2304]{1,0:T(8,128)(2,1)} %pad_maximum_fusion.15), channel_id=1, source_target_pairs={{0,8},{8,12},{12,4},{4,0},{16,24},{24,28},{28,20},{20,16},{1,9},{9... | collective-permute-start | bytes 3538952 | tf_op jit(solution)/shard_map/ppermute | solution.py:102
  882.6 34.4 %collective-permute-start.60 = (bf16[256,2304]{1,0:T(8,128)(2,1)}, bf16[256,2304]{1,0:T(8,128)(2,1)S(1)}, u32[]{:S(2)}, u32[]{:S(2)}) collective-permute-start(bf16[256,2304]{1,0:T(8,128)(2,1)} %pad_maximum_fusion.18), channel_id=1, source_target_pairs={{8,0},{12,8},{4,12},{0,4},{24,16},{28,24},{20,28},{16,20},{9,1},{1... | collective-permute-start | bytes 3538952 | tf_op jit(solution)/shard_map/ppermute | solution.py:102
  884.9 32.1 %collective-permute-start.59 = (bf16[256,2304]{1,0:T(8,128)(2,1)}, bf16[256,2304]{1,0:T(8,128)(2,1)}, u32[]{:S(2)}, u32[]{:S(2)}) collective-permute-start(bf16[256,2304]{1,0:T(8,128)(2,1)} %pad_maximum_fusion.17), channel_id=1, source_target_pairs={{0,8},{8,12},{12,4},{4,0},{16,24},{24,28},{28,20},{20,16},{1,9},{9... | collective-permute-start | bytes 3538952 | tf_op jit(solution)/shard_map/ppermute | solution.py:102
  1072.2 60.3 %collective-permute-start.68 = (bf16[2,288,2304]{2,1,0:T(8,128)(2,1)}, bf16[2,288,2304]{2,1,0:T(8,128)(2,1)}, u32[]{:S(2)}, u32[]{:S(2)}) collective-permute-start(bf16[2,288,2304]{2,1,0:T(8,128)(2,1)} %slice_bitcast_fusion.10), channel_id=1, source_target_pairs={{0,2},{1,3},{2,0},{3,1},{4,6},{5,7},{6,4},{7,5},{8,10},{9,11},{10,... | collective-permute-start | bytes 7962632 | tf_op jit(solution)/shard_map/ppermute | solution.py:157
  1075.5 57.0 %all-to-all-start.8 = ((bf16[8,128,512]{2,1,0:T(8,128)(2,1)}), bf16[8,128,512]{2,1,0:T(8,128)(2,1)S(1)}, u32[]{:S(2)}, u32[]{:S(2)}) async-start(bf16[8,128,512]{2,1,0:T(8,128)(2,1)} %bitcast.89), calls=%async_computation.8 | async-start | bytes 2097152 | tf_op jit(solution)/shard_map/all_to_all | solution.py:161
  1132.5 34.2 %collective-permute-start.69 = (bf16[2,256,512]{2,1,0:T(8,128)(2,1)}, bf16[2,256,512]{2,1,0:T(8,128)(2,1)S(1)}, u32[]{:S(2)}, u32[]{:S(2)}) collective-permute-start(bf16[2,256,512]{2,1,0:T(8,128)(2,1)} %get-tuple-element.720), channel_id=1, source_target_pairs={{0,4},{4,0},{8,12},{12,8},{16,20},{20,16},{24,28},{28,24},{1,5},{5... | collective-permute-start | bytes 1572872 | tf_op jit(solution)/shard_map/ppermute | solution.py:177
  1134.0 32.9 %all-to-all-start.9 = ((bf16[8,128,512]{2,1,0:T(8,128)(2,1)}), bf16[8,128,512]{2,1,0:T(8,128)(2,1)S(1)}, u32[]{:S(2)}, u32[]{:S(2)}) async-start(bf16[8,128,512]{2,1,0:T(8,128)(2,1)} %bitcast.299), calls=%async_computation.9 | async-start | bytes 2097152 | tf_op jit(solution)/shard_map/all_to_all | solution.py:161
  1172.5 62.9 %collective-permute-start.71 = (bf16[2,576,2304]{2,1,0:T(8,128)(2,1)}, bf16[2,576,2304]{2,1,0:T(8,128)(2,1)}, u32[]{:S(2)}, u32[]{:S(2)}) collective-permute-start(bf16[2,576,2304]{2,1,0:T(8,128)(2,1)} %slice_bitcast_fusion.2), channel_id=1, source_target_pairs={{0,1},{1,0},{2,3},{3,2},{4,5},{5,4},{6,7},{7,6},{8,9},{9,8},{10,11... | collective-permute-start | bytes 15925256 | tf_op jit(solution)/shard_map/ppermute | solution.py:157
  1175.8 54.0 %collective-permute-start.72 = (bf16[2304,512]{1,0:T(8,128)(2,1)}, bf16[2304,512]{1,0:T(8,128)(2,1)}, u32[]{:S(2)}, u32[]{:S(2)}) collective-permute-start(bf16[2304,512]{1,0:T(8,128)(2,1)} %constant_dynamic-slice_fusion.16), channel_id=1, source_target_pairs={{0,2},{1,3},{2,0},{3,1},{4,6},{5,7},{6,4},{7,5},{8,10},{9,11},{10,... | collective-permute-start | bytes 7077896 | tf_op jit(solution)/shard_map/ppermute | solution.py:157
  1177.1 55.8 %collective-permute-start.70 = (bf16[4,256,512]{2,1,0:T(8,128)(2,1)}, bf16[4,256,512]{2,1,0:T(8,128)(2,1)}, u32[]{:S(2)}, u32[]{:S(2)}) collective-permute-start(bf16[4,256,512]{2,1,0:T(8,128)(2,1)} %get-tuple-element.729), channel_id=1, source_target_pairs={{0,4},{4,0},{8,12},{12,8},{16,20},{20,16},{24,28},{28,24},{1,5},{5... | collective-permute-start | bytes 3145736 | tf_op jit(solution)/shard_map/ppermute | solution.py:177
  1181.8 61.3 %all-to-all-start.10 = ((bf16[4,256,512]{2,1,0:T(8,128)(2,1)}), bf16[4,256,512]{2,1,0:T(8,128)(2,1)S(1)}, u32[]{:S(2)}, u32[]{:S(2)}) async-start(bf16[4,256,512]{2,1,0:T(8,128)(2,1)} %pad_maximum_fusion.21), calls=%async_computation.10 | async-start | bytes 2097152 | tf_op jit(solution)/shard_map/all_to_all | solution.py:168
  1243.0 34.6 %all-to-all-start.11 = ((bf16[4,256,512]{2,1,0:T(8,128)(2,1)}), bf16[4,256,512]{2,1,0:T(8,128)(2,1)}, u32[]{:S(2)}, u32[]{:S(2)}) async-start(bf16[4,256,512]{2,1,0:T(8,128)(2,1)} %add_convert_fusion.11), calls=%async_computation.11 | async-start | bytes 2097152 | tf_op jit(solution)/shard_map/all_to_all | solution.py:168
  1309.6 59.6 %collective-permute-start.76 = (bf16[2,288,2304]{2,1,0:T(8,128)(2,1)S(1)}, bf16[2,288,2304]{2,1,0:T(8,128)(2,1)S(1)}, u32[]{:S(2)}, u32[]{:S(2)}) collective-permute-start(bf16[2,288,2304]{2,1,0:T(8,128)(2,1)S(1)} %slice_bitcast_fusion.9), channel_id=1, source_target_pairs={{0,2},{1,3},{2,0},{3,1},{4,6},{5,7},{6,4},{7,5},{8,10},{9,11},{10,... | collective-permute-start | bytes 7962632 | tf_op jit(solution)/shard_map/ppermute | solution.py:157
  1312.2 60.4 %collective-permute-start.73 = (bf16[288,2304]{1,0:T(8,128)(2,1)S(1)}, bf16[288,2304]{1,0:T(8,128)(2,1)S(1)}, u32[]{:S(2)}, u32[]{:S(2)}) collective-permute-start(bf16[288,2304]{1,0:T(8,128)(2,1)S(1)} %slice_bitcast_fusion.17), channel_id=1, source_target_pairs={{0,16},{4,20},{8,24},{12,28},{16,0},{20,4},{24,8},{28,12},{1,17},{... | collective-permute-start | bytes 3981320 | tf_op jit(solution)/shard_map/ppermute | solution.py:157
  1408.5 76.9 %collective-permute-start.83 = (bf16[2,288,2304]{2,1,0:T(8,128)(2,1)}, bf16[2,288,2304]{2,1,0:T(8,128)(2,1)}, u32[]{:S(2)}, u32[]{:S(2)}) collective-permute-start(bf16[2,288,2304]{2,1,0:T(8,128)(2,1)} %slice_bitcast_fusion.7), channel_id=1, source_target_pairs={{0,2},{1,3},{2,0},{3,1},{4,6},{5,7},{6,4},{7,5},{8,10},{9,11},{10,... | collective-permute-start | bytes 7962632 | tf_op jit(solution)/shard_map/ppermute | solution.py:157
  1445.7 34.1 %collective-permute-start.80 = (bf16[288,2560]{1,0:T(8,128)(2,1)S(1)}, bf16[288,2560]{1,0:T(8,128)(2,1)S(1)}, u32[]{:S(2)}, u32[]{:S(2)}) collective-permute-start(bf16[288,2560]{1,0:T(8,128)(2,1)S(1)} %pad_maximum_fusion.12), channel_id=1, source_target_pairs={{8,0},{16,8},{24,16},{28,24},{20,28},{12,20},{4,12},{0,4},{9,1},{1... | collective-permute-start | bytes 4423688 | tf_op jit(solution)/shard_map/ppermute | solution.py:102
  1447.9 32.6 %collective-permute-start.79 = (bf16[288,2560]{1,0:T(8,128)(2,1)S(1)}, bf16[288,2560]{1,0:T(8,128)(2,1)S(1)}, u32[]{:S(2)}, u32[]{:S(2)}) collective-permute-start(bf16[288,2560]{1,0:T(8,128)(2,1)S(1)} %fusion.44), channel_id=1, source_target_pairs={{0,8},{8,16},{16,24},{24,28},{28,20},{20,12},{12,4},{4,0},{1,9},{9... | collective-permute-start | bytes 4423688 | tf_op jit(solution)/shard_map/ppermute | solution.py:102
  1481.0 33.2 %collective-permute-start.82 = (bf16[288,2560]{1,0:T(8,128)(2,1)S(1)}, bf16[288,2560]{1,0:T(8,128)(2,1)S(1)}, u32[]{:S(2)}, u32[]{:S(2)}) collective-permute-start(bf16[288,2560]{1,0:T(8,128)(2,1)S(1)} %add_convert_fusion.6), channel_id=1, source_target_pairs={{8,0},{16,8},{24,16},{28,24},{20,28},{12,20},{4,12},{0,4},{9,1},{1... | collective-permute-start | bytes 4423688 | tf_op jit(solution)/shard_map/ppermute | solution.py:102
  1484.0 32.5 %collective-permute-start.81 = (bf16[288,2560]{1,0:T(8,128)(2,1)S(1)}, bf16[288,2560]{1,0:T(8,128)(2,1)S(1)}, u32[]{:S(2)}, u32[]{:S(2)}) collective-permute-start(bf16[288,2560]{1,0:T(8,128)(2,1)S(1)} %add_convert_fusion.7), channel_id=1, source_target_pairs={{0,8},{8,16},{16,24},{24,28},{28,20},{20,12},{12,4},{4,0},{1,9},{9... | collective-permute-start | bytes 4423688 | tf_op jit(solution)/shard_map/ppermute | solution.py:102
  1484.4 35.3 %collective-permute-start.86 = (bf16[288,2304]{1,0:T(8,128)(2,1)S(1)}, bf16[288,2304]{1,0:T(8,128)(2,1)S(1)}, u32[]{:S(2)}, u32[]{:S(2)}) collective-permute-start(bf16[288,2304]{1,0:T(8,128)(2,1)S(1)} %fusion.14), channel_id=1, source_target_pairs={{0,2},{1,3},{2,0},{3,1},{4,6},{5,7},{6,4},{7,5},{8,10},{9,11},{10,... | collective-permute-start | bytes 3981320 | tf_op jit(solution)/shard_map/ppermute | solution.py:157
  1517.0 31.7 %collective-permute-start.85 = (bf16[288,2560]{1,0:T(8,128)(2,1)S(1)}, bf16[288,2560]{1,0:T(8,128)(2,1)}, u32[]{:S(2)}, u32[]{:S(2)}) collective-permute-start(bf16[288,2560]{1,0:T(8,128)(2,1)S(1)} %add_convert_fusion.4), channel_id=1, source_target_pairs={{8,0},{16,8},{24,16},{28,24},{20,28},{12,20},{4,12},{0,4},{9,1},{1... | collective-permute-start | bytes 4423688 | tf_op jit(solution)/shard_map/ppermute | solution.py:102
  1562.5 54.4 %collective-permute-start.89 = (bf16[288,2304]{1,0:T(8,128)(2,1)S(1)}, bf16[288,2304]{1,0:T(8,128)(2,1)S(1)}, u32[]{:S(2)}, u32[]{:S(2)}) collective-permute-start(bf16[288,2304]{1,0:T(8,128)(2,1)S(1)} %slice_bitcast_fusion.15), channel_id=1, source_target_pairs={{0,16},{4,20},{8,24},{12,28},{16,0},{20,4},{24,8},{28,12},{1,17},{... | collective-permute-start | bytes 3981320 | tf_op jit(solution)/shard_map/ppermute | solution.py:157
  1617.7 34.4 %collective-permute-start.93 = (bf16[288,3072]{1,0:T(8,128)(2,1)S(1)}, bf16[288,3072]{1,0:T(8,128)(2,1)S(1)}, u32[]{:S(2)}, u32[]{:S(2)}) collective-permute-start(bf16[288,3072]{1,0:T(8,128)(2,1)S(1)} %pad_maximum_fusion.9), channel_id=1, source_target_pairs={{0,1},{1,0},{2,3},{3,2},{4,5},{5,4},{6,7},{7,6},{8,9},{9,8},{10,11... | collective-permute-start | bytes 5308424 | tf_op jit(solution)/shard_map/ppermute | solution.py:157
  1618.1 32.4 %collective-permute-start.92 = (bf16[288,2304]{1,0:T(8,128)(2,1)S(1)}, bf16[288,2304]{1,0:T(8,128)(2,1)S(1)}, u32[]{:S(2)}, u32[]{:S(2)}) collective-permute-start(bf16[288,2304]{1,0:T(8,128)(2,1)S(1)} %fusion.13), channel_id=1, source_target_pairs={{0,2},{1,3},{2,0},{3,1},{4,6},{5,7},{6,4},{7,5},{8,10},{9,11},{10,... | collective-permute-start | bytes 3981320 | tf_op jit(solution)/shard_map/ppermute | solution.py:157
  1623.4 32.6 %collective-permute-start.94 = (bf16[576,2304]{1,0:T(8,128)(2,1)S(1)}, bf16[576,2304]{1,0:T(8,128)(2,1)S(1)}, u32[]{:S(2)}, u32[]{:S(2)}) collective-permute-start(bf16[576,2304]{1,0:T(8,128)(2,1)S(1)} %pad_maximum_fusion.3), channel_id=1, source_target_pairs={{0,1},{1,0},{2,3},{3,2},{4,5},{5,4},{6,7},{7,6},{8,9},{9,8},{10,11... | collective-permute-start | bytes 7962632 | tf_op jit(solution)/shard_map/ppermute | solution.py:157
  1626.2 60.3 %collective-permute-start.91 = (bf16[288,2304]{1,0:T(8,128)(2,1)}, bf16[288,2304]{1,0:T(8,128)(2,1)}, u32[]{:S(2)}, u32[]{:S(2)}) collective-permute-start(bf16[288,2304]{1,0:T(8,128)(2,1)} %slice_bitcast_fusion.16), channel_id=1, source_target_pairs={{0,16},{4,20},{8,24},{12,28},{16,0},{20,4},{24,8},{28,12},{1,17},{... | collective-permute-start | bytes 3981320 | tf_op jit(solution)/shard_map/ppermute | solution.py:157
  1686.5 33.4 %collective-permute-start.99 = (bf16[576,2304]{1,0:T(8,128)(2,1)S(1)}, bf16[576,2304]{1,0:T(8,128)(2,1)S(1)}, u32[]{:S(2)}, u32[]{:S(2)}) collective-permute-start(bf16[576,2304]{1,0:T(8,128)(2,1)S(1)} %copy-done.25), channel_id=1, source_target_pairs={{0,1},{1,0},{2,3},{3,2},{4,5},{5,4},{6,7},{7,6},{8,9},{9,8},{10,11... | collective-permute-start | bytes 7962632 | tf_op jit(solution)/shard_map/ppermute | solution.py:157
  1688.2 31.6 %collective-permute-start.98 = (bf16[288,2304]{1,0:T(8,128)(2,1)S(1)}, bf16[288,2304]{1,0:T(8,128)(2,1)S(1)}, u32[]{:S(2)}, u32[]{:S(2)}) collective-permute-start(bf16[288,2304]{1,0:T(8,128)(2,1)S(1)} %fusion.12), channel_id=1, source_target_pairs={{0,2},{1,3},{2,0},{3,1},{4,6},{5,7},{6,4},{7,5},{8,10},{9,11},{10,... | collective-permute-start | bytes 3981320 | tf_op jit(solution)/shard_map/ppermute | solution.py:157
  (199 other events, 3108.3 us)

commit v7 on v6

--- a/solution.py
+++ b/solution.py
@@ -351,32 +351,37 @@
     )(info, *pieces, scale, *weights)
 
 
-def unpack_kernel(pieces, grad_ref, *refs):
-    refs[-1][0] = grad_ref[...].astype(f32)
-
-
-def unpack(grad, pieces, matrix, held):
+def unpack_kernel(pieces, *refs, parts):
+    first = 0
+    for ref in refs[:parts]:
+        width = ref.shape[1]
+        refs[-1][0, :, first : first + width] = ref[...].astype(f32)
+        first += width
+
+
+def unpack(grads, pieces, matrix, held):
     steps = pieces.shape[0]
-    rows, cols = grad.shape
+    rows = grads[0].shape[0]
+    cols = sum(g.shape[1] for g in grads)
     piece = rows // steps
     grid_spec = pltpu.PrefetchScalarGridSpec(
         num_scalar_prefetch=1,
         grid=(steps,),
-        in_specs=[pl.BlockSpec((piece, cols), lambda j, p: (j, 0))]
+        in_specs=[pl.BlockSpec((piece, g.shape[1]), lambda j, p: (j, 0)) for g in grads]
         + [pl.BlockSpec(memory_space=pl.ANY)] * len(held),
         out_specs=pl.BlockSpec((1, piece, cols), lambda j, p: (matrix, p[j], 0)),
     )
     return pl.pallas_call(
-        unpack_kernel,
+        functools.partial(unpack_kernel, parts=len(grads)),
         grid_spec=grid_spec,
         out_shape=jax.ShapeDtypeStruct((3, rows, cols), f32),
-        input_output_aliases={2: 0} if held else {},
+        input_output_aliases={1 + len(grads): 0} if held else {},
         compiler_params=pltpu.CompilerParams(vmem_limit_bytes=VMEM_LIMIT),
         cost_estimate=pl.CostEstimate(
             flops=rows * cols, bytes_accessed=6 * rows * cols, transcendentals=0
         ),
         name="unpack",
-    )(pieces, grad, *held)
+    )(pieces, *grads, *held)
 
 
 def tile_of(size):
@@ -988,12 +993,9 @@
         query, pair = project(normed[s], proj_weights[s], cosine, sine)
         query_send.append(query.reshape(wide, class_rows, head_cols))
         pair_send.append(pair)
-    own_out = jnp.stack([clock.hold(v)[:, half_proj:] for v in blocks])
-    other_out = jnp.stack([v[:, half_proj:] for v in others])
-    out_own = share([own_out], far_bits)
-    sent = clock.sync(received, *query_send, *pair_send, *out_own)
+    sent = clock.sync(received, *query_send, *pair_send)
     received, sent = sent[0], sent[1:]
-    query_send, pair_send, out_own = sent[:count], sent[count : 2 * count], sent[2 * count :]
+    query_send, pair_send = sent[:count], sent[count:]
 
     def spread(pair):
         held = [pair]
@@ -1016,27 +1018,27 @@
         exact.append(work[1])
         lse.append(work[2])
 
-    out_other = [other_out] + [swap(v, "seq", 1) for v in out_own[1:]]
-    pair_first, *out_other = clock.sync(heads_all_to_all(clock.hold(pair_send[0])), *out_other)
-    gate_held = share([clock.hold(received)], far_bits)
+    pair_first = heads_all_to_all(clock.hold(pair_send[0]))
+    own_out = jnp.stack([clock.hold(v)[:, half_proj:] for v in blocks])
+    other_out = jnp.stack([clock.hold(v)[:, half_proj:] for v in others])
+    pair_first, own_out, other_out = clock.sync(pair_first, own_out, other_out)
+    out_own = share([clock.hold(own_out)], far_bits)
     moved = spread(pair_first)
-    pair_last = heads_all_to_all(clock.hold(pair_send[1]))
-    out_weights = out_slices(out_own, out_other, places, info, output_scale, count)
-    work = clock.sync(pair_last, *moved, *out_weights, *gate_held)
-    pair_last, work = work[0], work[1:]
-    pairs.append([pair_first] + work[: classes - 1])
-    out_weights = work[classes - 1 : classes - 1 + count]
-    gate_held = share(work[classes - 1 + count :], seq_bits[:1])
+    pair_last, *work = clock.sync(heads_all_to_all(clock.hold(pair_send[1])), *moved)
+    pairs.append([pair_first] + work)
     part_a, part_b = two_parts(pair_last)
     query = all_to_all(clock.hold(query_send[0]))
-    query, *work = clock.sync(query, *spread(part_a), *gate_held)
-    moved_a, gate_held = work[: classes - 1], work[classes - 1 :]
+    query, *work = clock.sync(query, *spread(part_a), *out_own)
+    moved_a, out_own = work[: classes - 1], work[classes - 1 :]
     queries.append(query.reshape(wide * class_rows, head_cols))
     moved_b = spread(clock.hold(part_b))
     query = all_to_all(clock.hold(query_send[1]))
-    query, *work = clock.sync(query, *moved_b, *attend(0))
-    moved_b = work[: classes - 1]
-    keep_attend(work[classes - 1 :])
+    out_other = [swap(v, "seq", 1) for v in out_own[1:]]
+    gate_held = share([clock.hold(received)], far_bits)
+    query, *work = clock.sync(query, *moved_b, *out_other, *attend(0))
+    moved_b, work = work[: classes - 1], work[classes - 1 :]
+    out_other, work = [other_out] + work[: len(out_other)], work[len(out_other) :]
+    keep_attend(work)
     queries.append(query.reshape(wide * class_rows, head_cols))
     pairs.append(
         [pair_last] + [jnp.concatenate([x, y], axis=0) for x, y in zip(moved_a, moved_b)]
@@ -1062,16 +1064,22 @@
     for s in seqs:
         back = all_to_all(clock.hold(attended_send[s]))
         if s == 0:
-            gate_weights = partner_weights(0, [clock.hold(v) for v in gate_held])
-            back, *work = clock.sync(back, *attend(count - 1), *gate_weights)
-            keep_attend(work[:3])
-            gate_weights = work[3:]
+            out_weights = out_slices(out_own, out_other, places, info, output_scale, count)
+            back, *work = clock.sync(back, *gate_held, *out_weights, *attend(count - 1))
+            gate_held, work = work[: len(gate_held)], work[len(gate_held) :]
+            out_weights, work = work[:count], work[count:]
+            keep_attend(work)
         else:
-            back, *work = clock.sync(back, *join(s - 1))
+            gate_held = share(gate_held, seq_bits[:1])
+            back, *work = clock.sync(back, *gate_held, *join(s - 1))
+            gate_held, work = work[: len(gate_held)], work[len(gate_held) :]
             keep_join(work)
         attended.append(heads_to_rows(back))
 
-    received, *work = clock.sync(exchange(1), *join(count - 1))
+    received = exchange(1)
+    gate_weights = partner_weights(0, [clock.hold(v) for v in gate_held])
+    received, *work = clock.sync(received, *gate_weights, *join(count - 1))
+    gate_weights, work = work[:count], work[count:]
     keep_join(work)
 
     def blocks_of(part):
@@ -1339,22 +1347,19 @@
     out_part = low_sum(
         half_dot(all_branch, clock.hold(all_attended), side, half_out), out_sent
     )
-    query, pair_a, out_part, down_move, *work = clock.sync(
-        query, pair_a, out_part, down_move, *attend_back(1)
-    )
-    down_grad = far_end(down_keep, down_move)
+    query, pair_a, out_part, *work = clock.sync(query, pair_a, out_part, *attend_back(1))
     query_back.append(query)
     grad_attend.append(work)
     dq, *dkv = grad_attend[1]
     query = all_to_all(clock.hold(dq))
     pair_b = class_sum([clock.hold(v[1]) for v in parts_of_pair])
     up_grad = weight_sum(grad_up, gathered)
-    query, pair_b, up_grad = clock.sync(query, pair_b, up_grad)
+    query, pair_b, down_move, up_grad = clock.sync(query, pair_b, down_move, up_grad)
     query_back.append(query)
 
     out_pieces = {
         t: lax.dynamic_slice_in_dim(
-            out_part, jnp.bitwise_xor(member, t) * split_out, split_out, 1
+            clock.hold(out_part), jnp.bitwise_xor(member, t) * split_out, split_out, 1
         )
         for t in range(members)
     }
@@ -1369,28 +1374,51 @@
     pair = heads_all_to_all(clock.hold(jnp.concatenate([pair_a, pair_b], axis=0)))
     pair_sum = class_sum([clock.hold(v) for v in dkv])
     up_grad = part_sum(up_grad, 1)
-    pair, pair_sum, up_grad, out_piece = clock.sync(pair, pair_sum, up_grad, out_piece)
+    down_grad = far_end(down_keep, down_move)
+    pair, pair_sum, up_grad, down_grad = clock.sync(pair, pair_sum, up_grad, down_grad)
     pair_back.append(pair)
     up_keep, up_move = far_start(up_grad)
     pair = heads_all_to_all(clock.hold(pair_sum))
     gate_grad = weight_sum(grad_gate, gathered)
-    pair, gate_grad = clock.sync(pair, gate_grad)
+    pair, out_piece, gate_grad = clock.sync(pair, out_piece, gate_grad)
     pair_back.append(pair)
 
-    def owner_start(grad):
-        return grad[0], swap(clock.hold(grad[1]), "wide", half_wide)
-
-    down_own, down_other = owner_start(down_grad)
-    grad_proj = turn_back(
-        [v.reshape(KEY_VALUE_HEADS, rows, head_cols) for v in query_back], pair_back, cosine, sine
-    )
-    proj_sent = swap(half_dot(all_normed, grad_proj, 1 - side, half_proj).astype(bf16), "seq", 1)
-    gate_grad = part_sum(gate_grad, 1)
-    proj_part = low_sum(half_dot(all_normed, grad_proj, side, half_proj), proj_sent)
-    down_other, proj_part, gate_grad, up_move = clock.sync(
-        down_other, proj_part, gate_grad, up_move
-    )
-    up_grad = far_end(up_keep, up_move)
+    def column_parts(value, count):
+        width = value.shape[1] // count
+        return [value[:, i * width : (i + 1) * width] for i in range(count)]
+
+    def exchange_grad(part):
+        return swap(clock.hold(part), "wide", half_wide)
+
+    def half_sum(grad):
+        split = grad.reshape(2, 2, grad.shape[1] // 2, model_dim)
+        return split[:, 0], split[:, 1]
+
+    down_own = column_parts(down_grad[0], 3)
+    down_send = column_parts(down_grad[1], 3)
+    gate_keep, gate_send = half_sum(gate_grad)
+    gate_moved = swap(gate_send, "seq", 1)
+    moved, grad_proj = clock.sync(
+        exchange_grad(down_send[0]),
+        turn_back(
+            [v.reshape(KEY_VALUE_HEADS, rows, head_cols) for v in query_back],
+            pair_back,
+            cosine,
+            sine,
+        ),
+    )
+    down_other = [moved]
+    moved = exchange_grad(down_send[1])
+    proj_send = half_dot(all_normed, clock.hold(grad_proj), 1 - side, half_proj).astype(bf16)
+    moved, gate_moved, proj_send = clock.sync(moved, gate_moved, proj_send)
+    down_other.append(moved)
+    moved = exchange_grad(down_send[2])
+    proj_sent = swap(proj_send, "seq", 1)
+    gate_grad = low_sum(gate_keep, gate_moved)
+    moved, proj_sent, up_move, gate_grad = clock.sync(moved, proj_sent, up_move, gate_grad)
+    down_other.append(moved)
+    proj_part = low_sum(half_dot(all_normed, clock.hold(grad_proj), side, half_proj), proj_sent)
+    (proj_part,) = clock.sync(proj_part)
     gate_keep, gate_move = far_start(gate_grad)
 
     def part_of(o):
@@ -1403,68 +1431,54 @@
             axis=1,
         )
 
-    def spread_grad(grad, bits):
+    def spread_grad(grads, bits):
         for bit in bits:
-            grad = jnp.concatenate([grad, swap(grad, "seq", bit)], axis=0)
-        return grad
-
-    grad_tokens, gain_first = [], 0.0
-
-    def back_tokens(s):
-        grad_normed = dot(clock.hold(grad_proj[s * rows : (s + 1) * rows]), proj_weights[s], NT)
-        grad_normed = lax.optimization_barrier(grad_normed)
-        grad, gain = norm_back(inputs[s], input_factor[s], gain_attn, grad_normed)
-        return [(grad_middle[s] + grad).astype(bf16), gain]
-
-    down_grad = low_sum(down_own, down_other)
-    ring_work = {}
-
-    def beside_ring(step):
-        if step == 0:
-            return back_tokens(0)
-        if step == 1:
-            return back_tokens(1)
-        if step == 2:
-            ring_work["down"] = spread_grad(clock.hold(down_grad), far_bits)
-            return (gate_move,)
-        if step == half_wide - 1:
-            return (ring_work["down"],)
-        return ()
+            grads = [jnp.concatenate([g, swap(g, "seq", bit)], axis=0) for g in grads]
+        return grads
 
     a, b = halves(clock.hold(part_of(wide // 2)))
     for k in range(wide // 2 - 1, -1, -1):
         step = wide // 2 - 1 - k
-        work = beside_ring(step)
         a, b = hop(a, b, wide)
+        work = []
+        if step == 2:
+            work = [gate_move]
+        elif step == half_wide - 1:
+            down_grad = spread_grad(
+                [low_sum(clock.hold(x), y) for x, y in zip(down_own, down_other)], far_bits
+            )
+            work = down_grad
         a, b, *work = clock.sync(a, b, *work)
-        if step < 2:
-            grad_tokens.append(work[0])
-            gain_first = gain_first + work[1]
-        elif step == 2:
-            gate_grad = far_end(gate_keep, work[0])
+        if step == 2:
+            gate_move = work[0]
         elif step == half_wide - 1:
-            down_grad = work[0]
+            down_grad = work
         if step == 0:
             a, b = add_first(part_of(k), a), add_last(part_of(-k), b)
         elif k > 0:
             a, b = low_sum(part_of(k), a), low_sum(part_of(-k), b)
     total = low_sum(part_of(0), a, b)
+    up_grad = far_end(up_keep, up_move)
+    up_own, up_send = column_parts(up_grad[0], 2), column_parts(up_grad[1], 2)
+    total, *up_send = clock.sync(total, *up_send)
+
+    def input_grad(s):
+        return dot(clock.hold(grad_proj[s * rows : (s + 1) * rows]), proj_weights[s], NT)
+
+    def back_tokens(s, grad_normed):
+        grad, gain = norm_back(inputs[s], input_factor[s], gain_attn, grad_normed)
+        return (grad_middle[s] + grad).astype(bf16), gain
 
     def add_swapped(gains, axis, bits):
         for bit in bits:
             gains = gains + swap(gains, axis, bit)
         return gains
 
-    gains = jnp.stack([gain_first, gain_second, gain_third, gain_fourth])
-    wide_bits = [1 << i for i in range(wide.bit_length() - 1)]
-    (gains,) = clock.sync(add_swapped(clock.hold(gains), "wide", wide_bits[1:]))
-
-    up_own, up_other = owner_start(up_grad)
     proj_total = total[:, :half_proj]
     out_totals = {0: total[:, half_proj:]}
     for bit in seq_bits[1:]:
         sent = jnp.concatenate([proj_total] + [out_totals[t] for t in sorted(out_totals)], axis=1)
-        moved = swap(clock.hold(sent), "seq", bit)
+        moved = swap(sent, "seq", bit)
         proj_total = low_sum(proj_total, moved[:, :half_proj])
         for i, t in enumerate(sorted(out_totals)):
             first = half_proj + i * split_out
@@ -1478,25 +1492,43 @@
         ],
         axis=1,
     )
-    up_other, low = clock.sync(up_other, low)
-    gains = add_swapped(add_swapped(clock.hold(gains), "wide", wide_bits[:1]), "seq", seq_bits)
-    up_grad = low_sum(up_own, up_other)
-    gate_own, gate_other = owner_start(gate_grad)
-    up_grad = spread_grad(clock.hold(up_grad), far_bits)
-    other = swap(low, "seq", 1)
+    moved, grad_first = clock.sync(exchange_grad(up_send[0]), input_grad(0))
+    up_grad = [low_sum(up_own[0], moved)]
+    moved, low, grad_last = clock.sync(exchange_grad(up_send[1]), low, input_grad(1))
+    up_grad.append(low_sum(up_own[1], moved))
+    gate_grad = far_end(gate_keep, gate_move)
+    gate_own, gate_send = column_parts(gate_grad[0], 2), column_parts(gate_grad[1], 2)
+    first_tokens, gain_first = back_tokens(0, grad_first)
+    last_tokens, gain = back_tokens(1, grad_last)
+    gains = jnp.stack([gain_first + gain, gain_second, gain_third, gain_fourth])
+    wide_bits = [1 << i for i in range(wide.bit_length() - 1)]
+    gains, *gate_send = clock.sync(add_swapped(gains, "wide", wide_bits[1:]), *gate_send)
+    moved = exchange_grad(gate_send[0])
+    up_grad = spread_grad([clock.hold(v) for v in up_grad], far_bits)
+    other = swap(clock.hold(low), "seq", 1)
+    moved, other, *up_grad = clock.sync(moved, other, *up_grad)
+    gate_grad = [low_sum(gate_own[0], moved)]
+    moved = exchange_grad(gate_send[1])
+    gate_grad = spread_grad([clock.hold(v) for v in gate_grad], far_bits)
+    gains = add_swapped(add_swapped(gains, "wide", wide_bits[:1]), "seq", seq_bits)
     left, right = jnp.where(is_low, low, other), jnp.where(is_low, other, low)
     attn_grad = jnp.concatenate(
         [left[:, :half_proj], right[:, :half_proj], left[:, half_proj:], right[:, half_proj:]],
         axis=1,
     ).astype(f32)
-    mlp_grad = unpack(spread_grad(clock.hold(down_grad), seq_bits[:1]), pieces, 2, [])
-    gate_other, up_grad, attn_grad, mlp_grad, gains = clock.sync(
-        gate_other, up_grad, attn_grad, mlp_grad, gains
-    )
-    gate_grad = spread_grad(low_sum(gate_own, gate_other), far_bits)
-    mlp_grad = unpack(spread_grad(clock.hold(up_grad), seq_bits[:1]), pieces, 1, [mlp_grad])
-    gate_grad, mlp_grad = clock.sync(gate_grad, mlp_grad)
-    mlp_grad = unpack(spread_grad(gate_grad, seq_bits[:1]), pieces, 0, [mlp_grad])
+    down_grad = spread_grad([clock.hold(v) for v in down_grad], seq_bits[:1])
+    mlp_grad = unpack(down_grad, pieces, 2, [])
+    moved, attn_grad, mlp_grad, gains, *gate_grad = clock.sync(
+        moved, attn_grad, mlp_grad, gains, *gate_grad
+    )
+    last = spread_grad([low_sum(gate_own[1], moved)], far_bits)
+    up_grad = spread_grad([clock.hold(v) for v in up_grad], seq_bits[:1])
+    mlp_grad = unpack(up_grad, pieces, 1, [mlp_grad])
+    gate_grad = spread_grad([clock.hold(v) for v in gate_grad], seq_bits[:1])
+    mlp_grad, *gate_grad = clock.sync(mlp_grad, *gate_grad, *last)
+    gate_grad[1:] = spread_grad(gate_grad[1:], seq_bits[:1])
+    mlp_grad = unpack(gate_grad, pieces, 0, [mlp_grad])
+    grad_tokens = [first_tokens, last_tokens]
     return (
         jnp.stack(layer_out),
         jnp.stack(grad_tokens),

time: 1760 us -> 1730 us (0.983)
  waiting for transfers between devices: 711 us -> 623 us
  starting transfers between devices: 142 us -> 179 us
    ppermute x47 -> x59, waiting for transfers between devices: 388 us -> 327 us  [swap(): return lax.ppermute(value, axis, [(i, i ^ bit) for i in range(size)])]
    ppermute x48, waiting for transfers between devices: 251 us -> 199 us  [hop(): return (lax.ppermute(a, 'wide', up), lax.ppermute(b, 'wide', down))]
    ppermute x6, waiting for transfers between devices: 33.2 us -> 68.1 us  [class_ring(): return lax.ppermute(value, 'wide', perm)]
    ppermute x47 -> x59, starting transfers between devices: 24.9 us -> 55.7 us  [swap(): return lax.ppermute(value, axis, [(i, i ^ bit) for i in range(size)])]
    convert_element_type x25 -> x28, other arithmetic: 51.7 us -> 54.8 us  [low_sum(): return sum((t.astype(f32) for t in terms)).astype(bf16)]
    unnamed x302 -> x318, local copies, waits for them, and re-layouts: 61.5 us -> 59.8 us
  transfers between devices with their start and end apart: 113 -> 125, of which waited for: 57 -> 64; matrix products, arithmetic and copies ran while one was open for 14% -> 16% of each run, Pallas kernels for 26% -> 27%
where the time goes in v7:
time: 1730 us; the launch traced here: 1720 us
  waiting for transfers between devices  623 us (36%)
  Pallas kernels  491 us (28%)
  starting transfers between devices  179 us (10%)
  other arithmetic  153 us (9%)
  local copies, waits for them, and re-layouts  151 us (9%)
  matrix products  121 us (7%)
    ppermute x59, waiting for transfers between devices, swap(): return lax.ppermute(value, axis, [(i, i ^ bit) for i in range(size)])  327 us
    ppermute x48, waiting for transfers between devices, hop(): return (lax.ppermute(a, 'wide', up), lax.ppermute(b, 'wide', down))  199 us
    dot_general x12, matrix products, dot(): return lax.dot_general(a, b, (dims, ((), ())), preferred_element_type=f32)  121 us
    pallas_call x3, Pallas kernels, weight_back(): kernel_call(functools.partial(weight_kernel, count=count), hidden // tile...  87.1 us
    pallas_call x4, Pallas kernels, input_back(): kernel_call(input_back_kernel, tiles, [whole_spec(grad_gate.shape)] * 2 +...  68.5 us
    ppermute x6, waiting for transfers between devices, class_ring(): return lax.ppermute(value, 'wide', perm)  68.1 us
    pallas_call x3, Pallas kernels, open_forward(): kernel_call(open_kernel, tiles, [whole_spec(x.shape)] + [row_spec(tile, d...  62.4 us
    unnamed x318, local copies, waits for them, and re-layouts  59.8 us
  transfers between devices with their start and end apart: 125, of which 64 were waited for; matrix products, arithmetic and copies ran while one was open for 16% of the time, Pallas kernels for 27%

profile of v7, /device:TPU:0, one launch (start us, length us, event | category | flops | bytes accessed | tf_op | source)
XLA Modules:
  0.0 1720.8 jit_solution(17698452903351157744)
XLA Ops:
  12.3 25.0 %own_slices.1 = (bf16[2304,2304]{1,0:T(8,128)(2,1)}, bf16[2304,2304]{1,0:T(8,128)(2,1)}, bf16[2304,2304]{1,0:T(8,128)(2,1)}, bf16[2304,2304]{1,0:T(8,128)(2,1)},...) custom-call(s32[4]{0:T(128)} %pad_add_fusion.pieces, s32[4]{0:T(128)} %pad_add_fusion.1.info, ...), custom_call_target="tpu_custom_call" | custom-call | flops 159252480 | bytes 63700992 | tf_op jit(solution)/shard_map/own_slices/pallas_call | solution.py:297
  49.0 27.9 %collective-permute-done.3.refs_0_ = bf16[288,2560]{1,0:T(8,128)(2,1)} collective-permute-done((bf16[288,2560]{1,0:T(8,128)(2,1)}, bf16[288,2560]{1,0:T(8,128)(2,1)}, u32[]{:S(2)}, u32[]{:S(2)}) %collective-permute-start.3) | collective-permute-done | bytes 1474592 | tf_op jit(solution)/shard_map/ppermute | solution.py:102
  92.3 21.5 %collective-permute-done.7.refs_0_ = bf16[288,2560]{1,0:T(8,128)(2,1)} collective-permute-done((bf16[288,2560]{1,0:T(8,128)(2,1)}, bf16[288,2560]{1,0:T(8,128)(2,1)}, u32[]{:S(2)}, u32[]{:S(2)}) %collective-permute-start.7) | collective-permute-done | bytes 1474592 | tf_op jit(solution)/shard_map/ppermute | solution.py:102
  178.5 25.6 %collective-permute-done.15.refs_0_ = bf16[288,2304]{1,0:T(8,128)(2,1)} collective-permute-done((bf16[288,2304]{1,0:T(8,128)(2,1)}, bf16[288,2304]{1,0:T(8,128)(2,1)}, u32[]{:S(2)}, u32[]{:S(2)}) %collective-permute-start.15) | collective-permute-done | bytes 1327136 | tf_op jit(solution)/shard_map/ppermute | solution.py:157
  243.7 22.1 %collective-permute-done.17.refs_1_ = bf16[4,256,512]{2,1,0:T(8,128)(2,1)} collective-permute-done((bf16[4,256,512]{2,1,0:T(8,128)(2,1)}, bf16[4,256,512]{2,1,0:T(8,128)(2,1)}, u32[]{:S(2)}, u32[]{:S(2)}) %collective-permute-start.17) | collective-permute-done | bytes 1048608 | tf_op jit(solution)/shard_map/ppermute | solution.py:177
  273.8 21.3 %collective-permute-done.18 = bf16[2,256,512]{2,1,0:T(8,128)(2,1)} collective-permute-done((bf16[2,256,512]{2,1,0:T(8,128)(2,1)S(1)}, bf16[2,256,512]{2,1,0:T(8,128)(2,1)}, u32[]{:S(2)}, u32[]{:S(2)}) %collective-permute-start.18) | collective-permute-done | bytes 524320 | tf_op jit(solution)/shard_map/ppermute | solution.py:177
  302.4 11.4 attn_forward.2
  313.8 12.4 collective-permute-done.20
  337.6 20.5 %out_slices.1 = (bf16[2304,2048]{1,0:T(8,128)(2,1)}, bf16[2304,2048]{1,0:T(8,128)(2,1)}) custom-call(s32[8]{0:T(128)} %stack.170.places, s32[4]{0:T(128)} %pad_add_fusion.1.info, bf16[8,288,512]{2,1,0:T(8,128)(2,1)} %bitcast_dynamic-update-slice_fusion.8.refs_0_, bf16[8,288,512]{2,1,0:T(8,128)(2,1)} %collective-permute-done.19.refs_1_, ...), custom_call_target="tpu_custom_call" | custom-call | flops 94371840 | bytes 28311552 | tf_op jit(solution)/shard_map/out_slices/pallas_call | solution.py:260
  360.2 11.4 attn_forward.3
  373.5 14.6 all-to-all-start.5
  398.1 16.0 all-to-all-done.5
  435.1 47.6 %collective-permute-done.25.refs_0_ = bf16[288,2304]{1,0:T(8,128)(2,1)} collective-permute-done((bf16[288,2304]{1,0:T(8,128)(2,1)S(1)}, bf16[288,2304]{1,0:T(8,128)(2,1)}, u32[]{:S(2)}, u32[]{:S(2)}) %collective-permute-start.25) | collective-permute-done | bytes 1327136 | tf_op jit(solution)/shard_map/ppermute | solution.py:157
  483.1 30.8 %collective-permute-done.27.refs_1_ = bf16[288,2304]{1,0:T(8,128)(2,1)S(1)} collective-permute-done((bf16[288,2304]{1,0:T(8,128)(2,1)}, bf16[288,2304]{1,0:T(8,128)(2,1)S(1)}, u32[]{:S(2)}, u32[]{:S(2)}) %collective-permute-start.27) | collective-permute-done | bytes 1327136 | tf_op jit(solution)/shard_map/ppermute | solution.py:157
  514.0 27.9 %collective-permute-done.26.refs_0_ = bf16[288,2304]{1,0:T(8,128)(2,1)} collective-permute-done((bf16[288,2304]{1,0:T(8,128)(2,1)S(1)}, bf16[288,2304]{1,0:T(8,128)(2,1)}, u32[]{:S(2)}, u32[]{:S(2)}) %collective-permute-start.26) | collective-permute-done | bytes 1327136 | tf_op jit(solution)/shard_map/ppermute | solution.py:157
  546.4 25.5 %collective-permute-done.28 = bf16[256,2304]{1,0:T(8,128)(2,1)S(1)} collective-permute-done((bf16[256,2304]{1,0:T(8,128)(2,1)S(1)}, bf16[256,2304]{1,0:T(8,128)(2,1)S(1)}, u32[]{:S(2)}, u32[]{:S(2)}) %collective-permute-start.28) | collective-permute-done | bytes 1179680 | tf_op jit(solution)/shard_map/ppermute | solution.py:102
  599.2 29.0 %open_forward.3 = (f32[1024,2304]{1,0:T(8,128)}, f32[1024,2304]{1,0:T(8,128)}, bf16[1024,2304]{1,0:T(8,128)(2,1)}) custom-call(bf16[1024,2304]{1,0:T(8,128)(2,1)} %constant_dynamic-update-slice_fusion.4.refs_0_.refs_2_, bf16[2304,2304]{1,0:T(8,128)(2,1)} %get-tuple-element.614.refs_1_.refs_2_, bf16[2304,2304]{1,0:T(8,128)(2,1)} %get-tuple-element.615.refs_2_.refs_3_), custom_call_target="tpu_custom_call" | custom-call | flops 21743271936 | bytes 49545216 | tf_op jit(solution)/shard_map/open_forward/pallas_call | solution.py:448
  645.0 14.9 convolution_convert_fusion.3
  663.9 18.1 %open_forward.4 = (f32[1024,2304]{1,0:T(8,128)}, f32[1024,2304]{1,0:T(8,128)}, bf16[1024,2304]{1,0:T(8,128)(2,1)}) custom-call(bf16[1024,2304]{1,0:T(8,128)(2,1)} %constant_dynamic-update-slice_fusion.9.refs_0_.refs_3_, bf16[2304,2304]{1,0:T(8,128)(2,1)} %get-tuple-element.644.refs_1_.refs_2_, bf16[2304,2304]{1,0:T(8,128)(2,1)} %get-tuple-element.645.refs_2_.refs_3_), custom_call_target="tpu_custom_call" | custom-call | flops 12079595520 | bytes 29622272 | tf_op jit(solution)/shard_map/open_forward/pallas_call | solution.py:448
  685.8 15.3 open_forward.5
  717.8 13.5 convolution_convert_fusion.2
  761.5 15.0 open_back.4
  781.7 12.8 open_back.5
  794.5 18.4 %input_back.4.refs_4_ = bf16[1024,2304]{1,0:T(8,128)(2,1)} custom-call(bf16[1024,2304]{1,0:T(8,128)(2,1)} %get-tuple-element.798.refs_0_, bf16[1024,2304]{1,0:T(8,128)(2,1)} %get-tuple-element.781.refs_1_.refs_0_, bf16[2304,2304]{1,0:T(8,128)(2,1)} %get-tuple-element.614.refs_1_.refs_2_, bf16[2304,2304]{1,0:T(8,128)(2,1)} %get-tuple-element.615.refs_2_.refs_3_), custom_call_target="tpu_custom_call" | custom-call | flops 12079595520 | bytes 23855104 | tf_op jit(solution)/shard_map/input_back/pallas_call | solution.py:505
  827.5 15.8 input_back.5
  851.8 12.6 collective-permute-done.55
  870.2 14.9 open_back.6
  891.6 12.8 open_back.7
  904.3 18.5 %input_back.6.refs_4_ = bf16[1024,2304]{1,0:T(8,128)(2,1)} custom-call(bf16[1024,2304]{1,0:T(8,128)(2,1)} %get-tuple-element.799.refs_0_.refs_1_, bf16[1024,2304]{1,0:T(8,128)(2,1)} %get-tuple-element.782.refs_1_, bf16[2304,2304]{1,0:T(8,128)(2,1)} %get-tuple-element.644.refs_1_.refs_2_, bf16[2304,2304]{1,0:T(8,128)(2,1)} %get-tuple-element.645.refs_2_.refs_3_), custom_call_target="tpu_custom_call" | custom-call | flops 12079595520 | bytes 23855104 | tf_op jit(solution)/shard_map/input_back/pallas_call | solution.py:505
  939.2 15.8 input_back.7
  958.7 12.9 collective-permute-done.61
  974.4 29.0 %weight_back.3 = bf16[2304,2304]{1,0:T(8,128)(2,1)} custom-call(bf16[1024,2304]{1,0:T(8,128)(2,1)} %get-tuple-element.736.refs_0_, bf16[1024,2304]{1,0:T(8,128)(2,1)} %get-tuple-element.737.refs_1_, bf16[1024,2304]{1,0:T(8,128)(2,1)} %copy-done.8, bf16[1024,2304]{1,0:T(8,128)(2,1)} %constant_dynamic-update-slice_fusion.19.refs_0_.refs_3_), custom_call_target="tpu_custom_call" | custom-call | flops 21743271936 | bytes 29491200 | tf_op jit(solution)/shard_map/weight_back/pallas_call | solution.py:531
  1056.0 17.4 %attn_backward.2 = (bf16[1024,512]{1,0:T(8,128)(2,1)}, bf16[4,256,512]{2,1,0:T(8,128)(2,1)}, bf16[4,256,512]{2,1,0:T(8,128)(2,1)}) custom-call(s32[1]{0:T(128)} %bitcast.43.info, bf16[1024,512]{1,0:T(8,128)(2,1)} %bitcast.44.q_ref, bf16[1024,512]{1,0:T(8,128)(2,1)} %bitcast.87.grad_ref, f32[1024,512]{1,0:T(8,128)} %get-tuple-element.754.exact_ref, ...), custom_call_target="tpu_custom_call" | custom-call | flops 10737418240 | bytes 9437184 | tf_op jit(solution)/shard_map/attn_backward/pallas_call | solution.py:821
  1084.8 17.6 %attn_backward.3 = (bf16[1024,512]{1,0:T(8,128)(2,1)}, bf16[4,256,512]{2,1,0:T(8,128)(2,1)}, bf16[4,256,512]{2,1,0:T(8,128)(2,1)}) custom-call(s32[1]{0:T(128)} %bitcast.43.info, bf16[1024,512]{1,0:T(8,128)(2,1)} %bitcast.46.q_ref, bf16[1024,512]{1,0:T(8,128)(2,1)} %bitcast.89.grad_ref, f32[1024,512]{1,0:T(8,128)} %get-tuple-element.768.exact_ref, ...), custom_call_target="tpu_custom_call" | custom-call | flops 10737418240 | bytes 9437184 | tf_op jit(solution)/shard_map/attn_backward/pallas_call | solution.py:821
  1116.5 29.1 %weight_back.4 = bf16[2304,2304]{1,0:T(8,128)(2,1)} custom-call(bf16[1024,2304]{1,0:T(8,128)(2,1)} %get-tuple-element.781.refs_1_.refs_0_, bf16[1024,2304]{1,0:T(8,128)(2,1)} %get-tuple-element.782.refs_1_, bf16[1024,2304]{1,0:T(8,128)(2,1)} %constant_dynamic-update-slice_fusion.4.refs_0_.refs_2_, ...), custom_call_target="tpu_custom_call" | custom-call | flops 21743271936 | bytes 29491200 | tf_op jit(solution)/shard_map/weight_back/pallas_call | solution.py:531
  1171.8 12.3 collective-permute-done.70
  1186.6 23.9 %collective-permute-done.72 = bf16[2304,512]{1,0:T(8,128)(2,1)} collective-permute-done((bf16[2304,512]{1,0:T(8,128)(2,1)}, bf16[2304,512]{1,0:T(8,128)(2,1)}, u32[]{:S(2)}, u32[]{:S(2)}) %collective-permute-start.72) | collective-permute-done | bytes 2359328 | tf_op jit(solution)/shard_map/ppermute | solution.py:157
  1226.0 29.0 %weight_back.5 = bf16[2304,2304]{1,0:T(8,128)(2,1)} custom-call(bf16[1024,2304]{1,0:T(8,128)(2,1)} %get-tuple-element.798.refs_0_, bf16[1024,2304]{1,0:T(8,128)(2,1)} %get-tuple-element.799.refs_0_.refs_1_, bf16[1024,2304]{1,0:T(8,128)(2,1)} %constant_dynamic-update-slice_fusion.4.refs_0_.refs_2_, ...), custom_call_target="tpu_custom_call" | custom-call | flops 21743271936 | bytes 29491200 | tf_op jit(solution)/shard_map/weight_back/pallas_call | solution.py:531
  1266.0 13.9 turn_back.1
  1295.4 13.1 collective-permute-done.74
  1321.3 49.3 %collective-permute-done.78 = bf16[2,288,2304]{2,1,0:T(8,128)(2,1)} collective-permute-done((bf16[2,288,2304]{2,1,0:T(8,128)(2,1)}, bf16[2,288,2304]{2,1,0:T(8,128)(2,1)}, u32[]{:S(2)}, u32[]{:S(2)}) %collective-permute-start.78) | collective-permute-done | bytes 2654240 | tf_op jit(solution)/shard_map/ppermute | solution.py:157
  1417.7 24.3 %collective-permute-done.82 = bf16[288,2560]{1,0:T(8,128)(2,1)S(1)} collective-permute-done((bf16[288,2560]{1,0:T(8,128)(2,1)S(1)}, bf16[288,2560]{1,0:T(8,128)(2,1)S(1)}, u32[]{:S(2)}, u32[]{:S(2)}) %collective-permute-start.82) | collective-permute-done | bytes 1474592 | tf_op jit(solution)/shard_map/ppermute | solution.py:102
  1452.8 20.9 %collective-permute-done.85 = bf16[2,288,2304]{2,1,0:T(8,128)(2,1)S(1)} collective-permute-done((bf16[2,288,2304]{2,1,0:T(8,128)(2,1)S(1)}, bf16[2,288,2304]{2,1,0:T(8,128)(2,1)S(1)}, u32[]{:S(2)}, u32[]{:S(2)}) %collective-permute-start.85) | collective-permute-done | bytes 2654240 | tf_op jit(solution)/shard_map/ppermute | solution.py:157
  1522.5 20.5 %fusion.86 = f32[256,2304]{1,0:T(8,128)} fusion(bf16[256,4096]{1,0:T(8,128)(2,1)} %get-tuple-element.848, bf16[2304,4096]{1,0:T(8,128)(2,1)} %get-tuple-element.492.wq_ref.wk_ref.wv_ref), kind=kOutput, calls=%fused_computation.349 | convolution fusion | flops 4831838208 | bytes 23330816 | tf_op jit(solution)/shard_map/dot_general | solution.py:26
  1544.7 20.5 %fusion.87 = f32[256,2304]{1,0:T(8,128)} fusion(bf16[256,4096]{1,0:T(8,128)(2,1)} %get-tuple-element.856, bf16[2304,4096]{1,0:T(8,128)(2,1)} %get-tuple-element.495.wq_ref.wk_ref.wv_ref), kind=kOutput, calls=%fused_computation.350 | convolution fusion | flops 4831838208 | bytes 23330816 | tf_op jit(solution)/shard_map/dot_general | solution.py:26
  1606.5 21.6 %collective-permute-done.106 = f32[4,2304]{1,0:T(4,128)S(1)} collective-permute-done((f32[4,2304]{1,0:T(4,128)S(1)}, f32[4,2304]{1,0:T(4,128)S(1)}, u32[]{:S(2)}, u32[]{:S(2)}) %collective-permute-start.106) | collective-permute-done | bytes 36896 | tf_op jit(solution)/shard_map/ppermute | solution.py:157
  1643.4 11.2 collective-permute-done.107
  1674.6 16.6 collective-permute-done.111
  (782 shorter events, 745.8 us)
Async XLA Ops:
  4.9 36.8 %collective-permute-start = (bf16[288,2560]{1,0:T(8,128)(2,1)}, bf16[288,2560]{1,0:T(8,128)(2,1)}, u32[]{:S(2)}, u32[]{:S(2)}) collective-permute-start(bf16[288,2560]{1,0:T(8,128)(2,1)} %pad_maximum_fusion.11.refs_0_), channel_id=1, source_target_pairs={{0,8},{8,16},{16,24},{24,28},{28,20},{20,12},{12,4},{4,0},{1,9},{9... | collective-permute-start | bytes 4423688 | tf_op jit(solution)/shard_map/ppermute | solution.py:102
  7.9 34.1 %collective-permute-start.1 = (bf16[288,2560]{1,0:T(8,128)(2,1)}, bf16[288,2560]{1,0:T(8,128)(2,1)}, u32[]{:S(2)}, u32[]{:S(2)}) collective-permute-start(bf16[288,2560]{1,0:T(8,128)(2,1)} %pad_maximum_fusion.11.refs_0_), channel_id=1, source_target_pairs={{8,0},{16,8},{24,16},{28,24},{20,28},{12,20},{4,12},{0,4},{9,1},{1... | collective-permute-start | bytes 4423688 | tf_op jit(solution)/shard_map/ppermute | solution.py:102
  7.9 34.1 %collective-permute-start.2 = (bf16[288,2560]{1,0:T(8,128)(2,1)}, bf16[288,2560]{1,0:T(8,128)(2,1)}, u32[]{:S(2)}, u32[]{:S(2)}) collective-permute-start(bf16[288,2560]{1,0:T(8,128)(2,1)} %pad_maximum_fusion.11.refs_0_), channel_id=1, source_target_pairs={{0,1},{1,0},{2,3},{3,2},{4,5},{5,4},{6,7},{7,6},{8,9},{9,8},{10,11... | collective-permute-start | bytes 4423688 | tf_op jit(solution)/shard_map/ppermute | solution.py:157
  42.0 35.0 %collective-permute-start.3 = (bf16[288,2560]{1,0:T(8,128)(2,1)}, bf16[288,2560]{1,0:T(8,128)(2,1)}, u32[]{:S(2)}, u32[]{:S(2)}) collective-permute-start(bf16[288,2560]{1,0:T(8,128)(2,1)} %collective-permute-done.refs_2_), channel_id=1, source_target_pairs={{0,8},{8,16},{16,24},{24,28},{28,20},{20,12},{12,4},{4,0},{1,9},{9... | collective-permute-start | bytes 4423688 | tf_op jit(solution)/shard_map/ppermute | solution.py:102
  43.8 35.0 %collective-permute-start.5 = (bf16[288,2560]{1,0:T(8,128)(2,1)}, bf16[288,2560]{1,0:T(8,128)(2,1)}, u32[]{:S(2)}, u32[]{:S(2)}) collective-permute-start(bf16[288,2560]{1,0:T(8,128)(2,1)} %collective-permute-done.refs_2_), channel_id=1, source_target_pairs={{0,1},{1,0},{2,3},{3,2},{4,5},{5,4},{6,7},{7,6},{8,9},{9,8},{10,11... | collective-permute-start | bytes 4423688 | tf_op jit(solution)/shard_map/ppermute | solution.py:157
  44.0 34.8 %collective-permute-start.4 = (bf16[288,2560]{1,0:T(8,128)(2,1)}, bf16[288,2560]{1,0:T(8,128)(2,1)}, u32[]{:S(2)}, u32[]{:S(2)}) collective-permute-start(bf16[288,2560]{1,0:T(8,128)(2,1)} %collective-permute-done.1.refs_4_), channel_id=1, source_target_pairs={{8,0},{16,8},{24,16},{28,24},{20,28},{12,20},{4,12},{0,4},{9,1},{1... | collective-permute-start | bytes 4423688 | tf_op jit(solution)/shard_map/ppermute | solution.py:102
  44.3 34.5 %collective-permute-start.6 = (bf16[288,2560]{1,0:T(8,128)(2,1)}, bf16[288,2560]{1,0:T(8,128)(2,1)}, u32[]{:S(2)}, u32[]{:S(2)}) collective-permute-start(bf16[288,2560]{1,0:T(8,128)(2,1)} %collective-permute-done.1.refs_4_), channel_id=1, source_target_pairs={{0,1},{1,0},{2,3},{3,2},{4,5},{5,4},{6,7},{7,6},{8,9},{9,8},{10,11... | collective-permute-start | bytes 4423688 | tf_op jit(solution)/shard_map/ppermute | solution.py:157
  78.8 35.0 %collective-permute-start.7 = (bf16[288,2560]{1,0:T(8,128)(2,1)}, bf16[288,2560]{1,0:T(8,128)(2,1)}, u32[]{:S(2)}, u32[]{:S(2)}) collective-permute-start(bf16[288,2560]{1,0:T(8,128)(2,1)} %collective-permute-done.3.refs_0_), channel_id=1, source_target_pairs={{0,8},{8,16},{16,24},{24,28},{28,20},{20,12},{12,4},{4,0},{1,9},{9... | collective-permute-start | bytes 4423688 | tf_op jit(solution)/shard_map/ppermute | solution.py:102
  80.4 34.7 %collective-permute-start.8 = (bf16[288,2560]{1,0:T(8,128)(2,1)}, bf16[288,2560]{1,0:T(8,128)(2,1)}, u32[]{:S(2)}, u32[]{:S(2)}) collective-permute-start(bf16[288,2560]{1,0:T(8,128)(2,1)} %collective-permute-done.4.refs_2_), channel_id=1, source_target_pairs={{8,0},{16,8},{24,16},{28,24},{20,28},{12,20},{4,12},{0,4},{9,1},{1... | collective-permute-start | bytes 4423688 | tf_op jit(solution)/shard_map/ppermute | solution.py:102
  80.9 34.2 %collective-permute-start.9 = (bf16[288,2560]{1,0:T(8,128)(2,1)}, bf16[288,2560]{1,0:T(8,128)(2,1)}, u32[]{:S(2)}, u32[]{:S(2)}) collective-permute-start(bf16[288,2560]{1,0:T(8,128)(2,1)} %collective-permute-done.3.refs_0_), channel_id=1, source_target_pairs={{0,1},{1,0},{2,3},{3,2},{4,5},{5,4},{6,7},{7,6},{8,9},{9,8},{10,11... | collective-permute-start | bytes 4423688 | tf_op jit(solution)/shard_map/ppermute | solution.py:157
  142.9 61.2 %collective-permute-start.15 = (bf16[288,2304]{1,0:T(8,128)(2,1)}, bf16[288,2304]{1,0:T(8,128)(2,1)}, u32[]{:S(2)}, u32[]{:S(2)}) collective-permute-start(bf16[288,2304]{1,0:T(8,128)(2,1)} %get-tuple-element.483), channel_id=1, source_target_pairs={{0,16},{4,20},{8,24},{12,28},{16,0},{20,4},{24,8},{28,12},{1,17},{... | collective-permute-start | bytes 3981320 | tf_op jit(solution)/shard_map/ppermute | solution.py:157
  242.1 52.9 %collective-permute-start.19 = (bf16[8,288,512]{2,1,0:T(8,128)(2,1)}, bf16[8,288,512]{2,1,0:T(8,128)(2,1)}, u32[]{:S(2)}, u32[]{:S(2)}) collective-permute-start(bf16[8,288,512]{2,1,0:T(8,128)(2,1)} %bitcast_dynamic-update-slice_fusion.8.refs_0_), channel_id=1, source_target_pairs={{0,2},{1,3},{2,0},{3,1},{4,6},{5,7},{6,4},{7,5},{8,10},{9,11},{10,... | collective-permute-start | bytes 7077896 | tf_op jit(solution)/shard_map/ppermute | solution.py:157
  327.2 44.4 %all-to-all-start.4 = ((bf16[8,128,512]{2,1,0:T(8,128)(2,1)}), bf16[8,128,512]{2,1,0:T(8,128)(2,1)S(1)}, u32[]{:S(2)}, u32[]{:S(2)}) async-start(bf16[8,128,512]{2,1,0:T(8,128)(2,1)} %bitcast.290), calls=%async_computation.4 | async-start | bytes 2097152 | tf_op jit(solution)/shard_map/all_to_all | solution.py:161
  332.9 38.8 %collective-permute-start.22 = (bf16[288,2304]{1,0:T(8,128)(2,1)}, bf16[288,2304]{1,0:T(8,128)(2,1)}, u32[]{:S(2)}, u32[]{:S(2)}) collective-permute-start(bf16[288,2304]{1,0:T(8,128)(2,1)} %collective-permute-done.15.refs_0_), channel_id=1, source_target_pairs={{0,2},{1,3},{2,0},{3,1},{4,6},{5,7},{6,4},{7,5},{8,10},{9,11},{10,... | collective-permute-start | bytes 3981320 | tf_op jit(solution)/shard_map/ppermute | solution.py:157
  373.5 40.6 %all-to-all-start.5 = ((bf16[8,128,512]{2,1,0:T(8,128)(2,1)}), bf16[8,128,512]{2,1,0:T(8,128)(2,1)}, u32[]{:S(2)}, u32[]{:S(2)}) async-start(bf16[8,128,512]{2,1,0:T(8,128)(2,1)} %bitcast.292), calls=%async_computation.5 | async-start | bytes 2097152 | tf_op jit(solution)/shard_map/all_to_all | solution.py:161
  423.3 59.4 %collective-permute-start.25 = (bf16[288,2304]{1,0:T(8,128)(2,1)S(1)}, bf16[288,2304]{1,0:T(8,128)(2,1)}, u32[]{:S(2)}, u32[]{:S(2)}) collective-permute-start(bf16[288,2304]{1,0:T(8,128)(2,1)S(1)} %copy-done.66), channel_id=1, source_target_pairs={{0,16},{4,20},{8,24},{12,28},{16,0},{20,4},{24,8},{28,12},{1,17},{... | collective-permute-start | bytes 3981320 | tf_op jit(solution)/shard_map/ppermute | solution.py:157
  482.7 31.3 %collective-permute-start.27 = (bf16[288,2304]{1,0:T(8,128)(2,1)}, bf16[288,2304]{1,0:T(8,128)(2,1)S(1)}, u32[]{:S(2)}, u32[]{:S(2)}) collective-permute-start(bf16[288,2304]{1,0:T(8,128)(2,1)} %collective-permute-done.25.refs_0_), channel_id=1, source_target_pairs={{0,2},{1,3},{2,0},{3,1},{4,6},{5,7},{6,4},{7,5},{8,10},{9,11},{10,... | collective-permute-start | bytes 3981320 | tf_op jit(solution)/shard_map/ppermute | solution.py:157
  483.1 58.8 %collective-permute-start.26 = (bf16[288,2304]{1,0:T(8,128)(2,1)S(1)}, bf16[288,2304]{1,0:T(8,128)(2,1)}, u32[]{:S(2)}, u32[]{:S(2)}) collective-permute-start(bf16[288,2304]{1,0:T(8,128)(2,1)S(1)} %copy-done.65), channel_id=1, source_target_pairs={{0,16},{4,20},{8,24},{12,28},{16,0},{20,4},{24,8},{28,12},{1,17},{... | collective-permute-start | bytes 3981320 | tf_op jit(solution)/shard_map/ppermute | solution.py:157
  541.9 31.4 %collective-permute-start.32 = (bf16[288,2304]{1,0:T(8,128)(2,1)}, bf16[288,2304]{1,0:T(8,128)(2,1)}, u32[]{:S(2)}, u32[]{:S(2)}) collective-permute-start(bf16[288,2304]{1,0:T(8,128)(2,1)} %collective-permute-done.26.refs_0_), channel_id=1, source_target_pairs={{0,2},{1,3},{2,0},{3,1},{4,6},{5,7},{6,4},{7,5},{8,10},{9,11},{10,... | collective-permute-start | bytes 3981320 | tf_op jit(solution)/shard_map/ppermute | solution.py:157
  595.4 33.9 %collective-permute-start.37 = (bf16[256,2304]{1,0:T(8,128)(2,1)S(1)}, bf16[256,2304]{1,0:T(8,128)(2,1)S(1)}, u32[]{:S(2)}, u32[]{:S(2)}) collective-permute-start(bf16[256,2304]{1,0:T(8,128)(2,1)S(1)} %multiply_convert_fusion), channel_id=1, source_target_pairs={{0,8},{8,12},{12,4},{4,0},{16,24},{24,28},{28,20},{20,16},{1,9},{9... | collective-permute-start | bytes 3538952 | tf_op jit(solution)/shard_map/ppermute | solution.py:102
  597.1 32.1 %collective-permute-start.38 = (bf16[256,2304]{1,0:T(8,128)(2,1)S(1)}, bf16[256,2304]{1,0:T(8,128)(2,1)S(1)}, u32[]{:S(2)}, u32[]{:S(2)}) collective-permute-start(bf16[256,2304]{1,0:T(8,128)(2,1)S(1)} %multiply_convert_fusion), channel_id=1, source_target_pairs={{8,0},{12,8},{4,12},{0,4},{24,16},{28,24},{20,28},{16,20},{9,1},{1... | collective-permute-start | bytes 3538952 | tf_op jit(solution)/shard_map/ppermute | solution.py:102
  778.4 34.5 %collective-permute-start.52 = (bf16[256,2304]{1,0:T(8,128)(2,1)S(1)}, bf16[256,2304]{1,0:T(8,128)(2,1)S(1)}, u32[]{:S(2)}, u32[]{:S(2)}) collective-permute-start(bf16[256,2304]{1,0:T(8,128)(2,1)S(1)} %pad_maximum_fusion.21), channel_id=1, source_target_pairs={{8,0},{12,8},{4,12},{0,4},{24,16},{28,24},{20,28},{16,20},{9,1},{1... | collective-permute-start | bytes 3538952 | tf_op jit(solution)/shard_map/ppermute | solution.py:102
  779.5 33.4 %collective-permute-start.51 = (bf16[256,2304]{1,0:T(8,128)(2,1)}, bf16[256,2304]{1,0:T(8,128)(2,1)S(1)}, u32[]{:S(2)}, u32[]{:S(2)}) collective-permute-start(bf16[256,2304]{1,0:T(8,128)(2,1)} %pad_maximum_fusion.20), channel_id=1, source_target_pairs={{0,8},{8,12},{12,4},{4,0},{16,24},{24,28},{28,20},{20,16},{1,9},{9... | collective-permute-start | bytes 3538952 | tf_op jit(solution)/shard_map/ppermute | solution.py:102
  888.1 34.8 %collective-permute-start.60 = (bf16[256,2304]{1,0:T(8,128)(2,1)}, bf16[256,2304]{1,0:T(8,128)(2,1)S(1)}, u32[]{:S(2)}, u32[]{:S(2)}) collective-permute-start(bf16[256,2304]{1,0:T(8,128)(2,1)} %pad_maximum_fusion.23), channel_id=1, source_target_pairs={{8,0},{12,8},{4,12},{0,4},{24,16},{28,24},{20,28},{16,20},{9,1},{1... | collective-permute-start | bytes 3538952 | tf_op jit(solution)/shard_map/ppermute | solution.py:102
  890.4 32.4 %collective-permute-start.59 = (bf16[256,2304]{1,0:T(8,128)(2,1)}, bf16[256,2304]{1,0:T(8,128)(2,1)}, u32[]{:S(2)}, u32[]{:S(2)}) collective-permute-start(bf16[256,2304]{1,0:T(8,128)(2,1)} %pad_maximum_fusion.22), channel_id=1, source_target_pairs={{0,8},{8,12},{12,4},{4,0},{16,24},{24,28},{28,20},{20,16},{1,9},{9... | collective-permute-start | bytes 3538952 | tf_op jit(solution)/shard_map/ppermute | solution.py:102
  972.0 31.4 %collective-permute-start.64 = (bf16[256,2304]{1,0:T(8,128)(2,1)S(1)}, bf16[256,2304]{1,0:T(8,128)(2,1)S(1)}, u32[]{:S(2)}, u32[]{:S(2)}) collective-permute-start(bf16[256,2304]{1,0:T(8,128)(2,1)S(1)} %pad_maximum_fusion.25), channel_id=1, source_target_pairs={{8,0},{12,8},{4,12},{0,4},{24,16},{28,24},{20,28},{16,20},{9,1},{1... | collective-permute-start | bytes 3538952 | tf_op jit(solution)/shard_map/ppermute | solution.py:102
  1078.4 69.1 %collective-permute-start.69 = (bf16[2,288,2304]{2,1,0:T(8,128)(2,1)}, bf16[2,288,2304]{2,1,0:T(8,128)(2,1)}, u32[]{:S(2)}, u32[]{:S(2)}) collective-permute-start(bf16[2,288,2304]{2,1,0:T(8,128)(2,1)} %slice_bitcast_fusion.11), channel_id=1, source_target_pairs={{0,2},{1,3},{2,0},{3,1},{4,6},{5,7},{6,4},{7,5},{8,10},{9,11},{10,... | collective-permute-start | bytes 7962632 | tf_op jit(solution)/shard_map/ppermute | solution.py:157
  1110.7 34.8 %collective-permute-start.68 = (bf16[2,256,512]{2,1,0:T(8,128)(2,1)}, bf16[2,256,512]{2,1,0:T(8,128)(2,1)}, u32[]{:S(2)}, u32[]{:S(2)}) collective-permute-start(bf16[2,256,512]{2,1,0:T(8,128)(2,1)} %get-tuple-element.778), channel_id=1, source_target_pairs={{0,4},{4,0},{8,12},{12,8},{16,20},{20,16},{24,28},{28,24},{1,5},{5... | collective-permute-start | bytes 1572872 | tf_op jit(solution)/shard_map/ppermute | solution.py:177
  1112.1 35.4 %all-to-all-start.9 = ((bf16[8,128,512]{2,1,0:T(8,128)(2,1)}), bf16[8,128,512]{2,1,0:T(8,128)(2,1)S(1)}, u32[]{:S(2)}, u32[]{:S(2)}) async-start(bf16[8,128,512]{2,1,0:T(8,128)(2,1)} %bitcast.291), calls=%async_computation.9 | async-start | bytes 2097152 | tf_op jit(solution)/shard_map/all_to_all | solution.py:161
  1153.1 61.7 %collective-permute-start.71 = (bf16[2,576,2304]{2,1,0:T(8,128)(2,1)}, bf16[2,576,2304]{2,1,0:T(8,128)(2,1)}, u32[]{:S(2)}, u32[]{:S(2)}) collective-permute-start(bf16[2,576,2304]{2,1,0:T(8,128)(2,1)} %slice_bitcast_fusion.2), channel_id=1, source_target_pairs={{0,1},{1,0},{2,3},{3,2},{4,5},{5,4},{6,7},{7,6},{8,9},{9,8},{10,11... | collective-permute-start | bytes 15925256 | tf_op jit(solution)/shard_map/ppermute | solution.py:157
  1156.4 54.1 %collective-permute-start.72 = (bf16[2304,512]{1,0:T(8,128)(2,1)}, bf16[2304,512]{1,0:T(8,128)(2,1)}, u32[]{:S(2)}, u32[]{:S(2)}) collective-permute-start(bf16[2304,512]{1,0:T(8,128)(2,1)} %constant_dynamic-slice_fusion.16), channel_id=1, source_target_pairs={{0,2},{1,3},{2,0},{3,1},{4,6},{5,7},{6,4},{7,5},{8,10},{9,11},{10,... | collective-permute-start | bytes 7077896 | tf_op jit(solution)/shard_map/ppermute | solution.py:157
  1162.5 58.4 %all-to-all-start.10 = ((bf16[4,256,512]{2,1,0:T(8,128)(2,1)}), bf16[4,256,512]{2,1,0:T(8,128)(2,1)S(1)}, u32[]{:S(2)}, u32[]{:S(2)}) async-start(bf16[4,256,512]{2,1,0:T(8,128)(2,1)} %pad_maximum_fusion.26), calls=%async_computation.10 | async-start | bytes 2097152 | tf_op jit(solution)/shard_map/all_to_all | solution.py:168
  1220.9 34.1 %all-to-all-start.11 = ((bf16[4,256,512]{2,1,0:T(8,128)(2,1)}), bf16[4,256,512]{2,1,0:T(8,128)(2,1)S(1)}, u32[]{:S(2)}, u32[]{:S(2)}) async-start(bf16[4,256,512]{2,1,0:T(8,128)(2,1)} %add_convert_fusion.11), calls=%async_computation.11 | async-start | bytes 2097152 | tf_op jit(solution)/shard_map/all_to_all | solution.py:168
  1261.4 47.0 %collective-permute-start.75 = (bf16[2,576,2304]{2,1,0:T(8,128)(2,1)}, bf16[2,576,2304]{2,1,0:T(8,128)(2,1)}, u32[]{:S(2)}, u32[]{:S(2)}) collective-permute-start(bf16[2,576,2304]{2,1,0:T(8,128)(2,1)} %slice_bitcast_fusion.1), channel_id=1, source_target_pairs={{0,1},{1,0},{2,3},{3,2},{4,5},{5,4},{6,7},{7,6},{8,9},{9,8},{10,11... | collective-permute-start | bytes 15925256 | tf_op jit(solution)/shard_map/ppermute | solution.py:157
  1308.5 62.1 %collective-permute-start.77 = (bf16[2304,2048]{1,0:T(8,128)(2,1)}, bf16[2304,2048]{1,0:T(8,128)(2,1)}, u32[]{:S(2)}, u32[]{:S(2)}) collective-permute-start(bf16[2304,2048]{1,0:T(8,128)(2,1)} %convolution_convert_fusion), channel_id=1, source_target_pairs={{0,1},{1,0},{2,3},{3,2},{4,5},{5,4},{6,7},{7,6},{8,9},{9,8},{10,11... | collective-permute-start | bytes 28311560 | tf_op jit(solution)/shard_map/ppermute | solution.py:157
  1310.3 60.3 %collective-permute-start.78 = (bf16[2,288,2304]{2,1,0:T(8,128)(2,1)}, bf16[2,288,2304]{2,1,0:T(8,128)(2,1)}, u32[]{:S(2)}, u32[]{:S(2)}) collective-permute-start(bf16[2,288,2304]{2,1,0:T(8,128)(2,1)} %slice_bitcast_fusion.9), channel_id=1, source_target_pairs={{0,2},{1,3},{2,0},{3,1},{4,6},{5,7},{6,4},{7,5},{8,10},{9,11},{10,... | collective-permute-start | bytes 7962632 | tf_op jit(solution)/shard_map/ppermute | solution.py:157
  1313.4 57.1 %collective-permute-start.76 = (bf16[288,768]{1,0:T(8,128)(2,1)S(1)}, bf16[288,768]{1,0:T(8,128)(2,1)S(1)}, u32[]{:S(2)}, u32[]{:S(2)}) collective-permute-start(bf16[288,768]{1,0:T(8,128)(2,1)S(1)} %get-tuple-element.812), channel_id=1, source_target_pairs={{0,16},{4,20},{8,24},{12,28},{16,0},{20,4},{24,8},{28,12},{1,17},{... | collective-permute-start | bytes 1327112 | tf_op jit(solution)/shard_map/ppermute | solution.py:157
  1408.9 33.1 %collective-permute-start.82 = (bf16[288,2560]{1,0:T(8,128)(2,1)S(1)}, bf16[288,2560]{1,0:T(8,128)(2,1)S(1)}, u32[]{:S(2)}, u32[]{:S(2)}) collective-permute-start(bf16[288,2560]{1,0:T(8,128)(2,1)S(1)} %pad_maximum_fusion.13), channel_id=1, source_target_pairs={{8,0},{16,8},{24,16},{28,24},{20,28},{12,20},{4,12},{0,4},{9,1},{1... | collective-permute-start | bytes 4423688 | tf_op jit(solution)/shard_map/ppermute | solution.py:102
  1412.3 32.5 %collective-permute-start.81 = (bf16[288,2560]{1,0:T(8,128)(2,1)S(1)}, bf16[288,2560]{1,0:T(8,128)(2,1)S(1)}, u32[]{:S(2)}, u32[]{:S(2)}) collective-permute-start(bf16[288,2560]{1,0:T(8,128)(2,1)S(1)} %fusion.41), channel_id=1, source_target_pairs={{0,8},{8,16},{16,24},{24,28},{28,20},{20,12},{12,4},{4,0},{1,9},{9... | collective-permute-start | bytes 4423688 | tf_op jit(solution)/shard_map/ppermute | solution.py:102
  1415.9 57.8 %collective-permute-start.85 = (bf16[2,288,2304]{2,1,0:T(8,128)(2,1)S(1)}, bf16[2,288,2304]{2,1,0:T(8,128)(2,1)S(1)}, u32[]{:S(2)}, u32[]{:S(2)}) collective-permute-start(bf16[2,288,2304]{2,1,0:T(8,128)(2,1)S(1)} %slice_bitcast_fusion.8), channel_id=1, source_target_pairs={{0,2},{1,3},{2,0},{3,1},{4,6},{5,7},{6,4},{7,5},{8,10},{9,11},{10,... | collective-permute-start | bytes 7962632 | tf_op jit(solution)/shard_map/ppermute | solution.py:157
  1445.2 31.5 %collective-permute-start.84 = (bf16[288,2560]{1,0:T(8,128)(2,1)S(1)}, bf16[288,2560]{1,0:T(8,128)(2,1)S(1)}, u32[]{:S(2)}, u32[]{:S(2)}) collective-permute-start(bf16[288,2560]{1,0:T(8,128)(2,1)S(1)} %add_convert_fusion.6), channel_id=1, source_target_pairs={{8,0},{16,8},{24,16},{28,24},{20,28},{12,20},{4,12},{0,4},{9,1},{1... | collective-permute-start | bytes 4423688 | tf_op jit(solution)/shard_map/ppermute | solution.py:102
  1447.2 31.3 %collective-permute-start.83 = (bf16[288,2560]{1,0:T(8,128)(2,1)S(1)}, bf16[288,2560]{1,0:T(8,128)(2,1)S(1)}, u32[]{:S(2)}, u32[]{:S(2)}) collective-permute-start(bf16[288,2560]{1,0:T(8,128)(2,1)S(1)} %add_convert_fusion.7), channel_id=1, source_target_pairs={{0,8},{8,16},{16,24},{24,28},{28,20},{20,12},{12,4},{4,0},{1,9},{9... | collective-permute-start | bytes 4423688 | tf_op jit(solution)/shard_map/ppermute | solution.py:102
  1513.4 31.2 %collective-permute-start.91 = (bf16[288,1152]{1,0:T(8,128)(2,1)}, bf16[288,1152]{1,0:T(8,128)(2,1)}, u32[]{:S(2)}, u32[]{:S(2)}) collective-permute-start(bf16[288,1152]{1,0:T(8,128)(2,1)} %get-tuple-element.847), channel_id=1, source_target_pairs={{0,16},{4,20},{8,24},{12,28},{16,0},{20,4},{24,8},{28,12},{1,17},{... | collective-permute-start | bytes 1990664 | tf_op jit(solution)/shard_map/ppermute | solution.py:157
  1584.9 48.7 %collective-permute-start.97 = (bf16[288,3072]{1,0:T(8,128)(2,1)}, bf16[288,3072]{1,0:T(8,128)(2,1)}, u32[]{:S(2)}, u32[]{:S(2)}) collective-permute-start(bf16[288,3072]{1,0:T(8,128)(2,1)} %pad_maximum_fusion.7), channel_id=1, source_target_pairs={{0,1},{1,0},{2,3},{3,2},{4,5},{5,4},{6,7},{7,6},{8,9},{9,8},{10,11... | collective-permute-start | bytes 5308424 | tf_op jit(solution)/shard_map/ppermute | solution.py:157
  1587.6 40.5 %collective-permute-start.99 = (bf16[288,1152]{1,0:T(8,128)(2,1)}, bf16[288,1152]{1,0:T(8,128)(2,1)}, u32[]{:S(2)}, u32[]{:S(2)}) collective-permute-start(bf16[288,1152]{1,0:T(8,128)(2,1)} %get-tuple-element.869), channel_id=1, source_target_pairs={{0,2},{1,3},{2,0},{3,1},{4,6},{5,7},{6,4},{7,5},{8,10},{9,11},{10,... | collective-permute-start | bytes 1990664 | tf_op jit(solution)/shard_map/ppermute | solution.py:157
  1597.6 31.9 %collective-permute-start.98 = (bf16[288,1152]{1,0:T(8,128)(2,1)}, bf16[288,1152]{1,0:T(8,128)(2,1)S(1)}, u32[]{:S(2)}, u32[]{:S(2)}) collective-permute-start(bf16[288,1152]{1,0:T(8,128)(2,1)} %get-tuple-element.867), channel_id=1, source_target_pairs={{0,2},{1,3},{2,0},{3,1},{4,6},{5,7},{6,4},{7,5},{8,10},{9,11},{10,... | collective-permute-start | bytes 1990664 | tf_op jit(solution)/shard_map/ppermute | solution.py:157
  1601.5 32.1 %collective-permute-start.96 = (bf16[288,1152]{1,0:T(8,128)(2,1)S(1)}, bf16[288,1152]{1,0:T(8,128)(2,1)S(1)}, u32[]{:S(2)}, u32[]{:S(2)}) collective-permute-start(bf16[288,1152]{1,0:T(8,128)(2,1)S(1)} %copy-done.80), channel_id=1, source_target_pairs={{0,16},{4,20},{8,24},{12,28},{16,0},{20,4},{24,8},{28,12},{1,17},{... | collective-permute-start | bytes 1990664 | tf_op jit(solution)/shard_map/ppermute | solution.py:157
  1640.1 32.5 %collective-permute-start.100 = (bf16[288,1152]{1,0:T(8,128)(2,1)S(1)}, bf16[288,1152]{1,0:T(8,128)(2,1)}, u32[]{:S(2)}, u32[]{:S(2)}) collective-permute-start(bf16[288,1152]{1,0:T(8,128)(2,1)S(1)} %copy-done.79), channel_id=1, source_target_pairs={{0,16},{4,20},{8,24},{12,28},{16,0},{20,4},{24,8},{28,12},{1,17},{... | collective-permute-start | bytes 1990664 | tf_op jit(solution)/shard_map/ppermute | solution.py:157
  (219 other events, 3428.6 us)

commit v8 on v7

--- a/solution.py
+++ b/solution.py
@@ -1304,12 +1304,16 @@
             total = low_sum(dkv[step % classes], class_ring(total))
         return total
 
-    def far_start(grad):
+    def far_parts(grad):
         split = grad.reshape(2, 2, grad.shape[1] // 2, model_dim)
-        return split[:, 0], swap(clock.hold(split[:, 1]), "seq", seq_bits[1])
-
-    def far_end(kept, moved):
-        grad = low_sum(kept, moved)
+        send = split[:, 1]
+        return split[:, 0], [send[:, :, : model_dim // 2], send[:, :, model_dim // 2 :]]
+
+    def far_move(part):
+        return swap(clock.hold(part), "seq", seq_bits[1])
+
+    def far_join(kept, moved):
+        grad = low_sum(kept, jnp.concatenate(moved, axis=2))
         for bit in seq_bits[2:]:
             grad = part_sum(grad, bit)
         return grad
@@ -1332,10 +1336,14 @@
     def half_dot(left, right, which, size):
         return dot(left, lax.dynamic_slice_in_dim(right, which * size, size, 1), TN)
 
-    down_keep, down_move = far_start(down_grad)
+    down_keep, down_parts = far_parts(down_grad)
+    down_moved = [far_move(down_parts[0])]
     back = all_to_all(clock.hold(grad_send[1]))
     out_send = half_dot(all_branch, clock.hold(all_attended), 1 - side, half_out).astype(bf16)
-    back, out_send, *work = clock.sync(back, out_send, *attend_back(0))
+    back, down_moved[0], out_send, *work = clock.sync(
+        back, down_moved[0], out_send, *attend_back(0)
+    )
+    down_moved.append(far_move(down_parts[1]))
     grad_heads.append(heads_of(back))
     grad_attend.append(work)
 
@@ -1347,40 +1355,54 @@
     out_part = low_sum(
         half_dot(all_branch, clock.hold(all_attended), side, half_out), out_sent
     )
-    query, pair_a, out_part, *work = clock.sync(query, pair_a, out_part, *attend_back(1))
+    query, pair_a, down_moved[1], out_part, *work = clock.sync(
+        query, pair_a, down_moved[1], out_part, *attend_back(1)
+    )
+    down_grad = far_join(down_keep, down_moved)
     query_back.append(query)
     grad_attend.append(work)
     dq, *dkv = grad_attend[1]
     query = all_to_all(clock.hold(dq))
     pair_b = class_sum([clock.hold(v[1]) for v in parts_of_pair])
-    up_grad = weight_sum(grad_up, gathered)
-    query, pair_b, down_move, up_grad = clock.sync(query, pair_b, down_move, up_grad)
-    query_back.append(query)
-
     out_pieces = {
         t: lax.dynamic_slice_in_dim(
             clock.hold(out_part), jnp.bitwise_xor(member, t) * split_out, split_out, 1
         )
         for t in range(members)
     }
-    for bit in seq_bits[1:]:
-        for t in sorted(out_pieces):
-            if not t & (bit // 2) and t | (bit // 2) in out_pieces:
-                out_pieces[t] = low_sum(
-                    out_pieces[t], swap(out_pieces.pop(t | (bit // 2)), "seq", bit)
-                )
-    out_piece = out_pieces[0]
+    out_moved = []
+    if members == 2:
+        out_parts = [out_pieces[1][:, : split_out // 2], out_pieces[1][:, split_out // 2 :]]
+        out_moved.append(swap(out_parts[0], "seq", seq_bits[1]))
+    else:
+        for bit in seq_bits[1:]:
+            for t in sorted(out_pieces):
+                if not t & (bit // 2) and t | (bit // 2) in out_pieces:
+                    out_pieces[t] = low_sum(
+                        out_pieces[t], swap(out_pieces.pop(t | (bit // 2)), "seq", bit)
+                    )
+    up_grad = weight_sum(grad_up, gathered)
+    query, pair_b, down_grad, up_grad, *out_moved = clock.sync(
+        query, pair_b, down_grad, up_grad, *out_moved
+    )
+    query_back.append(query)
 
     pair = heads_all_to_all(clock.hold(jnp.concatenate([pair_a, pair_b], axis=0)))
     pair_sum = class_sum([clock.hold(v) for v in dkv])
     up_grad = part_sum(up_grad, 1)
-    down_grad = far_end(down_keep, down_move)
-    pair, pair_sum, up_grad, down_grad = clock.sync(pair, pair_sum, up_grad, down_grad)
+    if members == 2:
+        out_moved.append(swap(clock.hold(out_parts[1]), "seq", seq_bits[1]))
+    pair, pair_sum, up_grad, *out_moved = clock.sync(pair, pair_sum, up_grad, *out_moved)
+    out_piece = out_pieces[0]
+    if out_moved:
+        out_piece = low_sum(out_piece, jnp.concatenate(out_moved, axis=1))
     pair_back.append(pair)
-    up_keep, up_move = far_start(up_grad)
+    up_keep, up_parts = far_parts(up_grad)
+    up_moved = [far_move(up_parts[0])]
     pair = heads_all_to_all(clock.hold(pair_sum))
     gate_grad = weight_sum(grad_gate, gathered)
-    pair, out_piece, gate_grad = clock.sync(pair, out_piece, gate_grad)
+    pair, up_moved[0], gate_grad = clock.sync(pair, up_moved[0], gate_grad)
+    up_moved.append(far_move(up_parts[1]))
     pair_back.append(pair)
 
     def column_parts(value, count):
@@ -1410,17 +1432,20 @@
     down_other = [moved]
     moved = exchange_grad(down_send[1])
     proj_send = half_dot(all_normed, clock.hold(grad_proj), 1 - side, half_proj).astype(bf16)
-    moved, gate_moved, proj_send = clock.sync(moved, gate_moved, proj_send)
+    moved, gate_moved, up_moved[1], proj_send = clock.sync(
+        moved, gate_moved, up_moved[1], proj_send
+    )
     down_other.append(moved)
+    up_grad = far_join(up_keep, up_moved)
     moved = exchange_grad(down_send[2])
     proj_sent = swap(proj_send, "seq", 1)
     gate_grad = low_sum(gate_keep, gate_moved)
-    moved, proj_sent, up_move, gate_grad = clock.sync(moved, proj_sent, up_move, gate_grad)
+    moved, proj_sent, up_grad, gate_grad = clock.sync(moved, proj_sent, up_grad, gate_grad)
     down_other.append(moved)
+    gate_keep, gate_parts = far_parts(gate_grad)
+    down_grad = [low_sum(x, y) for x, y in zip(down_own, down_other)]
     proj_part = low_sum(half_dot(all_normed, clock.hold(grad_proj), side, half_proj), proj_sent)
     (proj_part,) = clock.sync(proj_part)
-    gate_keep, gate_move = far_start(gate_grad)
-
     def part_of(o):
         first = index_at(o) * attn_rows
         return jnp.concatenate(
@@ -1437,20 +1462,18 @@
         return grads
 
     a, b = halves(clock.hold(part_of(wide // 2)))
+    gate_moved = []
     for k in range(wide // 2 - 1, -1, -1):
         step = wide // 2 - 1 - k
         a, b = hop(a, b, wide)
         work = []
-        if step == 2:
-            work = [gate_move]
+        if step in (1, 2):
+            work = [far_move(gate_parts[step - 1])]
         elif step == half_wide - 1:
-            down_grad = spread_grad(
-                [low_sum(clock.hold(x), y) for x, y in zip(down_own, down_other)], far_bits
-            )
-            work = down_grad
+            work = spread_grad([clock.hold(v) for v in down_grad], far_bits)
         a, b, *work = clock.sync(a, b, *work)
-        if step == 2:
-            gate_move = work[0]
+        if step in (1, 2):
+            gate_moved += work
         elif step == half_wide - 1:
             down_grad = work
         if step == 0:
@@ -1458,9 +1481,9 @@
         elif k > 0:
             a, b = low_sum(part_of(k), a), low_sum(part_of(-k), b)
     total = low_sum(part_of(0), a, b)
-    up_grad = far_end(up_keep, up_move)
+    gate_grad = far_join(gate_keep, gate_moved)
     up_own, up_send = column_parts(up_grad[0], 2), column_parts(up_grad[1], 2)
-    total, *up_send = clock.sync(total, *up_send)
+    total, gate_grad, *up_send = clock.sync(total, gate_grad, *up_send)
 
     def input_grad(s):
         return dot(clock.hold(grad_proj[s * rows : (s + 1) * rows]), proj_weights[s], NT)
@@ -1496,7 +1519,6 @@
     up_grad = [low_sum(up_own[0], moved)]
     moved, low, grad_last = clock.sync(exchange_grad(up_send[1]), low, input_grad(1))
     up_grad.append(low_sum(up_own[1], moved))
-    gate_grad = far_end(gate_keep, gate_move)
     gate_own, gate_send = column_parts(gate_grad[0], 2), column_parts(gate_grad[1], 2)
     first_tokens, gain_first = back_tokens(0, grad_first)
     last_tokens, gain = back_tokens(1, grad_last)
@@ -1510,7 +1532,6 @@
     gate_grad = [low_sum(gate_own[0], moved)]
     moved = exchange_grad(gate_send[1])
     gate_grad = spread_grad([clock.hold(v) for v in gate_grad], far_bits)
-    gains = add_swapped(add_swapped(gains, "wide", wide_bits[:1]), "seq", seq_bits)
     left, right = jnp.where(is_low, low, other), jnp.where(is_low, other, low)
     attn_grad = jnp.concatenate(
         [left[:, :half_proj], right[:, :half_proj], left[:, half_proj:], right[:, half_proj:]],
@@ -1518,14 +1539,14 @@
     ).astype(f32)
     down_grad = spread_grad([clock.hold(v) for v in down_grad], seq_bits[:1])
     mlp_grad = unpack(down_grad, pieces, 2, [])
-    moved, attn_grad, mlp_grad, gains, *gate_grad = clock.sync(
-        moved, attn_grad, mlp_grad, gains, *gate_grad
-    )
+    moved, attn_grad, mlp_grad, *gate_grad = clock.sync(moved, attn_grad, mlp_grad, *gate_grad)
     last = spread_grad([low_sum(gate_own[1], moved)], far_bits)
     up_grad = spread_grad([clock.hold(v) for v in up_grad], seq_bits[:1])
     mlp_grad = unpack(up_grad, pieces, 1, [mlp_grad])
     gate_grad = spread_grad([clock.hold(v) for v in gate_grad], seq_bits[:1])
-    mlp_grad, *gate_grad = clock.sync(mlp_grad, *gate_grad, *last)
+    gains = add_swapped(clock.hold(gains), "wide", wide_bits[:1])
+    gains = add_swapped(add_swapped(gains, "seq", seq_bits[:1]), "seq", seq_bits[1:])
+    mlp_grad, gains, *gate_grad = clock.sync(mlp_grad, gains, *gate_grad, *last)
     gate_grad[1:] = spread_grad(gate_grad[1:], seq_bits[:1])
     mlp_grad = unpack(gate_grad, pieces, 0, [mlp_grad])
     grad_tokens = [first_tokens, last_tokens]

time: 1730 us -> 1680 us (0.971)
  waiting for transfers between devices: 623 us -> 579 us
  starting transfers between devices: 179 us -> 150 us
    ppermute x48, waiting for transfers between devices: 199 us -> 168 us  [hop(): return (lax.ppermute(a, 'wide', up), lax.ppermute(b, 'wide', down))]
    ppermute x59 -> x63, starting transfers between devices: 55.7 us -> 34 us  [swap(): return lax.ppermute(value, axis, [(i, i ^ bit) for i in range(size)])]
    ppermute x59 -> x63, waiting for transfers between devices: 327 us -> 311 us  [swap(): return lax.ppermute(value, axis, [(i, i ^ bit) for i in range(size)])]
    convert_element_type x28 -> x27, other arithmetic: 54.8 us -> 62.9 us  [low_sum(): return sum((t.astype(f32) for t in terms)).astype(bf16)]
    unnamed x318 -> x314, local copies, waits for them, and re-layouts: 59.8 us -> 60.6 us
  transfers between devices with their start and end apart: 125 -> 129, of which waited for: 64 -> 64; matrix products, arithmetic and copies ran while one was open for 16% -> 17% of each run, Pallas kernels for 27% -> 28%
where the time goes in v8:
time: 1680 us; the launch traced here: 1660 us
  waiting for transfers between devices  579 us (34%)
  Pallas kernels  492 us (29%)
  other arithmetic  161 us (10%)
  local copies, waits for them, and re-layouts  156 us (9%)
  starting transfers between devices  150 us (9%)
  matrix products  120 us (7%)
    ppermute x63, waiting for transfers between devices, swap(): return lax.ppermute(value, axis, [(i, i ^ bit) for i in range(size)])  311 us
    ppermute x48, waiting for transfers between devices, hop(): return (lax.ppermute(a, 'wide', up), lax.ppermute(b, 'wide', down))  168 us
    dot_general x12, matrix products, dot(): return lax.dot_general(a, b, (dims, ((), ())), preferred_element_type=f32)  120 us
    pallas_call x3, Pallas kernels, weight_back(): kernel_call(functools.partial(weight_kernel, count=count), hidden // tile...  87.3 us
    ppermute x6, waiting for transfers between devices, class_ring(): return lax.ppermute(value, 'wide', perm)  73 us
    pallas_call x4, Pallas kernels, input_back(): kernel_call(input_back_kernel, tiles, [whole_spec(grad_gate.shape)] * 2 +...  68.4 us
    convert_element_type x27, other arithmetic, low_sum(): return sum((t.astype(f32) for t in terms)).astype(bf16)  62.9 us
    pallas_call x3, Pallas kernels, open_forward(): kernel_call(open_kernel, tiles, [whole_spec(x.shape)] + [row_spec(tile, d...  62.5 us
  transfers between devices with their start and end apart: 129, of which 64 were waited for; matrix products, arithmetic and copies ran while one was open for 17% of the time, Pallas kernels for 28%

profile of v8, /device:TPU:0, one launch (start us, length us, event | category | flops | bytes accessed | tf_op | source)
XLA Modules:
  0.0 1660.0 jit_solution(15516875469038782174)
XLA Ops:
  12.2 25.0 %own_slices.1 = (bf16[2304,2304]{1,0:T(8,128)(2,1)}, bf16[2304,2304]{1,0:T(8,128)(2,1)}, bf16[2304,2304]{1,0:T(8,128)(2,1)}, bf16[2304,2304]{1,0:T(8,128)(2,1)},...) custom-call(s32[4]{0:T(128)} %pad_add_fusion.pieces, s32[4]{0:T(128)} %pad_add_fusion.1.info, ...), custom_call_target="tpu_custom_call" | custom-call | flops 159252480 | bytes 63700992 | tf_op jit(solution)/shard_map/own_slices/pallas_call | solution.py:297
  49.0 27.9 %collective-permute-done.3.refs_0_ = bf16[288,2560]{1,0:T(8,128)(2,1)} collective-permute-done((bf16[288,2560]{1,0:T(8,128)(2,1)}, bf16[288,2560]{1,0:T(8,128)(2,1)}, u32[]{:S(2)}, u32[]{:S(2)}) %collective-permute-start.3) | collective-permute-done | bytes 1474592 | tf_op jit(solution)/shard_map/ppermute | solution.py:102
  92.3 21.4 %collective-permute-done.7.refs_0_ = bf16[288,2560]{1,0:T(8,128)(2,1)} collective-permute-done((bf16[288,2560]{1,0:T(8,128)(2,1)}, bf16[288,2560]{1,0:T(8,128)(2,1)}, u32[]{:S(2)}, u32[]{:S(2)}) %collective-permute-start.7) | collective-permute-done | bytes 1474592 | tf_op jit(solution)/shard_map/ppermute | solution.py:102
  156.7 10.9 project.3
  178.5 25.4 %collective-permute-done.15.refs_0_ = bf16[288,2304]{1,0:T(8,128)(2,1)} collective-permute-done((bf16[288,2304]{1,0:T(8,128)(2,1)}, bf16[288,2304]{1,0:T(8,128)(2,1)}, u32[]{:S(2)}, u32[]{:S(2)}) %collective-permute-start.15) | collective-permute-done | bytes 1327136 | tf_op jit(solution)/shard_map/ppermute | solution.py:157
  243.6 22.1 %collective-permute-done.17.refs_1_ = bf16[4,256,512]{2,1,0:T(8,128)(2,1)} collective-permute-done((bf16[4,256,512]{2,1,0:T(8,128)(2,1)}, bf16[4,256,512]{2,1,0:T(8,128)(2,1)}, u32[]{:S(2)}, u32[]{:S(2)}) %collective-permute-start.17) | collective-permute-done | bytes 1048608 | tf_op jit(solution)/shard_map/ppermute | solution.py:177
  273.7 21.3 %collective-permute-done.18 = bf16[2,256,512]{2,1,0:T(8,128)(2,1)} collective-permute-done((bf16[2,256,512]{2,1,0:T(8,128)(2,1)S(1)}, bf16[2,256,512]{2,1,0:T(8,128)(2,1)}, u32[]{:S(2)}, u32[]{:S(2)}) %collective-permute-start.18) | collective-permute-done | bytes 524320 | tf_op jit(solution)/shard_map/ppermute | solution.py:177
  302.3 11.5 attn_forward.2
  313.7 12.4 collective-permute-done.20
  337.5 20.6 %out_slices.1 = (bf16[2304,2048]{1,0:T(8,128)(2,1)}, bf16[2304,2048]{1,0:T(8,128)(2,1)}) custom-call(s32[8]{0:T(128)} %stack.170.places, s32[4]{0:T(128)} %pad_add_fusion.1.info, bf16[8,288,512]{2,1,0:T(8,128)(2,1)} %bitcast_dynamic-update-slice_fusion.8.refs_0_, bf16[8,288,512]{2,1,0:T(8,128)(2,1)} %collective-permute-done.19.refs_1_, ...), custom_call_target="tpu_custom_call" | custom-call | flops 94371840 | bytes 28311552 | tf_op jit(solution)/shard_map/out_slices/pallas_call | solution.py:260
  360.2 11.4 attn_forward.3
  389.9 16.0 all-to-all-done.5
  426.8 47.6 %collective-permute-done.25.refs_0_ = bf16[288,2304]{1,0:T(8,128)(2,1)} collective-permute-done((bf16[288,2304]{1,0:T(8,128)(2,1)S(1)}, bf16[288,2304]{1,0:T(8,128)(2,1)}, u32[]{:S(2)}, u32[]{:S(2)}) %collective-permute-start.25) | collective-permute-done | bytes 1327136 | tf_op jit(solution)/shard_map/ppermute | solution.py:157
  474.9 30.8 %collective-permute-done.27.refs_1_ = bf16[288,2304]{1,0:T(8,128)(2,1)S(1)} collective-permute-done((bf16[288,2304]{1,0:T(8,128)(2,1)}, bf16[288,2304]{1,0:T(8,128)(2,1)S(1)}, u32[]{:S(2)}, u32[]{:S(2)}) %collective-permute-start.27) | collective-permute-done | bytes 1327136 | tf_op jit(solution)/shard_map/ppermute | solution.py:157
  505.7 27.9 %collective-permute-done.26.refs_0_ = bf16[288,2304]{1,0:T(8,128)(2,1)} collective-permute-done((bf16[288,2304]{1,0:T(8,128)(2,1)S(1)}, bf16[288,2304]{1,0:T(8,128)(2,1)}, u32[]{:S(2)}, u32[]{:S(2)}) %collective-permute-start.26) | collective-permute-done | bytes 1327136 | tf_op jit(solution)/shard_map/ppermute | solution.py:157
  538.0 25.7 %collective-permute-done.28 = bf16[256,2304]{1,0:T(8,128)(2,1)S(1)} collective-permute-done((bf16[256,2304]{1,0:T(8,128)(2,1)S(1)}, bf16[256,2304]{1,0:T(8,128)(2,1)S(1)}, u32[]{:S(2)}, u32[]{:S(2)}) %collective-permute-start.28) | collective-permute-done | bytes 1179680 | tf_op jit(solution)/shard_map/ppermute | solution.py:102
  590.7 29.1 %open_forward.3 = (f32[1024,2304]{1,0:T(8,128)}, f32[1024,2304]{1,0:T(8,128)}, bf16[1024,2304]{1,0:T(8,128)(2,1)}) custom-call(bf16[1024,2304]{1,0:T(8,128)(2,1)} %constant_dynamic-update-slice_fusion.4.refs_0_.refs_2_, bf16[2304,2304]{1,0:T(8,128)(2,1)} %get-tuple-element.626.refs_1_.refs_2_, bf16[2304,2304]{1,0:T(8,128)(2,1)} %get-tuple-element.627.refs_2_.refs_3_), custom_call_target="tpu_custom_call" | custom-call | flops 21743271936 | bytes 49545216 | tf_op jit(solution)/shard_map/open_forward/pallas_call | solution.py:448
  636.6 14.9 convolution_convert_fusion.3
  655.6 18.1 %open_forward.4 = (f32[1024,2304]{1,0:T(8,128)}, f32[1024,2304]{1,0:T(8,128)}, bf16[1024,2304]{1,0:T(8,128)(2,1)}) custom-call(bf16[1024,2304]{1,0:T(8,128)(2,1)} %constant_dynamic-update-slice_fusion.9.refs_0_.refs_3_, bf16[2304,2304]{1,0:T(8,128)(2,1)} %get-tuple-element.656.refs_1_.refs_2_, bf16[2304,2304]{1,0:T(8,128)(2,1)} %get-tuple-element.657.refs_2_.refs_3_), custom_call_target="tpu_custom_call" | custom-call | flops 12079595520 | bytes 29622272 | tf_op jit(solution)/shard_map/open_forward/pallas_call | solution.py:448
  677.6 15.3 open_forward.5
  709.7 13.5 convolution_convert_fusion.2
  753.4 15.0 open_back.4
  773.6 12.7 open_back.5
  786.3 18.4 %input_back.4.refs_4_ = bf16[1024,2304]{1,0:T(8,128)(2,1)} custom-call(bf16[1024,2304]{1,0:T(8,128)(2,1)} %get-tuple-element.816.refs_0_, bf16[1024,2304]{1,0:T(8,128)(2,1)} %get-tuple-element.795.refs_1_.refs_0_, bf16[2304,2304]{1,0:T(8,128)(2,1)} %get-tuple-element.626.refs_1_.refs_2_, bf16[2304,2304]{1,0:T(8,128)(2,1)} %get-tuple-element.627.refs_2_.refs_3_), custom_call_target="tpu_custom_call" | custom-call | flops 12079595520 | bytes 23855104 | tf_op jit(solution)/shard_map/input_back/pallas_call | solution.py:505
  819.3 15.8 input_back.5
  843.5 12.6 collective-permute-done.55
  862.0 14.9 open_back.6
  883.1 12.8 open_back.7
  895.9 18.4 %input_back.6.refs_4_ = bf16[1024,2304]{1,0:T(8,128)(2,1)} custom-call(bf16[1024,2304]{1,0:T(8,128)(2,1)} %get-tuple-element.817.refs_0_.refs_1_, bf16[1024,2304]{1,0:T(8,128)(2,1)} %get-tuple-element.796.refs_1_, bf16[2304,2304]{1,0:T(8,128)(2,1)} %get-tuple-element.656.refs_1_.refs_2_, bf16[2304,2304]{1,0:T(8,128)(2,1)} %get-tuple-element.657.refs_2_.refs_3_), custom_call_target="tpu_custom_call" | custom-call | flops 12079595520 | bytes 23855104 | tf_op jit(solution)/shard_map/input_back/pallas_call | solution.py:505
  930.6 15.8 input_back.7
  950.2 13.1 collective-permute-done.61
  966.3 29.0 %weight_back.3 = bf16[2304,2304]{1,0:T(8,128)(2,1)} custom-call(bf16[1024,2304]{1,0:T(8,128)(2,1)} %get-tuple-element.748.refs_0_, bf16[1024,2304]{1,0:T(8,128)(2,1)} %get-tuple-element.749.refs_1_, bf16[1024,2304]{1,0:T(8,128)(2,1)} %copy-done.8, bf16[1024,2304]{1,0:T(8,128)(2,1)} %constant_dynamic-update-slice_fusion.19.refs_0_.refs_3_), custom_call_target="tpu_custom_call" | custom-call | flops 21743271936 | bytes 29491200 | tf_op jit(solution)/shard_map/weight_back/pallas_call | solution.py:531
  1051.8 17.5 %attn_backward.2 = (bf16[1024,512]{1,0:T(8,128)(2,1)}, bf16[4,256,512]{2,1,0:T(8,128)(2,1)}, bf16[4,256,512]{2,1,0:T(8,128)(2,1)}) custom-call(s32[1]{0:T(128)} %bitcast.43.info, bf16[1024,512]{1,0:T(8,128)(2,1)} %bitcast.44.q_ref, bf16[1024,512]{1,0:T(8,128)(2,1)} %bitcast.89.grad_ref, f32[1024,512]{1,0:T(8,128)} %get-tuple-element.768.exact_ref, ...), custom_call_target="tpu_custom_call" | custom-call | flops 10737418240 | bytes 9437184 | tf_op jit(solution)/shard_map/attn_backward/pallas_call | solution.py:821
  1080.0 17.5 %attn_backward.3 = (bf16[1024,512]{1,0:T(8,128)(2,1)}, bf16[4,256,512]{2,1,0:T(8,128)(2,1)}, bf16[4,256,512]{2,1,0:T(8,128)(2,1)}) custom-call(s32[1]{0:T(128)} %bitcast.43.info, bf16[1024,512]{1,0:T(8,128)(2,1)} %bitcast.46.q_ref, bf16[1024,512]{1,0:T(8,128)(2,1)} %bitcast.91.grad_ref, f32[1024,512]{1,0:T(8,128)} %get-tuple-element.783.exact_ref, ...), custom_call_target="tpu_custom_call" | custom-call | flops 10737418240 | bytes 9437184 | tf_op jit(solution)/shard_map/attn_backward/pallas_call | solution.py:821
  1122.8 29.2 %weight_back.4 = bf16[2304,2304]{1,0:T(8,128)(2,1)} custom-call(bf16[1024,2304]{1,0:T(8,128)(2,1)} %get-tuple-element.795.refs_1_.refs_0_, bf16[1024,2304]{1,0:T(8,128)(2,1)} %get-tuple-element.796.refs_1_, bf16[1024,2304]{1,0:T(8,128)(2,1)} %constant_dynamic-update-slice_fusion.4.refs_0_.refs_2_, ...), custom_call_target="tpu_custom_call" | custom-call | flops 21743271936 | bytes 29491200 | tf_op jit(solution)/shard_map/weight_back/pallas_call | solution.py:531
  1172.0 17.3 %collective-permute-done.72 = bf16[4,256,512]{2,1,0:T(8,128)(2,1)} collective-permute-done((bf16[4,256,512]{2,1,0:T(8,128)(2,1)}, bf16[4,256,512]{2,1,0:T(8,128)(2,1)}, u32[]{:S(2)}, u32[]{:S(2)}) %collective-permute-start.72) | collective-permute-done | bytes 1048608 | tf_op jit(solution)/shard_map/ppermute | solution.py:177
  1208.7 29.0 %weight_back.5 = bf16[2304,2304]{1,0:T(8,128)(2,1)} custom-call(bf16[1024,2304]{1,0:T(8,128)(2,1)} %get-tuple-element.816.refs_0_, bf16[1024,2304]{1,0:T(8,128)(2,1)} %get-tuple-element.817.refs_0_.refs_1_, bf16[1024,2304]{1,0:T(8,128)(2,1)} %constant_dynamic-update-slice_fusion.4.refs_0_.refs_2_, ...), custom_call_target="tpu_custom_call" | custom-call | flops 21743271936 | bytes 29491200 | tf_op jit(solution)/shard_map/weight_back/pallas_call | solution.py:531
  1250.6 13.9 turn_back.1
  1278.8 13.1 collective-permute-done.77
  1306.8 11.9 collective-permute-done.80
  1338.3 16.2 collective-permute-done.82
  1365.8 25.3 %collective-permute-done.86 = bf16[2,288,1152]{2,1,0:T(8,128)(2,1)} collective-permute-done((bf16[2,288,1152]{2,1,0:T(8,128)(2,1)}, bf16[2,288,1152]{2,1,0:T(8,128)(2,1)}, u32[]{:S(2)}, u32[]{:S(2)}) %collective-permute-start.86) | collective-permute-done | bytes 1327136 | tf_op jit(solution)/shard_map/ppermute | solution.py:157
  1404.6 24.8 %collective-permute-done.89 = bf16[2,288,1152]{2,1,0:T(8,128)(2,1)S(1)} collective-permute-done((bf16[2,288,1152]{2,1,0:T(8,128)(2,1)S(1)}, bf16[2,288,1152]{2,1,0:T(8,128)(2,1)S(1)}, u32[]{:S(2)}, u32[]{:S(2)}) %collective-permute-start.89) | collective-permute-done | bytes 1327136 | tf_op jit(solution)/shard_map/ppermute | solution.py:157
  1464.7 20.6 %fusion.86 = f32[256,2304]{1,0:T(8,128)} fusion(bf16[256,4096]{1,0:T(8,128)(2,1)} %get-tuple-element.871, bf16[2304,4096]{1,0:T(8,128)(2,1)} %get-tuple-element.504.wq_ref.wk_ref.wv_ref), kind=kOutput, calls=%fused_computation.352 | convolution fusion | flops 4831838208 | bytes 23330816 | tf_op jit(solution)/shard_map/dot_general | solution.py:26
  1491.0 20.6 %fusion.87 = f32[256,2304]{1,0:T(8,128)} fusion(bf16[256,4096]{1,0:T(8,128)(2,1)} %get-tuple-element.879, bf16[2304,4096]{1,0:T(8,128)(2,1)} %get-tuple-element.507.wq_ref.wk_ref.wv_ref), kind=kOutput, calls=%fused_computation.353 | convolution fusion | flops 4831838208 | bytes 23330816 | tf_op jit(solution)/shard_map/dot_general | solution.py:26
  1542.5 12.4 collective-permute-done.103
  1556.3 12.3 collective-permute-done.102
  1582.3 11.6 collective-permute-done.108
  (786 shorter events, 736.3 us)
Async XLA Ops:
  4.9 36.7 %collective-permute-start = (bf16[288,2560]{1,0:T(8,128)(2,1)}, bf16[288,2560]{1,0:T(8,128)(2,1)}, u32[]{:S(2)}, u32[]{:S(2)}) collective-permute-start(bf16[288,2560]{1,0:T(8,128)(2,1)} %pad_maximum_fusion.11.refs_0_), channel_id=1, source_target_pairs={{0,8},{8,16},{16,24},{24,28},{28,20},{20,12},{12,4},{4,0},{1,9},{9... | collective-permute-start | bytes 4423688 | tf_op jit(solution)/shard_map/ppermute | solution.py:102
  7.9 34.1 %collective-permute-start.1 = (bf16[288,2560]{1,0:T(8,128)(2,1)}, bf16[288,2560]{1,0:T(8,128)(2,1)}, u32[]{:S(2)}, u32[]{:S(2)}) collective-permute-start(bf16[288,2560]{1,0:T(8,128)(2,1)} %pad_maximum_fusion.11.refs_0_), channel_id=1, source_target_pairs={{8,0},{16,8},{24,16},{28,24},{20,28},{12,20},{4,12},{0,4},{9,1},{1... | collective-permute-start | bytes 4423688 | tf_op jit(solution)/shard_map/ppermute | solution.py:102
  7.9 34.1 %collective-permute-start.2 = (bf16[288,2560]{1,0:T(8,128)(2,1)}, bf16[288,2560]{1,0:T(8,128)(2,1)}, u32[]{:S(2)}, u32[]{:S(2)}) collective-permute-start(bf16[288,2560]{1,0:T(8,128)(2,1)} %pad_maximum_fusion.11.refs_0_), channel_id=1, source_target_pairs={{0,1},{1,0},{2,3},{3,2},{4,5},{5,4},{6,7},{7,6},{8,9},{9,8},{10,11... | collective-permute-start | bytes 4423688 | tf_op jit(solution)/shard_map/ppermute | solution.py:157
  42.0 34.9 %collective-permute-start.3 = (bf16[288,2560]{1,0:T(8,128)(2,1)}, bf16[288,2560]{1,0:T(8,128)(2,1)}, u32[]{:S(2)}, u32[]{:S(2)}) collective-permute-start(bf16[288,2560]{1,0:T(8,128)(2,1)} %collective-permute-done.refs_2_), channel_id=1, source_target_pairs={{0,8},{8,16},{16,24},{24,28},{28,20},{20,12},{12,4},{4,0},{1,9},{9... | collective-permute-start | bytes 4423688 | tf_op jit(solution)/shard_map/ppermute | solution.py:102
  43.7 35.0 %collective-permute-start.5 = (bf16[288,2560]{1,0:T(8,128)(2,1)}, bf16[288,2560]{1,0:T(8,128)(2,1)}, u32[]{:S(2)}, u32[]{:S(2)}) collective-permute-start(bf16[288,2560]{1,0:T(8,128)(2,1)} %collective-permute-done.refs_2_), channel_id=1, source_target_pairs={{0,1},{1,0},{2,3},{3,2},{4,5},{5,4},{6,7},{7,6},{8,9},{9,8},{10,11... | collective-permute-start | bytes 4423688 | tf_op jit(solution)/shard_map/ppermute | solution.py:157
  43.9 34.8 %collective-permute-start.4 = (bf16[288,2560]{1,0:T(8,128)(2,1)}, bf16[288,2560]{1,0:T(8,128)(2,1)}, u32[]{:S(2)}, u32[]{:S(2)}) collective-permute-start(bf16[288,2560]{1,0:T(8,128)(2,1)} %collective-permute-done.1.refs_4_), channel_id=1, source_target_pairs={{8,0},{16,8},{24,16},{28,24},{20,28},{12,20},{4,12},{0,4},{9,1},{1... | collective-permute-start | bytes 4423688 | tf_op jit(solution)/shard_map/ppermute | solution.py:102
  44.2 34.5 %collective-permute-start.6 = (bf16[288,2560]{1,0:T(8,128)(2,1)}, bf16[288,2560]{1,0:T(8,128)(2,1)}, u32[]{:S(2)}, u32[]{:S(2)}) collective-permute-start(bf16[288,2560]{1,0:T(8,128)(2,1)} %collective-permute-done.1.refs_4_), channel_id=1, source_target_pairs={{0,1},{1,0},{2,3},{3,2},{4,5},{5,4},{6,7},{7,6},{8,9},{9,8},{10,11... | collective-permute-start | bytes 4423688 | tf_op jit(solution)/shard_map/ppermute | solution.py:157
  78.7 35.0 %collective-permute-start.7 = (bf16[288,2560]{1,0:T(8,128)(2,1)}, bf16[288,2560]{1,0:T(8,128)(2,1)}, u32[]{:S(2)}, u32[]{:S(2)}) collective-permute-start(bf16[288,2560]{1,0:T(8,128)(2,1)} %collective-permute-done.3.refs_0_), channel_id=1, source_target_pairs={{0,8},{8,16},{16,24},{24,28},{28,20},{20,12},{12,4},{4,0},{1,9},{9... | collective-permute-start | bytes 4423688 | tf_op jit(solution)/shard_map/ppermute | solution.py:102
  80.4 34.7 %collective-permute-start.8 = (bf16[288,2560]{1,0:T(8,128)(2,1)}, bf16[288,2560]{1,0:T(8,128)(2,1)}, u32[]{:S(2)}, u32[]{:S(2)}) collective-permute-start(bf16[288,2560]{1,0:T(8,128)(2,1)} %collective-permute-done.4.refs_2_), channel_id=1, source_target_pairs={{8,0},{16,8},{24,16},{28,24},{20,28},{12,20},{4,12},{0,4},{9,1},{1... | collective-permute-start | bytes 4423688 | tf_op jit(solution)/shard_map/ppermute | solution.py:102
  80.8 34.2 %collective-permute-start.9 = (bf16[288,2560]{1,0:T(8,128)(2,1)}, bf16[288,2560]{1,0:T(8,128)(2,1)}, u32[]{:S(2)}, u32[]{:S(2)}) collective-permute-start(bf16[288,2560]{1,0:T(8,128)(2,1)} %collective-permute-done.3.refs_0_), channel_id=1, source_target_pairs={{0,1},{1,0},{2,3},{3,2},{4,5},{5,4},{6,7},{7,6},{8,9},{9,8},{10,11... | collective-permute-start | bytes 4423688 | tf_op jit(solution)/shard_map/ppermute | solution.py:157
  142.8 61.2 %collective-permute-start.15 = (bf16[288,2304]{1,0:T(8,128)(2,1)}, bf16[288,2304]{1,0:T(8,128)(2,1)}, u32[]{:S(2)}, u32[]{:S(2)}) collective-permute-start(bf16[288,2304]{1,0:T(8,128)(2,1)} %get-tuple-element.495), channel_id=1, source_target_pairs={{0,16},{4,20},{8,24},{12,28},{16,0},{20,4},{24,8},{28,12},{1,17},{... | collective-permute-start | bytes 3981320 | tf_op jit(solution)/shard_map/ppermute | solution.py:157
  242.0 53.0 %collective-permute-start.19 = (bf16[8,288,512]{2,1,0:T(8,128)(2,1)}, bf16[8,288,512]{2,1,0:T(8,128)(2,1)}, u32[]{:S(2)}, u32[]{:S(2)}) collective-permute-start(bf16[8,288,512]{2,1,0:T(8,128)(2,1)} %bitcast_dynamic-update-slice_fusion.8.refs_0_), channel_id=1, source_target_pairs={{0,2},{1,3},{2,0},{3,1},{4,6},{5,7},{6,4},{7,5},{8,10},{9,11},{10,... | collective-permute-start | bytes 7077896 | tf_op jit(solution)/shard_map/ppermute | solution.py:157
  327.1 44.5 %all-to-all-start.4 = ((bf16[8,128,512]{2,1,0:T(8,128)(2,1)}), bf16[8,128,512]{2,1,0:T(8,128)(2,1)S(1)}, u32[]{:S(2)}, u32[]{:S(2)}) async-start(bf16[8,128,512]{2,1,0:T(8,128)(2,1)} %bitcast.289), calls=%async_computation.4 | async-start | bytes 2097152 | tf_op jit(solution)/shard_map/all_to_all | solution.py:161
  332.8 38.8 %collective-permute-start.22 = (bf16[288,2304]{1,0:T(8,128)(2,1)}, bf16[288,2304]{1,0:T(8,128)(2,1)}, u32[]{:S(2)}, u32[]{:S(2)}) collective-permute-start(bf16[288,2304]{1,0:T(8,128)(2,1)} %collective-permute-done.15.refs_0_), channel_id=1, source_target_pairs={{0,2},{1,3},{2,0},{3,1},{4,6},{5,7},{6,4},{7,5},{8,10},{9,11},{10,... | collective-permute-start | bytes 3981320 | tf_op jit(solution)/shard_map/ppermute | solution.py:157
  373.5 32.4 %all-to-all-start.5 = ((bf16[8,128,512]{2,1,0:T(8,128)(2,1)}), bf16[8,128,512]{2,1,0:T(8,128)(2,1)}, u32[]{:S(2)}, u32[]{:S(2)}) async-start(bf16[8,128,512]{2,1,0:T(8,128)(2,1)} %bitcast.290), calls=%async_computation.5 | async-start | bytes 2097152 | tf_op jit(solution)/shard_map/all_to_all | solution.py:161
  415.0 59.4 %collective-permute-start.25 = (bf16[288,2304]{1,0:T(8,128)(2,1)S(1)}, bf16[288,2304]{1,0:T(8,128)(2,1)}, u32[]{:S(2)}, u32[]{:S(2)}) collective-permute-start(bf16[288,2304]{1,0:T(8,128)(2,1)S(1)} %copy-done.67), channel_id=1, source_target_pairs={{0,16},{4,20},{8,24},{12,28},{16,0},{20,4},{24,8},{28,12},{1,17},{... | collective-permute-start | bytes 3981320 | tf_op jit(solution)/shard_map/ppermute | solution.py:157
  474.5 31.3 %collective-permute-start.27 = (bf16[288,2304]{1,0:T(8,128)(2,1)}, bf16[288,2304]{1,0:T(8,128)(2,1)S(1)}, u32[]{:S(2)}, u32[]{:S(2)}) collective-permute-start(bf16[288,2304]{1,0:T(8,128)(2,1)} %collective-permute-done.25.refs_0_), channel_id=1, source_target_pairs={{0,2},{1,3},{2,0},{3,1},{4,6},{5,7},{6,4},{7,5},{8,10},{9,11},{10,... | collective-permute-start | bytes 3981320 | tf_op jit(solution)/shard_map/ppermute | solution.py:157
  474.9 58.8 %collective-permute-start.26 = (bf16[288,2304]{1,0:T(8,128)(2,1)S(1)}, bf16[288,2304]{1,0:T(8,128)(2,1)}, u32[]{:S(2)}, u32[]{:S(2)}) collective-permute-start(bf16[288,2304]{1,0:T(8,128)(2,1)S(1)} %copy-done.66), channel_id=1, source_target_pairs={{0,16},{4,20},{8,24},{12,28},{16,0},{20,4},{24,8},{28,12},{1,17},{... | collective-permute-start | bytes 3981320 | tf_op jit(solution)/shard_map/ppermute | solution.py:157
  533.6 31.4 %collective-permute-start.32 = (bf16[288,2304]{1,0:T(8,128)(2,1)}, bf16[288,2304]{1,0:T(8,128)(2,1)}, u32[]{:S(2)}, u32[]{:S(2)}) collective-permute-start(bf16[288,2304]{1,0:T(8,128)(2,1)} %collective-permute-done.26.refs_0_), channel_id=1, source_target_pairs={{0,2},{1,3},{2,0},{3,1},{4,6},{5,7},{6,4},{7,5},{8,10},{9,11},{10,... | collective-permute-start | bytes 3981320 | tf_op jit(solution)/shard_map/ppermute | solution.py:157
  586.9 34.0 %collective-permute-start.37 = (bf16[256,2304]{1,0:T(8,128)(2,1)S(1)}, bf16[256,2304]{1,0:T(8,128)(2,1)S(1)}, u32[]{:S(2)}, u32[]{:S(2)}) collective-permute-start(bf16[256,2304]{1,0:T(8,128)(2,1)S(1)} %multiply_convert_fusion), channel_id=1, source_target_pairs={{0,8},{8,12},{12,4},{4,0},{16,24},{24,28},{28,20},{20,16},{1,9},{9... | collective-permute-start | bytes 3538952 | tf_op jit(solution)/shard_map/ppermute | solution.py:102
  588.7 32.2 %collective-permute-start.38 = (bf16[256,2304]{1,0:T(8,128)(2,1)S(1)}, bf16[256,2304]{1,0:T(8,128)(2,1)S(1)}, u32[]{:S(2)}, u32[]{:S(2)}) collective-permute-start(bf16[256,2304]{1,0:T(8,128)(2,1)S(1)} %multiply_convert_fusion), channel_id=1, source_target_pairs={{8,0},{12,8},{4,12},{0,4},{24,16},{28,24},{20,28},{16,20},{9,1},{1... | collective-permute-start | bytes 3538952 | tf_op jit(solution)/shard_map/ppermute | solution.py:102
  770.2 34.5 %collective-permute-start.52 = (bf16[256,2304]{1,0:T(8,128)(2,1)S(1)}, bf16[256,2304]{1,0:T(8,128)(2,1)S(1)}, u32[]{:S(2)}, u32[]{:S(2)}) collective-permute-start(bf16[256,2304]{1,0:T(8,128)(2,1)S(1)} %pad_maximum_fusion.21), channel_id=1, source_target_pairs={{8,0},{12,8},{4,12},{0,4},{24,16},{28,24},{20,28},{16,20},{9,1},{1... | collective-permute-start | bytes 3538952 | tf_op jit(solution)/shard_map/ppermute | solution.py:102
  771.4 33.3 %collective-permute-start.51 = (bf16[256,2304]{1,0:T(8,128)(2,1)}, bf16[256,2304]{1,0:T(8,128)(2,1)S(1)}, u32[]{:S(2)}, u32[]{:S(2)}) collective-permute-start(bf16[256,2304]{1,0:T(8,128)(2,1)} %pad_maximum_fusion.20), channel_id=1, source_target_pairs={{0,8},{8,12},{12,4},{4,0},{16,24},{24,28},{28,20},{20,16},{1,9},{9... | collective-permute-start | bytes 3538952 | tf_op jit(solution)/shard_map/ppermute | solution.py:102
  879.8 34.5 %collective-permute-start.60 = (bf16[256,2304]{1,0:T(8,128)(2,1)}, bf16[256,2304]{1,0:T(8,128)(2,1)S(1)}, u32[]{:S(2)}, u32[]{:S(2)}) collective-permute-start(bf16[256,2304]{1,0:T(8,128)(2,1)} %pad_maximum_fusion.23), channel_id=1, source_target_pairs={{8,0},{12,8},{4,12},{0,4},{24,16},{28,24},{20,28},{16,20},{9,1},{1... | collective-permute-start | bytes 3538952 | tf_op jit(solution)/shard_map/ppermute | solution.py:102
  882.1 32.2 %collective-permute-start.59 = (bf16[256,2304]{1,0:T(8,128)(2,1)}, bf16[256,2304]{1,0:T(8,128)(2,1)}, u32[]{:S(2)}, u32[]{:S(2)}) collective-permute-start(bf16[256,2304]{1,0:T(8,128)(2,1)} %pad_maximum_fusion.22), channel_id=1, source_target_pairs={{0,8},{8,12},{12,4},{4,0},{16,24},{24,28},{28,20},{20,16},{1,9},{9... | collective-permute-start | bytes 3538952 | tf_op jit(solution)/shard_map/ppermute | solution.py:102
  963.6 31.7 %collective-permute-start.64 = (bf16[256,2304]{1,0:T(8,128)(2,1)S(1)}, bf16[256,2304]{1,0:T(8,128)(2,1)S(1)}, u32[]{:S(2)}, u32[]{:S(2)}) collective-permute-start(bf16[256,2304]{1,0:T(8,128)(2,1)S(1)} %pad_maximum_fusion.25), channel_id=1, source_target_pairs={{8,0},{12,8},{4,12},{0,4},{24,16},{28,24},{20,28},{16,20},{9,1},{1... | collective-permute-start | bytes 3538952 | tf_op jit(solution)/shard_map/ppermute | solution.py:102
  964.1 31.3 %collective-permute-start.63 = (bf16[256,2304]{1,0:T(8,128)(2,1)S(1)}, bf16[256,2304]{1,0:T(8,128)(2,1)S(1)}, u32[]{:S(2)}, u32[]{:S(2)}) collective-permute-start(bf16[256,2304]{1,0:T(8,128)(2,1)S(1)} %pad_maximum_fusion.24), channel_id=1, source_target_pairs={{0,8},{8,12},{12,4},{4,0},{16,24},{24,28},{28,20},{20,16},{1,9},{9... | collective-permute-start | bytes 3538952 | tf_op jit(solution)/shard_map/ppermute | solution.py:102
  1039.9 31.1 %collective-permute-start.66 = (bf16[2,288,1152]{2,1,0:T(8,128)(2,1)}, bf16[2,288,1152]{2,1,0:T(8,128)(2,1)}, u32[]{:S(2)}, u32[]{:S(2)}) collective-permute-start(bf16[2,288,1152]{2,1,0:T(8,128)(2,1)} %get-tuple-element.762), channel_id=1, source_target_pairs={{0,2},{1,3},{2,0},{3,1},{4,6},{5,7},{6,4},{7,5},{8,10},{9,11},{10,... | collective-permute-start | bytes 3981320 | tf_op jit(solution)/shard_map/ppermute | solution.py:157
  1070.9 34.2 %collective-permute-start.69 = (bf16[2304,1024]{1,0:T(8,128)(2,1)}, bf16[2304,1024]{1,0:T(8,128)(2,1)}, u32[]{:S(2)}, u32[]{:S(2)}) collective-permute-start(bf16[2304,1024]{1,0:T(8,128)(2,1)} %convolution_convert_fusion.1), channel_id=1, source_target_pairs={{0,1},{1,0},{2,3},{3,2},{4,5},{5,4},{6,7},{7,6},{8,9},{9,8},{10,11... | collective-permute-start | bytes 14155784 | tf_op jit(solution)/shard_map/ppermute | solution.py:157
  1070.9 40.7 %collective-permute-start.68 = (bf16[2,288,1152]{2,1,0:T(8,128)(2,1)}, bf16[2,288,1152]{2,1,0:T(8,128)(2,1)}, u32[]{:S(2)}, u32[]{:S(2)}) collective-permute-start(bf16[2,288,1152]{2,1,0:T(8,128)(2,1)} %get-tuple-element.778), channel_id=1, source_target_pairs={{0,2},{1,3},{2,0},{3,1},{4,6},{5,7},{6,4},{7,5},{8,10},{9,11},{10,... | collective-permute-start | bytes 3981320 | tf_op jit(solution)/shard_map/ppermute | solution.py:157
  1075.5 36.1 %all-to-all-start.8 = ((bf16[8,128,512]{2,1,0:T(8,128)(2,1)}), bf16[8,128,512]{2,1,0:T(8,128)(2,1)}, u32[]{:S(2)}, u32[]{:S(2)}) async-start(bf16[8,128,512]{2,1,0:T(8,128)(2,1)} %bitcast.287), calls=%async_computation.8 | async-start | bytes 2097152 | tf_op jit(solution)/shard_map/all_to_all | solution.py:161
  1115.0 42.0 %collective-permute-start.71 = (bf16[2304,256]{1,0:T(8,128)(2,1)}, bf16[2304,256]{1,0:T(8,128)(2,1)S(1)}, u32[]{:S(2)}, u32[]{:S(2)}) collective-permute-start(bf16[2304,256]{1,0:T(8,128)(2,1)} %get-tuple-element.961), channel_id=1, source_target_pairs={{0,2},{1,3},{2,0},{3,1},{4,6},{5,7},{6,4},{7,5},{8,10},{9,11},{10,... | collective-permute-start | bytes 3538952 | tf_op jit(solution)/shard_map/ppermute | solution.py:157
  1116.2 39.6 %collective-permute-start.70 = (bf16[2,256,512]{2,1,0:T(8,128)(2,1)}, bf16[2,256,512]{2,1,0:T(8,128)(2,1)}, u32[]{:S(2)}, u32[]{:S(2)}) collective-permute-start(bf16[2,256,512]{2,1,0:T(8,128)(2,1)} %get-tuple-element.792), channel_id=1, source_target_pairs={{0,4},{4,0},{8,12},{12,8},{16,20},{20,16},{24,28},{28,24},{1,5},{5... | collective-permute-start | bytes 1572872 | tf_op jit(solution)/shard_map/ppermute | solution.py:177
  1118.2 38.8 %all-to-all-start.9 = ((bf16[8,128,512]{2,1,0:T(8,128)(2,1)}), bf16[8,128,512]{2,1,0:T(8,128)(2,1)S(1)}, u32[]{:S(2)}, u32[]{:S(2)}) async-start(bf16[8,128,512]{2,1,0:T(8,128)(2,1)} %bitcast.288), calls=%async_computation.9 | async-start | bytes 2097152 | tf_op jit(solution)/shard_map/all_to_all | solution.py:161
  1166.3 33.1 %all-to-all-start.10 = ((bf16[4,256,512]{2,1,0:T(8,128)(2,1)}), bf16[4,256,512]{2,1,0:T(8,128)(2,1)S(1)}, u32[]{:S(2)}, u32[]{:S(2)}) async-start(bf16[4,256,512]{2,1,0:T(8,128)(2,1)} %pad_maximum_fusion.26), calls=%async_computation.10 | async-start | bytes 2097152 | tf_op jit(solution)/shard_map/all_to_all | solution.py:168
  1203.0 34.7 %collective-permute-start.75 = (bf16[2,288,1152]{2,1,0:T(8,128)(2,1)S(1)}, bf16[2,288,1152]{2,1,0:T(8,128)(2,1)}, u32[]{:S(2)}, u32[]{:S(2)}) collective-permute-start(bf16[2,288,1152]{2,1,0:T(8,128)(2,1)S(1)} %get-tuple-element.815), channel_id=1, source_target_pairs={{0,2},{1,3},{2,0},{3,1},{4,6},{5,7},{6,4},{7,5},{8,10},{9,11},{10,... | collective-permute-start | bytes 3981320 | tf_op jit(solution)/shard_map/ppermute | solution.py:157
  1203.8 33.9 %all-to-all-start.11 = ((bf16[4,256,512]{2,1,0:T(8,128)(2,1)}), bf16[4,256,512]{2,1,0:T(8,128)(2,1)S(1)}, u32[]{:S(2)}, u32[]{:S(2)}) async-start(bf16[4,256,512]{2,1,0:T(8,128)(2,1)} %add_convert_fusion.11), calls=%async_computation.11 | async-start | bytes 2097152 | tf_op jit(solution)/shard_map/all_to_all | solution.py:168
  1244.1 48.9 %collective-permute-start.78 = (bf16[2,576,2304]{2,1,0:T(8,128)(2,1)}, bf16[2,576,2304]{2,1,0:T(8,128)(2,1)}, u32[]{:S(2)}, u32[]{:S(2)}) collective-permute-start(bf16[2,576,2304]{2,1,0:T(8,128)(2,1)} %slice_bitcast_fusion.1), channel_id=1, source_target_pairs={{0,1},{1,0},{2,3},{3,2},{4,5},{5,4},{6,7},{7,6},{8,9},{9,8},{10,11... | collective-permute-start | bytes 15925256 | tf_op jit(solution)/shard_map/ppermute | solution.py:157
  1249.3 42.6 %collective-permute-start.79 = (bf16[2,288,1152]{2,1,0:T(8,128)(2,1)S(1)}, bf16[2,288,1152]{2,1,0:T(8,128)(2,1)S(1)}, u32[]{:S(2)}, u32[]{:S(2)}) collective-permute-start(bf16[2,288,1152]{2,1,0:T(8,128)(2,1)S(1)} %copy-done.65), channel_id=1, source_target_pairs={{0,2},{1,3},{2,0},{3,1},{4,6},{5,7},{6,4},{7,5},{8,10},{9,11},{10,... | collective-permute-start | bytes 3981320 | tf_op jit(solution)/shard_map/ppermute | solution.py:157
  1355.9 35.2 %collective-permute-start.85 = (bf16[288,2560]{1,0:T(8,128)(2,1)}, bf16[288,2560]{1,0:T(8,128)(2,1)}, u32[]{:S(2)}, u32[]{:S(2)}) collective-permute-start(bf16[288,2560]{1,0:T(8,128)(2,1)} %pad_maximum_fusion.13), channel_id=1, source_target_pairs={{8,0},{16,8},{24,16},{28,24},{20,28},{12,20},{4,12},{0,4},{9,1},{1... | collective-permute-start | bytes 4423688 | tf_op jit(solution)/shard_map/ppermute | solution.py:102
  1359.0 33.2 %collective-permute-start.84 = (bf16[288,2560]{1,0:T(8,128)(2,1)}, bf16[288,2560]{1,0:T(8,128)(2,1)}, u32[]{:S(2)}, u32[]{:S(2)}) collective-permute-start(bf16[288,2560]{1,0:T(8,128)(2,1)} %fusion.41), channel_id=1, source_target_pairs={{0,8},{8,16},{16,24},{24,28},{28,20},{20,12},{12,4},{4,0},{1,9},{9... | collective-permute-start | bytes 4423688 | tf_op jit(solution)/shard_map/ppermute | solution.py:102
  1394.5 35.0 %collective-permute-start.88 = (bf16[288,2560]{1,0:T(8,128)(2,1)S(1)}, bf16[288,2560]{1,0:T(8,128)(2,1)S(1)}, u32[]{:S(2)}, u32[]{:S(2)}) collective-permute-start(bf16[288,2560]{1,0:T(8,128)(2,1)S(1)} %add_convert_fusion.6), channel_id=1, source_target_pairs={{8,0},{16,8},{24,16},{28,24},{20,28},{12,20},{4,12},{0,4},{9,1},{1... | collective-permute-start | bytes 4423688 | tf_op jit(solution)/shard_map/ppermute | solution.py:102
  1397.7 31.8 %collective-permute-start.87 = (bf16[288,2560]{1,0:T(8,128)(2,1)S(1)}, bf16[288,2560]{1,0:T(8,128)(2,1)S(1)}, u32[]{:S(2)}, u32[]{:S(2)}) collective-permute-start(bf16[288,2560]{1,0:T(8,128)(2,1)S(1)} %add_convert_fusion.7), channel_id=1, source_target_pairs={{0,8},{8,16},{16,24},{24,28},{28,20},{20,12},{12,4},{4,0},{1,9},{9... | collective-permute-start | bytes 4423688 | tf_op jit(solution)/shard_map/ppermute | solution.py:102
  1429.9 32.1 %collective-permute-start.91 = (bf16[288,2560]{1,0:T(8,128)(2,1)S(1)}, bf16[288,2560]{1,0:T(8,128)(2,1)S(1)}, u32[]{:S(2)}, u32[]{:S(2)}) collective-permute-start(bf16[288,2560]{1,0:T(8,128)(2,1)S(1)} %add_convert_fusion.4), channel_id=1, source_target_pairs={{8,0},{16,8},{24,16},{28,24},{20,28},{12,20},{4,12},{0,4},{9,1},{1... | collective-permute-start | bytes 4423688 | tf_op jit(solution)/shard_map/ppermute | solution.py:102
  1491.0 31.4 %collective-permute-start.96 = (bf16[288,1152]{1,0:T(8,128)(2,1)}, bf16[288,1152]{1,0:T(8,128)(2,1)}, u32[]{:S(2)}, u32[]{:S(2)}) collective-permute-start(bf16[288,1152]{1,0:T(8,128)(2,1)} %get-tuple-element.877), channel_id=1, source_target_pairs={{0,16},{4,20},{8,24},{12,28},{16,0},{20,4},{24,8},{28,12},{1,17},{... | collective-permute-start | bytes 1990664 | tf_op jit(solution)/shard_map/ppermute | solution.py:157
  1534.1 39.0 %collective-permute-start.101 = (bf16[288,3072]{1,0:T(8,128)(2,1)}, bf16[288,3072]{1,0:T(8,128)(2,1)}, u32[]{:S(2)}, u32[]{:S(2)}) collective-permute-start(bf16[288,3072]{1,0:T(8,128)(2,1)} %pad_maximum_fusion.7), channel_id=1, source_target_pairs={{0,1},{1,0},{2,3},{3,2},{4,5},{5,4},{6,7},{7,6},{8,9},{9,8},{10,11... | collective-permute-start | bytes 5308424 | tf_op jit(solution)/shard_map/ppermute | solution.py:157
  1541.8 31.3 %collective-permute-start.100 = (bf16[288,1152]{1,0:T(8,128)(2,1)S(1)}, bf16[288,1152]{1,0:T(8,128)(2,1)S(1)}, u32[]{:S(2)}, u32[]{:S(2)}) collective-permute-start(bf16[288,1152]{1,0:T(8,128)(2,1)S(1)} %copy-done.83), channel_id=1, source_target_pairs={{0,16},{4,20},{8,24},{12,28},{16,0},{20,4},{24,8},{28,12},{1,17},{... | collective-permute-start | bytes 1990664 | tf_op jit(solution)/shard_map/ppermute | solution.py:157
  1578.9 31.9 %collective-permute-start.104 = (bf16[288,1152]{1,0:T(8,128)(2,1)S(1)}, bf16[288,1152]{1,0:T(8,128)(2,1)}, u32[]{:S(2)}, u32[]{:S(2)}) collective-permute-start(bf16[288,1152]{1,0:T(8,128)(2,1)S(1)} %copy-done.82), channel_id=1, source_target_pairs={{0,16},{4,20},{8,24},{12,28},{16,0},{20,4},{24,8},{28,12},{1,17},{... | collective-permute-start | bytes 1990664 | tf_op jit(solution)/shard_map/ppermute | solution.py:157
  (221 other events, 3183.7 us)

commit v9 on v8

--- a/solution.py
+++ b/solution.py
@@ -359,22 +359,24 @@
         first += width
 
 
-def unpack(grads, pieces, matrix, held):
+def unpack(grads, pieces, matrix, held, column=None):
     steps = pieces.shape[0]
     rows = grads[0].shape[0]
     cols = sum(g.shape[1] for g in grads)
+    total = held[0].shape[2] if held else cols
+    first = column or 0
     piece = rows // steps
     grid_spec = pltpu.PrefetchScalarGridSpec(
         num_scalar_prefetch=1,
         grid=(steps,),
         in_specs=[pl.BlockSpec((piece, g.shape[1]), lambda j, p: (j, 0)) for g in grads]
         + [pl.BlockSpec(memory_space=pl.ANY)] * len(held),
-        out_specs=pl.BlockSpec((1, piece, cols), lambda j, p: (matrix, p[j], 0)),
+        out_specs=pl.BlockSpec((1, piece, cols), lambda j, p: (matrix, p[j], first)),
     )
     return pl.pallas_call(
         functools.partial(unpack_kernel, parts=len(grads)),
         grid_spec=grid_spec,
-        out_shape=jax.ShapeDtypeStruct((3, rows, cols), f32),
+        out_shape=jax.ShapeDtypeStruct((3, rows, total), f32),
         input_output_aliases={1 + len(grads): 0} if held else {},
         compiler_params=pltpu.CompilerParams(vmem_limit_bytes=VMEM_LIMIT),
         cost_estimate=pl.CostEstimate(
@@ -1132,7 +1134,8 @@
         if step == 0:
             return open_part(0, None)
         if step == 1:
-            return partner_weights(2, [clock.hold(v) for v in down_held])
+            weights = partner_weights(2, [clock.hold(v) for v in down_held])
+            return [dot(clock.hold(hidden_rows[0]), weights[0], NN).astype(bf16)] + list(weights)
         return ()
 
     a = b = clock.hold(normed_mlp[1])
@@ -1146,10 +1149,10 @@
         if k == 1:
             keep_open(work)
         elif k == 2:
-            down_weights = work
+            parts.append(work[0])
+            down_weights = work[1:]
         blocks += [a, b]
     gathered.append(jnp.concatenate(blocks, axis=0))
-    parts.append(clock.sync(mix(0))[0])
 
     layer_out, grad_mixed, gain_fourth = [], [], 0.0
 
@@ -1243,7 +1246,8 @@
 
     def back_branch(s):
         nonlocal gain_third, gain_second
-        grad, gain = norm_back(middle[s], middle_factor[s], gain_mlp, grad_normed_mlp[s])
+        grad_normed = clock.hold(grad_normed_mlp[s])
+        grad, gain = norm_back(middle[s], middle_factor[s], gain_mlp, grad_normed)
         gain_third = gain_third + gain
         grad_mid = grad_out[s] + grad
         grad, gain = norm_back(branch[s], branch_factor[s], gain_post_attn, grad_mid)
@@ -1352,11 +1356,8 @@
     out_sent = swap(out_send, "seq", 1)
     query = all_to_all(clock.hold(dq))
     pair_a = class_sum([v[0] for v in parts_of_pair])
-    out_part = low_sum(
-        half_dot(all_branch, clock.hold(all_attended), side, half_out), out_sent
-    )
-    query, pair_a, down_moved[1], out_part, *work = clock.sync(
-        query, pair_a, down_moved[1], out_part, *attend_back(1)
+    query, pair_a, down_moved[1], out_sent, *work = clock.sync(
+        query, pair_a, down_moved[1], out_sent, *attend_back(1)
     )
     down_grad = far_join(down_keep, down_moved)
     query_back.append(query)
@@ -1364,16 +1365,24 @@
     dq, *dkv = grad_attend[1]
     query = all_to_all(clock.hold(dq))
     pair_b = class_sum([clock.hold(v[1]) for v in parts_of_pair])
+    up_grad = weight_sum(grad_up, gathered)
+    query, pair_b, down_grad, up_grad = clock.sync(query, pair_b, down_grad, up_grad)
+    query_back.append(query)
+
+    pair = heads_all_to_all(clock.hold(jnp.concatenate([pair_a, pair_b], axis=0)))
+    pair_sum = class_sum([clock.hold(v) for v in dkv])
+    up_grad = part_sum(up_grad, 1)
+    out_part = low_sum(
+        half_dot(all_branch, clock.hold(all_attended), side, half_out), out_sent
+    )
+    pair, pair_sum, up_grad, out_part = clock.sync(pair, pair_sum, up_grad, out_part)
     out_pieces = {
-        t: lax.dynamic_slice_in_dim(
-            clock.hold(out_part), jnp.bitwise_xor(member, t) * split_out, split_out, 1
-        )
+        t: lax.dynamic_slice_in_dim(out_part, jnp.bitwise_xor(member, t) * split_out, split_out, 1)
         for t in range(members)
     }
-    out_moved = []
+    out_parts = None
     if members == 2:
         out_parts = [out_pieces[1][:, : split_out // 2], out_pieces[1][:, split_out // 2 :]]
-        out_moved.append(swap(out_parts[0], "seq", seq_bits[1]))
     else:
         for bit in seq_bits[1:]:
             for t in sorted(out_pieces):
@@ -1381,28 +1390,16 @@
                     out_pieces[t] = low_sum(
                         out_pieces[t], swap(out_pieces.pop(t | (bit // 2)), "seq", bit)
                     )
-    up_grad = weight_sum(grad_up, gathered)
-    query, pair_b, down_grad, up_grad, *out_moved = clock.sync(
-        query, pair_b, down_grad, up_grad, *out_moved
-    )
-    query_back.append(query)
-
-    pair = heads_all_to_all(clock.hold(jnp.concatenate([pair_a, pair_b], axis=0)))
-    pair_sum = class_sum([clock.hold(v) for v in dkv])
-    up_grad = part_sum(up_grad, 1)
-    if members == 2:
-        out_moved.append(swap(clock.hold(out_parts[1]), "seq", seq_bits[1]))
-    pair, pair_sum, up_grad, *out_moved = clock.sync(pair, pair_sum, up_grad, *out_moved)
-    out_piece = out_pieces[0]
-    if out_moved:
-        out_piece = low_sum(out_piece, jnp.concatenate(out_moved, axis=1))
+
+    def out_move(part):
+        return [swap(clock.hold(out_parts[part]), "seq", seq_bits[1])] if out_parts else []
+
     pair_back.append(pair)
     up_keep, up_parts = far_parts(up_grad)
     up_moved = [far_move(up_parts[0])]
     pair = heads_all_to_all(clock.hold(pair_sum))
     gate_grad = weight_sum(grad_gate, gathered)
     pair, up_moved[0], gate_grad = clock.sync(pair, up_moved[0], gate_grad)
-    up_moved.append(far_move(up_parts[1]))
     pair_back.append(pair)
 
     def column_parts(value, count):
@@ -1420,7 +1417,8 @@
     down_send = column_parts(down_grad[1], 3)
     gate_keep, gate_send = half_sum(gate_grad)
     gate_moved = swap(gate_send, "seq", 1)
-    moved, grad_proj = clock.sync(
+    out_moved = out_move(0)
+    moved, grad_proj, *out_moved = clock.sync(
         exchange_grad(down_send[0]),
         turn_back(
             [v.reshape(KEY_VALUE_HEADS, rows, head_cols) for v in query_back],
@@ -1428,8 +1426,10 @@
             cosine,
             sine,
         ),
+        *out_moved,
     )
     down_other = [moved]
+    up_moved.append(far_move(up_parts[1]))
     moved = exchange_grad(down_send[1])
     proj_send = half_dot(all_normed, clock.hold(grad_proj), 1 - side, half_proj).astype(bf16)
     moved, gate_moved, up_moved[1], proj_send = clock.sync(
@@ -1440,7 +1440,13 @@
     moved = exchange_grad(down_send[2])
     proj_sent = swap(proj_send, "seq", 1)
     gate_grad = low_sum(gate_keep, gate_moved)
-    moved, proj_sent, up_grad, gate_grad = clock.sync(moved, proj_sent, up_grad, gate_grad)
+    out_moved += out_move(1)
+    moved, proj_sent, up_grad, gate_grad, *out_moved = clock.sync(
+        moved, proj_sent, up_grad, gate_grad, *out_moved
+    )
+    out_piece = out_pieces[0]
+    if out_moved:
+        out_piece = low_sum(out_piece, jnp.concatenate(out_moved, axis=1))
     down_other.append(moved)
     gate_keep, gate_parts = far_parts(gate_grad)
     down_grad = [low_sum(x, y) for x, y in zip(down_own, down_other)]
@@ -1538,17 +1544,17 @@
         axis=1,
     ).astype(f32)
     down_grad = spread_grad([clock.hold(v) for v in down_grad], seq_bits[:1])
+    up_grad = spread_grad([clock.hold(v) for v in up_grad], seq_bits[:1])
     mlp_grad = unpack(down_grad, pieces, 2, [])
+    mlp_grad = unpack(up_grad, pieces, 1, [mlp_grad])
     moved, attn_grad, mlp_grad, *gate_grad = clock.sync(moved, attn_grad, mlp_grad, *gate_grad)
     last = spread_grad([low_sum(gate_own[1], moved)], far_bits)
-    up_grad = spread_grad([clock.hold(v) for v in up_grad], seq_bits[:1])
-    mlp_grad = unpack(up_grad, pieces, 1, [mlp_grad])
-    gate_grad = spread_grad([clock.hold(v) for v in gate_grad], seq_bits[:1])
     gains = add_swapped(clock.hold(gains), "wide", wide_bits[:1])
     gains = add_swapped(add_swapped(gains, "seq", seq_bits[:1]), "seq", seq_bits[1:])
-    mlp_grad, gains, *gate_grad = clock.sync(mlp_grad, gains, *gate_grad, *last)
-    gate_grad[1:] = spread_grad(gate_grad[1:], seq_bits[:1])
-    mlp_grad = unpack(gate_grad, pieces, 0, [mlp_grad])
+    gate_grad = spread_grad([clock.hold(v) for v in gate_grad], seq_bits[:1])
+    mlp_grad = unpack(gate_grad, pieces, 0, [mlp_grad], 0)
+    mlp_grad, gains, *last = clock.sync(mlp_grad, gains, *last)
+    mlp_grad = unpack(spread_grad(last, seq_bits[:1]), pieces, 0, [mlp_grad], 1)
     grad_tokens = [first_tokens, last_tokens]
     return (
         jnp.stack(layer_out),

time: 1680 us -> 1710 us (1.018)
  starting transfers between devices: 150 us -> 169 us
    ppermute x63, waiting for transfers between devices: 311 us -> 329 us  [swap(): return lax.ppermute(value, axis, [(i, i ^ bit) for i in range(size)])]
    unnamed x314 -> x296, local copies, waits for them, and re-layouts: 60.6 us -> 60.9 us
  transfers between devices with their start and end apart: 129 -> 129, of which waited for: 64 -> 65; matrix products, arithmetic and copies ran while one was open for 17% -> 18% of each run, Pallas kernels for 28% -> 27%
where the time goes in v9:
time: 1710 us; the launch traced here: 1700 us
  waiting for transfers between devices  586 us (34%)
  Pallas kernels  494 us (29%)
  starting transfers between devices  169 us (10%)
  other arithmetic  163 us (10%)
  local copies, waits for them, and re-layouts  159 us (9%)
  matrix products  125 us (7%)
    ppermute x63, waiting for transfers between devices, swap(): return lax.ppermute(value, axis, [(i, i ^ bit) for i in range(size)])  329 us
    ppermute x48, waiting for transfers between devices, hop(): return (lax.ppermute(a, 'wide', up), lax.ppermute(b, 'wide', down))  168 us
    dot_general x12, matrix products, dot(): return lax.dot_general(a, b, (dims, ((), ())), preferred_element_type=f32)  125 us
    pallas_call x3, Pallas kernels, weight_back(): kernel_call(functools.partial(weight_kernel, count=count), hidden // tile...  87.3 us
    pallas_call x4, Pallas kernels, input_back(): kernel_call(input_back_kernel, tiles, [whole_spec(grad_gate.shape)] * 2 +...  68.6 us
    ppermute x6, waiting for transfers between devices, class_ring(): return lax.ppermute(value, 'wide', perm)  66.7 us
    pallas_call x3, Pallas kernels, open_forward(): kernel_call(open_kernel, tiles, [whole_spec(x.shape)] + [row_spec(tile, d...  62.5 us
    unnamed x296, local copies, waits for them, and re-layouts  60.9 us
  transfers between devices with their start and end apart: 129, of which 65 were waited for; matrix products, arithmetic and copies ran while one was open for 18% of the time, Pallas kernels for 27%

profile of v9, /device:TPU:0, one launch (start us, length us, event | category | flops | bytes accessed | tf_op | source)
XLA Modules:
  0.0 1699.1 jit_solution(17921712361646349649)
XLA Ops:
  12.3 25.0 %own_slices.1 = (bf16[2304,2304]{1,0:T(8,128)(2,1)}, bf16[2304,2304]{1,0:T(8,128)(2,1)}, bf16[2304,2304]{1,0:T(8,128)(2,1)}, bf16[2304,2304]{1,0:T(8,128)(2,1)},...) custom-call(s32[4]{0:T(128)} %pad_add_fusion.pieces, s32[4]{0:T(128)} %pad_add_fusion.1.info, ...), custom_call_target="tpu_custom_call" | custom-call | flops 159252480 | bytes 63700992 | tf_op jit(solution)/shard_map/own_slices/pallas_call | solution.py:297
  49.0 27.9 %collective-permute-done.3.refs_0_ = bf16[288,2560]{1,0:T(8,128)(2,1)} collective-permute-done((bf16[288,2560]{1,0:T(8,128)(2,1)}, bf16[288,2560]{1,0:T(8,128)(2,1)}, u32[]{:S(2)}, u32[]{:S(2)}) %collective-permute-start.3) | collective-permute-done | bytes 1474592 | tf_op jit(solution)/shard_map/ppermute | solution.py:102
  92.3 21.5 %collective-permute-done.7.refs_0_ = bf16[288,2560]{1,0:T(8,128)(2,1)} collective-permute-done((bf16[288,2560]{1,0:T(8,128)(2,1)}, bf16[288,2560]{1,0:T(8,128)(2,1)}, u32[]{:S(2)}, u32[]{:S(2)}) %collective-permute-start.7) | collective-permute-done | bytes 1474592 | tf_op jit(solution)/shard_map/ppermute | solution.py:102
  156.8 10.9 project.3
  167.7 10.9 project.2
  178.7 25.5 %collective-permute-done.15.refs_0_ = bf16[288,2304]{1,0:T(8,128)(2,1)} collective-permute-done((bf16[288,2304]{1,0:T(8,128)(2,1)}, bf16[288,2304]{1,0:T(8,128)(2,1)}, u32[]{:S(2)}, u32[]{:S(2)}) %collective-permute-start.15) | collective-permute-done | bytes 1327136 | tf_op jit(solution)/shard_map/ppermute | solution.py:157
  243.8 22.1 %collective-permute-done.17.refs_1_ = bf16[4,256,512]{2,1,0:T(8,128)(2,1)} collective-permute-done((bf16[4,256,512]{2,1,0:T(8,128)(2,1)}, bf16[4,256,512]{2,1,0:T(8,128)(2,1)}, u32[]{:S(2)}, u32[]{:S(2)}) %collective-permute-start.17) | collective-permute-done | bytes 1048608 | tf_op jit(solution)/shard_map/ppermute | solution.py:177
  273.8 21.3 %collective-permute-done.18 = bf16[2,256,512]{2,1,0:T(8,128)(2,1)} collective-permute-done((bf16[2,256,512]{2,1,0:T(8,128)(2,1)S(1)}, bf16[2,256,512]{2,1,0:T(8,128)(2,1)}, u32[]{:S(2)}, u32[]{:S(2)}) %collective-permute-start.18) | collective-permute-done | bytes 524320 | tf_op jit(solution)/shard_map/ppermute | solution.py:177
  302.4 11.5 attn_forward.2
  313.9 12.4 collective-permute-done.20
  337.7 20.6 %out_slices.1 = (bf16[2304,2048]{1,0:T(8,128)(2,1)}, bf16[2304,2048]{1,0:T(8,128)(2,1)}) custom-call(s32[8]{0:T(128)} %stack.170.places, s32[4]{0:T(128)} %pad_add_fusion.1.info, bf16[8,288,512]{2,1,0:T(8,128)(2,1)} %bitcast_dynamic-update-slice_fusion.8.refs_0_, bf16[8,288,512]{2,1,0:T(8,128)(2,1)} %collective-permute-done.19.refs_1_, ...), custom_call_target="tpu_custom_call" | custom-call | flops 94371840 | bytes 28311552 | tf_op jit(solution)/shard_map/out_slices/pallas_call | solution.py:260
  360.3 11.4 attn_forward.3
  373.6 14.5 all-to-all-start.5
  398.1 16.0 all-to-all-done.5
  435.2 47.6 %collective-permute-done.25.refs_0_ = bf16[288,2304]{1,0:T(8,128)(2,1)} collective-permute-done((bf16[288,2304]{1,0:T(8,128)(2,1)S(1)}, bf16[288,2304]{1,0:T(8,128)(2,1)}, u32[]{:S(2)}, u32[]{:S(2)}) %collective-permute-start.25) | collective-permute-done | bytes 1327136 | tf_op jit(solution)/shard_map/ppermute | solution.py:157
  483.2 30.8 %collective-permute-done.27.refs_1_ = bf16[288,2304]{1,0:T(8,128)(2,1)S(1)} collective-permute-done((bf16[288,2304]{1,0:T(8,128)(2,1)}, bf16[288,2304]{1,0:T(8,128)(2,1)S(1)}, u32[]{:S(2)}, u32[]{:S(2)}) %collective-permute-start.27) | collective-permute-done | bytes 1327136 | tf_op jit(solution)/shard_map/ppermute | solution.py:157
  514.0 27.9 %collective-permute-done.26.refs_0_ = bf16[288,2304]{1,0:T(8,128)(2,1)} collective-permute-done((bf16[288,2304]{1,0:T(8,128)(2,1)S(1)}, bf16[288,2304]{1,0:T(8,128)(2,1)}, u32[]{:S(2)}, u32[]{:S(2)}) %collective-permute-start.26) | collective-permute-done | bytes 1327136 | tf_op jit(solution)/shard_map/ppermute | solution.py:157
  546.5 25.5 %collective-permute-done.28 = bf16[256,2304]{1,0:T(8,128)(2,1)S(1)} collective-permute-done((bf16[256,2304]{1,0:T(8,128)(2,1)S(1)}, bf16[256,2304]{1,0:T(8,128)(2,1)S(1)}, u32[]{:S(2)}, u32[]{:S(2)}) %collective-permute-start.28) | collective-permute-done | bytes 1179680 | tf_op jit(solution)/shard_map/ppermute | solution.py:102
  599.2 29.1 %open_forward.3 = (f32[1024,2304]{1,0:T(8,128)}, f32[1024,2304]{1,0:T(8,128)}, bf16[1024,2304]{1,0:T(8,128)(2,1)}) custom-call(bf16[1024,2304]{1,0:T(8,128)(2,1)} %constant_dynamic-update-slice_fusion.4.refs_0_.refs_2_, bf16[2304,2304]{1,0:T(8,128)(2,1)} %get-tuple-element.627.refs_1_.refs_2_, bf16[2304,2304]{1,0:T(8,128)(2,1)} %get-tuple-element.628.refs_2_.refs_3_), custom_call_target="tpu_custom_call" | custom-call | flops 21743271936 | bytes 49545216 | tf_op jit(solution)/shard_map/open_forward/pallas_call | solution.py:450
  641.4 14.9 convolution_convert_fusion.3
  662.6 18.1 %open_forward.4 = (f32[1024,2304]{1,0:T(8,128)}, f32[1024,2304]{1,0:T(8,128)}, bf16[1024,2304]{1,0:T(8,128)(2,1)}) custom-call(bf16[1024,2304]{1,0:T(8,128)(2,1)} %constant_dynamic-update-slice_fusion.9.refs_0_.refs_3_, bf16[2304,2304]{1,0:T(8,128)(2,1)} %get-tuple-element.655.refs_1_.refs_2_, bf16[2304,2304]{1,0:T(8,128)(2,1)} %get-tuple-element.656.refs_2_.refs_3_), custom_call_target="tpu_custom_call" | custom-call | flops 12079595520 | bytes 29622272 | tf_op jit(solution)/shard_map/open_forward/pallas_call | solution.py:450
  684.4 15.3 open_forward.5
  718.0 13.5 convolution_convert_fusion.2
  759.6 14.9 open_back.4
  779.8 12.8 open_back.5
  792.6 18.5 %input_back.4.refs_4_ = bf16[1024,2304]{1,0:T(8,128)(2,1)} custom-call(bf16[1024,2304]{1,0:T(8,128)(2,1)} %get-tuple-element.815.refs_0_, bf16[1024,2304]{1,0:T(8,128)(2,1)} %get-tuple-element.796.refs_1_.refs_0_, bf16[2304,2304]{1,0:T(8,128)(2,1)} %get-tuple-element.627.refs_1_.refs_2_, bf16[2304,2304]{1,0:T(8,128)(2,1)} %get-tuple-element.628.refs_2_.refs_3_), custom_call_target="tpu_custom_call" | custom-call | flops 12079595520 | bytes 23855104 | tf_op jit(solution)/shard_map/input_back/pallas_call | solution.py:507
  825.7 15.8 input_back.5
  851.0 12.4 collective-permute-done.55
  871.0 14.9 open_back.6
  892.3 12.7 open_back.7
  905.0 18.5 %input_back.6.refs_4_ = bf16[1024,2304]{1,0:T(8,128)(2,1)} custom-call(bf16[1024,2304]{1,0:T(8,128)(2,1)} %get-tuple-element.816.refs_0_.refs_1_, bf16[1024,2304]{1,0:T(8,128)(2,1)} %get-tuple-element.797.refs_1_, bf16[2304,2304]{1,0:T(8,128)(2,1)} %get-tuple-element.655.refs_1_.refs_2_, bf16[2304,2304]{1,0:T(8,128)(2,1)} %get-tuple-element.656.refs_2_.refs_3_), custom_call_target="tpu_custom_call" | custom-call | flops 12079595520 | bytes 23855104 | tf_op jit(solution)/shard_map/input_back/pallas_call | solution.py:507
  923.5 15.8 input_back.7
  960.3 12.9 collective-permute-done.61
  977.2 29.1 %weight_back.3 = bf16[2304,2304]{1,0:T(8,128)(2,1)} custom-call(bf16[1024,2304]{1,0:T(8,128)(2,1)} %get-tuple-element.749.refs_0_, bf16[1024,2304]{1,0:T(8,128)(2,1)} %get-tuple-element.750.refs_1_, bf16[1024,2304]{1,0:T(8,128)(2,1)} %copy-done.6, bf16[1024,2304]{1,0:T(8,128)(2,1)} %constant_dynamic-update-slice_fusion.19.refs_0_.refs_3_), custom_call_target="tpu_custom_call" | custom-call | flops 21743271936 | bytes 29491200 | tf_op jit(solution)/shard_map/weight_back/pallas_call | solution.py:533
  1068.0 17.5 %attn_backward.2 = (bf16[1024,512]{1,0:T(8,128)(2,1)}, bf16[4,256,512]{2,1,0:T(8,128)(2,1)}, bf16[4,256,512]{2,1,0:T(8,128)(2,1)}) custom-call(s32[1]{0:T(128)} %bitcast.43.info, bf16[1024,512]{1,0:T(8,128)(2,1)} %bitcast.44.q_ref, bf16[1024,512]{1,0:T(8,128)(2,1)} %bitcast.290, f32[1024,512]{1,0:T(8,128)} %get-tuple-element.770.exact_ref, ...), custom_call_target="tpu_custom_call" | custom-call | flops 10737418240 | bytes 9437184 | tf_op jit(solution)/shard_map/attn_backward/pallas_call | solution.py:823
  1096.1 17.4 %attn_backward.3 = (bf16[1024,512]{1,0:T(8,128)(2,1)}, bf16[4,256,512]{2,1,0:T(8,128)(2,1)}, bf16[4,256,512]{2,1,0:T(8,128)(2,1)}) custom-call(s32[1]{0:T(128)} %bitcast.43.info, bf16[1024,512]{1,0:T(8,128)(2,1)} %bitcast.46.q_ref, bf16[1024,512]{1,0:T(8,128)(2,1)} %bitcast.91.grad_ref, f32[1024,512]{1,0:T(8,128)} %get-tuple-element.784.exact_ref, ...), custom_call_target="tpu_custom_call" | custom-call | flops 10737418240 | bytes 9437184 | tf_op jit(solution)/shard_map/attn_backward/pallas_call | solution.py:823
  1131.0 29.2 %weight_back.4 = bf16[2304,2304]{1,0:T(8,128)(2,1)} custom-call(bf16[1024,2304]{1,0:T(8,128)(2,1)} %get-tuple-element.796.refs_1_.refs_0_, bf16[1024,2304]{1,0:T(8,128)(2,1)} %get-tuple-element.797.refs_1_, bf16[1024,2304]{1,0:T(8,128)(2,1)} %constant_dynamic-update-slice_fusion.4.refs_0_.refs_2_, ...), custom_call_target="tpu_custom_call" | custom-call | flops 21743271936 | bytes 29491200 | tf_op jit(solution)/shard_map/weight_back/pallas_call | solution.py:533
  1217.0 29.1 %weight_back.5 = bf16[2304,2304]{1,0:T(8,128)(2,1)} custom-call(bf16[1024,2304]{1,0:T(8,128)(2,1)} %get-tuple-element.815.refs_0_, bf16[1024,2304]{1,0:T(8,128)(2,1)} %get-tuple-element.816.refs_0_.refs_1_, bf16[1024,2304]{1,0:T(8,128)(2,1)} %constant_dynamic-update-slice_fusion.4.refs_0_.refs_2_, ...), custom_call_target="tpu_custom_call" | custom-call | flops 21743271936 | bytes 29491200 | tf_op jit(solution)/shard_map/weight_back/pallas_call | solution.py:533
  1262.0 13.1 turn_back.1
  1327.5 17.3 %collective-permute-done.79 = bf16[288,768]{1,0:T(8,128)(2,1)S(1)} collective-permute-done((bf16[288,768]{1,0:T(8,128)(2,1)S(1)}, bf16[288,768]{1,0:T(8,128)(2,1)S(1)}, u32[]{:S(2)}, u32[]{:S(2)}) %collective-permute-start.79) | collective-permute-done | bytes 442400 | tf_op jit(solution)/shard_map/ppermute | solution.py:157
  1344.8 10.9 add_convert_fusion
  1368.8 15.5 collective-permute-done.82
  1397.5 25.0 %collective-permute-done.86 = bf16[2,288,1152]{2,1,0:T(8,128)(2,1)} collective-permute-done((bf16[2,288,1152]{2,1,0:T(8,128)(2,1)}, bf16[2,288,1152]{2,1,0:T(8,128)(2,1)}, u32[]{:S(2)}, u32[]{:S(2)}) %collective-permute-start.86) | collective-permute-done | bytes 1327136 | tf_op jit(solution)/shard_map/ppermute | solution.py:157
  1435.7 24.5 %collective-permute-done.89 = bf16[2,288,1152]{2,1,0:T(8,128)(2,1)S(1)} collective-permute-done((bf16[2,288,1152]{2,1,0:T(8,128)(2,1)S(1)}, bf16[2,288,1152]{2,1,0:T(8,128)(2,1)S(1)}, u32[]{:S(2)}, u32[]{:S(2)}) %collective-permute-start.89) | collective-permute-done | bytes 1327136 | tf_op jit(solution)/shard_map/ppermute | solution.py:157
  1495.7 20.9 %fusion.86 = f32[256,2304]{1,0:T(8,128)} fusion(bf16[256,4096]{1,0:T(8,128)(2,1)} %get-tuple-element.874, bf16[2304,4096]{1,0:T(8,128)(2,1)} %get-tuple-element.505.wq_ref.wk_ref.wv_ref), kind=kOutput, calls=%fused_computation.352 | convolution fusion | flops 4831838208 | bytes 23330816 | tf_op jit(solution)/shard_map/dot_general | solution.py:26
  1522.6 20.5 %fusion.87 = f32[256,2304]{1,0:T(8,128)} fusion(bf16[256,4096]{1,0:T(8,128)(2,1)} %get-tuple-element.882, bf16[2304,4096]{1,0:T(8,128)(2,1)} %get-tuple-element.508.wq_ref.wk_ref.wv_ref), kind=kOutput, calls=%fused_computation.353 | convolution fusion | flops 4831838208 | bytes 23330816 | tf_op jit(solution)/shard_map/dot_general | solution.py:26
  1574.1 12.7 collective-permute-done.103
  1588.1 12.3 collective-permute-done.102
  (771 shorter events, 777.9 us)
Async XLA Ops:
  4.9 36.8 %collective-permute-start = (bf16[288,2560]{1,0:T(8,128)(2,1)}, bf16[288,2560]{1,0:T(8,128)(2,1)}, u32[]{:S(2)}, u32[]{:S(2)}) collective-permute-start(bf16[288,2560]{1,0:T(8,128)(2,1)} %pad_maximum_fusion.11.refs_0_), channel_id=1, source_target_pairs={{0,8},{8,16},{16,24},{24,28},{28,20},{20,12},{12,4},{4,0},{1,9},{9... | collective-permute-start | bytes 4423688 | tf_op jit(solution)/shard_map/ppermute | solution.py:102
  7.9 34.1 %collective-permute-start.1 = (bf16[288,2560]{1,0:T(8,128)(2,1)}, bf16[288,2560]{1,0:T(8,128)(2,1)}, u32[]{:S(2)}, u32[]{:S(2)}) collective-permute-start(bf16[288,2560]{1,0:T(8,128)(2,1)} %pad_maximum_fusion.11.refs_0_), channel_id=1, source_target_pairs={{8,0},{16,8},{24,16},{28,24},{20,28},{12,20},{4,12},{0,4},{9,1},{1... | collective-permute-start | bytes 4423688 | tf_op jit(solution)/shard_map/ppermute | solution.py:102
  7.9 34.1 %collective-permute-start.2 = (bf16[288,2560]{1,0:T(8,128)(2,1)}, bf16[288,2560]{1,0:T(8,128)(2,1)}, u32[]{:S(2)}, u32[]{:S(2)}) collective-permute-start(bf16[288,2560]{1,0:T(8,128)(2,1)} %pad_maximum_fusion.11.refs_0_), channel_id=1, source_target_pairs={{0,1},{1,0},{2,3},{3,2},{4,5},{5,4},{6,7},{7,6},{8,9},{9,8},{10,11... | collective-permute-start | bytes 4423688 | tf_op jit(solution)/shard_map/ppermute | solution.py:157
  42.0 35.0 %collective-permute-start.3 = (bf16[288,2560]{1,0:T(8,128)(2,1)}, bf16[288,2560]{1,0:T(8,128)(2,1)}, u32[]{:S(2)}, u32[]{:S(2)}) collective-permute-start(bf16[288,2560]{1,0:T(8,128)(2,1)} %collective-permute-done.refs_2_), channel_id=1, source_target_pairs={{0,8},{8,16},{16,24},{24,28},{28,20},{20,12},{12,4},{4,0},{1,9},{9... | collective-permute-start | bytes 4423688 | tf_op jit(solution)/shard_map/ppermute | solution.py:102
  43.8 35.0 %collective-permute-start.5 = (bf16[288,2560]{1,0:T(8,128)(2,1)}, bf16[288,2560]{1,0:T(8,128)(2,1)}, u32[]{:S(2)}, u32[]{:S(2)}) collective-permute-start(bf16[288,2560]{1,0:T(8,128)(2,1)} %collective-permute-done.refs_2_), channel_id=1, source_target_pairs={{0,1},{1,0},{2,3},{3,2},{4,5},{5,4},{6,7},{7,6},{8,9},{9,8},{10,11... | collective-permute-start | bytes 4423688 | tf_op jit(solution)/shard_map/ppermute | solution.py:157
  44.0 34.8 %collective-permute-start.4 = (bf16[288,2560]{1,0:T(8,128)(2,1)}, bf16[288,2560]{1,0:T(8,128)(2,1)}, u32[]{:S(2)}, u32[]{:S(2)}) collective-permute-start(bf16[288,2560]{1,0:T(8,128)(2,1)} %collective-permute-done.1.refs_4_), channel_id=1, source_target_pairs={{8,0},{16,8},{24,16},{28,24},{20,28},{12,20},{4,12},{0,4},{9,1},{1... | collective-permute-start | bytes 4423688 | tf_op jit(solution)/shard_map/ppermute | solution.py:102
  44.3 34.5 %collective-permute-start.6 = (bf16[288,2560]{1,0:T(8,128)(2,1)}, bf16[288,2560]{1,0:T(8,128)(2,1)}, u32[]{:S(2)}, u32[]{:S(2)}) collective-permute-start(bf16[288,2560]{1,0:T(8,128)(2,1)} %collective-permute-done.1.refs_4_), channel_id=1, source_target_pairs={{0,1},{1,0},{2,3},{3,2},{4,5},{5,4},{6,7},{7,6},{8,9},{9,8},{10,11... | collective-permute-start | bytes 4423688 | tf_op jit(solution)/shard_map/ppermute | solution.py:157
  78.8 35.0 %collective-permute-start.7 = (bf16[288,2560]{1,0:T(8,128)(2,1)}, bf16[288,2560]{1,0:T(8,128)(2,1)}, u32[]{:S(2)}, u32[]{:S(2)}) collective-permute-start(bf16[288,2560]{1,0:T(8,128)(2,1)} %collective-permute-done.3.refs_0_), channel_id=1, source_target_pairs={{0,8},{8,16},{16,24},{24,28},{28,20},{20,12},{12,4},{4,0},{1,9},{9... | collective-permute-start | bytes 4423688 | tf_op jit(solution)/shard_map/ppermute | solution.py:102
  80.4 34.7 %collective-permute-start.8 = (bf16[288,2560]{1,0:T(8,128)(2,1)}, bf16[288,2560]{1,0:T(8,128)(2,1)}, u32[]{:S(2)}, u32[]{:S(2)}) collective-permute-start(bf16[288,2560]{1,0:T(8,128)(2,1)} %collective-permute-done.4.refs_2_), channel_id=1, source_target_pairs={{8,0},{16,8},{24,16},{28,24},{20,28},{12,20},{4,12},{0,4},{9,1},{1... | collective-permute-start | bytes 4423688 | tf_op jit(solution)/shard_map/ppermute | solution.py:102
  80.9 34.2 %collective-permute-start.9 = (bf16[288,2560]{1,0:T(8,128)(2,1)}, bf16[288,2560]{1,0:T(8,128)(2,1)}, u32[]{:S(2)}, u32[]{:S(2)}) collective-permute-start(bf16[288,2560]{1,0:T(8,128)(2,1)} %collective-permute-done.3.refs_0_), channel_id=1, source_target_pairs={{0,1},{1,0},{2,3},{3,2},{4,5},{5,4},{6,7},{7,6},{8,9},{9,8},{10,11... | collective-permute-start | bytes 4423688 | tf_op jit(solution)/shard_map/ppermute | solution.py:157
  143.0 61.2 %collective-permute-start.15 = (bf16[288,2304]{1,0:T(8,128)(2,1)}, bf16[288,2304]{1,0:T(8,128)(2,1)}, u32[]{:S(2)}, u32[]{:S(2)}) collective-permute-start(bf16[288,2304]{1,0:T(8,128)(2,1)} %get-tuple-element.496), channel_id=1, source_target_pairs={{0,16},{4,20},{8,24},{12,28},{16,0},{20,4},{24,8},{28,12},{1,17},{... | collective-permute-start | bytes 3981320 | tf_op jit(solution)/shard_map/ppermute | solution.py:157
  242.2 52.9 %collective-permute-start.19 = (bf16[8,288,512]{2,1,0:T(8,128)(2,1)}, bf16[8,288,512]{2,1,0:T(8,128)(2,1)}, u32[]{:S(2)}, u32[]{:S(2)}) collective-permute-start(bf16[8,288,512]{2,1,0:T(8,128)(2,1)} %bitcast_dynamic-update-slice_fusion.8.refs_0_), channel_id=1, source_target_pairs={{0,2},{1,3},{2,0},{3,1},{4,6},{5,7},{6,4},{7,5},{8,10},{9,11},{10,... | collective-permute-start | bytes 7077896 | tf_op jit(solution)/shard_map/ppermute | solution.py:157
  296.3 31.0 %collective-permute-start.21 = (bf16[8,288,512]{2,1,0:T(8,128)(2,1)}, bf16[8,288,512]{2,1,0:T(8,128)(2,1)}, u32[]{:S(2)}, u32[]{:S(2)}) collective-permute-start(bf16[8,288,512]{2,1,0:T(8,128)(2,1)} %collective-permute-done.19.refs_1_), channel_id=1, source_target_pairs={{0,1},{1,0},{2,3},{3,2},{4,5},{5,4},{6,7},{7,6},{8,9},{9,8},{10,11... | collective-permute-start | bytes 7077896 | tf_op jit(solution)/shard_map/ppermute | solution.py:157
  327.3 44.5 %all-to-all-start.4 = ((bf16[8,128,512]{2,1,0:T(8,128)(2,1)}), bf16[8,128,512]{2,1,0:T(8,128)(2,1)S(1)}, u32[]{:S(2)}, u32[]{:S(2)}) async-start(bf16[8,128,512]{2,1,0:T(8,128)(2,1)} %bitcast.292), calls=%async_computation.4 | async-start | bytes 2097152 | tf_op jit(solution)/shard_map/all_to_all | solution.py:161
  333.0 38.8 %collective-permute-start.22 = (bf16[288,2304]{1,0:T(8,128)(2,1)}, bf16[288,2304]{1,0:T(8,128)(2,1)}, u32[]{:S(2)}, u32[]{:S(2)}) collective-permute-start(bf16[288,2304]{1,0:T(8,128)(2,1)} %collective-permute-done.15.refs_0_), channel_id=1, source_target_pairs={{0,2},{1,3},{2,0},{3,1},{4,6},{5,7},{6,4},{7,5},{8,10},{9,11},{10,... | collective-permute-start | bytes 3981320 | tf_op jit(solution)/shard_map/ppermute | solution.py:157
  373.6 40.5 %all-to-all-start.5 = ((bf16[8,128,512]{2,1,0:T(8,128)(2,1)}), bf16[8,128,512]{2,1,0:T(8,128)(2,1)}, u32[]{:S(2)}, u32[]{:S(2)}) async-start(bf16[8,128,512]{2,1,0:T(8,128)(2,1)} %bitcast.294), calls=%async_computation.5 | async-start | bytes 2097152 | tf_op jit(solution)/shard_map/all_to_all | solution.py:161
  423.3 59.4 %collective-permute-start.25 = (bf16[288,2304]{1,0:T(8,128)(2,1)S(1)}, bf16[288,2304]{1,0:T(8,128)(2,1)}, u32[]{:S(2)}, u32[]{:S(2)}) collective-permute-start(bf16[288,2304]{1,0:T(8,128)(2,1)S(1)} %copy-done.55), channel_id=1, source_target_pairs={{0,16},{4,20},{8,24},{12,28},{16,0},{20,4},{24,8},{28,12},{1,17},{... | collective-permute-start | bytes 3981320 | tf_op jit(solution)/shard_map/ppermute | solution.py:157
  482.7 31.3 %collective-permute-start.27 = (bf16[288,2304]{1,0:T(8,128)(2,1)}, bf16[288,2304]{1,0:T(8,128)(2,1)S(1)}, u32[]{:S(2)}, u32[]{:S(2)}) collective-permute-start(bf16[288,2304]{1,0:T(8,128)(2,1)} %collective-permute-done.25.refs_0_), channel_id=1, source_target_pairs={{0,2},{1,3},{2,0},{3,1},{4,6},{5,7},{6,4},{7,5},{8,10},{9,11},{10,... | collective-permute-start | bytes 3981320 | tf_op jit(solution)/shard_map/ppermute | solution.py:157
  483.2 58.8 %collective-permute-start.26 = (bf16[288,2304]{1,0:T(8,128)(2,1)S(1)}, bf16[288,2304]{1,0:T(8,128)(2,1)}, u32[]{:S(2)}, u32[]{:S(2)}) collective-permute-start(bf16[288,2304]{1,0:T(8,128)(2,1)S(1)} %copy-done.54), channel_id=1, source_target_pairs={{0,16},{4,20},{8,24},{12,28},{16,0},{20,4},{24,8},{28,12},{1,17},{... | collective-permute-start | bytes 3981320 | tf_op jit(solution)/shard_map/ppermute | solution.py:157
  541.9 31.5 %collective-permute-start.32 = (bf16[288,2304]{1,0:T(8,128)(2,1)}, bf16[288,2304]{1,0:T(8,128)(2,1)}, u32[]{:S(2)}, u32[]{:S(2)}) collective-permute-start(bf16[288,2304]{1,0:T(8,128)(2,1)} %collective-permute-done.26.refs_0_), channel_id=1, source_target_pairs={{0,2},{1,3},{2,0},{3,1},{4,6},{5,7},{6,4},{7,5},{8,10},{9,11},{10,... | collective-permute-start | bytes 3981320 | tf_op jit(solution)/shard_map/ppermute | solution.py:157
  595.5 33.9 %collective-permute-start.37 = (bf16[256,2304]{1,0:T(8,128)(2,1)S(1)}, bf16[256,2304]{1,0:T(8,128)(2,1)S(1)}, u32[]{:S(2)}, u32[]{:S(2)}) collective-permute-start(bf16[256,2304]{1,0:T(8,128)(2,1)S(1)} %multiply_convert_fusion), channel_id=1, source_target_pairs={{0,8},{8,12},{12,4},{4,0},{16,24},{24,28},{28,20},{20,16},{1,9},{9... | collective-permute-start | bytes 3538952 | tf_op jit(solution)/shard_map/ppermute | solution.py:102
  597.2 32.2 %collective-permute-start.38 = (bf16[256,2304]{1,0:T(8,128)(2,1)S(1)}, bf16[256,2304]{1,0:T(8,128)(2,1)S(1)}, u32[]{:S(2)}, u32[]{:S(2)}) collective-permute-start(bf16[256,2304]{1,0:T(8,128)(2,1)S(1)} %multiply_convert_fusion), channel_id=1, source_target_pairs={{8,0},{12,8},{4,12},{0,4},{24,16},{28,24},{20,28},{16,20},{9,1},{1... | collective-permute-start | bytes 3538952 | tf_op jit(solution)/shard_map/ppermute | solution.py:102
  776.5 34.6 %collective-permute-start.52 = (bf16[256,2304]{1,0:T(8,128)(2,1)S(1)}, bf16[256,2304]{1,0:T(8,128)(2,1)S(1)}, u32[]{:S(2)}, u32[]{:S(2)}) collective-permute-start(bf16[256,2304]{1,0:T(8,128)(2,1)S(1)} %pad_maximum_fusion.21), channel_id=1, source_target_pairs={{8,0},{12,8},{4,12},{0,4},{24,16},{28,24},{20,28},{16,20},{9,1},{1... | collective-permute-start | bytes 3538952 | tf_op jit(solution)/shard_map/ppermute | solution.py:102
  779.4 31.8 %collective-permute-start.51 = (bf16[256,2304]{1,0:T(8,128)(2,1)}, bf16[256,2304]{1,0:T(8,128)(2,1)S(1)}, u32[]{:S(2)}, u32[]{:S(2)}) collective-permute-start(bf16[256,2304]{1,0:T(8,128)(2,1)} %pad_maximum_fusion.20), channel_id=1, source_target_pairs={{0,8},{8,12},{12,4},{4,0},{16,24},{24,28},{28,20},{20,16},{1,9},{9... | collective-permute-start | bytes 3538952 | tf_op jit(solution)/shard_map/ppermute | solution.py:102
  888.8 34.7 %collective-permute-start.60 = (bf16[256,2304]{1,0:T(8,128)(2,1)}, bf16[256,2304]{1,0:T(8,128)(2,1)}, u32[]{:S(2)}, u32[]{:S(2)}) collective-permute-start(bf16[256,2304]{1,0:T(8,128)(2,1)} %pad_maximum_fusion.23), channel_id=1, source_target_pairs={{8,0},{12,8},{4,12},{0,4},{24,16},{28,24},{20,28},{16,20},{9,1},{1... | collective-permute-start | bytes 3538952 | tf_op jit(solution)/shard_map/ppermute | solution.py:102
  889.9 33.6 %collective-permute-start.59 = (bf16[256,2304]{1,0:T(8,128)(2,1)}, bf16[256,2304]{1,0:T(8,128)(2,1)S(1)}, u32[]{:S(2)}, u32[]{:S(2)}) collective-permute-start(bf16[256,2304]{1,0:T(8,128)(2,1)} %pad_maximum_fusion.22), channel_id=1, source_target_pairs={{0,8},{8,12},{12,4},{4,0},{16,24},{24,28},{28,20},{20,16},{1,9},{9... | collective-permute-start | bytes 3538952 | tf_op jit(solution)/shard_map/ppermute | solution.py:102
  974.8 31.4 %collective-permute-start.64 = (bf16[256,2304]{1,0:T(8,128)(2,1)S(1)}, bf16[256,2304]{1,0:T(8,128)(2,1)S(1)}, u32[]{:S(2)}, u32[]{:S(2)}) collective-permute-start(bf16[256,2304]{1,0:T(8,128)(2,1)S(1)} %pad_maximum_fusion.25), channel_id=1, source_target_pairs={{8,0},{12,8},{4,12},{0,4},{24,16},{28,24},{20,28},{16,20},{9,1},{1... | collective-permute-start | bytes 3538952 | tf_op jit(solution)/shard_map/ppermute | solution.py:102
  1054.2 31.4 %collective-permute-start.66 = (bf16[2,288,1152]{2,1,0:T(8,128)(2,1)}, bf16[2,288,1152]{2,1,0:T(8,128)(2,1)}, u32[]{:S(2)}, u32[]{:S(2)}) collective-permute-start(bf16[2,288,1152]{2,1,0:T(8,128)(2,1)} %get-tuple-element.764), channel_id=1, source_target_pairs={{0,2},{1,3},{2,0},{3,1},{4,6},{5,7},{6,4},{7,5},{8,10},{9,11},{10,... | collective-permute-start | bytes 3981320 | tf_op jit(solution)/shard_map/ppermute | solution.py:157
  1054.8 31.8 %all-to-all-start.7 = ((bf16[8,128,512]{2,1,0:T(8,128)(2,1)}), bf16[8,128,512]{2,1,0:T(8,128)(2,1)}, u32[]{:S(2)}, u32[]{:S(2)}) async-start(bf16[8,128,512]{2,1,0:T(8,128)(2,1)} %bitcast.86), calls=%async_computation.7 | async-start | bytes 2097152 | tf_op jit(solution)/shard_map/all_to_all | solution.py:161
  1086.6 36.6 %collective-permute-start.69 = (bf16[2304,1024]{1,0:T(8,128)(2,1)}, bf16[2304,1024]{1,0:T(8,128)(2,1)}, u32[]{:S(2)}, u32[]{:S(2)}) collective-permute-start(bf16[2304,1024]{1,0:T(8,128)(2,1)} %convolution_convert_fusion.1), channel_id=1, source_target_pairs={{0,1},{1,0},{2,3},{3,2},{4,5},{5,4},{6,7},{7,6},{8,9},{9,8},{10,11... | collective-permute-start | bytes 14155784 | tf_op jit(solution)/shard_map/ppermute | solution.py:157
  1086.6 36.6 %all-to-all-start.8 = ((bf16[8,128,512]{2,1,0:T(8,128)(2,1)}), bf16[8,128,512]{2,1,0:T(8,128)(2,1)S(1)}, u32[]{:S(2)}, u32[]{:S(2)}) async-start(bf16[8,128,512]{2,1,0:T(8,128)(2,1)} %bitcast.291), calls=%async_computation.8 | async-start | bytes 2097152 | tf_op jit(solution)/shard_map/all_to_all | solution.py:161
  1091.7 31.4 %collective-permute-start.68 = (bf16[2,288,1152]{2,1,0:T(8,128)(2,1)}, bf16[2,288,1152]{2,1,0:T(8,128)(2,1)}, u32[]{:S(2)}, u32[]{:S(2)}) collective-permute-start(bf16[2,288,1152]{2,1,0:T(8,128)(2,1)} %get-tuple-element.780), channel_id=1, source_target_pairs={{0,2},{1,3},{2,0},{3,1},{4,6},{5,7},{6,4},{7,5},{8,10},{9,11},{10,... | collective-permute-start | bytes 3981320 | tf_op jit(solution)/shard_map/ppermute | solution.py:157
  1124.1 39.9 %collective-permute-start.70 = (bf16[2,256,512]{2,1,0:T(8,128)(2,1)}, bf16[2,256,512]{2,1,0:T(8,128)(2,1)}, u32[]{:S(2)}, u32[]{:S(2)}) collective-permute-start(bf16[2,256,512]{2,1,0:T(8,128)(2,1)} %get-tuple-element.793), channel_id=1, source_target_pairs={{0,4},{4,0},{8,12},{12,8},{16,20},{20,16},{24,28},{28,24},{1,5},{5... | collective-permute-start | bytes 1572872 | tf_op jit(solution)/shard_map/ppermute | solution.py:177
  1125.9 39.3 %all-to-all-start.9 = ((bf16[8,128,512]{2,1,0:T(8,128)(2,1)}), bf16[8,128,512]{2,1,0:T(8,128)(2,1)S(1)}, u32[]{:S(2)}, u32[]{:S(2)}) async-start(bf16[8,128,512]{2,1,0:T(8,128)(2,1)} %bitcast.293), calls=%async_computation.9 | async-start | bytes 2097152 | tf_op jit(solution)/shard_map/all_to_all | solution.py:161
  1173.9 33.5 %all-to-all-start.10 = ((bf16[4,256,512]{2,1,0:T(8,128)(2,1)}), bf16[4,256,512]{2,1,0:T(8,128)(2,1)}, u32[]{:S(2)}, u32[]{:S(2)}) async-start(bf16[4,256,512]{2,1,0:T(8,128)(2,1)} %pad_maximum_fusion.26), calls=%async_computation.10 | async-start | bytes 2097152 | tf_op jit(solution)/shard_map/all_to_all | solution.py:168
  1210.6 35.5 %collective-permute-start.73 = (bf16[2,288,1152]{2,1,0:T(8,128)(2,1)}, bf16[2,288,1152]{2,1,0:T(8,128)(2,1)}, u32[]{:S(2)}, u32[]{:S(2)}) collective-permute-start(bf16[2,288,1152]{2,1,0:T(8,128)(2,1)} %get-tuple-element.814), channel_id=1, source_target_pairs={{0,2},{1,3},{2,0},{3,1},{4,6},{5,7},{6,4},{7,5},{8,10},{9,11},{10,... | collective-permute-start | bytes 3981320 | tf_op jit(solution)/shard_map/ppermute | solution.py:157
  1212.0 34.1 %all-to-all-start.11 = ((bf16[4,256,512]{2,1,0:T(8,128)(2,1)}), bf16[4,256,512]{2,1,0:T(8,128)(2,1)S(1)}, u32[]{:S(2)}, u32[]{:S(2)}) async-start(bf16[4,256,512]{2,1,0:T(8,128)(2,1)} %add_convert_fusion.11), calls=%async_computation.11 | async-start | bytes 2097152 | tf_op jit(solution)/shard_map/all_to_all | solution.py:168
  1251.7 63.9 %collective-permute-start.77 = (bf16[2,576,2304]{2,1,0:T(8,128)(2,1)}, bf16[2,576,2304]{2,1,0:T(8,128)(2,1)}, u32[]{:S(2)}, u32[]{:S(2)}) collective-permute-start(bf16[2,576,2304]{2,1,0:T(8,128)(2,1)} %slice_bitcast_fusion.1), channel_id=1, source_target_pairs={{0,1},{1,0},{2,3},{3,2},{4,5},{5,4},{6,7},{7,6},{8,9},{9,8},{10,11... | collective-permute-start | bytes 15925256 | tf_op jit(solution)/shard_map/ppermute | solution.py:157
  1387.1 35.4 %collective-permute-start.85 = (bf16[288,2560]{1,0:T(8,128)(2,1)}, bf16[288,2560]{1,0:T(8,128)(2,1)}, u32[]{:S(2)}, u32[]{:S(2)}) collective-permute-start(bf16[288,2560]{1,0:T(8,128)(2,1)} %pad_maximum_fusion.13), channel_id=1, source_target_pairs={{8,0},{16,8},{24,16},{28,24},{20,28},{12,20},{4,12},{0,4},{9,1},{1... | collective-permute-start | bytes 4423688 | tf_op jit(solution)/shard_map/ppermute | solution.py:102
  1388.9 33.6 %collective-permute-start.84 = (bf16[288,2560]{1,0:T(8,128)(2,1)}, bf16[288,2560]{1,0:T(8,128)(2,1)}, u32[]{:S(2)}, u32[]{:S(2)}) collective-permute-start(bf16[288,2560]{1,0:T(8,128)(2,1)} %fusion.41), channel_id=1, source_target_pairs={{0,8},{8,16},{16,24},{24,28},{28,20},{20,12},{12,4},{4,0},{1,9},{9... | collective-permute-start | bytes 4423688 | tf_op jit(solution)/shard_map/ppermute | solution.py:102
  1424.7 35.4 %collective-permute-start.88 = (bf16[288,2560]{1,0:T(8,128)(2,1)S(1)}, bf16[288,2560]{1,0:T(8,128)(2,1)S(1)}, u32[]{:S(2)}, u32[]{:S(2)}) collective-permute-start(bf16[288,2560]{1,0:T(8,128)(2,1)S(1)} %add_convert_fusion.6), channel_id=1, source_target_pairs={{8,0},{16,8},{24,16},{28,24},{20,28},{12,20},{4,12},{0,4},{9,1},{1... | collective-permute-start | bytes 4423688 | tf_op jit(solution)/shard_map/ppermute | solution.py:102
  1428.0 32.2 %collective-permute-start.87 = (bf16[288,2560]{1,0:T(8,128)(2,1)S(1)}, bf16[288,2560]{1,0:T(8,128)(2,1)S(1)}, u32[]{:S(2)}, u32[]{:S(2)}) collective-permute-start(bf16[288,2560]{1,0:T(8,128)(2,1)S(1)} %add_convert_fusion.7), channel_id=1, source_target_pairs={{0,8},{8,16},{16,24},{24,28},{28,20},{20,12},{12,4},{4,0},{1,9},{9... | collective-permute-start | bytes 4423688 | tf_op jit(solution)/shard_map/ppermute | solution.py:102
  1460.7 32.1 %collective-permute-start.91 = (bf16[288,2560]{1,0:T(8,128)(2,1)S(1)}, bf16[288,2560]{1,0:T(8,128)(2,1)S(1)}, u32[]{:S(2)}, u32[]{:S(2)}) collective-permute-start(bf16[288,2560]{1,0:T(8,128)(2,1)S(1)} %add_convert_fusion.4), channel_id=1, source_target_pairs={{8,0},{16,8},{24,16},{28,24},{20,28},{12,20},{4,12},{0,4},{9,1},{1... | collective-permute-start | bytes 4423688 | tf_op jit(solution)/shard_map/ppermute | solution.py:102
  1462.8 31.1 %collective-permute-start.90 = (bf16[288,2560]{1,0:T(8,128)(2,1)S(1)}, bf16[288,2560]{1,0:T(8,128)(2,1)S(1)}, u32[]{:S(2)}, u32[]{:S(2)}) collective-permute-start(bf16[288,2560]{1,0:T(8,128)(2,1)S(1)} %add_convert_fusion.5), channel_id=1, source_target_pairs={{0,8},{8,16},{16,24},{24,28},{28,20},{20,12},{12,4},{4,0},{1,9},{9... | collective-permute-start | bytes 4423688 | tf_op jit(solution)/shard_map/ppermute | solution.py:102
  1522.6 31.6 %collective-permute-start.96 = (bf16[288,1152]{1,0:T(8,128)(2,1)}, bf16[288,1152]{1,0:T(8,128)(2,1)}, u32[]{:S(2)}, u32[]{:S(2)}) collective-permute-start(bf16[288,1152]{1,0:T(8,128)(2,1)} %get-tuple-element.880), channel_id=1, source_target_pairs={{0,16},{4,20},{8,24},{12,28},{16,0},{20,4},{24,8},{28,12},{1,17},{... | collective-permute-start | bytes 1990664 | tf_op jit(solution)/shard_map/ppermute | solution.py:157
  1566.0 39.1 %collective-permute-start.101 = (bf16[288,3072]{1,0:T(8,128)(2,1)}, bf16[288,3072]{1,0:T(8,128)(2,1)}, u32[]{:S(2)}, u32[]{:S(2)}) collective-permute-start(bf16[288,3072]{1,0:T(8,128)(2,1)} %pad_maximum_fusion.7), channel_id=1, source_target_pairs={{0,1},{1,0},{2,3},{3,2},{4,5},{5,4},{6,7},{7,6},{8,9},{9,8},{10,11... | collective-permute-start | bytes 5308424 | tf_op jit(solution)/shard_map/ppermute | solution.py:157
  1573.7 31.3 %collective-permute-start.100 = (bf16[288,1152]{1,0:T(8,128)(2,1)S(1)}, bf16[288,1152]{1,0:T(8,128)(2,1)S(1)}, u32[]{:S(2)}, u32[]{:S(2)}) collective-permute-start(bf16[288,1152]{1,0:T(8,128)(2,1)S(1)} %copy-done.70), channel_id=1, source_target_pairs={{0,16},{4,20},{8,24},{12,28},{16,0},{20,4},{24,8},{28,12},{1,17},{... | collective-permute-start | bytes 1990664 | tf_op jit(solution)/shard_map/ppermute | solution.py:157
  1625.9 32.0 %collective-permute-start.104 = (bf16[288,1152]{1,0:T(8,128)(2,1)S(1)}, bf16[288,1152]{1,0:T(8,128)(2,1)}, u32[]{:S(2)}, u32[]{:S(2)}) collective-permute-start(bf16[288,1152]{1,0:T(8,128)(2,1)S(1)} %copy-done.69), channel_id=1, source_target_pairs={{0,16},{4,20},{8,24},{12,28},{16,0},{20,4},{24,8},{28,12},{1,17},{... | collective-permute-start | bytes 1990664 | tf_op jit(solution)/shard_map/ppermute | solution.py:157
  (212 other events, 3210.6 us)

commit v10 on v8

--- a/solution.py
+++ b/solution.py
@@ -1352,11 +1352,8 @@
     out_sent = swap(out_send, "seq", 1)
     query = all_to_all(clock.hold(dq))
     pair_a = class_sum([v[0] for v in parts_of_pair])
-    out_part = low_sum(
-        half_dot(all_branch, clock.hold(all_attended), side, half_out), out_sent
-    )
-    query, pair_a, down_moved[1], out_part, *work = clock.sync(
-        query, pair_a, down_moved[1], out_part, *attend_back(1)
+    query, pair_a, down_moved[1], out_sent, *work = clock.sync(
+        query, pair_a, down_moved[1], out_sent, *attend_back(1)
     )
     down_grad = far_join(down_keep, down_moved)
     query_back.append(query)
@@ -1364,16 +1361,18 @@
     dq, *dkv = grad_attend[1]
     query = all_to_all(clock.hold(dq))
     pair_b = class_sum([clock.hold(v[1]) for v in parts_of_pair])
+    out_part = low_sum(
+        half_dot(all_branch, clock.hold(all_attended), side, half_out), out_sent
+    )
+    query, pair_b, down_grad, out_part = clock.sync(query, pair_b, down_grad, out_part)
+    query_back.append(query)
     out_pieces = {
-        t: lax.dynamic_slice_in_dim(
-            clock.hold(out_part), jnp.bitwise_xor(member, t) * split_out, split_out, 1
-        )
+        t: lax.dynamic_slice_in_dim(out_part, jnp.bitwise_xor(member, t) * split_out, split_out, 1)
         for t in range(members)
     }
-    out_moved = []
+    out_parts = None
     if members == 2:
         out_parts = [out_pieces[1][:, : split_out // 2], out_pieces[1][:, split_out // 2 :]]
-        out_moved.append(swap(out_parts[0], "seq", seq_bits[1]))
     else:
         for bit in seq_bits[1:]:
             for t in sorted(out_pieces):
@@ -1381,29 +1380,22 @@
                     out_pieces[t] = low_sum(
                         out_pieces[t], swap(out_pieces.pop(t | (bit // 2)), "seq", bit)
                     )
-    up_grad = weight_sum(grad_up, gathered)
-    query, pair_b, down_grad, up_grad, *out_moved = clock.sync(
-        query, pair_b, down_grad, up_grad, *out_moved
-    )
-    query_back.append(query)
+
+    def out_move(part):
+        return [swap(clock.hold(out_parts[part]), "seq", seq_bits[1])] if out_parts else []
 
     pair = heads_all_to_all(clock.hold(jnp.concatenate([pair_a, pair_b], axis=0)))
     pair_sum = class_sum([clock.hold(v) for v in dkv])
-    up_grad = part_sum(up_grad, 1)
-    if members == 2:
-        out_moved.append(swap(clock.hold(out_parts[1]), "seq", seq_bits[1]))
-    pair, pair_sum, up_grad, *out_moved = clock.sync(pair, pair_sum, up_grad, *out_moved)
+    pair, pair_sum, *out_moved = clock.sync(pair, pair_sum, *out_move(0))
+    pair_back.append(pair)
+    out_moved += out_move(1)
+    pair = heads_all_to_all(clock.hold(pair_sum))
+    up_grad = weight_sum(grad_up, gathered)
+    pair, up_grad, *out_moved = clock.sync(pair, up_grad, *out_moved)
+    pair_back.append(pair)
     out_piece = out_pieces[0]
     if out_moved:
         out_piece = low_sum(out_piece, jnp.concatenate(out_moved, axis=1))
-    pair_back.append(pair)
-    up_keep, up_parts = far_parts(up_grad)
-    up_moved = [far_move(up_parts[0])]
-    pair = heads_all_to_all(clock.hold(pair_sum))
-    gate_grad = weight_sum(grad_gate, gathered)
-    pair, up_moved[0], gate_grad = clock.sync(pair, up_moved[0], gate_grad)
-    up_moved.append(far_move(up_parts[1]))
-    pair_back.append(pair)
 
     def column_parts(value, count):
         width = value.shape[1] // count
@@ -1418,8 +1410,8 @@
 
     down_own = column_parts(down_grad[0], 3)
     down_send = column_parts(down_grad[1], 3)
-    gate_keep, gate_send = half_sum(gate_grad)
-    gate_moved = swap(gate_send, "seq", 1)
+    up_keep, up_send = half_sum(up_grad)
+    up_moved = swap(up_send, "seq", 1)
     moved, grad_proj = clock.sync(
         exchange_grad(down_send[0]),
         turn_back(
@@ -1432,18 +1424,16 @@
     down_other = [moved]
     moved = exchange_grad(down_send[1])
     proj_send = half_dot(all_normed, clock.hold(grad_proj), 1 - side, half_proj).astype(bf16)
-    moved, gate_moved, up_moved[1], proj_send = clock.sync(
-        moved, gate_moved, up_moved[1], proj_send
-    )
+    moved, up_moved, proj_send = clock.sync(moved, up_moved, proj_send)
     down_other.append(moved)
-    up_grad = far_join(up_keep, up_moved)
     moved = exchange_grad(down_send[2])
     proj_sent = swap(proj_send, "seq", 1)
-    gate_grad = low_sum(gate_keep, gate_moved)
-    moved, proj_sent, up_grad, gate_grad = clock.sync(moved, proj_sent, up_grad, gate_grad)
+    up_grad = low_sum(up_keep, up_moved)
+    moved, proj_sent, up_grad = clock.sync(moved, proj_sent, up_grad)
     down_other.append(moved)
-    gate_keep, gate_parts = far_parts(gate_grad)
+    up_keep, up_parts = far_parts(up_grad)
     down_grad = [low_sum(x, y) for x, y in zip(down_own, down_other)]
+    far_down = [swap(clock.hold(v), "seq", far_bits[0]) for v in down_grad]
     proj_part = low_sum(half_dot(all_normed, clock.hold(grad_proj), side, half_proj), proj_sent)
     (proj_part,) = clock.sync(proj_part)
     def part_of(o):
@@ -1462,28 +1452,41 @@
         return grads
 
     a, b = halves(clock.hold(part_of(wide // 2)))
-    gate_moved = []
+    up_moved = []
     for k in range(wide // 2 - 1, -1, -1):
         step = wide // 2 - 1 - k
         a, b = hop(a, b, wide)
         work = []
-        if step in (1, 2):
-            work = [far_move(gate_parts[step - 1])]
+        if step == 0:
+            work = far_down
+        elif step == 1:
+            work = [far_move(up_parts[0]), weight_sum(grad_gate, gathered)]
+        elif step == 2:
+            gate_keep, gate_send = half_sum(gate_grad)
+            work = [far_move(up_parts[1]), swap(clock.hold(gate_send), "seq", 1)]
         elif step == half_wide - 1:
-            work = spread_grad([clock.hold(v) for v in down_grad], far_bits)
+            gate_keep, gate_parts = far_parts(low_sum(gate_keep, gate_moved))
+            work = [far_move(gate_parts[0])]
         a, b, *work = clock.sync(a, b, *work)
-        if step in (1, 2):
-            gate_moved += work
+        if step == 0:
+            down_grad = [jnp.concatenate(v, axis=0) for v in zip(down_grad, work)]
+            down_grad = spread_grad(down_grad, far_bits[1:])
+        elif step == 1:
+            up_moved.append(work[0])
+            gate_grad = work[1]
+        elif step == 2:
+            up_moved.append(work[0])
+            gate_moved = work[1]
         elif step == half_wide - 1:
-            down_grad = work
+            gate_moved = work
         if step == 0:
             a, b = add_first(part_of(k), a), add_last(part_of(-k), b)
         elif k > 0:
             a, b = low_sum(part_of(k), a), low_sum(part_of(-k), b)
     total = low_sum(part_of(0), a, b)
-    gate_grad = far_join(gate_keep, gate_moved)
+    up_grad = far_join(up_keep, up_moved)
     up_own, up_send = column_parts(up_grad[0], 2), column_parts(up_grad[1], 2)
-    total, gate_grad, *up_send = clock.sync(total, gate_grad, *up_send)
+    total, *up_send = clock.sync(total, *up_send)
 
     def input_grad(s):
         return dot(clock.hold(grad_proj[s * rows : (s + 1) * rows]), proj_weights[s], NT)
@@ -1497,11 +1500,16 @@
             gains = gains + swap(gains, axis, bit)
         return gains
 
+    moved, grad_first, last = clock.sync(
+        exchange_grad(up_send[0]), input_grad(0), far_move(gate_parts[1])
+    )
+    gate_grad = far_join(gate_keep, gate_moved + [last])
+    up_grad = [low_sum(up_own[0], moved)]
     proj_total = total[:, :half_proj]
     out_totals = {0: total[:, half_proj:]}
     for bit in seq_bits[1:]:
         sent = jnp.concatenate([proj_total] + [out_totals[t] for t in sorted(out_totals)], axis=1)
-        moved = swap(sent, "seq", bit)
+        moved = swap(clock.hold(sent), "seq", bit)
         proj_total = low_sum(proj_total, moved[:, :half_proj])
         for i, t in enumerate(sorted(out_totals)):
             first = half_proj + i * split_out
@@ -1515,8 +1523,6 @@
         ],
         axis=1,
     )
-    moved, grad_first = clock.sync(exchange_grad(up_send[0]), input_grad(0))
-    up_grad = [low_sum(up_own[0], moved)]
     moved, low, grad_last = clock.sync(exchange_grad(up_send[1]), low, input_grad(1))
     up_grad.append(low_sum(up_own[1], moved))
     gate_own, gate_send = column_parts(gate_grad[0], 2), column_parts(gate_grad[1], 2)
@@ -1528,7 +1534,9 @@
     moved = exchange_grad(gate_send[0])
     up_grad = spread_grad([clock.hold(v) for v in up_grad], far_bits)
     other = swap(clock.hold(low), "seq", 1)
-    moved, other, *up_grad = clock.sync(moved, other, *up_grad)
+    down_grad = spread_grad([clock.hold(v) for v in down_grad], seq_bits[:1])
+    mlp_grad = unpack(down_grad, pieces, 2, [])
+    moved, other, mlp_grad, *up_grad = clock.sync(moved, other, mlp_grad, *up_grad)
     gate_grad = [low_sum(gate_own[0], moved)]
     moved = exchange_grad(gate_send[1])
     gate_grad = spread_grad([clock.hold(v) for v in gate_grad], far_bits)
@@ -1537,12 +1545,10 @@
         [left[:, :half_proj], right[:, :half_proj], left[:, half_proj:], right[:, half_proj:]],
         axis=1,
     ).astype(f32)
-    down_grad = spread_grad([clock.hold(v) for v in down_grad], seq_bits[:1])
-    mlp_grad = unpack(down_grad, pieces, 2, [])
+    up_grad = spread_grad([clock.hold(v) for v in up_grad], seq_bits[:1])
+    mlp_grad = unpack(up_grad, pieces, 1, [mlp_grad])
     moved, attn_grad, mlp_grad, *gate_grad = clock.sync(moved, attn_grad, mlp_grad, *gate_grad)
     last = spread_grad([low_sum(gate_own[1], moved)], far_bits)
-    up_grad = spread_grad([clock.hold(v) for v in up_grad], seq_bits[:1])
-    mlp_grad = unpack(up_grad, pieces, 1, [mlp_grad])
     gate_grad = spread_grad([clock.hold(v) for v in gate_grad], seq_bits[:1])
     gains = add_swapped(clock.hold(gains), "wide", wide_bits[:1])
     gains = add_swapped(add_swapped(gains, "seq", seq_bits[:1]), "seq", seq_bits[1:])

time: 1680 us -> 1690 us (level)
    ppermute x63, waiting for transfers between devices: 311 us -> 329 us  [swap(): return lax.ppermute(value, axis, [(i, i ^ bit) for i in range(size)])]
    unnamed x314 -> x260, local copies, waits for them, and re-layouts: 60.6 us -> 62.3 us
  transfers between devices with their start and end apart: 129 -> 129, of which waited for: 64 -> 69; matrix products, arithmetic and copies ran while one was open for 17% -> 17% of each run, Pallas kernels for 28% -> 28%
where the time goes in v10:
time: 1690 us; the launch traced here: 1680 us
  waiting for transfers between devices  595 us (35%)
  Pallas kernels  489 us (29%)
  other arithmetic  163 us (10%)
  starting transfers between devices  160 us (9%)
  local copies, waits for them, and re-layouts  153 us (9%)
  matrix products  113 us (7%)
    ppermute x63, waiting for transfers between devices, swap(): return lax.ppermute(value, axis, [(i, i ^ bit) for i in range(size)])  329 us
    ppermute x48, waiting for transfers between devices, hop(): return (lax.ppermute(a, 'wide', up), lax.ppermute(b, 'wide', down))  166 us
    dot_general x12, matrix products, dot(): return lax.dot_general(a, b, (dims, ((), ())), preferred_element_type=f32)  113 us
    pallas_call x3, Pallas kernels, weight_back(): kernel_call(functools.partial(weight_kernel, count=count), hidden // tile...  87 us
    ppermute x6, waiting for transfers between devices, class_ring(): return lax.ppermute(value, 'wide', perm)  70.3 us
    pallas_call x4, Pallas kernels, input_back(): kernel_call(input_back_kernel, tiles, [whole_spec(grad_gate.shape)] * 2 +...  68.4 us
    convert_element_type x27, other arithmetic, low_sum(): return sum((t.astype(f32) for t in terms)).astype(bf16)  67.1 us
    pallas_call x3, Pallas kernels, open_forward(): kernel_call(open_kernel, tiles, [whole_spec(x.shape)] + [row_spec(tile, d...  62.5 us
  transfers between devices with their start and end apart: 129, of which 69 were waited for; matrix products, arithmetic and copies ran while one was open for 17% of the time, Pallas kernels for 28%

profile of v10, /device:TPU:0, one launch (start us, length us, event | category | flops | bytes accessed | tf_op | source)
XLA Modules:
  0.0 1676.0 jit_solution(12726428053690748729)
XLA Ops:
  12.2 25.0 %own_slices.1 = (bf16[2304,2304]{1,0:T(8,128)(2,1)}, bf16[2304,2304]{1,0:T(8,128)(2,1)}, bf16[2304,2304]{1,0:T(8,128)(2,1)}, bf16[2304,2304]{1,0:T(8,128)(2,1)},...) custom-call(s32[4]{0:T(128)} %pad_add_fusion.pieces, s32[4]{0:T(128)} %pad_add_fusion.1.info, ...), custom_call_target="tpu_custom_call" | custom-call | flops 159252480 | bytes 63700992 | tf_op jit(solution)/shard_map/own_slices/pallas_call | solution.py:297
  49.0 27.9 %collective-permute-done.3.refs_0_ = bf16[288,2560]{1,0:T(8,128)(2,1)} collective-permute-done((bf16[288,2560]{1,0:T(8,128)(2,1)}, bf16[288,2560]{1,0:T(8,128)(2,1)}, u32[]{:S(2)}, u32[]{:S(2)}) %collective-permute-start.3) | collective-permute-done | bytes 1474592 | tf_op jit(solution)/shard_map/ppermute | solution.py:102
  92.1 21.6 %collective-permute-done.7.refs_0_ = bf16[288,2560]{1,0:T(8,128)(2,1)} collective-permute-done((bf16[288,2560]{1,0:T(8,128)(2,1)}, bf16[288,2560]{1,0:T(8,128)(2,1)}, u32[]{:S(2)}, u32[]{:S(2)}) %collective-permute-start.7) | collective-permute-done | bytes 1474592 | tf_op jit(solution)/shard_map/ppermute | solution.py:102
  156.5 11.0 project.3
  178.4 25.7 %collective-permute-done.15.refs_0_ = bf16[288,2304]{1,0:T(8,128)(2,1)} collective-permute-done((bf16[288,2304]{1,0:T(8,128)(2,1)}, bf16[288,2304]{1,0:T(8,128)(2,1)}, u32[]{:S(2)}, u32[]{:S(2)}) %collective-permute-start.15) | collective-permute-done | bytes 1327136 | tf_op jit(solution)/shard_map/ppermute | solution.py:157
  243.7 22.1 %collective-permute-done.17.refs_1_ = bf16[4,256,512]{2,1,0:T(8,128)(2,1)} collective-permute-done((bf16[4,256,512]{2,1,0:T(8,128)(2,1)}, bf16[4,256,512]{2,1,0:T(8,128)(2,1)}, u32[]{:S(2)}, u32[]{:S(2)}) %collective-permute-start.17) | collective-permute-done | bytes 1048608 | tf_op jit(solution)/shard_map/ppermute | solution.py:177
  273.8 21.3 %collective-permute-done.18 = bf16[2,256,512]{2,1,0:T(8,128)(2,1)} collective-permute-done((bf16[2,256,512]{2,1,0:T(8,128)(2,1)S(1)}, bf16[2,256,512]{2,1,0:T(8,128)(2,1)}, u32[]{:S(2)}, u32[]{:S(2)}) %collective-permute-start.18) | collective-permute-done | bytes 524320 | tf_op jit(solution)/shard_map/ppermute | solution.py:177
  302.3 11.4 attn_forward.2
  313.8 12.4 collective-permute-done.20
  337.6 20.6 %out_slices.1 = (bf16[2304,2048]{1,0:T(8,128)(2,1)}, bf16[2304,2048]{1,0:T(8,128)(2,1)}) custom-call(s32[8]{0:T(128)} %stack.170.places, s32[4]{0:T(128)} %pad_add_fusion.1.info, bf16[8,288,512]{2,1,0:T(8,128)(2,1)} %bitcast_dynamic-update-slice_fusion.8.refs_0_, bf16[8,288,512]{2,1,0:T(8,128)(2,1)} %collective-permute-done.19.refs_1_, ...), custom_call_target="tpu_custom_call" | custom-call | flops 94371840 | bytes 28311552 | tf_op jit(solution)/shard_map/out_slices/pallas_call | solution.py:260
  360.2 11.4 attn_forward.3
  373.5 14.6 all-to-all-start.5
  398.0 16.0 all-to-all-done.5
  435.1 47.6 %collective-permute-done.25.refs_0_ = bf16[288,2304]{1,0:T(8,128)(2,1)} collective-permute-done((bf16[288,2304]{1,0:T(8,128)(2,1)S(1)}, bf16[288,2304]{1,0:T(8,128)(2,1)}, u32[]{:S(2)}, u32[]{:S(2)}) %collective-permute-start.25) | collective-permute-done | bytes 1327136 | tf_op jit(solution)/shard_map/ppermute | solution.py:157
  483.1 30.8 %collective-permute-done.27.refs_1_ = bf16[288,2304]{1,0:T(8,128)(2,1)S(1)} collective-permute-done((bf16[288,2304]{1,0:T(8,128)(2,1)}, bf16[288,2304]{1,0:T(8,128)(2,1)S(1)}, u32[]{:S(2)}, u32[]{:S(2)}) %collective-permute-start.27) | collective-permute-done | bytes 1327136 | tf_op jit(solution)/shard_map/ppermute | solution.py:157
  513.9 27.9 %collective-permute-done.26.refs_0_ = bf16[288,2304]{1,0:T(8,128)(2,1)} collective-permute-done((bf16[288,2304]{1,0:T(8,128)(2,1)S(1)}, bf16[288,2304]{1,0:T(8,128)(2,1)}, u32[]{:S(2)}, u32[]{:S(2)}) %collective-permute-start.26) | collective-permute-done | bytes 1327136 | tf_op jit(solution)/shard_map/ppermute | solution.py:157
  546.4 25.5 %collective-permute-done.28 = bf16[256,2304]{1,0:T(8,128)(2,1)S(1)} collective-permute-done((bf16[256,2304]{1,0:T(8,128)(2,1)S(1)}, bf16[256,2304]{1,0:T(8,128)(2,1)S(1)}, u32[]{:S(2)}, u32[]{:S(2)}) %collective-permute-start.28) | collective-permute-done | bytes 1179680 | tf_op jit(solution)/shard_map/ppermute | solution.py:102
  599.0 29.1 %open_forward.3 = (f32[1024,2304]{1,0:T(8,128)}, f32[1024,2304]{1,0:T(8,128)}, bf16[1024,2304]{1,0:T(8,128)(2,1)}) custom-call(bf16[1024,2304]{1,0:T(8,128)(2,1)} %constant_dynamic-update-slice_fusion.4.refs_0_.refs_2_, bf16[2304,2304]{1,0:T(8,128)(2,1)} %get-tuple-element.628.refs_1_.refs_2_, bf16[2304,2304]{1,0:T(8,128)(2,1)} %get-tuple-element.629.refs_2_.refs_3_), custom_call_target="tpu_custom_call" | custom-call | flops 21743271936 | bytes 49545216 | tf_op jit(solution)/shard_map/open_forward/pallas_call | solution.py:448
  644.9 14.9 convolution_convert_fusion.3
  663.8 18.1 %open_forward.4 = (f32[1024,2304]{1,0:T(8,128)}, f32[1024,2304]{1,0:T(8,128)}, bf16[1024,2304]{1,0:T(8,128)(2,1)}) custom-call(bf16[1024,2304]{1,0:T(8,128)(2,1)} %constant_dynamic-update-slice_fusion.9.refs_0_.refs_3_, bf16[2304,2304]{1,0:T(8,128)(2,1)} %get-tuple-element.658.refs_1_.refs_2_, bf16[2304,2304]{1,0:T(8,128)(2,1)} %get-tuple-element.659.refs_2_.refs_3_), custom_call_target="tpu_custom_call" | custom-call | flops 12079595520 | bytes 29622272 | tf_op jit(solution)/shard_map/open_forward/pallas_call | solution.py:448
  685.7 15.4 open_forward.5
  717.8 13.5 convolution_convert_fusion.2
  761.5 14.9 open_back.4
  781.7 12.7 open_back.5
  794.4 18.4 %input_back.4.refs_4_ = bf16[1024,2304]{1,0:T(8,128)(2,1)} custom-call(bf16[1024,2304]{1,0:T(8,128)(2,1)} %get-tuple-element.850.refs_0_, bf16[1024,2304]{1,0:T(8,128)(2,1)} %get-tuple-element.812.refs_1_.refs_0_, bf16[2304,2304]{1,0:T(8,128)(2,1)} %get-tuple-element.628.refs_1_.refs_2_, bf16[2304,2304]{1,0:T(8,128)(2,1)} %get-tuple-element.629.refs_2_.refs_3_), custom_call_target="tpu_custom_call" | custom-call | flops 12079595520 | bytes 23855104 | tf_op jit(solution)/shard_map/input_back/pallas_call | solution.py:505
  827.4 15.8 input_back.5
  851.7 12.7 collective-permute-done.55
  870.1 14.9 open_back.6
  891.4 12.7 open_back.7
  904.1 18.4 %input_back.6.refs_4_ = bf16[1024,2304]{1,0:T(8,128)(2,1)} custom-call(bf16[1024,2304]{1,0:T(8,128)(2,1)} %get-tuple-element.851.refs_0_.refs_1_, bf16[1024,2304]{1,0:T(8,128)(2,1)} %get-tuple-element.813.refs_1_, bf16[2304,2304]{1,0:T(8,128)(2,1)} %get-tuple-element.658.refs_1_.refs_2_, bf16[2304,2304]{1,0:T(8,128)(2,1)} %get-tuple-element.659.refs_2_.refs_3_), custom_call_target="tpu_custom_call" | custom-call | flops 12079595520 | bytes 23855104 | tf_op jit(solution)/shard_map/input_back/pallas_call | solution.py:505
  938.9 15.8 input_back.7
  958.4 12.9 collective-permute-done.61
  974.0 29.0 %weight_back.3 = bf16[2304,2304]{1,0:T(8,128)(2,1)} custom-call(bf16[1024,2304]{1,0:T(8,128)(2,1)} %get-tuple-element.750.refs_0_, bf16[1024,2304]{1,0:T(8,128)(2,1)} %get-tuple-element.751.refs_1_, bf16[1024,2304]{1,0:T(8,128)(2,1)} %copy-done.8, bf16[1024,2304]{1,0:T(8,128)(2,1)} %constant_dynamic-update-slice_fusion.19.refs_0_.refs_3_), custom_call_target="tpu_custom_call" | custom-call | flops 21743271936 | bytes 29491200 | tf_op jit(solution)/shard_map/weight_back/pallas_call | solution.py:531
  1059.7 17.5 %attn_backward.2 = (bf16[1024,512]{1,0:T(8,128)(2,1)}, bf16[4,256,512]{2,1,0:T(8,128)(2,1)}, bf16[4,256,512]{2,1,0:T(8,128)(2,1)}) custom-call(s32[1]{0:T(128)} %bitcast.43.info, bf16[1024,512]{1,0:T(8,128)(2,1)} %bitcast.44.q_ref, bf16[1024,512]{1,0:T(8,128)(2,1)} %bitcast.89.grad_ref, f32[1024,512]{1,0:T(8,128)} %get-tuple-element.770.exact_ref, ...), custom_call_target="tpu_custom_call" | custom-call | flops 10737418240 | bytes 9437184 | tf_op jit(solution)/shard_map/attn_backward/pallas_call | solution.py:821
  1088.2 17.5 %attn_backward.3 = (bf16[1024,512]{1,0:T(8,128)(2,1)}, bf16[4,256,512]{2,1,0:T(8,128)(2,1)}, bf16[4,256,512]{2,1,0:T(8,128)(2,1)}) custom-call(s32[1]{0:T(128)} %bitcast.43.info, bf16[1024,512]{1,0:T(8,128)(2,1)} %bitcast.46.q_ref, bf16[1024,512]{1,0:T(8,128)(2,1)} %bitcast.91.grad_ref, f32[1024,512]{1,0:T(8,128)} %get-tuple-element.784.exact_ref, ...), custom_call_target="tpu_custom_call" | custom-call | flops 10737418240 | bytes 9437184 | tf_op jit(solution)/shard_map/attn_backward/pallas_call | solution.py:821
  1158.4 11.5 collective-permute-done.71
  1172.3 11.0 collective-permute-done.72
  1189.9 29.0 %weight_back.4 = bf16[2304,2304]{1,0:T(8,128)(2,1)} custom-call(bf16[1024,2304]{1,0:T(8,128)(2,1)} %get-tuple-element.812.refs_1_.refs_0_, bf16[1024,2304]{1,0:T(8,128)(2,1)} %get-tuple-element.813.refs_1_, bf16[1024,2304]{1,0:T(8,128)(2,1)} %constant_dynamic-update-slice_fusion.4.refs_0_.refs_2_, ...), custom_call_target="tpu_custom_call" | custom-call | flops 21743271936 | bytes 29491200 | tf_op jit(solution)/shard_map/weight_back/pallas_call | solution.py:531
  1228.6 13.0 turn_back.1
  1257.8 13.4 collective-permute-done.75
  1281.2 16.1 collective-permute-done.77
  1341.4 29.0 %weight_back.5 = bf16[2304,2304]{1,0:T(8,128)(2,1)} custom-call(bf16[1024,2304]{1,0:T(8,128)(2,1)} %get-tuple-element.850.refs_0_, bf16[1024,2304]{1,0:T(8,128)(2,1)} %get-tuple-element.851.refs_0_.refs_1_, bf16[1024,2304]{1,0:T(8,128)(2,1)} %constant_dynamic-update-slice_fusion.4.refs_0_.refs_2_, ...), custom_call_target="tpu_custom_call" | custom-call | flops 21743271936 | bytes 29491200 | tf_op jit(solution)/shard_map/weight_back/pallas_call | solution.py:531
  1393.3 22.7 %collective-permute-done.89 = bf16[2,288,1152]{2,1,0:T(8,128)(2,1)} collective-permute-done((bf16[2,288,1152]{2,1,0:T(8,128)(2,1)}, bf16[2,288,1152]{2,1,0:T(8,128)(2,1)}, u32[]{:S(2)}, u32[]{:S(2)}) %collective-permute-start.89) | collective-permute-done | bytes 1327136 | tf_op jit(solution)/shard_map/ppermute | solution.py:157
  1437.8 19.4 %collective-permute-done.93 = bf16[2,288,1152]{2,1,0:T(8,128)(2,1)S(1)} collective-permute-done((bf16[2,288,1152]{2,1,0:T(8,128)(2,1)S(1)}, bf16[2,288,1152]{2,1,0:T(8,128)(2,1)S(1)}, u32[]{:S(2)}, u32[]{:S(2)}) %collective-permute-start.93) | collective-permute-done | bytes 1327136 | tf_op jit(solution)/shard_map/ppermute | solution.py:157
  1481.9 16.2 collective-permute-done.94
  1504.4 20.5 %fusion.87 = f32[256,2304]{1,0:T(8,128)} fusion(bf16[256,4096]{1,0:T(8,128)(2,1)} %get-tuple-element.881, bf16[2304,4096]{1,0:T(8,128)(2,1)} %get-tuple-element.509.wq_ref.wk_ref.wv_ref), kind=kOutput, calls=%fused_computation.353 | convolution fusion | flops 4831838208 | bytes 23330816 | tf_op jit(solution)/shard_map/dot_general | solution.py:26
  1589.4 13.9 collective-permute-done.100
  1612.1 12.4 collective-permute-done.110
  (731 shorter events, 768.2 us)
Async XLA Ops:
  4.9 36.7 %collective-permute-start = (bf16[288,2560]{1,0:T(8,128)(2,1)}, bf16[288,2560]{1,0:T(8,128)(2,1)}, u32[]{:S(2)}, u32[]{:S(2)}) collective-permute-start(bf16[288,2560]{1,0:T(8,128)(2,1)} %pad_maximum_fusion.11.refs_0_), channel_id=1, source_target_pairs={{0,8},{8,16},{16,24},{24,28},{28,20},{20,12},{12,4},{4,0},{1,9},{9... | collective-permute-start | bytes 4423688 | tf_op jit(solution)/shard_map/ppermute | solution.py:102
  7.9 34.1 %collective-permute-start.1 = (bf16[288,2560]{1,0:T(8,128)(2,1)}, bf16[288,2560]{1,0:T(8,128)(2,1)}, u32[]{:S(2)}, u32[]{:S(2)}) collective-permute-start(bf16[288,2560]{1,0:T(8,128)(2,1)} %pad_maximum_fusion.11.refs_0_), channel_id=1, source_target_pairs={{8,0},{16,8},{24,16},{28,24},{20,28},{12,20},{4,12},{0,4},{9,1},{1... | collective-permute-start | bytes 4423688 | tf_op jit(solution)/shard_map/ppermute | solution.py:102
  7.9 34.1 %collective-permute-start.2 = (bf16[288,2560]{1,0:T(8,128)(2,1)}, bf16[288,2560]{1,0:T(8,128)(2,1)}, u32[]{:S(2)}, u32[]{:S(2)}) collective-permute-start(bf16[288,2560]{1,0:T(8,128)(2,1)} %pad_maximum_fusion.11.refs_0_), channel_id=1, source_target_pairs={{0,1},{1,0},{2,3},{3,2},{4,5},{5,4},{6,7},{7,6},{8,9},{9,8},{10,11... | collective-permute-start | bytes 4423688 | tf_op jit(solution)/shard_map/ppermute | solution.py:157
  42.0 34.9 %collective-permute-start.3 = (bf16[288,2560]{1,0:T(8,128)(2,1)}, bf16[288,2560]{1,0:T(8,128)(2,1)}, u32[]{:S(2)}, u32[]{:S(2)}) collective-permute-start(bf16[288,2560]{1,0:T(8,128)(2,1)} %collective-permute-done.refs_2_), channel_id=1, source_target_pairs={{0,8},{8,16},{16,24},{24,28},{28,20},{20,12},{12,4},{4,0},{1,9},{9... | collective-permute-start | bytes 4423688 | tf_op jit(solution)/shard_map/ppermute | solution.py:102
  43.7 35.0 %collective-permute-start.5 = (bf16[288,2560]{1,0:T(8,128)(2,1)}, bf16[288,2560]{1,0:T(8,128)(2,1)}, u32[]{:S(2)}, u32[]{:S(2)}) collective-permute-start(bf16[288,2560]{1,0:T(8,128)(2,1)} %collective-permute-done.refs_2_), channel_id=1, source_target_pairs={{0,1},{1,0},{2,3},{3,2},{4,5},{5,4},{6,7},{7,6},{8,9},{9,8},{10,11... | collective-permute-start | bytes 4423688 | tf_op jit(solution)/shard_map/ppermute | solution.py:157
  43.9 34.8 %collective-permute-start.4 = (bf16[288,2560]{1,0:T(8,128)(2,1)}, bf16[288,2560]{1,0:T(8,128)(2,1)}, u32[]{:S(2)}, u32[]{:S(2)}) collective-permute-start(bf16[288,2560]{1,0:T(8,128)(2,1)} %collective-permute-done.1.refs_4_), channel_id=1, source_target_pairs={{8,0},{16,8},{24,16},{28,24},{20,28},{12,20},{4,12},{0,4},{9,1},{1... | collective-permute-start | bytes 4423688 | tf_op jit(solution)/shard_map/ppermute | solution.py:102
  44.2 34.5 %collective-permute-start.6 = (bf16[288,2560]{1,0:T(8,128)(2,1)}, bf16[288,2560]{1,0:T(8,128)(2,1)}, u32[]{:S(2)}, u32[]{:S(2)}) collective-permute-start(bf16[288,2560]{1,0:T(8,128)(2,1)} %collective-permute-done.1.refs_4_), channel_id=1, source_target_pairs={{0,1},{1,0},{2,3},{3,2},{4,5},{5,4},{6,7},{7,6},{8,9},{9,8},{10,11... | collective-permute-start | bytes 4423688 | tf_op jit(solution)/shard_map/ppermute | solution.py:157
  78.7 35.0 %collective-permute-start.7 = (bf16[288,2560]{1,0:T(8,128)(2,1)}, bf16[288,2560]{1,0:T(8,128)(2,1)}, u32[]{:S(2)}, u32[]{:S(2)}) collective-permute-start(bf16[288,2560]{1,0:T(8,128)(2,1)} %collective-permute-done.3.refs_0_), channel_id=1, source_target_pairs={{0,8},{8,16},{16,24},{24,28},{28,20},{20,12},{12,4},{4,0},{1,9},{9... | collective-permute-start | bytes 4423688 | tf_op jit(solution)/shard_map/ppermute | solution.py:102
  80.4 34.7 %collective-permute-start.8 = (bf16[288,2560]{1,0:T(8,128)(2,1)}, bf16[288,2560]{1,0:T(8,128)(2,1)}, u32[]{:S(2)}, u32[]{:S(2)}) collective-permute-start(bf16[288,2560]{1,0:T(8,128)(2,1)} %collective-permute-done.4.refs_2_), channel_id=1, source_target_pairs={{8,0},{16,8},{24,16},{28,24},{20,28},{12,20},{4,12},{0,4},{9,1},{1... | collective-permute-start | bytes 4423688 | tf_op jit(solution)/shard_map/ppermute | solution.py:102
  80.8 34.2 %collective-permute-start.9 = (bf16[288,2560]{1,0:T(8,128)(2,1)}, bf16[288,2560]{1,0:T(8,128)(2,1)}, u32[]{:S(2)}, u32[]{:S(2)}) collective-permute-start(bf16[288,2560]{1,0:T(8,128)(2,1)} %collective-permute-done.3.refs_0_), channel_id=1, source_target_pairs={{0,1},{1,0},{2,3},{3,2},{4,5},{5,4},{6,7},{7,6},{8,9},{9,8},{10,11... | collective-permute-start | bytes 4423688 | tf_op jit(solution)/shard_map/ppermute | solution.py:157
  142.9 61.2 %collective-permute-start.15 = (bf16[288,2304]{1,0:T(8,128)(2,1)}, bf16[288,2304]{1,0:T(8,128)(2,1)}, u32[]{:S(2)}, u32[]{:S(2)}) collective-permute-start(bf16[288,2304]{1,0:T(8,128)(2,1)} %get-tuple-element.497), channel_id=1, source_target_pairs={{0,16},{4,20},{8,24},{12,28},{16,0},{20,4},{24,8},{28,12},{1,17},{... | collective-permute-start | bytes 3981320 | tf_op jit(solution)/shard_map/ppermute | solution.py:157
  242.1 52.9 %collective-permute-start.19 = (bf16[8,288,512]{2,1,0:T(8,128)(2,1)}, bf16[8,288,512]{2,1,0:T(8,128)(2,1)}, u32[]{:S(2)}, u32[]{:S(2)}) collective-permute-start(bf16[8,288,512]{2,1,0:T(8,128)(2,1)} %bitcast_dynamic-update-slice_fusion.8.refs_0_), channel_id=1, source_target_pairs={{0,2},{1,3},{2,0},{3,1},{4,6},{5,7},{6,4},{7,5},{8,10},{9,11},{10,... | collective-permute-start | bytes 7077896 | tf_op jit(solution)/shard_map/ppermute | solution.py:157
  327.2 44.5 %all-to-all-start.4 = ((bf16[8,128,512]{2,1,0:T(8,128)(2,1)}), bf16[8,128,512]{2,1,0:T(8,128)(2,1)S(1)}, u32[]{:S(2)}, u32[]{:S(2)}) async-start(bf16[8,128,512]{2,1,0:T(8,128)(2,1)} %bitcast.287), calls=%async_computation.4 | async-start | bytes 2097152 | tf_op jit(solution)/shard_map/all_to_all | solution.py:161
  332.9 38.8 %collective-permute-start.22 = (bf16[288,2304]{1,0:T(8,128)(2,1)}, bf16[288,2304]{1,0:T(8,128)(2,1)}, u32[]{:S(2)}, u32[]{:S(2)}) collective-permute-start(bf16[288,2304]{1,0:T(8,128)(2,1)} %collective-permute-done.15.refs_0_), channel_id=1, source_target_pairs={{0,2},{1,3},{2,0},{3,1},{4,6},{5,7},{6,4},{7,5},{8,10},{9,11},{10,... | collective-permute-start | bytes 3981320 | tf_op jit(solution)/shard_map/ppermute | solution.py:157
  373.5 40.5 %all-to-all-start.5 = ((bf16[8,128,512]{2,1,0:T(8,128)(2,1)}), bf16[8,128,512]{2,1,0:T(8,128)(2,1)}, u32[]{:S(2)}, u32[]{:S(2)}) async-start(bf16[8,128,512]{2,1,0:T(8,128)(2,1)} %bitcast.288), calls=%async_computation.5 | async-start | bytes 2097152 | tf_op jit(solution)/shard_map/all_to_all | solution.py:161
  423.2 59.4 %collective-permute-start.25 = (bf16[288,2304]{1,0:T(8,128)(2,1)S(1)}, bf16[288,2304]{1,0:T(8,128)(2,1)}, u32[]{:S(2)}, u32[]{:S(2)}) collective-permute-start(bf16[288,2304]{1,0:T(8,128)(2,1)S(1)} %copy-done.55), channel_id=1, source_target_pairs={{0,16},{4,20},{8,24},{12,28},{16,0},{20,4},{24,8},{28,12},{1,17},{... | collective-permute-start | bytes 3981320 | tf_op jit(solution)/shard_map/ppermute | solution.py:157
  482.7 31.3 %collective-permute-start.27 = (bf16[288,2304]{1,0:T(8,128)(2,1)}, bf16[288,2304]{1,0:T(8,128)(2,1)S(1)}, u32[]{:S(2)}, u32[]{:S(2)}) collective-permute-start(bf16[288,2304]{1,0:T(8,128)(2,1)} %collective-permute-done.25.refs_0_), channel_id=1, source_target_pairs={{0,2},{1,3},{2,0},{3,1},{4,6},{5,7},{6,4},{7,5},{8,10},{9,11},{10,... | collective-permute-start | bytes 3981320 | tf_op jit(solution)/shard_map/ppermute | solution.py:157
  483.1 58.8 %collective-permute-start.26 = (bf16[288,2304]{1,0:T(8,128)(2,1)S(1)}, bf16[288,2304]{1,0:T(8,128)(2,1)}, u32[]{:S(2)}, u32[]{:S(2)}) collective-permute-start(bf16[288,2304]{1,0:T(8,128)(2,1)S(1)} %copy-done.54), channel_id=1, source_target_pairs={{0,16},{4,20},{8,24},{12,28},{16,0},{20,4},{24,8},{28,12},{1,17},{... | collective-permute-start | bytes 3981320 | tf_op jit(solution)/shard_map/ppermute | solution.py:157
  541.8 31.4 %collective-permute-start.32 = (bf16[288,2304]{1,0:T(8,128)(2,1)}, bf16[288,2304]{1,0:T(8,128)(2,1)}, u32[]{:S(2)}, u32[]{:S(2)}) collective-permute-start(bf16[288,2304]{1,0:T(8,128)(2,1)} %collective-permute-done.26.refs_0_), channel_id=1, source_target_pairs={{0,2},{1,3},{2,0},{3,1},{4,6},{5,7},{6,4},{7,5},{8,10},{9,11},{10,... | collective-permute-start | bytes 3981320 | tf_op jit(solution)/shard_map/ppermute | solution.py:157
  595.3 34.0 %collective-permute-start.37 = (bf16[256,2304]{1,0:T(8,128)(2,1)S(1)}, bf16[256,2304]{1,0:T(8,128)(2,1)S(1)}, u32[]{:S(2)}, u32[]{:S(2)}) collective-permute-start(bf16[256,2304]{1,0:T(8,128)(2,1)S(1)} %multiply_convert_fusion), channel_id=1, source_target_pairs={{0,8},{8,12},{12,4},{4,0},{16,24},{24,28},{28,20},{20,16},{1,9},{9... | collective-permute-start | bytes 3538952 | tf_op jit(solution)/shard_map/ppermute | solution.py:102
  597.0 32.2 %collective-permute-start.38 = (bf16[256,2304]{1,0:T(8,128)(2,1)S(1)}, bf16[256,2304]{1,0:T(8,128)(2,1)S(1)}, u32[]{:S(2)}, u32[]{:S(2)}) collective-permute-start(bf16[256,2304]{1,0:T(8,128)(2,1)S(1)} %multiply_convert_fusion), channel_id=1, source_target_pairs={{8,0},{12,8},{4,12},{0,4},{24,16},{28,24},{20,28},{16,20},{9,1},{1... | collective-permute-start | bytes 3538952 | tf_op jit(solution)/shard_map/ppermute | solution.py:102
  778.3 34.5 %collective-permute-start.52 = (bf16[256,2304]{1,0:T(8,128)(2,1)S(1)}, bf16[256,2304]{1,0:T(8,128)(2,1)S(1)}, u32[]{:S(2)}, u32[]{:S(2)}) collective-permute-start(bf16[256,2304]{1,0:T(8,128)(2,1)S(1)} %pad_maximum_fusion.21), channel_id=1, source_target_pairs={{8,0},{12,8},{4,12},{0,4},{24,16},{28,24},{20,28},{16,20},{9,1},{1... | collective-permute-start | bytes 3538952 | tf_op jit(solution)/shard_map/ppermute | solution.py:102
  779.5 33.4 %collective-permute-start.51 = (bf16[256,2304]{1,0:T(8,128)(2,1)}, bf16[256,2304]{1,0:T(8,128)(2,1)S(1)}, u32[]{:S(2)}, u32[]{:S(2)}) collective-permute-start(bf16[256,2304]{1,0:T(8,128)(2,1)} %pad_maximum_fusion.20), channel_id=1, source_target_pairs={{0,8},{8,12},{12,4},{4,0},{16,24},{24,28},{28,20},{20,16},{1,9},{9... | collective-permute-start | bytes 3538952 | tf_op jit(solution)/shard_map/ppermute | solution.py:102
  887.9 34.6 %collective-permute-start.60 = (bf16[256,2304]{1,0:T(8,128)(2,1)}, bf16[256,2304]{1,0:T(8,128)(2,1)S(1)}, u32[]{:S(2)}, u32[]{:S(2)}) collective-permute-start(bf16[256,2304]{1,0:T(8,128)(2,1)} %pad_maximum_fusion.23), channel_id=1, source_target_pairs={{8,0},{12,8},{4,12},{0,4},{24,16},{28,24},{20,28},{16,20},{9,1},{1... | collective-permute-start | bytes 3538952 | tf_op jit(solution)/shard_map/ppermute | solution.py:102
  890.3 32.1 %collective-permute-start.59 = (bf16[256,2304]{1,0:T(8,128)(2,1)}, bf16[256,2304]{1,0:T(8,128)(2,1)}, u32[]{:S(2)}, u32[]{:S(2)}) collective-permute-start(bf16[256,2304]{1,0:T(8,128)(2,1)} %pad_maximum_fusion.22), channel_id=1, source_target_pairs={{0,8},{8,12},{12,4},{4,0},{16,24},{24,28},{28,20},{20,16},{1,9},{9... | collective-permute-start | bytes 3538952 | tf_op jit(solution)/shard_map/ppermute | solution.py:102
  971.6 31.4 %collective-permute-start.64 = (bf16[256,2304]{1,0:T(8,128)(2,1)S(1)}, bf16[256,2304]{1,0:T(8,128)(2,1)S(1)}, u32[]{:S(2)}, u32[]{:S(2)}) collective-permute-start(bf16[256,2304]{1,0:T(8,128)(2,1)S(1)} %pad_maximum_fusion.25), channel_id=1, source_target_pairs={{8,0},{12,8},{4,12},{0,4},{24,16},{28,24},{20,28},{16,20},{9,1},{1... | collective-permute-start | bytes 3538952 | tf_op jit(solution)/shard_map/ppermute | solution.py:102
  1047.6 31.1 %collective-permute-start.66 = (bf16[2,288,1152]{2,1,0:T(8,128)(2,1)}, bf16[2,288,1152]{2,1,0:T(8,128)(2,1)}, u32[]{:S(2)}, u32[]{:S(2)}) collective-permute-start(bf16[2,288,1152]{2,1,0:T(8,128)(2,1)} %get-tuple-element.764), channel_id=1, source_target_pairs={{0,2},{1,3},{2,0},{3,1},{4,6},{5,7},{6,4},{7,5},{8,10},{9,11},{10,... | collective-permute-start | bytes 3981320 | tf_op jit(solution)/shard_map/ppermute | solution.py:157
  1078.7 36.1 %collective-permute-start.69 = (bf16[2304,1024]{1,0:T(8,128)(2,1)}, bf16[2304,1024]{1,0:T(8,128)(2,1)}, u32[]{:S(2)}, u32[]{:S(2)}) collective-permute-start(bf16[2304,1024]{1,0:T(8,128)(2,1)} %convolution_convert_fusion.1), channel_id=1, source_target_pairs={{0,1},{1,0},{2,3},{3,2},{4,5},{5,4},{6,7},{7,6},{8,9},{9,8},{10,11... | collective-permute-start | bytes 14155784 | tf_op jit(solution)/shard_map/ppermute | solution.py:157
  1078.7 36.1 %all-to-all-start.8 = ((bf16[8,128,512]{2,1,0:T(8,128)(2,1)}), bf16[8,128,512]{2,1,0:T(8,128)(2,1)S(1)}, u32[]{:S(2)}, u32[]{:S(2)}) async-start(bf16[8,128,512]{2,1,0:T(8,128)(2,1)} %bitcast.285), calls=%async_computation.8 | async-start | bytes 2097152 | tf_op jit(solution)/shard_map/all_to_all | solution.py:161
  1083.4 31.3 %collective-permute-start.68 = (bf16[2,288,1152]{2,1,0:T(8,128)(2,1)S(1)}, bf16[2,288,1152]{2,1,0:T(8,128)(2,1)}, u32[]{:S(2)}, u32[]{:S(2)}) collective-permute-start(bf16[2,288,1152]{2,1,0:T(8,128)(2,1)S(1)} %copy-done.53), channel_id=1, source_target_pairs={{0,2},{1,3},{2,0},{3,1},{4,6},{5,7},{6,4},{7,5},{8,10},{9,11},{10,... | collective-permute-start | bytes 3981320 | tf_op jit(solution)/shard_map/ppermute | solution.py:157
  1149.5 33.8 %all-to-all-start.10 = ((bf16[4,256,512]{2,1,0:T(8,128)(2,1)}), bf16[4,256,512]{2,1,0:T(8,128)(2,1)}, u32[]{:S(2)}, u32[]{:S(2)}) async-start(bf16[4,256,512]{2,1,0:T(8,128)(2,1)} %pad_maximum_fusion.26), calls=%async_computation.10 | async-start | bytes 2097152 | tf_op jit(solution)/shard_map/all_to_all | solution.py:168
  1183.3 35.6 %collective-permute-start.73 = (bf16[2304,256]{1,0:T(8,128)(2,1)}, bf16[2304,256]{1,0:T(8,128)(2,1)}, u32[]{:S(2)}, u32[]{:S(2)}) collective-permute-start(bf16[2304,256]{1,0:T(8,128)(2,1)} %get-tuple-element.815), channel_id=1, source_target_pairs={{0,2},{1,3},{2,0},{3,1},{4,6},{5,7},{6,4},{7,5},{8,10},{9,11},{10,... | collective-permute-start | bytes 3538952 | tf_op jit(solution)/shard_map/ppermute | solution.py:157
  1184.9 34.0 %all-to-all-start.11 = ((bf16[4,256,512]{2,1,0:T(8,128)(2,1)}), bf16[4,256,512]{2,1,0:T(8,128)(2,1)}, u32[]{:S(2)}, u32[]{:S(2)}) async-start(bf16[4,256,512]{2,1,0:T(8,128)(2,1)} %add_convert_fusion.11), calls=%async_computation.11 | async-start | bytes 2097152 | tf_op jit(solution)/shard_map/all_to_all | solution.py:168
  1224.1 47.1 %collective-permute-start.76 = (bf16[2,576,2304]{2,1,0:T(8,128)(2,1)}, bf16[2,576,2304]{2,1,0:T(8,128)(2,1)}, u32[]{:S(2)}, u32[]{:S(2)}) collective-permute-start(bf16[2,576,2304]{2,1,0:T(8,128)(2,1)} %slice_bitcast_fusion.3), channel_id=1, source_target_pairs={{0,1},{1,0},{2,3},{3,2},{4,5},{5,4},{6,7},{7,6},{8,9},{9,8},{10,11... | collective-permute-start | bytes 15925256 | tf_op jit(solution)/shard_map/ppermute | solution.py:157
  1335.0 35.4 %collective-permute-start.86 = (bf16[2,288,1152]{2,1,0:T(8,128)(2,1)}, bf16[2,288,1152]{2,1,0:T(8,128)(2,1)}, u32[]{:S(2)}, u32[]{:S(2)}) collective-permute-start(bf16[2,288,1152]{2,1,0:T(8,128)(2,1)} %get-tuple-element.849), channel_id=1, source_target_pairs={{0,2},{1,3},{2,0},{3,1},{4,6},{5,7},{6,4},{7,5},{8,10},{9,11},{10,... | collective-permute-start | bytes 3981320 | tf_op jit(solution)/shard_map/ppermute | solution.py:157
  1337.9 32.5 %collective-permute-start.85 = (bf16[288,2560]{1,0:T(8,128)(2,1)}, bf16[288,2560]{1,0:T(8,128)(2,1)}, u32[]{:S(2)}, u32[]{:S(2)}) collective-permute-start(bf16[288,2560]{1,0:T(8,128)(2,1)} %pad_maximum_fusion.13), channel_id=1, source_target_pairs={{8,0},{16,8},{24,16},{28,24},{20,28},{12,20},{4,12},{0,4},{9,1},{1... | collective-permute-start | bytes 4423688 | tf_op jit(solution)/shard_map/ppermute | solution.py:102
  1341.0 31.9 %collective-permute-start.84 = (bf16[288,2560]{1,0:T(8,128)(2,1)}, bf16[288,2560]{1,0:T(8,128)(2,1)S(1)}, u32[]{:S(2)}, u32[]{:S(2)}) collective-permute-start(bf16[288,2560]{1,0:T(8,128)(2,1)} %fusion.41), channel_id=1, source_target_pairs={{0,8},{8,16},{16,24},{24,28},{28,20},{20,12},{12,4},{4,0},{1,9},{9... | collective-permute-start | bytes 4423688 | tf_op jit(solution)/shard_map/ppermute | solution.py:102
  1378.2 39.7 %collective-permute-start.90 = (bf16[2,576,2304]{2,1,0:T(8,128)(2,1)}, bf16[2,576,2304]{2,1,0:T(8,128)(2,1)}, u32[]{:S(2)}, u32[]{:S(2)}) collective-permute-start(bf16[2,576,2304]{2,1,0:T(8,128)(2,1)} %slice_bitcast_fusion.1), channel_id=1, source_target_pairs={{0,1},{1,0},{2,3},{3,2},{4,5},{5,4},{6,7},{7,6},{8,9},{9,8},{10,11... | collective-permute-start | bytes 15925256 | tf_op jit(solution)/shard_map/ppermute | solution.py:157
  1381.1 35.0 %collective-permute-start.88 = (bf16[288,2560]{1,0:T(8,128)(2,1)}, bf16[288,2560]{1,0:T(8,128)(2,1)}, u32[]{:S(2)}, u32[]{:S(2)}) collective-permute-start(bf16[288,2560]{1,0:T(8,128)(2,1)} %add_convert_fusion.6), channel_id=1, source_target_pairs={{8,0},{16,8},{24,16},{28,24},{20,28},{12,20},{4,12},{0,4},{9,1},{1... | collective-permute-start | bytes 4423688 | tf_op jit(solution)/shard_map/ppermute | solution.py:102
  1383.2 34.7 %collective-permute-start.87 = (bf16[288,2560]{1,0:T(8,128)(2,1)}, bf16[288,2560]{1,0:T(8,128)(2,1)}, u32[]{:S(2)}, u32[]{:S(2)}) collective-permute-start(bf16[288,2560]{1,0:T(8,128)(2,1)} %add_convert_fusion.7), channel_id=1, source_target_pairs={{0,8},{8,16},{16,24},{24,28},{28,20},{20,12},{12,4},{4,0},{1,9},{9... | collective-permute-start | bytes 4423688 | tf_op jit(solution)/shard_map/ppermute | solution.py:102
  1384.7 31.2 %collective-permute-start.89 = (bf16[2,288,1152]{2,1,0:T(8,128)(2,1)}, bf16[2,288,1152]{2,1,0:T(8,128)(2,1)}, u32[]{:S(2)}, u32[]{:S(2)}) collective-permute-start(bf16[2,288,1152]{2,1,0:T(8,128)(2,1)} %get-tuple-element.855), channel_id=1, source_target_pairs={{0,2},{1,3},{2,0},{3,1},{4,6},{5,7},{6,4},{7,5},{8,10},{9,11},{10,... | collective-permute-start | bytes 3981320 | tf_op jit(solution)/shard_map/ppermute | solution.py:157
  1429.3 33.6 %collective-permute-start.92 = (bf16[288,2560]{1,0:T(8,128)(2,1)S(1)}, bf16[288,2560]{1,0:T(8,128)(2,1)S(1)}, u32[]{:S(2)}, u32[]{:S(2)}) collective-permute-start(bf16[288,2560]{1,0:T(8,128)(2,1)S(1)} %add_convert_fusion.4), channel_id=1, source_target_pairs={{8,0},{16,8},{24,16},{28,24},{20,28},{12,20},{4,12},{0,4},{9,1},{1... | collective-permute-start | bytes 4423688 | tf_op jit(solution)/shard_map/ppermute | solution.py:102
  1432.0 33.3 %collective-permute-start.91 = (bf16[288,2560]{1,0:T(8,128)(2,1)S(1)}, bf16[288,2560]{1,0:T(8,128)(2,1)S(1)}, u32[]{:S(2)}, u32[]{:S(2)}) collective-permute-start(bf16[288,2560]{1,0:T(8,128)(2,1)S(1)} %add_convert_fusion.5), channel_id=1, source_target_pairs={{0,8},{8,16},{16,24},{24,28},{28,20},{20,12},{12,4},{4,0},{1,9},{9... | collective-permute-start | bytes 4423688 | tf_op jit(solution)/shard_map/ppermute | solution.py:102
  1467.1 31.0 %collective-permute-start.95 = (bf16[2,288,1152]{2,1,0:T(8,128)(2,1)}, bf16[2,288,1152]{2,1,0:T(8,128)(2,1)}, u32[]{:S(2)}, u32[]{:S(2)}) collective-permute-start(bf16[2,288,1152]{2,1,0:T(8,128)(2,1)} %get-tuple-element.872), channel_id=1, source_target_pairs={{0,2},{1,3},{2,0},{3,1},{4,6},{5,7},{6,4},{7,5},{8,10},{9,11},{10,... | collective-permute-start | bytes 3981320 | tf_op jit(solution)/shard_map/ppermute | solution.py:157
  1498.1 33.8 %collective-permute-start.97 = (bf16[288,2560]{1,0:T(8,128)(2,1)}, bf16[288,2560]{1,0:T(8,128)(2,1)}, u32[]{:S(2)}, u32[]{:S(2)}) collective-permute-start(bf16[288,2560]{1,0:T(8,128)(2,1)} %add_convert_fusion.3), channel_id=1, source_target_pairs={{0,2},{1,3},{2,0},{3,1},{4,6},{5,7},{6,4},{7,5},{8,10},{9,11},{10,... | collective-permute-start | bytes 4423688 | tf_op jit(solution)/shard_map/ppermute | solution.py:157
  1499.2 37.5 %collective-permute-start.96 = (bf16[288,1152]{1,0:T(8,128)(2,1)S(1)}, bf16[288,1152]{1,0:T(8,128)(2,1)}, u32[]{:S(2)}, u32[]{:S(2)}) collective-permute-start(bf16[288,1152]{1,0:T(8,128)(2,1)S(1)} %get-tuple-element.878), channel_id=1, source_target_pairs={{0,16},{4,20},{8,24},{12,28},{16,0},{20,4},{24,8},{28,12},{1,17},{... | collective-permute-start | bytes 1990664 | tf_op jit(solution)/shard_map/ppermute | solution.py:157
  1554.9 48.4 %collective-permute-start.101 = (bf16[288,3072]{1,0:T(8,128)(2,1)}, bf16[288,3072]{1,0:T(8,128)(2,1)}, u32[]{:S(2)}, u32[]{:S(2)}) collective-permute-start(bf16[288,3072]{1,0:T(8,128)(2,1)} %pad_maximum_fusion.7), channel_id=1, source_target_pairs={{0,1},{1,0},{2,3},{3,2},{4,5},{5,4},{6,7},{7,6},{8,9},{9,8},{10,11... | collective-permute-start | bytes 5308424 | tf_op jit(solution)/shard_map/ppermute | solution.py:157
  1608.7 31.1 %collective-permute-start.107 = (bf16[288,1152]{1,0:T(8,128)(2,1)S(1)}, bf16[288,1152]{1,0:T(8,128)(2,1)}, u32[]{:S(2)}, u32[]{:S(2)}) collective-permute-start(bf16[288,1152]{1,0:T(8,128)(2,1)S(1)} %get-tuple-element.903), channel_id=1, source_target_pairs={{0,16},{4,20},{8,24},{12,28},{16,0},{20,4},{24,8},{28,12},{1,17},{... | collective-permute-start | bytes 1990664 | tf_op jit(solution)/shard_map/ppermute | solution.py:157
  (194 other events, 2854.2 us)

commit v11 on v8

--- a/solution.py
+++ b/solution.py
@@ -43,7 +43,7 @@
     scaled = grad * gain
     inner = jnp.mean(values * scaled, axis=-1, keepdims=True)
     grad_values = factor * scaled - values * (factor * factor * factor * inner)
-    return grad_values, jnp.sum(grad * values * factor, axis=0)
+    return grad_values, jnp.sum(grad * values * factor, axis=0, keepdims=True)
 
 
 def gelu_parts(values):
@@ -538,6 +538,153 @@
         2 * count * rows * (hidden + depth) + 2 * hidden * depth,
         "weight_back",
     )(*lefts, *rights)
+
+
+def fixed_spec(shape):
+    return pl.BlockSpec(shape, lambda i: (0,) * len(shape))
+
+
+def join_kernel(att_ref, w_ref, x_ref, gain_ref, next_ref, branch_ref, mid_ref, normed_ref, sum_ref):
+    step = pl.program_id(0)
+    heads, _, cols = att_ref.shape
+    tile = w_ref.shape[0]
+    total = dot(att_ref[0], w_ref[:, :cols], NT)
+    for h in range(1, heads):
+        total = total + dot(att_ref[h], w_ref[:, h * cols : (h + 1) * cols], NT)
+    sum_ref[:, pl.ds(pl.multiple_of(step * tile, 128), tile)] = total
+
+    @pl.when(step == pl.num_programs(0) - 1)
+    def _():
+        value = sum_ref[...]
+        mid = x_ref[...].astype(f32) + value * norm_factor(value) * gain_ref[...]
+        branch_ref[...] = value
+        mid_ref[...] = mid
+        normed_ref[...] = (mid * norm_factor(mid) * next_ref[...]).astype(bf16)
+
+
+def join_rows(attended, weights, x, gain, next_gain):
+    rows, depth = x.shape
+    tile = tile_of(depth)
+    return pl.pallas_call(
+        join_kernel,
+        grid=(depth // tile,),
+        in_specs=[
+            fixed_spec(attended.shape),
+            row_spec(tile, weights.shape[1]),
+            fixed_spec(x.shape),
+            fixed_spec((1, depth)),
+            fixed_spec((1, depth)),
+        ],
+        out_specs=[fixed_spec((rows, depth))] * 3,
+        out_shape=[jax.ShapeDtypeStruct((rows, depth), t) for t in (f32, f32, bf16)],
+        scratch_shapes=[pltpu.VMEM((rows, depth), f32)],
+        compiler_params=pltpu.CompilerParams(vmem_limit_bytes=VMEM_LIMIT),
+        cost_estimate=pl.CostEstimate(
+            flops=2 * rows * weights.size,
+            bytes_accessed=2 * weights.size + 12 * rows * depth,
+            transcendentals=0,
+        ),
+        name="join_rows",
+    )(attended, weights, x, gain[None], next_gain[None])
+
+
+def finish_kernel(part_ref, a_ref, b_ref, mid_ref, cot_ref, gain_ref, out_ref, grad_ref, dg_ref):
+    value = part_ref[...].astype(f32) + a_ref[...].astype(f32) + b_ref[...].astype(f32)
+    factor = norm_factor(value)
+    gain = gain_ref[...]
+    out_ref[...] = (mid_ref[...] + value * factor * gain).astype(bf16)
+    grad, dg = norm_back(value, factor, gain, cot_ref[...].astype(f32))
+    grad_ref[...] = grad.astype(bf16)
+    dg_ref[...] = dg
+
+
+def finish_rows(part, a, b, mid, cotangent, gain):
+    rows, depth = mid.shape
+    spec = fixed_spec((rows, depth))
+    return pl.pallas_call(
+        finish_kernel,
+        grid=(1,),
+        in_specs=[spec] * 5 + [fixed_spec((1, depth))],
+        out_specs=[spec, spec, fixed_spec((1, depth))],
+        out_shape=[
+            jax.ShapeDtypeStruct((rows, depth), bf16),
+            jax.ShapeDtypeStruct((rows, depth), bf16),
+            jax.ShapeDtypeStruct((1, depth), f32),
+        ],
+        compiler_params=pltpu.CompilerParams(vmem_limit_bytes=VMEM_LIMIT),
+        cost_estimate=pl.CostEstimate(
+            flops=20 * rows * depth, bytes_accessed=16 * rows * depth, transcendentals=0
+        ),
+        name="finish_rows",
+    )(part, a, b, mid, cotangent, gain[None])
+
+
+def branch_back_kernel(
+    part_ref,
+    a_ref,
+    b_ref,
+    mid_ref,
+    branch_ref,
+    cot_ref,
+    mlp_gain_ref,
+    gain_ref,
+    w_ref,
+    grad_mid_ref,
+    grad_ref,
+    send_ref,
+    mlp_dg_ref,
+    dg_ref,
+    held_ref,
+):
+    @pl.when(pl.program_id(0) == 0)
+    def _():
+        normed = part_ref[...].astype(f32) + a_ref[...].astype(f32) + b_ref[...].astype(f32)
+        mid = mid_ref[...]
+        grad, dg = norm_back(mid, norm_factor(mid), mlp_gain_ref[...], normed)
+        mlp_dg_ref[...] = dg
+        grad_mid = cot_ref[...].astype(f32) + grad
+        grad_mid_ref[...] = grad_mid
+        branch = branch_ref[...]
+        grad, dg = norm_back(branch, norm_factor(branch), gain_ref[...], grad_mid)
+        dg_ref[...] = dg
+        held_ref[...] = grad.astype(bf16)
+        grad_ref[...] = grad.astype(bf16)
+
+    send_ref[0] = dot(held_ref[...], w_ref[...], NN).astype(bf16)
+
+
+def branch_back(part, a, b, mid, branch, cotangent, mlp_gain, gain, weights):
+    rows, depth = mid.shape
+    cols = PAIRED * HEAD_SIZE
+    spec = fixed_spec((rows, depth))
+    line = fixed_spec((1, depth))
+    return pl.pallas_call(
+        branch_back_kernel,
+        grid=(KEY_VALUE_HEADS,),
+        in_specs=[spec] * 6 + [line] * 2 + [column_spec(depth, cols)],
+        out_specs=[
+            spec,
+            spec,
+            pl.BlockSpec((1, rows, cols), lambda i: (i, 0, 0)),
+            line,
+            line,
+        ],
+        out_shape=[
+            jax.ShapeDtypeStruct((rows, depth), f32),
+            jax.ShapeDtypeStruct((rows, depth), bf16),
+            jax.ShapeDtypeStruct((KEY_VALUE_HEADS, rows, cols), bf16),
+            jax.ShapeDtypeStruct((1, depth), f32),
+            jax.ShapeDtypeStruct((1, depth), f32),
+        ],
+        scratch_shapes=[pltpu.VMEM((rows, depth), bf16)],
+        compiler_params=pltpu.CompilerParams(vmem_limit_bytes=VMEM_LIMIT),
+        cost_estimate=pl.CostEstimate(
+            flops=2 * rows * weights.size,
+            bytes_accessed=2 * weights.size + 22 * rows * depth,
+            transcendentals=0,
+        ),
+        name="branch_back",
+    )(part, a, b, mid, branch, cotangent, mlp_gain[None], gain[None], weights)
 
 
 def turn(values, cosine, sine):
@@ -920,7 +1067,6 @@
     ).astype(bf16)
     piece_codes = lax.dynamic_slice_in_dim(mlp_codes, seq_index * piece_rows, piece_rows, 1)
     inputs = [tokens[s].astype(f32) for s in seqs]
-    grad_out = [cotangent[s].astype(f32) for s in seqs]
     cosine, sine = rotary_rows(wide_index * rows + jnp.arange(rows))
 
     blocks, others = [clock.hold(payload)], []
@@ -1044,21 +1190,19 @@
         [pair_last] + [jnp.concatenate([x, y], axis=0) for x, y in zip(moved_a, moved_b)]
     )
 
-    attended, branch, branch_factor, middle, middle_factor, normed_mlp = [], [], [], [], [], []
+    attended, heads_back, branch, middle, normed_mlp = [], [], [], [], []
 
     def heads_to_rows(values):
         split = values.reshape(KEY_VALUE_HEADS, rows, head_cols)
         return jnp.transpose(split, (1, 0, 2)).reshape(rows, KEY_VALUE_HEADS * head_cols)
 
     def join(s):
-        value = dot(attended[s], out_weights[s], NT)
-        factor = norm_factor(value)
-        mid = inputs[s] + value * factor * gain_post_attn
-        mid_factor = norm_factor(mid)
-        return [value, factor, mid, mid_factor, (mid * mid_factor * gain_mlp).astype(bf16)]
+        return join_rows(
+            heads_back[s], out_weights[s], tokens[s], gain_post_attn, gain_mlp
+        )
 
     def keep_join(work):
-        for held, value in zip((branch, branch_factor, middle, middle_factor, normed_mlp), work):
+        for held, value in zip((branch, middle, normed_mlp), work):
             held.append(value)
 
     for s in seqs:
@@ -1074,6 +1218,7 @@
             back, *work = clock.sync(back, *gate_held, *join(s - 1))
             gate_held, work = work[: len(gate_held)], work[len(gate_held) :]
             keep_join(work)
+        heads_back.append(back.reshape(KEY_VALUE_HEADS, rows, head_cols))
         attended.append(heads_to_rows(back))
 
     received = exchange(1)
@@ -1155,10 +1300,9 @@
 
     def finish(s):
         nonlocal gain_fourth
-        factor = norm_factor(mixed[s])
-        layer_out.append((middle[s] + mixed[s] * factor * gain_post_mlp).astype(bf16))
-        grad, gain = norm_back(mixed[s], factor, gain_post_mlp, grad_out[s])
-        grad_mixed.append(grad.astype(bf16))
+        out, grad, gain = finish_rows(*mixed[s], middle[s], cotangent[s], gain_post_mlp)
+        layer_out.append(out)
+        grad_mixed.append(grad)
         gain_fourth = gain_fourth + gain
 
     grad_group, grad_gate, grad_up, grad_parts, grad_normed_mlp = [], [], [], [], []
@@ -1193,7 +1337,7 @@
             a, b = hop(a, b, half_wide)
             a, b, *work = clock.sync(a, b, *work)
             other.append(work)
-        return part_of(0).astype(f32) + a.astype(f32) + b.astype(f32), other
+        return (part, a, b), other
 
     a, b = first_sum(parts[0])
     a, b, *opened = clock.sync(a, b, *open_part(1, 0))
@@ -1243,14 +1387,17 @@
 
     def back_branch(s):
         nonlocal gain_third, gain_second
-        grad, gain = norm_back(middle[s], middle_factor[s], gain_mlp, grad_normed_mlp[s])
-        gain_third = gain_third + gain
-        grad_mid = grad_out[s] + grad
-        grad, gain = norm_back(branch[s], branch_factor[s], gain_post_attn, grad_mid)
-        gain_second = gain_second + gain
-        grad = grad.astype(bf16)
-        send = dot(grad, out_weights[s], NN).astype(bf16)
-        send = jnp.transpose(send.reshape(rows, KEY_VALUE_HEADS, head_cols), (1, 0, 2))
+        grad_mid, grad, send, third, second = branch_back(
+            *[clock.hold(v) for v in grad_normed_mlp[s]],
+            middle[s],
+            branch[s],
+            cotangent[s],
+            gain_mlp,
+            gain_post_attn,
+            out_weights[s],
+        )
+        gain_third = gain_third + third
+        gain_second = gain_second + second
         return [grad_mid, grad, send.reshape(wide, class_rows, head_cols)]
 
     def keep_branch(work):
@@ -1522,7 +1669,7 @@
     gate_own, gate_send = column_parts(gate_grad[0], 2), column_parts(gate_grad[1], 2)
     first_tokens, gain_first = back_tokens(0, grad_first)
     last_tokens, gain = back_tokens(1, grad_last)
-    gains = jnp.stack([gain_first + gain, gain_second, gain_third, gain_fourth])
+    gains = jnp.concatenate([gain_first + gain, gain_second, gain_third, gain_fourth], axis=0)
     wide_bits = [1 << i for i in range(wide.bit_length() - 1)]
     gains, *gate_send = clock.sync(add_swapped(gains, "wide", wide_bits[1:]), *gate_send)
     moved = exchange_grad(gate_send[0])

time: 1680 us -> 1630 us (0.970)
  Pallas kernels: 492 us -> 557 us
  waiting for transfers between devices: 579 us -> 536 us
  other arithmetic: 161 us -> 124 us
  local copies, waits for them, and re-layouts: 156 us -> 135 us
  matrix products: 120 us -> 99.9 us
    pallas_call x0 -> x6, Pallas kernels: none -> 65.3 us  [the longest x2 26.5 us: branch_back(): pl.pallas_call(branch_back_kernel, grid=(KEY_VALUE_HEADS,), in_specs=[spe...]
    ppermute x63, waiting for transfers between devices: 311 us -> 285 us  [swap(): return lax.ppermute(value, axis, [(i, i ^ bit) for i in range(size)])]
    reduce_sum x7 -> x1, other arithmetic: 23.2 us -> 1.39 us  [norm_back(): return (grad_values, jnp.sum(grad * values * factor, axis=0, keepdims=True))]
    dot_general x12 -> x8, matrix products: 120 us -> 99.9 us  [dot(): return lax.dot_general(a, b, (dims, ((), ())), preferred_element_type=f32)]
    unnamed x314 -> x274, local copies, waits for them, and re-layouts: 60.6 us -> 53.4 us
  transfers between devices with their start and end apart: 129 -> 129, of which waited for: 64 -> 61; matrix products, arithmetic and copies ran while one was open for 17% -> 16% of each run, Pallas kernels for 28% -> 32%
where the time goes in v11:
time: 1630 us; the launch traced here: 1620 us
  Pallas kernels  557 us (34%)
  waiting for transfers between devices  536 us (33%)
  starting transfers between devices  162 us (10%)
  local copies, waits for them, and re-layouts  135 us (8%)
  other arithmetic  124 us (8%)
  matrix products  99.9 us (6%)
    ppermute x63, waiting for transfers between devices, swap(): return lax.ppermute(value, axis, [(i, i ^ bit) for i in range(size)])  285 us
    ppermute x48, waiting for transfers between devices, hop(): return (lax.ppermute(a, 'wide', up), lax.ppermute(b, 'wide', down))  158 us
    dot_general x8, matrix products, dot(): return lax.dot_general(a, b, (dims, ((), ())), preferred_element_type=f32)  99.9 us
    pallas_call x3, Pallas kernels, weight_back(): kernel_call(functools.partial(weight_kernel, count=count), hidden // tile...  87.1 us
    ppermute x6, waiting for transfers between devices, class_ring(): return lax.ppermute(value, 'wide', perm)  71.9 us
    pallas_call x4, Pallas kernels, input_back(): kernel_call(input_back_kernel, tiles, [whole_spec(grad_gate.shape)] * 2 +...  69.2 us
    convert_element_type x27, other arithmetic, low_sum(): return sum((t.astype(f32) for t in terms)).astype(bf16)  62.7 us
    pallas_call x3, Pallas kernels, open_forward(): kernel_call(open_kernel, tiles, [whole_spec(x.shape)] + [row_spec(tile, d...  62.5 us
  transfers between devices with their start and end apart: 129, of which 61 were waited for; matrix products, arithmetic and copies ran while one was open for 16% of the time, Pallas kernels for 32%

profile of v11, /device:TPU:0, one launch (start us, length us, event | category | flops | bytes accessed | tf_op | source)
XLA Modules:
  0.0 1616.4 jit_solution(14715024243822941267)
XLA Ops:
  11.2 25.1 %own_slices.1 = (bf16[2304,2304]{1,0:T(8,128)(2,1)}, bf16[2304,2304]{1,0:T(8,128)(2,1)}, bf16[2304,2304]{1,0:T(8,128)(2,1)}, bf16[2304,2304]{1,0:T(8,128)(2,1)},...) custom-call(s32[4]{0:T(128)} %pad_add_fusion.pieces, s32[4]{0:T(128)} %pad_add_fusion.1.info, ...), custom_call_target="tpu_custom_call" | custom-call | flops 159252480 | bytes 63700992 | tf_op jit(solution)/shard_map/own_slices/pallas_call | solution.py:297
  49.6 27.7 %collective-permute-done.3.refs_0_ = bf16[288,2560]{1,0:T(8,128)(2,1)} collective-permute-done((bf16[288,2560]{1,0:T(8,128)(2,1)S(1)}, bf16[288,2560]{1,0:T(8,128)(2,1)}, u32[]{:S(2)}, u32[]{:S(2)}) %collective-permute-start.3) | collective-permute-done | bytes 1474592 | tf_op jit(solution)/shard_map/ppermute | solution.py:102
  94.2 20.1 %collective-permute-done.7.refs_0_ = bf16[288,2560]{1,0:T(8,128)(2,1)S(1)} collective-permute-done((bf16[288,2560]{1,0:T(8,128)(2,1)}, bf16[288,2560]{1,0:T(8,128)(2,1)S(1)}, u32[]{:S(2)}, u32[]{:S(2)}) %collective-permute-start.7) | collective-permute-done | bytes 1474592 | tf_op jit(solution)/shard_map/ppermute | solution.py:102
  177.7 24.5 %collective-permute-done.15.refs_0_ = bf16[288,2304]{1,0:T(8,128)(2,1)} collective-permute-done((bf16[288,2304]{1,0:T(8,128)(2,1)}, bf16[288,2304]{1,0:T(8,128)(2,1)}, u32[]{:S(2)}, u32[]{:S(2)}) %collective-permute-start.15) | collective-permute-done | bytes 1327136 | tf_op jit(solution)/shard_map/ppermute | solution.py:157
  240.0 21.8 %collective-permute-done.17.refs_1_ = bf16[4,256,512]{2,1,0:T(8,128)(2,1)} collective-permute-done((bf16[4,256,512]{2,1,0:T(8,128)(2,1)S(1)}, bf16[4,256,512]{2,1,0:T(8,128)(2,1)}, u32[]{:S(2)}, u32[]{:S(2)}) %collective-permute-start.17) | collective-permute-done | bytes 1048608 | tf_op jit(solution)/shard_map/ppermute | solution.py:177
  270.1 20.5 %collective-permute-done.18 = bf16[2,256,512]{2,1,0:T(8,128)(2,1)S(1)} collective-permute-done((bf16[2,256,512]{2,1,0:T(8,128)(2,1)S(1)}, bf16[2,256,512]{2,1,0:T(8,128)(2,1)S(1)}, u32[]{:S(2)}, u32[]{:S(2)}) %collective-permute-start.18) | collective-permute-done | bytes 524320 | tf_op jit(solution)/shard_map/ppermute | solution.py:177
  298.2 11.5 attn_forward.2
  309.7 12.0 collective-permute-done.20
  330.0 20.6 %out_slices.1 = (bf16[2304,2048]{1,0:T(8,128)(2,1)}, bf16[2304,2048]{1,0:T(8,128)(2,1)}) custom-call(s32[8]{0:T(128)} %stack.163.places, s32[4]{0:T(128)} %pad_add_fusion.1.info, bf16[8,288,512]{2,1,0:T(8,128)(2,1)} %copy-done.41, bf16[8,288,512]{2,1,0:T(8,128)(2,1)} %collective-permute-done.19.refs_1_, ...), custom_call_target="tpu_custom_call" | custom-call | flops 94371840 | bytes 28311552 | tf_op jit(solution)/shard_map/out_slices/pallas_call | solution.py:260
  351.6 11.4 attn_forward.3
  370.7 13.1 join_rows.2
  405.1 13.2 join_rows.3
  418.3 34.0 %collective-permute-done.25.refs_0_ = bf16[288,2304]{1,0:T(8,128)(2,1)} collective-permute-done((bf16[288,2304]{1,0:T(8,128)(2,1)S(1)}, bf16[288,2304]{1,0:T(8,128)(2,1)}, u32[]{:S(2)}, u32[]{:S(2)}) %collective-permute-start.25) | collective-permute-done | bytes 1327136 | tf_op jit(solution)/shard_map/ppermute | solution.py:157
  452.8 30.8 %collective-permute-done.27.refs_1_ = bf16[288,2304]{1,0:T(8,128)(2,1)S(1)} collective-permute-done((bf16[288,2304]{1,0:T(8,128)(2,1)}, bf16[288,2304]{1,0:T(8,128)(2,1)S(1)}, u32[]{:S(2)}, u32[]{:S(2)}) %collective-permute-start.27) | collective-permute-done | bytes 1327136 | tf_op jit(solution)/shard_map/ppermute | solution.py:157
  483.6 28.5 %collective-permute-done.26.refs_0_ = bf16[288,2304]{1,0:T(8,128)(2,1)} collective-permute-done((bf16[288,2304]{1,0:T(8,128)(2,1)S(1)}, bf16[288,2304]{1,0:T(8,128)(2,1)}, u32[]{:S(2)}, u32[]{:S(2)}) %collective-permute-start.26) | collective-permute-done | bytes 1327136 | tf_op jit(solution)/shard_map/ppermute | solution.py:157
  516.3 26.3 %collective-permute-done.28 = bf16[256,2304]{1,0:T(8,128)(2,1)S(1)} collective-permute-done((bf16[256,2304]{1,0:T(8,128)(2,1)}, bf16[256,2304]{1,0:T(8,128)(2,1)S(1)}, u32[]{:S(2)}, u32[]{:S(2)}) %collective-permute-start.28) | collective-permute-done | bytes 1179680 | tf_op jit(solution)/shard_map/ppermute | solution.py:102
  570.3 29.1 %open_forward.3 = (f32[1024,2304]{1,0:T(8,128)}, f32[1024,2304]{1,0:T(8,128)}, bf16[1024,2304]{1,0:T(8,128)(2,1)}) custom-call(bf16[1024,2304]{1,0:T(8,128)(2,1)} %constant_dynamic-update-slice_fusion.4.refs_0_.refs_2_, bf16[2304,2304]{1,0:T(8,128)(2,1)} %get-tuple-element.655.refs_1_.refs_2_, bf16[2304,2304]{1,0:T(8,128)(2,1)} %get-tuple-element.656.refs_2_.refs_3_), custom_call_target="tpu_custom_call" | custom-call | flops 21743271936 | bytes 49545216 | tf_op jit(solution)/shard_map/open_forward/pallas_call | solution.py:448
  616.2 14.9 convolution_convert_fusion.3.part_ref
  635.8 18.1 %open_forward.4 = (f32[1024,2304]{1,0:T(8,128)}, f32[1024,2304]{1,0:T(8,128)}, bf16[1024,2304]{1,0:T(8,128)(2,1)}) custom-call(bf16[1024,2304]{1,0:T(8,128)(2,1)} %constant_dynamic-update-slice_fusion.9.refs_0_.refs_3_, bf16[2304,2304]{1,0:T(8,128)(2,1)} %get-tuple-element.685.refs_1_.refs_2_, bf16[2304,2304]{1,0:T(8,128)(2,1)} %get-tuple-element.686.refs_2_.refs_3_), custom_call_target="tpu_custom_call" | custom-call | flops 12079595520 | bytes 29622272 | tf_op jit(solution)/shard_map/open_forward/pallas_call | solution.py:448
  658.8 15.3 open_forward.5
  689.5 13.5 convolution_convert_fusion.2.part_ref
  732.1 15.0 open_back.4
  750.9 12.8 open_back.5
  763.7 18.4 %input_back.4.refs_4_ = bf16[1024,2304]{1,0:T(8,128)(2,1)} custom-call(bf16[1024,2304]{1,0:T(8,128)(2,1)} %get-tuple-element.858.refs_0_, bf16[1024,2304]{1,0:T(8,128)(2,1)} %get-tuple-element.837.refs_1_.refs_0_, bf16[2304,2304]{1,0:T(8,128)(2,1)} %get-tuple-element.655.refs_1_.refs_2_, bf16[2304,2304]{1,0:T(8,128)(2,1)} %get-tuple-element.656.refs_2_.refs_3_), custom_call_target="tpu_custom_call" | custom-call | flops 12079595520 | bytes 23855104 | tf_op jit(solution)/shard_map/input_back/pallas_call | solution.py:505
  794.1 15.8 input_back.5.part_ref
  817.1 13.6 collective-permute-done.55
  835.8 14.9 open_back.6
  853.8 12.8 open_back.7
  866.6 18.4 %input_back.6.refs_4_ = bf16[1024,2304]{1,0:T(8,128)(2,1)} custom-call(bf16[1024,2304]{1,0:T(8,128)(2,1)} %get-tuple-element.859.refs_0_.refs_1_, bf16[1024,2304]{1,0:T(8,128)(2,1)} %get-tuple-element.838.refs_1_, bf16[2304,2304]{1,0:T(8,128)(2,1)} %get-tuple-element.685.refs_1_.refs_2_, bf16[2304,2304]{1,0:T(8,128)(2,1)} %get-tuple-element.686.refs_2_.refs_3_), custom_call_target="tpu_custom_call" | custom-call | flops 12079595520 | bytes 23855104 | tf_op jit(solution)/shard_map/input_back/pallas_call | solution.py:505
  885.0 16.6 %input_back.7.part_ref = bf16[1024,2304]{1,0:T(8,128)(2,1)} custom-call(bf16[1024,2304]{1,0:T(8,128)(2,1)} %get-tuple-element.859.refs_0_.refs_1_, bf16[1024,2304]{1,0:T(8,128)(2,1)} %get-tuple-element.838.refs_1_, bf16[2304,2304]{1,0:T(8,128)(2,1)} %get-tuple-element.685.refs_1_.refs_2_, ...), custom_call_target="tpu_custom_call", output_to_operand_aliasing={{}: (4, {})} | custom-call | flops 9663676416 | bytes 20971520 | tf_op jit(solution)/shard_map/input_back/pallas_call | solution.py:505
  905.2 13.2 branch_back.2
  922.8 29.0 %weight_back.3 = bf16[2304,2304]{1,0:T(8,128)(2,1)} custom-call(bf16[1024,2304]{1,0:T(8,128)(2,1)} %get-tuple-element.786.refs_0_, bf16[1024,2304]{1,0:T(8,128)(2,1)} %get-tuple-element.787.refs_1_, bf16[1024,2304]{1,0:T(8,128)(2,1)} %copy-done.3, bf16[1024,2304]{1,0:T(8,128)(2,1)} %constant_dynamic-update-slice_fusion.19.refs_0_.refs_3_), custom_call_target="tpu_custom_call" | custom-call | flops 21743271936 | bytes 29491200 | tf_op jit(solution)/shard_map/weight_back/pallas_call | solution.py:531
  967.1 13.3 branch_back.3
  1008.0 17.4 %attn_backward.2 = (bf16[1024,512]{1,0:T(8,128)(2,1)}, bf16[4,256,512]{2,1,0:T(8,128)(2,1)}, bf16[4,256,512]{2,1,0:T(8,128)(2,1)}) custom-call(s32[1]{0:T(128)} %bitcast.41.info, bf16[1024,512]{1,0:T(8,128)(2,1)} %bitcast.256, bf16[1024,512]{1,0:T(8,128)(2,1)} %bitcast.262, f32[1024,512]{1,0:T(8,128)} %get-tuple-element.810.exact_ref, ...), custom_call_target="tpu_custom_call" | custom-call | flops 10737418240 | bytes 9437184 | tf_op jit(solution)/shard_map/attn_backward/pallas_call | solution.py:968
  1035.4 17.5 %attn_backward.3 = (bf16[1024,512]{1,0:T(8,128)(2,1)}, bf16[4,256,512]{2,1,0:T(8,128)(2,1)}, bf16[4,256,512]{2,1,0:T(8,128)(2,1)}) custom-call(s32[1]{0:T(128)} %bitcast.41.info, bf16[1024,512]{1,0:T(8,128)(2,1)} %bitcast.254, bf16[1024,512]{1,0:T(8,128)(2,1)} %bitcast.69.grad_ref, f32[1024,512]{1,0:T(8,128)} %get-tuple-element.825.exact_ref, ...), custom_call_target="tpu_custom_call" | custom-call | flops 10737418240 | bytes 9437184 | tf_op jit(solution)/shard_map/attn_backward/pallas_call | solution.py:968
  1078.3 29.1 %weight_back.4 = bf16[2304,2304]{1,0:T(8,128)(2,1)} custom-call(bf16[1024,2304]{1,0:T(8,128)(2,1)} %get-tuple-element.837.refs_1_.refs_0_, bf16[1024,2304]{1,0:T(8,128)(2,1)} %get-tuple-element.838.refs_1_, bf16[1024,2304]{1,0:T(8,128)(2,1)} %constant_dynamic-update-slice_fusion.4.refs_0_.refs_2_, ...), custom_call_target="tpu_custom_call" | custom-call | flops 21743271936 | bytes 29491200 | tf_op jit(solution)/shard_map/weight_back/pallas_call | solution.py:531
  1127.2 17.6 %collective-permute-done.72 = bf16[4,256,512]{2,1,0:T(8,128)(2,1)} collective-permute-done((bf16[4,256,512]{2,1,0:T(8,128)(2,1)}, bf16[4,256,512]{2,1,0:T(8,128)(2,1)}, u32[]{:S(2)}, u32[]{:S(2)}) %collective-permute-start.72) | collective-permute-done | bytes 1048608 | tf_op jit(solution)/shard_map/ppermute | solution.py:177
  1164.0 29.0 %weight_back.5 = bf16[2304,2304]{1,0:T(8,128)(2,1)} custom-call(bf16[1024,2304]{1,0:T(8,128)(2,1)} %get-tuple-element.858.refs_0_, bf16[1024,2304]{1,0:T(8,128)(2,1)} %get-tuple-element.859.refs_0_.refs_1_, bf16[1024,2304]{1,0:T(8,128)(2,1)} %constant_dynamic-update-slice_fusion.4.refs_0_.refs_2_, ...), custom_call_target="tpu_custom_call" | custom-call | flops 21743271936 | bytes 29491200 | tf_op jit(solution)/shard_map/weight_back/pallas_call | solution.py:531
  1206.2 13.8 turn_back.1
  1234.1 13.1 collective-permute-done.77
  1262.1 11.9 collective-permute-done.80
  1293.7 16.2 %collective-permute-done.82 = bf16[144,2560]{1,0:T(8,128)(2,1)S(1)} collective-permute-done((bf16[144,2560]{1,0:T(8,128)(2,1)S(1)}, bf16[144,2560]{1,0:T(8,128)(2,1)S(1)}, u32[]{:S(2)}, u32[]{:S(2)}) %collective-permute-start.82) | collective-permute-done | bytes 737312 | tf_op jit(solution)/shard_map/ppermute | solution.py:102
  1321.5 25.1 %collective-permute-done.86 = bf16[2,288,1152]{2,1,0:T(8,128)(2,1)} collective-permute-done((bf16[2,288,1152]{2,1,0:T(8,128)(2,1)}, bf16[2,288,1152]{2,1,0:T(8,128)(2,1)}, u32[]{:S(2)}, u32[]{:S(2)}) %collective-permute-start.86) | collective-permute-done | bytes 1327136 | tf_op jit(solution)/shard_map/ppermute | solution.py:157
  1360.0 24.9 %collective-permute-done.89 = bf16[2,288,1152]{2,1,0:T(8,128)(2,1)S(1)} collective-permute-done((bf16[2,288,1152]{2,1,0:T(8,128)(2,1)S(1)}, bf16[2,288,1152]{2,1,0:T(8,128)(2,1)S(1)}, u32[]{:S(2)}, u32[]{:S(2)}) %collective-permute-start.89) | collective-permute-done | bytes 1327136 | tf_op jit(solution)/shard_map/ppermute | solution.py:157
  1427.3 20.8 %fusion.50 = f32[256,2304]{1,0:T(8,128)} fusion(bf16[256,4096]{1,0:T(8,128)(2,1)} %get-tuple-element.913, bf16[2304,4096]{1,0:T(8,128)(2,1)} %get-tuple-element.529.wq_ref.wk_ref.wv_ref), kind=kOutput, calls=%fused_computation.268 | convolution fusion | flops 4831838208 | bytes 23330816 | tf_op jit(solution)/shard_map/dot_general | solution.py:26
  1449.6 20.6 %fusion.51 = f32[256,2304]{1,0:T(8,128)} fusion(bf16[256,4096]{1,0:T(8,128)(2,1)} %get-tuple-element.921, bf16[2304,4096]{1,0:T(8,128)(2,1)} %get-tuple-element.532.wq_ref.wk_ref.wv_ref), kind=kOutput, calls=%fused_computation.269 | convolution fusion | flops 4831838208 | bytes 23330816 | tf_op jit(solution)/shard_map/dot_general | solution.py:26
  1510.6 12.3 collective-permute-done.102
  1537.0 11.7 collective-permute-done.108
  (711 shorter events, 706.7 us)
Async XLA Ops:
  3.8 38.4 %collective-permute-start = (bf16[288,2560]{1,0:T(8,128)(2,1)S(1)}, bf16[288,2560]{1,0:T(8,128)(2,1)S(1)}, u32[]{:S(2)}, u32[]{:S(2)}) collective-permute-start(bf16[288,2560]{1,0:T(8,128)(2,1)S(1)} %pad_maximum_fusion.11.refs_0_), channel_id=1, source_target_pairs={{0,8},{8,16},{16,24},{24,28},{28,20},{20,12},{12,4},{4,0},{1,9},{9... | collective-permute-start | bytes 4423688 | tf_op jit(solution)/shard_map/ppermute | solution.py:102
  6.9 35.3 %collective-permute-start.1 = (bf16[288,2560]{1,0:T(8,128)(2,1)S(1)}, bf16[288,2560]{1,0:T(8,128)(2,1)}, u32[]{:S(2)}, u32[]{:S(2)}) collective-permute-start(bf16[288,2560]{1,0:T(8,128)(2,1)S(1)} %pad_maximum_fusion.11.refs_0_), channel_id=1, source_target_pairs={{8,0},{16,8},{24,16},{28,24},{20,28},{12,20},{4,12},{0,4},{9,1},{1... | collective-permute-start | bytes 4423688 | tf_op jit(solution)/shard_map/ppermute | solution.py:102
  6.9 35.3 %collective-permute-start.2 = (bf16[288,2560]{1,0:T(8,128)(2,1)S(1)}, bf16[288,2560]{1,0:T(8,128)(2,1)}, u32[]{:S(2)}, u32[]{:S(2)}) collective-permute-start(bf16[288,2560]{1,0:T(8,128)(2,1)S(1)} %pad_maximum_fusion.11.refs_0_), channel_id=1, source_target_pairs={{0,1},{1,0},{2,3},{3,2},{4,5},{5,4},{6,7},{7,6},{8,9},{9,8},{10,11... | collective-permute-start | bytes 4423688 | tf_op jit(solution)/shard_map/ppermute | solution.py:157
  42.2 35.0 %collective-permute-start.3 = (bf16[288,2560]{1,0:T(8,128)(2,1)S(1)}, bf16[288,2560]{1,0:T(8,128)(2,1)}, u32[]{:S(2)}, u32[]{:S(2)}) collective-permute-start(bf16[288,2560]{1,0:T(8,128)(2,1)S(1)} %collective-permute-done.refs_2_), channel_id=1, source_target_pairs={{0,8},{8,16},{16,24},{24,28},{28,20},{20,12},{12,4},{4,0},{1,9},{9... | collective-permute-start | bytes 4423688 | tf_op jit(solution)/shard_map/ppermute | solution.py:102
  44.3 35.0 %collective-permute-start.5 = (bf16[288,2560]{1,0:T(8,128)(2,1)S(1)}, bf16[288,2560]{1,0:T(8,128)(2,1)S(1)}, u32[]{:S(2)}, u32[]{:S(2)}) collective-permute-start(bf16[288,2560]{1,0:T(8,128)(2,1)S(1)} %collective-permute-done.refs_2_), channel_id=1, source_target_pairs={{0,1},{1,0},{2,3},{3,2},{4,5},{5,4},{6,7},{7,6},{8,9},{9,8},{10,11... | collective-permute-start | bytes 4423688 | tf_op jit(solution)/shard_map/ppermute | solution.py:157
  44.5 34.8 %collective-permute-start.4 = (bf16[288,2560]{1,0:T(8,128)(2,1)}, bf16[288,2560]{1,0:T(8,128)(2,1)}, u32[]{:S(2)}, u32[]{:S(2)}) collective-permute-start(bf16[288,2560]{1,0:T(8,128)(2,1)} %collective-permute-done.1.refs_4_), channel_id=1, source_target_pairs={{8,0},{16,8},{24,16},{28,24},{20,28},{12,20},{4,12},{0,4},{9,1},{1... | collective-permute-start | bytes 4423688 | tf_op jit(solution)/shard_map/ppermute | solution.py:102
  44.8 34.5 %collective-permute-start.6 = (bf16[288,2560]{1,0:T(8,128)(2,1)}, bf16[288,2560]{1,0:T(8,128)(2,1)S(1)}, u32[]{:S(2)}, u32[]{:S(2)}) collective-permute-start(bf16[288,2560]{1,0:T(8,128)(2,1)} %collective-permute-done.1.refs_4_), channel_id=1, source_target_pairs={{0,1},{1,0},{2,3},{3,2},{4,5},{5,4},{6,7},{7,6},{8,9},{9,8},{10,11... | collective-permute-start | bytes 4423688 | tf_op jit(solution)/shard_map/ppermute | solution.py:157
  80.4 33.9 %collective-permute-start.7 = (bf16[288,2560]{1,0:T(8,128)(2,1)}, bf16[288,2560]{1,0:T(8,128)(2,1)S(1)}, u32[]{:S(2)}, u32[]{:S(2)}) collective-permute-start(bf16[288,2560]{1,0:T(8,128)(2,1)} %collective-permute-done.3.refs_0_), channel_id=1, source_target_pairs={{0,8},{8,16},{16,24},{24,28},{28,20},{20,12},{12,4},{4,0},{1,9},{9... | collective-permute-start | bytes 4423688 | tf_op jit(solution)/shard_map/ppermute | solution.py:102
  82.0 34.0 %collective-permute-start.8 = (bf16[288,2560]{1,0:T(8,128)(2,1)}, bf16[288,2560]{1,0:T(8,128)(2,1)S(1)}, u32[]{:S(2)}, u32[]{:S(2)}) collective-permute-start(bf16[288,2560]{1,0:T(8,128)(2,1)} %collective-permute-done.4.refs_2_), channel_id=1, source_target_pairs={{8,0},{16,8},{24,16},{28,24},{20,28},{12,20},{4,12},{0,4},{9,1},{1... | collective-permute-start | bytes 4423688 | tf_op jit(solution)/shard_map/ppermute | solution.py:102
  82.9 33.2 %collective-permute-start.9 = (bf16[288,2560]{1,0:T(8,128)(2,1)}, bf16[288,2560]{1,0:T(8,128)(2,1)}, u32[]{:S(2)}, u32[]{:S(2)}) collective-permute-start(bf16[288,2560]{1,0:T(8,128)(2,1)} %collective-permute-done.3.refs_0_), channel_id=1, source_target_pairs={{0,1},{1,0},{2,3},{3,2},{4,5},{5,4},{6,7},{7,6},{8,9},{9,8},{10,11... | collective-permute-start | bytes 4423688 | tf_op jit(solution)/shard_map/ppermute | solution.py:157
  141.0 61.1 %collective-permute-start.15 = (bf16[288,2304]{1,0:T(8,128)(2,1)}, bf16[288,2304]{1,0:T(8,128)(2,1)}, u32[]{:S(2)}, u32[]{:S(2)}) collective-permute-start(bf16[288,2304]{1,0:T(8,128)(2,1)} %get-tuple-element.520), channel_id=1, source_target_pairs={{0,16},{4,20},{8,24},{12,28},{16,0},{20,4},{24,8},{28,12},{1,17},{... | collective-permute-start | bytes 3981320 | tf_op jit(solution)/shard_map/ppermute | solution.py:157
  238.5 53.0 %collective-permute-start.19 = (bf16[8,288,512]{2,1,0:T(8,128)(2,1)}, bf16[8,288,512]{2,1,0:T(8,128)(2,1)}, u32[]{:S(2)}, u32[]{:S(2)}) collective-permute-start(bf16[8,288,512]{2,1,0:T(8,128)(2,1)} %copy-done.41), channel_id=1, source_target_pairs={{0,2},{1,3},{2,0},{3,1},{4,6},{5,7},{6,4},{7,5},{8,10},{9,11},{10,... | collective-permute-start | bytes 7077896 | tf_op jit(solution)/shard_map/ppermute | solution.py:157
  322.6 40.4 %all-to-all-start.4 = ((bf16[8,128,512]{2,1,0:T(8,128)(2,1)}), bf16[8,128,512]{2,1,0:T(8,128)(2,1)S(1)}, u32[]{:S(2)}, u32[]{:S(2)}) async-start(bf16[8,128,512]{2,1,0:T(8,128)(2,1)} %bitcast.264), calls=%async_computation.4 | async-start | bytes 2097152 | tf_op jit(solution)/shard_map/all_to_all | solution.py:161
  326.3 36.7 %collective-permute-start.22 = (bf16[288,2304]{1,0:T(8,128)(2,1)}, bf16[288,2304]{1,0:T(8,128)(2,1)}, u32[]{:S(2)}, u32[]{:S(2)}) collective-permute-start(bf16[288,2304]{1,0:T(8,128)(2,1)} %collective-permute-done.15.refs_0_), channel_id=1, source_target_pairs={{0,2},{1,3},{2,0},{3,1},{4,6},{5,7},{6,4},{7,5},{8,10},{9,11},{10,... | collective-permute-start | bytes 3981320 | tf_op jit(solution)/shard_map/ppermute | solution.py:157
  363.0 31.3 %all-to-all-start.5 = ((bf16[8,128,512]{2,1,0:T(8,128)(2,1)}), bf16[8,128,512]{2,1,0:T(8,128)(2,1)S(1)}, u32[]{:S(2)}, u32[]{:S(2)}) async-start(bf16[8,128,512]{2,1,0:T(8,128)(2,1)} %bitcast.265), calls=%async_computation.5 | async-start | bytes 2097152 | tf_op jit(solution)/shard_map/all_to_all | solution.py:161
  394.3 58.1 %collective-permute-start.25 = (bf16[288,2304]{1,0:T(8,128)(2,1)S(1)}, bf16[288,2304]{1,0:T(8,128)(2,1)}, u32[]{:S(2)}, u32[]{:S(2)}) collective-permute-start(bf16[288,2304]{1,0:T(8,128)(2,1)S(1)} %copy-done.54), channel_id=1, source_target_pairs={{0,16},{4,20},{8,24},{12,28},{16,0},{20,4},{24,8},{28,12},{1,17},{... | collective-permute-start | bytes 3981320 | tf_op jit(solution)/shard_map/ppermute | solution.py:157
  452.3 31.3 %collective-permute-start.27 = (bf16[288,2304]{1,0:T(8,128)(2,1)}, bf16[288,2304]{1,0:T(8,128)(2,1)S(1)}, u32[]{:S(2)}, u32[]{:S(2)}) collective-permute-start(bf16[288,2304]{1,0:T(8,128)(2,1)} %collective-permute-done.25.refs_0_), channel_id=1, source_target_pairs={{0,2},{1,3},{2,0},{3,1},{4,6},{5,7},{6,4},{7,5},{8,10},{9,11},{10,... | collective-permute-start | bytes 3981320 | tf_op jit(solution)/shard_map/ppermute | solution.py:157
  452.8 59.3 %collective-permute-start.26 = (bf16[288,2304]{1,0:T(8,128)(2,1)S(1)}, bf16[288,2304]{1,0:T(8,128)(2,1)}, u32[]{:S(2)}, u32[]{:S(2)}) collective-permute-start(bf16[288,2304]{1,0:T(8,128)(2,1)S(1)} %copy-done.53), channel_id=1, source_target_pairs={{0,16},{4,20},{8,24},{12,28},{16,0},{20,4},{24,8},{28,12},{1,17},{... | collective-permute-start | bytes 3981320 | tf_op jit(solution)/shard_map/ppermute | solution.py:157
  512.1 31.4 %collective-permute-start.32 = (bf16[288,2304]{1,0:T(8,128)(2,1)}, bf16[288,2304]{1,0:T(8,128)(2,1)}, u32[]{:S(2)}, u32[]{:S(2)}) collective-permute-start(bf16[288,2304]{1,0:T(8,128)(2,1)} %collective-permute-done.26.refs_0_), channel_id=1, source_target_pairs={{0,2},{1,3},{2,0},{3,1},{4,6},{5,7},{6,4},{7,5},{8,10},{9,11},{10,... | collective-permute-start | bytes 3981320 | tf_op jit(solution)/shard_map/ppermute | solution.py:157
  566.5 34.0 %collective-permute-start.37 = (bf16[256,2304]{1,0:T(8,128)(2,1)S(1)}, bf16[256,2304]{1,0:T(8,128)(2,1)S(1)}, u32[]{:S(2)}, u32[]{:S(2)}) collective-permute-start(bf16[256,2304]{1,0:T(8,128)(2,1)S(1)} %copy-done.71), channel_id=1, source_target_pairs={{0,8},{8,12},{12,4},{4,0},{16,24},{24,28},{28,20},{20,16},{1,9},{9... | collective-permute-start | bytes 3538952 | tf_op jit(solution)/shard_map/ppermute | solution.py:102
  568.3 32.3 %collective-permute-start.38 = (bf16[256,2304]{1,0:T(8,128)(2,1)S(1)}, bf16[256,2304]{1,0:T(8,128)(2,1)S(1)}, u32[]{:S(2)}, u32[]{:S(2)}) collective-permute-start(bf16[256,2304]{1,0:T(8,128)(2,1)S(1)} %copy-done.71), channel_id=1, source_target_pairs={{8,0},{12,8},{4,12},{0,4},{24,16},{28,24},{20,28},{16,20},{9,1},{1... | collective-permute-start | bytes 3538952 | tf_op jit(solution)/shard_map/ppermute | solution.py:102
  748.7 33.4 %collective-permute-start.52 = (bf16[256,2304]{1,0:T(8,128)(2,1)S(1)}, bf16[256,2304]{1,0:T(8,128)(2,1)S(1)}, u32[]{:S(2)}, u32[]{:S(2)}) collective-permute-start(bf16[256,2304]{1,0:T(8,128)(2,1)S(1)} %pad_maximum_fusion.21), channel_id=1, source_target_pairs={{8,0},{12,8},{4,12},{0,4},{24,16},{28,24},{20,28},{16,20},{9,1},{1... | collective-permute-start | bytes 3538952 | tf_op jit(solution)/shard_map/ppermute | solution.py:102
  750.1 32.0 %collective-permute-start.51 = (bf16[256,2304]{1,0:T(8,128)(2,1)S(1)}, bf16[256,2304]{1,0:T(8,128)(2,1)S(1)}, u32[]{:S(2)}, u32[]{:S(2)}) collective-permute-start(bf16[256,2304]{1,0:T(8,128)(2,1)S(1)} %pad_maximum_fusion.20), channel_id=1, source_target_pairs={{0,8},{8,12},{12,4},{4,0},{16,24},{24,28},{28,20},{20,16},{1,9},{9... | collective-permute-start | bytes 3538952 | tf_op jit(solution)/shard_map/ppermute | solution.py:102
  851.2 33.9 %collective-permute-start.60 = (bf16[256,2304]{1,0:T(8,128)(2,1)S(1)}, bf16[256,2304]{1,0:T(8,128)(2,1)S(1)}, u32[]{:S(2)}, u32[]{:S(2)}) collective-permute-start(bf16[256,2304]{1,0:T(8,128)(2,1)S(1)} %pad_maximum_fusion.23), channel_id=1, source_target_pairs={{8,0},{12,8},{4,12},{0,4},{24,16},{28,24},{20,28},{16,20},{9,1},{1... | collective-permute-start | bytes 3538952 | tf_op jit(solution)/shard_map/ppermute | solution.py:102
  852.2 32.9 %collective-permute-start.59 = (bf16[256,2304]{1,0:T(8,128)(2,1)S(1)}, bf16[256,2304]{1,0:T(8,128)(2,1)S(1)}, u32[]{:S(2)}, u32[]{:S(2)}) collective-permute-start(bf16[256,2304]{1,0:T(8,128)(2,1)S(1)} %pad_maximum_fusion.22), channel_id=1, source_target_pairs={{0,8},{8,12},{12,4},{4,0},{16,24},{24,28},{28,20},{20,16},{1,9},{9... | collective-permute-start | bytes 3538952 | tf_op jit(solution)/shard_map/ppermute | solution.py:102
  920.4 31.4 %collective-permute-start.64 = (bf16[256,2304]{1,0:T(8,128)(2,1)S(1)}, bf16[256,2304]{1,0:T(8,128)(2,1)S(1)}, u32[]{:S(2)}, u32[]{:S(2)}) collective-permute-start(bf16[256,2304]{1,0:T(8,128)(2,1)S(1)} %pad_maximum_fusion.25), channel_id=1, source_target_pairs={{8,0},{12,8},{4,12},{0,4},{24,16},{28,24},{20,28},{16,20},{9,1},{1... | collective-permute-start | bytes 3538952 | tf_op jit(solution)/shard_map/ppermute | solution.py:102
  993.7 31.7 %collective-permute-start.66 = (bf16[2,288,1152]{2,1,0:T(8,128)(2,1)S(1)}, bf16[2,288,1152]{2,1,0:T(8,128)(2,1)}, u32[]{:S(2)}, u32[]{:S(2)}) collective-permute-start(bf16[2,288,1152]{2,1,0:T(8,128)(2,1)S(1)} %get-tuple-element.804), channel_id=1, source_target_pairs={{0,2},{1,3},{2,0},{3,1},{4,6},{5,7},{6,4},{7,5},{8,10},{9,11},{10,... | collective-permute-start | bytes 3981320 | tf_op jit(solution)/shard_map/ppermute | solution.py:157
  1025.4 35.0 %collective-permute-start.69 = (bf16[2304,1024]{1,0:T(8,128)(2,1)}, bf16[2304,1024]{1,0:T(8,128)(2,1)}, u32[]{:S(2)}, u32[]{:S(2)}) collective-permute-start(bf16[2304,1024]{1,0:T(8,128)(2,1)} %convolution_convert_fusion.1), channel_id=1, source_target_pairs={{0,1},{1,0},{2,3},{3,2},{4,5},{5,4},{6,7},{7,6},{8,9},{9,8},{10,11... | collective-permute-start | bytes 14155784 | tf_op jit(solution)/shard_map/ppermute | solution.py:157
  1025.5 41.5 %collective-permute-start.68 = (bf16[2,288,1152]{2,1,0:T(8,128)(2,1)}, bf16[2,288,1152]{2,1,0:T(8,128)(2,1)}, u32[]{:S(2)}, u32[]{:S(2)}) collective-permute-start(bf16[2,288,1152]{2,1,0:T(8,128)(2,1)} %get-tuple-element.820), channel_id=1, source_target_pairs={{0,2},{1,3},{2,0},{3,1},{4,6},{5,7},{6,4},{7,5},{8,10},{9,11},{10,... | collective-permute-start | bytes 3981320 | tf_op jit(solution)/shard_map/ppermute | solution.py:157
  1030.3 36.7 %all-to-all-start.8 = ((bf16[8,128,512]{2,1,0:T(8,128)(2,1)}), bf16[8,128,512]{2,1,0:T(8,128)(2,1)}, u32[]{:S(2)}, u32[]{:S(2)}) async-start(bf16[8,128,512]{2,1,0:T(8,128)(2,1)} %bitcast.260), calls=%async_computation.8 | async-start | bytes 2097152 | tf_op jit(solution)/shard_map/all_to_all | solution.py:161
  1070.3 42.2 %collective-permute-start.71 = (bf16[2304,256]{1,0:T(8,128)(2,1)}, bf16[2304,256]{1,0:T(8,128)(2,1)S(1)}, u32[]{:S(2)}, u32[]{:S(2)}) collective-permute-start(bf16[2304,256]{1,0:T(8,128)(2,1)} %get-tuple-element.987), channel_id=1, source_target_pairs={{0,2},{1,3},{2,0},{3,1},{4,6},{5,7},{6,4},{7,5},{8,10},{9,11},{10,... | collective-permute-start | bytes 3538952 | tf_op jit(solution)/shard_map/ppermute | solution.py:157
  1071.7 39.6 %collective-permute-start.70 = (bf16[2,256,512]{2,1,0:T(8,128)(2,1)}, bf16[2,256,512]{2,1,0:T(8,128)(2,1)}, u32[]{:S(2)}, u32[]{:S(2)}) collective-permute-start(bf16[2,256,512]{2,1,0:T(8,128)(2,1)} %get-tuple-element.834), channel_id=1, source_target_pairs={{0,4},{4,0},{8,12},{12,8},{16,20},{20,16},{24,28},{28,24},{1,5},{5... | collective-permute-start | bytes 1572872 | tf_op jit(solution)/shard_map/ppermute | solution.py:177
  1073.8 38.8 %all-to-all-start.9 = ((bf16[8,128,512]{2,1,0:T(8,128)(2,1)}), bf16[8,128,512]{2,1,0:T(8,128)(2,1)S(1)}, u32[]{:S(2)}, u32[]{:S(2)}) async-start(bf16[8,128,512]{2,1,0:T(8,128)(2,1)} %bitcast.261), calls=%async_computation.9 | async-start | bytes 2097152 | tf_op jit(solution)/shard_map/all_to_all | solution.py:161
  1121.8 33.1 %all-to-all-start.10 = ((bf16[4,256,512]{2,1,0:T(8,128)(2,1)}), bf16[4,256,512]{2,1,0:T(8,128)(2,1)S(1)}, u32[]{:S(2)}, u32[]{:S(2)}) async-start(bf16[4,256,512]{2,1,0:T(8,128)(2,1)} %pad_maximum_fusion.26), calls=%async_computation.10 | async-start | bytes 2097152 | tf_op jit(solution)/shard_map/all_to_all | solution.py:168
  1158.6 34.4 %collective-permute-start.75 = (bf16[2,288,1152]{2,1,0:T(8,128)(2,1)S(1)}, bf16[2,288,1152]{2,1,0:T(8,128)(2,1)}, u32[]{:S(2)}, u32[]{:S(2)}) collective-permute-start(bf16[2,288,1152]{2,1,0:T(8,128)(2,1)S(1)} %get-tuple-element.857), channel_id=1, source_target_pairs={{0,2},{1,3},{2,0},{3,1},{4,6},{5,7},{6,4},{7,5},{8,10},{9,11},{10,... | collective-permute-start | bytes 3981320 | tf_op jit(solution)/shard_map/ppermute | solution.py:157
  1159.1 33.8 %all-to-all-start.11 = ((bf16[4,256,512]{2,1,0:T(8,128)(2,1)}), bf16[4,256,512]{2,1,0:T(8,128)(2,1)S(1)}, u32[]{:S(2)}, u32[]{:S(2)}) async-start(bf16[4,256,512]{2,1,0:T(8,128)(2,1)} %add_convert_fusion.11), calls=%async_computation.11 | async-start | bytes 2097152 | tf_op jit(solution)/shard_map/all_to_all | solution.py:168
  1199.3 48.9 %collective-permute-start.78 = (bf16[2,576,2304]{2,1,0:T(8,128)(2,1)}, bf16[2,576,2304]{2,1,0:T(8,128)(2,1)}, u32[]{:S(2)}, u32[]{:S(2)}) collective-permute-start(bf16[2,576,2304]{2,1,0:T(8,128)(2,1)} %slice_bitcast_fusion.1), channel_id=1, source_target_pairs={{0,1},{1,0},{2,3},{3,2},{4,5},{5,4},{6,7},{7,6},{8,9},{9,8},{10,11... | collective-permute-start | bytes 15925256 | tf_op jit(solution)/shard_map/ppermute | solution.py:157
  1204.6 42.6 %collective-permute-start.79 = (bf16[2,288,1152]{2,1,0:T(8,128)(2,1)S(1)}, bf16[2,288,1152]{2,1,0:T(8,128)(2,1)S(1)}, u32[]{:S(2)}, u32[]{:S(2)}) collective-permute-start(bf16[2,288,1152]{2,1,0:T(8,128)(2,1)S(1)} %copy-done.51), channel_id=1, source_target_pairs={{0,2},{1,3},{2,0},{3,1},{4,6},{5,7},{6,4},{7,5},{8,10},{9,11},{10,... | collective-permute-start | bytes 3981320 | tf_op jit(solution)/shard_map/ppermute | solution.py:157
  1311.4 35.3 %collective-permute-start.85 = (bf16[288,2560]{1,0:T(8,128)(2,1)}, bf16[288,2560]{1,0:T(8,128)(2,1)}, u32[]{:S(2)}, u32[]{:S(2)}) collective-permute-start(bf16[288,2560]{1,0:T(8,128)(2,1)} %pad_maximum_fusion.13), channel_id=1, source_target_pairs={{8,0},{16,8},{24,16},{28,24},{20,28},{12,20},{4,12},{0,4},{9,1},{1... | collective-permute-start | bytes 4423688 | tf_op jit(solution)/shard_map/ppermute | solution.py:102
  1314.5 33.2 %collective-permute-start.84 = (bf16[288,2560]{1,0:T(8,128)(2,1)}, bf16[288,2560]{1,0:T(8,128)(2,1)}, u32[]{:S(2)}, u32[]{:S(2)}) collective-permute-start(bf16[288,2560]{1,0:T(8,128)(2,1)} %fusion.11), channel_id=1, source_target_pairs={{0,8},{8,16},{16,24},{24,28},{28,20},{20,12},{12,4},{4,0},{1,9},{9... | collective-permute-start | bytes 4423688 | tf_op jit(solution)/shard_map/ppermute | solution.py:102
  1349.9 35.1 %collective-permute-start.88 = (bf16[288,2560]{1,0:T(8,128)(2,1)S(1)}, bf16[288,2560]{1,0:T(8,128)(2,1)S(1)}, u32[]{:S(2)}, u32[]{:S(2)}) collective-permute-start(bf16[288,2560]{1,0:T(8,128)(2,1)S(1)} %add_convert_fusion.6), channel_id=1, source_target_pairs={{8,0},{16,8},{24,16},{28,24},{20,28},{12,20},{4,12},{0,4},{9,1},{1... | collective-permute-start | bytes 4423688 | tf_op jit(solution)/shard_map/ppermute | solution.py:102
  1353.1 31.8 %collective-permute-start.87 = (bf16[288,2560]{1,0:T(8,128)(2,1)S(1)}, bf16[288,2560]{1,0:T(8,128)(2,1)S(1)}, u32[]{:S(2)}, u32[]{:S(2)}) collective-permute-start(bf16[288,2560]{1,0:T(8,128)(2,1)S(1)} %add_convert_fusion.7), channel_id=1, source_target_pairs={{0,8},{8,16},{16,24},{24,28},{28,20},{20,12},{12,4},{4,0},{1,9},{9... | collective-permute-start | bytes 4423688 | tf_op jit(solution)/shard_map/ppermute | solution.py:102
  1385.4 32.1 %collective-permute-start.91 = (bf16[288,2560]{1,0:T(8,128)(2,1)S(1)}, bf16[288,2560]{1,0:T(8,128)(2,1)S(1)}, u32[]{:S(2)}, u32[]{:S(2)}) collective-permute-start(bf16[288,2560]{1,0:T(8,128)(2,1)S(1)} %add_convert_fusion.4), channel_id=1, source_target_pairs={{8,0},{16,8},{24,16},{28,24},{20,28},{12,20},{4,12},{0,4},{9,1},{1... | collective-permute-start | bytes 4423688 | tf_op jit(solution)/shard_map/ppermute | solution.py:102
  1387.3 30.8 %collective-permute-start.90 = (bf16[288,2560]{1,0:T(8,128)(2,1)S(1)}, bf16[288,2560]{1,0:T(8,128)(2,1)S(1)}, u32[]{:S(2)}, u32[]{:S(2)}) collective-permute-start(bf16[288,2560]{1,0:T(8,128)(2,1)S(1)} %add_convert_fusion.5), channel_id=1, source_target_pairs={{0,8},{8,16},{16,24},{24,28},{28,20},{20,12},{12,4},{4,0},{1,9},{9... | collective-permute-start | bytes 4423688 | tf_op jit(solution)/shard_map/ppermute | solution.py:102
  1418.7 30.8 %collective-permute-start.95 = (bf16[288,1152]{1,0:T(8,128)(2,1)S(1)}, bf16[288,1152]{1,0:T(8,128)(2,1)}, u32[]{:S(2)}, u32[]{:S(2)}) collective-permute-start(bf16[288,1152]{1,0:T(8,128)(2,1)S(1)} %get-tuple-element.912), channel_id=1, source_target_pairs={{0,16},{4,20},{8,24},{12,28},{16,0},{20,4},{24,8},{28,12},{1,17},{... | collective-permute-start | bytes 1990664 | tf_op jit(solution)/shard_map/ppermute | solution.py:157
  1488.3 39.7 %collective-permute-start.101 = (bf16[288,3072]{1,0:T(8,128)(2,1)}, bf16[288,3072]{1,0:T(8,128)(2,1)}, u32[]{:S(2)}, u32[]{:S(2)}) collective-permute-start(bf16[288,3072]{1,0:T(8,128)(2,1)} %pad_maximum_fusion.7), channel_id=1, source_target_pairs={{0,1},{1,0},{2,3},{3,2},{4,5},{5,4},{6,7},{7,6},{8,9},{9,8},{10,11... | collective-permute-start | bytes 5308424 | tf_op jit(solution)/shard_map/ppermute | solution.py:157
  1496.5 31.6 %collective-permute-start.100 = (bf16[288,1152]{1,0:T(8,128)(2,1)S(1)}, bf16[288,1152]{1,0:T(8,128)(2,1)S(1)}, u32[]{:S(2)}, u32[]{:S(2)}) collective-permute-start(bf16[288,1152]{1,0:T(8,128)(2,1)S(1)} %copy-done.84), channel_id=1, source_target_pairs={{0,16},{4,20},{8,24},{12,28},{16,0},{20,4},{24,8},{28,12},{1,17},{... | collective-permute-start | bytes 1990664 | tf_op jit(solution)/shard_map/ppermute | solution.py:157
  1533.7 32.0 %collective-permute-start.104 = (bf16[288,1152]{1,0:T(8,128)(2,1)}, bf16[288,1152]{1,0:T(8,128)(2,1)}, u32[]{:S(2)}, u32[]{:S(2)}) collective-permute-start(bf16[288,1152]{1,0:T(8,128)(2,1)} %get-tuple-element.942), channel_id=1, source_target_pairs={{0,16},{4,20},{8,24},{12,28},{16,0},{20,4},{24,8},{28,12},{1,17},{... | collective-permute-start | bytes 1990664 | tf_op jit(solution)/shard_map/ppermute | solution.py:157
  (201 other events, 2963.7 us)

commit v12 on v11

--- a/solution.py
+++ b/solution.py
@@ -271,6 +271,11 @@
     )(places, info, *inputs, scale)
 
 
+def piece_at(j, steps, block):
+    half = steps // 2
+    return j + j // half * half + block * half
+
+
 def own_slice_kernel(pieces, info, code_ref, row_ref, col_ref, *out_refs):
     count = len(out_refs) // 3
     for m in range(3):
@@ -289,10 +294,11 @@
         grid=(steps,),
         in_specs=[
             pl.BlockSpec((three, piece, cols), lambda j, p, i: (0, p[j], 0)),
-            pl.BlockSpec((2, piece, 1), lambda j, p, i: (0, j, 0)),
+            pl.BlockSpec((2, piece, 1), lambda j, p, i: (0, piece_at(j, steps, 0), 0)),
             pl.BlockSpec((1, cols), lambda j, p, i: (0, 0)),
         ],
-        out_specs=[pl.BlockSpec((piece, cols), lambda j, p, i: (j, 0))] * (three * count),
+        out_specs=[pl.BlockSpec((piece, cols), lambda j, p, i: (piece_at(j, steps, 0), 0))]
+        * (three * count),
     )
     return pl.pallas_call(
         own_slice_kernel,
@@ -327,14 +333,14 @@
     if by_column:
         scale_spec = pl.BlockSpec((1, cols), lambda j, i: (0, 0))
     else:
-        scale_spec = pl.BlockSpec((piece, 1), lambda j, i: (steps + j, 0))
+        scale_spec = pl.BlockSpec((piece, 1), lambda j, i: (piece_at(j, steps, 1), 0))
     grid_spec = pltpu.PrefetchScalarGridSpec(
         num_scalar_prefetch=1,
         grid=(steps,),
         in_specs=[pl.BlockSpec((piece, cols), lambda j, i: (0, 0))] * steps
         + [scale_spec]
         + [pl.BlockSpec(memory_space=pl.ANY)] * count,
-        out_specs=[pl.BlockSpec((piece, cols), lambda j, i: (steps + j, 0))] * count,
+        out_specs=[pl.BlockSpec((piece, cols), lambda j, i: (piece_at(j, steps, 1), 0))] * count,
     )
     return pl.pallas_call(
         functools.partial(partner_slice_kernel, steps=steps, count=count),
@@ -515,25 +521,45 @@
     )(grad_gate, grad_up, gate_weights, up_weights, *held)
 
 
-def weight_kernel(*refs, count):
-    out_ref = refs[-1]
+def weight_kernel(*refs, count, tiles):
+    keep_ref, send_ref = refs[-2:]
     total = dot(refs[0][...], refs[count][...], TN)
     for s in range(1, count):
         total = total + dot(refs[s][...], refs[count + s][...], TN)
-    out_ref[...] = total.astype(bf16)
+    total = total.astype(bf16)
+    if tiles == 1:
+        half = keep_ref.shape[0]
+        keep_ref[...] = total[:half]
+        send_ref[...] = total[half:]
+        return
+    step = pl.program_id(0)
+
+    @pl.when(step < tiles // 2)
+    def _():
+        keep_ref[...] = total
+
+    @pl.when(step >= tiles // 2)
+    def _():
+        send_ref[...] = total
 
 
 def weight_back(lefts, rights):
     count = len(lefts)
     rows, hidden = lefts[0].shape
     depth = rights[0].shape[1]
-    tile = tile_of(hidden)
+    tile = 384 if hidden % 768 == 0 else hidden
+    tiles = hidden // tile
+    half = max(tiles // 2, 1)
+    out = (tile if tiles > 1 else hidden // 2, depth)
     return kernel_call(
-        functools.partial(weight_kernel, count=count),
-        hidden // tile,
+        functools.partial(weight_kernel, count=count, tiles=tiles),
+        tiles,
         [column_spec(rows, tile)] * count + [whole_spec((rows, depth))] * count,
-        row_spec(tile, depth),
-        jax.ShapeDtypeStruct((hidden, depth), bf16),
+        [
+            pl.BlockSpec(out, lambda i: (jnp.minimum(i, half - 1), 0)),
+            pl.BlockSpec(out, lambda i: (jnp.maximum(i - half, 0), 0)),
+        ],
+        [jax.ShapeDtypeStruct((hidden // 2, depth), bf16)] * 2,
         2 * count * rows * depth * hidden,
         2 * count * rows * (hidden + depth) + 2 * hidden * depth,
         "weight_back",
@@ -1048,8 +1074,9 @@
             lax.dynamic_slice_in_dim(
                 gate_scale, block * hidden + pieces[j] * piece_rows, piece_rows, 1
             )
+            for group in (range(seq_size // 2), range(seq_size // 2, seq_size))
             for block in (wide_index, partner)
-            for j in range(seq_size)
+            for j in group
         ],
         axis=1,
     )[:, :, None]
@@ -1376,7 +1403,7 @@
 
     def weight_sum(lefts, rights):
         lefts = [clock.hold(v) for v in lefts]
-        return weight_back(lefts, rights).reshape(2, hidden, model_dim)
+        return [v.reshape(2, hidden // 2, model_dim) for v in weight_back(lefts, rights)]
 
     def part_sum(grad, bit):
         split = grad.reshape(2, 2, grad.shape[1] // 2, model_dim)
@@ -1427,9 +1454,9 @@
         grad_parts[1],
         a,
         b,
-        lambda step: () if step else (weight_sum(hidden_rows, grad_group),),
-    )
-    down_grad = work[0][0]
+        lambda step: () if step else tuple(weight_sum(hidden_rows, grad_group)),
+    )
+    down_keep, down_send = work[0]
     grad_normed_mlp.append(total)
 
     def attend_back(s):
@@ -1472,7 +1499,7 @@
         return value.reshape(wide * class_rows, head_cols)
 
     back = all_to_all(clock.hold(grad_send[0]))
-    down_grad = part_sum(down_grad, 1)
+    down_grad = low_sum(down_keep, swap(down_send, "seq", 1))
     back, down_grad, *work = clock.sync(back, down_grad, *back_branch(1))
     keep_branch(work)
     grad_heads.append(heads_of(back))
@@ -1528,15 +1555,15 @@
                     out_pieces[t] = low_sum(
                         out_pieces[t], swap(out_pieces.pop(t | (bit // 2)), "seq", bit)
                     )
-    up_grad = weight_sum(grad_up, gathered)
-    query, pair_b, down_grad, up_grad, *out_moved = clock.sync(
-        query, pair_b, down_grad, up_grad, *out_moved
+    up_keep, up_send = weight_sum(grad_up, gathered)
+    query, pair_b, down_grad, up_keep, up_send, *out_moved = clock.sync(
+        query, pair_b, down_grad, up_keep, up_send, *out_moved
     )
     query_back.append(query)
 
     pair = heads_all_to_all(clock.hold(jnp.concatenate([pair_a, pair_b], axis=0)))
     pair_sum = class_sum([clock.hold(v) for v in dkv])
-    up_grad = part_sum(up_grad, 1)
+    up_grad = low_sum(up_keep, swap(up_send, "seq", 1))
     if members == 2:
         out_moved.append(swap(clock.hold(out_parts[1]), "seq", seq_bits[1]))
     pair, pair_sum, up_grad, *out_moved = clock.sync(pair, pair_sum, up_grad, *out_moved)
@@ -1547,8 +1574,8 @@
     up_keep, up_parts = far_parts(up_grad)
     up_moved = [far_move(up_parts[0])]
     pair = heads_all_to_all(clock.hold(pair_sum))
-    gate_grad = weight_sum(grad_gate, gathered)
-    pair, up_moved[0], gate_grad = clock.sync(pair, up_moved[0], gate_grad)
+    gate_keep, gate_send = weight_sum(grad_gate, gathered)
+    pair, up_moved[0], gate_keep, gate_send = clock.sync(pair, up_moved[0], gate_keep, gate_send)
     up_moved.append(far_move(up_parts[1]))
     pair_back.append(pair)
 
@@ -1559,13 +1586,8 @@
     def exchange_grad(part):
         return swap(clock.hold(part), "wide", half_wide)
 
-    def half_sum(grad):
-        split = grad.reshape(2, 2, grad.shape[1] // 2, model_dim)
-        return split[:, 0], split[:, 1]
-
     down_own = column_parts(down_grad[0], 3)
     down_send = column_parts(down_grad[1], 3)
-    gate_keep, gate_send = half_sum(gate_grad)
     gate_moved = swap(gate_send, "seq", 1)
     moved, grad_proj = clock.sync(
         exchange_grad(down_send[0]),
@@ -1597,8 +1619,8 @@
         first = index_at(o) * attn_rows
         return jnp.concatenate(
             [
-                lax.dynamic_slice_in_dim(proj_part, first, attn_rows, 0),
-                lax.dynamic_slice_in_dim(out_piece, first, attn_rows, 0),
+                lax.dynamic_slice_in_dim(clock.hold(proj_part), first, attn_rows, 0),
+                lax.dynamic_slice_in_dim(clock.hold(out_piece), first, attn_rows, 0),
             ],
             axis=1,
         )
@@ -1671,7 +1693,8 @@
     last_tokens, gain = back_tokens(1, grad_last)
     gains = jnp.concatenate([gain_first + gain, gain_second, gain_third, gain_fourth], axis=0)
     wide_bits = [1 << i for i in range(wide.bit_length() - 1)]
-    gains, *gate_send = clock.sync(add_swapped(gains, "wide", wide_bits[1:]), *gate_send)
+    gains = add_swapped(add_swapped(gains, "wide", wide_bits), "seq", seq_bits)
+    gains, *gate_send = clock.sync(gains, *gate_send)
     moved = exchange_grad(gate_send[0])
     up_grad = spread_grad([clock.hold(v) for v in up_grad], far_bits)
     other = swap(clock.hold(low), "seq", 1)
@@ -1691,9 +1714,7 @@
     up_grad = spread_grad([clock.hold(v) for v in up_grad], seq_bits[:1])
     mlp_grad = unpack(up_grad, pieces, 1, [mlp_grad])
     gate_grad = spread_grad([clock.hold(v) for v in gate_grad], seq_bits[:1])
-    gains = add_swapped(clock.hold(gains), "wide", wide_bits[:1])
-    gains = add_swapped(add_swapped(gains, "seq", seq_bits[:1]), "seq", seq_bits[1:])
-    mlp_grad, gains, *gate_grad = clock.sync(mlp_grad, gains, *gate_grad, *last)
+    mlp_grad, *gate_grad = clock.sync(mlp_grad, *gate_grad, *last)
     gate_grad[1:] = spread_grad(gate_grad[1:], seq_bits[:1])
     mlp_grad = unpack(gate_grad, pieces, 0, [mlp_grad])
     grad_tokens = [first_tokens, last_tokens]

time: 1630 us -> 1620 us (level)
  waiting for transfers between devices: 536 us -> 553 us
    squeeze x3 -> x0, local copies, waits for them, and re-layouts: 17.5 us -> none  [the longest x2 12.1 us: part_sum(): return low_sum(split[:, 0], swap(split[:, 1], 'seq', bit))]
    unnamed x274 -> x252, local copies, waits for them, and re-layouts: 53.4 us -> 52.2 us
  transfers between devices with their start and end apart: 129 -> 129, of which waited for: 61 -> 63; matrix products, arithmetic and copies ran while one was open for 16% -> 15% of each run, Pallas kernels for 32% -> 33%
where the time goes in v12:
time: 1620 us; the launch traced here: 1610 us
  Pallas kernels  562 us (35%)
  waiting for transfers between devices  553 us (34%)
  starting transfers between devices  155 us (10%)
  other arithmetic  122 us (8%)
  local copies, waits for them, and re-layouts  119 us (7%)
  matrix products  99.9 us (6%)
    ppermute x63, waiting for transfers between devices, swap(): return lax.ppermute(value, axis, [(i, i ^ bit) for i in range(size)])  300 us
    ppermute x48, waiting for transfers between devices, hop(): return (lax.ppermute(a, 'wide', up), lax.ppermute(b, 'wide', down))  159 us
    dot_general x8, matrix products, dot(): return lax.dot_general(a, b, (dims, ((), ())), preferred_element_type=f32)  99.9 us
    pallas_call x3, Pallas kernels, weight_back(): kernel_call(functools.partial(weight_kernel, count=count, tiles=tiles), t...  91.4 us
    ppermute x6, waiting for transfers between devices, class_ring(): return lax.ppermute(value, 'wide', perm)  72.1 us
    pallas_call x4, Pallas kernels, input_back(): kernel_call(input_back_kernel, tiles, [whole_spec(grad_gate.shape)] * 2 +...  69.2 us
    pallas_call x3, Pallas kernels, open_forward(): kernel_call(open_kernel, tiles, [whole_spec(x.shape)] + [row_spec(tile, d...  62.6 us
    convert_element_type x27, other arithmetic, low_sum(): return sum((t.astype(f32) for t in terms)).astype(bf16)  60.5 us
  transfers between devices with their start and end apart: 129, of which 63 were waited for; matrix products, arithmetic and copies ran while one was open for 15% of the time, Pallas kernels for 33%

profile of v12, /device:TPU:0, one launch (start us, length us, event | category | flops | bytes accessed | tf_op | source)
XLA Modules:
  0.0 1613.9 jit_solution(13331536722262553466)
XLA Ops:
  11.2 25.0 %own_slices.1 = (bf16[2304,2304]{1,0:T(8,128)(2,1)}, bf16[2304,2304]{1,0:T(8,128)(2,1)}, bf16[2304,2304]{1,0:T(8,128)(2,1)}, bf16[2304,2304]{1,0:T(8,128)(2,1)},...) custom-call(s32[4]{0:T(128)} %pad_add_fusion.pieces, s32[4]{0:T(128)} %pad_add_fusion.1.info, ...), custom_call_target="tpu_custom_call" | custom-call | flops 159252480 | bytes 63700992 | tf_op jit(solution)/shard_map/own_slices/pallas_call | solution.py:303
  49.6 27.7 %collective-permute-done.3.refs_0_ = bf16[288,2560]{1,0:T(8,128)(2,1)} collective-permute-done((bf16[288,2560]{1,0:T(8,128)(2,1)S(1)}, bf16[288,2560]{1,0:T(8,128)(2,1)}, u32[]{:S(2)}, u32[]{:S(2)}) %collective-permute-start.3) | collective-permute-done | bytes 1474592 | tf_op jit(solution)/shard_map/ppermute | solution.py:102
  94.2 20.1 %collective-permute-done.7.refs_0_ = bf16[288,2560]{1,0:T(8,128)(2,1)S(1)} collective-permute-done((bf16[288,2560]{1,0:T(8,128)(2,1)}, bf16[288,2560]{1,0:T(8,128)(2,1)S(1)}, u32[]{:S(2)}, u32[]{:S(2)}) %collective-permute-start.7) | collective-permute-done | bytes 1474592 | tf_op jit(solution)/shard_map/ppermute | solution.py:102
  177.7 24.4 %collective-permute-done.15.refs_0_ = bf16[288,2304]{1,0:T(8,128)(2,1)} collective-permute-done((bf16[288,2304]{1,0:T(8,128)(2,1)}, bf16[288,2304]{1,0:T(8,128)(2,1)}, u32[]{:S(2)}, u32[]{:S(2)}) %collective-permute-start.15) | collective-permute-done | bytes 1327136 | tf_op jit(solution)/shard_map/ppermute | solution.py:157
  240.0 21.8 %collective-permute-done.17.refs_1_ = bf16[4,256,512]{2,1,0:T(8,128)(2,1)} collective-permute-done((bf16[4,256,512]{2,1,0:T(8,128)(2,1)S(1)}, bf16[4,256,512]{2,1,0:T(8,128)(2,1)}, u32[]{:S(2)}, u32[]{:S(2)}) %collective-permute-start.17) | collective-permute-done | bytes 1048608 | tf_op jit(solution)/shard_map/ppermute | solution.py:177
  270.1 20.5 %collective-permute-done.18 = bf16[2,256,512]{2,1,0:T(8,128)(2,1)S(1)} collective-permute-done((bf16[2,256,512]{2,1,0:T(8,128)(2,1)S(1)}, bf16[2,256,512]{2,1,0:T(8,128)(2,1)S(1)}, u32[]{:S(2)}, u32[]{:S(2)}) %collective-permute-start.18) | collective-permute-done | bytes 524320 | tf_op jit(solution)/shard_map/ppermute | solution.py:177
  309.6 12.0 collective-permute-done.20
  329.9 20.6 %out_slices.1 = (bf16[2304,2048]{1,0:T(8,128)(2,1)}, bf16[2304,2048]{1,0:T(8,128)(2,1)}) custom-call(s32[8]{0:T(128)} %stack.163.places, s32[4]{0:T(128)} %pad_add_fusion.1.info, bf16[8,288,512]{2,1,0:T(8,128)(2,1)} %copy-done.37, bf16[8,288,512]{2,1,0:T(8,128)(2,1)} %collective-permute-done.19.refs_1_, ...), custom_call_target="tpu_custom_call" | custom-call | flops 94371840 | bytes 28311552 | tf_op jit(solution)/shard_map/out_slices/pallas_call | solution.py:260
  370.7 13.1 join_rows.2
  405.2 13.2 join_rows.3
  418.4 33.9 %collective-permute-done.25.refs_0_ = bf16[288,2304]{1,0:T(8,128)(2,1)} collective-permute-done((bf16[288,2304]{1,0:T(8,128)(2,1)S(1)}, bf16[288,2304]{1,0:T(8,128)(2,1)}, u32[]{:S(2)}, u32[]{:S(2)}) %collective-permute-start.25) | collective-permute-done | bytes 1327136 | tf_op jit(solution)/shard_map/ppermute | solution.py:157
  452.7 30.8 %collective-permute-done.27.refs_1_ = bf16[288,2304]{1,0:T(8,128)(2,1)S(1)} collective-permute-done((bf16[288,2304]{1,0:T(8,128)(2,1)}, bf16[288,2304]{1,0:T(8,128)(2,1)S(1)}, u32[]{:S(2)}, u32[]{:S(2)}) %collective-permute-start.27) | collective-permute-done | bytes 1327136 | tf_op jit(solution)/shard_map/ppermute | solution.py:157
  483.6 28.5 %collective-permute-done.26.refs_0_ = bf16[288,2304]{1,0:T(8,128)(2,1)} collective-permute-done((bf16[288,2304]{1,0:T(8,128)(2,1)S(1)}, bf16[288,2304]{1,0:T(8,128)(2,1)}, u32[]{:S(2)}, u32[]{:S(2)}) %collective-permute-start.26) | collective-permute-done | bytes 1327136 | tf_op jit(solution)/shard_map/ppermute | solution.py:157
  516.3 26.3 %collective-permute-done.28 = bf16[256,2304]{1,0:T(8,128)(2,1)S(1)} collective-permute-done((bf16[256,2304]{1,0:T(8,128)(2,1)}, bf16[256,2304]{1,0:T(8,128)(2,1)S(1)}, u32[]{:S(2)}, u32[]{:S(2)}) %collective-permute-start.28) | collective-permute-done | bytes 1179680 | tf_op jit(solution)/shard_map/ppermute | solution.py:102
  570.4 29.1 %open_forward.3 = (f32[1024,2304]{1,0:T(8,128)}, f32[1024,2304]{1,0:T(8,128)}, bf16[1024,2304]{1,0:T(8,128)(2,1)}) custom-call(bf16[1024,2304]{1,0:T(8,128)(2,1)} %constant_dynamic-update-slice_fusion.4.refs_0_.refs_2_, bf16[2304,2304]{1,0:T(8,128)(2,1)} %get-tuple-element.672.refs_1_.refs_2_, bf16[2304,2304]{1,0:T(8,128)(2,1)} %get-tuple-element.673.refs_2_.refs_3_), custom_call_target="tpu_custom_call" | custom-call | flops 21743271936 | bytes 49545216 | tf_op jit(solution)/shard_map/open_forward/pallas_call | solution.py:454
  616.4 14.9 convolution_convert_fusion.3.part_ref
  636.0 18.1 %open_forward.4 = (f32[1024,2304]{1,0:T(8,128)}, f32[1024,2304]{1,0:T(8,128)}, bf16[1024,2304]{1,0:T(8,128)(2,1)}) custom-call(bf16[1024,2304]{1,0:T(8,128)(2,1)} %constant_dynamic-update-slice_fusion.9.refs_0_.refs_3_, bf16[2304,2304]{1,0:T(8,128)(2,1)} %get-tuple-element.702.refs_1_.refs_2_, bf16[2304,2304]{1,0:T(8,128)(2,1)} %get-tuple-element.703.refs_2_.refs_3_), custom_call_target="tpu_custom_call" | custom-call | flops 12079595520 | bytes 29622272 | tf_op jit(solution)/shard_map/open_forward/pallas_call | solution.py:454
  659.0 15.4 open_forward.5
  689.7 13.5 convolution_convert_fusion.2.part_ref
  732.2 14.9 open_back.4
  751.0 12.8 open_back.5
  763.7 18.4 %input_back.4.refs_4_ = bf16[1024,2304]{1,0:T(8,128)(2,1)} custom-call(bf16[1024,2304]{1,0:T(8,128)(2,1)} %get-tuple-element.881.refs_0_, bf16[1024,2304]{1,0:T(8,128)(2,1)} %get-tuple-element.857.refs_1_.refs_0_, bf16[2304,2304]{1,0:T(8,128)(2,1)} %get-tuple-element.672.refs_1_.refs_2_, bf16[2304,2304]{1,0:T(8,128)(2,1)} %get-tuple-element.673.refs_2_.refs_3_), custom_call_target="tpu_custom_call" | custom-call | flops 12079595520 | bytes 23855104 | tf_op jit(solution)/shard_map/input_back/pallas_call | solution.py:511
  794.4 15.8 input_back.5.part_ref
  817.3 13.6 collective-permute-done.55
  836.1 15.0 open_back.6
  854.0 12.7 open_back.7
  866.8 18.4 %input_back.6.refs_4_ = bf16[1024,2304]{1,0:T(8,128)(2,1)} custom-call(bf16[1024,2304]{1,0:T(8,128)(2,1)} %get-tuple-element.882.refs_0_.refs_1_, bf16[1024,2304]{1,0:T(8,128)(2,1)} %get-tuple-element.858.refs_1_, bf16[2304,2304]{1,0:T(8,128)(2,1)} %get-tuple-element.702.refs_1_.refs_2_, bf16[2304,2304]{1,0:T(8,128)(2,1)} %get-tuple-element.703.refs_2_.refs_3_), custom_call_target="tpu_custom_call" | custom-call | flops 12079595520 | bytes 23855104 | tf_op jit(solution)/shard_map/input_back/pallas_call | solution.py:511
  885.2 16.6 %input_back.7.part_ref = bf16[1024,2304]{1,0:T(8,128)(2,1)} custom-call(bf16[1024,2304]{1,0:T(8,128)(2,1)} %get-tuple-element.882.refs_0_.refs_1_, bf16[1024,2304]{1,0:T(8,128)(2,1)} %get-tuple-element.858.refs_1_, bf16[2304,2304]{1,0:T(8,128)(2,1)} %get-tuple-element.702.refs_1_.refs_2_, ...), custom_call_target="tpu_custom_call", output_to_operand_aliasing={{}: (4, {})} | custom-call | flops 9663676416 | bytes 20971520 | tf_op jit(solution)/shard_map/input_back/pallas_call | solution.py:511
  905.3 13.3 branch_back.2
  922.9 30.3 %weight_back.3 = (bf16[1152,2304]{1,0:T(8,128)(2,1)}, bf16[1152,2304]{1,0:T(8,128)(2,1)}) custom-call(bf16[1024,2304]{1,0:T(8,128)(2,1)} %get-tuple-element.803.refs_0_, bf16[1024,2304]{1,0:T(8,128)(2,1)} %get-tuple-element.804.refs_1_, bf16[1024,2304]{1,0:T(8,128)(2,1)} %copy-done.3, bf16[1024,2304]{1,0:T(8,128)(2,1)} %constant_dynamic-update-slice_fusion.19.refs_0_.refs_3_), custom_call_target="tpu_custom_call" | custom-call | flops 21743271936 | bytes 29491200 | tf_op jit(solution)/shard_map/weight_back/pallas_call | solution.py:554
  962.4 13.9 branch_back.3
  1003.3 17.5 %attn_backward.2 = (bf16[1024,512]{1,0:T(8,128)(2,1)}, bf16[4,256,512]{2,1,0:T(8,128)(2,1)}, bf16[4,256,512]{2,1,0:T(8,128)(2,1)}) custom-call(s32[1]{0:T(128)} %bitcast.41.info, bf16[1024,512]{1,0:T(8,128)(2,1)} %bitcast.228, bf16[1024,512]{1,0:T(8,128)(2,1)} %bitcast.233, f32[1024,512]{1,0:T(8,128)} %get-tuple-element.830.exact_ref, ...), custom_call_target="tpu_custom_call" | custom-call | flops 10737418240 | bytes 9437184 | tf_op jit(solution)/shard_map/attn_backward/pallas_call | solution.py:994
  1030.4 17.5 %attn_backward.3 = (bf16[1024,512]{1,0:T(8,128)(2,1)}, bf16[4,256,512]{2,1,0:T(8,128)(2,1)}, bf16[4,256,512]{2,1,0:T(8,128)(2,1)}) custom-call(s32[1]{0:T(128)} %bitcast.41.info, bf16[1024,512]{1,0:T(8,128)(2,1)} %bitcast.226, bf16[1024,512]{1,0:T(8,128)(2,1)} %bitcast.67.grad_ref, f32[1024,512]{1,0:T(8,128)} %get-tuple-element.845.exact_ref, ...), custom_call_target="tpu_custom_call" | custom-call | flops 10737418240 | bytes 9437184 | tf_op jit(solution)/shard_map/attn_backward/pallas_call | solution.py:994
  1073.6 30.5 %weight_back.4 = (bf16[1152,2304]{1,0:T(8,128)(2,1)}, bf16[1152,2304]{1,0:T(8,128)(2,1)}) custom-call(bf16[1024,2304]{1,0:T(8,128)(2,1)} %get-tuple-element.857.refs_1_.refs_0_, bf16[1024,2304]{1,0:T(8,128)(2,1)} %get-tuple-element.858.refs_1_, bf16[1024,2304]{1,0:T(8,128)(2,1)} %constant_dynamic-update-slice_fusion.4.refs_0_.refs_2_, ...), custom_call_target="tpu_custom_call" | custom-call | flops 21743271936 | bytes 29491200 | tf_op jit(solution)/shard_map/weight_back/pallas_call | solution.py:554
  1116.6 17.8 %collective-permute-done.72 = bf16[4,256,512]{2,1,0:T(8,128)(2,1)} collective-permute-done((bf16[4,256,512]{2,1,0:T(8,128)(2,1)}, bf16[4,256,512]{2,1,0:T(8,128)(2,1)}, u32[]{:S(2)}, u32[]{:S(2)}) %collective-permute-start.72) | collective-permute-done | bytes 1048608 | tf_op jit(solution)/shard_map/ppermute | solution.py:177
  1154.7 30.6 %weight_back.5 = (bf16[1152,2304]{1,0:T(8,128)(2,1)}, bf16[1152,2304]{1,0:T(8,128)(2,1)}) custom-call(bf16[1024,2304]{1,0:T(8,128)(2,1)} %get-tuple-element.881.refs_0_, bf16[1024,2304]{1,0:T(8,128)(2,1)} %get-tuple-element.882.refs_0_.refs_1_, bf16[1024,2304]{1,0:T(8,128)(2,1)} %constant_dynamic-update-slice_fusion.4.refs_0_.refs_2_, ...), custom_call_target="tpu_custom_call" | custom-call | flops 21743271936 | bytes 29491200 | tf_op jit(solution)/shard_map/weight_back/pallas_call | solution.py:554
  1192.1 13.8 turn_back.1
  1219.8 13.3 collective-permute-done.77
  1248.5 11.8 collective-permute-done.80
  1275.2 16.3 %collective-permute-done.82 = bf16[144,2560]{1,0:T(8,128)(2,1)S(1)} collective-permute-done((bf16[144,2560]{1,0:T(8,128)(2,1)S(1)}, bf16[144,2560]{1,0:T(8,128)(2,1)S(1)}, u32[]{:S(2)}, u32[]{:S(2)}) %collective-permute-start.82) | collective-permute-done | bytes 737312 | tf_op jit(solution)/shard_map/ppermute | solution.py:102
  1305.8 25.2 %collective-permute-done.86 = bf16[2,288,1152]{2,1,0:T(8,128)(2,1)} collective-permute-done((bf16[2,288,1152]{2,1,0:T(8,128)(2,1)}, bf16[2,288,1152]{2,1,0:T(8,128)(2,1)}, u32[]{:S(2)}, u32[]{:S(2)}) %collective-permute-start.86) | collective-permute-done | bytes 1327136 | tf_op jit(solution)/shard_map/ppermute | solution.py:157
  1346.2 24.7 %collective-permute-done.89 = bf16[2,288,1152]{2,1,0:T(8,128)(2,1)S(1)} collective-permute-done((bf16[2,288,1152]{2,1,0:T(8,128)(2,1)S(1)}, bf16[2,288,1152]{2,1,0:T(8,128)(2,1)S(1)}, u32[]{:S(2)}, u32[]{:S(2)}) %collective-permute-start.89) | collective-permute-done | bytes 1327136 | tf_op jit(solution)/shard_map/ppermute | solution.py:157
  1409.1 20.8 %fusion.47 = f32[256,2304]{1,0:T(8,128)} fusion(bf16[256,4096]{1,0:T(8,128)(2,1)} %get-tuple-element.948, bf16[2304,4096]{1,0:T(8,128)(2,1)} %get-tuple-element.546.wq_ref.wk_ref.wv_ref), kind=kOutput, calls=%fused_computation.259 | convolution fusion | flops 4831838208 | bytes 23330816 | tf_op jit(solution)/shard_map/dot_general | solution.py:26
  1435.5 20.8 %fusion.48 = f32[256,2304]{1,0:T(8,128)} fusion(bf16[256,4096]{1,0:T(8,128)(2,1)} %get-tuple-element.956, bf16[2304,4096]{1,0:T(8,128)(2,1)} %get-tuple-element.549.wq_ref.wk_ref.wv_ref), kind=kOutput, calls=%fused_computation.260 | convolution fusion | flops 4831838208 | bytes 23330816 | tf_op jit(solution)/shard_map/dot_general | solution.py:26
  1495.4 11.6 collective-permute-done.106
  1508.4 12.3 collective-permute-done.105
  1535.3 11.5 collective-permute-done.111
  1566.7 16.0 collective-permute-done.115
  (695 shorter events, 694.4 us)
Async XLA Ops:
  3.8 38.4 %collective-permute-start = (bf16[288,2560]{1,0:T(8,128)(2,1)S(1)}, bf16[288,2560]{1,0:T(8,128)(2,1)S(1)}, u32[]{:S(2)}, u32[]{:S(2)}) collective-permute-start(bf16[288,2560]{1,0:T(8,128)(2,1)S(1)} %pad_maximum_fusion.11.refs_0_), channel_id=1, source_target_pairs={{0,8},{8,16},{16,24},{24,28},{28,20},{20,12},{12,4},{4,0},{1,9},{9... | collective-permute-start | bytes 4423688 | tf_op jit(solution)/shard_map/ppermute | solution.py:102
  6.9 35.3 %collective-permute-start.1 = (bf16[288,2560]{1,0:T(8,128)(2,1)S(1)}, bf16[288,2560]{1,0:T(8,128)(2,1)}, u32[]{:S(2)}, u32[]{:S(2)}) collective-permute-start(bf16[288,2560]{1,0:T(8,128)(2,1)S(1)} %pad_maximum_fusion.11.refs_0_), channel_id=1, source_target_pairs={{8,0},{16,8},{24,16},{28,24},{20,28},{12,20},{4,12},{0,4},{9,1},{1... | collective-permute-start | bytes 4423688 | tf_op jit(solution)/shard_map/ppermute | solution.py:102
  6.9 35.3 %collective-permute-start.2 = (bf16[288,2560]{1,0:T(8,128)(2,1)S(1)}, bf16[288,2560]{1,0:T(8,128)(2,1)}, u32[]{:S(2)}, u32[]{:S(2)}) collective-permute-start(bf16[288,2560]{1,0:T(8,128)(2,1)S(1)} %pad_maximum_fusion.11.refs_0_), channel_id=1, source_target_pairs={{0,1},{1,0},{2,3},{3,2},{4,5},{5,4},{6,7},{7,6},{8,9},{9,8},{10,11... | collective-permute-start | bytes 4423688 | tf_op jit(solution)/shard_map/ppermute | solution.py:157
  42.2 35.0 %collective-permute-start.3 = (bf16[288,2560]{1,0:T(8,128)(2,1)S(1)}, bf16[288,2560]{1,0:T(8,128)(2,1)}, u32[]{:S(2)}, u32[]{:S(2)}) collective-permute-start(bf16[288,2560]{1,0:T(8,128)(2,1)S(1)} %collective-permute-done.refs_2_), channel_id=1, source_target_pairs={{0,8},{8,16},{16,24},{24,28},{28,20},{20,12},{12,4},{4,0},{1,9},{9... | collective-permute-start | bytes 4423688 | tf_op jit(solution)/shard_map/ppermute | solution.py:102
  44.3 35.0 %collective-permute-start.5 = (bf16[288,2560]{1,0:T(8,128)(2,1)S(1)}, bf16[288,2560]{1,0:T(8,128)(2,1)S(1)}, u32[]{:S(2)}, u32[]{:S(2)}) collective-permute-start(bf16[288,2560]{1,0:T(8,128)(2,1)S(1)} %collective-permute-done.refs_2_), channel_id=1, source_target_pairs={{0,1},{1,0},{2,3},{3,2},{4,5},{5,4},{6,7},{7,6},{8,9},{9,8},{10,11... | collective-permute-start | bytes 4423688 | tf_op jit(solution)/shard_map/ppermute | solution.py:157
  44.5 34.8 %collective-permute-start.4 = (bf16[288,2560]{1,0:T(8,128)(2,1)}, bf16[288,2560]{1,0:T(8,128)(2,1)}, u32[]{:S(2)}, u32[]{:S(2)}) collective-permute-start(bf16[288,2560]{1,0:T(8,128)(2,1)} %collective-permute-done.1.refs_4_), channel_id=1, source_target_pairs={{8,0},{16,8},{24,16},{28,24},{20,28},{12,20},{4,12},{0,4},{9,1},{1... | collective-permute-start | bytes 4423688 | tf_op jit(solution)/shard_map/ppermute | solution.py:102
  44.8 34.5 %collective-permute-start.6 = (bf16[288,2560]{1,0:T(8,128)(2,1)}, bf16[288,2560]{1,0:T(8,128)(2,1)S(1)}, u32[]{:S(2)}, u32[]{:S(2)}) collective-permute-start(bf16[288,2560]{1,0:T(8,128)(2,1)} %collective-permute-done.1.refs_4_), channel_id=1, source_target_pairs={{0,1},{1,0},{2,3},{3,2},{4,5},{5,4},{6,7},{7,6},{8,9},{9,8},{10,11... | collective-permute-start | bytes 4423688 | tf_op jit(solution)/shard_map/ppermute | solution.py:157
  80.4 33.9 %collective-permute-start.7 = (bf16[288,2560]{1,0:T(8,128)(2,1)}, bf16[288,2560]{1,0:T(8,128)(2,1)S(1)}, u32[]{:S(2)}, u32[]{:S(2)}) collective-permute-start(bf16[288,2560]{1,0:T(8,128)(2,1)} %collective-permute-done.3.refs_0_), channel_id=1, source_target_pairs={{0,8},{8,16},{16,24},{24,28},{28,20},{20,12},{12,4},{4,0},{1,9},{9... | collective-permute-start | bytes 4423688 | tf_op jit(solution)/shard_map/ppermute | solution.py:102
  82.0 34.1 %collective-permute-start.8 = (bf16[288,2560]{1,0:T(8,128)(2,1)}, bf16[288,2560]{1,0:T(8,128)(2,1)S(1)}, u32[]{:S(2)}, u32[]{:S(2)}) collective-permute-start(bf16[288,2560]{1,0:T(8,128)(2,1)} %collective-permute-done.4.refs_2_), channel_id=1, source_target_pairs={{8,0},{16,8},{24,16},{28,24},{20,28},{12,20},{4,12},{0,4},{9,1},{1... | collective-permute-start | bytes 4423688 | tf_op jit(solution)/shard_map/ppermute | solution.py:102
  82.9 33.2 %collective-permute-start.9 = (bf16[288,2560]{1,0:T(8,128)(2,1)}, bf16[288,2560]{1,0:T(8,128)(2,1)}, u32[]{:S(2)}, u32[]{:S(2)}) collective-permute-start(bf16[288,2560]{1,0:T(8,128)(2,1)} %collective-permute-done.3.refs_0_), channel_id=1, source_target_pairs={{0,1},{1,0},{2,3},{3,2},{4,5},{5,4},{6,7},{7,6},{8,9},{9,8},{10,11... | collective-permute-start | bytes 4423688 | tf_op jit(solution)/shard_map/ppermute | solution.py:157
  141.0 61.1 %collective-permute-start.15 = (bf16[288,2304]{1,0:T(8,128)(2,1)}, bf16[288,2304]{1,0:T(8,128)(2,1)}, u32[]{:S(2)}, u32[]{:S(2)}) collective-permute-start(bf16[288,2304]{1,0:T(8,128)(2,1)} %get-tuple-element.537), channel_id=1, source_target_pairs={{0,16},{4,20},{8,24},{12,28},{16,0},{20,4},{24,8},{28,12},{1,17},{... | collective-permute-start | bytes 3981320 | tf_op jit(solution)/shard_map/ppermute | solution.py:157
  238.4 53.0 %collective-permute-start.19 = (bf16[8,288,512]{2,1,0:T(8,128)(2,1)}, bf16[8,288,512]{2,1,0:T(8,128)(2,1)}, u32[]{:S(2)}, u32[]{:S(2)}) collective-permute-start(bf16[8,288,512]{2,1,0:T(8,128)(2,1)} %copy-done.37), channel_id=1, source_target_pairs={{0,2},{1,3},{2,0},{3,1},{4,6},{5,7},{6,4},{7,5},{8,10},{9,11},{10,... | collective-permute-start | bytes 7077896 | tf_op jit(solution)/shard_map/ppermute | solution.py:157
  322.6 40.4 %all-to-all-start.4 = ((bf16[8,128,512]{2,1,0:T(8,128)(2,1)}), bf16[8,128,512]{2,1,0:T(8,128)(2,1)S(1)}, u32[]{:S(2)}, u32[]{:S(2)}) async-start(bf16[8,128,512]{2,1,0:T(8,128)(2,1)} %bitcast.235), calls=%async_computation.4 | async-start | bytes 2097152 | tf_op jit(solution)/shard_map/all_to_all | solution.py:161
  326.3 36.7 %collective-permute-start.22 = (bf16[288,2304]{1,0:T(8,128)(2,1)}, bf16[288,2304]{1,0:T(8,128)(2,1)}, u32[]{:S(2)}, u32[]{:S(2)}) collective-permute-start(bf16[288,2304]{1,0:T(8,128)(2,1)} %collective-permute-done.15.refs_0_), channel_id=1, source_target_pairs={{0,2},{1,3},{2,0},{3,1},{4,6},{5,7},{6,4},{7,5},{8,10},{9,11},{10,... | collective-permute-start | bytes 3981320 | tf_op jit(solution)/shard_map/ppermute | solution.py:157
  363.0 31.3 %all-to-all-start.5 = ((bf16[8,128,512]{2,1,0:T(8,128)(2,1)}), bf16[8,128,512]{2,1,0:T(8,128)(2,1)S(1)}, u32[]{:S(2)}, u32[]{:S(2)}) async-start(bf16[8,128,512]{2,1,0:T(8,128)(2,1)} %bitcast.236), calls=%async_computation.5 | async-start | bytes 2097152 | tf_op jit(solution)/shard_map/all_to_all | solution.py:161
  394.3 58.1 %collective-permute-start.25 = (bf16[288,2304]{1,0:T(8,128)(2,1)S(1)}, bf16[288,2304]{1,0:T(8,128)(2,1)}, u32[]{:S(2)}, u32[]{:S(2)}) collective-permute-start(bf16[288,2304]{1,0:T(8,128)(2,1)S(1)} %copy-done.50), channel_id=1, source_target_pairs={{0,16},{4,20},{8,24},{12,28},{16,0},{20,4},{24,8},{28,12},{1,17},{... | collective-permute-start | bytes 3981320 | tf_op jit(solution)/shard_map/ppermute | solution.py:157
  452.3 31.3 %collective-permute-start.27 = (bf16[288,2304]{1,0:T(8,128)(2,1)}, bf16[288,2304]{1,0:T(8,128)(2,1)S(1)}, u32[]{:S(2)}, u32[]{:S(2)}) collective-permute-start(bf16[288,2304]{1,0:T(8,128)(2,1)} %collective-permute-done.25.refs_0_), channel_id=1, source_target_pairs={{0,2},{1,3},{2,0},{3,1},{4,6},{5,7},{6,4},{7,5},{8,10},{9,11},{10,... | collective-permute-start | bytes 3981320 | tf_op jit(solution)/shard_map/ppermute | solution.py:157
  452.7 59.3 %collective-permute-start.26 = (bf16[288,2304]{1,0:T(8,128)(2,1)S(1)}, bf16[288,2304]{1,0:T(8,128)(2,1)}, u32[]{:S(2)}, u32[]{:S(2)}) collective-permute-start(bf16[288,2304]{1,0:T(8,128)(2,1)S(1)} %copy-done.49), channel_id=1, source_target_pairs={{0,16},{4,20},{8,24},{12,28},{16,0},{20,4},{24,8},{28,12},{1,17},{... | collective-permute-start | bytes 3981320 | tf_op jit(solution)/shard_map/ppermute | solution.py:157
  512.0 31.4 %collective-permute-start.32 = (bf16[288,2304]{1,0:T(8,128)(2,1)}, bf16[288,2304]{1,0:T(8,128)(2,1)}, u32[]{:S(2)}, u32[]{:S(2)}) collective-permute-start(bf16[288,2304]{1,0:T(8,128)(2,1)} %collective-permute-done.26.refs_0_), channel_id=1, source_target_pairs={{0,2},{1,3},{2,0},{3,1},{4,6},{5,7},{6,4},{7,5},{8,10},{9,11},{10,... | collective-permute-start | bytes 3981320 | tf_op jit(solution)/shard_map/ppermute | solution.py:157
  566.6 34.1 %collective-permute-start.37 = (bf16[256,2304]{1,0:T(8,128)(2,1)S(1)}, bf16[256,2304]{1,0:T(8,128)(2,1)S(1)}, u32[]{:S(2)}, u32[]{:S(2)}) collective-permute-start(bf16[256,2304]{1,0:T(8,128)(2,1)S(1)} %copy-done.62), channel_id=1, source_target_pairs={{0,8},{8,12},{12,4},{4,0},{16,24},{24,28},{28,20},{20,16},{1,9},{9... | collective-permute-start | bytes 3538952 | tf_op jit(solution)/shard_map/ppermute | solution.py:102
  568.4 32.3 %collective-permute-start.38 = (bf16[256,2304]{1,0:T(8,128)(2,1)S(1)}, bf16[256,2304]{1,0:T(8,128)(2,1)S(1)}, u32[]{:S(2)}, u32[]{:S(2)}) collective-permute-start(bf16[256,2304]{1,0:T(8,128)(2,1)S(1)} %copy-done.62), channel_id=1, source_target_pairs={{8,0},{12,8},{4,12},{0,4},{24,16},{28,24},{20,28},{16,20},{9,1},{1... | collective-permute-start | bytes 3538952 | tf_op jit(solution)/shard_map/ppermute | solution.py:102
  748.8 33.4 %collective-permute-start.52 = (bf16[256,2304]{1,0:T(8,128)(2,1)S(1)}, bf16[256,2304]{1,0:T(8,128)(2,1)S(1)}, u32[]{:S(2)}, u32[]{:S(2)}) collective-permute-start(bf16[256,2304]{1,0:T(8,128)(2,1)S(1)} %pad_maximum_fusion.21), channel_id=1, source_target_pairs={{8,0},{12,8},{4,12},{0,4},{24,16},{28,24},{20,28},{16,20},{9,1},{1... | collective-permute-start | bytes 3538952 | tf_op jit(solution)/shard_map/ppermute | solution.py:102
  750.2 31.9 %collective-permute-start.51 = (bf16[256,2304]{1,0:T(8,128)(2,1)S(1)}, bf16[256,2304]{1,0:T(8,128)(2,1)S(1)}, u32[]{:S(2)}, u32[]{:S(2)}) collective-permute-start(bf16[256,2304]{1,0:T(8,128)(2,1)S(1)} %pad_maximum_fusion.20), channel_id=1, source_target_pairs={{0,8},{8,12},{12,4},{4,0},{16,24},{24,28},{28,20},{20,16},{1,9},{9... | collective-permute-start | bytes 3538952 | tf_op jit(solution)/shard_map/ppermute | solution.py:102
  851.4 33.7 %collective-permute-start.60 = (bf16[256,2304]{1,0:T(8,128)(2,1)S(1)}, bf16[256,2304]{1,0:T(8,128)(2,1)S(1)}, u32[]{:S(2)}, u32[]{:S(2)}) collective-permute-start(bf16[256,2304]{1,0:T(8,128)(2,1)S(1)} %pad_maximum_fusion.23), channel_id=1, source_target_pairs={{8,0},{12,8},{4,12},{0,4},{24,16},{28,24},{20,28},{16,20},{9,1},{1... | collective-permute-start | bytes 3538952 | tf_op jit(solution)/shard_map/ppermute | solution.py:102
  852.5 32.7 %collective-permute-start.59 = (bf16[256,2304]{1,0:T(8,128)(2,1)S(1)}, bf16[256,2304]{1,0:T(8,128)(2,1)S(1)}, u32[]{:S(2)}, u32[]{:S(2)}) collective-permute-start(bf16[256,2304]{1,0:T(8,128)(2,1)S(1)} %pad_maximum_fusion.22), channel_id=1, source_target_pairs={{0,8},{8,12},{12,4},{4,0},{16,24},{24,28},{28,20},{20,16},{1,9},{9... | collective-permute-start | bytes 3538952 | tf_op jit(solution)/shard_map/ppermute | solution.py:102
  920.5 32.7 %collective-permute-start.64 = (bf16[256,2304]{1,0:T(8,128)(2,1)S(1)}, bf16[256,2304]{1,0:T(8,128)(2,1)}, u32[]{:S(2)}, u32[]{:S(2)}) collective-permute-start(bf16[256,2304]{1,0:T(8,128)(2,1)S(1)} %pad_maximum_fusion.25), channel_id=1, source_target_pairs={{8,0},{12,8},{4,12},{0,4},{24,16},{28,24},{20,28},{16,20},{9,1},{1... | collective-permute-start | bytes 3538952 | tf_op jit(solution)/shard_map/ppermute | solution.py:102
  922.1 31.1 %collective-permute-start.63 = (bf16[256,2304]{1,0:T(8,128)(2,1)S(1)}, bf16[256,2304]{1,0:T(8,128)(2,1)}, u32[]{:S(2)}, u32[]{:S(2)}) collective-permute-start(bf16[256,2304]{1,0:T(8,128)(2,1)S(1)} %pad_maximum_fusion.24), channel_id=1, source_target_pairs={{0,8},{8,12},{12,4},{4,0},{16,24},{24,28},{28,20},{20,16},{1,9},{9... | collective-permute-start | bytes 3538952 | tf_op jit(solution)/shard_map/ppermute | solution.py:102
  989.1 31.7 %collective-permute-start.66 = (bf16[2,288,1152]{2,1,0:T(8,128)(2,1)S(1)}, bf16[2,288,1152]{2,1,0:T(8,128)(2,1)}, u32[]{:S(2)}, u32[]{:S(2)}) collective-permute-start(bf16[2,288,1152]{2,1,0:T(8,128)(2,1)S(1)} %get-tuple-element.824), channel_id=1, source_target_pairs={{0,2},{1,3},{2,0},{3,1},{4,6},{5,7},{6,4},{7,5},{8,10},{9,11},{10,... | collective-permute-start | bytes 3981320 | tf_op jit(solution)/shard_map/ppermute | solution.py:157
  1020.8 34.6 %collective-permute-start.69 = (bf16[2304,1024]{1,0:T(8,128)(2,1)}, bf16[2304,1024]{1,0:T(8,128)(2,1)}, u32[]{:S(2)}, u32[]{:S(2)}) collective-permute-start(bf16[2304,1024]{1,0:T(8,128)(2,1)} %convolution_convert_fusion.1), channel_id=1, source_target_pairs={{0,1},{1,0},{2,3},{3,2},{4,5},{5,4},{6,7},{7,6},{8,9},{9,8},{10,11... | collective-permute-start | bytes 14155784 | tf_op jit(solution)/shard_map/ppermute | solution.py:157
  1020.9 41.1 %collective-permute-start.68 = (bf16[2,288,1152]{2,1,0:T(8,128)(2,1)}, bf16[2,288,1152]{2,1,0:T(8,128)(2,1)}, u32[]{:S(2)}, u32[]{:S(2)}) collective-permute-start(bf16[2,288,1152]{2,1,0:T(8,128)(2,1)} %get-tuple-element.840), channel_id=1, source_target_pairs={{0,2},{1,3},{2,0},{3,1},{4,6},{5,7},{6,4},{7,5},{8,10},{9,11},{10,... | collective-permute-start | bytes 3981320 | tf_op jit(solution)/shard_map/ppermute | solution.py:157
  1025.8 36.2 %all-to-all-start.8 = ((bf16[8,128,512]{2,1,0:T(8,128)(2,1)}), bf16[8,128,512]{2,1,0:T(8,128)(2,1)}, u32[]{:S(2)}, u32[]{:S(2)}) async-start(bf16[8,128,512]{2,1,0:T(8,128)(2,1)} %bitcast.232), calls=%async_computation.8 | async-start | bytes 2097152 | tf_op jit(solution)/shard_map/all_to_all | solution.py:161
  1065.3 42.9 %collective-permute-start.71 = (bf16[2304,256]{1,0:T(8,128)(2,1)}, bf16[2304,256]{1,0:T(8,128)(2,1)}, u32[]{:S(2)}, u32[]{:S(2)}) collective-permute-start(bf16[2304,256]{1,0:T(8,128)(2,1)} %get-tuple-element.1018), channel_id=1, source_target_pairs={{0,2},{1,3},{2,0},{3,1},{4,6},{5,7},{6,4},{7,5},{8,10},{9,11},{10,... | collective-permute-start | bytes 3538952 | tf_op jit(solution)/shard_map/ppermute | solution.py:157
  1066.6 41.4 %collective-permute-start.70 = (bf16[2,256,512]{2,1,0:T(8,128)(2,1)}, bf16[2,256,512]{2,1,0:T(8,128)(2,1)S(1)}, u32[]{:S(2)}, u32[]{:S(2)}) collective-permute-start(bf16[2,256,512]{2,1,0:T(8,128)(2,1)} %get-tuple-element.854), channel_id=1, source_target_pairs={{0,4},{4,0},{8,12},{12,8},{16,20},{20,16},{24,28},{28,24},{1,5},{5... | collective-permute-start | bytes 1572872 | tf_op jit(solution)/shard_map/ppermute | solution.py:177
  1068.6 39.6 %all-to-all-start.9 = ((bf16[8,128,512]{2,1,0:T(8,128)(2,1)}), bf16[8,128,512]{2,1,0:T(8,128)(2,1)S(1)}, u32[]{:S(2)}, u32[]{:S(2)}) async-start(bf16[8,128,512]{2,1,0:T(8,128)(2,1)} %bitcast.68), calls=%async_computation.9 | async-start | bytes 2097152 | tf_op jit(solution)/shard_map/all_to_all | solution.py:161
  1111.5 33.6 %all-to-all-start.10 = ((bf16[4,256,512]{2,1,0:T(8,128)(2,1)}), bf16[4,256,512]{2,1,0:T(8,128)(2,1)S(1)}, u32[]{:S(2)}, u32[]{:S(2)}) async-start(bf16[4,256,512]{2,1,0:T(8,128)(2,1)} %pad_maximum_fusion.26), calls=%async_computation.10 | async-start | bytes 2097152 | tf_op jit(solution)/shard_map/all_to_all | solution.py:168
  1149.1 36.2 %collective-permute-start.75 = (bf16[2,288,1152]{2,1,0:T(8,128)(2,1)}, bf16[2,288,1152]{2,1,0:T(8,128)(2,1)}, u32[]{:S(2)}, u32[]{:S(2)}) collective-permute-start(bf16[2,288,1152]{2,1,0:T(8,128)(2,1)} %get-tuple-element.880), channel_id=1, source_target_pairs={{0,2},{1,3},{2,0},{3,1},{4,6},{5,7},{6,4},{7,5},{8,10},{9,11},{10,... | collective-permute-start | bytes 3981320 | tf_op jit(solution)/shard_map/ppermute | solution.py:157
  1149.7 35.6 %all-to-all-start.11 = ((bf16[4,256,512]{2,1,0:T(8,128)(2,1)}), bf16[4,256,512]{2,1,0:T(8,128)(2,1)}, u32[]{:S(2)}, u32[]{:S(2)}) async-start(bf16[4,256,512]{2,1,0:T(8,128)(2,1)} %add_convert_fusion.14), calls=%async_computation.11 | async-start | bytes 2097152 | tf_op jit(solution)/shard_map/all_to_all | solution.py:168
  1185.3 48.8 %collective-permute-start.78 = (bf16[2,576,2304]{2,1,0:T(8,128)(2,1)}, bf16[2,576,2304]{2,1,0:T(8,128)(2,1)}, u32[]{:S(2)}, u32[]{:S(2)}) collective-permute-start(bf16[2,576,2304]{2,1,0:T(8,128)(2,1)} %bitcast.247), channel_id=1, source_target_pairs={{0,1},{1,0},{2,3},{3,2},{4,5},{5,4},{6,7},{7,6},{8,9},{9,8},{10,11... | collective-permute-start | bytes 15925256 | tf_op jit(solution)/shard_map/ppermute | solution.py:157
  1190.5 42.5 %collective-permute-start.79 = (bf16[2,288,1152]{2,1,0:T(8,128)(2,1)S(1)}, bf16[2,288,1152]{2,1,0:T(8,128)(2,1)S(1)}, u32[]{:S(2)}, u32[]{:S(2)}) collective-permute-start(bf16[2,288,1152]{2,1,0:T(8,128)(2,1)S(1)} %copy-done.48), channel_id=1, source_target_pairs={{0,2},{1,3},{2,0},{3,1},{4,6},{5,7},{6,4},{7,5},{8,10},{9,11},{10,... | collective-permute-start | bytes 3981320 | tf_op jit(solution)/shard_map/ppermute | solution.py:157
  1295.9 35.2 %collective-permute-start.85 = (bf16[288,2560]{1,0:T(8,128)(2,1)}, bf16[288,2560]{1,0:T(8,128)(2,1)}, u32[]{:S(2)}, u32[]{:S(2)}) collective-permute-start(bf16[288,2560]{1,0:T(8,128)(2,1)} %pad_maximum_fusion.13), channel_id=1, source_target_pairs={{8,0},{16,8},{24,16},{28,24},{20,28},{12,20},{4,12},{0,4},{9,1},{1... | collective-permute-start | bytes 4423688 | tf_op jit(solution)/shard_map/ppermute | solution.py:102
  1299.1 33.2 %collective-permute-start.84 = (bf16[288,2560]{1,0:T(8,128)(2,1)}, bf16[288,2560]{1,0:T(8,128)(2,1)}, u32[]{:S(2)}, u32[]{:S(2)}) collective-permute-start(bf16[288,2560]{1,0:T(8,128)(2,1)} %fusion.8), channel_id=1, source_target_pairs={{0,8},{8,16},{16,24},{24,28},{28,20},{20,12},{12,4},{4,0},{1,9},{9... | collective-permute-start | bytes 4423688 | tf_op jit(solution)/shard_map/ppermute | solution.py:102
  1336.0 35.0 %collective-permute-start.88 = (bf16[288,2560]{1,0:T(8,128)(2,1)S(1)}, bf16[288,2560]{1,0:T(8,128)(2,1)S(1)}, u32[]{:S(2)}, u32[]{:S(2)}) collective-permute-start(bf16[288,2560]{1,0:T(8,128)(2,1)S(1)} %add_convert_fusion.9), channel_id=1, source_target_pairs={{8,0},{16,8},{24,16},{28,24},{20,28},{12,20},{4,12},{0,4},{9,1},{1... | collective-permute-start | bytes 4423688 | tf_op jit(solution)/shard_map/ppermute | solution.py:102
  1339.3 31.8 %collective-permute-start.87 = (bf16[288,2560]{1,0:T(8,128)(2,1)S(1)}, bf16[288,2560]{1,0:T(8,128)(2,1)S(1)}, u32[]{:S(2)}, u32[]{:S(2)}) collective-permute-start(bf16[288,2560]{1,0:T(8,128)(2,1)S(1)} %add_convert_fusion.10), channel_id=1, source_target_pairs={{0,8},{8,16},{16,24},{24,28},{28,20},{20,12},{12,4},{4,0},{1,9},{9... | collective-permute-start | bytes 4423688 | tf_op jit(solution)/shard_map/ppermute | solution.py:102
  1373.4 31.0 %collective-permute-start.91 = (bf16[288,2560]{1,0:T(8,128)(2,1)S(1)}, bf16[288,2560]{1,0:T(8,128)(2,1)S(1)}, u32[]{:S(2)}, u32[]{:S(2)}) collective-permute-start(bf16[288,2560]{1,0:T(8,128)(2,1)S(1)} %add_convert_fusion.7), channel_id=1, source_target_pairs={{8,0},{16,8},{24,16},{28,24},{20,28},{12,20},{4,12},{0,4},{9,1},{1... | collective-permute-start | bytes 4423688 | tf_op jit(solution)/shard_map/ppermute | solution.py:102
  1435.5 30.9 %collective-permute-start.96 = (bf16[288,1152]{1,0:T(8,128)(2,1)}, bf16[288,1152]{1,0:T(8,128)(2,1)}, u32[]{:S(2)}, u32[]{:S(2)}) collective-permute-start(bf16[288,1152]{1,0:T(8,128)(2,1)} %get-tuple-element.954), channel_id=1, source_target_pairs={{0,16},{4,20},{8,24},{12,28},{16,0},{20,4},{24,8},{28,12},{1,17},{... | collective-permute-start | bytes 1990664 | tf_op jit(solution)/shard_map/ppermute | solution.py:157
  1486.4 39.7 %collective-permute-start.104 = (bf16[288,3072]{1,0:T(8,128)(2,1)}, bf16[288,3072]{1,0:T(8,128)(2,1)}, u32[]{:S(2)}, u32[]{:S(2)}) collective-permute-start(bf16[288,3072]{1,0:T(8,128)(2,1)} %pad_maximum_fusion.7), channel_id=1, source_target_pairs={{0,1},{1,0},{2,3},{3,2},{4,5},{5,4},{6,7},{7,6},{8,9},{9,8},{10,11... | collective-permute-start | bytes 5308424 | tf_op jit(solution)/shard_map/ppermute | solution.py:157
  1494.3 31.7 %collective-permute-start.103 = (bf16[288,1152]{1,0:T(8,128)(2,1)S(1)}, bf16[288,1152]{1,0:T(8,128)(2,1)S(1)}, u32[]{:S(2)}, u32[]{:S(2)}) collective-permute-start(bf16[288,1152]{1,0:T(8,128)(2,1)S(1)} %copy-done.71), channel_id=1, source_target_pairs={{0,16},{4,20},{8,24},{12,28},{16,0},{20,4},{24,8},{28,12},{1,17},{... | collective-permute-start | bytes 1990664 | tf_op jit(solution)/shard_map/ppermute | solution.py:157
  1531.9 32.1 %collective-permute-start.107 = (bf16[288,1152]{1,0:T(8,128)(2,1)}, bf16[288,1152]{1,0:T(8,128)(2,1)}, u32[]{:S(2)}, u32[]{:S(2)}) collective-permute-start(bf16[288,1152]{1,0:T(8,128)(2,1)} %get-tuple-element.977), channel_id=1, source_target_pairs={{0,16},{4,20},{8,24},{12,28},{16,0},{20,4},{24,8},{28,12},{1,17},{... | collective-permute-start | bytes 1990664 | tf_op jit(solution)/shard_map/ppermute | solution.py:157
  (190 other events, 2863.3 us)

commit v13 on v12

--- a/solution.py
+++ b/solution.py
@@ -711,6 +711,41 @@
         ),
         name="branch_back",
     )(part, a, b, mid, branch, cotangent, mlp_gain[None], gain[None], weights)
+
+
+def out_product_kernel(info, branch_ref, att_ref, received_ref, own_ref, send_ref):
+    total = dot(branch_ref[...], att_ref[...], TN) + received_ref[...].astype(f32)
+    total = total.astype(bf16)
+    width = own_ref.shape[1]
+    first = info[1] == 0
+    own_ref[...] = jnp.where(first, total[:, :width], total[:, width:])
+    send_ref[...] = jnp.where(first, total[:, width:], total[:, :width])
+
+
+def out_product(info, branch, attended, received):
+    rows, depth = branch.shape
+    cols = attended.shape[1] // 2
+    tile = tile_of(depth)
+    out = pl.BlockSpec((tile, cols // 2), lambda i, c: (i, 0))
+    return pl.pallas_call(
+        out_product_kernel,
+        grid_spec=pltpu.PrefetchScalarGridSpec(
+            num_scalar_prefetch=1,
+            grid=(depth // tile,),
+            in_specs=[
+                pl.BlockSpec((rows, tile), lambda i, c: (0, i)),
+                pl.BlockSpec((rows, cols), lambda i, c: (0, c[0])),
+                pl.BlockSpec((tile, cols), lambda i, c: (i, 0)),
+            ],
+            out_specs=[out, out],
+        ),
+        out_shape=[jax.ShapeDtypeStruct((depth, cols // 2), bf16)] * 2,
+        compiler_params=pltpu.CompilerParams(vmem_limit_bytes=VMEM_LIMIT),
+        cost_estimate=pl.CostEstimate(
+            flops=2 * rows * depth * cols, bytes_accessed=4 * depth * cols, transcendentals=0
+        ),
+        name="out_product",
+    )(info, branch, attended, received)
 
 
 def turn(values, cosine, sine):
@@ -1526,35 +1561,49 @@
     out_sent = swap(out_send, "seq", 1)
     query = all_to_all(clock.hold(dq))
     pair_a = class_sum([v[0] for v in parts_of_pair])
-    out_part = low_sum(
-        half_dot(all_branch, clock.hold(all_attended), side, half_out), out_sent
-    )
-    query, pair_a, down_moved[1], out_part, *work = clock.sync(
-        query, pair_a, down_moved[1], out_part, *attend_back(1)
-    )
+    if members == 2:
+        out_pair = out_product(
+            jnp.stack([side, member]).astype(jnp.int32),
+            all_branch,
+            clock.hold(all_attended),
+            out_sent,
+        )
+    else:
+        out_pair = [
+            low_sum(half_dot(all_branch, clock.hold(all_attended), side, half_out), out_sent)
+        ]
+    query, pair_a, down_moved[1], *work = clock.sync(
+        query, pair_a, down_moved[1], *out_pair, *attend_back(1)
+    )
+    out_pair, work = work[: len(out_pair)], work[len(out_pair) :]
     down_grad = far_join(down_keep, down_moved)
     query_back.append(query)
     grad_attend.append(work)
     dq, *dkv = grad_attend[1]
     query = all_to_all(clock.hold(dq))
     pair_b = class_sum([clock.hold(v[1]) for v in parts_of_pair])
-    out_pieces = {
-        t: lax.dynamic_slice_in_dim(
-            clock.hold(out_part), jnp.bitwise_xor(member, t) * split_out, split_out, 1
-        )
-        for t in range(members)
-    }
     out_moved = []
     if members == 2:
-        out_parts = [out_pieces[1][:, : split_out // 2], out_pieces[1][:, split_out // 2 :]]
+        out_piece = out_pair[0]
+        out_parts = [
+            clock.hold(out_pair[1])[:, : split_out // 2],
+            out_pair[1][:, split_out // 2 :],
+        ]
         out_moved.append(swap(out_parts[0], "seq", seq_bits[1]))
     else:
+        out_pieces = {
+            t: lax.dynamic_slice_in_dim(
+                clock.hold(out_pair[0]), jnp.bitwise_xor(member, t) * split_out, split_out, 1
+            )
+            for t in range(members)
+        }
         for bit in seq_bits[1:]:
             for t in sorted(out_pieces):
                 if not t & (bit // 2) and t | (bit // 2) in out_pieces:
                     out_pieces[t] = low_sum(
                         out_pieces[t], swap(out_pieces.pop(t | (bit // 2)), "seq", bit)
                     )
+        out_piece = out_pieces[0]
     up_keep, up_send = weight_sum(grad_up, gathered)
     query, pair_b, down_grad, up_keep, up_send, *out_moved = clock.sync(
         query, pair_b, down_grad, up_keep, up_send, *out_moved
@@ -1567,7 +1616,6 @@
     if members == 2:
         out_moved.append(swap(clock.hold(out_parts[1]), "seq", seq_bits[1]))
     pair, pair_sum, up_grad, *out_moved = clock.sync(pair, pair_sum, up_grad, *out_moved)
-    out_piece = out_pieces[0]
     if out_moved:
         out_piece = low_sum(out_piece, jnp.concatenate(out_moved, axis=1))
     pair_back.append(pair)
@@ -1630,18 +1678,23 @@
             grads = [jnp.concatenate([g, swap(g, "seq", bit)], axis=0) for g in grads]
         return grads
 
+    rows_out = jnp.stack(layer_out)
     a, b = halves(clock.hold(part_of(wide // 2)))
     gate_moved = []
     for k in range(wide // 2 - 1, -1, -1):
         step = wide // 2 - 1 - k
         a, b = hop(a, b, wide)
         work = []
-        if step in (1, 2):
+        if step == 0:
+            work = [clock.hold(rows_out)]
+        elif step in (1, 2):
             work = [far_move(gate_parts[step - 1])]
         elif step == half_wide - 1:
             work = spread_grad([clock.hold(v) for v in down_grad], far_bits)
         a, b, *work = clock.sync(a, b, *work)
-        if step in (1, 2):
+        if step == 0:
+            rows_out = work[0]
+        elif step in (1, 2):
             gate_moved += work
         elif step == half_wide - 1:
             down_grad = work
@@ -1709,18 +1762,22 @@
     ).astype(f32)
     down_grad = spread_grad([clock.hold(v) for v in down_grad], seq_bits[:1])
     mlp_grad = unpack(down_grad, pieces, 2, [])
-    moved, attn_grad, mlp_grad, *gate_grad = clock.sync(moved, attn_grad, mlp_grad, *gate_grad)
+    up_grad = spread_grad([clock.hold(v) for v in up_grad], seq_bits[:1])
+    tokens_out = jnp.stack([first_tokens, last_tokens])
+    parts_up = len(up_grad)
+    moved, attn_grad, mlp_grad, tokens_out, *work = clock.sync(
+        moved, attn_grad, mlp_grad, tokens_out, *up_grad, *gate_grad
+    )
+    up_grad, gate_grad = work[:parts_up], work[parts_up:]
     last = spread_grad([low_sum(gate_own[1], moved)], far_bits)
-    up_grad = spread_grad([clock.hold(v) for v in up_grad], seq_bits[:1])
-    mlp_grad = unpack(up_grad, pieces, 1, [mlp_grad])
+    mlp_grad = unpack(up_grad, pieces, 1, [clock.hold(mlp_grad)])
     gate_grad = spread_grad([clock.hold(v) for v in gate_grad], seq_bits[:1])
     mlp_grad, *gate_grad = clock.sync(mlp_grad, *gate_grad, *last)
     gate_grad[1:] = spread_grad(gate_grad[1:], seq_bits[:1])
     mlp_grad = unpack(gate_grad, pieces, 0, [mlp_grad])
-    grad_tokens = [first_tokens, last_tokens]
     return (
-        jnp.stack(layer_out),
-        jnp.stack(grad_tokens),
+        rows_out,
+        tokens_out,
         attn_grad,
         mlp_grad,
         gains[0],

time: 1620 us -> 1640 us (1.012)
  waiting for transfers between devices: 553 us -> 593 us
  other arithmetic: 122 us -> 104 us
  matrix products: 99.9 us -> 83.4 us
    ppermute x63, waiting for transfers between devices: 300 us -> 338 us  [swap(): return lax.ppermute(value, axis, [(i, i ^ bit) for i in range(size)])]
    dot_general x8 -> x7, matrix products: 99.9 us -> 83.4 us  [dot(): return lax.dot_general(a, b, (dims, ((), ())), preferred_element_type=f32)]
    convert_element_type x27 -> x26, other arithmetic: 60.5 us -> 52.9 us  [low_sum(): return sum((t.astype(f32) for t in terms)).astype(bf16)]
    unnamed x252 -> x249, local copies, waits for them, and re-layouts: 52.2 us -> 58.3 us
  transfers between devices with their start and end apart: 129 -> 129, of which waited for: 63 -> 68; matrix products, arithmetic and copies ran while one was open for 15% -> 12% of each run, Pallas kernels for 33% -> 33%
where the time goes in v13:
time: 1640 us; the launch traced here: 1630 us
  waiting for transfers between devices  593 us (36%)
  Pallas kernels  571 us (35%)
  starting transfers between devices  153 us (9%)
  local copies, waits for them, and re-layouts  123 us (8%)
  other arithmetic  104 us (6%)
  matrix products  83.4 us (5%)
    ppermute x63, waiting for transfers between devices, swap(): return lax.ppermute(value, axis, [(i, i ^ bit) for i in range(size)])  338 us
    ppermute x48, waiting for transfers between devices, hop(): return (lax.ppermute(a, 'wide', up), lax.ppermute(b, 'wide', down))  159 us
    pallas_call x3, Pallas kernels, weight_back(): kernel_call(functools.partial(weight_kernel, count=count, tiles=tiles), t...  91.4 us
    dot_general x7, matrix products, dot(): return lax.dot_general(a, b, (dims, ((), ())), preferred_element_type=f32)  83.4 us
    ppermute x6, waiting for transfers between devices, class_ring(): return lax.ppermute(value, 'wide', perm)  73.6 us
    pallas_call x4, Pallas kernels, input_back(): kernel_call(input_back_kernel, tiles, [whole_spec(grad_gate.shape)] * 2 +...  69.2 us
    pallas_call x3, Pallas kernels, open_forward(): kernel_call(open_kernel, tiles, [whole_spec(x.shape)] + [row_spec(tile, d...  62.7 us
    unnamed x249, local copies, waits for them, and re-layouts  58.3 us
  transfers between devices with their start and end apart: 129, of which 68 were waited for; matrix products, arithmetic and copies ran while one was open for 12% of the time, Pallas kernels for 33%

profile of v13, /device:TPU:0, one launch (start us, length us, event | category | flops | bytes accessed | tf_op | source)
XLA Modules:
  0.0 1630.5 jit_solution(3806831505364205147)
XLA Ops:
  11.2 25.0 %own_slices.1 = (bf16[2304,2304]{1,0:T(8,128)(2,1)}, bf16[2304,2304]{1,0:T(8,128)(2,1)}, bf16[2304,2304]{1,0:T(8,128)(2,1)}, bf16[2304,2304]{1,0:T(8,128)(2,1)},...) custom-call(s32[4]{0:T(128)} %pad_add_fusion.pieces, s32[4]{0:T(128)} %pad_add_fusion.1.info, ...), custom_call_target="tpu_custom_call" | custom-call | flops 159252480 | bytes 63700992 | tf_op jit(solution)/shard_map/own_slices/pallas_call | solution.py:303
  49.5 27.7 %collective-permute-done.3.refs_0_ = bf16[288,2560]{1,0:T(8,128)(2,1)} collective-permute-done((bf16[288,2560]{1,0:T(8,128)(2,1)S(1)}, bf16[288,2560]{1,0:T(8,128)(2,1)}, u32[]{:S(2)}, u32[]{:S(2)}) %collective-permute-start.3) | collective-permute-done | bytes 1474592 | tf_op jit(solution)/shard_map/ppermute | solution.py:102
  93.9 20.3 %collective-permute-done.7.refs_0_ = bf16[288,2560]{1,0:T(8,128)(2,1)S(1)} collective-permute-done((bf16[288,2560]{1,0:T(8,128)(2,1)}, bf16[288,2560]{1,0:T(8,128)(2,1)S(1)}, u32[]{:S(2)}, u32[]{:S(2)}) %collective-permute-start.7) | collective-permute-done | bytes 1474592 | tf_op jit(solution)/shard_map/ppermute | solution.py:102
  177.4 24.4 %collective-permute-done.15.refs_0_ = bf16[288,2304]{1,0:T(8,128)(2,1)} collective-permute-done((bf16[288,2304]{1,0:T(8,128)(2,1)}, bf16[288,2304]{1,0:T(8,128)(2,1)}, u32[]{:S(2)}, u32[]{:S(2)}) %collective-permute-start.15) | collective-permute-done | bytes 1327136 | tf_op jit(solution)/shard_map/ppermute | solution.py:157
  239.7 21.8 %collective-permute-done.17.refs_1_ = bf16[4,256,512]{2,1,0:T(8,128)(2,1)} collective-permute-done((bf16[4,256,512]{2,1,0:T(8,128)(2,1)S(1)}, bf16[4,256,512]{2,1,0:T(8,128)(2,1)}, u32[]{:S(2)}, u32[]{:S(2)}) %collective-permute-start.17) | collective-permute-done | bytes 1048608 | tf_op jit(solution)/shard_map/ppermute | solution.py:177
  270.0 20.5 %collective-permute-done.18 = bf16[2,256,512]{2,1,0:T(8,128)(2,1)S(1)} collective-permute-done((bf16[2,256,512]{2,1,0:T(8,128)(2,1)S(1)}, bf16[2,256,512]{2,1,0:T(8,128)(2,1)S(1)}, u32[]{:S(2)}, u32[]{:S(2)}) %collective-permute-start.18) | collective-permute-done | bytes 524320 | tf_op jit(solution)/shard_map/ppermute | solution.py:177
  309.5 12.0 collective-permute-done.20
  329.8 20.6 %out_slices.1 = (bf16[2304,2048]{1,0:T(8,128)(2,1)}, bf16[2304,2048]{1,0:T(8,128)(2,1)}) custom-call(s32[8]{0:T(128)} %stack.168.places, s32[4]{0:T(128)} %pad_add_fusion.1.info, bf16[8,288,512]{2,1,0:T(8,128)(2,1)} %copy-done.34, bf16[8,288,512]{2,1,0:T(8,128)(2,1)} %collective-permute-done.19.refs_1_, ...), custom_call_target="tpu_custom_call" | custom-call | flops 94371840 | bytes 28311552 | tf_op jit(solution)/shard_map/out_slices/pallas_call | solution.py:260
  370.6 13.1 join_rows.2
  405.1 13.2 join_rows.3
  418.3 33.9 %collective-permute-done.25.refs_0_ = bf16[288,2304]{1,0:T(8,128)(2,1)} collective-permute-done((bf16[288,2304]{1,0:T(8,128)(2,1)S(1)}, bf16[288,2304]{1,0:T(8,128)(2,1)}, u32[]{:S(2)}, u32[]{:S(2)}) %collective-permute-start.25) | collective-permute-done | bytes 1327136 | tf_op jit(solution)/shard_map/ppermute | solution.py:157
  452.6 30.8 %collective-permute-done.27.refs_1_ = bf16[288,2304]{1,0:T(8,128)(2,1)S(1)} collective-permute-done((bf16[288,2304]{1,0:T(8,128)(2,1)}, bf16[288,2304]{1,0:T(8,128)(2,1)S(1)}, u32[]{:S(2)}, u32[]{:S(2)}) %collective-permute-start.27) | collective-permute-done | bytes 1327136 | tf_op jit(solution)/shard_map/ppermute | solution.py:157
  483.5 28.5 %collective-permute-done.26.refs_0_ = bf16[288,2304]{1,0:T(8,128)(2,1)} collective-permute-done((bf16[288,2304]{1,0:T(8,128)(2,1)S(1)}, bf16[288,2304]{1,0:T(8,128)(2,1)}, u32[]{:S(2)}, u32[]{:S(2)}) %collective-permute-start.26) | collective-permute-done | bytes 1327136 | tf_op jit(solution)/shard_map/ppermute | solution.py:157
  516.2 26.3 %collective-permute-done.28 = bf16[256,2304]{1,0:T(8,128)(2,1)S(1)} collective-permute-done((bf16[256,2304]{1,0:T(8,128)(2,1)}, bf16[256,2304]{1,0:T(8,128)(2,1)S(1)}, u32[]{:S(2)}, u32[]{:S(2)}) %collective-permute-start.28) | collective-permute-done | bytes 1179680 | tf_op jit(solution)/shard_map/ppermute | solution.py:102
  570.0 29.0 %open_forward.3 = (f32[1024,2304]{1,0:T(8,128)}, f32[1024,2304]{1,0:T(8,128)}, bf16[1024,2304]{1,0:T(8,128)(2,1)}) custom-call(bf16[1024,2304]{1,0:T(8,128)(2,1)} %constant_dynamic-update-slice_fusion.6.refs_0_.refs_2_, bf16[2304,2304]{1,0:T(8,128)(2,1)} %get-tuple-element.681.refs_1_.refs_2_, bf16[2304,2304]{1,0:T(8,128)(2,1)} %get-tuple-element.682.refs_2_.refs_3_), custom_call_target="tpu_custom_call" | custom-call | flops 21743271936 | bytes 49545216 | tf_op jit(solution)/shard_map/open_forward/pallas_call | solution.py:454
  615.9 14.9 convolution_convert_fusion.3.part_ref
  635.6 18.2 %open_forward.4 = (f32[1024,2304]{1,0:T(8,128)}, f32[1024,2304]{1,0:T(8,128)}, bf16[1024,2304]{1,0:T(8,128)(2,1)}) custom-call(bf16[1024,2304]{1,0:T(8,128)(2,1)} %constant_dynamic-update-slice_fusion.11.refs_0_.refs_3_, bf16[2304,2304]{1,0:T(8,128)(2,1)} %get-tuple-element.711.refs_1_.refs_2_, bf16[2304,2304]{1,0:T(8,128)(2,1)} %get-tuple-element.712.refs_2_.refs_3_), custom_call_target="tpu_custom_call" | custom-call | flops 12079595520 | bytes 29622272 | tf_op jit(solution)/shard_map/open_forward/pallas_call | solution.py:454
  658.7 15.5 open_forward.5
  689.4 13.5 convolution_convert_fusion.2.part_ref
  731.9 14.9 open_back.4
  750.7 12.8 open_back.5
  763.4 18.5 %input_back.4.refs_4_ = bf16[1024,2304]{1,0:T(8,128)(2,1)} custom-call(bf16[1024,2304]{1,0:T(8,128)(2,1)} %get-tuple-element.888.refs_0_, bf16[1024,2304]{1,0:T(8,128)(2,1)} %get-tuple-element.864.refs_1_.refs_0_, bf16[2304,2304]{1,0:T(8,128)(2,1)} %get-tuple-element.681.refs_1_.refs_2_, bf16[2304,2304]{1,0:T(8,128)(2,1)} %get-tuple-element.682.refs_2_.refs_3_), custom_call_target="tpu_custom_call" | custom-call | flops 12079595520 | bytes 23855104 | tf_op jit(solution)/shard_map/input_back/pallas_call | solution.py:511
  794.1 15.8 input_back.5.part_ref
  817.2 13.6 collective-permute-done.55
  836.0 14.9 open_back.6
  853.7 12.7 open_back.7
  866.5 18.4 %input_back.6.refs_4_ = bf16[1024,2304]{1,0:T(8,128)(2,1)} custom-call(bf16[1024,2304]{1,0:T(8,128)(2,1)} %get-tuple-element.889.refs_0_.refs_1_, bf16[1024,2304]{1,0:T(8,128)(2,1)} %get-tuple-element.865.refs_1_, bf16[2304,2304]{1,0:T(8,128)(2,1)} %get-tuple-element.711.refs_1_.refs_2_, bf16[2304,2304]{1,0:T(8,128)(2,1)} %get-tuple-element.712.refs_2_.refs_3_), custom_call_target="tpu_custom_call" | custom-call | flops 12079595520 | bytes 23855104 | tf_op jit(solution)/shard_map/input_back/pallas_call | solution.py:511
  884.9 16.6 %input_back.7.part_ref = bf16[1024,2304]{1,0:T(8,128)(2,1)} custom-call(bf16[1024,2304]{1,0:T(8,128)(2,1)} %get-tuple-element.889.refs_0_.refs_1_, bf16[1024,2304]{1,0:T(8,128)(2,1)} %get-tuple-element.865.refs_1_, bf16[2304,2304]{1,0:T(8,128)(2,1)} %get-tuple-element.711.refs_1_.refs_2_, ...), custom_call_target="tpu_custom_call", output_to_operand_aliasing={{}: (4, {})} | custom-call | flops 9663676416 | bytes 20971520 | tf_op jit(solution)/shard_map/input_back/pallas_call | solution.py:511
  905.0 13.3 branch_back.2
  922.6 30.3 %weight_back.3 = (bf16[1152,2304]{1,0:T(8,128)(2,1)}, bf16[1152,2304]{1,0:T(8,128)(2,1)}) custom-call(bf16[1024,2304]{1,0:T(8,128)(2,1)} %get-tuple-element.808.refs_0_, bf16[1024,2304]{1,0:T(8,128)(2,1)} %get-tuple-element.809.refs_1_, bf16[1024,2304]{1,0:T(8,128)(2,1)} %copy-done.3, bf16[1024,2304]{1,0:T(8,128)(2,1)} %constant_dynamic-update-slice_fusion.21.refs_0_.refs_3_), custom_call_target="tpu_custom_call" | custom-call | flops 21743271936 | bytes 29491200 | tf_op jit(solution)/shard_map/weight_back/pallas_call | solution.py:554
  961.4 13.3 branch_back.3
  1001.2 17.4 %attn_backward.2 = (bf16[1024,512]{1,0:T(8,128)(2,1)}, bf16[4,256,512]{2,1,0:T(8,128)(2,1)}, bf16[4,256,512]{2,1,0:T(8,128)(2,1)}) custom-call(s32[1]{0:T(128)} %bitcast.41.info, bf16[1024,512]{1,0:T(8,128)(2,1)} %bitcast.228, bf16[1024,512]{1,0:T(8,128)(2,1)} %bitcast.234, f32[1024,512]{1,0:T(8,128)} %get-tuple-element.835.exact_ref, ...), custom_call_target="tpu_custom_call" | custom-call | flops 10737418240 | bytes 9437184 | tf_op jit(solution)/shard_map/attn_backward/pallas_call | solution.py:1029
  1029.5 17.4 %attn_backward.3 = (bf16[1024,512]{1,0:T(8,128)(2,1)}, bf16[4,256,512]{2,1,0:T(8,128)(2,1)}, bf16[4,256,512]{2,1,0:T(8,128)(2,1)}) custom-call(s32[1]{0:T(128)} %bitcast.41.info, bf16[1024,512]{1,0:T(8,128)(2,1)} %bitcast.226, bf16[1024,512]{1,0:T(8,128)(2,1)} %bitcast.62.grad_ref, f32[1024,512]{1,0:T(8,128)} %get-tuple-element.852.exact_ref, ...), custom_call_target="tpu_custom_call" | custom-call | flops 10737418240 | bytes 9437184 | tf_op jit(solution)/shard_map/attn_backward/pallas_call | solution.py:1029
  1072.2 30.5 %weight_back.4 = (bf16[1152,2304]{1,0:T(8,128)(2,1)}, bf16[1152,2304]{1,0:T(8,128)(2,1)}) custom-call(bf16[1024,2304]{1,0:T(8,128)(2,1)} %get-tuple-element.864.refs_1_.refs_0_, bf16[1024,2304]{1,0:T(8,128)(2,1)} %get-tuple-element.865.refs_1_, bf16[1024,2304]{1,0:T(8,128)(2,1)} %constant_dynamic-update-slice_fusion.6.refs_0_.refs_2_, ...), custom_call_target="tpu_custom_call" | custom-call | flops 21743271936 | bytes 29491200 | tf_op jit(solution)/shard_map/weight_back/pallas_call | solution.py:554
  1118.0 16.0 collective-permute-done.72
  1154.9 30.6 %weight_back.5 = (bf16[1152,2304]{1,0:T(8,128)(2,1)}, bf16[1152,2304]{1,0:T(8,128)(2,1)}) custom-call(bf16[1024,2304]{1,0:T(8,128)(2,1)} %get-tuple-element.888.refs_0_, bf16[1024,2304]{1,0:T(8,128)(2,1)} %get-tuple-element.889.refs_0_.refs_1_, bf16[1024,2304]{1,0:T(8,128)(2,1)} %constant_dynamic-update-slice_fusion.6.refs_0_.refs_2_, ...), custom_call_target="tpu_custom_call" | custom-call | flops 21743271936 | bytes 29491200 | tf_op jit(solution)/shard_map/weight_back/pallas_call | solution.py:554
  1193.4 13.0 turn_back.1
  1220.5 12.7 collective-permute-done.77
  1250.5 11.8 collective-permute-done.80
  1277.2 16.3 collective-permute-done.82
  1307.5 25.5 %collective-permute-done.86 = bf16[2,288,1152]{2,1,0:T(8,128)(2,1)} collective-permute-done((bf16[2,288,1152]{2,1,0:T(8,128)(2,1)}, bf16[2,288,1152]{2,1,0:T(8,128)(2,1)}, u32[]{:S(2)}, u32[]{:S(2)}) %collective-permute-start.86) | collective-permute-done | bytes 1327136 | tf_op jit(solution)/shard_map/ppermute | solution.py:157
  1347.9 25.1 %collective-permute-done.89 = bf16[2,288,1152]{2,1,0:T(8,128)(2,1)S(1)} collective-permute-done((bf16[2,288,1152]{2,1,0:T(8,128)(2,1)S(1)}, bf16[2,288,1152]{2,1,0:T(8,128)(2,1)S(1)}, u32[]{:S(2)}, u32[]{:S(2)}) %collective-permute-start.89) | collective-permute-done | bytes 1327136 | tf_op jit(solution)/shard_map/ppermute | solution.py:157
  1410.5 20.8 %fusion.44 = f32[256,2304]{1,0:T(8,128)} fusion(bf16[256,4096]{1,0:T(8,128)(2,1)} %get-tuple-element.960, bf16[2304,4096]{1,0:T(8,128)(2,1)} %get-tuple-element.556.wq_ref.wk_ref.wv_ref), kind=kOutput, calls=%fused_computation.255 | convolution fusion | flops 4831838208 | bytes 23330816 | tf_op jit(solution)/shard_map/dot_general | solution.py:26
  1438.1 21.0 %collective-permute-done.95 = bf16[288,1152]{1,0:T(8,128)(2,1)S(1)} collective-permute-done((bf16[288,1152]{1,0:T(8,128)(2,1)}, bf16[288,1152]{1,0:T(8,128)(2,1)S(1)}, u32[]{:S(2)}, u32[]{:S(2)}) %collective-permute-start.95) | collective-permute-done | bytes 663584 | tf_op jit(solution)/shard_map/ppermute | solution.py:157
  1473.9 17.2 %collective-permute-done.96 = bf16[288,1152]{1,0:T(8,128)(2,1)} collective-permute-done((bf16[288,1152]{1,0:T(8,128)(2,1)}, bf16[288,1152]{1,0:T(8,128)(2,1)}, u32[]{:S(2)}, u32[]{:S(2)}) %collective-permute-start.96) | collective-permute-done | bytes 663584 | tf_op jit(solution)/shard_map/ppermute | solution.py:157
  1516.7 12.3 collective-permute-done.106
  1529.1 12.1 collective-permute-done.105
  1583.0 14.2 collective-permute-done.107
  (692 shorter events, 709.4 us)
Async XLA Ops:
  3.8 38.4 %collective-permute-start = (bf16[288,2560]{1,0:T(8,128)(2,1)S(1)}, bf16[288,2560]{1,0:T(8,128)(2,1)S(1)}, u32[]{:S(2)}, u32[]{:S(2)}) collective-permute-start(bf16[288,2560]{1,0:T(8,128)(2,1)S(1)} %pad_maximum_fusion.10.refs_0_), channel_id=1, source_target_pairs={{0,8},{8,16},{16,24},{24,28},{28,20},{20,12},{12,4},{4,0},{1,9},{9... | collective-permute-start | bytes 4423688 | tf_op jit(solution)/shard_map/ppermute | solution.py:102
  6.9 35.3 %collective-permute-start.1 = (bf16[288,2560]{1,0:T(8,128)(2,1)S(1)}, bf16[288,2560]{1,0:T(8,128)(2,1)}, u32[]{:S(2)}, u32[]{:S(2)}) collective-permute-start(bf16[288,2560]{1,0:T(8,128)(2,1)S(1)} %pad_maximum_fusion.10.refs_0_), channel_id=1, source_target_pairs={{8,0},{16,8},{24,16},{28,24},{20,28},{12,20},{4,12},{0,4},{9,1},{1... | collective-permute-start | bytes 4423688 | tf_op jit(solution)/shard_map/ppermute | solution.py:102
  6.9 35.3 %collective-permute-start.2 = (bf16[288,2560]{1,0:T(8,128)(2,1)S(1)}, bf16[288,2560]{1,0:T(8,128)(2,1)}, u32[]{:S(2)}, u32[]{:S(2)}) collective-permute-start(bf16[288,2560]{1,0:T(8,128)(2,1)S(1)} %pad_maximum_fusion.10.refs_0_), channel_id=1, source_target_pairs={{0,1},{1,0},{2,3},{3,2},{4,5},{5,4},{6,7},{7,6},{8,9},{9,8},{10,11... | collective-permute-start | bytes 4423688 | tf_op jit(solution)/shard_map/ppermute | solution.py:157
  42.2 35.0 %collective-permute-start.3 = (bf16[288,2560]{1,0:T(8,128)(2,1)S(1)}, bf16[288,2560]{1,0:T(8,128)(2,1)}, u32[]{:S(2)}, u32[]{:S(2)}) collective-permute-start(bf16[288,2560]{1,0:T(8,128)(2,1)S(1)} %collective-permute-done.refs_2_), channel_id=1, source_target_pairs={{0,8},{8,16},{16,24},{24,28},{28,20},{20,12},{12,4},{4,0},{1,9},{9... | collective-permute-start | bytes 4423688 | tf_op jit(solution)/shard_map/ppermute | solution.py:102
  44.2 35.0 %collective-permute-start.5 = (bf16[288,2560]{1,0:T(8,128)(2,1)S(1)}, bf16[288,2560]{1,0:T(8,128)(2,1)S(1)}, u32[]{:S(2)}, u32[]{:S(2)}) collective-permute-start(bf16[288,2560]{1,0:T(8,128)(2,1)S(1)} %collective-permute-done.refs_2_), channel_id=1, source_target_pairs={{0,1},{1,0},{2,3},{3,2},{4,5},{5,4},{6,7},{7,6},{8,9},{9,8},{10,11... | collective-permute-start | bytes 4423688 | tf_op jit(solution)/shard_map/ppermute | solution.py:157
  44.5 34.8 %collective-permute-start.4 = (bf16[288,2560]{1,0:T(8,128)(2,1)}, bf16[288,2560]{1,0:T(8,128)(2,1)}, u32[]{:S(2)}, u32[]{:S(2)}) collective-permute-start(bf16[288,2560]{1,0:T(8,128)(2,1)} %collective-permute-done.1.refs_4_), channel_id=1, source_target_pairs={{8,0},{16,8},{24,16},{28,24},{20,28},{12,20},{4,12},{0,4},{9,1},{1... | collective-permute-start | bytes 4423688 | tf_op jit(solution)/shard_map/ppermute | solution.py:102
  44.7 34.5 %collective-permute-start.6 = (bf16[288,2560]{1,0:T(8,128)(2,1)}, bf16[288,2560]{1,0:T(8,128)(2,1)S(1)}, u32[]{:S(2)}, u32[]{:S(2)}) collective-permute-start(bf16[288,2560]{1,0:T(8,128)(2,1)} %collective-permute-done.1.refs_4_), channel_id=1, source_target_pairs={{0,1},{1,0},{2,3},{3,2},{4,5},{5,4},{6,7},{7,6},{8,9},{9,8},{10,11... | collective-permute-start | bytes 4423688 | tf_op jit(solution)/shard_map/ppermute | solution.py:157
  80.4 33.9 %collective-permute-start.7 = (bf16[288,2560]{1,0:T(8,128)(2,1)}, bf16[288,2560]{1,0:T(8,128)(2,1)S(1)}, u32[]{:S(2)}, u32[]{:S(2)}) collective-permute-start(bf16[288,2560]{1,0:T(8,128)(2,1)} %collective-permute-done.3.refs_0_), channel_id=1, source_target_pairs={{0,8},{8,16},{16,24},{24,28},{28,20},{20,12},{12,4},{4,0},{1,9},{9... | collective-permute-start | bytes 4423688 | tf_op jit(solution)/shard_map/ppermute | solution.py:102
  82.0 33.8 %collective-permute-start.8 = (bf16[288,2560]{1,0:T(8,128)(2,1)}, bf16[288,2560]{1,0:T(8,128)(2,1)S(1)}, u32[]{:S(2)}, u32[]{:S(2)}) collective-permute-start(bf16[288,2560]{1,0:T(8,128)(2,1)} %collective-permute-done.4.refs_2_), channel_id=1, source_target_pairs={{8,0},{16,8},{24,16},{28,24},{20,28},{12,20},{4,12},{0,4},{9,1},{1... | collective-permute-start | bytes 4423688 | tf_op jit(solution)/shard_map/ppermute | solution.py:102
  82.6 33.2 %collective-permute-start.9 = (bf16[288,2560]{1,0:T(8,128)(2,1)}, bf16[288,2560]{1,0:T(8,128)(2,1)}, u32[]{:S(2)}, u32[]{:S(2)}) collective-permute-start(bf16[288,2560]{1,0:T(8,128)(2,1)} %collective-permute-done.3.refs_0_), channel_id=1, source_target_pairs={{0,1},{1,0},{2,3},{3,2},{4,5},{5,4},{6,7},{7,6},{8,9},{9,8},{10,11... | collective-permute-start | bytes 4423688 | tf_op jit(solution)/shard_map/ppermute | solution.py:157
  140.7 61.1 %collective-permute-start.15 = (bf16[288,2304]{1,0:T(8,128)(2,1)}, bf16[288,2304]{1,0:T(8,128)(2,1)}, u32[]{:S(2)}, u32[]{:S(2)}) collective-permute-start(bf16[288,2304]{1,0:T(8,128)(2,1)} %get-tuple-element.548), channel_id=1, source_target_pairs={{0,16},{4,20},{8,24},{12,28},{16,0},{20,4},{24,8},{28,12},{1,17},{... | collective-permute-start | bytes 3981320 | tf_op jit(solution)/shard_map/ppermute | solution.py:157
  238.1 53.2 %collective-permute-start.19 = (bf16[8,288,512]{2,1,0:T(8,128)(2,1)}, bf16[8,288,512]{2,1,0:T(8,128)(2,1)}, u32[]{:S(2)}, u32[]{:S(2)}) collective-permute-start(bf16[8,288,512]{2,1,0:T(8,128)(2,1)} %copy-done.34), channel_id=1, source_target_pairs={{0,2},{1,3},{2,0},{3,1},{4,6},{5,7},{6,4},{7,5},{8,10},{9,11},{10,... | collective-permute-start | bytes 7077896 | tf_op jit(solution)/shard_map/ppermute | solution.py:157
  322.5 40.3 %all-to-all-start.4 = ((bf16[8,128,512]{2,1,0:T(8,128)(2,1)}), bf16[8,128,512]{2,1,0:T(8,128)(2,1)S(1)}, u32[]{:S(2)}, u32[]{:S(2)}) async-start(bf16[8,128,512]{2,1,0:T(8,128)(2,1)} %bitcast.236), calls=%async_computation.4 | async-start | bytes 2097152 | tf_op jit(solution)/shard_map/all_to_all | solution.py:161
  326.2 36.6 %collective-permute-start.22 = (bf16[288,2304]{1,0:T(8,128)(2,1)}, bf16[288,2304]{1,0:T(8,128)(2,1)}, u32[]{:S(2)}, u32[]{:S(2)}) collective-permute-start(bf16[288,2304]{1,0:T(8,128)(2,1)} %collective-permute-done.15.refs_0_), channel_id=1, source_target_pairs={{0,2},{1,3},{2,0},{3,1},{4,6},{5,7},{6,4},{7,5},{8,10},{9,11},{10,... | collective-permute-start | bytes 3981320 | tf_op jit(solution)/shard_map/ppermute | solution.py:157
  362.9 31.3 %all-to-all-start.5 = ((bf16[8,128,512]{2,1,0:T(8,128)(2,1)}), bf16[8,128,512]{2,1,0:T(8,128)(2,1)S(1)}, u32[]{:S(2)}, u32[]{:S(2)}) async-start(bf16[8,128,512]{2,1,0:T(8,128)(2,1)} %bitcast.237), calls=%async_computation.5 | async-start | bytes 2097152 | tf_op jit(solution)/shard_map/all_to_all | solution.py:161
  394.2 58.1 %collective-permute-start.25 = (bf16[288,2304]{1,0:T(8,128)(2,1)S(1)}, bf16[288,2304]{1,0:T(8,128)(2,1)}, u32[]{:S(2)}, u32[]{:S(2)}) collective-permute-start(bf16[288,2304]{1,0:T(8,128)(2,1)S(1)} %copy-done.46), channel_id=1, source_target_pairs={{0,16},{4,20},{8,24},{12,28},{16,0},{20,4},{24,8},{28,12},{1,17},{... | collective-permute-start | bytes 3981320 | tf_op jit(solution)/shard_map/ppermute | solution.py:157
  452.2 31.3 %collective-permute-start.27 = (bf16[288,2304]{1,0:T(8,128)(2,1)}, bf16[288,2304]{1,0:T(8,128)(2,1)S(1)}, u32[]{:S(2)}, u32[]{:S(2)}) collective-permute-start(bf16[288,2304]{1,0:T(8,128)(2,1)} %collective-permute-done.25.refs_0_), channel_id=1, source_target_pairs={{0,2},{1,3},{2,0},{3,1},{4,6},{5,7},{6,4},{7,5},{8,10},{9,11},{10,... | collective-permute-start | bytes 3981320 | tf_op jit(solution)/shard_map/ppermute | solution.py:157
  452.6 59.3 %collective-permute-start.26 = (bf16[288,2304]{1,0:T(8,128)(2,1)S(1)}, bf16[288,2304]{1,0:T(8,128)(2,1)}, u32[]{:S(2)}, u32[]{:S(2)}) collective-permute-start(bf16[288,2304]{1,0:T(8,128)(2,1)S(1)} %copy-done.45), channel_id=1, source_target_pairs={{0,16},{4,20},{8,24},{12,28},{16,0},{20,4},{24,8},{28,12},{1,17},{... | collective-permute-start | bytes 3981320 | tf_op jit(solution)/shard_map/ppermute | solution.py:157
  511.9 31.4 %collective-permute-start.32 = (bf16[288,2304]{1,0:T(8,128)(2,1)}, bf16[288,2304]{1,0:T(8,128)(2,1)}, u32[]{:S(2)}, u32[]{:S(2)}) collective-permute-start(bf16[288,2304]{1,0:T(8,128)(2,1)} %collective-permute-done.26.refs_0_), channel_id=1, source_target_pairs={{0,2},{1,3},{2,0},{3,1},{4,6},{5,7},{6,4},{7,5},{8,10},{9,11},{10,... | collective-permute-start | bytes 3981320 | tf_op jit(solution)/shard_map/ppermute | solution.py:157
  566.2 34.0 %collective-permute-start.37 = (bf16[256,2304]{1,0:T(8,128)(2,1)S(1)}, bf16[256,2304]{1,0:T(8,128)(2,1)S(1)}, u32[]{:S(2)}, u32[]{:S(2)}) collective-permute-start(bf16[256,2304]{1,0:T(8,128)(2,1)S(1)} %copy-done.59), channel_id=1, source_target_pairs={{0,8},{8,12},{12,4},{4,0},{16,24},{24,28},{28,20},{20,16},{1,9},{9... | collective-permute-start | bytes 3538952 | tf_op jit(solution)/shard_map/ppermute | solution.py:102
  568.0 32.2 %collective-permute-start.38 = (bf16[256,2304]{1,0:T(8,128)(2,1)S(1)}, bf16[256,2304]{1,0:T(8,128)(2,1)S(1)}, u32[]{:S(2)}, u32[]{:S(2)}) collective-permute-start(bf16[256,2304]{1,0:T(8,128)(2,1)S(1)} %copy-done.59), channel_id=1, source_target_pairs={{8,0},{12,8},{4,12},{0,4},{24,16},{28,24},{20,28},{16,20},{9,1},{1... | collective-permute-start | bytes 3538952 | tf_op jit(solution)/shard_map/ppermute | solution.py:102
  748.5 33.4 %collective-permute-start.52 = (bf16[256,2304]{1,0:T(8,128)(2,1)S(1)}, bf16[256,2304]{1,0:T(8,128)(2,1)S(1)}, u32[]{:S(2)}, u32[]{:S(2)}) collective-permute-start(bf16[256,2304]{1,0:T(8,128)(2,1)S(1)} %pad_maximum_fusion.20), channel_id=1, source_target_pairs={{8,0},{12,8},{4,12},{0,4},{24,16},{28,24},{20,28},{16,20},{9,1},{1... | collective-permute-start | bytes 3538952 | tf_op jit(solution)/shard_map/ppermute | solution.py:102
  750.1 31.8 %collective-permute-start.51 = (bf16[256,2304]{1,0:T(8,128)(2,1)S(1)}, bf16[256,2304]{1,0:T(8,128)(2,1)S(1)}, u32[]{:S(2)}, u32[]{:S(2)}) collective-permute-start(bf16[256,2304]{1,0:T(8,128)(2,1)S(1)} %pad_maximum_fusion.19), channel_id=1, source_target_pairs={{0,8},{8,12},{12,4},{4,0},{16,24},{24,28},{28,20},{20,16},{1,9},{9... | collective-permute-start | bytes 3538952 | tf_op jit(solution)/shard_map/ppermute | solution.py:102
  851.3 33.5 %collective-permute-start.60 = (bf16[256,2304]{1,0:T(8,128)(2,1)S(1)}, bf16[256,2304]{1,0:T(8,128)(2,1)S(1)}, u32[]{:S(2)}, u32[]{:S(2)}) collective-permute-start(bf16[256,2304]{1,0:T(8,128)(2,1)S(1)} %pad_maximum_fusion.22), channel_id=1, source_target_pairs={{8,0},{12,8},{4,12},{0,4},{24,16},{28,24},{20,28},{16,20},{9,1},{1... | collective-permute-start | bytes 3538952 | tf_op jit(solution)/shard_map/ppermute | solution.py:102
  852.1 32.8 %collective-permute-start.59 = (bf16[256,2304]{1,0:T(8,128)(2,1)S(1)}, bf16[256,2304]{1,0:T(8,128)(2,1)S(1)}, u32[]{:S(2)}, u32[]{:S(2)}) collective-permute-start(bf16[256,2304]{1,0:T(8,128)(2,1)S(1)} %pad_maximum_fusion.21), channel_id=1, source_target_pairs={{0,8},{8,12},{12,4},{4,0},{16,24},{24,28},{28,20},{20,16},{1,9},{9... | collective-permute-start | bytes 3538952 | tf_op jit(solution)/shard_map/ppermute | solution.py:102
  920.2 32.8 %collective-permute-start.64 = (bf16[256,2304]{1,0:T(8,128)(2,1)S(1)}, bf16[256,2304]{1,0:T(8,128)(2,1)S(1)}, u32[]{:S(2)}, u32[]{:S(2)}) collective-permute-start(bf16[256,2304]{1,0:T(8,128)(2,1)S(1)} %pad_maximum_fusion.24), channel_id=1, source_target_pairs={{8,0},{12,8},{4,12},{0,4},{24,16},{28,24},{20,28},{16,20},{9,1},{1... | collective-permute-start | bytes 3538952 | tf_op jit(solution)/shard_map/ppermute | solution.py:102
  921.8 31.2 %collective-permute-start.63 = (bf16[256,2304]{1,0:T(8,128)(2,1)S(1)}, bf16[256,2304]{1,0:T(8,128)(2,1)}, u32[]{:S(2)}, u32[]{:S(2)}) collective-permute-start(bf16[256,2304]{1,0:T(8,128)(2,1)S(1)} %pad_maximum_fusion.23), channel_id=1, source_target_pairs={{0,8},{8,12},{12,4},{4,0},{16,24},{24,28},{28,20},{20,16},{1,9},{9... | collective-permute-start | bytes 3538952 | tf_op jit(solution)/shard_map/ppermute | solution.py:102
  1020.7 40.5 %all-to-all-start.8 = ((bf16[8,128,512]{2,1,0:T(8,128)(2,1)}), bf16[8,128,512]{2,1,0:T(8,128)(2,1)S(1)}, u32[]{:S(2)}, u32[]{:S(2)}) async-start(bf16[8,128,512]{2,1,0:T(8,128)(2,1)} %bitcast.232), calls=%async_computation.8 | async-start | bytes 2097152 | tf_op jit(solution)/shard_map/all_to_all | solution.py:161
  1025.5 35.7 %collective-permute-start.68 = (bf16[2,288,1152]{2,1,0:T(8,128)(2,1)}, bf16[2,288,1152]{2,1,0:T(8,128)(2,1)}, u32[]{:S(2)}, u32[]{:S(2)}) collective-permute-start(bf16[2,288,1152]{2,1,0:T(8,128)(2,1)} %get-tuple-element.845), channel_id=1, source_target_pairs={{0,2},{1,3},{2,0},{3,1},{4,6},{5,7},{6,4},{7,5},{8,10},{9,11},{10,... | collective-permute-start | bytes 3981320 | tf_op jit(solution)/shard_map/ppermute | solution.py:157
  1064.6 43.1 %collective-permute-start.71 = (bf16[2304,256]{1,0:T(8,128)(2,1)}, bf16[2304,256]{1,0:T(8,128)(2,1)}, u32[]{:S(2)}, u32[]{:S(2)}) collective-permute-start(bf16[2304,256]{1,0:T(8,128)(2,1)} %slice.482), channel_id=1, source_target_pairs={{0,2},{1,3},{2,0},{3,1},{4,6},{5,7},{6,4},{7,5},{8,10},{9,11},{10,... | collective-permute-start | bytes 3538952 | tf_op jit(solution)/shard_map/ppermute | solution.py:157
  1065.7 40.8 %collective-permute-start.70 = (bf16[2,256,512]{2,1,0:T(8,128)(2,1)}, bf16[2,256,512]{2,1,0:T(8,128)(2,1)}, u32[]{:S(2)}, u32[]{:S(2)}) collective-permute-start(bf16[2,256,512]{2,1,0:T(8,128)(2,1)} %get-tuple-element.861), channel_id=1, source_target_pairs={{0,4},{4,0},{8,12},{12,8},{16,20},{20,16},{24,28},{28,24},{1,5},{5... | collective-permute-start | bytes 1572872 | tf_op jit(solution)/shard_map/ppermute | solution.py:177
  1065.8 41.9 %all-to-all-start.9 = ((bf16[8,128,512]{2,1,0:T(8,128)(2,1)}), bf16[8,128,512]{2,1,0:T(8,128)(2,1)S(1)}, u32[]{:S(2)}, u32[]{:S(2)}) async-start(bf16[8,128,512]{2,1,0:T(8,128)(2,1)} %bitcast.233), calls=%async_computation.9 | async-start | bytes 2097152 | tf_op jit(solution)/shard_map/all_to_all | solution.py:161
  1111.0 34.0 %all-to-all-start.10 = ((bf16[4,256,512]{2,1,0:T(8,128)(2,1)}), bf16[4,256,512]{2,1,0:T(8,128)(2,1)S(1)}, u32[]{:S(2)}, u32[]{:S(2)}) async-start(bf16[4,256,512]{2,1,0:T(8,128)(2,1)} %pad_maximum_fusion.25), calls=%async_computation.10 | async-start | bytes 2097152 | tf_op jit(solution)/shard_map/all_to_all | solution.py:168
  1149.0 36.5 %collective-permute-start.75 = (bf16[2,288,1152]{2,1,0:T(8,128)(2,1)}, bf16[2,288,1152]{2,1,0:T(8,128)(2,1)}, u32[]{:S(2)}, u32[]{:S(2)}) collective-permute-start(bf16[2,288,1152]{2,1,0:T(8,128)(2,1)} %get-tuple-element.887), channel_id=1, source_target_pairs={{0,2},{1,3},{2,0},{3,1},{4,6},{5,7},{6,4},{7,5},{8,10},{9,11},{10,... | collective-permute-start | bytes 3981320 | tf_op jit(solution)/shard_map/ppermute | solution.py:157
  1149.9 35.6 %all-to-all-start.11 = ((bf16[4,256,512]{2,1,0:T(8,128)(2,1)}), bf16[4,256,512]{2,1,0:T(8,128)(2,1)}, u32[]{:S(2)}, u32[]{:S(2)}) async-start(bf16[4,256,512]{2,1,0:T(8,128)(2,1)} %add_convert_fusion.13), calls=%async_computation.11 | async-start | bytes 2097152 | tf_op jit(solution)/shard_map/all_to_all | solution.py:168
  1185.5 48.9 %collective-permute-start.78 = (bf16[2,576,2304]{2,1,0:T(8,128)(2,1)}, bf16[2,576,2304]{2,1,0:T(8,128)(2,1)}, u32[]{:S(2)}, u32[]{:S(2)}) collective-permute-start(bf16[2,576,2304]{2,1,0:T(8,128)(2,1)} %bitcast.248), channel_id=1, source_target_pairs={{0,1},{1,0},{2,3},{3,2},{4,5},{5,4},{6,7},{7,6},{8,9},{9,8},{10,11... | collective-permute-start | bytes 15925256 | tf_op jit(solution)/shard_map/ppermute | solution.py:157
  1190.7 42.6 %collective-permute-start.79 = (bf16[2,288,1152]{2,1,0:T(8,128)(2,1)S(1)}, bf16[2,288,1152]{2,1,0:T(8,128)(2,1)S(1)}, u32[]{:S(2)}, u32[]{:S(2)}) collective-permute-start(bf16[2,288,1152]{2,1,0:T(8,128)(2,1)S(1)} %copy-done.44), channel_id=1, source_target_pairs={{0,2},{1,3},{2,0},{3,1},{4,6},{5,7},{6,4},{7,5},{8,10},{9,11},{10,... | collective-permute-start | bytes 3981320 | tf_op jit(solution)/shard_map/ppermute | solution.py:157
  1297.9 35.2 %collective-permute-start.85 = (bf16[288,2560]{1,0:T(8,128)(2,1)}, bf16[288,2560]{1,0:T(8,128)(2,1)}, u32[]{:S(2)}, u32[]{:S(2)}) collective-permute-start(bf16[288,2560]{1,0:T(8,128)(2,1)} %pad_maximum_fusion.12), channel_id=1, source_target_pairs={{8,0},{16,8},{24,16},{28,24},{20,28},{12,20},{4,12},{0,4},{9,1},{1... | collective-permute-start | bytes 4423688 | tf_op jit(solution)/shard_map/ppermute | solution.py:102
  1301.1 33.1 %collective-permute-start.84 = (bf16[288,2560]{1,0:T(8,128)(2,1)}, bf16[288,2560]{1,0:T(8,128)(2,1)}, u32[]{:S(2)}, u32[]{:S(2)}) collective-permute-start(bf16[288,2560]{1,0:T(8,128)(2,1)} %fusion.8), channel_id=1, source_target_pairs={{0,8},{8,16},{16,24},{24,28},{28,20},{20,12},{12,4},{4,0},{1,9},{9... | collective-permute-start | bytes 4423688 | tf_op jit(solution)/shard_map/ppermute | solution.py:102
  1338.0 35.0 %collective-permute-start.88 = (bf16[288,2560]{1,0:T(8,128)(2,1)S(1)}, bf16[288,2560]{1,0:T(8,128)(2,1)S(1)}, u32[]{:S(2)}, u32[]{:S(2)}) collective-permute-start(bf16[288,2560]{1,0:T(8,128)(2,1)S(1)} %add_convert_fusion.8), channel_id=1, source_target_pairs={{8,0},{16,8},{24,16},{28,24},{20,28},{12,20},{4,12},{0,4},{9,1},{1... | collective-permute-start | bytes 4423688 | tf_op jit(solution)/shard_map/ppermute | solution.py:102
  1341.0 32.0 %collective-permute-start.87 = (bf16[288,2560]{1,0:T(8,128)(2,1)S(1)}, bf16[288,2560]{1,0:T(8,128)(2,1)S(1)}, u32[]{:S(2)}, u32[]{:S(2)}) collective-permute-start(bf16[288,2560]{1,0:T(8,128)(2,1)S(1)} %add_convert_fusion.9), channel_id=1, source_target_pairs={{0,8},{8,16},{16,24},{24,28},{28,20},{20,12},{12,4},{4,0},{1,9},{9... | collective-permute-start | bytes 4423688 | tf_op jit(solution)/shard_map/ppermute | solution.py:102
  1375.3 31.0 %collective-permute-start.91 = (bf16[288,2560]{1,0:T(8,128)(2,1)S(1)}, bf16[288,2560]{1,0:T(8,128)(2,1)S(1)}, u32[]{:S(2)}, u32[]{:S(2)}) collective-permute-start(bf16[288,2560]{1,0:T(8,128)(2,1)S(1)} %add_convert_fusion.6), channel_id=1, source_target_pairs={{8,0},{16,8},{24,16},{28,24},{20,28},{12,20},{4,12},{0,4},{9,1},{1... | collective-permute-start | bytes 4423688 | tf_op jit(solution)/shard_map/ppermute | solution.py:102
  1376.6 30.8 %collective-permute-start.90 = (bf16[288,2560]{1,0:T(8,128)(2,1)S(1)}, bf16[288,2560]{1,0:T(8,128)(2,1)S(1)}, u32[]{:S(2)}, u32[]{:S(2)}) collective-permute-start(bf16[288,2560]{1,0:T(8,128)(2,1)S(1)} %add_convert_fusion.7), channel_id=1, source_target_pairs={{0,8},{8,16},{16,24},{24,28},{28,20},{20,12},{12,4},{4,0},{1,9},{9... | collective-permute-start | bytes 4423688 | tf_op jit(solution)/shard_map/ppermute | solution.py:102
  1432.9 37.4 %collective-permute-start.97 = (bf16[288,2560]{1,0:T(8,128)(2,1)}, bf16[288,2560]{1,0:T(8,128)(2,1)}, u32[]{:S(2)}, u32[]{:S(2)}) collective-permute-start(bf16[288,2560]{1,0:T(8,128)(2,1)} %add_convert_fusion.5), channel_id=1, source_target_pairs={{0,2},{1,3},{2,0},{3,1},{4,6},{5,7},{6,4},{7,5},{8,10},{9,11},{10,... | collective-permute-start | bytes 4423688 | tf_op jit(solution)/shard_map/ppermute | solution.py:157
  1460.0 31.1 %collective-permute-start.96 = (bf16[288,1152]{1,0:T(8,128)(2,1)}, bf16[288,1152]{1,0:T(8,128)(2,1)}, u32[]{:S(2)}, u32[]{:S(2)}) collective-permute-start(bf16[288,1152]{1,0:T(8,128)(2,1)} %get-tuple-element.965), channel_id=1, source_target_pairs={{0,16},{4,20},{8,24},{12,28},{16,0},{20,4},{24,8},{28,12},{1,17},{... | collective-permute-start | bytes 1990664 | tf_op jit(solution)/shard_map/ppermute | solution.py:157
  1512.3 33.8 %collective-permute-start.104 = (bf16[288,3072]{1,0:T(8,128)(2,1)S(1)}, bf16[288,3072]{1,0:T(8,128)(2,1)S(1)}, u32[]{:S(2)}, u32[]{:S(2)}) collective-permute-start(bf16[288,3072]{1,0:T(8,128)(2,1)S(1)} %pad_maximum_fusion.6), channel_id=1, source_target_pairs={{0,1},{1,0},{2,3},{3,2},{4,5},{5,4},{6,7},{7,6},{8,9},{9,8},{10,11... | collective-permute-start | bytes 5308424 | tf_op jit(solution)/shard_map/ppermute | solution.py:157
  1514.4 31.7 %collective-permute-start.103 = (bf16[288,1152]{1,0:T(8,128)(2,1)S(1)}, bf16[288,1152]{1,0:T(8,128)(2,1)S(1)}, u32[]{:S(2)}, u32[]{:S(2)}) collective-permute-start(bf16[288,1152]{1,0:T(8,128)(2,1)S(1)} %copy-done.73), channel_id=1, source_target_pairs={{0,16},{4,20},{8,24},{12,28},{16,0},{20,4},{24,8},{28,12},{1,17},{... | collective-permute-start | bytes 1990664 | tf_op jit(solution)/shard_map/ppermute | solution.py:157
  1565.0 32.3 %collective-permute-start.107 = (bf16[288,1152]{1,0:T(8,128)(2,1)}, bf16[288,1152]{1,0:T(8,128)(2,1)}, u32[]{:S(2)}, u32[]{:S(2)}) collective-permute-start(bf16[288,1152]{1,0:T(8,128)(2,1)} %get-tuple-element.989), channel_id=1, source_target_pairs={{0,16},{4,20},{8,24},{12,28},{16,0},{20,4},{24,8},{28,12},{1,17},{... | collective-permute-start | bytes 1990664 | tf_op jit(solution)/shard_map/ppermute | solution.py:157
  (188 other events, 2849.9 us)

commit v14 on v12

--- a/solution.py
+++ b/solution.py
@@ -1630,21 +1630,31 @@
             grads = [jnp.concatenate([g, swap(g, "seq", bit)], axis=0) for g in grads]
         return grads
 
+    rows_out = jnp.stack(layer_out)
+    far_down = [swap(clock.hold(v), "seq", far_bits[0]) for v in down_grad]
     a, b = halves(clock.hold(part_of(wide // 2)))
     gate_moved = []
     for k in range(wide // 2 - 1, -1, -1):
         step = wide // 2 - 1 - k
         a, b = hop(a, b, wide)
         work = []
-        if step in (1, 2):
-            work = [far_move(gate_parts[step - 1])]
-        elif step == half_wide - 1:
-            work = spread_grad([clock.hold(v) for v in down_grad], far_bits)
+        if step == 0:
+            work = far_down
+        elif step == 1:
+            near_down = [swap(clock.hold(v), "seq", 1) for v in down_grad]
+            work = [far_move(gate_parts[0]), *near_down]
+        elif step == 2:
+            work = [far_move(gate_parts[1]), unpack(down_grad, pieces, 2, [])]
         a, b, *work = clock.sync(a, b, *work)
-        if step in (1, 2):
-            gate_moved += work
-        elif step == half_wide - 1:
-            down_grad = work
+        if step == 0:
+            down_grad = [jnp.concatenate(v, axis=0) for v in zip(down_grad, work)]
+            down_grad = spread_grad(down_grad, far_bits[1:])
+        elif step == 1:
+            gate_moved.append(work[0])
+            down_grad = [jnp.concatenate(v, axis=0) for v in zip(down_grad, work[1:])]
+        elif step == 2:
+            gate_moved.append(work[0])
+            mlp_grad = work[1]
         if step == 0:
             a, b = add_first(part_of(k), a), add_last(part_of(-k), b)
         elif k > 0:
@@ -1707,19 +1717,20 @@
         [left[:, :half_proj], right[:, :half_proj], left[:, half_proj:], right[:, half_proj:]],
         axis=1,
     ).astype(f32)
-    down_grad = spread_grad([clock.hold(v) for v in down_grad], seq_bits[:1])
-    mlp_grad = unpack(down_grad, pieces, 2, [])
-    moved, attn_grad, mlp_grad, *gate_grad = clock.sync(moved, attn_grad, mlp_grad, *gate_grad)
+    up_other = [swap(clock.hold(v), "seq", 1) for v in up_grad]
+    parts_up = len(up_other)
+    moved, attn_grad, *work = clock.sync(moved, attn_grad, *up_other, *gate_grad)
+    up_other, gate_grad = work[:parts_up], work[parts_up:]
     last = spread_grad([low_sum(gate_own[1], moved)], far_bits)
-    up_grad = spread_grad([clock.hold(v) for v in up_grad], seq_bits[:1])
-    mlp_grad = unpack(up_grad, pieces, 1, [mlp_grad])
+    up_grad = [jnp.concatenate(v, axis=0) for v in zip(up_grad, up_other)]
+    mlp_grad = unpack([clock.hold(v) for v in up_grad], pieces, 1, [mlp_grad])
     gate_grad = spread_grad([clock.hold(v) for v in gate_grad], seq_bits[:1])
     mlp_grad, *gate_grad = clock.sync(mlp_grad, *gate_grad, *last)
     gate_grad[1:] = spread_grad(gate_grad[1:], seq_bits[:1])
     mlp_grad = unpack(gate_grad, pieces, 0, [mlp_grad])
     grad_tokens = [first_tokens, last_tokens]
     return (
-        jnp.stack(layer_out),
+        rows_out,
         jnp.stack(grad_tokens),
         attn_grad,
         mlp_grad,

time: 1620 us -> 1630 us (level)
    ppermute x48, waiting for transfers between devices: 159 us -> 179 us  [hop(): return (lax.ppermute(a, 'wide', up), lax.ppermute(b, 'wide', down))]
    unnamed x252 -> x270, local copies, waits for them, and re-layouts: 52.2 us -> 52.1 us
  transfers between devices with their start and end apart: 129 -> 129, of which waited for: 63 -> 65; matrix products, arithmetic and copies ran while one was open for 15% -> 16% of each run, Pallas kernels for 33% -> 33%
where the time goes in v14:
time: 1630 us; the launch traced here: 1620 us
  Pallas kernels  562 us (34%)
  waiting for transfers between devices  557 us (34%)
  starting transfers between devices  155 us (10%)
  other arithmetic  124 us (8%)
  local copies, waits for them, and re-layouts  115 us (7%)
  matrix products  99.8 us (6%)
    ppermute x63, waiting for transfers between devices, swap(): return lax.ppermute(value, axis, [(i, i ^ bit) for i in range(size)])  284 us
    ppermute x48, waiting for transfers between devices, hop(): return (lax.ppermute(a, 'wide', up), lax.ppermute(b, 'wide', down))  179 us
    dot_general x8, matrix products, dot(): return lax.dot_general(a, b, (dims, ((), ())), preferred_element_type=f32)  99.8 us
    pallas_call x3, Pallas kernels, weight_back(): kernel_call(functools.partial(weight_kernel, count=count, tiles=tiles), t...  91.3 us
    ppermute x6, waiting for transfers between devices, class_ring(): return lax.ppermute(value, 'wide', perm)  72.1 us
    pallas_call x4, Pallas kernels, input_back(): kernel_call(input_back_kernel, tiles, [whole_spec(grad_gate.shape)] * 2 +...  69.2 us
    convert_element_type x27, other arithmetic, low_sum(): return sum((t.astype(f32) for t in terms)).astype(bf16)  63.1 us
    pallas_call x3, Pallas kernels, open_forward(): kernel_call(open_kernel, tiles, [whole_spec(x.shape)] + [row_spec(tile, d...  62.7 us
  transfers between devices with their start and end apart: 129, of which 65 were waited for; matrix products, arithmetic and copies ran while one was open for 16% of the time, Pallas kernels for 33%

profile of v14, /device:TPU:0, one launch (start us, length us, event | category | flops | bytes accessed | tf_op | source)
XLA Modules:
  0.0 1616.0 jit_solution(16067349742863271245)
XLA Ops:
  11.2 25.3 %own_slices.1 = (bf16[2304,2304]{1,0:T(8,128)(2,1)}, bf16[2304,2304]{1,0:T(8,128)(2,1)}, bf16[2304,2304]{1,0:T(8,128)(2,1)}, bf16[2304,2304]{1,0:T(8,128)(2,1)},...) custom-call(s32[4]{0:T(128)} %pad_add_fusion.pieces, s32[4]{0:T(128)} %pad_add_fusion.1.info, ...), custom_call_target="tpu_custom_call" | custom-call | flops 159252480 | bytes 63700992 | tf_op jit(solution)/shard_map/own_slices/pallas_call | solution.py:303
  49.7 27.6 %collective-permute-done.3.refs_0_ = bf16[288,2560]{1,0:T(8,128)(2,1)} collective-permute-done((bf16[288,2560]{1,0:T(8,128)(2,1)S(1)}, bf16[288,2560]{1,0:T(8,128)(2,1)}, u32[]{:S(2)}, u32[]{:S(2)}) %collective-permute-start.3) | collective-permute-done | bytes 1474592 | tf_op jit(solution)/shard_map/ppermute | solution.py:102
  94.8 19.8 %collective-permute-done.7.refs_0_ = bf16[288,2560]{1,0:T(8,128)(2,1)S(1)} collective-permute-done((bf16[288,2560]{1,0:T(8,128)(2,1)}, bf16[288,2560]{1,0:T(8,128)(2,1)S(1)}, u32[]{:S(2)}, u32[]{:S(2)}) %collective-permute-start.7) | collective-permute-done | bytes 1474592 | tf_op jit(solution)/shard_map/ppermute | solution.py:102
  178.4 24.1 %collective-permute-done.15.refs_0_ = bf16[288,2304]{1,0:T(8,128)(2,1)} collective-permute-done((bf16[288,2304]{1,0:T(8,128)(2,1)}, bf16[288,2304]{1,0:T(8,128)(2,1)}, u32[]{:S(2)}, u32[]{:S(2)}) %collective-permute-start.15) | collective-permute-done | bytes 1327136 | tf_op jit(solution)/shard_map/ppermute | solution.py:157
  240.0 22.2 %collective-permute-done.17.refs_1_ = bf16[4,256,512]{2,1,0:T(8,128)(2,1)} collective-permute-done((bf16[4,256,512]{2,1,0:T(8,128)(2,1)S(1)}, bf16[4,256,512]{2,1,0:T(8,128)(2,1)}, u32[]{:S(2)}, u32[]{:S(2)}) %collective-permute-start.17) | collective-permute-done | bytes 1048608 | tf_op jit(solution)/shard_map/ppermute | solution.py:177
  270.5 20.5 %collective-permute-done.18 = bf16[2,256,512]{2,1,0:T(8,128)(2,1)S(1)} collective-permute-done((bf16[2,256,512]{2,1,0:T(8,128)(2,1)S(1)}, bf16[2,256,512]{2,1,0:T(8,128)(2,1)S(1)}, u32[]{:S(2)}, u32[]{:S(2)}) %collective-permute-start.18) | collective-permute-done | bytes 524320 | tf_op jit(solution)/shard_map/ppermute | solution.py:177
  298.6 11.5 attn_forward.2
  310.0 12.0 collective-permute-done.20
  329.9 20.5 %out_slices.1 = (bf16[2304,2048]{1,0:T(8,128)(2,1)}, bf16[2304,2048]{1,0:T(8,128)(2,1)}) custom-call(s32[8]{0:T(128)} %stack.163.places, s32[4]{0:T(128)} %pad_add_fusion.1.info, bf16[8,288,512]{2,1,0:T(8,128)(2,1)} %copy-done.35, bf16[8,288,512]{2,1,0:T(8,128)(2,1)} %collective-permute-done.19.refs_1_, ...), custom_call_target="tpu_custom_call" | custom-call | flops 94371840 | bytes 28311552 | tf_op jit(solution)/shard_map/out_slices/pallas_call | solution.py:260
  370.8 13.2 join_rows.2
  405.2 13.2 join_rows.3
  418.4 34.0 %collective-permute-done.25.refs_0_ = bf16[288,2304]{1,0:T(8,128)(2,1)} collective-permute-done((bf16[288,2304]{1,0:T(8,128)(2,1)S(1)}, bf16[288,2304]{1,0:T(8,128)(2,1)}, u32[]{:S(2)}, u32[]{:S(2)}) %collective-permute-start.25) | collective-permute-done | bytes 1327136 | tf_op jit(solution)/shard_map/ppermute | solution.py:157
  453.3 30.5 %collective-permute-done.27.refs_1_ = bf16[288,2304]{1,0:T(8,128)(2,1)S(1)} collective-permute-done((bf16[288,2304]{1,0:T(8,128)(2,1)}, bf16[288,2304]{1,0:T(8,128)(2,1)S(1)}, u32[]{:S(2)}, u32[]{:S(2)}) %collective-permute-start.27) | collective-permute-done | bytes 1327136 | tf_op jit(solution)/shard_map/ppermute | solution.py:157
  483.7 28.8 %collective-permute-done.26.refs_0_ = bf16[288,2304]{1,0:T(8,128)(2,1)} collective-permute-done((bf16[288,2304]{1,0:T(8,128)(2,1)S(1)}, bf16[288,2304]{1,0:T(8,128)(2,1)}, u32[]{:S(2)}, u32[]{:S(2)}) %collective-permute-start.26) | collective-permute-done | bytes 1327136 | tf_op jit(solution)/shard_map/ppermute | solution.py:157
  516.4 26.3 %collective-permute-done.28 = bf16[256,2304]{1,0:T(8,128)(2,1)S(1)} collective-permute-done((bf16[256,2304]{1,0:T(8,128)(2,1)}, bf16[256,2304]{1,0:T(8,128)(2,1)S(1)}, u32[]{:S(2)}, u32[]{:S(2)}) %collective-permute-start.28) | collective-permute-done | bytes 1179680 | tf_op jit(solution)/shard_map/ppermute | solution.py:102
  570.4 29.1 %open_forward.3 = (f32[1024,2304]{1,0:T(8,128)}, f32[1024,2304]{1,0:T(8,128)}, bf16[1024,2304]{1,0:T(8,128)(2,1)}) custom-call(bf16[1024,2304]{1,0:T(8,128)(2,1)} %constant_dynamic-update-slice_fusion.4.refs_0_.refs_2_, bf16[2304,2304]{1,0:T(8,128)(2,1)} %get-tuple-element.679.refs_1_.refs_2_, bf16[2304,2304]{1,0:T(8,128)(2,1)} %get-tuple-element.680.refs_2_.refs_3_), custom_call_target="tpu_custom_call" | custom-call | flops 21743271936 | bytes 49545216 | tf_op jit(solution)/shard_map/open_forward/pallas_call | solution.py:454
  616.5 14.9 convolution_convert_fusion.3.part_ref
  636.2 18.1 %open_forward.4 = (f32[1024,2304]{1,0:T(8,128)}, f32[1024,2304]{1,0:T(8,128)}, bf16[1024,2304]{1,0:T(8,128)(2,1)}) custom-call(bf16[1024,2304]{1,0:T(8,128)(2,1)} %constant_dynamic-update-slice_fusion.9.refs_0_.refs_3_, bf16[2304,2304]{1,0:T(8,128)(2,1)} %get-tuple-element.709.refs_1_.refs_2_, bf16[2304,2304]{1,0:T(8,128)(2,1)} %get-tuple-element.710.refs_2_.refs_3_), custom_call_target="tpu_custom_call" | custom-call | flops 12079595520 | bytes 29622272 | tf_op jit(solution)/shard_map/open_forward/pallas_call | solution.py:454
  659.1 15.4 open_forward.5
  690.1 13.5 convolution_convert_fusion.2.part_ref
  732.8 14.9 open_back.4
  751.5 12.7 open_back.5
  764.2 18.4 %input_back.4.refs_4_ = bf16[1024,2304]{1,0:T(8,128)(2,1)} custom-call(bf16[1024,2304]{1,0:T(8,128)(2,1)} %get-tuple-element.888.refs_0_, bf16[1024,2304]{1,0:T(8,128)(2,1)} %get-tuple-element.864.refs_1_.refs_0_, bf16[2304,2304]{1,0:T(8,128)(2,1)} %get-tuple-element.679.refs_1_.refs_2_, bf16[2304,2304]{1,0:T(8,128)(2,1)} %get-tuple-element.680.refs_2_.refs_3_), custom_call_target="tpu_custom_call" | custom-call | flops 12079595520 | bytes 23855104 | tf_op jit(solution)/shard_map/input_back/pallas_call | solution.py:511
  794.6 15.8 input_back.5.part_ref
  817.6 13.6 collective-permute-done.55
  836.3 14.9 open_back.6
  854.2 12.8 open_back.7
  867.0 18.4 %input_back.6.refs_4_ = bf16[1024,2304]{1,0:T(8,128)(2,1)} custom-call(bf16[1024,2304]{1,0:T(8,128)(2,1)} %get-tuple-element.889.refs_0_.refs_1_, bf16[1024,2304]{1,0:T(8,128)(2,1)} %get-tuple-element.865.refs_1_, bf16[2304,2304]{1,0:T(8,128)(2,1)} %get-tuple-element.709.refs_1_.refs_2_, bf16[2304,2304]{1,0:T(8,128)(2,1)} %get-tuple-element.710.refs_2_.refs_3_), custom_call_target="tpu_custom_call" | custom-call | flops 12079595520 | bytes 23855104 | tf_op jit(solution)/shard_map/input_back/pallas_call | solution.py:511
  885.4 16.6 %input_back.7.part_ref = bf16[1024,2304]{1,0:T(8,128)(2,1)} custom-call(bf16[1024,2304]{1,0:T(8,128)(2,1)} %get-tuple-element.889.refs_0_.refs_1_, bf16[1024,2304]{1,0:T(8,128)(2,1)} %get-tuple-element.865.refs_1_, bf16[2304,2304]{1,0:T(8,128)(2,1)} %get-tuple-element.709.refs_1_.refs_2_, ...), custom_call_target="tpu_custom_call", output_to_operand_aliasing={{}: (4, {})} | custom-call | flops 9663676416 | bytes 20971520 | tf_op jit(solution)/shard_map/input_back/pallas_call | solution.py:511
  905.6 13.2 branch_back.2
  923.1 30.3 %weight_back.3 = (bf16[1152,2304]{1,0:T(8,128)(2,1)}, bf16[1152,2304]{1,0:T(8,128)(2,1)}) custom-call(bf16[1024,2304]{1,0:T(8,128)(2,1)} %get-tuple-element.810.refs_0_, bf16[1024,2304]{1,0:T(8,128)(2,1)} %get-tuple-element.811.refs_1_, bf16[1024,2304]{1,0:T(8,128)(2,1)} %copy-done.3, bf16[1024,2304]{1,0:T(8,128)(2,1)} %constant_dynamic-update-slice_fusion.19.refs_0_.refs_3_), custom_call_target="tpu_custom_call" | custom-call | flops 21743271936 | bytes 29491200 | tf_op jit(solution)/shard_map/weight_back/pallas_call | solution.py:554
  962.7 13.8 branch_back.3
  1003.2 17.4 %attn_backward.2 = (bf16[1024,512]{1,0:T(8,128)(2,1)}, bf16[4,256,512]{2,1,0:T(8,128)(2,1)}, bf16[4,256,512]{2,1,0:T(8,128)(2,1)}) custom-call(s32[1]{0:T(128)} %bitcast.41.info, bf16[1024,512]{1,0:T(8,128)(2,1)} %bitcast.228, bf16[1024,512]{1,0:T(8,128)(2,1)} %bitcast.233, f32[1024,512]{1,0:T(8,128)} %get-tuple-element.837.exact_ref, ...), custom_call_target="tpu_custom_call" | custom-call | flops 10737418240 | bytes 9437184 | tf_op jit(solution)/shard_map/attn_backward/pallas_call | solution.py:994
  1030.6 17.5 %attn_backward.3 = (bf16[1024,512]{1,0:T(8,128)(2,1)}, bf16[4,256,512]{2,1,0:T(8,128)(2,1)}, bf16[4,256,512]{2,1,0:T(8,128)(2,1)}) custom-call(s32[1]{0:T(128)} %bitcast.41.info, bf16[1024,512]{1,0:T(8,128)(2,1)} %bitcast.226, bf16[1024,512]{1,0:T(8,128)(2,1)} %bitcast.67.grad_ref, f32[1024,512]{1,0:T(8,128)} %get-tuple-element.852.exact_ref, ...), custom_call_target="tpu_custom_call" | custom-call | flops 10737418240 | bytes 9437184 | tf_op jit(solution)/shard_map/attn_backward/pallas_call | solution.py:994
  1073.6 30.5 %weight_back.4 = (bf16[1152,2304]{1,0:T(8,128)(2,1)}, bf16[1152,2304]{1,0:T(8,128)(2,1)}) custom-call(bf16[1024,2304]{1,0:T(8,128)(2,1)} %get-tuple-element.864.refs_1_.refs_0_, bf16[1024,2304]{1,0:T(8,128)(2,1)} %get-tuple-element.865.refs_1_, bf16[1024,2304]{1,0:T(8,128)(2,1)} %constant_dynamic-update-slice_fusion.4.refs_0_.refs_2_, ...), custom_call_target="tpu_custom_call" | custom-call | flops 21743271936 | bytes 29491200 | tf_op jit(solution)/shard_map/weight_back/pallas_call | solution.py:554
  1117.0 17.5 %collective-permute-done.72 = bf16[4,256,512]{2,1,0:T(8,128)(2,1)} collective-permute-done((bf16[4,256,512]{2,1,0:T(8,128)(2,1)}, bf16[4,256,512]{2,1,0:T(8,128)(2,1)}, u32[]{:S(2)}, u32[]{:S(2)}) %collective-permute-start.72) | collective-permute-done | bytes 1048608 | tf_op jit(solution)/shard_map/ppermute | solution.py:177
  1155.1 30.5 %weight_back.5 = (bf16[1152,2304]{1,0:T(8,128)(2,1)}, bf16[1152,2304]{1,0:T(8,128)(2,1)}) custom-call(bf16[1024,2304]{1,0:T(8,128)(2,1)} %get-tuple-element.888.refs_0_, bf16[1024,2304]{1,0:T(8,128)(2,1)} %get-tuple-element.889.refs_0_.refs_1_, bf16[1024,2304]{1,0:T(8,128)(2,1)} %constant_dynamic-update-slice_fusion.4.refs_0_.refs_2_, ...), custom_call_target="tpu_custom_call" | custom-call | flops 21743271936 | bytes 29491200 | tf_op jit(solution)/shard_map/weight_back/pallas_call | solution.py:554
  1191.3 13.9 turn_back.1
  1219.6 13.1 collective-permute-done.77
  1248.2 11.6 collective-permute-done.80
  1318.1 24.4 %collective-permute-done.89 = bf16[2,288,1152]{2,1,0:T(8,128)(2,1)} collective-permute-done((bf16[2,288,1152]{2,1,0:T(8,128)(2,1)}, bf16[2,288,1152]{2,1,0:T(8,128)(2,1)}, u32[]{:S(2)}, u32[]{:S(2)}) %collective-permute-start.89) | collective-permute-done | bytes 1327136 | tf_op jit(solution)/shard_map/ppermute | solution.py:157
  1400.7 21.9 %collective-permute-done.97 = bf16[288,2560]{1,0:T(8,128)(2,1)S(1)} collective-permute-done((bf16[288,2560]{1,0:T(8,128)(2,1)S(1)}, bf16[288,2560]{1,0:T(8,128)(2,1)S(1)}, u32[]{:S(2)}, u32[]{:S(2)}) %collective-permute-start.97) | collective-permute-done | bytes 1474592 | tf_op jit(solution)/shard_map/ppermute | solution.py:102
  1429.1 20.8 %fusion.47 = f32[256,2304]{1,0:T(8,128)} fusion(bf16[256,4096]{1,0:T(8,128)(2,1)} %get-tuple-element.964, bf16[2304,4096]{1,0:T(8,128)(2,1)} %get-tuple-element.553.wq_ref.wk_ref.wv_ref), kind=kOutput, calls=%fused_computation.259 | convolution fusion | flops 4831838208 | bytes 23330816 | tf_op jit(solution)/shard_map/dot_general | solution.py:26
  1457.1 20.6 %fusion.48 = f32[256,2304]{1,0:T(8,128)} fusion(bf16[256,4096]{1,0:T(8,128)(2,1)} %get-tuple-element.972, bf16[2304,4096]{1,0:T(8,128)(2,1)} %get-tuple-element.556.wq_ref.wk_ref.wv_ref), kind=kOutput, calls=%fused_computation.260 | convolution fusion | flops 4831838208 | bytes 23330816 | tf_op jit(solution)/shard_map/dot_general | solution.py:26
  1516.2 13.3 collective-permute-done.109
  1529.6 13.7 collective-permute-done.108
  1551.5 12.4 collective-permute-done.113
  1563.9 15.7 collective-permute-done.110
  (713 shorter events, 702.4 us)
Async XLA Ops:
  3.8 38.6 %collective-permute-start = (bf16[288,2560]{1,0:T(8,128)(2,1)S(1)}, bf16[288,2560]{1,0:T(8,128)(2,1)S(1)}, u32[]{:S(2)}, u32[]{:S(2)}) collective-permute-start(bf16[288,2560]{1,0:T(8,128)(2,1)S(1)} %pad_maximum_fusion.11.refs_0_), channel_id=1, source_target_pairs={{0,8},{8,16},{16,24},{24,28},{28,20},{20,12},{12,4},{4,0},{1,9},{9... | collective-permute-start | bytes 4423688 | tf_op jit(solution)/shard_map/ppermute | solution.py:102
  6.9 35.5 %collective-permute-start.1 = (bf16[288,2560]{1,0:T(8,128)(2,1)S(1)}, bf16[288,2560]{1,0:T(8,128)(2,1)}, u32[]{:S(2)}, u32[]{:S(2)}) collective-permute-start(bf16[288,2560]{1,0:T(8,128)(2,1)S(1)} %pad_maximum_fusion.11.refs_0_), channel_id=1, source_target_pairs={{8,0},{16,8},{24,16},{28,24},{20,28},{12,20},{4,12},{0,4},{9,1},{1... | collective-permute-start | bytes 4423688 | tf_op jit(solution)/shard_map/ppermute | solution.py:102
  6.9 35.5 %collective-permute-start.2 = (bf16[288,2560]{1,0:T(8,128)(2,1)S(1)}, bf16[288,2560]{1,0:T(8,128)(2,1)}, u32[]{:S(2)}, u32[]{:S(2)}) collective-permute-start(bf16[288,2560]{1,0:T(8,128)(2,1)S(1)} %pad_maximum_fusion.11.refs_0_), channel_id=1, source_target_pairs={{0,1},{1,0},{2,3},{3,2},{4,5},{5,4},{6,7},{7,6},{8,9},{9,8},{10,11... | collective-permute-start | bytes 4423688 | tf_op jit(solution)/shard_map/ppermute | solution.py:157
  42.4 34.9 %collective-permute-start.3 = (bf16[288,2560]{1,0:T(8,128)(2,1)S(1)}, bf16[288,2560]{1,0:T(8,128)(2,1)}, u32[]{:S(2)}, u32[]{:S(2)}) collective-permute-start(bf16[288,2560]{1,0:T(8,128)(2,1)S(1)} %collective-permute-done.refs_2_), channel_id=1, source_target_pairs={{0,8},{8,16},{16,24},{24,28},{28,20},{20,12},{12,4},{4,0},{1,9},{9... | collective-permute-start | bytes 4423688 | tf_op jit(solution)/shard_map/ppermute | solution.py:102
  44.5 35.0 %collective-permute-start.5 = (bf16[288,2560]{1,0:T(8,128)(2,1)S(1)}, bf16[288,2560]{1,0:T(8,128)(2,1)S(1)}, u32[]{:S(2)}, u32[]{:S(2)}) collective-permute-start(bf16[288,2560]{1,0:T(8,128)(2,1)S(1)} %collective-permute-done.refs_2_), channel_id=1, source_target_pairs={{0,1},{1,0},{2,3},{3,2},{4,5},{5,4},{6,7},{7,6},{8,9},{9,8},{10,11... | collective-permute-start | bytes 4423688 | tf_op jit(solution)/shard_map/ppermute | solution.py:157
  44.5 34.9 %collective-permute-start.4 = (bf16[288,2560]{1,0:T(8,128)(2,1)}, bf16[288,2560]{1,0:T(8,128)(2,1)}, u32[]{:S(2)}, u32[]{:S(2)}) collective-permute-start(bf16[288,2560]{1,0:T(8,128)(2,1)} %collective-permute-done.1.refs_4_), channel_id=1, source_target_pairs={{8,0},{16,8},{24,16},{28,24},{20,28},{12,20},{4,12},{0,4},{9,1},{1... | collective-permute-start | bytes 4423688 | tf_op jit(solution)/shard_map/ppermute | solution.py:102
  44.8 34.7 %collective-permute-start.6 = (bf16[288,2560]{1,0:T(8,128)(2,1)}, bf16[288,2560]{1,0:T(8,128)(2,1)S(1)}, u32[]{:S(2)}, u32[]{:S(2)}) collective-permute-start(bf16[288,2560]{1,0:T(8,128)(2,1)} %collective-permute-done.1.refs_4_), channel_id=1, source_target_pairs={{0,1},{1,0},{2,3},{3,2},{4,5},{5,4},{6,7},{7,6},{8,9},{9,8},{10,11... | collective-permute-start | bytes 4423688 | tf_op jit(solution)/shard_map/ppermute | solution.py:157
  80.6 34.1 %collective-permute-start.7 = (bf16[288,2560]{1,0:T(8,128)(2,1)}, bf16[288,2560]{1,0:T(8,128)(2,1)S(1)}, u32[]{:S(2)}, u32[]{:S(2)}) collective-permute-start(bf16[288,2560]{1,0:T(8,128)(2,1)} %collective-permute-done.3.refs_0_), channel_id=1, source_target_pairs={{0,8},{8,16},{16,24},{24,28},{28,20},{20,12},{12,4},{4,0},{1,9},{9... | collective-permute-start | bytes 4423688 | tf_op jit(solution)/shard_map/ppermute | solution.py:102
  82.2 34.2 %collective-permute-start.8 = (bf16[288,2560]{1,0:T(8,128)(2,1)}, bf16[288,2560]{1,0:T(8,128)(2,1)S(1)}, u32[]{:S(2)}, u32[]{:S(2)}) collective-permute-start(bf16[288,2560]{1,0:T(8,128)(2,1)} %collective-permute-done.4.refs_2_), channel_id=1, source_target_pairs={{8,0},{16,8},{24,16},{28,24},{20,28},{12,20},{4,12},{0,4},{9,1},{1... | collective-permute-start | bytes 4423688 | tf_op jit(solution)/shard_map/ppermute | solution.py:102
  83.1 33.3 %collective-permute-start.9 = (bf16[288,2560]{1,0:T(8,128)(2,1)}, bf16[288,2560]{1,0:T(8,128)(2,1)}, u32[]{:S(2)}, u32[]{:S(2)}) collective-permute-start(bf16[288,2560]{1,0:T(8,128)(2,1)} %collective-permute-done.3.refs_0_), channel_id=1, source_target_pairs={{0,1},{1,0},{2,3},{3,2},{4,5},{5,4},{6,7},{7,6},{8,9},{9,8},{10,11... | collective-permute-start | bytes 4423688 | tf_op jit(solution)/shard_map/ppermute | solution.py:157
  141.4 61.1 %collective-permute-start.15 = (bf16[288,2304]{1,0:T(8,128)(2,1)}, bf16[288,2304]{1,0:T(8,128)(2,1)}, u32[]{:S(2)}, u32[]{:S(2)}) collective-permute-start(bf16[288,2304]{1,0:T(8,128)(2,1)} %get-tuple-element.544), channel_id=1, source_target_pairs={{0,16},{4,20},{8,24},{12,28},{16,0},{20,4},{24,8},{28,12},{1,17},{... | collective-permute-start | bytes 3981320 | tf_op jit(solution)/shard_map/ppermute | solution.py:157
  238.8 53.0 %collective-permute-start.19 = (bf16[8,288,512]{2,1,0:T(8,128)(2,1)}, bf16[8,288,512]{2,1,0:T(8,128)(2,1)}, u32[]{:S(2)}, u32[]{:S(2)}) collective-permute-start(bf16[8,288,512]{2,1,0:T(8,128)(2,1)} %copy-done.35), channel_id=1, source_target_pairs={{0,2},{1,3},{2,0},{3,1},{4,6},{5,7},{6,4},{7,5},{8,10},{9,11},{10,... | collective-permute-start | bytes 7077896 | tf_op jit(solution)/shard_map/ppermute | solution.py:157
  323.0 40.0 %all-to-all-start.4 = ((bf16[8,128,512]{2,1,0:T(8,128)(2,1)}), bf16[8,128,512]{2,1,0:T(8,128)(2,1)S(1)}, u32[]{:S(2)}, u32[]{:S(2)}) async-start(bf16[8,128,512]{2,1,0:T(8,128)(2,1)} %bitcast.235), calls=%async_computation.4 | async-start | bytes 2097152 | tf_op jit(solution)/shard_map/all_to_all | solution.py:161
  326.7 36.3 %collective-permute-start.22 = (bf16[288,2304]{1,0:T(8,128)(2,1)}, bf16[288,2304]{1,0:T(8,128)(2,1)}, u32[]{:S(2)}, u32[]{:S(2)}) collective-permute-start(bf16[288,2304]{1,0:T(8,128)(2,1)} %collective-permute-done.15.refs_0_), channel_id=1, source_target_pairs={{0,2},{1,3},{2,0},{3,1},{4,6},{5,7},{6,4},{7,5},{8,10},{9,11},{10,... | collective-permute-start | bytes 3981320 | tf_op jit(solution)/shard_map/ppermute | solution.py:157
  363.0 31.4 %all-to-all-start.5 = ((bf16[8,128,512]{2,1,0:T(8,128)(2,1)}), bf16[8,128,512]{2,1,0:T(8,128)(2,1)S(1)}, u32[]{:S(2)}, u32[]{:S(2)}) async-start(bf16[8,128,512]{2,1,0:T(8,128)(2,1)} %bitcast.236), calls=%async_computation.5 | async-start | bytes 2097152 | tf_op jit(solution)/shard_map/all_to_all | solution.py:161
  394.4 58.1 %collective-permute-start.25 = (bf16[288,2304]{1,0:T(8,128)(2,1)S(1)}, bf16[288,2304]{1,0:T(8,128)(2,1)}, u32[]{:S(2)}, u32[]{:S(2)}) collective-permute-start(bf16[288,2304]{1,0:T(8,128)(2,1)S(1)} %copy-done.53), channel_id=1, source_target_pairs={{0,16},{4,20},{8,24},{12,28},{16,0},{20,4},{24,8},{28,12},{1,17},{... | collective-permute-start | bytes 3981320 | tf_op jit(solution)/shard_map/ppermute | solution.py:157
  453.3 59.3 %collective-permute-start.26 = (bf16[288,2304]{1,0:T(8,128)(2,1)S(1)}, bf16[288,2304]{1,0:T(8,128)(2,1)}, u32[]{:S(2)}, u32[]{:S(2)}) collective-permute-start(bf16[288,2304]{1,0:T(8,128)(2,1)S(1)} %copy-done.52), channel_id=1, source_target_pairs={{0,16},{4,20},{8,24},{12,28},{16,0},{20,4},{24,8},{28,12},{1,17},{... | collective-permute-start | bytes 3981320 | tf_op jit(solution)/shard_map/ppermute | solution.py:157
  512.6 31.4 %collective-permute-start.32 = (bf16[288,2304]{1,0:T(8,128)(2,1)}, bf16[288,2304]{1,0:T(8,128)(2,1)}, u32[]{:S(2)}, u32[]{:S(2)}) collective-permute-start(bf16[288,2304]{1,0:T(8,128)(2,1)} %collective-permute-done.26.refs_0_), channel_id=1, source_target_pairs={{0,2},{1,3},{2,0},{3,1},{4,6},{5,7},{6,4},{7,5},{8,10},{9,11},{10,... | collective-permute-start | bytes 3981320 | tf_op jit(solution)/shard_map/ppermute | solution.py:157
  566.6 34.1 %collective-permute-start.37 = (bf16[256,2304]{1,0:T(8,128)(2,1)S(1)}, bf16[256,2304]{1,0:T(8,128)(2,1)S(1)}, u32[]{:S(2)}, u32[]{:S(2)}) collective-permute-start(bf16[256,2304]{1,0:T(8,128)(2,1)S(1)} %copy-done.65), channel_id=1, source_target_pairs={{0,8},{8,12},{12,4},{4,0},{16,24},{24,28},{28,20},{20,16},{1,9},{9... | collective-permute-start | bytes 3538952 | tf_op jit(solution)/shard_map/ppermute | solution.py:102
  568.4 32.3 %collective-permute-start.38 = (bf16[256,2304]{1,0:T(8,128)(2,1)S(1)}, bf16[256,2304]{1,0:T(8,128)(2,1)S(1)}, u32[]{:S(2)}, u32[]{:S(2)}) collective-permute-start(bf16[256,2304]{1,0:T(8,128)(2,1)S(1)} %copy-done.65), channel_id=1, source_target_pairs={{8,0},{12,8},{4,12},{0,4},{24,16},{28,24},{20,28},{16,20},{9,1},{1... | collective-permute-start | bytes 3538952 | tf_op jit(solution)/shard_map/ppermute | solution.py:102
  749.3 33.3 %collective-permute-start.52 = (bf16[256,2304]{1,0:T(8,128)(2,1)S(1)}, bf16[256,2304]{1,0:T(8,128)(2,1)S(1)}, u32[]{:S(2)}, u32[]{:S(2)}) collective-permute-start(bf16[256,2304]{1,0:T(8,128)(2,1)S(1)} %pad_maximum_fusion.21), channel_id=1, source_target_pairs={{8,0},{12,8},{4,12},{0,4},{24,16},{28,24},{20,28},{16,20},{9,1},{1... | collective-permute-start | bytes 3538952 | tf_op jit(solution)/shard_map/ppermute | solution.py:102
  750.7 31.9 %collective-permute-start.51 = (bf16[256,2304]{1,0:T(8,128)(2,1)S(1)}, bf16[256,2304]{1,0:T(8,128)(2,1)S(1)}, u32[]{:S(2)}, u32[]{:S(2)}) collective-permute-start(bf16[256,2304]{1,0:T(8,128)(2,1)S(1)} %pad_maximum_fusion.20), channel_id=1, source_target_pairs={{0,8},{8,12},{12,4},{4,0},{16,24},{24,28},{28,20},{20,16},{1,9},{9... | collective-permute-start | bytes 3538952 | tf_op jit(solution)/shard_map/ppermute | solution.py:102
  851.6 33.8 %collective-permute-start.60 = (bf16[256,2304]{1,0:T(8,128)(2,1)S(1)}, bf16[256,2304]{1,0:T(8,128)(2,1)S(1)}, u32[]{:S(2)}, u32[]{:S(2)}) collective-permute-start(bf16[256,2304]{1,0:T(8,128)(2,1)S(1)} %pad_maximum_fusion.23), channel_id=1, source_target_pairs={{8,0},{12,8},{4,12},{0,4},{24,16},{28,24},{20,28},{16,20},{9,1},{1... | collective-permute-start | bytes 3538952 | tf_op jit(solution)/shard_map/ppermute | solution.py:102
  852.6 32.8 %collective-permute-start.59 = (bf16[256,2304]{1,0:T(8,128)(2,1)S(1)}, bf16[256,2304]{1,0:T(8,128)(2,1)S(1)}, u32[]{:S(2)}, u32[]{:S(2)}) collective-permute-start(bf16[256,2304]{1,0:T(8,128)(2,1)S(1)} %pad_maximum_fusion.22), channel_id=1, source_target_pairs={{0,8},{8,12},{12,4},{4,0},{16,24},{24,28},{28,20},{20,16},{1,9},{9... | collective-permute-start | bytes 3538952 | tf_op jit(solution)/shard_map/ppermute | solution.py:102
  920.7 32.7 %collective-permute-start.64 = (bf16[256,2304]{1,0:T(8,128)(2,1)S(1)}, bf16[256,2304]{1,0:T(8,128)(2,1)}, u32[]{:S(2)}, u32[]{:S(2)}) collective-permute-start(bf16[256,2304]{1,0:T(8,128)(2,1)S(1)} %pad_maximum_fusion.25), channel_id=1, source_target_pairs={{8,0},{12,8},{4,12},{0,4},{24,16},{28,24},{20,28},{16,20},{9,1},{1... | collective-permute-start | bytes 3538952 | tf_op jit(solution)/shard_map/ppermute | solution.py:102
  989.3 31.3 %collective-permute-start.66 = (bf16[2,288,1152]{2,1,0:T(8,128)(2,1)S(1)}, bf16[2,288,1152]{2,1,0:T(8,128)(2,1)}, u32[]{:S(2)}, u32[]{:S(2)}) collective-permute-start(bf16[2,288,1152]{2,1,0:T(8,128)(2,1)S(1)} %get-tuple-element.831), channel_id=1, source_target_pairs={{0,2},{1,3},{2,0},{3,1},{4,6},{5,7},{6,4},{7,5},{8,10},{9,11},{10,... | collective-permute-start | bytes 3981320 | tf_op jit(solution)/shard_map/ppermute | solution.py:157
  1020.6 35.1 %collective-permute-start.69 = (bf16[2304,1024]{1,0:T(8,128)(2,1)}, bf16[2304,1024]{1,0:T(8,128)(2,1)}, u32[]{:S(2)}, u32[]{:S(2)}) collective-permute-start(bf16[2304,1024]{1,0:T(8,128)(2,1)} %convolution_convert_fusion.1), channel_id=1, source_target_pairs={{0,1},{1,0},{2,3},{3,2},{4,5},{5,4},{6,7},{7,6},{8,9},{9,8},{10,11... | collective-permute-start | bytes 14155784 | tf_op jit(solution)/shard_map/ppermute | solution.py:157
  1020.7 41.5 %collective-permute-start.68 = (bf16[2,288,1152]{2,1,0:T(8,128)(2,1)}, bf16[2,288,1152]{2,1,0:T(8,128)(2,1)}, u32[]{:S(2)}, u32[]{:S(2)}) collective-permute-start(bf16[2,288,1152]{2,1,0:T(8,128)(2,1)} %get-tuple-element.847), channel_id=1, source_target_pairs={{0,2},{1,3},{2,0},{3,1},{4,6},{5,7},{6,4},{7,5},{8,10},{9,11},{10,... | collective-permute-start | bytes 3981320 | tf_op jit(solution)/shard_map/ppermute | solution.py:157
  1026.0 36.3 %all-to-all-start.8 = ((bf16[8,128,512]{2,1,0:T(8,128)(2,1)}), bf16[8,128,512]{2,1,0:T(8,128)(2,1)}, u32[]{:S(2)}, u32[]{:S(2)}) async-start(bf16[8,128,512]{2,1,0:T(8,128)(2,1)} %bitcast.232), calls=%async_computation.8 | async-start | bytes 2097152 | tf_op jit(solution)/shard_map/all_to_all | solution.py:161
  1065.6 42.6 %collective-permute-start.71 = (bf16[2304,256]{1,0:T(8,128)(2,1)}, bf16[2304,256]{1,0:T(8,128)(2,1)}, u32[]{:S(2)}, u32[]{:S(2)}) collective-permute-start(bf16[2304,256]{1,0:T(8,128)(2,1)} %get-tuple-element.1032), channel_id=1, source_target_pairs={{0,2},{1,3},{2,0},{3,1},{4,6},{5,7},{6,4},{7,5},{8,10},{9,11},{10,... | collective-permute-start | bytes 3538952 | tf_op jit(solution)/shard_map/ppermute | solution.py:157
  1066.6 41.4 %collective-permute-start.70 = (bf16[2,256,512]{2,1,0:T(8,128)(2,1)}, bf16[2,256,512]{2,1,0:T(8,128)(2,1)S(1)}, u32[]{:S(2)}, u32[]{:S(2)}) collective-permute-start(bf16[2,256,512]{2,1,0:T(8,128)(2,1)} %get-tuple-element.861), channel_id=1, source_target_pairs={{0,4},{4,0},{8,12},{12,8},{16,20},{20,16},{24,28},{28,24},{1,5},{5... | collective-permute-start | bytes 1572872 | tf_op jit(solution)/shard_map/ppermute | solution.py:177
  1068.6 39.6 %all-to-all-start.9 = ((bf16[8,128,512]{2,1,0:T(8,128)(2,1)}), bf16[8,128,512]{2,1,0:T(8,128)(2,1)S(1)}, u32[]{:S(2)}, u32[]{:S(2)}) async-start(bf16[8,128,512]{2,1,0:T(8,128)(2,1)} %bitcast.68), calls=%async_computation.9 | async-start | bytes 2097152 | tf_op jit(solution)/shard_map/all_to_all | solution.py:161
  1111.4 33.6 %all-to-all-start.10 = ((bf16[4,256,512]{2,1,0:T(8,128)(2,1)}), bf16[4,256,512]{2,1,0:T(8,128)(2,1)S(1)}, u32[]{:S(2)}, u32[]{:S(2)}) async-start(bf16[4,256,512]{2,1,0:T(8,128)(2,1)} %pad_maximum_fusion.26), calls=%async_computation.10 | async-start | bytes 2097152 | tf_op jit(solution)/shard_map/all_to_all | solution.py:168
  1149.0 36.5 %collective-permute-start.75 = (bf16[2,288,1152]{2,1,0:T(8,128)(2,1)}, bf16[2,288,1152]{2,1,0:T(8,128)(2,1)}, u32[]{:S(2)}, u32[]{:S(2)}) collective-permute-start(bf16[2,288,1152]{2,1,0:T(8,128)(2,1)} %get-tuple-element.887), channel_id=1, source_target_pairs={{0,2},{1,3},{2,0},{3,1},{4,6},{5,7},{6,4},{7,5},{8,10},{9,11},{10,... | collective-permute-start | bytes 3981320 | tf_op jit(solution)/shard_map/ppermute | solution.py:157
  1150.0 35.5 %all-to-all-start.11 = ((bf16[4,256,512]{2,1,0:T(8,128)(2,1)}), bf16[4,256,512]{2,1,0:T(8,128)(2,1)}, u32[]{:S(2)}, u32[]{:S(2)}) async-start(bf16[4,256,512]{2,1,0:T(8,128)(2,1)} %add_convert_fusion.14), calls=%async_computation.11 | async-start | bytes 2097152 | tf_op jit(solution)/shard_map/all_to_all | solution.py:168
  1185.5 48.3 %collective-permute-start.78 = (bf16[2,576,2304]{2,1,0:T(8,128)(2,1)}, bf16[2,576,2304]{2,1,0:T(8,128)(2,1)}, u32[]{:S(2)}, u32[]{:S(2)}) collective-permute-start(bf16[2,576,2304]{2,1,0:T(8,128)(2,1)} %bitcast.247), channel_id=1, source_target_pairs={{0,1},{1,0},{2,3},{3,2},{4,5},{5,4},{6,7},{7,6},{8,9},{9,8},{10,11... | collective-permute-start | bytes 15925256 | tf_op jit(solution)/shard_map/ppermute | solution.py:157
  1190.1 42.6 %collective-permute-start.79 = (bf16[2,288,1152]{2,1,0:T(8,128)(2,1)S(1)}, bf16[2,288,1152]{2,1,0:T(8,128)(2,1)S(1)}, u32[]{:S(2)}, u32[]{:S(2)}) collective-permute-start(bf16[2,288,1152]{2,1,0:T(8,128)(2,1)S(1)} %copy-done.51), channel_id=1, source_target_pairs={{0,2},{1,3},{2,0},{3,1},{4,6},{5,7},{6,4},{7,5},{8,10},{9,11},{10,... | collective-permute-start | bytes 3981320 | tf_op jit(solution)/shard_map/ppermute | solution.py:157
  1306.0 36.4 %collective-permute-start.88 = (bf16[288,2560]{1,0:T(8,128)(2,1)}, bf16[288,2560]{1,0:T(8,128)(2,1)}, u32[]{:S(2)}, u32[]{:S(2)}) collective-permute-start(bf16[288,2560]{1,0:T(8,128)(2,1)} %pad_maximum_fusion.13), channel_id=1, source_target_pairs={{8,0},{16,8},{24,16},{28,24},{20,28},{12,20},{4,12},{0,4},{9,1},{1... | collective-permute-start | bytes 4423688 | tf_op jit(solution)/shard_map/ppermute | solution.py:102
  1308.9 34.7 %collective-permute-start.87 = (bf16[288,2560]{1,0:T(8,128)(2,1)}, bf16[288,2560]{1,0:T(8,128)(2,1)}, u32[]{:S(2)}, u32[]{:S(2)}) collective-permute-start(bf16[288,2560]{1,0:T(8,128)(2,1)} %fusion.8), channel_id=1, source_target_pairs={{0,8},{8,16},{16,24},{24,28},{28,20},{20,12},{12,4},{4,0},{1,9},{9... | collective-permute-start | bytes 4423688 | tf_op jit(solution)/shard_map/ppermute | solution.py:102
  1349.6 33.6 %collective-permute-start.94 = (bf16[288,2560]{1,0:T(8,128)(2,1)}, bf16[288,2560]{1,0:T(8,128)(2,1)}, u32[]{:S(2)}, u32[]{:S(2)}) collective-permute-start(bf16[288,2560]{1,0:T(8,128)(2,1)} %add_convert_fusion.9), channel_id=1, source_target_pairs={{8,0},{16,8},{24,16},{28,24},{20,28},{12,20},{4,12},{0,4},{9,1},{1... | collective-permute-start | bytes 4423688 | tf_op jit(solution)/shard_map/ppermute | solution.py:102
  1353.0 33.6 %collective-permute-start.93 = (bf16[288,2560]{1,0:T(8,128)(2,1)}, bf16[288,2560]{1,0:T(8,128)(2,1)}, u32[]{:S(2)}, u32[]{:S(2)}) collective-permute-start(bf16[288,2560]{1,0:T(8,128)(2,1)} %add_convert_fusion.10), channel_id=1, source_target_pairs={{0,8},{8,16},{16,24},{24,28},{28,20},{20,12},{12,4},{4,0},{1,9},{9... | collective-permute-start | bytes 4423688 | tf_op jit(solution)/shard_map/ppermute | solution.py:102
  1390.3 32.4 %collective-permute-start.97 = (bf16[288,2560]{1,0:T(8,128)(2,1)S(1)}, bf16[288,2560]{1,0:T(8,128)(2,1)S(1)}, u32[]{:S(2)}, u32[]{:S(2)}) collective-permute-start(bf16[288,2560]{1,0:T(8,128)(2,1)S(1)} %add_convert_fusion.7), channel_id=1, source_target_pairs={{8,0},{16,8},{24,16},{28,24},{20,28},{12,20},{4,12},{0,4},{9,1},{1... | collective-permute-start | bytes 4423688 | tf_op jit(solution)/shard_map/ppermute | solution.py:102
  1393.9 32.2 %collective-permute-start.96 = (bf16[288,2560]{1,0:T(8,128)(2,1)S(1)}, bf16[288,2560]{1,0:T(8,128)(2,1)S(1)}, u32[]{:S(2)}, u32[]{:S(2)}) collective-permute-start(bf16[288,2560]{1,0:T(8,128)(2,1)S(1)} %add_convert_fusion.8), channel_id=1, source_target_pairs={{0,8},{8,16},{16,24},{24,28},{28,20},{20,12},{12,4},{4,0},{1,9},{9... | collective-permute-start | bytes 4423688 | tf_op jit(solution)/shard_map/ppermute | solution.py:102
  1510.0 35.7 %collective-permute-start.107 = (bf16[288,3072]{1,0:T(8,128)(2,1)S(1)}, bf16[288,3072]{1,0:T(8,128)(2,1)S(1)}, u32[]{:S(2)}, u32[]{:S(2)}) collective-permute-start(bf16[288,3072]{1,0:T(8,128)(2,1)S(1)} %copy-done.23), channel_id=1, source_target_pairs={{0,1},{1,0},{2,3},{3,2},{4,5},{5,4},{6,7},{7,6},{8,9},{9,8},{10,11... | collective-permute-start | bytes 5308424 | tf_op jit(solution)/shard_map/ppermute | solution.py:157
  1513.9 31.9 %collective-permute-start.106 = (bf16[288,1152]{1,0:T(8,128)(2,1)S(1)}, bf16[288,1152]{1,0:T(8,128)(2,1)S(1)}, u32[]{:S(2)}, u32[]{:S(2)}) collective-permute-start(bf16[288,1152]{1,0:T(8,128)(2,1)S(1)} %get-tuple-element.985), channel_id=1, source_target_pairs={{0,16},{4,20},{8,24},{12,28},{16,0},{20,4},{24,8},{28,12},{1,17},{... | collective-permute-start | bytes 1990664 | tf_op jit(solution)/shard_map/ppermute | solution.py:157
  1545.7 33.9 %collective-permute-start.112 = (bf16[576,1152]{1,0:T(8,128)(2,1)S(1)}, bf16[576,1152]{1,0:T(8,128)(2,1)S(1)}, u32[]{:S(2)}, u32[]{:S(2)}) collective-permute-start(bf16[576,1152]{1,0:T(8,128)(2,1)S(1)} %pad_maximum_fusion.15), channel_id=1, source_target_pairs={{0,1},{1,0},{2,3},{3,2},{4,5},{5,4},{6,7},{7,6},{8,9},{9,8},{10,11... | collective-permute-start | bytes 3981320 | tf_op jit(solution)/shard_map/ppermute | solution.py:157
  1545.7 33.9 %collective-permute-start.111 = (bf16[576,1152]{1,0:T(8,128)(2,1)S(1)}, bf16[576,1152]{1,0:T(8,128)(2,1)S(1)}, u32[]{:S(2)}, u32[]{:S(2)}) collective-permute-start(bf16[576,1152]{1,0:T(8,128)(2,1)S(1)} %pad_maximum_fusion.14), channel_id=1, source_target_pairs={{0,1},{1,0},{2,3},{3,2},{4,5},{5,4},{6,7},{7,6},{8,9},{9,8},{10,11... | collective-permute-start | bytes 3981320 | tf_op jit(solution)/shard_map/ppermute | solution.py:157
  1548.0 31.7 %collective-permute-start.110 = (bf16[288,1152]{1,0:T(8,128)(2,1)S(1)}, bf16[288,1152]{1,0:T(8,128)(2,1)S(1)}, u32[]{:S(2)}, u32[]{:S(2)}) collective-permute-start(bf16[288,1152]{1,0:T(8,128)(2,1)S(1)} %get-tuple-element.993), channel_id=1, source_target_pairs={{0,16},{4,20},{8,24},{12,28},{16,0},{20,4},{24,8},{28,12},{1,17},{... | collective-permute-start | bytes 1990664 | tf_op jit(solution)/shard_map/ppermute | solution.py:157
  (199 other events, 2964.3 us)
